TPU v7x, 32 devices: a whole 2x2x4 slice. The times are simulated.
32 devices in a mesh: dp: 2 (over core), seq: 4 (over y, x), tensor: 4 (over z).
Axes of the slice: x: 2, y: 2, z: 4, core: 2. Of those that a mesh axis runs over, the one named last changes fastest.
Arguments:
- pool: bfloat16 [512, 16, 1792], P(('dp', 'seq'), 'tensor')
- page_table: int32 [8, 64], replicated, may hold values from 0 to 511, as said below
- reassign: int32 [8], replicated, may hold values from 0 to 7, as said below
- lengths: int32 [8], replicated, may hold values from 1 to 1024, as said below
- gain_one: float32 [1792], replicated, may hold values from 0.1 to 1.9
- w_featmap: bfloat16 [1792, 2, 256], P(None, None, 'tensor'), may hold values from -0.25 to 0.25
- w_value: bfloat16 [1792, 1792], P(None, 'tensor'), may hold values from -0.125 to 0.125
- w_out_one: bfloat16 [1792, 1792], P('tensor'), may hold values from -0.5 to 0.5
- gain_two: float32 [1792], replicated, may hold values from 0.1 to 1.9
- w_window: bfloat16 [1792, 3, 1792], P(None, None, 'tensor')
- conv_window: float32 [3, 3, 1792], P(None, None, 'tensor')
- w_out_two: bfloat16 [1792, 1792], P('tensor'), may hold values from -0.125 to 0.125
Outputs:
- out: bfloat16 [8, 64, 16, 1792], P('dp', 'seq', 'tensor')
Inputs may be any that keep to these rules, and one draw needn't show every extreme that they name: A permutation: output slot i holds request reassign[i]; requests are dealt by falling length to the 2 groups of 4 slots in alternating order, so the first slot of every group holds a request of length 1024. page_table[r, p] is the pool page that holds positions p * 16 to p * 16 + 15 of request r, and every pool page is named once. Take the pool in aligned blocks of 64 pages, and the pages that the output needs in blocks: block g * 4 + b holds positions b * 256 to b * 256 + 255 of slots g * 4 to g * 4 + 3. No pool block holds more than 8 pages of one such block, and 8 is reached. `lengths`: at least 2 requests have length 1024.
All inputs are finite; a program needn't handle non-finite values.
Results may differ from a plain program's by a relative error of at most 0.039.
Values may be sent and summed in bfloat16 or wider, within the bound.
No kernel may reach another device: no remote copies, remote signals or barrier semaphores. Data moves between devices by JAX's collectives and lax.ppermute only.
A program may use at most 256 MiB of HBM per device.

v0:
```python
import math

import jax
import jax.numpy as jnp
from jax import lax
from jax.sharding import PartitionSpec as P

HEAD = 112
WINDOW = 64


norm_eps = 1e-05


def entering(array, axis, combine, identity):
    peers, mine = (lax.axis_size(axis), lax.axis_index(axis))
    everything = jax.tree.map(
        lambda part, kind: lax.all_gather(part.astype(kind), axis),
        array,
        (jnp.bfloat16, jnp.bfloat16),
    )
    start = jax.tree.map(
        lambda part, zero: jnp.broadcast_to(jnp.asarray(zero, part.dtype), part.shape),
        array,
        identity,
    )

    def hop(k, before):
        reached = k < mine
        new = combine(
            before, jax.tree.map(lambda part, own: part[k].astype(own.dtype), everything, array)
        )
        return jax.tree.map(lambda a, b: jnp.where(reached, a, b), new, before)

    return lax.fori_loop(0, peers, hop, start)


def passed_along(array, axis, by):
    peers = lax.axis_size(axis)
    pairs = [(i, i + by) for i in range(peers) if 0 <= i + by < peers]
    return lax.ppermute(array, axis, pairs)


def rms_normed(row_block, gain_vector):
    values = row_block.astype(jnp.float32)
    scale = lax.rsqrt(jnp.mean(values * values, axis=-1, keepdims=True) + norm_eps)
    return (values * scale * gain_vector).astype(jnp.bfloat16)


def taylor_features(vectors):
    feature_dim = vectors.shape[-1]
    linear_part = vectors * feature_dim ** (-0.25)
    second = (
        vectors[..., :, None] * vectors[..., None, :] * (feature_dim ** (-0.5) / math.sqrt(2.0))
    )
    second = second.reshape(vectors.shape[:-1] + (feature_dim * feature_dim,))
    constant = jnp.ones(vectors.shape[:-1] + (1,), jnp.float32)
    return jnp.concatenate([constant, linear_part, second], axis=-1)


def project_rows(normed, weight):
    return jnp.dot(
        lax.all_gather(normed, "tensor", axis=2, tiled=True),
        weight,
        preferred_element_type=jnp.float32,
    )


def head_sum(mixed, weight, out_shape):
    partial_value = jnp.dot(mixed, weight, preferred_element_type=jnp.float32).reshape(out_shape)
    return lax.psum_scatter(
        partial_value.astype(jnp.bfloat16), "tensor", scatter_dimension=2, tiled=True
    ).astype(jnp.float32)


def add_pair(earlier, later):
    return (earlier[0] + later[0], earlier[1] + later[1])


def on_device(
    pool,
    page_table,
    reassign,
    lengths,
    gain_one,
    w_featmap,
    w_value,
    w_out_one,
    gain_two,
    w_window,
    conv_window,
    w_out_two,
):
    highest = lax.Precision.HIGHEST
    groups = lax.axis_size(("dp", "seq"))
    device_place = lax.axis_index(("dp", "seq"))
    seq_count = lax.axis_size("seq")
    seq_place = lax.axis_index("seq")
    group_place = lax.axis_index("dp")
    tensor_place = lax.axis_index("tensor")
    pages_dev, page_share, model_width = pool.shape
    slots_total, pages_total = page_table.shape
    req_dev = slots_total // lax.axis_size("dp")
    page_span = pages_total // seq_count
    page_rows = page_share * lax.axis_size("tensor")
    block_rows = page_span * page_rows
    capacity = (pages_dev + groups - 1) // groups
    target = jnp.arange(groups, dtype=jnp.int32)[:, None]
    local_page = jnp.arange(pages_dev, dtype=jnp.int32)[None, :]
    wanted = reassign[target // seq_count * req_dev + local_page // page_span]
    source_page = page_table[wanted, target % seq_count * page_span + local_page % page_span]
    page_owner = source_page // pages_dev
    pool_slot = source_page % pages_dev
    before = jnp.arange(pages_dev)[None, :] < jnp.arange(pages_dev)[:, None]
    pair_rank = jnp.sum((page_owner[:, :, None] == page_owner[:, None, :]) & before[None], axis=2)
    send_hit = (page_owner == device_place)[:, None, :] & (
        pair_rank[:, None, :] == jnp.arange(capacity)[None, :, None]
    )
    send_slot = jnp.sum(jnp.where(send_hit, pool_slot[:, None, :], 0), axis=2)
    outgoing = jnp.take(pool, send_slot.reshape(-1), axis=0).reshape(
        groups, capacity, page_share, model_width
    )
    arrived = lax.all_to_all(outgoing, ("dp", "seq"), split_axis=0, concat_axis=0, tiled=True)
    pick_rows = page_owner[device_place] * capacity + pair_rank[device_place]
    tokens = jnp.take(
        arrived.reshape(groups * capacity, page_share, model_width), pick_rows, axis=0
    )
    tokens = tokens.reshape(req_dev, page_span, page_share, model_width)
    slot_ids = lax.dynamic_slice_in_dim(reassign, group_place * req_dev, req_dev)
    prompt_length = lengths[slot_ids]
    out_shape = (req_dev, page_span, page_rows, model_width)
    heads_dev = w_value.shape[1] // HEAD
    head_cols = heads_dev * HEAD
    feat_cols = w_featmap.shape[2]
    feature_dim = feat_cols // heads_dev
    normed_one = rms_normed(tokens, gain_one)
    weight_one = jnp.concatenate([w_featmap.reshape(model_width, 2 * feat_cols), w_value], axis=1)
    projected_one = project_rows(normed_one, weight_one).reshape(
        req_dev, block_rows, 2 * feat_cols + head_cols
    )
    queries = (
        projected_one[..., :feat_cols]
        .astype(jnp.bfloat16)
        .reshape(req_dev, block_rows, heads_dev, feature_dim)
    )
    key_rows = (
        projected_one[..., feat_cols : 2 * feat_cols]
        .astype(jnp.bfloat16)
        .reshape(req_dev, block_rows, heads_dev, feature_dim)
    )
    values = (
        projected_one[..., 2 * feat_cols :]
        .astype(jnp.bfloat16)
        .reshape(req_dev, block_rows, heads_dev, HEAD)
    )
    scores = jnp.einsum(
        "rthf,ruhf->rhtu", queries, key_rows, preferred_element_type=jnp.float32
    ) * feature_dim ** (-0.5)
    causal = jnp.arange(block_rows)[None, :] <= jnp.arange(block_rows)[:, None]
    kernel = jnp.where(causal[None, None], 1.0 + scores + 0.5 * scores * scores, 0.0)
    values_wide = values.astype(jnp.float32)
    numerator = jnp.einsum("rhtu,ruhd->rthd", kernel, values_wide, precision=highest)
    denominator = jnp.sum(kernel, axis=3).transpose(0, 2, 1)
    query_features = taylor_features(queries.astype(jnp.float32))
    key_features = taylor_features(key_rows.astype(jnp.float32))
    block_state = jnp.einsum("ruhf,ruhd->rhfd", key_features, values_wide, precision=highest)
    block_norm = jnp.sum(key_features, axis=1)
    prior_state, prior_norm = entering(
        (block_state, block_norm),
        "seq",
        add_pair,
        (jnp.zeros_like(block_state), jnp.zeros_like(block_norm)),
    )
    numerator = numerator + jnp.einsum(
        "rthf,rhfd->rthd", query_features, prior_state, precision=highest
    )
    denominator = denominator + jnp.einsum(
        "rthf,rhf->rth", query_features, prior_norm, precision=highest
    )
    mixed_one = (
        (numerator / denominator[..., None])
        .astype(jnp.bfloat16)
        .reshape(req_dev, block_rows, head_cols)
    )
    branch_one = head_sum(mixed_one, w_out_one, out_shape)
    residual_one = (tokens.astype(jnp.float32) + branch_one).astype(jnp.bfloat16)
    normed_two = rms_normed(residual_one, gain_two)
    projected_two = project_rows(normed_two, w_window.reshape(model_width, 3 * head_cols)).reshape(
        req_dev, block_rows, 3 * head_cols
    )
    tap_count = conv_window.shape[0]
    reach_rows = WINDOW + tap_count - 1
    tail_rows = projected_two[:, block_rows - reach_rows :, :]
    previous = passed_along(tail_rows.astype(jnp.bfloat16), "seq", 1).astype(tail_rows.dtype)
    extended = jnp.concatenate([previous, projected_two], axis=1)
    tap_table = conv_window.reshape(tap_count, 3 * head_cols)
    span_rows = WINDOW + block_rows
    convolved = tap_table[0] * extended[:, tap_count - 1 : tap_count - 1 + span_rows]
    for offset in range(1, tap_count):
        convolved = (
            convolved
            + tap_table[offset]
            * extended[:, tap_count - 1 - offset : tap_count - 1 - offset + span_rows]
        )
    convolved = convolved.astype(jnp.bfloat16)
    queries_two = convolved[:, WINDOW:, :head_cols].reshape(req_dev, block_rows, heads_dev, HEAD)
    keys_two = convolved[:, :, head_cols : 2 * head_cols].reshape(
        req_dev, span_rows, heads_dev, HEAD
    )
    values_two = convolved[:, :, 2 * head_cols :].reshape(req_dev, span_rows, heads_dev, HEAD)
    logits = jnp.einsum(
        "rthd,ruhd->rhtu", queries_two, keys_two, preferred_element_type=jnp.float32
    ) * HEAD ** (-0.5)
    query_pos = jnp.arange(block_rows)[:, None]
    key_pos = jnp.arange(span_rows)[None, :] - WINDOW
    allowed = (
        (key_pos <= query_pos)
        & (key_pos > query_pos - WINDOW)
        & (key_pos + seq_place * block_rows >= 0)
    )
    logits = jnp.where(allowed[None, None], logits, -jnp.inf)
    row_top = jnp.max(logits, axis=3, keepdims=True)
    weights = jnp.exp(logits - row_top)
    attention = (weights / jnp.sum(weights, axis=3, keepdims=True)).astype(jnp.bfloat16)
    mixed_two = jnp.einsum(
        "rhtu,ruhd->rthd", attention, values_two, preferred_element_type=jnp.float32
    )
    mixed_two = mixed_two.astype(jnp.bfloat16).reshape(req_dev, block_rows, head_cols)
    branch_two = head_sum(mixed_two, w_out_two, out_shape)
    result = (residual_one.astype(jnp.float32) + branch_two).astype(jnp.bfloat16)
    position = (
        seq_place * block_rows
        + jnp.arange(page_span)[:, None] * page_rows
        + tensor_place * page_share
        + jnp.arange(page_share)[None, :]
    )
    is_live = position[None] < prompt_length[:, None, None]
    return jnp.where(is_live[..., None], result, jnp.zeros_like(result))


def solution(mesh):
    return jax.shard_map(
        on_device,
        mesh=mesh,
        in_specs=(
            P(("dp", "seq"), "tensor", None),
            P(),
            P(),
            P(),
            P(),
            P(None, None, "tensor"),
            P(None, "tensor"),
            P("tensor", None),
            P(),
            P(None, None, "tensor"),
            P(None, None, "tensor"),
            P("tensor", None),
        ),
        out_specs=P("dp", "seq", "tensor", None),
        check_vma=False,
    )
```

profile of v0, /device:TPU:0, one launch (start us, length us, event | category | flops | bytes accessed | tf_op | source)
XLA Modules:
  0.0 517.0 jit_solution(11609165507890648512)
XLA Ops:
  6.7 3.6 gather_fusion.1
  10.6 2.6 gather_fusion.2
  13.3 0.3 convert_reduce_fusion
  14.0 1.4 gather_fusion.3
  15.3 1.4 broadcast_select_fusion
  16.8 5.3 %all-to-all-start = ((bf16[8,8,4,1792]{3,2,1,0:T(4,128)(2,1)}), bf16[8,8,4,1792]{3,2,1,0:T(4,128)(2,1)S(1)}, u32[]{:S(2)}, u32[]{:S(2)}) async-start(bf16[8,8,4,1792]{3,2,1,0:T(4,128)(2,1)} %bitcast.1), calls=%async_computation | async-start | bytes 1835008 | tf_op jit(solution)/shard_map/all_to_all | solution.py:123
  22.1 13.4 %all-to-all-done = bf16[8,8,4,1792]{3,2,1,0:T(4,128)(2,1)S(1)} async-done(((bf16[8,8,4,1792]{3,2,1,0:T(4,128)(2,1)}), bf16[8,8,4,1792]{3,2,1,0:T(4,128)(2,1)S(1)}, u32[]{:S(2)}, u32[]{:S(2)}) %all-to-all-start) | async-done | bytes 917536 | tf_op jit(solution)/shard_map/all_to_all | solution.py:123
  35.5 2.2 gather_fusion.4
  37.7 1.6 select_convert_fusion
  39.3 2.6 multiply_reduce_fusion
  42.0 1.3 multiply_convert_fusion
  43.4 0.3 all-gather.10.cloned.1.call-start
  43.7 71.9 %all-gather.6.cloned.1.call-done = bf16[4,16,16,1792]{3,1,0,2:T(8,128)(2,1)} async-done(((bf16[4,16,4,1792]{3,1,0,2:T(8,128)(2,1)}), bf16[4,16,16,1792]{3,1,0,2:T(8,128)(2,1)}) %all-gather.6.cloned.1.call-update) | async-done | bytes 3670032 | tf_op jit(solution)/shard_map/all_gather | solution.py:63
  115.6 6.9 %fusion.39 = bf16[4,16,16,576]{3,2,1,0:T(8,128)(2,1)S(1)} fusion(bf16[1792,448]{0,1:T(8,128)(2,1)} %param.22, bf16[1792,128]{0,1:T(8,128)(2,1)} %bitcast.110, bf16[4,16,16,1792]{3,1,0,2:T(8,128)(2,1)} %all-gather.6.cloned.1.call-done), kind=kOutput, calls=%fused_computation.72 | convolution fusion | flops 2118647808 | bytes 6914048 | tf_op jit(solution)/shard_map/dot_general | solution.py:62
  122.9 2.7 multiply_multiply_fusion.1
  125.6 1.3 copy.88
  126.9 5.0 fusion.42
  131.9 1.4 copy.92
  133.6 3.2 fusion.14
  136.8 9.0 %all-gather.1 = bf16[16,4,273]{2,1,0:T(4,128)(2,1)S(1)} all-gather(bf16[4,4,273]{2,1,0:T(4,128)(2,1)S(1)} %fusion.14), channel_id=3, replica_groups=mesh['dp'=2,'seq'=4,'tensor'=4] {'seq'}, dimensions={0}, use_global_device_ids=true | all-gather | bytes 43680 | tf_op jit(solution)/shard_map/all_gather | solution.py:18
  145.8 1.4 fusion.16
  147.2 2.7 multiply_multiply_fusion
  149.9 3.8 fusion.17
  153.6 33.5 %all-gather.10.cloned.1.call-done = bf16[16,4,273,112]{3,1,2,0:T(4,128)(2,1)} async-done(((bf16[4,4,273,112]{3,1,2,0:T(4,128)(2,1)}), bf16[16,4,273,112]{3,1,2,0:T(4,128)(2,1)}) %all-gather.10.cloned.1.call-update) | async-done | bytes 3913744 | tf_op jit(solution)/shard_map/all_gather | solution.py:18
  187.2 18.3 %while.16 = (s32[]{:T(128)}, f32[4,4,273,112]{3,2,1,0:T(8,128)}, f32[4,4,273]{2,1,0:T(4,128)S(1)}, s32[]{:T(128)}, bf16[4,4,4,273,112]{4,2,3,1,0:T(4,128)(2,1)},...) while((s32[]{:T(128)}, f32[4,4,273,112]{3,2,1,0:T(8,128)}, ...), condition=%wide.region_5.7_spmd.clone, body=%wide.region_4.6_spmd.clone.sunk | while | flops 1974340 | bytes 6892819 | solution.py:35
  187.2 1.6 constant_dynamic-slice_fusion.2
  188.8 1.7 add_select_fusion.9
  190.5 1.6 constant_dynamic-slice_fusion.2
  192.2 3.3 add_select_fusion.9
  195.5 1.6 constant_dynamic-slice_fusion.2
  197.2 3.3 add_select_fusion.9
  200.5 1.6 constant_dynamic-slice_fusion.2
  202.2 3.3 add_select_fusion.9
  205.5 5.2 %fusion.12 = f32[4,4,1,256]{3,2,1,0:T(1,128)S(1)} fusion(f32[4,256,4,256]{1,3,2,0:T(8,128)} %bitcast.93, f32[4,256,4,16]{1,3,2,0:T(8,128)S(1)} %broadcast_multiply_fusion, f32[273]{0:T(512)S(1)} %pad.5.clone, f32[4,4,273,1]{2,1,0,3:T(4,128)S(1)} %bitcast.106), kind=kOutput, calls=%fused_computation.36 | convolution fusion | flops 15654912 | bytes 4491396 | tf_op jit(solution)/shard_map/rthf,rhf->rth/dot_general | solution.py:177
  210.8 8.7 %fusion.36 = bf16[4,256,4,112]{1,3,2,0:T(8,128)(2,1)} fusion(f32[4,4,112,256]{3,2,1,0:T(8,128)S(1)} %copy-done.16, f32[4,4,273,112]{3,2,1,0:T(8,128)S(1)} %copy-done.5, f32[4,256,4,256]{1,3,2,0:T(8,128)} %bitcast.94, f32[4,256,4,16]{1,3,2,0:T(8,128)S(1)} %broadcast_multiply_fusion, f32[273]{0:T(512)S(1)} %pad.5.clone, f32[4,256,4]{1,2,0:T(4,128)S(1)} %fusion.52), kind=kOutput, calls=%fused_computation.66 | convolution fusion | flops 1506484224 | bytes 9183300 | tf_op jit(solution)/shard_map/rthf,rhfd->rthd/dot_general | solution.py:174
  219.5 1.6 copy.94
  221.2 1.6 dot_general.45
  222.8 3.3 convolution_convert_fusion.1
  226.1 2.9 copy.95
  229.1 68.5 %reduce-scatter.3.cloned.1.call-done = bf16[4,16,4,1792]{3,1,0,2:T(8,128)(2,1)} async-done(((bf16[4,16,16,1792]{3,1,0,2:T(8,128)(2,1)}), bf16[4,16,4,1792]{3,1,0,2:T(8,128)(2,1)}) %reduce-scatter.3.cloned.1.call-update) | async-done | bytes 917520 | tf_op jit(solution)/shard_map/reduce_scatter | solution.py:71
  297.6 1.6 fusion.32
  299.2 1.2 fusion.34
  300.5 72.6 %all-gather.8.cloned.1.call-done = bf16[4,16,16,1792]{3,1,0,2:T(8,128)(2,1)} async-done(((bf16[4,16,4,1792]{3,1,0,2:T(8,128)(2,1)}), bf16[4,16,16,1792]{3,1,0,2:T(8,128)(2,1)}) %all-gather.8.cloned.1.call-update) | async-done | bytes 3670032 | tf_op jit(solution)/shard_map/all_gather | solution.py:63
  373.1 4.0 copy.97
  377.1 7.1 %fusion.76 = f32[4,256,1344]{1,2,0:T(8,128)S(1)} fusion(bf16[4,256,1792]{2,1,0:T(8,128)(2,1)S(1)} %bitcast.95, bf16[1792,1344,1]{0,1,2:T(8,128)(2,1)} %bitcast.109), kind=kOutput, calls=%fused_computation.156 | convolution fusion | flops 4932501504 | bytes 13991936 | tf_op jit(solution)/shard_map/dot_general | solution.py:62
  384.2 2.4 copy-done.8
  386.6 0.4 slice.105
  387.1 1.4 copy.98
  388.5 3.5 collective-permute-start
  392.4 15.4 %collective-permute-done = bf16[4,66,1344]{2,0,1:T(4,128)(2,1)S(1)} collective-permute-done((bf16[4,66,1344]{2,0,1:T(4,128)(2,1)S(1)}, bf16[4,66,1344]{2,0,1:T(4,128)(2,1)S(1)}, u32[]{:S(2)}, u32[]{:S(2)}) %collective-permute-start) | collective-permute-done | bytes 709664 | tf_op jit(solution)/shard_map/ppermute | solution.py:41
  407.7 1.7 copy.99
  409.6 11.3 %fusion.5 = bf16[4,320,1344]{1,2,0:T(8,128)(2,1)S(1)} fusion(f32[4,256,1344]{1,2,0:T(8,128)} %copy-done.8, f32[4,66,1344]{1,2,0:T(8,128)S(1)} %convert_element_type.138, f32[1344]{0:T(1024)S(1)} %mul.223, f32[1344]{0:T(1024)S(1)} %mul.220, f32[1344]{0:T(1024)S(1)} %mul.212), kind=kLoop, calls=%fused_computation.18 | loop fusion | flops 15482880 | bytes 10381056 | tf_op jit(solution)/shard_map/convert_element_type | solution.py:205
  420.9 0.3 fusion.72
  421.2 1.3 slice.78
  422.5 5.3 %fusion.75 = (f32[4,4,256]{2,1,0:T(4,128)S(1)}, f32[4,4,256,320]{2,3,1,0:T(8,128)}) fusion(pred[256,320]{0,1:T(8,128)(4,1)S(1)} %fusion.47, bf16[4,256,4,112]{1,3,2,0:T(8,128)(2,1)} %bitcast.103, bf16[4,320,4,112]{1,3,2,0:T(8,128)(2,1)S(1)} %bitcast.100), kind=kOutput, calls=%fused_computation.153 | convolution fusion | flops 298844480 | bytes 7405568 | tf_op jit(solution)/shard_map/sub | solution.py:223
  427.9 3.2 fusion.44
  431.1 0.7 copy.102
  431.7 0.7 dot_general.51
  432.4 3.5 convolution_convert_fusion
  436.0 2.9 copy.103
  439.0 0.6 gather_fusion
  439.7 67.4 %reduce-scatter.5.cloned.1.call-done = bf16[4,16,4,1792]{3,1,0,2:T(8,128)(2,1)} async-done(((bf16[4,16,16,1792]{3,1,0,2:T(8,128)(2,1)}), bf16[4,16,4,1792]{3,1,0,2:T(8,128)(2,1)}) %reduce-scatter.5.cloned.1.call-update) | async-done | bytes 917520 | tf_op jit(solution)/shard_map/reduce_scatter | solution.py:71
  507.2 1.5 fusion.45
  508.6 1.6 copy.104
  (95 shorter events, 2.7 us)
Async XLA Ops:
  6.5 216.3 %copy-start = (bf16[448,1792]{1,0:T(8,128)(2,1)S(1)}, bf16[448,1792]{1,0:T(8,128)(2,1)}, u32[]{:S(2)}) copy-start(bf16[448,1792]{1,0:T(8,128)(2,1)} %param.23) | copy-start | bytes 4816900
  6.5 4.0 copy-start.3
  6.7 7.2 %copy-start.11 = (bf16[64,4,1792]{2,1,0:T(4,128)(2,1)S(1)}, bf16[64,4,1792]{2,1,0:T(4,128)(2,1)}, u32[]{:S(2)}) copy-start(bf16[64,4,1792]{2,1,0:T(4,128)(2,1)} %param.16) | copy-start | bytes 2752516
  16.8 25.3 %copy-start.14 = (f32[1792]{0:T(1024)S(1)}, f32[1792]{0:T(1024)}, u32[]{:S(2)}) copy-start(f32[1792]{0:T(1024)} %param.20) | copy-start | bytes 21508
  16.8 18.8 %all-to-all-start = ((bf16[8,8,4,1792]{3,2,1,0:T(4,128)(2,1)}), bf16[8,8,4,1792]{3,2,1,0:T(4,128)(2,1)S(1)}, u32[]{:S(2)}, u32[]{:S(2)}) async-start(bf16[8,8,4,1792]{3,2,1,0:T(4,128)(2,1)} %bitcast.1), calls=%async_computation | async-start | bytes 1835008 | tf_op jit(solution)/shard_map/all_to_all | solution.py:123
  22.1 93.5 %all-gather.6.cloned.1.call-start = ((), (), s32[]{:S(2)}) async-start(), calls=%async_computation.3 | async-start | bytes 4587520 | tf_op jit(solution)/shard_map/all_gather | solution.py:63
  39.3 83.2 %copy-start.6 = (f32[64,4,1792]{2,1,0:T(4,128)}, f32[64,4,1792]{2,1,0:T(4,128)S(1)}, u32[]{:S(2)}) copy-start(f32[64,4,1792]{2,1,0:T(4,128)S(1)} %select_convert_fusion) | copy-start | bytes 5505028
  43.4 143.8 %all-gather.10.cloned.1.call-start = ((), (), s32[]{:S(2)}) async-start(), calls=%async_computation.7 | async-start | bytes 5591040 | tf_op jit(solution)/shard_map/all_gather | solution.py:18
  133.4 164.2 %reduce-scatter.3.cloned.1.call-start = ((), (), s32[]{:S(2)}) async-start(), calls=%async_computation.4 | async-start | bytes 4587520 | tf_op jit(solution)/shard_map/reduce_scatter | solution.py:71
  147.2 2.7 copy-start.12
  205.5 5.3 %copy-start.5 = (f32[4,4,273,112]{3,2,1,0:T(8,128)S(1)}, f32[4,4,273,112]{3,2,1,0:T(8,128)}, u32[]{:S(2)}) copy-start(f32[4,4,273,112]{3,2,1,0:T(8,128)} %get-tuple-element.116) | copy-start | bytes 5870596
  205.5 5.3 %copy-start.16 = (f32[4,4,112,256]{3,2,1,0:T(8,128)S(1)}, f32[4,4,112,256]{3,2,1,0:T(8,128)}, u32[]{:S(2)}) copy-start(f32[4,4,112,256]{3,2,1,0:T(8,128)} %fusion.17) | copy-start | bytes 5505028
  226.1 71.5 %copy-start.7 = (f32[64,4,1792]{2,1,0:T(4,128)S(1)}, f32[64,4,1792]{2,1,0:T(4,128)}, u32[]{:S(2)}) copy-start(f32[64,4,1792]{2,1,0:T(4,128)} %copy-done.6) | copy-start | bytes 5505028
  229.0 70.2 %copy-start.15 = (f32[1792]{0:T(1024)S(1)}, f32[1792]{0:T(1024)}, u32[]{:S(2)}) copy-start(f32[1792]{0:T(1024)} %param.24) | copy-start | bytes 21508
  229.0 144.1 %all-gather.8.cloned.1.call-start = ((), (), s32[]{:S(2)}) async-start(), calls=%async_computation.5 | async-start | bytes 4587520 | tf_op jit(solution)/shard_map/all_gather | solution.py:63
  299.2 78.0 %copy-start.9 = (bf16[4,16,4,1792]{3,1,0,2:T(8,128)(2,1)}, bf16[4,16,4,1792]{3,1,0,2:T(8,128)(2,1)S(1)}, u32[]{:S(2)}) copy-start(bf16[4,16,4,1792]{3,1,0,2:T(8,128)(2,1)S(1)} %get-tuple-element.176) | copy-start | bytes 2752516
  300.4 206.7 %reduce-scatter.5.cloned.1.call-start = ((), (), s32[]{:S(2)}) async-start(), calls=%async_computation.6 | async-start | bytes 4587520 | tf_op jit(solution)/shard_map/reduce_scatter | solution.py:71
  384.2 2.4 copy-start.8
  386.6 5.3 %copy-start.13 = (f32[3,3,448]{2,1,0:T(4,128)S(1)}, f32[3,3,448]{2,1,0:T(4,128)}, u32[]{:S(2)}) copy-start(f32[3,3,448]{2,1,0:T(4,128)} %param.26) | copy-start | bytes 48388
  388.5 19.3 %collective-permute-start = (bf16[4,66,1344]{2,0,1:T(4,128)(2,1)S(1)}, bf16[4,66,1344]{2,0,1:T(4,128)(2,1)S(1)}, u32[]{:S(2)}, u32[]{:S(2)}) collective-permute-start(bf16[4,66,1344]{2,0,1:T(4,128)(2,1)S(1)} %copy.98), channel_id=1, source_target_pairs={{0,4},{4,8},{8,12},{1,5},{5,9},{9,13},{2,6},{6,10},{10,14},{3,7},{... | collective-permute-start | bytes 2128904 | tf_op jit(solution)/shard_map/ppermute | solution.py:41
  435.9 3.0 copy-start.2
  436.0 3.0 copy-start.4
  436.0 71.2 %copy-start.10 = (bf16[4,16,4,1792]{3,1,0,2:T(8,128)(2,1)S(1)}, bf16[4,16,4,1792]{3,1,0,2:T(8,128)(2,1)}, u32[]{:S(2)}) copy-start(bf16[4,16,4,1792]{3,1,0,2:T(8,128)(2,1)} %copy-done.9) | copy-start | bytes 2752516
  438.9 71.4 %copy-start.1 = (bf16[448,1792]{1,0:T(8,128)(2,1)S(1)}, bf16[448,1792]{1,0:T(8,128)(2,1)}, u32[]{:S(2)}) copy-start(bf16[448,1792]{1,0:T(8,128)(2,1)} %param.23) | copy-start | bytes 4816900
Sparse Core Ops, SparseCore 0:
  43.5 71.9 all-gather.5
  133.5 53.6 all-gather.9
  229.2 68.3 reduce-scatter.2
  300.6 72.4 all-gather.7
  439.0 68.1 reduce-scatter.4
where the time goes:
time: 523 us; the launch traced here: 517 us
  waiting for transfers between devices  343 us (66%)
  matrix products  53.4 us (10%)
  local copies, waits for them, and re-layouts  44.5 us (9%)
  other arithmetic  44.1 us (8%)
  between operations  13.9 us (3%)
  starting transfers between devices  9.17 us (2%)
  blocking collectives  8.97 us (2%)
    all_gather x2, waiting for transfers between devices, project_rows(): lax.all_gather(normed, 'tensor', axis=2, tiled=True)  144 us
    reduce_scatter x2, waiting for transfers between devices, head_sum(): lax.psum_scatter(partial_value.astype(jnp.bfloat16), 'tensor', scatter_di...  136 us
    all_gather x1, waiting for transfers between devices, entering(): lax.all_gather(part.astype(kind), axis)  33.5 us
    ppermute x1, waiting for transfers between devices, passed_along(): return lax.ppermute(array, axis, pairs)  15.4 us
    dot_general x2, matrix products, project_rows(): jnp.dot(lax.all_gather(normed, 'tensor', axis=2, tiled=True), weight, pre...  14 us
    all_to_all x1, waiting for transfers between devices, on_device(): lax.all_to_all(outgoing, ('dp', 'seq'), split_axis=0, concat_axis=0, tile...  13.4 us
    select_n x8, other arithmetic, hop(): return jax.tree.map(lambda a, b: jnp.where(reached, a, b), new, before)  11.7 us
    convert_element_type x1, other arithmetic, on_device(): convolved = convolved.astype(jnp.bfloat16)  11.3 us
  transfers between devices with their start and end apart: 7, of which 7 were waited for; matrix products, arithmetic and copies ran while one was open for 2% of the time, Pallas kernels for 0%

commit v1 on v0

v1 whole, which is shorter than its diff:
```python
import functools

import jax
import jax.numpy as jnp
import numpy as np
from jax import lax
from jax.experimental import pallas as pl
from jax.experimental.pallas import tpu as pltpu
from jax.sharding import PartitionSpec as P

HEAD = 112
WINDOW = 64
EPS = 1e-05
SLOT = 128
FEAT_SLOT = 256
HALO = 80
VMEM = 60 * 1024 * 1024
F32 = jnp.float32
BF16 = jnp.bfloat16


def dot(a, b, dims=((1,), (0,))):
    return lax.dot_general(a, b, (dims, ((), ())), preferred_element_type=F32)


def normed_rows(rows, gain):
    scale = lax.rsqrt(jnp.mean(rows * rows, axis=-1, keepdims=True) + EPS)
    return (rows * scale * gain).astype(BF16)


def feature_tables(heads, feature_dim):
    pairs = [(i, j) for i in range(feature_dim) for j in range(i, feature_dim)]
    pairs += [(i, -1) for i in range(feature_dim)] + [(-1, -1)]
    first = np.zeros((heads * feature_dim, heads * FEAT_SLOT), np.float32)
    second = np.zeros_like(first)
    ones = np.zeros((2, heads * FEAT_SLOT), np.float32)
    scale = np.zeros((1, heads * FEAT_SLOT), np.float32)
    for h in range(heads):
        for n, (i, j) in enumerate(pairs):
            at = h * FEAT_SLOT + n
            if i >= 0:
                first[h * feature_dim + i, at] = 1
            else:
                ones[0, at] = 1
            if j >= 0:
                second[h * feature_dim + j, at] = 1
            else:
                ones[1, at] = 1
            if i < 0:
                scale[0, at] = 1
            elif j < 0:
                scale[0, at] = feature_dim**-0.5
            else:
                scale[0, at] = (0.5 if i == j else 1.0) / feature_dim
    return first, second, ones, scale, -(-len(pairs) // 16) * 16


def spread_table(heads):
    spread = np.zeros((heads * HEAD, heads * SLOT), np.float32)
    ones = np.zeros((1, heads * SLOT), np.float32)
    for h in range(heads):
        spread[h * HEAD : (h + 1) * HEAD, h * SLOT : h * SLOT + HEAD] = np.eye(HEAD)
        ones[0, h * SLOT + HEAD] = 1
    return spread, ones


def features(rows, first, second, ones):
    return (dot(rows, first) + ones[0:1]) * (dot(rows, second) + ones[1:2])


def linear_kernel(
    heads,
    feature_dim,
    kept,
    x_ref,
    gain_ref,
    w_ref,
    first_ref,
    second_ref,
    ones_ref,
    spread_ref,
    column_ref,
    num_ref,
    q_ref,
    state_ref,
    normed_ref,
):
    @pl.when(pl.program_id(0) == 0)
    def _():
        normed_ref[...] = normed_rows(x_ref[...].astype(F32), gain_ref[...])

    rows = x_ref.shape[0]
    width = heads * feature_dim
    projected = dot(normed_ref[...], w_ref[0]).astype(BF16)
    queries = projected[:, :width]
    keys = projected[:, width : 2 * width]
    values = dot(projected[:, 2 * width :], spread_ref[...]) + column_ref[...]
    values = values.astype(BF16)
    q_ref[0] = queries
    lane_head = lax.broadcasted_iota(jnp.int32, (rows, width), 1) // feature_dim
    causal = lax.broadcasted_iota(jnp.int32, (rows, rows), 1) <= lax.broadcasted_iota(
        jnp.int32, (rows, rows), 0
    )
    key_features = features(keys, first_ref[...], second_ref[...], ones_ref[...]).astype(BF16)
    for h in range(heads):
        own = jnp.where(lane_head == h, queries, jnp.zeros_like(queries))
        scores = dot(own, keys, ((1,), (1,))) * feature_dim**-0.5
        kernel = jnp.where(causal, 1.0 + scores + 0.5 * scores * scores, 0.0).astype(BF16)
        value = values[:, h * SLOT : (h + 1) * SLOT]
        num_ref[0, :, h * SLOT : (h + 1) * SLOT] = dot(kernel, value)
        state = dot(key_features[:, h * FEAT_SLOT : h * FEAT_SLOT + kept], value, ((0,), (0,)))
        state_ref[0, h * kept : (h + 1) * kept, :] = state.astype(BF16)


def padded_heads(heads, w, padded_ref):
    cols = w.shape[1]
    for h in range(heads):
        padded_ref[h * SLOT : h * SLOT + HEAD, :] = w[h * HEAD : (h + 1) * HEAD, :]
        padded_ref[h * SLOT + HEAD : (h + 1) * SLOT, :] = jnp.zeros((SLOT - HEAD, cols), BF16)


def add_branch(heads, mixed, w_ref, padded_ref, total_ref):
    parts, cols = w_ref.shape[1], w_ref.shape[3]
    for part in range(parts):
        padded_heads(heads, w_ref[0, part], padded_ref)
        share = dot(mixed, padded_ref[...]).astype(BF16).astype(F32)
        total_ref[:, part * cols : (part + 1) * cols] += share


def out_one_kernel(
    heads,
    kept,
    priors,
    *refs,
):
    num_ref, q_ref, first_ref, second_ref, ones_ref, scale_ref = refs[:6]
    prior_refs = refs[6 : 6 + priors]
    w_ref, x_ref, gain_ref, residual_ref, normed_ref, total_ref, padded_ref, mixed_ref = refs[
        6 + priors :
    ]
    step = pl.program_id(0)

    @pl.when(step == 0)
    def _():
        total_ref[...] = jnp.zeros_like(total_ref)

    query_features = features(q_ref[0], first_ref[...], second_ref[...], ones_ref[...])
    query_features = (query_features * scale_ref[...]).astype(BF16)
    for h in range(heads):
        at = slice(h * kept, (h + 1) * kept)
        prior = prior_refs[0][0, at, :].astype(F32)
        for ref in prior_refs[1:]:
            prior = prior + ref[0, at, :].astype(F32)
        lanes = slice(h * SLOT, (h + 1) * SLOT)
        total = num_ref[0, :, lanes] + dot(
            query_features[:, h * FEAT_SLOT : h * FEAT_SLOT + kept], prior.astype(BF16)
        )
        mixed_ref[:, lanes] = (total / total[:, HEAD : HEAD + 1]).astype(BF16)
    add_branch(heads, mixed_ref[...], w_ref, padded_ref, total_ref)

    @pl.when(step == pl.num_programs(0) - 1)
    def _():
        residual = (x_ref[...].astype(F32) + total_ref[...]).astype(BF16)
        residual_ref[...] = residual
        normed_ref[...] = normed_rows(residual.astype(F32), gain_ref[...])


def window_kernel(heads, first_ref, x_ref, halo_ref, w_ref, tap_ref, mixed_ref, rows_ref):
    @pl.when(pl.program_id(0) == 0)
    def _():
        rows_ref[:HALO] = halo_ref[...]
        rows_ref[HALO:] = x_ref[...]

    rows = x_ref.shape[0]
    lead = HALO - WINDOW
    cols = heads * HEAD
    projected = dot(rows_ref[...], w_ref[0])
    taps = tap_ref[0]
    convolved = taps[0:1] * projected
    for offset in range(1, taps.shape[0]):
        convolved = convolved + taps[offset : offset + 1] * pltpu.roll(projected, offset, 0)
    convolved = convolved[lead:].astype(BF16)
    tile = 128
    span = tile + WINDOW
    row = lax.broadcasted_iota(jnp.int32, (tile, span), 0)
    col = lax.broadcasted_iota(jnp.int32, (tile, span), 1)
    band = (col > row) & (col <= row + WINDOW)
    for h in range(heads):
        queries = convolved[WINDOW:, h * HEAD : (h + 1) * HEAD]
        keys = convolved[:, cols + h * HEAD : cols + (h + 1) * HEAD]
        values = convolved[:, 2 * cols + h * HEAD : 2 * cols + (h + 1) * HEAD]
        for start in range(0, rows, tile):
            logits = dot(queries[start : start + tile], keys[start : start + span], ((1,), (1,)))
            allowed = band
            if start < WINDOW:
                allowed = band & (col >= WINDOW - start - first_ref[0])
            logits = jnp.where(allowed, logits * HEAD**-0.5, -jnp.inf)
            weights = jnp.exp(logits - jnp.max(logits, axis=1, keepdims=True))
            weights = weights / jnp.sum(weights, axis=1, keepdims=True)
            mixed = dot(weights.astype(BF16), values[start : start + span])
            mixed_ref[0, start : start + tile, h * SLOT : h * SLOT + HEAD] = mixed.astype(BF16)
    for h in range(heads):
        mixed_ref[0, :, h * SLOT + HEAD : (h + 1) * SLOT] = jnp.zeros((rows, SLOT - HEAD), BF16)


def out_two_kernel(heads, live_ref, mixed_ref, w_ref, residual_ref, out_ref, total_ref, padded_ref):
    step = pl.program_id(0)

    @pl.when(step == 0)
    def _():
        total_ref[...] = jnp.zeros_like(total_ref)

    add_branch(heads, mixed_ref[0], w_ref, padded_ref, total_ref)

    @pl.when(step == pl.num_programs(0) - 1)
    def _():
        result = (residual_ref[...].astype(F32) + total_ref[...]).astype(BF16)
        row = lax.broadcasted_iota(jnp.int32, result.shape, 0)
        out_ref[...] = jnp.where(row < live_ref[0], result, jnp.zeros_like(result))


def whole(shape):
    return pl.BlockSpec(shape, lambda g: (0,) * len(shape))


def each(shape):
    return pl.BlockSpec((1,) + shape, lambda g: (g,) + (0,) * len(shape))


SMEM = pl.BlockSpec(memory_space=pltpu.SMEM)


def call(kernel, groups, in_specs, out_specs, out_shape, scratch, flops, moved, name):
    return pl.pallas_call(
        kernel,
        grid=(groups,),
        in_specs=in_specs,
        out_specs=out_specs,
        out_shape=out_shape,
        scratch_shapes=scratch,
        compiler_params=pltpu.CompilerParams(
            dimension_semantics=("arbitrary",), vmem_limit_bytes=VMEM
        ),
        cost_estimate=pl.CostEstimate(flops=flops, bytes_accessed=moved, transcendentals=0),
        name=name,
    )


def from_all_planes(piece):
    names = ("tensor", "dp", "seq")
    gathered = lax.all_gather(piece, names)
    return gathered.reshape(tuple(lax.axis_size(n) for n in names) + piece.shape)


def earlier_blocks(state, axis):
    peers = lax.axis_size(axis)
    if peers <= 4:
        return [
            lax.ppermute(state, axis, [(i, i + by) for i in range(peers - by)])
            for by in range(1, peers)
        ]
    everything = lax.all_gather(state, axis).astype(F32)
    reached = jnp.arange(peers) < lax.axis_index(axis)
    return [jnp.sum(jnp.where(reached[:, None, None, None], everything, 0.0), axis=0)]


def on_device(
    pool,
    page_table,
    reassign,
    lengths,
    gain_one,
    w_featmap,
    w_value,
    w_out_one,
    gain_two,
    w_window,
    conv_window,
    w_out_two,
):
    dp_count, seq_count, group_count = (lax.axis_size(n) for n in ("dp", "seq", "tensor"))
    groups = dp_count * seq_count
    device_place = lax.axis_index(("dp", "seq"))
    dp_place, seq_place, tensor_place = (lax.axis_index(n) for n in ("dp", "seq", "tensor"))
    pages_dev, page_share, width = pool.shape
    slots_total, pages_total = page_table.shape
    req_dev = slots_total // dp_count
    page_span = pages_total // seq_count
    page_rows = page_share * group_count
    rows = page_span * page_rows
    assert req_dev == group_count
    heads = w_value.shape[1] // HEAD
    head_cols = heads * HEAD
    feat_cols = w_featmap.shape[2]
    feature_dim = feat_cols // heads
    tap_count = conv_window.shape[0]

    plane_rows = width // groups
    row_at = device_place * plane_rows
    out_rows, out_cols = head_cols // seq_count, width // dp_count

    def row_piece(w):
        return lax.dynamic_slice_in_dim(w, row_at, plane_rows).reshape(plane_rows, -1)

    def out_piece(w):
        return lax.dynamic_slice(w, (seq_place * out_rows, dp_place * out_cols), (out_rows, out_cols))

    piece_one = jnp.concatenate([row_piece(w_featmap), row_piece(w_value)], axis=1)
    all_one = from_all_planes(piece_one).reshape(group_count, width, -1)
    all_out_one = from_all_planes(out_piece(w_out_one)).reshape(
        group_count, dp_count, head_cols, out_cols
    )
    all_window = from_all_planes(row_piece(w_window)).reshape(group_count, width, -1)
    all_out_two = from_all_planes(out_piece(w_out_two)).reshape(
        group_count, dp_count, head_cols, out_cols
    )
    all_taps = lax.all_gather(conv_window.reshape(tap_count, 3 * head_cols), "tensor")

    placed = reassign[:, None] == jnp.arange(slots_total, dtype=jnp.int32)[None, :]
    table = jnp.sum(jnp.where(placed[:, :, None], page_table[None], 0), axis=1)
    slot_lengths = jnp.sum(jnp.where(placed, lengths[None, :], 0), axis=1)
    source_page = (
        table.reshape(dp_count, req_dev, seq_count, page_span)
        .transpose(0, 2, 1, 3)
        .reshape(groups, req_dev * page_span)
    )
    capacity = (pages_dev + groups - 1) // groups
    page_owner = source_page // pages_dev
    pool_slot = source_page % pages_dev
    before = jnp.arange(pages_dev)[None, :] < jnp.arange(pages_dev)[:, None]
    pair_rank = jnp.sum((page_owner[:, :, None] == page_owner[:, None, :]) & before[None], axis=2)
    send_hit = (page_owner == device_place)[:, None, :] & (
        pair_rank[:, None, :] == jnp.arange(capacity)[None, :, None]
    )
    send_slot = jnp.sum(jnp.where(send_hit, pool_slot[:, None, :], 0), axis=2)
    outgoing = pool.at[send_slot.reshape(-1)].get(mode="promise_in_bounds")
    outgoing = outgoing.reshape(groups, capacity, page_share, width)
    arrived = lax.all_to_all(outgoing, ("dp", "seq"), split_axis=0, concat_axis=0, tiled=True)
    own_row = jnp.arange(groups)[:, None] == device_place
    pick_rows = jnp.sum(jnp.where(own_row, page_owner * capacity + pair_rank, 0), axis=0)
    picked = arrived.reshape(groups * capacity, page_share, width)
    picked = picked.at[pick_rows].get(mode="promise_in_bounds")

    picked = picked.reshape(req_dev, page_span, page_share, width)
    swapped = lax.all_to_all(picked, "tensor", split_axis=0, concat_axis=0, tiled=True)
    tokens = swapped.transpose(1, 0, 2, 3).reshape(rows, width)
    slot = dp_place * req_dev + tensor_place
    length = jnp.sum(jnp.where(jnp.arange(slots_total) == slot, slot_lengths, 0))

    first, second, ones, scale, kept = feature_tables(heads, feature_dim)
    first, second = jnp.asarray(first, BF16), jnp.asarray(second, BF16)
    spread, column = spread_table(heads)
    spread = jnp.asarray(spread, BF16)
    one_cols = 2 * feat_cols + head_cols
    slots = heads * SLOT
    num, queries, state = call(
        functools.partial(linear_kernel, heads, feature_dim, kept),
        group_count,
        [
            whole((rows, width)),
            whole((1, width)),
            each((width, one_cols)),
            whole(first.shape),
            whole(second.shape),
            whole(ones.shape),
            whole(spread.shape),
            whole(column.shape),
        ],
        [each((rows, slots)), each((rows, feat_cols)), each((heads * kept, SLOT))],
        [
            jax.ShapeDtypeStruct((group_count, rows, slots), F32),
            jax.ShapeDtypeStruct((group_count, rows, feat_cols), BF16),
            jax.ShapeDtypeStruct((group_count, heads * kept, SLOT), BF16),
        ],
        [pltpu.VMEM((rows, width), BF16)],
        3 * group_count * rows * width * one_cols,
        group_count * width * one_cols * 2,
        "linear_rows",
    )(tokens, gain_one[None], all_one, first, second, ones, spread, column)
    priors = earlier_blocks(state, "seq")
    residual, normed_two = call(
        functools.partial(out_one_kernel, heads, kept, len(priors)),
        group_count,
        [
            each((rows, slots)),
            each((rows, feat_cols)),
            whole(first.shape),
            whole(second.shape),
            whole(ones.shape),
            whole(scale.shape),
        ]
        + [each((heads * kept, SLOT))] * len(priors)
        + [
            each((dp_count, head_cols, out_cols)),
            whole((rows, width)),
            whole((1, width)),
        ],
        [whole((rows, width)), whole((rows, width))],
        [jax.ShapeDtypeStruct((rows, width), BF16)] * 2,
        [
            pltpu.VMEM((rows, width), F32),
            pltpu.VMEM((slots, out_cols), BF16),
            pltpu.VMEM((rows, slots), BF16),
        ],
        3 * group_count * rows * width * head_cols,
        group_count * width * head_cols * 2,
        "linear_out",
    )(num, queries, first, second, ones, scale, *priors, all_out_one, tokens, gain_two[None])

    halo = lax.ppermute(
        normed_two[rows - HALO :], "seq", [(i, i + 1) for i in range(seq_count - 1)]
    )
    block_start = (seq_place * rows).astype(jnp.int32)[None]
    mixed_two = call(
        functools.partial(window_kernel, heads),
        group_count,
        [
            SMEM,
            whole((rows, width)),
            whole((HALO, width)),
            each((width, 3 * head_cols)),
            each((tap_count, 3 * head_cols)),
        ],
        each((rows, slots)),
        jax.ShapeDtypeStruct((group_count, rows, slots), BF16),
        [pltpu.VMEM((HALO + rows, width), BF16)],
        3 * group_count * rows * width * 3 * head_cols,
        group_count * width * 3 * head_cols * 2,
        "window_rows",
    )(block_start, normed_two, halo, all_window, all_taps)
    live = (length - seq_place * rows).astype(jnp.int32)[None]
    result = call(
        functools.partial(out_two_kernel, heads),
        group_count,
        [
            SMEM,
            each((rows, slots)),
            each((dp_count, head_cols, out_cols)),
            whole((rows, width)),
        ],
        whole((rows, width)),
        jax.ShapeDtypeStruct((rows, width), BF16),
        [pltpu.VMEM((rows, width), F32), pltpu.VMEM((slots, out_cols), BF16)],
        2 * group_count * rows * width * head_cols,
        group_count * width * head_cols * 2,
        "window_out",
    )(live, mixed_two, all_out_two, residual)

    result = result.reshape(page_span, group_count, page_share, width).transpose(1, 0, 2, 3)
    return lax.all_to_all(result, "tensor", split_axis=0, concat_axis=0, tiled=True)


def solution(mesh):
    return jax.shard_map(
        on_device,
        mesh=mesh,
        in_specs=(
            P(("dp", "seq"), "tensor", None),
            P(),
            P(),
            P(),
            P(),
            P(None, None, "tensor"),
            P(None, "tensor"),
            P("tensor", None),
            P(),
            P(None, None, "tensor"),
            P(None, None, "tensor"),
            P("tensor", None),
        ),
        out_specs=P("dp", "seq", "tensor", None),
        check_vma=False,
    )
```

time: 523 us -> 426 us (0.81)
  waiting for transfers between devices: 343 us -> 274 us
  matrix products: 53.4 us -> 0 us
  Pallas kernels: 0 us -> 50.7 us
  other arithmetic: 44.1 us -> 2.44 us
  blocking collectives: 8.97 us -> 40.8 us
  local copies, waits for them, and re-layouts: 44.5 us -> 21.8 us
  starting transfers between devices: 9.17 us -> 21.6 us
    reduce_scatter x2 -> x0, waiting for transfers between devices: 136 us -> none  [head_sum(): lax.psum_scatter(partial_value.astype(jnp.bfloat16), 'tensor', scatter_di...]
    pallas_call x0 -> x4, Pallas kernels: none -> 50.7 us  [the longest x1 22.4 us: on_device(): call(functools.partial(window_kernel, heads), group_count, [SMEM, whole((...]
    dot_general x10 -> x0, matrix products: 48.1 us -> none  [the longest x2 14 us: project_rows(): jnp.dot(lax.all_gather(normed, 'tensor', axis=2, tiled=True), weight, pre...]
    all_gather x3 -> x4, waiting for transfers between devices: 178 us -> 220 us  [from_all_planes(): gathered = lax.all_gather(piece, names)]
    all_to_all x0 -> x1, waiting for transfers between devices: none -> 40.6 us  [on_device(): lax.all_to_all(picked, 'tensor', split_axis=0, concat_axis=0, tiled=True)]
    all_to_all x0 -> x1, blocking collectives: none -> 26.2 us  [on_device(): lax.all_to_all(result, 'tensor', split_axis=0, concat_axis=0, tiled=True)]
    convert_element_type x7 -> x0, other arithmetic: 15.7 us -> none  [the longest x1 11.3 us: on_device(): convolved = convolved.astype(jnp.bfloat16)]
    ppermute x1 -> x4, waiting for transfers between devices: 15.4 us -> 0.01 us  [the longest x3 0.01 us: earlier_blocks(): lax.ppermute(state, axis, [(i, i + by) for i in range(peers - by)])]
  transfers between devices with their start and end apart: 7 -> 10, of which waited for: 7 -> 6; matrix products, arithmetic and copies ran while one was open for 2% -> 4% of each run, Pallas kernels for 0% -> 10%
where the time goes in v1:
time: 426 us; the launch traced here: 425 us
  waiting for transfers between devices  274 us (64%)
  Pallas kernels  50.7 us (12%)
  blocking collectives  40.8 us (10%)
  local copies, waits for them, and re-layouts  21.8 us (5%)
  starting transfers between devices  21.6 us (5%)
  between operations  14 us (3%)
    all_gather x4, waiting for transfers between devices, from_all_planes(): gathered = lax.all_gather(piece, names)  220 us
    all_to_all x1, waiting for transfers between devices, on_device(): lax.all_to_all(picked, 'tensor', split_axis=0, concat_axis=0, tiled=True)  40.6 us
    all_to_all x1, blocking collectives, on_device(): lax.all_to_all(result, 'tensor', split_axis=0, concat_axis=0, tiled=True)  26.2 us
    pallas_call x1, Pallas kernels, on_device(): call(functools.partial(window_kernel, heads), group_count, [SMEM, whole((...  22.4 us
    all_gather x1, blocking collectives, on_device(): lax.all_gather(conv_window.reshape(tap_count, 3 * head_cols), 'tensor')  14.5 us
    all_to_all x1, waiting for transfers between devices, on_device(): lax.all_to_all(outgoing, ('dp', 'seq'), split_axis=0, concat_axis=0, tile...  13.2 us
    pallas_call x1, Pallas kernels, on_device(): call(functools.partial(linear_kernel, heads, feature_dim, kept), group_co...  11.5 us
    pallas_call x1, Pallas kernels, on_device(): call(functools.partial(out_one_kernel, heads, kept, len(priors)), group_c...  9.86 us
  transfers between devices with their start and end apart: 10, of which 6 were waited for; matrix products, arithmetic and copies ran while one was open for 4% of the time, Pallas kernels for 10%

profile of v1, /device:TPU:0, one launch (start us, length us, event | category | flops | bytes accessed | tf_op | source)
XLA Modules:
  0.0 425.0 jit_solution(3735667854487418858)
XLA Ops:
  6.5 0.0 all-gather.10.cloned.1.call-start
  6.6 1.4 copy-done
  8.0 0.1 constant_dynamic-slice_fusion
  8.1 0.1 copy.61
  8.2 1.0 constant_dynamic-slice_fusion.1
  9.2 0.1 copy.56
  9.3 0.7 pad_maximum_fusion
  10.1 0.0 all-gather.10.cloned.1.call-update
  10.1 0.0 all-gather.12.cloned.1.call-start
  10.2 1.6 dynamic_slice.17
  11.8 0.0 all-gather.12.cloned.1.call-update
  11.8 0.0 all-gather.8.cloned.1.call-start
  11.9 1.5 constant_dynamic-slice_fusion.2
  13.4 1.1 copy.57
  14.5 0.0 all-gather.8.cloned.1.call-update
  14.5 0.0 all-gather.14.cloned.1.call-start
  14.6 1.6 dynamic_slice.19
  16.2 0.0 all-gather.14.cloned.1.call-update
  16.2 0.1 iota_compare_fusion.2
  16.3 0.1 select_reduce_fusion.1
  16.4 0.1 reshape.218
  16.5 0.1 reshape.219
  16.6 0.3 convert_reduce_fusion
  16.9 0.2 select_reduce_fusion
  17.2 0.1 reshape.220
  17.3 2.2 gather_fusion
  19.5 5.2 %all-to-all-start = ((bf16[8,8,4,1792]{3,2,1,0:T(4,128)(2,1)}), bf16[8,8,4,1792]{3,2,1,0:T(4,128)(2,1)S(1)}, u32[]{:S(2)}, u32[]{:S(2)}) async-start(bf16[8,8,4,1792]{3,2,1,0:T(4,128)(2,1)} %bitcast.4), calls=%async_computation | async-start | bytes 1835008 | tf_op jit(solution)/shard_map/all_to_all | solution.py:338
  24.7 0.1 reduce_sum.63
  24.7 0.1 fusion.5
  24.8 0.1 reduce_sum.65
  24.9 13.2 %all-to-all-done = bf16[8,8,4,1792]{3,2,1,0:T(4,128)(2,1)S(1)} async-done(((bf16[8,8,4,1792]{3,2,1,0:T(4,128)(2,1)}), bf16[8,8,4,1792]{3,2,1,0:T(4,128)(2,1)S(1)}, u32[]{:S(2)}, u32[]{:S(2)}) %all-to-all-start) | async-done | bytes 917536 | tf_op jit(solution)/shard_map/all_to_all | solution.py:338
  38.1 1.3 gather_fusion.1
  39.5 1.0 copy.53
  40.5 4.9 %all-to-all-start.1 = ((bf16[4,16,4,1792]{3,1,2,0:T(8,128)(2,1)}), bf16[4,16,4,1792]{3,1,2,0:T(8,128)(2,1)S(1)}, u32[]{:S(2)}, u32[]{:S(2)}) async-start(bf16[4,16,4,1792]{3,1,2,0:T(8,128)(2,1)} %copy.53), calls=%async_computation.1 | async-start | bytes 1835008 | tf_op jit(solution)/shard_map/all_to_all | solution.py:345
  45.4 0.6 broadcast_in_dim.95.gain_ref
  46.0 40.6 %all-to-all-done.1 = bf16[4,16,4,1792]{3,1,2,0:T(8,128)(2,1)S(1)} async-done(((bf16[4,16,4,1792]{3,1,2,0:T(8,128)(2,1)}), bf16[4,16,4,1792]{3,1,2,0:T(8,128)(2,1)S(1)}, u32[]{:S(2)}, u32[]{:S(2)}) %all-to-all-start.1) | async-done | bytes 917536 | tf_op jit(solution)/shard_map/all_to_all | solution.py:345
  86.6 0.5 copy.54
  87.1 1.1 reshape.224.x_ref.refs_10_
  88.2 13.9 %all-gather.10.cloned.1.call-done = bf16[7168,576]{1,0:T(8,128)(2,1)} async-done(((bf16[224,576]{1,0:T(8,128)(2,1)}), bf16[7168,576]{1,0:T(8,128)(2,1)}) %all-gather.10.cloned.1.call-update) | async-done | bytes 8257552 | tf_op jit(solution)/shard_map/all_gather | solution.py:251
  102.2 11.5 %linear_rows.1 = (f32[4,256,512]{2,1,0:T(8,128)}, bf16[4,256,64]{2,1,0:T(8,128)(2,1)}, bf16[4,640,128]{2,1,0:T(8,128)(2,1)}) custom-call(bf16[256,1792]{1,0:T(8,128)(2,1)} %reshape.224.x_ref.refs_10_, f32[1,1792]{1,0:T(1,128)} %broadcast_in_dim.95.gain_ref, bf16[4,1792,576]{2,1,0:T(8,128)(2,1)} %bitcast.31, ...), custom_call_target="tpu_custom_call" | custom-call | flops 3170893824 | bytes 8257536 | tf_op jit(solution)/shard_map/linear_rows/pallas_call | solution.py:356
  113.6 3.4 collective-permute-start
  117.0 3.3 collective-permute-start.1
  120.3 1.3 collective-permute-start.2
  121.7 0.6 broadcast_in_dim.96.refs_11_
  122.3 55.2 %all-gather.12.cloned.1.call-done = bf16[3584,896]{1,0:T(8,128)(2,1)} async-done(((bf16[112,896]{1,0:T(8,128)(2,1)}), bf16[3584,896]{1,0:T(8,128)(2,1)}) %all-gather.12.cloned.1.call-update) | async-done | bytes 6422544 | tf_op jit(solution)/shard_map/all_gather | solution.py:251
  177.5 0.0 collective-permute-done.2.refs_8_
  177.5 0.8 copy-done.3
  178.3 0.2 copy-done.4
  178.5 0.2 copy-done.5
  178.7 9.9 %linear_out.1 = (bf16[256,1792]{1,0:T(8,128)(2,1)}, bf16[256,1792]{1,0:T(8,128)(2,1)}) custom-call(f32[4,256,512]{2,1,0:T(8,128)} %get-tuple-element.10.refs_0_, bf16[4,256,64]{2,1,0:T(8,128)(2,1)} %get-tuple-element.11.refs_1_, bf16[64,1024]{1,0:T(8,128)(2,1)} %constant.73.clone.first_ref.refs_2_, bf16[64,1024]{1,0:T(8,128)(2,1)} %constant.74.clone.second_ref.refs_3_, ...), custom_call_target="tpu_custom_call" | custom-call | flops 2466250752 | bytes 6422528 | tf_op jit(solution)/shard_map/linear_out/pallas_call | solution.py:381
  188.6 1.0 slice.3
  189.6 3.4 collective-permute-start.3
  193.0 0.1 all_gather_reshape.7
  193.1 0.2 select_reduce_fusion.2
  193.2 0.6 fusion.9
  194.5 14.5 %all_gather.29.tap_ref = f32[4,3,1344]{2,1,0:T(4,128)} all-gather(f32[1,3,1344]{2,1,0:T(4,128)S(1)} %all_gather_reshape.7), channel_id=1, replica_groups=mesh['dp'=2,'seq'=4,'tensor'=4] {'tensor'}, dimensions={0}, use_global_device_ids=true | all-gather | bytes 80640 | tf_op jit(solution)/shard_map/all_gather | solution.py:317
  209.0 102.0 %all-gather.8.cloned.1.call-done = bf16[32,224,1344]{2,1,0:T(8,128)(2,1)} async-done(((bf16[1,224,1344]{2,1,0:T(8,128)(2,1)}), bf16[32,224,1344]{2,1,0:T(8,128)(2,1)}) %all-gather.8.cloned.1.call-update) | async-done | bytes 19267600 | tf_op jit(solution)/shard_map/all_gather | solution.py:251
  311.1 22.4 %window_rows.1.mixed_ref = bf16[4,256,512]{2,1,0:T(8,128)(2,1)} custom-call(s32[1]{0:T(128)} %bitcast.1.first_ref, bf16[256,1792]{1,0:T(8,128)(2,1)} %get-tuple-element.13.x_ref, bf16[80,1792]{1,0:T(8,128)(2,1)} %copy-done.10, bf16[4,1792,1344]{2,1,0:T(8,128)(2,1)} %bitcast.30, f32[4,3,1344]{2,1,0:T(4,128)} %all_gather.29.tap_ref), custom_call_target="tpu_custom_call" | custom-call | flops 7398752256 | bytes 19267584 | tf_op jit(solution)/shard_map/window_rows/pallas_call | solution.py:414
  333.4 48.7 %all-gather.14.cloned.1.call-done = bf16[3584,896]{1,0:T(8,128)(2,1)} async-done(((bf16[112,896]{1,0:T(8,128)(2,1)}), bf16[3584,896]{1,0:T(8,128)(2,1)}) %all-gather.14.cloned.1.call-update) | async-done | bytes 6422544 | tf_op jit(solution)/shard_map/all_gather | solution.py:251
  382.2 7.0 %window_out.1 = bf16[256,1792]{1,0:T(8,128)(2,1)} custom-call(s32[1]{0:T(128)} %bitcast.live_ref, bf16[4,256,512]{2,1,0:T(8,128)(2,1)} %window_rows.1.mixed_ref, bf16[4,2,448,896]{3,2,1,0:T(8,128)(2,1)} %bitcast.21, bf16[256,1792]{1,0:T(8,128)(2,1)} %get-tuple-element.14.residual_ref), custom_call_target="tpu_custom_call" | custom-call | flops 1644167168 | bytes 6422528 | tf_op jit(solution)/shard_map/window_out/pallas_call | solution.py:432
  389.2 1.8 reshape.226
  391.0 0.3 copy.66
  391.3 26.2 %all_to_all.15 = bf16[4,16,4,1792]{3,2,1,0:T(4,128)(2,1)S(1)} all-to-all(bf16[4,16,4,1792]{3,2,1,0:T(4,128)(2,1)S(1)} %bitcast.24), channel_id=1, replica_groups=mesh['dp'=2,'seq'=4,'tensor'=4] {'tensor'}, dimensions={0} | all-to-all | bytes 1835008 | tf_op jit(solution)/shard_map/all_to_all | solution.py:450
  417.5 0.9 copy.68
  (34 shorter events, 0.1 us)
Async XLA Ops:
  6.5 1.4 copy-start
  6.5 9.7 %copy-start.12 = (s32[8]{0:T(128)S(1)}, s32[8]{0:T(128)}, u32[]{:S(2)}) copy-start(s32[8]{0:T(128)} %param.20) | copy-start | bytes 100
  6.5 9.8 %copy-start.9 = (s32[8,64]{1,0:T(8,128)S(1)}, s32[8,64]{1,0:T(8,128)}, u32[]{:S(2)}) copy-start(s32[8,64]{1,0:T(8,128)} %param.19) | copy-start | bytes 6148
  6.5 10.7 %copy-start.2 = (bf16[64,4,1792]{2,1,0:T(4,128)(2,1)S(1)}, bf16[64,4,1792]{2,1,0:T(4,128)(2,1)}, u32[]{:S(2)}) copy-start(bf16[64,4,1792]{2,1,0:T(4,128)(2,1)} %param.18) | copy-start | bytes 2752516
  6.5 95.6 %all-gather.10.cloned.1.call-start = ((), (), s32[]{:S(2)}) async-start(), calls=%async_computation.4 | async-start | bytes 9461760 | tf_op jit(solution)/shard_map/all_gather | solution.py:251
  10.1 167.3 %all-gather.12.cloned.1.call-start = ((), (), s32[]{:S(2)}) async-start(), calls=%async_computation.5 | async-start | bytes 6623232 | tf_op jit(solution)/shard_map/all_gather | solution.py:251
  11.8 299.2 %all-gather.8.cloned.1.call-start = ((), (), s32[]{:S(2)}) async-start(), calls=%async_computation.3 | async-start | bytes 20815872 | tf_op jit(solution)/shard_map/all_gather | solution.py:251
  14.5 367.6 %all-gather.14.cloned.1.call-start = ((), (), s32[]{:S(2)}) async-start(), calls=%async_computation.6 | async-start | bytes 6623232 | tf_op jit(solution)/shard_map/all_gather | solution.py:251
  16.2 29.2 %copy-start.7 = (f32[1792]{0:T(1024)S(1)}, f32[1792]{0:T(1024)}, u32[]{:S(2)}) copy-start(f32[1792]{0:T(1024)} %param.22) | copy-start | bytes 21508
  19.5 18.7 %all-to-all-start = ((bf16[8,8,4,1792]{3,2,1,0:T(4,128)(2,1)}), bf16[8,8,4,1792]{3,2,1,0:T(4,128)(2,1)S(1)}, u32[]{:S(2)}, u32[]{:S(2)}) async-start(bf16[8,8,4,1792]{3,2,1,0:T(4,128)(2,1)} %bitcast.4), calls=%async_computation | async-start | bytes 1835008 | tf_op jit(solution)/shard_map/all_to_all | solution.py:338
  40.5 46.1 %all-to-all-start.1 = ((bf16[4,16,4,1792]{3,1,2,0:T(8,128)(2,1)}), bf16[4,16,4,1792]{3,1,2,0:T(8,128)(2,1)S(1)}, u32[]{:S(2)}, u32[]{:S(2)}) async-start(bf16[4,16,4,1792]{3,1,2,0:T(8,128)(2,1)} %copy.53), calls=%async_computation.1 | async-start | bytes 1835008 | tf_op jit(solution)/shard_map/all_to_all | solution.py:345
  102.2 19.5 %copy-start.8 = (f32[1792]{0:T(1024)S(1)}, f32[1792]{0:T(1024)}, u32[]{:S(2)}) copy-start(f32[1792]{0:T(1024)} %param.26) | copy-start | bytes 21508
  113.6 63.8 %collective-permute-start = (bf16[4,640,128]{2,1,0:T(8,128)(2,1)}, bf16[4,640,128]{2,1,0:T(8,128)(2,1)S(1)}, u32[]{:S(2)}, u32[]{:S(2)}) collective-permute-start(bf16[4,640,128]{2,1,0:T(8,128)(2,1)} %get-tuple-element.12), channel_id=1, source_target_pairs={{0,4},{4,8},{8,12},{1,5},{5,9},{9,13},{2,6},{6,10},{10,14},{3,7},{... | collective-permute-start | bytes 1966088 | tf_op jit(solution)/shard_map/ppermute | solution.py:259
  117.0 60.5 %collective-permute-start.1 = (bf16[4,640,128]{2,1,0:T(8,128)(2,1)}, bf16[4,640,128]{2,1,0:T(8,128)(2,1)S(1)}, u32[]{:S(2)}, u32[]{:S(2)}) collective-permute-start(bf16[4,640,128]{2,1,0:T(8,128)(2,1)} %get-tuple-element.12), channel_id=1, source_target_pairs={{0,8},{4,12},{1,9},{5,13},{2,10},{6,14},{3,11},{7,15},{16,24},{20,... | collective-permute-start | bytes 1966088 | tf_op jit(solution)/shard_map/ppermute | solution.py:259
  120.3 57.2 %collective-permute-start.2 = (bf16[4,640,128]{2,1,0:T(8,128)(2,1)}, bf16[4,640,128]{2,1,0:T(8,128)(2,1)S(1)}, u32[]{:S(2)}, u32[]{:S(2)}) collective-permute-start(bf16[4,640,128]{2,1,0:T(8,128)(2,1)} %get-tuple-element.12), channel_id=1, source_target_pairs={{0,12},{1,13},{2,14},{3,15},{16,28},{17,29},{18,30},{19,31}} | collective-permute-start | bytes 1966088 | tf_op jit(solution)/shard_map/ppermute | solution.py:259
  177.4 0.8 copy-start.3
  177.5 1.1 copy-start.4
  177.5 1.2 copy-start.5
  178.7 14.2 %copy-start.6 = (f32[3,3,448]{2,1,0:T(4,128)S(1)}, f32[3,3,448]{2,1,0:T(4,128)}, u32[]{:S(2)}) copy-start(f32[3,3,448]{2,1,0:T(4,128)} %param.28) | copy-start | bytes 48388
  178.7 14.3 %copy-start.11 = (s32[8]{0:T(128)S(1)}, s32[8]{0:T(128)}, u32[]{:S(2)}) copy-start(s32[8]{0:T(128)} %param.21) | copy-start | bytes 100
  189.6 19.5 %collective-permute-start.3 = (bf16[80,1792]{1,0:T(8,128)(2,1)S(1)}, bf16[80,1792]{1,0:T(8,128)(2,1)S(1)}, u32[]{:S(2)}, u32[]{:S(2)}) collective-permute-start(bf16[80,1792]{1,0:T(8,128)(2,1)S(1)} %slice.3), channel_id=1, source_target_pairs={{0,4},{4,8},{8,12},{1,5},{5,9},{9,13},{2,6},{6,10},{10,14},{3,7},{... | collective-permute-start | bytes 860168 | tf_op jit(solution)/shard_map/ppermute | solution.py:410
  209.0 102.0 %copy-start.10 = (bf16[80,1792]{1,0:T(8,128)(2,1)}, bf16[80,1792]{1,0:T(8,128)(2,1)S(1)}, u32[]{:S(2)}) copy-start(bf16[80,1792]{1,0:T(8,128)(2,1)S(1)} %collective-permute-done.3.halo_ref) | copy-start | bytes 860164
  382.2 36.3 %copy-start.1 = (bf16[1792,448]{0,1:T(8,128)(2,1)S(1)}, bf16[1792,448]{0,1:T(8,128)(2,1)}, u32[]{:S(2)}) copy-start(bf16[1792,448]{0,1:T(8,128)(2,1)} %param.24) | copy-start | bytes 4816900
Sparse Core Ops, SparseCore 0:
  10.2 91.8 all-gather.9
  105.0 72.4 all-gather.11
  180.3 130.7 all-gather.7
  313.7 68.3 all-gather.13

commit v2 on v1

--- a/solution.py
+++ b/solution.py
@@ -14,6 +14,7 @@
 SLOT = 128
 FEAT_SLOT = 256
 HALO = 80
+NEAR = 4
 VMEM = 60 * 1024 * 1024
 F32 = jnp.float32
 BF16 = jnp.bfloat16
@@ -31,7 +32,7 @@
 def feature_tables(heads, feature_dim):
     pairs = [(i, j) for i in range(feature_dim) for j in range(i, feature_dim)]
     pairs += [(i, -1) for i in range(feature_dim)] + [(-1, -1)]
-    first = np.zeros((heads * feature_dim, heads * FEAT_SLOT), np.float32)
+    first = np.zeros((2 * heads * feature_dim, heads * FEAT_SLOT), np.float32)
     second = np.zeros_like(first)
     ones = np.zeros((2, heads * FEAT_SLOT), np.float32)
     scale = np.zeros((1, heads * FEAT_SLOT), np.float32)
@@ -39,11 +40,11 @@
         for n, (i, j) in enumerate(pairs):
             at = h * FEAT_SLOT + n
             if i >= 0:
-                first[h * feature_dim + i, at] = 1
+                first[2 * h * feature_dim + i, at] = 1
             else:
                 ones[0, at] = 1
             if j >= 0:
-                second[h * feature_dim + j, at] = 1
+                second[2 * h * feature_dim + j, at] = 1
             else:
                 ones[1, at] = 1
             if i < 0:
@@ -55,55 +56,132 @@
     return first, second, ones, scale, -(-len(pairs) // 16) * 16
 
 
-def spread_table(heads):
-    spread = np.zeros((heads * HEAD, heads * SLOT), np.float32)
-    ones = np.zeros((1, heads * SLOT), np.float32)
-    for h in range(heads):
-        spread[h * HEAD : (h + 1) * HEAD, h * SLOT : h * SLOT + HEAD] = np.eye(HEAD)
-        ones[0, h * SLOT + HEAD] = 1
-    return spread, ones
-
-
 def features(rows, first, second, ones):
     return (dot(rows, first) + ones[0:1]) * (dot(rows, second) + ones[1:2])
+
+
+def run_copies(copies_of, groups, meanwhile=None):
+    step = pl.program_id(0)
+
+    @pl.when(step == 0)
+    def _():
+        for group in range(groups):
+            for copy in copies_of(group):
+                copy.start()
+        if meanwhile is not None:
+            meanwhile()
+
+    for group in range(groups):
+
+        @pl.when(step == group)
+        def _(group=group):
+            for copy in copies_of(group):
+                copy.wait()
+
+
+def weight_copies(place_ref, near_ref, far_ref, targets, sems, group):
+    near = near_ref.shape[0]
+    cols = near_ref.shape[3]
+    found = []
+    for n in range(2 * near):
+        at = 0
+        for own_ref, kind, rows, w_ref, off in targets:
+            if group == 0:
+                part, head = n // near, n % near
+                src = own_ref.at[
+                    kind, head * rows : (head + 1) * rows, part * cols : (part + 1) * cols
+                ]
+            else:
+                part, head = place_ref[near], place_ref[n % near]
+                if n >= near:
+                    part = 1 - part
+                src = (near_ref if n < near else far_ref).at[
+                    n % near, group - 1, at : at + rows, :
+                ]
+            dst = w_ref.at[group, part, head, off : off + rows, :]
+            found.append(pltpu.make_async_copy(src, dst, sems.at[group, len(found)]))
+            at += rows
+    return found
+
+
+def zero_between_heads(w_ref):
+    groups, parts, heads, rows, cols = w_ref.shape
+    for at in range(HEAD, rows, SLOT):
+        w_ref[:, :, :, at : at + SLOT - HEAD, :] = jnp.zeros(
+            (groups, parts, heads, SLOT - HEAD, cols), BF16
+        )
+
+
+def group_weights(w_ref, step, part):
+    heads, rows, cols = w_ref.shape[2:]
+    return w_ref[step, part].reshape(heads * rows, cols)
+
+
+def project(rows_ref, w_ref, step):
+    parts, cols = w_ref.shape[1], w_ref.shape[4]
+    total = None
+    for part in range(parts):
+        rows = rows_ref[:, part * cols : (part + 1) * cols]
+        share = dot(rows, group_weights(w_ref, step, part), ((1,), (1,)))
+        total = share if total is None else total + share
+    return total
 
 
 def linear_kernel(
     heads,
     feature_dim,
     kept,
+    place_ref,
     x_ref,
     gain_ref,
-    w_ref,
+    value_ref,
+    featmap_ref,
+    near_ref,
+    far_ref,
     first_ref,
     second_ref,
     ones_ref,
-    spread_ref,
     column_ref,
     num_ref,
     q_ref,
     state_ref,
     normed_ref,
+    value_w_ref,
+    feat_w_ref,
+    sems,
 ):
-    @pl.when(pl.program_id(0) == 0)
+    step = pl.program_id(0)
+    targets = [
+        (value_ref, 0, HEAD, value_w_ref, 0),
+        (featmap_ref, 0, feature_dim, feat_w_ref, 0),
+        (featmap_ref, 1, feature_dim, feat_w_ref, feature_dim),
+    ]
+
+    @pl.when(step == 0)
     def _():
-        normed_ref[...] = normed_rows(x_ref[...].astype(F32), gain_ref[...])
-
+        zero_between_heads(value_w_ref)
+
+    run_copies(
+        functools.partial(weight_copies, place_ref, near_ref, far_ref, targets, sems),
+        value_w_ref.shape[0],
+        lambda: normed_ref.__setitem__(
+            ..., normed_rows(x_ref[...].astype(F32), gain_ref[...])
+        ),
+    )
     rows = x_ref.shape[0]
-    width = heads * feature_dim
-    projected = dot(normed_ref[...], w_ref[0]).astype(BF16)
-    queries = projected[:, :width]
-    keys = projected[:, width : 2 * width]
-    values = dot(projected[:, 2 * width :], spread_ref[...]) + column_ref[...]
-    values = values.astype(BF16)
+    width = 2 * heads * feature_dim
+    queries = project(normed_ref, feat_w_ref, step).astype(BF16)
+    keys = pltpu.roll(queries.astype(F32), width - feature_dim, 1).astype(BF16)
+    values = (project(normed_ref, value_w_ref, step) + column_ref[...]).astype(BF16)
     q_ref[0] = queries
-    lane_head = lax.broadcasted_iota(jnp.int32, (rows, width), 1) // feature_dim
+    lane = lax.broadcasted_iota(jnp.int32, (rows, width), 1)
     causal = lax.broadcasted_iota(jnp.int32, (rows, rows), 1) <= lax.broadcasted_iota(
         jnp.int32, (rows, rows), 0
     )
     key_features = features(keys, first_ref[...], second_ref[...], ones_ref[...]).astype(BF16)
     for h in range(heads):
-        own = jnp.where(lane_head == h, queries, jnp.zeros_like(queries))
+        at = 2 * h * feature_dim
+        own = jnp.where((lane >= at) & (lane < at + feature_dim), queries, jnp.zeros_like(queries))
         scores = dot(own, keys, ((1,), (1,))) * feature_dim**-0.5
         kernel = jnp.where(causal, 1.0 + scores + 0.5 * scores * scores, 0.0).astype(BF16)
         value = values[:, h * SLOT : (h + 1) * SLOT]
@@ -112,18 +190,11 @@
         state_ref[0, h * kept : (h + 1) * kept, :] = state.astype(BF16)
 
 
-def padded_heads(heads, w, padded_ref):
-    cols = w.shape[1]
-    for h in range(heads):
-        padded_ref[h * SLOT : h * SLOT + HEAD, :] = w[h * HEAD : (h + 1) * HEAD, :]
-        padded_ref[h * SLOT + HEAD : (h + 1) * SLOT, :] = jnp.zeros((SLOT - HEAD, cols), BF16)
-
-
-def add_branch(heads, mixed, w_ref, padded_ref, total_ref):
-    parts, cols = w_ref.shape[1], w_ref.shape[3]
+def add_branch(mixed, w_ref, total_ref):
+    step = pl.program_id(0)
+    parts, cols = w_ref.shape[1], w_ref.shape[4]
     for part in range(parts):
-        padded_heads(heads, w_ref[0, part], padded_ref)
-        share = dot(mixed, padded_ref[...]).astype(BF16).astype(F32)
+        share = dot(mixed, group_weights(w_ref, step, part)).astype(BF16).astype(F32)
         total_ref[:, part * cols : (part + 1) * cols] += share
 
 
@@ -133,16 +204,23 @@
     priors,
     *refs,
 ):
-    num_ref, q_ref, first_ref, second_ref, ones_ref, scale_ref = refs[:6]
-    prior_refs = refs[6 : 6 + priors]
-    w_ref, x_ref, gain_ref, residual_ref, normed_ref, total_ref, padded_ref, mixed_ref = refs[
-        6 + priors :
-    ]
+    place_ref, num_ref, q_ref, first_ref, second_ref, ones_ref, scale_ref = refs[:7]
+    prior_refs = refs[7 : 7 + priors]
+    own_ref, near_ref, far_ref, x_ref, gain_ref = refs[7 + priors : 12 + priors]
+    residual_ref, normed_ref, total_ref, mixed_ref, w_ref, sems = refs[12 + priors :]
     step = pl.program_id(0)
 
     @pl.when(step == 0)
     def _():
         total_ref[...] = jnp.zeros_like(total_ref)
+        zero_between_heads(w_ref)
+
+    run_copies(
+        functools.partial(
+            weight_copies, place_ref, near_ref, far_ref, [(own_ref, 0, HEAD, w_ref, 0)], sems
+        ),
+        w_ref.shape[0],
+    )
 
     query_features = features(q_ref[0], first_ref[...], second_ref[...], ones_ref[...])
     query_features = (query_features * scale_ref[...]).astype(BF16)
@@ -156,7 +234,7 @@
             query_features[:, h * FEAT_SLOT : h * FEAT_SLOT + kept], prior.astype(BF16)
         )
         mixed_ref[:, lanes] = (total / total[:, HEAD : HEAD + 1]).astype(BF16)
-    add_branch(heads, mixed_ref[...], w_ref, padded_ref, total_ref)
+    add_branch(mixed_ref[...], w_ref, total_ref)
 
     @pl.when(step == pl.num_programs(0) - 1)
     def _():
@@ -165,16 +243,40 @@
         normed_ref[...] = normed_rows(residual.astype(F32), gain_ref[...])
 
 
-def window_kernel(heads, first_ref, x_ref, halo_ref, w_ref, tap_ref, mixed_ref, rows_ref):
-    @pl.when(pl.program_id(0) == 0)
-    def _():
+def window_kernel(
+    heads,
+    place_ref,
+    first_ref,
+    x_ref,
+    halo_ref,
+    own_ref,
+    near_ref,
+    far_ref,
+    tap_ref,
+    mixed_ref,
+    rows_ref,
+    w_ref,
+    sems,
+):
+    step = pl.program_id(0)
+    targets = [(own_ref, kind, HEAD, w_ref, kind * SLOT) for kind in range(3)]
+
+    def place_rows():
         rows_ref[:HALO] = halo_ref[...]
         rows_ref[HALO:] = x_ref[...]
 
+    @pl.when(step == 0)
+    def _():
+        zero_between_heads(w_ref)
+
+    run_copies(
+        functools.partial(weight_copies, place_ref, near_ref, far_ref, targets, sems),
+        w_ref.shape[0],
+        place_rows,
+    )
     rows = x_ref.shape[0]
     lead = HALO - WINDOW
-    cols = heads * HEAD
-    projected = dot(rows_ref[...], w_ref[0])
+    projected = project(rows_ref, w_ref, step)
     taps = tap_ref[0]
     convolved = taps[0:1] * projected
     for offset in range(1, taps.shape[0]):
@@ -186,9 +288,10 @@
     col = lax.broadcasted_iota(jnp.int32, (tile, span), 1)
     band = (col > row) & (col <= row + WINDOW)
     for h in range(heads):
-        queries = convolved[WINDOW:, h * HEAD : (h + 1) * HEAD]
-        keys = convolved[:, cols + h * HEAD : cols + (h + 1) * HEAD]
-        values = convolved[:, 2 * cols + h * HEAD : 2 * cols + (h + 1) * HEAD]
+        at = 3 * h * SLOT
+        queries = convolved[WINDOW:, at : at + SLOT]
+        keys = convolved[:, at + SLOT : at + 2 * SLOT]
+        values = convolved[:, at + 2 * SLOT : at + 3 * SLOT]
         for start in range(0, rows, tile):
             logits = dot(queries[start : start + tile], keys[start : start + span], ((1,), (1,)))
             allowed = band
@@ -198,19 +301,36 @@
             weights = jnp.exp(logits - jnp.max(logits, axis=1, keepdims=True))
             weights = weights / jnp.sum(weights, axis=1, keepdims=True)
             mixed = dot(weights.astype(BF16), values[start : start + span])
-            mixed_ref[0, start : start + tile, h * SLOT : h * SLOT + HEAD] = mixed.astype(BF16)
-    for h in range(heads):
-        mixed_ref[0, :, h * SLOT + HEAD : (h + 1) * SLOT] = jnp.zeros((rows, SLOT - HEAD), BF16)
-
-
-def out_two_kernel(heads, live_ref, mixed_ref, w_ref, residual_ref, out_ref, total_ref, padded_ref):
+            mixed_ref[0, start : start + tile, h * SLOT : (h + 1) * SLOT] = mixed.astype(BF16)
+
+
+def out_two_kernel(
+    place_ref,
+    live_ref,
+    mixed_ref,
+    own_ref,
+    near_ref,
+    far_ref,
+    residual_ref,
+    out_ref,
+    total_ref,
+    w_ref,
+    sems,
+):
     step = pl.program_id(0)
 
     @pl.when(step == 0)
     def _():
         total_ref[...] = jnp.zeros_like(total_ref)
-
-    add_branch(heads, mixed_ref[0], w_ref, padded_ref, total_ref)
+        zero_between_heads(w_ref)
+
+    run_copies(
+        functools.partial(
+            weight_copies, place_ref, near_ref, far_ref, [(own_ref, 0, HEAD, w_ref, 0)], sems
+        ),
+        w_ref.shape[0],
+    )
+    add_branch(mixed_ref[0], w_ref, total_ref)
 
     @pl.when(step == pl.num_programs(0) - 1)
     def _():
@@ -228,6 +348,7 @@
 
 
 SMEM = pl.BlockSpec(memory_space=pltpu.SMEM)
+HBM = pl.BlockSpec(memory_space=pl.ANY)
 
 
 def call(kernel, groups, in_specs, out_specs, out_shape, scratch, flops, moved, name):
@@ -246,10 +367,34 @@
     )
 
 
-def from_all_planes(piece):
-    names = ("tensor", "dp", "seq")
-    gathered = lax.all_gather(piece, names)
-    return gathered.reshape(tuple(lax.axis_size(n) for n in names) + piece.shape)
+def own_piece(whole_weights):
+    head, part = lax.axis_index("seq") % NEAR, lax.axis_index("dp")
+    found = []
+    for weights in whole_weights:
+        kinds, rows, cols = weights.shape
+        rows, cols = rows // NEAR, cols // lax.axis_size("dp")
+        piece = lax.dynamic_slice(weights, (0, head * rows, part * cols), (kinds, rows, cols))
+        found.append(piece.reshape(kinds * rows, cols))
+    return jnp.concatenate(found, axis=0)
+
+
+def from_other_groups(piece, after):
+    groups, mine = lax.axis_size("tensor"), lax.axis_index("tensor")
+    order = (mine + 1 + after + jnp.arange(groups - 1)) % groups
+    held = lax.all_gather(piece, "tensor").at[order].get(mode="promise_in_bounds")
+
+    def across(array, bit):
+        return lax.ppermute(array, "seq", [(i, i ^ bit) for i in range(lax.axis_size("seq"))])
+
+    half = -(-piece.shape[0] // 32) * 16
+    beside, above = across(held, 1), across(held, 2)
+    opposite = jnp.concatenate([across(above[:, :half], 1), across(beside[:, half:], 2)], axis=1)
+    near = jnp.stack([held, beside, above, opposite])
+    return near, lax.ppermute(near, "dp", [(0, 1), (1, 0)])
+
+
+def nothing_of(array):
+    return (array.reshape(-1)[0].astype(F32) * 0.0).astype(jnp.int32)
 
 
 def earlier_blocks(state, axis):
@@ -295,27 +440,6 @@
     feature_dim = feat_cols // heads
     tap_count = conv_window.shape[0]
 
-    plane_rows = width // groups
-    row_at = device_place * plane_rows
-    out_rows, out_cols = head_cols // seq_count, width // dp_count
-
-    def row_piece(w):
-        return lax.dynamic_slice_in_dim(w, row_at, plane_rows).reshape(plane_rows, -1)
-
-    def out_piece(w):
-        return lax.dynamic_slice(w, (seq_place * out_rows, dp_place * out_cols), (out_rows, out_cols))
-
-    piece_one = jnp.concatenate([row_piece(w_featmap), row_piece(w_value)], axis=1)
-    all_one = from_all_planes(piece_one).reshape(group_count, width, -1)
-    all_out_one = from_all_planes(out_piece(w_out_one)).reshape(
-        group_count, dp_count, head_cols, out_cols
-    )
-    all_window = from_all_planes(row_piece(w_window)).reshape(group_count, width, -1)
-    all_out_two = from_all_planes(out_piece(w_out_two)).reshape(
-        group_count, dp_count, head_cols, out_cols
-    )
-    all_taps = lax.all_gather(conv_window.reshape(tap_count, 3 * head_cols), "tensor")
-
     placed = reassign[:, None] == jnp.arange(slots_total, dtype=jnp.int32)[None, :]
     table = jnp.sum(jnp.where(placed[:, :, None], page_table[None], 0), axis=1)
     slot_lengths = jnp.sum(jnp.where(placed, lengths[None, :], 0), axis=1)
@@ -347,51 +471,83 @@
     slot = dp_place * req_dev + tensor_place
     length = jnp.sum(jnp.where(jnp.arange(slots_total) == slot, slot_lengths, 0))
 
+    assert heads == NEAR and dp_count == 2
+    values_t = w_value.T[None]
+    featmap_t = w_featmap.transpose(1, 2, 0)
+    window_t = w_window.transpose(1, 2, 0)
+    out_one, out_two = w_out_one[None], w_out_two[None]
+    near_one = from_other_groups(own_piece([values_t, featmap_t]), 0)
+    near_out_one = from_other_groups(own_piece([out_one]), 0)
+    near_window = from_other_groups(own_piece([window_t]), nothing_of(picked))
+    near_out_two = from_other_groups(own_piece([out_two]), nothing_of(swapped))
+    places = jnp.concatenate([(seq_place % NEAR) ^ jnp.arange(NEAR), dp_place[None]])
+    places = places.astype(jnp.int32)
+    group_order = (tensor_place + jnp.arange(group_count)) % group_count
+    taps = conv_window.reshape(tap_count, 3, heads, HEAD).transpose(0, 2, 1, 3)
+    taps = jnp.pad(taps, ((0, 0), (0, 0), (0, 0), (0, SLOT - HEAD)))
+    taps = lax.all_gather(taps.reshape(tap_count, 3 * heads * SLOT), "tensor")
+    taps = taps.at[group_order].get(mode="promise_in_bounds")
+
     first, second, ones, scale, kept = feature_tables(heads, feature_dim)
     first, second = jnp.asarray(first, BF16), jnp.asarray(second, BF16)
-    spread, column = spread_table(heads)
-    spread = jnp.asarray(spread, BF16)
+    column = np.zeros((1, heads * SLOT), np.float32)
+    column[0, HEAD::SLOT] = 1
     one_cols = 2 * feat_cols + head_cols
+
+    def copy_sems(kinds):
+        return pltpu.SemaphoreType.DMA((group_count, dp_count * NEAR * kinds))
+
+    def weights_of(rows_of_head):
+        return pltpu.VMEM((group_count, dp_count, heads, rows_of_head, width // dp_count), BF16)
+
     slots = heads * SLOT
     num, queries, state = call(
         functools.partial(linear_kernel, heads, feature_dim, kept),
         group_count,
         [
+            SMEM,
             whole((rows, width)),
             whole((1, width)),
-            each((width, one_cols)),
+            *[HBM] * 4,
             whole(first.shape),
             whole(second.shape),
             whole(ones.shape),
-            whole(spread.shape),
             whole(column.shape),
         ],
-        [each((rows, slots)), each((rows, feat_cols)), each((heads * kept, SLOT))],
+        [each((rows, slots)), each((rows, 2 * feat_cols)), each((heads * kept, SLOT))],
         [
             jax.ShapeDtypeStruct((group_count, rows, slots), F32),
-            jax.ShapeDtypeStruct((group_count, rows, feat_cols), BF16),
+            jax.ShapeDtypeStruct((group_count, rows, 2 * feat_cols), BF16),
             jax.ShapeDtypeStruct((group_count, heads * kept, SLOT), BF16),
         ],
-        [pltpu.VMEM((rows, width), BF16)],
+        [
+            pltpu.VMEM((rows, width), BF16),
+            weights_of(SLOT),
+            weights_of(2 * feature_dim),
+            copy_sems(3),
+        ],
         3 * group_count * rows * width * one_cols,
         group_count * width * one_cols * 2,
         "linear_rows",
-    )(tokens, gain_one[None], all_one, first, second, ones, spread, column)
+    )(
+        places, tokens, gain_one[None], values_t, featmap_t, *near_one, first, second, ones, column
+    )
     priors = earlier_blocks(state, "seq")
     residual, normed_two = call(
         functools.partial(out_one_kernel, heads, kept, len(priors)),
         group_count,
         [
+            SMEM,
             each((rows, slots)),
-            each((rows, feat_cols)),
+            each((rows, 2 * feat_cols)),
             whole(first.shape),
             whole(second.shape),
             whole(ones.shape),
             whole(scale.shape),
         ]
         + [each((heads * kept, SLOT))] * len(priors)
+        + [HBM] * 3
         + [
-            each((dp_count, head_cols, out_cols)),
             whole((rows, width)),
             whole((1, width)),
         ],
@@ -399,13 +555,17 @@
         [jax.ShapeDtypeStruct((rows, width), BF16)] * 2,
         [
             pltpu.VMEM((rows, width), F32),
-            pltpu.VMEM((slots, out_cols), BF16),
             pltpu.VMEM((rows, slots), BF16),
+            weights_of(SLOT),
+            copy_sems(1),
         ],
         3 * group_count * rows * width * head_cols,
         group_count * width * head_cols * 2,
         "linear_out",
-    )(num, queries, first, second, ones, scale, *priors, all_out_one, tokens, gain_two[None])
+    )(
+        places, num, queries, first, second, ones, scale, *priors, out_one, *near_out_one, tokens,
+        gain_two[None],
+    )
 
     halo = lax.ppermute(
         normed_two[rows - HALO :], "seq", [(i, i + 1) for i in range(seq_count - 1)]
@@ -416,35 +576,45 @@
         group_count,
         [
             SMEM,
+            SMEM,
             whole((rows, width)),
             whole((HALO, width)),
-            each((width, 3 * head_cols)),
-            each((tap_count, 3 * head_cols)),
+            *[HBM] * 3,
+            each((tap_count, 3 * slots)),
         ],
         each((rows, slots)),
         jax.ShapeDtypeStruct((group_count, rows, slots), BF16),
-        [pltpu.VMEM((HALO + rows, width), BF16)],
+        [
+            pltpu.VMEM((HALO + rows, width), BF16),
+            weights_of(3 * SLOT),
+            copy_sems(3),
+        ],
         3 * group_count * rows * width * 3 * head_cols,
         group_count * width * 3 * head_cols * 2,
         "window_rows",
-    )(block_start, normed_two, halo, all_window, all_taps)
+    )(places, block_start, normed_two, halo, window_t, *near_window, taps)
     live = (length - seq_place * rows).astype(jnp.int32)[None]
     result = call(
-        functools.partial(out_two_kernel, heads),
+        out_two_kernel,
         group_count,
         [
+            SMEM,
             SMEM,
             each((rows, slots)),
-            each((dp_count, head_cols, out_cols)),
+            *[HBM] * 3,
             whole((rows, width)),
         ],
         whole((rows, width)),
         jax.ShapeDtypeStruct((rows, width), BF16),
-        [pltpu.VMEM((rows, width), F32), pltpu.VMEM((slots, out_cols), BF16)],
+        [
+            pltpu.VMEM((rows, width), F32),
+            weights_of(SLOT),
+            copy_sems(1),
+        ],
         2 * group_count * rows * width * head_cols,
         group_count * width * head_cols * 2,
         "window_out",
-    )(live, mixed_two, all_out_two, residual)
+    )(places, live, mixed_two, out_two, *near_out_two, residual)
 
     result = result.reshape(page_span, group_count, page_share, width).transpose(1, 0, 2, 3)
     return lax.all_to_all(result, "tensor", split_axis=0, concat_axis=0, tiled=True)

time: 426 us -> 422 us (level)
  waiting for transfers between devices: 274 us -> 163 us
  blocking collectives: 40.8 us -> 98.4 us
  starting transfers between devices: 21.6 us -> 41.1 us
  other arithmetic: 2.44 us -> 16 us
  local copies, waits for them, and re-layouts: 21.8 us -> 30.1 us
  Pallas kernels: 50.7 us -> 57.2 us
    all_gather x4 -> x1, waiting for transfers between devices: 220 us -> 28.3 us  [from_other_groups(): lax.all_gather(piece, 'tensor').at[order].get(mode='promise_in_bounds')]
    ppermute x0 -> x20, waiting for transfers between devices: none -> 98.3 us  [the longest x16 98.3 us: across(): lax.ppermute(array, 'seq', [(i, i ^ bit) for i in range(lax.axis_size('se...]
    all_gather x1 -> x4, blocking collectives: 14.5 us -> 74 us  [the longest x3 60.2 us: from_other_groups(): lax.all_gather(piece, 'tensor').at[order].get(mode='promise_in_bounds')]
    all_to_all x1, waiting for transfers between devices: 40.6 us -> 0.01 us  [on_device(): lax.all_to_all(picked, 'tensor', split_axis=0, concat_axis=0, tiled=True)]
    ppermute x3, waiting for transfers between devices: 0.01 us -> 23 us  [earlier_blocks(): lax.ppermute(state, axis, [(i, i + by) for i in range(peers - by)])]
    ppermute x0 -> x20, starting transfers between devices: none -> 19.6 us  [the longest x16 19.5 us: across(): lax.ppermute(array, 'seq', [(i, i ^ bit) for i in range(lax.axis_size('se...]
    another operation x0 -> x8, other arithmetic: none -> 12.3 us  [from_other_groups(): near = jnp.stack([held, beside, above, opposite])]
    dynamic_slice x5 -> x0, local copies, waits for them, and re-layouts: 5.9 us -> none  [the longest x2 3.25 us: out_piece(): lax.dynamic_slice(w, (seq_place * out_rows, dp_place * out_cols), (out_ro...]
  transfers between devices with their start and end apart: 10 -> 27, of which waited for: 6 -> 13; matrix products, arithmetic and copies ran while one was open for 4% -> 8% of each run, Pallas kernels for 10% -> 12%
where the time goes in v2:
time: 422 us; the launch traced here: 421 us
  waiting for transfers between devices  163 us (39%)
  blocking collectives  98.4 us (23%)
  Pallas kernels  57.2 us (14%)
  starting transfers between devices  41.1 us (10%)
  local copies, waits for them, and re-layouts  30.1 us (7%)
  other arithmetic  16 us (4%)
  between operations  15.7 us (4%)
    ppermute x16, waiting for transfers between devices, across(): lax.ppermute(array, 'seq', [(i, i ^ bit) for i in range(lax.axis_size('se...  98.3 us
    all_gather x3, blocking collectives, from_other_groups(): lax.all_gather(piece, 'tensor').at[order].get(mode='promise_in_bounds')  60.2 us
    all_gather x1, waiting for transfers between devices, from_other_groups(): lax.all_gather(piece, 'tensor').at[order].get(mode='promise_in_bounds')  28.3 us
    pallas_call x1, Pallas kernels, on_device(): call(functools.partial(window_kernel, heads), group_count, [SMEM, SMEM, w...  25.6 us
    all_to_all x1, blocking collectives, on_device(): lax.all_to_all(result, 'tensor', split_axis=0, concat_axis=0, tiled=True)  24.4 us
    ppermute x3, waiting for transfers between devices, earlier_blocks(): lax.ppermute(state, axis, [(i, i + by) for i in range(peers - by)])  23 us
    ppermute x16, starting transfers between devices, across(): lax.ppermute(array, 'seq', [(i, i ^ bit) for i in range(lax.axis_size('se...  19.5 us
    all_gather x1, blocking collectives, on_device(): taps = lax.all_gather(taps.reshape(tap_count, 3 * heads * SLOT), 'tensor')  13.8 us
  transfers between devices with their start and end apart: 27, of which 13 were waited for; matrix products, arithmetic and copies ran while one was open for 8% of the time, Pallas kernels for 12%

profile of v2, /device:TPU:0, one launch (start us, length us, event | category | flops | bytes accessed | tf_op | source)
XLA Modules:
  0.0 421.3 jit_solution(930335954765736632)
XLA Ops:
  6.5 2.0 constant_dynamic-slice_fusion
  8.6 0.7 iota_compare_fusion.2
  9.3 0.8 select_reduce_fusion.1
  11.0 2.2 gather_fusion
  13.2 5.2 %all-to-all-start = ((bf16[8,8,4,1792]{3,2,1,0:T(4,128)(2,1)}), bf16[8,8,4,1792]{3,2,1,0:T(4,128)(2,1)S(1)}, u32[]{:S(2)}, u32[]{:S(2)}) async-start(bf16[8,8,4,1792]{3,2,1,0:T(4,128)(2,1)} %bitcast.5), calls=%async_computation | async-start | bytes 1835008 | tf_op jit(solution)/shard_map/all_to_all | solution.py:462
  18.6 13.2 %all-to-all-done = bf16[8,8,4,1792]{3,2,1,0:T(4,128)(2,1)S(1)} async-done(((bf16[8,8,4,1792]{3,2,1,0:T(4,128)(2,1)}), bf16[8,8,4,1792]{3,2,1,0:T(4,128)(2,1)S(1)}, u32[]{:S(2)}, u32[]{:S(2)}) %all-to-all-start) | async-done | bytes 917536 | tf_op jit(solution)/shard_map/all_to_all | solution.py:462
  31.8 1.3 gather_fusion.1
  34.7 28.3 %all-gather.5.cloned.1.call-done = bf16[4,336,896]{2,1,0:T(8,128)(2,1)} async-done(((bf16[1,336,896]{2,1,0:T(8,128)(2,1)}), bf16[4,336,896]{2,1,0:T(8,128)(2,1)}) %all-gather.5.cloned.1.call-update) | async-done | bytes 2408464 | tf_op jit(solution)/shard_map/all_gather | solution.py:384
  63.0 2.6 gather_fusion.4
  65.6 1.5 collective-permute-start.15
  67.1 1.5 collective-permute-start.14
  68.6 38.1 %collective-permute-done.15 = bf16[3,336,896]{2,1,0:T(8,128)(2,1)S(1)} collective-permute-done((bf16[3,336,896]{2,1,0:T(8,128)(2,1)S(1)}, bf16[3,336,896]{2,1,0:T(8,128)(2,1)S(1)}, u32[]{:S(2)}, u32[]{:S(2)}) %collective-permute-start.15) | collective-permute-done | bytes 1806368 | tf_op jit(solution)/shard_map/ppermute | solution.py:387
  106.8 1.5 collective-permute-start.16
  108.4 1.5 collective-permute-start.17
  110.0 18.2 %collective-permute-done.17 = bf16[3,160,896]{2,1,0:T(8,128)(2,1)S(1)} collective-permute-done((bf16[3,160,896]{2,1,0:T(8,128)(2,1)S(1)}, bf16[3,160,896]{2,1,0:T(8,128)(2,1)S(1)}, u32[]{:S(2)}, u32[]{:S(2)}) %collective-permute-start.17) | collective-permute-done | bytes 860192 | tf_op jit(solution)/shard_map/ppermute | solution.py:387
  128.8 3.6 pad_maximum_fusion.near_ref
  132.4 0.8 constant_dynamic-slice_fusion.1
  133.3 0.9 dynamic-slice_bitcast_fusion
  134.3 21.9 %all-gather = bf16[576,896]{1,0:T(8,128)(2,1)S(1)} all-gather(bf16[144,896]{1,0:T(8,128)(2,1)S(1)} %pad_maximum_fusion.4), channel_id=2, replica_groups=mesh['dp'=2,'seq'=4,'tensor'=4] {'tensor'}, dimensions={0}, use_global_device_ids=true | all-gather | bytes 1290240 | tf_op jit(solution)/shard_map/all_gather | solution.py:384
  156.9 1.5 collective-permute-start.1
  158.4 1.5 collective-permute-start
  159.9 15.3 %collective-permute-done.1 = bf16[3,144,896]{2,1,0:T(8,128)(2,1)S(1)} collective-permute-done((bf16[3,144,896]{2,1,0:T(8,128)(2,1)S(1)}, bf16[3,144,896]{2,1,0:T(8,128)(2,1)S(1)}, u32[]{:S(2)}, u32[]{:S(2)}) %collective-permute-start.1) | collective-permute-done | bytes 774176 | tf_op jit(solution)/shard_map/ppermute | solution.py:387
  175.2 0.9 slice.58
  176.1 1.5 collective-permute-start.2
  177.6 0.9 slice.59
  178.4 1.5 collective-permute-start.3
  179.9 17.9 %all-gather.1 = bf16[448,896]{1,0:T(8,128)(2,1)S(1)} all-gather(bf16[112,896]{1,0:T(8,128)(2,1)S(1)} %dynamic-slice-done.1), channel_id=3, replica_groups=mesh['dp'=2,'seq'=4,'tensor'=4] {'tensor'}, dimensions={0}, use_global_device_ids=true | all-gather | bytes 1003520 | tf_op jit(solution)/shard_map/all_gather | solution.py:384
  199.7 1.0 copy.41
  200.7 3.6 all-to-all-start.1
  204.3 1.0 maximum_bitcast_fusion.1
  205.3 2.9 pad_maximum_fusion.1.near_ref
  208.2 1.8 collective-permute-done.9
  210.0 1.0 slice.60
  211.0 1.5 collective-permute-start.10
  212.6 1.0 slice.61
  214.1 6.0 %collective-permute-done.11 = bf16[3,48,896]{2,1,0:T(8,128)(2,1)S(1)} collective-permute-done((bf16[3,48,896]{2,1,0:T(8,128)(2,1)S(1)}, bf16[3,48,896]{2,1,0:T(8,128)(2,1)S(1)}, u32[]{:S(2)}, u32[]{:S(2)}) %collective-permute-start.11) | collective-permute-done | bytes 258080 | tf_op jit(solution)/shard_map/ppermute | solution.py:387
  220.2 3.1 pad_maximum_fusion.2.refs_11_
  223.3 20.3 %all-gather.2 = bf16[448,896]{1,0:T(8,128)(2,1)S(1)} all-gather(bf16[112,896]{1,0:T(8,128)(2,1)S(1)} %dynamic-slice-done), channel_id=4, replica_groups=mesh['dp'=2,'seq'=4,'tensor'=4] {'tensor'}, dimensions={0}, use_global_device_ids=true | all-gather | bytes 1003520 | tf_op jit(solution)/shard_map/all_gather | solution.py:384
  246.4 1.5 collective-permute-start.20
  247.9 1.1 collective-permute-start.19
  249.0 11.2 %collective-permute-done.20 = bf16[3,112,896]{2,1,0:T(8,128)(2,1)S(1)} collective-permute-done((bf16[3,112,896]{2,1,0:T(8,128)(2,1)S(1)}, bf16[3,112,896]{2,1,0:T(8,128)(2,1)S(1)}, u32[]{:S(2)}, u32[]{:S(2)}) %collective-permute-start.20) | collective-permute-done | bytes 602144 | tf_op jit(solution)/shard_map/ppermute | solution.py:387
  260.2 1.1 collective-permute-start.21
  261.3 1.2 collective-permute-done.19
  262.9 6.0 %collective-permute-done.22 = bf16[3,48,896]{2,1,0:T(8,128)(2,1)S(1)} collective-permute-done((bf16[3,48,896]{2,1,0:T(8,128)(2,1)S(1)}, bf16[3,48,896]{2,1,0:T(8,128)(2,1)S(1)}, u32[]{:S(2)}, u32[]{:S(2)}) %collective-permute-start.22) | collective-permute-done | bytes 258080 | tf_op jit(solution)/shard_map/ppermute | solution.py:387
  269.0 1.4 pad_maximum_fusion.3.near_ref
  270.5 0.7 broadcast_in_dim.113.gain_ref
  271.9 1.4 copy.42
  273.3 2.4 reshape.441.x_ref.refs_13_
  275.7 13.4 %linear_rows.1 = (f32[4,256,512]{2,1,0:T(8,128)}, bf16[4,256,128]{2,1,0:T(8,128)(2,1)}, bf16[4,640,128]{2,1,0:T(8,128)(2,1)}) custom-call(s32[5]{0:T(128)} %pad_add_fusion.place_ref.refs_0_, bf16[256,1792]{1,0:T(8,128)(2,1)} %reshape.441.x_ref.refs_13_, f32[1,1792]{1,0:T(1,128)} %broadcast_in_dim.113.gain_ref, bf16[1,448,1792]{2,1,0:T(8,128)(2,1)} %bitcast.91, ...), custom_call_target="tpu_custom_call" | custom-call | flops 3170893824 | bytes 8257536 | tf_op jit(solution)/shard_map/linear_rows/pallas_call | solution.py:504
  289.1 3.0 collective-permute-start.5
  292.1 3.1 collective-permute-start.6
  295.2 2.1 collective-permute-start.7
  298.1 9.3 %collective-permute-done.5.refs_7_ = bf16[4,640,128]{2,1,0:T(8,128)(2,1)S(1)} collective-permute-done((bf16[4,640,128]{2,1,0:T(8,128)(2,1)}, bf16[4,640,128]{2,1,0:T(8,128)(2,1)S(1)}, u32[]{:S(2)}, u32[]{:S(2)}) %collective-permute-start.5) | collective-permute-done | bytes 655392 | tf_op jit(solution)/shard_map/ppermute | solution.py:404
  307.5 13.7 %collective-permute-done.6.refs_8_ = bf16[4,640,128]{2,1,0:T(8,128)(2,1)} collective-permute-done((bf16[4,640,128]{2,1,0:T(8,128)(2,1)}, bf16[4,640,128]{2,1,0:T(8,128)(2,1)}, u32[]{:S(2)}, u32[]{:S(2)}) %collective-permute-start.6) | collective-permute-done | bytes 655392 | tf_op jit(solution)/shard_map/ppermute | solution.py:404
  321.1 10.6 %linear_out.1 = (bf16[256,1792]{1,0:T(8,128)(2,1)}, bf16[256,1792]{1,0:T(8,128)(2,1)}) custom-call(s32[5]{0:T(128)} %pad_add_fusion.place_ref.refs_0_, f32[4,256,512]{2,1,0:T(8,128)} %get-tuple-element.10.refs_1_, bf16[4,256,128]{2,1,0:T(8,128)(2,1)} %get-tuple-element.11.refs_2_, bf16[128,1024]{1,0:T(8,128)(2,1)} %constant.129.clone.first_ref.refs_3_, ...), custom_call_target="tpu_custom_call" | custom-call | flops 2466250752 | bytes 6422528 | tf_op jit(solution)/shard_map/linear_out/pallas_call | solution.py:536
  331.7 1.0 slice.37
  332.7 4.5 %collective-permute-start.13 = (bf16[80,1792]{1,0:T(8,128)(2,1)S(1)}, bf16[80,1792]{1,0:T(8,128)(2,1)}, u32[]{:S(2)}, u32[]{:S(2)}) collective-permute-start(bf16[80,1792]{1,0:T(8,128)(2,1)S(1)} %slice.37), channel_id=1, source_target_pairs={{0,4},{4,8},{8,12},{1,5},{5,9},{9,13},{2,6},{6,10},{10,14},{3,7},{... | collective-permute-start | bytes 860168 | tf_op jit(solution)/shard_map/ppermute | solution.py:570
  338.6 13.8 %all_gather.22 = f32[4,3,1536]{2,1,0:T(4,128)S(1)} all-gather(f32[1,3,1536]{2,1,0:T(4,128)S(1)} %all_gather_reshape.7), channel_id=1, replica_groups=mesh['dp'=2,'seq'=4,'tensor'=4] {'tensor'}, dimensions={0}, use_global_device_ids=true | all-gather | bytes 92160 | tf_op jit(solution)/shard_map/all_gather | solution.py:488
  352.4 1.2 gather_fusion.5
  353.7 25.6 %window_rows.1.mixed_ref = bf16[4,256,512]{2,1,0:T(8,128)(2,1)} custom-call(s32[5]{0:T(128)} %pad_add_fusion.place_ref.refs_0_, s32[1]{0:T(128)} %bitcast.2.first_ref, bf16[256,1792]{1,0:T(8,128)(2,1)} %get-tuple-element.13.x_ref, bf16[80,1792]{1,0:T(8,128)(2,1)} %collective-permute-done.13.halo_ref, bf16[3,448,1792]{2,1,0:T(8,128)(2,1)} %bitcast.90, ...), custom_call_target="tpu_custom_call" | custom-call | flops 7398752256 | bytes 19267584 | tf_op jit(solution)/shard_map/window_rows/pallas_call | solution.py:574
  379.3 7.7 %window_out.1 = bf16[256,1792]{1,0:T(8,128)(2,1)} custom-call(s32[5]{0:T(128)} %pad_add_fusion.place_ref.refs_0_, s32[1]{0:T(128)} %bitcast.1.live_ref, bf16[4,256,512]{2,1,0:T(8,128)(2,1)} %window_rows.1.mixed_ref, bf16[1,448,1792]{2,1,0:T(8,128)(2,1)} %bitcast.81, bf16[4,3,112,896]{3,2,1,0:T(8,128)(2,1)} %copy-done.2, ...), custom_call_target="tpu_custom_call" | custom-call | flops 1644167168 | bytes 6422528 | tf_op jit(solution)/shard_map/window_out/pallas_call | solution.py:597
  387.0 1.9 reshape.446
  389.2 24.4 %all_to_all.15 = bf16[4,16,4,1792]{3,2,1,0:T(4,128)(2,1)S(1)} all-to-all(bf16[4,16,4,1792]{3,2,1,0:T(4,128)(2,1)S(1)} %bitcast.72), channel_id=1, replica_groups=mesh['dp'=2,'seq'=4,'tensor'=4] {'tensor'}, dimensions={0} | all-to-all | bytes 1835008 | tf_op jit(solution)/shard_map/all_to_all | solution.py:620
  413.5 0.9 copy.56
  (106 shorter events, 11.2 us)
Async XLA Ops:
  6.5 4.4 %copy-start = (bf16[64,4,1792]{2,1,0:T(4,128)(2,1)S(1)}, bf16[64,4,1792]{2,1,0:T(4,128)(2,1)}, u32[]{:S(2)}) copy-start(bf16[64,4,1792]{2,1,0:T(4,128)(2,1)} %param.17) | copy-start | bytes 2752516
  6.5 56.5 %all-gather.5.cloned.1.call-start = ((), (), s32[]{:S(2)}) async-start(), calls=%async_computation.3 | async-start | bytes 3010560 | tf_op jit(solution)/shard_map/all_gather | solution.py:384
  13.2 18.6 %all-to-all-start = ((bf16[8,8,4,1792]{3,2,1,0:T(4,128)(2,1)}), bf16[8,8,4,1792]{3,2,1,0:T(4,128)(2,1)S(1)}, u32[]{:S(2)}, u32[]{:S(2)}) async-start(bf16[8,8,4,1792]{3,2,1,0:T(4,128)(2,1)} %bitcast.5), calls=%async_computation | async-start | bytes 1835008 | tf_op jit(solution)/shard_map/all_to_all | solution.py:462
  65.6 41.2 %collective-permute-start.15 = (bf16[3,336,896]{2,1,0:T(8,128)(2,1)S(1)}, bf16[3,336,896]{2,1,0:T(8,128)(2,1)S(1)}, u32[]{:S(2)}, u32[]{:S(2)}) collective-permute-start(bf16[3,336,896]{2,1,0:T(8,128)(2,1)S(1)} %gather_fusion.4), channel_id=1, source_target_pairs={{0,8},{4,12},{8,0},{12,4},{1,9},{5,13},{9,1},{13,5},{2,10},{6,14},... | collective-permute-start | bytes 5419016 | tf_op jit(solution)/shard_map/ppermute | solution.py:387
  67.1 41.2 %collective-permute-start.14 = (bf16[3,336,896]{2,1,0:T(8,128)(2,1)S(1)}, bf16[3,336,896]{2,1,0:T(8,128)(2,1)S(1)}, u32[]{:S(2)}, u32[]{:S(2)}) collective-permute-start(bf16[3,336,896]{2,1,0:T(8,128)(2,1)S(1)} %gather_fusion.4), channel_id=1, source_target_pairs={{0,4},{4,0},{8,12},{12,8},{1,5},{5,1},{9,13},{13,9},{2,6},{6,2},{1... | collective-permute-start | bytes 5419016 | tf_op jit(solution)/shard_map/ppermute | solution.py:387
  106.8 21.8 %collective-permute-start.16 = (bf16[3,176,896]{2,1,0:T(8,128)(2,1)S(1)}, bf16[3,176,896]{2,1,0:T(8,128)(2,1)S(1)}, u32[]{:S(2)}, u32[]{:S(2)}) collective-permute-start(bf16[3,176,896]{2,1,0:T(8,128)(2,1)S(1)} %slice.63), channel_id=1, source_target_pairs={{0,4},{4,0},{8,12},{12,8},{1,5},{5,1},{9,13},{13,9},{2,6},{6,2},{1... | collective-permute-start | bytes 2838536 | tf_op jit(solution)/shard_map/ppermute | solution.py:387
  108.4 19.7 %collective-permute-start.17 = (bf16[3,160,896]{2,1,0:T(8,128)(2,1)S(1)}, bf16[3,160,896]{2,1,0:T(8,128)(2,1)S(1)}, u32[]{:S(2)}, u32[]{:S(2)}) collective-permute-start(bf16[3,160,896]{2,1,0:T(8,128)(2,1)S(1)} %slice.64), channel_id=1, source_target_pairs={{0,8},{4,12},{8,0},{12,4},{1,9},{5,13},{9,1},{13,5},{2,10},{6,14},... | collective-permute-start | bytes 2580488 | tf_op jit(solution)/shard_map/ppermute | solution.py:387
  132.4 221.2 %collective-permute-start.18 = (bf16[4,3,336,896]{3,2,1,0:T(8,128)(2,1)}, bf16[4,3,336,896]{3,2,1,0:T(8,128)(2,1)}, u32[]{:S(2)}, u32[]{:S(2)}) collective-permute-start(bf16[4,3,336,896]{3,2,1,0:T(8,128)(2,1)} %pad_maximum_fusion.near_ref), channel_id=1, source_target_pairs={{0,16},{16,0},{1,17},{17,1},{2,18},{18,2},{3,19},{19,3},{4,20},{20... | collective-permute-start | bytes 21676040 | tf_op jit(solution)/shard_map/ppermute | solution.py:393
  134.3 45.6 %dynamic-slice-start.1 = ((bf16[448,1792]{1,0:T(8,128)(2,1)}, s32[]{:T(128)}, s32[]{:T(128)}), bf16[112,896]{1,0:T(8,128)(2,1)S(1)}, s32[]{:S(2)}) async-start(bf16[448,1792]{1,0:T(8,128)(2,1)} %param.24, s32[]{:T(128)} %select_n.204, s32[]{:T(128)} %select_n.203), calls=%async_computation.5 | async-start | bytes 401920 | tf_op jit(solution)/shard_map/dynamic-slice.2
  156.9 18.3 %collective-permute-start.1 = (bf16[3,144,896]{2,1,0:T(8,128)(2,1)S(1)}, bf16[3,144,896]{2,1,0:T(8,128)(2,1)S(1)}, u32[]{:S(2)}, u32[]{:S(2)}) collective-permute-start(bf16[3,144,896]{2,1,0:T(8,128)(2,1)S(1)} %gather_fusion.2), channel_id=1, source_target_pairs={{0,8},{4,12},{8,0},{12,4},{1,9},{5,13},{9,1},{13,5},{2,10},{6,14},... | collective-permute-start | bytes 2322440 | tf_op jit(solution)/shard_map/ppermute | solution.py:387
  158.4 19.1 %collective-permute-start = (bf16[3,144,896]{2,1,0:T(8,128)(2,1)S(1)}, bf16[3,144,896]{2,1,0:T(8,128)(2,1)S(1)}, u32[]{:S(2)}, u32[]{:S(2)}) collective-permute-start(bf16[3,144,896]{2,1,0:T(8,128)(2,1)S(1)} %gather_fusion.2), channel_id=1, source_target_pairs={{0,4},{4,0},{8,12},{12,8},{1,5},{5,1},{9,13},{13,9},{2,6},{6,2},{1... | collective-permute-start | bytes 2322440 | tf_op jit(solution)/shard_map/ppermute | solution.py:387
  175.2 22.6 %copy-start.4 = (bf16[3,144,896]{2,1,0:T(8,128)(2,1)}, bf16[3,144,896]{2,1,0:T(8,128)(2,1)S(1)}, u32[]{:S(2)}) copy-start(bf16[3,144,896]{2,1,0:T(8,128)(2,1)S(1)} %collective-permute-done.1) | copy-start | bytes 2322436
  176.1 28.2 %collective-permute-start.2 = (bf16[3,80,896]{2,1,0:T(8,128)(2,1)}, bf16[3,80,896]{2,1,0:T(8,128)(2,1)S(1)}, u32[]{:S(2)}, u32[]{:S(2)}) collective-permute-start(bf16[3,80,896]{2,1,0:T(8,128)(2,1)} %slice.58), channel_id=1, source_target_pairs={{0,4},{4,0},{8,12},{12,8},{1,5},{5,1},{9,13},{13,9},{2,6},{6,2},{1... | collective-permute-start | bytes 1290248 | tf_op jit(solution)/shard_map/ppermute | solution.py:387
  177.6 20.3 %copy-start.6 = (bf16[3,144,896]{2,1,0:T(8,128)(2,1)}, bf16[3,144,896]{2,1,0:T(8,128)(2,1)S(1)}, u32[]{:S(2)}) copy-start(bf16[3,144,896]{2,1,0:T(8,128)(2,1)S(1)} %collective-permute-done) | copy-start | bytes 2322436
  178.4 25.9 %collective-permute-start.3 = (bf16[3,64,896]{2,1,0:T(8,128)(2,1)}, bf16[3,64,896]{2,1,0:T(8,128)(2,1)}, u32[]{:S(2)}, u32[]{:S(2)}) collective-permute-start(bf16[3,64,896]{2,1,0:T(8,128)(2,1)} %slice.59), channel_id=1, source_target_pairs={{0,8},{4,12},{8,0},{12,4},{1,9},{5,13},{9,1},{13,5},{2,10},{6,14},... | collective-permute-start | bytes 1032200 | tf_op jit(solution)/shard_map/ppermute | solution.py:387
  198.5 14.1 %collective-permute-start.8 = (bf16[3,112,896]{2,1,0:T(8,128)(2,1)S(1)}, bf16[3,112,896]{2,1,0:T(8,128)(2,1)}, u32[]{:S(2)}, u32[]{:S(2)}) collective-permute-start(bf16[3,112,896]{2,1,0:T(8,128)(2,1)S(1)} %gather_fusion.3), channel_id=1, source_target_pairs={{0,4},{4,0},{8,12},{12,8},{1,5},{5,1},{9,13},{13,9},{2,6},{6,2},{1... | collective-permute-start | bytes 1806344 | tf_op jit(solution)/shard_map/ppermute | solution.py:387
  199.1 10.9 %collective-permute-start.9 = (bf16[3,112,896]{2,1,0:T(8,128)(2,1)S(1)}, bf16[3,112,896]{2,1,0:T(8,128)(2,1)}, u32[]{:S(2)}, u32[]{:S(2)}) collective-permute-start(bf16[3,112,896]{2,1,0:T(8,128)(2,1)S(1)} %gather_fusion.3), channel_id=1, source_target_pairs={{0,8},{4,12},{8,0},{12,4},{1,9},{5,13},{9,1},{13,5},{2,10},{6,14},... | collective-permute-start | bytes 1806344 | tf_op jit(solution)/shard_map/ppermute | solution.py:387
  199.7 5.6 %copy-start.5 = (bf16[3,144,896]{2,1,0:T(8,128)(2,1)S(1)}, bf16[3,144,896]{2,1,0:T(8,128)(2,1)}, u32[]{:S(2)}) copy-start(bf16[3,144,896]{2,1,0:T(8,128)(2,1)} %copy-done.4) | copy-start | bytes 2322436
  200.7 42.9 %all-to-all-start.1 = ((bf16[4,16,4,1792]{3,1,2,0:T(8,128)(2,1)}), bf16[4,16,4,1792]{3,1,2,0:T(8,128)(2,1)S(1)}, u32[]{:S(2)}, u32[]{:S(2)}) async-start(bf16[4,16,4,1792]{3,1,2,0:T(8,128)(2,1)} %copy.41), calls=%async_computation.1 | async-start | bytes 1835008 | tf_op jit(solution)/shard_map/all_to_all | solution.py:469
  208.2 67.5 %collective-permute-start.4 = (bf16[4,3,144,896]{3,2,1,0:T(8,128)(2,1)}, bf16[4,3,144,896]{3,2,1,0:T(8,128)(2,1)}, u32[]{:S(2)}, u32[]{:S(2)}) collective-permute-start(bf16[4,3,144,896]{3,2,1,0:T(8,128)(2,1)} %pad_maximum_fusion.1.near_ref), channel_id=1, source_target_pairs={{0,16},{16,0},{1,17},{17,1},{2,18},{18,2},{3,19},{19,3},{4,20},{20... | collective-permute-start | bytes 9289736 | tf_op jit(solution)/shard_map/ppermute | solution.py:393
  211.0 9.1 %collective-permute-start.10 = (bf16[3,64,896]{2,1,0:T(8,128)(2,1)S(1)}, bf16[3,64,896]{2,1,0:T(8,128)(2,1)S(1)}, u32[]{:S(2)}, u32[]{:S(2)}) collective-permute-start(bf16[3,64,896]{2,1,0:T(8,128)(2,1)S(1)} %slice.60), channel_id=1, source_target_pairs={{0,4},{4,0},{8,12},{12,8},{1,5},{5,1},{9,13},{13,9},{2,6},{6,2},{1... | collective-permute-start | bytes 1032200 | tf_op jit(solution)/shard_map/ppermute | solution.py:387
  213.5 6.6 %collective-permute-start.11 = (bf16[3,48,896]{2,1,0:T(8,128)(2,1)S(1)}, bf16[3,48,896]{2,1,0:T(8,128)(2,1)S(1)}, u32[]{:S(2)}, u32[]{:S(2)}) collective-permute-start(bf16[3,48,896]{2,1,0:T(8,128)(2,1)S(1)} %slice.61), channel_id=1, source_target_pairs={{0,8},{4,12},{8,0},{12,4},{1,9},{5,13},{9,1},{13,5},{2,10},{6,14},... | collective-permute-start | bytes 774152 | tf_op jit(solution)/shard_map/ppermute | solution.py:387
  220.2 3.1 dynamic-slice-start
  223.3 71.9 %collective-permute-start.12 = (bf16[4,3,112,896]{3,2,1,0:T(8,128)(2,1)}, bf16[4,3,112,896]{3,2,1,0:T(8,128)(2,1)}, u32[]{:S(2)}, u32[]{:S(2)}) collective-permute-start(bf16[4,3,112,896]{3,2,1,0:T(8,128)(2,1)} %pad_maximum_fusion.2.refs_11_), channel_id=1, source_target_pairs={{0,16},{16,0},{1,17},{17,1},{2,18},{18,2},{3,19},{19,3},{4,20},{20... | collective-permute-start | bytes 7225352 | tf_op jit(solution)/shard_map/ppermute | solution.py:393
  246.3 22.6 %copy-start.3 = (bf16[3,112,896]{2,1,0:T(8,128)(2,1)}, bf16[3,112,896]{2,1,0:T(8,128)(2,1)S(1)}, u32[]{:S(2)}) copy-start(bf16[3,112,896]{2,1,0:T(8,128)(2,1)S(1)} %gather_fusion.6) | copy-start | bytes 1806340
  246.4 13.8 %collective-permute-start.20 = (bf16[3,112,896]{2,1,0:T(8,128)(2,1)S(1)}, bf16[3,112,896]{2,1,0:T(8,128)(2,1)S(1)}, u32[]{:S(2)}, u32[]{:S(2)}) collective-permute-start(bf16[3,112,896]{2,1,0:T(8,128)(2,1)S(1)} %gather_fusion.6), channel_id=1, source_target_pairs={{0,8},{4,12},{8,0},{12,4},{1,9},{5,13},{9,1},{13,5},{2,10},{6,14},... | collective-permute-start | bytes 1806344 | tf_op jit(solution)/shard_map/ppermute | solution.py:387
  247.9 14.6 %collective-permute-start.19 = (bf16[3,112,896]{2,1,0:T(8,128)(2,1)S(1)}, bf16[3,112,896]{2,1,0:T(8,128)(2,1)S(1)}, u32[]{:S(2)}, u32[]{:S(2)}) collective-permute-start(bf16[3,112,896]{2,1,0:T(8,128)(2,1)S(1)} %gather_fusion.6), channel_id=1, source_target_pairs={{0,4},{4,0},{8,12},{12,8},{1,5},{5,1},{9,13},{13,9},{2,6},{6,2},{1... | collective-permute-start | bytes 1806344 | tf_op jit(solution)/shard_map/ppermute | solution.py:387
  260.2 8.7 %collective-permute-start.21 = (bf16[3,64,896]{2,1,0:T(8,128)(2,1)S(1)}, bf16[3,64,896]{2,1,0:T(8,128)(2,1)S(1)}, u32[]{:S(2)}, u32[]{:S(2)}) collective-permute-start(bf16[3,64,896]{2,1,0:T(8,128)(2,1)S(1)} %slice.66), channel_id=1, source_target_pairs={{0,4},{4,0},{8,12},{12,8},{1,5},{5,1},{9,13},{13,9},{2,6},{6,2},{1... | collective-permute-start | bytes 1032200 | tf_op jit(solution)/shard_map/ppermute | solution.py:387
  262.5 6.4 %collective-permute-start.22 = (bf16[3,48,896]{2,1,0:T(8,128)(2,1)S(1)}, bf16[3,48,896]{2,1,0:T(8,128)(2,1)S(1)}, u32[]{:S(2)}, u32[]{:S(2)}) collective-permute-start(bf16[3,48,896]{2,1,0:T(8,128)(2,1)S(1)} %slice.67), channel_id=1, source_target_pairs={{0,8},{4,12},{8,0},{12,4},{1,9},{5,13},{9,1},{13,5},{2,10},{6,14},... | collective-permute-start | bytes 774152 | tf_op jit(solution)/shard_map/ppermute | solution.py:387
  269.0 1.6 copy-start.9
  270.4 18.7 %copy-start.2 = (bf16[4,3,112,896]{3,2,1,0:T(8,128)(2,1)}, bf16[4,3,112,896]{3,2,1,0:T(8,128)(2,1)S(1)}, u32[]{:S(2)}) copy-start(bf16[4,3,112,896]{3,2,1,0:T(8,128)(2,1)S(1)} %pad_maximum_fusion.3.near_ref) | copy-start | bytes 7225348
  270.4 108.8 %collective-permute-start.23 = (bf16[4,3,112,896]{3,2,1,0:T(8,128)(2,1)S(1)}, bf16[4,3,112,896]{3,2,1,0:T(8,128)(2,1)}, u32[]{:S(2)}, u32[]{:S(2)}) collective-permute-start(bf16[4,3,112,896]{3,2,1,0:T(8,128)(2,1)S(1)} %pad_maximum_fusion.3.near_ref), channel_id=1, source_target_pairs={{0,16},{16,0},{1,17},{17,1},{2,18},{18,2},{3,19},{19,3},{4,20},{20... | collective-permute-start | bytes 7225352 | tf_op jit(solution)/shard_map/ppermute | solution.py:393
  275.7 21.7 %copy-start.10 = (f32[1792]{0:T(1024)S(1)}, f32[1792]{0:T(1024)}, u32[]{:S(2)}) copy-start(f32[1792]{0:T(1024)} %param.25) | copy-start | bytes 21508
  275.7 22.3 %copy-start.11 = (s32[8]{0:T(128)S(1)}, s32[8]{0:T(128)}, u32[]{:S(2)}) copy-start(s32[8]{0:T(128)} %param.20) | copy-start | bytes 100
  275.7 22.3 %copy-start.12 = (s32[8]{0:T(128)S(1)}, s32[8]{0:T(128)}, u32[]{:S(2)}) copy-start(s32[8]{0:T(128)} %param.19) | copy-start | bytes 100
  289.1 18.4 %collective-permute-start.5 = (bf16[4,640,128]{2,1,0:T(8,128)(2,1)}, bf16[4,640,128]{2,1,0:T(8,128)(2,1)S(1)}, u32[]{:S(2)}, u32[]{:S(2)}) collective-permute-start(bf16[4,640,128]{2,1,0:T(8,128)(2,1)} %get-tuple-element.12), channel_id=1, source_target_pairs={{0,4},{4,8},{8,12},{1,5},{5,9},{9,13},{2,6},{6,10},{10,14},{3,7},{... | collective-permute-start | bytes 1966088 | tf_op jit(solution)/shard_map/ppermute | solution.py:404
  292.1 29.0 %collective-permute-start.6 = (bf16[4,640,128]{2,1,0:T(8,128)(2,1)}, bf16[4,640,128]{2,1,0:T(8,128)(2,1)}, u32[]{:S(2)}, u32[]{:S(2)}) collective-permute-start(bf16[4,640,128]{2,1,0:T(8,128)(2,1)} %get-tuple-element.12), channel_id=1, source_target_pairs={{0,8},{4,12},{1,9},{5,13},{2,10},{6,14},{3,11},{7,15},{16,24},{20,... | collective-permute-start | bytes 1966088 | tf_op jit(solution)/shard_map/ppermute | solution.py:404
  295.2 25.9 %collective-permute-start.7 = (bf16[4,640,128]{2,1,0:T(8,128)(2,1)}, bf16[4,640,128]{2,1,0:T(8,128)(2,1)}, u32[]{:S(2)}, u32[]{:S(2)}) collective-permute-start(bf16[4,640,128]{2,1,0:T(8,128)(2,1)} %get-tuple-element.12), channel_id=1, source_target_pairs={{0,12},{1,13},{2,14},{3,15},{16,28},{17,29},{18,30},{19,31}} | collective-permute-start | bytes 1966088 | tf_op jit(solution)/shard_map/ppermute | solution.py:404
  307.5 13.7 %copy-start.7 = (bf16[4,640,128]{2,1,0:T(8,128)(2,1)}, bf16[4,640,128]{2,1,0:T(8,128)(2,1)S(1)}, u32[]{:S(2)}) copy-start(bf16[4,640,128]{2,1,0:T(8,128)(2,1)S(1)} %collective-permute-done.5.refs_7_) | copy-start | bytes 1966084
  321.1 16.7 %copy-start.8 = (f32[3,3,448]{2,1,0:T(4,128)S(1)}, f32[3,3,448]{2,1,0:T(4,128)}, u32[]{:S(2)}) copy-start(f32[3,3,448]{2,1,0:T(4,128)} %param.27) | copy-start | bytes 48388
  332.7 20.9 %collective-permute-start.13 = (bf16[80,1792]{1,0:T(8,128)(2,1)S(1)}, bf16[80,1792]{1,0:T(8,128)(2,1)}, u32[]{:S(2)}, u32[]{:S(2)}) collective-permute-start(bf16[80,1792]{1,0:T(8,128)(2,1)S(1)} %slice.37), channel_id=1, source_target_pairs={{0,4},{4,8},{8,12},{1,5},{5,9},{9,13},{2,6},{6,10},{10,14},{3,7},{... | collective-permute-start | bytes 860168 | tf_op jit(solution)/shard_map/ppermute | solution.py:570
  386.9 27.5 %copy-start.1 = (bf16[64,4,1792]{2,1,0:T(4,128)(2,1)S(1)}, bf16[64,4,1792]{2,1,0:T(4,128)(2,1)}, u32[]{:S(2)}) copy-start(bf16[64,4,1792]{2,1,0:T(4,128)(2,1)} %param.17) | copy-start | bytes 2752516
Sparse Core Ops, SparseCore 0:
  8.9 54.0 all-gather.4

commit v3 on v2

--- a/solution.py
+++ b/solution.py
@@ -247,7 +247,8 @@
     heads,
     place_ref,
     first_ref,
-    x_ref,
+    low_ref,
+    high_ref,
     halo_ref,
     own_ref,
     near_ref,
@@ -261,9 +262,12 @@
     step = pl.program_id(0)
     targets = [(own_ref, kind, HEAD, w_ref, kind * SLOT) for kind in range(3)]
 
+    mid = low_ref.shape[0]
+
     def place_rows():
         rows_ref[:HALO] = halo_ref[...]
-        rows_ref[HALO:] = x_ref[...]
+        rows_ref[HALO : HALO + mid] = low_ref[...]
+        rows_ref[HALO + mid :] = high_ref[...]
 
     @pl.when(step == 0)
     def _():
@@ -274,7 +278,7 @@
         w_ref.shape[0],
         place_rows,
     )
-    rows = x_ref.shape[0]
+    rows = 2 * mid
     lead = HALO - WINDOW
     projected = project(rows_ref, w_ref, step)
     taps = tap_ref[0]
@@ -308,6 +312,7 @@
     place_ref,
     live_ref,
     mixed_ref,
+    pair_ref,
     own_ref,
     near_ref,
     far_ref,
@@ -330,7 +335,8 @@
         ),
         w_ref.shape[0],
     )
-    add_branch(mixed_ref[0], w_ref, total_ref)
+    mixed = jnp.where(step < 2, mixed_ref[step % 2], pair_ref[step % 2])
+    add_branch(mixed, w_ref, total_ref)
 
     @pl.when(step == pl.num_programs(0) - 1)
     def _():
@@ -378,23 +384,35 @@
     return jnp.concatenate(found, axis=0)
 
 
-def from_other_groups(piece, after):
-    groups, mine = lax.axis_size("tensor"), lax.axis_index("tensor")
-    order = (mine + 1 + after + jnp.arange(groups - 1)) % groups
-    held = lax.all_gather(piece, "tensor").at[order].get(mode="promise_in_bounds")
-
-    def across(array, bit):
-        return lax.ppermute(array, "seq", [(i, i ^ bit) for i in range(lax.axis_size("seq"))])
-
-    half = -(-piece.shape[0] // 32) * 16
-    beside, above = across(held, 1), across(held, 2)
-    opposite = jnp.concatenate([across(above[:, :half], 1), across(beside[:, half:], 2)], axis=1)
-    near = jnp.stack([held, beside, above, opposite])
-    return near, lax.ppermute(near, "dp", [(0, 1), (1, 0)])
-
-
-def nothing_of(array):
-    return (array.reshape(-1)[0].astype(F32) * 0.0).astype(jnp.int32)
+def across(array, axis, bit):
+    return lax.ppermute(array, axis, [(i, i ^ bit) for i in range(lax.axis_size(axis))])
+
+
+def after(array, others):
+    if not others:
+        return array
+    zero = sum(other.reshape(-1)[0].astype(F32) * 0.0 for other in others)
+    return jnp.where(zero == 0.0, array, jnp.zeros_like(array))
+
+
+def from_groups(piece, offsets, over_z):
+    piece = after(piece, over_z)
+    return jnp.stack([across(piece, "tensor", offset) for offset in offsets])
+
+
+def from_plane(held, over_xy, diagonal, over_cores):
+    held = after(held, over_xy)
+    half = -(-held.shape[1] // 32) * 16
+    beside, above = across(held, "seq", 1), across(held, "seq", 2)
+    opposite = jnp.concatenate(
+        [
+            across(after(above[:, :half], diagonal), "seq", 1),
+            across(after(beside[:, half:], diagonal), "seq", 2),
+        ],
+        axis=1,
+    )
+    near = after(jnp.stack([held, beside, above, opposite]), over_cores)
+    return near, across(near, "dp", 1)
 
 
 def earlier_blocks(state, axis):
@@ -476,17 +494,17 @@
     featmap_t = w_featmap.transpose(1, 2, 0)
     window_t = w_window.transpose(1, 2, 0)
     out_one, out_two = w_out_one[None], w_out_two[None]
-    near_one = from_other_groups(own_piece([values_t, featmap_t]), 0)
-    near_out_one = from_other_groups(own_piece([out_one]), 0)
-    near_window = from_other_groups(own_piece([window_t]), nothing_of(picked))
-    near_out_two = from_other_groups(own_piece([out_two]), nothing_of(swapped))
+    held_one = from_groups(own_piece([values_t, featmap_t]), (1, 2, 3), ())
+    held_out_one = from_groups(own_piece([out_one]), (1, 2, 3), (picked,))
+    near_one = from_plane(held_one, (picked,), (swapped,), (held_out_one,))
+    held_window = from_groups(own_piece([window_t]), (2,), (swapped,))
+    held_out_two = from_groups(own_piece([out_two]), (2, 1, 3), (swapped,))
     places = jnp.concatenate([(seq_place % NEAR) ^ jnp.arange(NEAR), dp_place[None]])
     places = places.astype(jnp.int32)
-    group_order = (tensor_place + jnp.arange(group_count)) % group_count
     taps = conv_window.reshape(tap_count, 3, heads, HEAD).transpose(0, 2, 1, 3)
     taps = jnp.pad(taps, ((0, 0), (0, 0), (0, 0), (0, SLOT - HEAD)))
-    taps = lax.all_gather(taps.reshape(tap_count, 3 * heads * SLOT), "tensor")
-    taps = taps.at[group_order].get(mode="promise_in_bounds")
+    taps = taps.reshape(tap_count, 3 * heads * SLOT)
+    taps = jnp.stack([taps, across(taps, "tensor", 2)])
 
     first, second, ones, scale, kept = feature_tables(heads, feature_dim)
     first, second = jnp.asarray(first, BF16), jnp.asarray(second, BF16)
@@ -533,6 +551,8 @@
         places, tokens, gain_one[None], values_t, featmap_t, *near_one, first, second, ones, column
     )
     priors = earlier_blocks(state, "seq")
+    held_window, held_out_two = after(held_window, (state,)), after(held_out_two, (state,))
+    near_out_one = from_plane(held_out_one, (swapped,), (held_window,), [*priors, held_out_two])
     residual, normed_two = call(
         functools.partial(out_one_kernel, heads, kept, len(priors)),
         group_count,
@@ -567,32 +587,51 @@
         gain_two[None],
     )
 
-    halo = lax.ppermute(
-        normed_two[rows - HALO :], "seq", [(i, i + 1) for i in range(seq_count - 1)]
-    )
+    tail = normed_two[rows - HALO :]
+    halo = lax.ppermute(tail, "seq", [(i, i + 1) for i in range(seq_count - 1)])
+    mid = rows // 2
+    pair_rows = [across(normed_two[at : at + mid], "tensor", 1) for at in (0, mid)]
+    pair_halo = lax.ppermute(
+        tail,
+        ("seq", "tensor"),
+        [
+            (i * group_count + j, (i + 1) * group_count + (j ^ 1))
+            for i in range(seq_count - 1)
+            for j in range(group_count)
+        ],
+    )
+    near_window = from_plane(held_window, (priors[0],), (residual,), (pair_rows[0],))
     block_start = (seq_place * rows).astype(jnp.int32)[None]
-    mixed_two = call(
-        functools.partial(window_kernel, heads),
-        group_count,
-        [
-            SMEM,
-            SMEM,
-            whole((rows, width)),
-            whole((HALO, width)),
-            *[HBM] * 3,
-            each((tap_count, 3 * slots)),
-        ],
-        each((rows, slots)),
-        jax.ShapeDtypeStruct((group_count, rows, slots), BF16),
-        [
-            pltpu.VMEM((HALO + rows, width), BF16),
-            weights_of(3 * SLOT),
-            copy_sems(3),
-        ],
-        3 * group_count * rows * width * 3 * head_cols,
-        group_count * width * 3 * head_cols * 2,
-        "window_rows",
-    )(places, block_start, normed_two, halo, window_t, *near_window, taps)
+
+    def window_rows(low, high, at, slot_halo):
+        return call(
+            functools.partial(window_kernel, heads),
+            2,
+            [
+                SMEM,
+                SMEM,
+                whole((mid, width)),
+                pl.BlockSpec((mid, width), lambda g: (at, 0)),
+                whole((HALO, width)),
+                *[HBM] * 3,
+                each((tap_count, 3 * slots)),
+            ],
+            each((rows, slots)),
+            jax.ShapeDtypeStruct((2, rows, slots), BF16),
+            [
+                pltpu.VMEM((HALO + rows, width), BF16),
+                pltpu.VMEM((2, dp_count, heads, 3 * SLOT, width // dp_count), BF16),
+                copy_sems(3),
+            ],
+            6 * rows * width * 3 * head_cols,
+            2 * width * 3 * head_cols * 2,
+            "window_rows",
+        )(places, block_start, low, high, slot_halo, window_t, *near_window, taps)
+
+    mixed_pair = window_rows(*pair_rows, 0, pair_halo)
+    near_out_two = from_plane(held_out_two, (pair_rows[0],), (pair_rows[1],), (mixed_pair,))
+    mixed_pair = across(mixed_pair, "tensor", 1)
+    mixed_own = window_rows(normed_two, normed_two, 1, halo)
     live = (length - seq_place * rows).astype(jnp.int32)[None]
     result = call(
         out_two_kernel,
@@ -600,7 +639,8 @@
         [
             SMEM,
             SMEM,
-            each((rows, slots)),
+            whole((2, rows, slots)),
+            whole((2, rows, slots)),
             *[HBM] * 3,
             whole((rows, width)),
         ],
@@ -614,7 +654,7 @@
         2 * group_count * rows * width * head_cols,
         group_count * width * head_cols * 2,
         "window_out",
-    )(places, live, mixed_two, out_two, *near_out_two, residual)
+    )(places, live, mixed_own, mixed_pair, out_two, *near_out_two, residual)
 
     result = result.reshape(page_span, group_count, page_share, width).transpose(1, 0, 2, 3)
     return lax.all_to_all(result, "tensor", split_axis=0, concat_axis=0, tiled=True)

time: 422 us -> 380 us (0.900)
  blocking collectives: 98.4 us -> 26.5 us
  waiting for transfers between devices: 163 us -> 139 us
  starting transfers between devices: 41.1 us -> 62.9 us
  other arithmetic: 16 us -> 35 us
  local copies, waits for them, and re-layouts: 30.1 us -> 43.6 us
  between operations: 15.7 us -> 9.27 us
  Pallas kernels: 57.2 us -> 62.1 us
    all_gather x4 -> x0, blocking collectives: 74 us -> none  [the longest x3 60.2 us: from_other_groups(): lax.all_gather(piece, 'tensor').at[order].get(mode='promise_in_bounds')]
    all_gather x1 -> x0, waiting for transfers between devices: 28.3 us -> none  [from_other_groups(): lax.all_gather(piece, 'tensor').at[order].get(mode='promise_in_bounds')]
    select_n x4 -> x23, other arithmetic: 0.05 us -> 26.4 us  [after(): return jnp.where(zero == 0.0, array, jnp.zeros_like(array))]
    ppermute x21 -> x36, waiting for transfers between devices: 98.3 us -> 120 us  [the longest x34 116 us: across(): lax.ppermute(array, axis, [(i, i ^ bit) for i in range(lax.axis_size(axis...]
    ppermute x21 -> x36, starting transfers between devices: 24.1 us -> 42.9 us  [the longest x34 37.2 us: across(): lax.ppermute(array, axis, [(i, i ^ bit) for i in range(lax.axis_size(axis...]
    ppermute x3, waiting for transfers between devices: 23 us -> 6.71 us  [earlier_blocks(): lax.ppermute(state, axis, [(i, i + by) for i in range(peers - by)])]
    slice x11 -> x15, local copies, waits for them, and re-layouts: 5.9 us -> 14.7 us  [the longest x13 12.2 us: after(): zero = sum((other.reshape(-1)[0].astype(F32) * 0.0 for other in others))]
    reshape x1 -> x7, local copies, waits for them, and re-layouts: 0.35 us -> 8.5 us  [the longest x6 8.47 us: after(): zero = sum((other.reshape(-1)[0].astype(F32) * 0.0 for other in others))]
  transfers between devices with their start and end apart: 27 -> 41, of which waited for: 13 -> 17; matrix products, arithmetic and copies ran while one was open for 8% -> 14% of each run, Pallas kernels for 12% -> 7%
where the time goes in v3:
time: 380 us; the launch traced here: 378 us
  waiting for transfers between devices  139 us (37%)
  starting transfers between devices  62.9 us (17%)
  Pallas kernels  62.1 us (16%)
  local copies, waits for them, and re-layouts  43.6 us (11%)
  other arithmetic  35 us (9%)
  blocking collectives  26.5 us (7%)
  between operations  9.27 us (2%)
    ppermute x34, waiting for transfers between devices, across(): lax.ppermute(array, axis, [(i, i ^ bit) for i in range(lax.axis_size(axis...  116 us
    ppermute x34, starting transfers between devices, across(): lax.ppermute(array, axis, [(i, i ^ bit) for i in range(lax.axis_size(axis...  37.2 us
    pallas_call x2, Pallas kernels, window_rows(): call(functools.partial(window_kernel, heads), 2, [SMEM, SMEM, whole((mid,...  30.7 us
    all_to_all x1, blocking collectives, on_device(): lax.all_to_all(result, 'tensor', split_axis=0, concat_axis=0, tiled=True)  26.5 us
    select_n x23, other arithmetic, after(): return jnp.where(zero == 0.0, array, jnp.zeros_like(array))  26.4 us
    pallas_call x1, Pallas kernels, on_device(): call(functools.partial(linear_kernel, heads, feature_dim, kept), group_co...  13.4 us
    all_to_all x1, waiting for transfers between devices, on_device(): lax.all_to_all(outgoing, ('dp', 'seq'), split_axis=0, concat_axis=0, tile...  12.2 us
    slice x13, local copies, waits for them, and re-layouts, after(): zero = sum((other.reshape(-1)[0].astype(F32) * 0.0 for other in others))  12.2 us
  transfers between devices with their start and end apart: 41, of which 17 were waited for; matrix products, arithmetic and copies ran while one was open for 14% of the time, Pallas kernels for 7%

profile of v3, /device:TPU:0, one launch (start us, length us, event | category | flops | bytes accessed | tf_op | source)
XLA Modules:
  0.0 377.9 jit_solution(8699867912454441033)
XLA Ops:
  2.5 2.2 gather_fusion
  4.7 5.2 %all-to-all-start = ((bf16[8,8,4,1792]{3,2,1,0:T(4,128)(2,1)}), bf16[8,8,4,1792]{3,2,1,0:T(4,128)(2,1)S(1)}, u32[]{:S(2)}, u32[]{:S(2)}) async-start(bf16[8,8,4,1792]{3,2,1,0:T(4,128)(2,1)} %bitcast.5), calls=%async_computation | async-start | bytes 1835008 | tf_op jit(solution)/shard_map/all_to_all | solution.py:480
  11.1 12.2 %all-to-all-done = bf16[8,8,4,1792]{3,2,1,0:T(4,128)(2,1)S(1)} async-done(((bf16[8,8,4,1792]{3,2,1,0:T(4,128)(2,1)}), bf16[8,8,4,1792]{3,2,1,0:T(4,128)(2,1)S(1)}, u32[]{:S(2)}, u32[]{:S(2)}) %all-to-all-start) | async-done | bytes 917536 | tf_op jit(solution)/shard_map/all_to_all | solution.py:480
  23.3 1.3 gather_fusion.1
  25.7 4.9 %all-to-all-start.1 = ((bf16[4,16,4,1792]{3,1,2,0:T(8,128)(2,1)}), bf16[4,16,4,1792]{3,1,2,0:T(8,128)(2,1)S(1)}, u32[]{:S(2)}, u32[]{:S(2)}) async-start(bf16[4,16,4,1792]{3,1,2,0:T(8,128)(2,1)} %copy.42), calls=%async_computation.1 | async-start | bytes 1835008 | tf_op jit(solution)/shard_map/all_to_all | solution.py:487
  31.4 3.9 %collective-permute-start.5 = (bf16[144,896]{1,0:T(8,128)(2,1)S(1)}, bf16[144,896]{1,0:T(8,128)(2,1)S(1)}, u32[]{:S(2)}, u32[]{:S(2)}) collective-permute-start(bf16[144,896]{1,0:T(8,128)(2,1)S(1)} %pad_maximum_fusion.1), channel_id=1, source_target_pairs={{0,3},{1,2},{2,1},{3,0},{4,7},{5,6},{6,5},{7,4},{8,11},{9,10},{10,... | collective-permute-start | bytes 774152 | tf_op jit(solution)/shard_map/ppermute | solution.py:388
  35.9 1.3 reshape_reshape.4
  39.0 17.6 %collective-permute-done.5 = bf16[144,896]{1,0:T(8,128)(2,1)S(1)} collective-permute-done((bf16[144,896]{1,0:T(8,128)(2,1)S(1)}, bf16[144,896]{1,0:T(8,128)(2,1)S(1)}, u32[]{:S(2)}, u32[]{:S(2)}) %collective-permute-start.5) | collective-permute-done | bytes 258080 | tf_op jit(solution)/shard_map/ppermute | solution.py:388
  56.5 19.5 %collective-permute-done.4 = bf16[144,896]{1,0:T(8,128)(2,1)S(1)} collective-permute-done((bf16[144,896]{1,0:T(8,128)(2,1)S(1)}, bf16[144,896]{1,0:T(8,128)(2,1)S(1)}, u32[]{:S(2)}, u32[]{:S(2)}) %collective-permute-start.4) | collective-permute-done | bytes 258080 | tf_op jit(solution)/shard_map/ppermute | solution.py:388
  78.8 1.3 reshape.573
  80.0 1.2 slice.113
  81.9 13.9 %collective-permute-done.6 = bf16[3,144,896]{2,1,0:T(8,128)(2,1)} collective-permute-done((bf16[3,144,896]{2,1,0:T(8,128)(2,1)}, bf16[3,144,896]{2,1,0:T(8,128)(2,1)}, u32[]{:S(2)}, u32[]{:S(2)}) %collective-permute-start.6) | collective-permute-done | bytes 774176 | tf_op jit(solution)/shard_map/ppermute | solution.py:388
  95.8 1.7 slice_select_fusion.3
  101.5 3.3 collective-permute-start
  105.9 4.3 %collective-permute-done.2 = bf16[112,896]{1,0:T(8,128)(2,1)S(1)} collective-permute-done((bf16[112,896]{1,0:T(8,128)(2,1)S(1)}, bf16[112,896]{1,0:T(8,128)(2,1)S(1)}, u32[]{:S(2)}, u32[]{:S(2)}) %collective-permute-start.2) | collective-permute-done | bytes 200736 | tf_op jit(solution)/shard_map/ppermute | solution.py:388
  110.1 6.6 %collective-permute-done.1 = bf16[112,896]{1,0:T(8,128)(2,1)S(1)} collective-permute-done((bf16[112,896]{1,0:T(8,128)(2,1)S(1)}, bf16[112,896]{1,0:T(8,128)(2,1)S(1)}, u32[]{:S(2)}, u32[]{:S(2)}) %collective-permute-start.1) | collective-permute-done | bytes 200736 | tf_op jit(solution)/shard_map/ppermute | solution.py:388
  117.7 1.4 reshape.570
  122.1 2.9 maximum_select_fusion.near_ref
  127.8 3.1 collective-permute-done.10.far_ref
  130.9 13.4 %linear_rows.1 = (f32[4,256,512]{2,1,0:T(8,128)}, bf16[4,256,128]{2,1,0:T(8,128)(2,1)}, bf16[4,640,128]{2,1,0:T(8,128)(2,1)}) custom-call(s32[5]{0:T(128)} %pad_add_fusion.place_ref.refs_0_, bf16[256,1792]{1,0:T(8,128)(2,1)} %reshape.568.x_ref.refs_13_, f32[1,1792]{1,0:T(1,128)} %broadcast_in_dim.133.gain_ref, bf16[1,448,1792]{2,1,0:T(8,128)(2,1)} %bitcast.130, ...), custom_call_target="tpu_custom_call" | custom-call | flops 3170893824 | bytes 8257536 | tf_op jit(solution)/shard_map/linear_rows/pallas_call | solution.py:522
  144.3 3.4 collective-permute-start.11
  147.7 1.2 dynamic-slice_select_fusion
  149.0 2.1 collective-permute-start.18
  151.1 1.6 dynamic-slice_select_fusion.1
  152.8 1.7 collective-permute-start.16
  156.3 6.7 %collective-permute-done.11.refs_7_ = bf16[4,640,128]{2,1,0:T(8,128)(2,1)S(1)} collective-permute-done((bf16[4,640,128]{2,1,0:T(8,128)(2,1)}, bf16[4,640,128]{2,1,0:T(8,128)(2,1)S(1)}, u32[]{:S(2)}, u32[]{:S(2)}) %collective-permute-start.11) | collective-permute-done | bytes 655392 | tf_op jit(solution)/shard_map/ppermute | solution.py:422
  164.2 17.8 %collective-permute-done.19 = bf16[336,896]{1,0:T(8,128)(2,1)S(1)} collective-permute-done((bf16[336,896]{1,0:T(8,128)(2,1)S(1)}, bf16[336,896]{1,0:T(8,128)(2,1)S(1)}, u32[]{:S(2)}, u32[]{:S(2)}) %collective-permute-start.19) | collective-permute-done | bytes 602144 | tf_op jit(solution)/shard_map/ppermute | solution.py:388
  182.0 4.4 %collective-permute-start.12 = (bf16[4,640,128]{2,1,0:T(8,128)(2,1)}, bf16[4,640,128]{2,1,0:T(8,128)(2,1)}, u32[]{:S(2)}, u32[]{:S(2)}) collective-permute-start(bf16[4,640,128]{2,1,0:T(8,128)(2,1)} %get-tuple-element.12), channel_id=1, source_target_pairs={{0,8},{4,12},{1,9},{5,13},{2,10},{6,14},{3,11},{7,15},{16,24},{20,... | collective-permute-start | bytes 1966088 | tf_op jit(solution)/shard_map/ppermute | solution.py:422
  189.2 2.1 collective-permute-start.13
  194.1 9.3 %collective-permute-done.14 = bf16[112,896]{1,0:T(8,128)(2,1)S(1)} collective-permute-done((bf16[112,896]{1,0:T(8,128)(2,1)}, bf16[112,896]{1,0:T(8,128)(2,1)S(1)}, u32[]{:S(2)}, u32[]{:S(2)}) %collective-permute-start.14) | collective-permute-done | bytes 200736 | tf_op jit(solution)/shard_map/ppermute | solution.py:388
  203.5 1.4 select_n.341
  204.9 1.2 slice.120
  206.8 1.2 slice.117
  208.6 1.2 slice.118
  210.5 1.8 collective-permute-done.20
  213.5 1.7 maximum_select_fusion.1.refs_11_
  216.9 9.5 %collective-permute-start.25 = (bf16[1,336,896]{2,1,0:T(8,128)(2,1)}, bf16[1,336,896]{2,1,0:T(8,128)(2,1)}, u32[]{:S(2)}, u32[]{:S(2)}) collective-permute-start(bf16[1,336,896]{2,1,0:T(8,128)(2,1)} %fusion.1), channel_id=1, source_target_pairs={{0,4},{4,0},{8,12},{12,8},{1,5},{5,1},{9,13},{13,9},{2,6},{6,2},{1... | collective-permute-start | bytes 1806344 | tf_op jit(solution)/shard_map/ppermute | solution.py:388
  226.4 1.5 copy-done.6
  227.9 10.6 %linear_out.1 = (bf16[256,1792]{1,0:T(8,128)(2,1)}, bf16[256,1792]{1,0:T(8,128)(2,1)}) custom-call(s32[5]{0:T(128)} %pad_add_fusion.place_ref.refs_0_, f32[4,256,512]{2,1,0:T(8,128)} %get-tuple-element.10.refs_1_, bf16[4,256,128]{2,1,0:T(8,128)(2,1)} %get-tuple-element.11.refs_2_, bf16[128,1024]{1,0:T(8,128)(2,1)} %constant.130.clone.first_ref.refs_3_, ...), custom_call_target="tpu_custom_call" | custom-call | flops 2466250752 | bytes 6422528 | tf_op jit(solution)/shard_map/linear_out/pallas_call | solution.py:556
  238.4 2.3 reshape.581
  244.4 2.5 collective-permute-start.28
  246.9 6.9 %collective-permute-done.28 = bf16[1,160,896]{2,1,0:T(8,128)(2,1)S(1)} collective-permute-done((bf16[1,160,896]{2,1,0:T(8,128)(2,1)S(1)}, bf16[1,160,896]{2,1,0:T(8,128)(2,1)S(1)}, u32[]{:S(2)}, u32[]{:S(2)}) %collective-permute-start.28) | collective-permute-done | bytes 286752 | tf_op jit(solution)/shard_map/ppermute | solution.py:388
  257.3 1.9 maximum_select_fusion.2.near_ref
  260.3 1.3 collective-permute-start.34
  261.9 1.5 collective-permute-start.35
  263.5 2.3 collective-permute-start.30
  265.9 1.7 slice.96
  267.6 7.5 %collective-permute-done.31.high_ref = bf16[128,1792]{1,0:T(8,128)(2,1)} collective-permute-done((bf16[128,1792]{1,0:T(8,128)(2,1)}, bf16[128,1792]{1,0:T(8,128)(2,1)}, u32[]{:S(2)}, u32[]{:S(2)}) %collective-permute-start.31) | collective-permute-done | bytes 458784 | tf_op jit(solution)/shard_map/ppermute | solution.py:388
  275.1 3.3 collective-permute-start.32
  278.4 2.4 reshape.585
  280.7 1.2 slice.129
  283.5 1.6 collective-permute-start.37
  287.8 3.9 %collective-permute-done.37 = bf16[3,48,896]{2,1,0:T(8,128)(2,1)S(1)} collective-permute-done((bf16[3,48,896]{2,1,0:T(8,128)(2,1)S(1)}, bf16[3,48,896]{2,1,0:T(8,128)(2,1)S(1)}, u32[]{:S(2)}, u32[]{:S(2)}) %collective-permute-start.37) | collective-permute-done | bytes 258080 | tf_op jit(solution)/shard_map/ppermute | solution.py:388
  291.6 3.1 collective-permute-done.36
  294.8 15.4 %window_rows.3 = bf16[2,256,512]{2,1,0:T(8,128)(2,1)} custom-call(s32[5]{0:T(128)} %pad_add_fusion.place_ref.refs_0_, s32[1]{0:T(128)} %bitcast.2.first_ref, bf16[128,1792]{1,0:T(8,128)(2,1)} %copy-done.22, bf16[128,1792]{1,0:T(8,128)(2,1)} %collective-permute-done.31.high_ref, bf16[80,1792]{1,0:T(8,128)(2,1)} %collective-permute-done.32.halo_ref, ...), custom_call_target="tpu_custom_call" | custom-call | flops 3699376128 | bytes 9633792 | tf_op jit(solution)/shard_map/window_rows/pallas_call | solution.py:607
  310.1 1.2 copy.49
  312.5 1.9 maximum_select_fusion.3.near_ref
  314.5 2.4 collective-permute-start.23
  316.9 2.2 collective-permute-start.33
  320.5 3.4 collective-permute-done.23.halo_ref
  324.6 15.3 %window_rows.2.mixed_ref = bf16[2,256,512]{2,1,0:T(8,128)(2,1)} custom-call(s32[5]{0:T(128)} %pad_add_fusion.place_ref.refs_0_, s32[1]{0:T(128)} %bitcast.2.first_ref, bf16[256,1792]{1,0:T(8,128)(2,1)} %get-tuple-element.13.low_ref.high_ref, bf16[256,1792]{1,0:T(8,128)(2,1)} %get-tuple-element.13.low_ref.high_ref, bf16[80,1792]{1,0:T(8,128)(2,1)} %copy-done.26, ...), custom_call_target="tpu_custom_call" | custom-call | flops 3699376128 | bytes 9633792 | tf_op jit(solution)/shard_map/window_rows/pallas_call | solution.py:607
  340.8 7.5 %window_out.1 = bf16[256,1792]{1,0:T(8,128)(2,1)} custom-call(s32[5]{0:T(128)} %pad_add_fusion.place_ref.refs_0_, s32[1]{0:T(128)} %bitcast.1.live_ref, bf16[2,256,512]{2,1,0:T(8,128)(2,1)} %window_rows.2.mixed_ref, bf16[2,256,512]{2,1,0:T(8,128)(2,1)} %copy-done.21, bf16[1,448,1792]{2,1,0:T(8,128)(2,1)} %bitcast.94, bf16[4,3,112,896]{3,2,1,0:T(8,128)(2,1)} %copy-done.2, ...), custom_call_target="tpu_custom_call" | custom-call | flops 1644167168 | bytes 6422528 | tf_op jit(solution)/shard_map/window_out/pallas_call | solution.py:636
  348.3 1.9 reshape.586
  350.5 26.5 %all_to_all.15 = bf16[4,16,4,1792]{3,2,1,0:T(4,128)(2,1)S(1)} all-to-all(bf16[4,16,4,1792]{3,2,1,0:T(4,128)(2,1)S(1)} %bitcast.92), channel_id=1, replica_groups=mesh['dp'=2,'seq'=4,'tensor'=4] {'tensor'}, dimensions={0} | all-to-all | bytes 1835008 | tf_op jit(solution)/shard_map/all_to_all | solution.py:660
  (177 shorter events, 46.1 us)
Async XLA Ops:
  0.0 2.5 copy-start
  4.7 18.6 %all-to-all-start = ((bf16[8,8,4,1792]{3,2,1,0:T(4,128)(2,1)}), bf16[8,8,4,1792]{3,2,1,0:T(4,128)(2,1)S(1)}, u32[]{:S(2)}, u32[]{:S(2)}) async-start(bf16[8,8,4,1792]{3,2,1,0:T(4,128)(2,1)} %bitcast.5), calls=%async_computation | async-start | bytes 1835008 | tf_op jit(solution)/shard_map/all_to_all | solution.py:480
  25.7 52.6 %all-to-all-start.1 = ((bf16[4,16,4,1792]{3,1,2,0:T(8,128)(2,1)}), bf16[4,16,4,1792]{3,1,2,0:T(8,128)(2,1)S(1)}, u32[]{:S(2)}, u32[]{:S(2)}) async-start(bf16[4,16,4,1792]{3,1,2,0:T(8,128)(2,1)} %copy.42), calls=%async_computation.1 | async-start | bytes 1835008 | tf_op jit(solution)/shard_map/all_to_all | solution.py:487
  31.4 25.1 %collective-permute-start.5 = (bf16[144,896]{1,0:T(8,128)(2,1)S(1)}, bf16[144,896]{1,0:T(8,128)(2,1)S(1)}, u32[]{:S(2)}, u32[]{:S(2)}) collective-permute-start(bf16[144,896]{1,0:T(8,128)(2,1)S(1)} %pad_maximum_fusion.1), channel_id=1, source_target_pairs={{0,3},{1,2},{2,1},{3,0},{4,7},{5,6},{6,5},{7,4},{8,11},{9,10},{10,... | collective-permute-start | bytes 774152 | tf_op jit(solution)/shard_map/ppermute | solution.py:388
  35.3 40.8 %collective-permute-start.4 = (bf16[144,896]{1,0:T(8,128)(2,1)S(1)}, bf16[144,896]{1,0:T(8,128)(2,1)S(1)}, u32[]{:S(2)}, u32[]{:S(2)}) collective-permute-start(bf16[144,896]{1,0:T(8,128)(2,1)S(1)} %pad_maximum_fusion.1), channel_id=1, source_target_pairs={{0,2},{1,3},{2,0},{3,1},{4,6},{5,7},{6,4},{7,5},{8,10},{9,11},{10,... | collective-permute-start | bytes 774152 | tf_op jit(solution)/shard_map/ppermute | solution.py:388
  35.3 40.8 %collective-permute-start.3 = (bf16[144,896]{1,0:T(8,128)(2,1)S(1)}, bf16[144,896]{1,0:T(8,128)(2,1)S(1)}, u32[]{:S(2)}, u32[]{:S(2)}) collective-permute-start(bf16[144,896]{1,0:T(8,128)(2,1)S(1)} %pad_maximum_fusion.1), channel_id=1, source_target_pairs={{0,1},{1,0},{2,3},{3,2},{4,5},{5,4},{6,7},{7,6},{8,9},{9,8},{10,11... | collective-permute-start | bytes 774152 | tf_op jit(solution)/shard_map/ppermute | solution.py:388
  77.1 18.7 %collective-permute-start.6 = (bf16[3,144,896]{2,1,0:T(8,128)(2,1)}, bf16[3,144,896]{2,1,0:T(8,128)(2,1)}, u32[]{:S(2)}, u32[]{:S(2)}) collective-permute-start(bf16[3,144,896]{2,1,0:T(8,128)(2,1)} %maximum_select_fusion.5), channel_id=1, source_target_pairs={{0,4},{4,0},{8,12},{12,8},{1,5},{5,1},{9,13},{13,9},{2,6},{6,2},{1... | collective-permute-start | bytes 2322440 | tf_op jit(solution)/shard_map/ppermute | solution.py:388
  77.9 19.9 %collective-permute-start.7 = (bf16[3,144,896]{2,1,0:T(8,128)(2,1)}, bf16[3,144,896]{2,1,0:T(8,128)(2,1)S(1)}, u32[]{:S(2)}, u32[]{:S(2)}) collective-permute-start(bf16[3,144,896]{2,1,0:T(8,128)(2,1)} %maximum_select_fusion.5), channel_id=1, source_target_pairs={{0,8},{4,12},{8,0},{12,4},{1,9},{5,13},{9,1},{13,5},{2,10},{6,14},... | collective-permute-start | bytes 2322440 | tf_op jit(solution)/shard_map/ppermute | solution.py:388
  97.5 23.3 %collective-permute-start.9 = (bf16[3,64,896]{2,1,0:T(8,128)(2,1)}, bf16[3,64,896]{2,1,0:T(8,128)(2,1)}, u32[]{:S(2)}, u32[]{:S(2)}) collective-permute-start(bf16[3,64,896]{2,1,0:T(8,128)(2,1)} %slice_select_fusion.3), channel_id=1, source_target_pairs={{0,8},{4,12},{8,0},{12,4},{1,9},{5,13},{9,1},{13,5},{2,10},{6,14},... | collective-permute-start | bytes 1032200 | tf_op jit(solution)/shard_map/ppermute | solution.py:388
  98.6 22.3 %collective-permute-start.8 = (bf16[3,80,896]{2,1,0:T(8,128)(2,1)}, bf16[3,80,896]{2,1,0:T(8,128)(2,1)}, u32[]{:S(2)}, u32[]{:S(2)}) collective-permute-start(bf16[3,80,896]{2,1,0:T(8,128)(2,1)} %slice_select_fusion), channel_id=1, source_target_pairs={{0,4},{4,0},{8,12},{12,8},{1,5},{5,1},{9,13},{13,9},{2,6},{6,2},{1... | collective-permute-start | bytes 1290248 | tf_op jit(solution)/shard_map/ppermute | solution.py:388
  100.3 9.8 %collective-permute-start.2 = (bf16[112,896]{1,0:T(8,128)(2,1)S(1)}, bf16[112,896]{1,0:T(8,128)(2,1)S(1)}, u32[]{:S(2)}, u32[]{:S(2)}) collective-permute-start(bf16[112,896]{1,0:T(8,128)(2,1)S(1)} %dynamic-slice_select_fusion.2), channel_id=1, source_target_pairs={{0,3},{1,2},{2,1},{3,0},{4,7},{5,6},{6,5},{7,4},{8,11},{9,10},{10,... | collective-permute-start | bytes 602120 | tf_op jit(solution)/shard_map/ppermute | solution.py:388
  101.5 15.3 %collective-permute-start.1 = (bf16[112,896]{1,0:T(8,128)(2,1)S(1)}, bf16[112,896]{1,0:T(8,128)(2,1)S(1)}, u32[]{:S(2)}, u32[]{:S(2)}) collective-permute-start(bf16[112,896]{1,0:T(8,128)(2,1)S(1)} %dynamic-slice_select_fusion.2), channel_id=1, source_target_pairs={{0,2},{1,3},{2,0},{3,1},{4,6},{5,7},{6,4},{7,5},{8,10},{9,11},{10,... | collective-permute-start | bytes 602120 | tf_op jit(solution)/shard_map/ppermute | solution.py:388
  101.5 15.3 %collective-permute-start = (bf16[112,896]{1,0:T(8,128)(2,1)S(1)}, bf16[112,896]{1,0:T(8,128)(2,1)S(1)}, u32[]{:S(2)}, u32[]{:S(2)}) collective-permute-start(bf16[112,896]{1,0:T(8,128)(2,1)S(1)} %dynamic-slice_select_fusion.2), channel_id=1, source_target_pairs={{0,1},{1,0},{2,3},{3,2},{4,5},{5,4},{6,7},{7,6},{8,9},{9,8},{10,11... | collective-permute-start | bytes 602120 | tf_op jit(solution)/shard_map/ppermute | solution.py:388
  110.1 6.6 %copy-start.15 = (bf16[112,896]{1,0:T(8,128)(2,1)}, bf16[112,896]{1,0:T(8,128)(2,1)S(1)}, u32[]{:S(2)}) copy-start(bf16[112,896]{1,0:T(8,128)(2,1)S(1)} %collective-permute-done.2) | copy-start | bytes 602116
  122.1 2.9 copy-start.24
  125.0 5.9 %collective-permute-start.10 = (bf16[4,3,144,896]{3,2,1,0:T(8,128)(2,1)}, bf16[4,3,144,896]{3,2,1,0:T(8,128)(2,1)}, u32[]{:S(2)}, u32[]{:S(2)}) collective-permute-start(bf16[4,3,144,896]{3,2,1,0:T(8,128)(2,1)} %maximum_select_fusion.near_ref), channel_id=1, source_target_pairs={{0,16},{16,0},{1,17},{17,1},{2,18},{18,2},{3,19},{19,3},{4,20},{20... | collective-permute-start | bytes 9289736 | tf_op jit(solution)/shard_map/ppermute | solution.py:388
  144.3 18.7 %collective-permute-start.11 = (bf16[4,640,128]{2,1,0:T(8,128)(2,1)}, bf16[4,640,128]{2,1,0:T(8,128)(2,1)S(1)}, u32[]{:S(2)}, u32[]{:S(2)}) collective-permute-start(bf16[4,640,128]{2,1,0:T(8,128)(2,1)} %get-tuple-element.12), channel_id=1, source_target_pairs={{0,4},{4,8},{8,12},{1,5},{5,9},{9,13},{2,6},{6,10},{10,14},{3,7},{... | collective-permute-start | bytes 1966088 | tf_op jit(solution)/shard_map/ppermute | solution.py:422
  148.9 44.2 %copy-start.16 = (bf16[112,896]{1,0:T(8,128)(2,1)S(1)}, bf16[112,896]{1,0:T(8,128)(2,1)}, u32[]{:S(2)}) copy-start(bf16[112,896]{1,0:T(8,128)(2,1)} %copy-done.15) | copy-start | bytes 602116
  148.9 44.2 %copy-start.18 = (bf16[112,896]{1,0:T(8,128)(2,1)S(1)}, bf16[112,896]{1,0:T(8,128)(2,1)}, u32[]{:S(2)}) copy-start(bf16[112,896]{1,0:T(8,128)(2,1)} %copy-done.17) | copy-start | bytes 602116
  148.9 33.2 %collective-permute-start.19 = (bf16[336,896]{1,0:T(8,128)(2,1)S(1)}, bf16[336,896]{1,0:T(8,128)(2,1)S(1)}, u32[]{:S(2)}, u32[]{:S(2)}) collective-permute-start(bf16[336,896]{1,0:T(8,128)(2,1)S(1)} %bitcast.122), channel_id=1, source_target_pairs={{0,2},{1,3},{2,0},{3,1},{4,6},{5,7},{6,4},{7,5},{8,10},{9,11},{10,... | collective-permute-start | bytes 1806344 | tf_op jit(solution)/shard_map/ppermute | solution.py:388
  149.0 40.2 %collective-permute-start.18 = (bf16[3,112,896]{2,1,0:T(8,128)(2,1)}, bf16[3,112,896]{2,1,0:T(8,128)(2,1)S(1)}, u32[]{:S(2)}, u32[]{:S(2)}) collective-permute-start(bf16[3,112,896]{2,1,0:T(8,128)(2,1)} %get-tuple-element.21), channel_id=1, source_target_pairs={{0,8},{4,12},{8,0},{12,4},{1,9},{5,13},{9,1},{13,5},{2,10},{6,14},... | collective-permute-start | bytes 1806344 | tf_op jit(solution)/shard_map/ppermute | solution.py:388
  151.1 41.1 %collective-permute-start.17 = (bf16[3,112,896]{2,1,0:T(8,128)(2,1)}, bf16[3,112,896]{2,1,0:T(8,128)(2,1)S(1)}, u32[]{:S(2)}, u32[]{:S(2)}) collective-permute-start(bf16[3,112,896]{2,1,0:T(8,128)(2,1)} %get-tuple-element.21), channel_id=1, source_target_pairs={{0,4},{4,0},{8,12},{12,8},{1,5},{5,1},{9,13},{13,9},{2,6},{6,2},{1... | collective-permute-start | bytes 1806344 | tf_op jit(solution)/shard_map/ppermute | solution.py:388
  152.8 39.4 %collective-permute-start.16 = (bf16[112,896]{1,0:T(8,128)(2,1)}, bf16[112,896]{1,0:T(8,128)(2,1)S(1)}, u32[]{:S(2)}, u32[]{:S(2)}) collective-permute-start(bf16[112,896]{1,0:T(8,128)(2,1)} %dynamic-slice_select_fusion.1), channel_id=1, source_target_pairs={{0,3},{1,2},{2,1},{3,0},{4,7},{5,6},{6,5},{7,4},{8,11},{9,10},{10,... | collective-permute-start | bytes 602120 | tf_op jit(solution)/shard_map/ppermute | solution.py:388
  163.0 23.4 %copy-start.20 = (bf16[4,640,128]{2,1,0:T(8,128)(2,1)}, bf16[4,640,128]{2,1,0:T(8,128)(2,1)S(1)}, u32[]{:S(2)}) copy-start(bf16[4,640,128]{2,1,0:T(8,128)(2,1)S(1)} %collective-permute-done.11.refs_7_) | copy-start | bytes 1966084
  163.0 30.0 %collective-permute-start.15 = (bf16[112,896]{1,0:T(8,128)(2,1)}, bf16[112,896]{1,0:T(8,128)(2,1)S(1)}, u32[]{:S(2)}, u32[]{:S(2)}) collective-permute-start(bf16[112,896]{1,0:T(8,128)(2,1)} %dynamic-slice_select_fusion.1), channel_id=1, source_target_pairs={{0,1},{1,0},{2,3},{3,2},{4,5},{5,4},{6,7},{7,6},{8,9},{9,8},{10,11... | collective-permute-start | bytes 602120 | tf_op jit(solution)/shard_map/ppermute | solution.py:388
  182.0 24.7 %collective-permute-start.12 = (bf16[4,640,128]{2,1,0:T(8,128)(2,1)}, bf16[4,640,128]{2,1,0:T(8,128)(2,1)}, u32[]{:S(2)}, u32[]{:S(2)}) collective-permute-start(bf16[4,640,128]{2,1,0:T(8,128)(2,1)} %get-tuple-element.12), channel_id=1, source_target_pairs={{0,8},{4,12},{1,9},{5,13},{2,10},{6,14},{3,11},{7,15},{16,24},{20,... | collective-permute-start | bytes 1966088 | tf_op jit(solution)/shard_map/ppermute | solution.py:422
  189.2 15.7 %copy-start.11 = (bf16[3,112,896]{2,1,0:T(8,128)(2,1)}, bf16[3,112,896]{2,1,0:T(8,128)(2,1)S(1)}, u32[]{:S(2)}) copy-start(bf16[3,112,896]{2,1,0:T(8,128)(2,1)S(1)} %collective-permute-done.18) | copy-start | bytes 1806340
  189.2 19.4 %collective-permute-start.13 = (bf16[4,640,128]{2,1,0:T(8,128)(2,1)}, bf16[4,640,128]{2,1,0:T(8,128)(2,1)}, u32[]{:S(2)}, u32[]{:S(2)}) collective-permute-start(bf16[4,640,128]{2,1,0:T(8,128)(2,1)} %get-tuple-element.12), channel_id=1, source_target_pairs={{0,12},{1,13},{2,14},{3,15},{16,28},{17,29},{18,30},{19,31}} | collective-permute-start | bytes 1966088 | tf_op jit(solution)/shard_map/ppermute | solution.py:422
  192.1 11.3 %collective-permute-start.14 = (bf16[112,896]{1,0:T(8,128)(2,1)}, bf16[112,896]{1,0:T(8,128)(2,1)S(1)}, u32[]{:S(2)}, u32[]{:S(2)}) collective-permute-start(bf16[112,896]{1,0:T(8,128)(2,1)} %dynamic-slice_select_fusion.1), channel_id=1, source_target_pairs={{0,2},{1,3},{2,0},{3,1},{4,6},{5,7},{6,4},{7,5},{8,10},{9,11},{10,... | collective-permute-start | bytes 602120 | tf_op jit(solution)/shard_map/ppermute | solution.py:388
  192.1 11.3 %copy-start.13 = (bf16[3,112,896]{2,1,0:T(8,128)(2,1)}, bf16[3,112,896]{2,1,0:T(8,128)(2,1)S(1)}, u32[]{:S(2)}) copy-start(bf16[3,112,896]{2,1,0:T(8,128)(2,1)S(1)} %collective-permute-done.17) | copy-start | bytes 1806340
  192.1 20.1 %collective-permute-start.20 = (bf16[3,64,896]{2,1,0:T(8,128)(2,1)}, bf16[3,64,896]{2,1,0:T(8,128)(2,1)}, u32[]{:S(2)}, u32[]{:S(2)}) collective-permute-start(bf16[3,64,896]{2,1,0:T(8,128)(2,1)} %slice_select_fusion.2), channel_id=1, source_target_pairs={{0,4},{4,0},{8,12},{12,8},{1,5},{5,1},{9,13},{13,9},{2,6},{6,2},{1... | collective-permute-start | bytes 1032200 | tf_op jit(solution)/shard_map/ppermute | solution.py:388
  193.0 17.4 %collective-permute-start.21 = (bf16[3,48,896]{2,1,0:T(8,128)(2,1)}, bf16[3,48,896]{2,1,0:T(8,128)(2,1)}, u32[]{:S(2)}, u32[]{:S(2)}) collective-permute-start(bf16[3,48,896]{2,1,0:T(8,128)(2,1)} %slice_select_fusion.7), channel_id=1, source_target_pairs={{0,8},{4,12},{8,0},{12,4},{1,9},{5,13},{9,1},{13,5},{2,10},{6,14},... | collective-permute-start | bytes 774152 | tf_op jit(solution)/shard_map/ppermute | solution.py:388
  203.4 10.1 %copy-start.7 = (bf16[112,896]{1,0:T(8,128)(2,1)}, bf16[112,896]{1,0:T(8,128)(2,1)S(1)}, u32[]{:S(2)}) copy-start(bf16[112,896]{1,0:T(8,128)(2,1)S(1)} %collective-permute-done.14) | copy-start | bytes 602116
  213.5 2.8 copy-start.25
  215.2 12.7 %copy-start.3 = (bf16[4,3,112,896]{3,2,1,0:T(8,128)(2,1)}, bf16[4,3,112,896]{3,2,1,0:T(8,128)(2,1)S(1)}, u32[]{:S(2)}) copy-start(bf16[4,3,112,896]{3,2,1,0:T(8,128)(2,1)S(1)} %maximum_select_fusion.1.refs_11_) | copy-start | bytes 7225348
  215.2 11.2 %collective-permute-start.22 = (bf16[4,3,112,896]{3,2,1,0:T(8,128)(2,1)S(1)}, bf16[4,3,112,896]{3,2,1,0:T(8,128)(2,1)S(1)}, u32[]{:S(2)}, u32[]{:S(2)}) collective-permute-start(bf16[4,3,112,896]{3,2,1,0:T(8,128)(2,1)S(1)} %maximum_select_fusion.1.refs_11_), channel_id=1, source_target_pairs={{0,16},{16,0},{1,17},{17,1},{2,18},{18,2},{3,19},{19,3},{4,20},{20... | collective-permute-start | bytes 7225352 | tf_op jit(solution)/shard_map/ppermute | solution.py:388
  216.3 25.6 %collective-permute-start.26 = (bf16[1,336,896]{2,1,0:T(8,128)(2,1)}, bf16[1,336,896]{2,1,0:T(8,128)(2,1)S(1)}, u32[]{:S(2)}, u32[]{:S(2)}) collective-permute-start(bf16[1,336,896]{2,1,0:T(8,128)(2,1)} %fusion.1), channel_id=1, source_target_pairs={{0,8},{4,12},{8,0},{12,4},{1,9},{5,13},{9,1},{13,5},{2,10},{6,14},... | collective-permute-start | bytes 1806344 | tf_op jit(solution)/shard_map/ppermute | solution.py:388
  216.9 26.5 %collective-permute-start.25 = (bf16[1,336,896]{2,1,0:T(8,128)(2,1)}, bf16[1,336,896]{2,1,0:T(8,128)(2,1)}, u32[]{:S(2)}, u32[]{:S(2)}) collective-permute-start(bf16[1,336,896]{2,1,0:T(8,128)(2,1)} %fusion.1), channel_id=1, source_target_pairs={{0,4},{4,0},{8,12},{12,8},{1,5},{5,1},{9,13},{13,9},{2,6},{6,2},{1... | collective-permute-start | bytes 1806344 | tf_op jit(solution)/shard_map/ppermute | solution.py:388
  238.4 4.1 %copy-start.10 = (bf16[256,1792]{1,0:T(8,128)(2,1)S(1)}, bf16[256,1792]{1,0:T(8,128)(2,1)}, u32[]{:S(2)}) copy-start(bf16[256,1792]{1,0:T(8,128)(2,1)} %get-tuple-element.13.low_ref.high_ref) | copy-start | bytes 2752516
  241.9 14.3 %copy-start.12 = (bf16[1,336,896]{2,1,0:T(8,128)(2,1)}, bf16[1,336,896]{2,1,0:T(8,128)(2,1)S(1)}, u32[]{:S(2)}) copy-start(bf16[1,336,896]{2,1,0:T(8,128)(2,1)S(1)} %collective-permute-done.26) | copy-start | bytes 1806340
  242.0 15.4 %copy-start.5 = (bf16[1,1,336,896]{3,2,1,0:T(8,128)(2,1)S(1)}, bf16[1,1,336,896]{3,2,1,0:T(8,128)(2,1)}, u32[]{:S(2)}) copy-start(bf16[1,1,336,896]{3,2,1,0:T(8,128)(2,1)} %get-tuple-element.15) | copy-start | bytes 1806340
  242.0 11.8 %collective-permute-start.27 = (bf16[1,176,896]{2,1,0:T(8,128)(2,1)S(1)}, bf16[1,176,896]{2,1,0:T(8,128)(2,1)S(1)}, u32[]{:S(2)}, u32[]{:S(2)}) collective-permute-start(bf16[1,176,896]{2,1,0:T(8,128)(2,1)S(1)} %slice_select_fusion.4), channel_id=1, source_target_pairs={{0,4},{4,0},{8,12},{12,8},{1,5},{5,1},{9,13},{13,9},{2,6},{6,2},{1... | collective-permute-start | bytes 946184 | tf_op jit(solution)/shard_map/ppermute | solution.py:388
  243.4 12.3 %collective-permute-start.24 = (bf16[128,1792]{1,0:T(8,128)(2,1)S(1)}, bf16[128,1792]{1,0:T(8,128)(2,1)S(1)}, u32[]{:S(2)}, u32[]{:S(2)}) collective-permute-start(bf16[128,1792]{1,0:T(8,128)(2,1)S(1)} %get-tuple-element.20), channel_id=1, source_target_pairs={{0,1},{1,0},{2,3},{3,2},{4,5},{5,4},{6,7},{7,6},{8,9},{9,8},{10,11... | collective-permute-start | bytes 1376264 | tf_op jit(solution)/shard_map/ppermute | solution.py:388
  244.4 9.4 %collective-permute-start.28 = (bf16[1,160,896]{2,1,0:T(8,128)(2,1)S(1)}, bf16[1,160,896]{2,1,0:T(8,128)(2,1)S(1)}, u32[]{:S(2)}, u32[]{:S(2)}) collective-permute-start(bf16[1,160,896]{2,1,0:T(8,128)(2,1)S(1)} %slice_select_fusion.5), channel_id=1, source_target_pairs={{0,8},{4,12},{8,0},{12,4},{1,9},{5,13},{9,1},{13,5},{2,10},{6,14},... | collective-permute-start | bytes 860168 | tf_op jit(solution)/shard_map/ppermute | solution.py:388
  255.7 1.6 copy-start.22
  257.3 2.0 copy-start.8
  257.3 6.0 %copy-start.23 = (f32[3,3,448]{2,1,0:T(4,128)S(1)}, f32[3,3,448]{2,1,0:T(4,128)}, u32[]{:S(2)}) copy-start(f32[3,3,448]{2,1,0:T(4,128)} %param.27) | copy-start | bytes 48388
  259.3 28.5 %copy-start.4 = (bf16[4,1,336,896]{3,2,1,0:T(8,128)(2,1)}, bf16[4,1,336,896]{3,2,1,0:T(8,128)(2,1)S(1)}, u32[]{:S(2)}) copy-start(bf16[4,1,336,896]{3,2,1,0:T(8,128)(2,1)S(1)} %maximum_select_fusion.2.near_ref) | copy-start | bytes 7225348
  259.3 27.5 %copy-start.9 = (bf16[112,896]{1,0:T(8,128)(2,1)S(1)}, bf16[112,896]{1,0:T(8,128)(2,1)}, u32[]{:S(2)}) copy-start(bf16[112,896]{1,0:T(8,128)(2,1)} %copy-done.7) | copy-start | bytes 602116
  259.3 35.5 %collective-permute-start.29 = (bf16[4,1,336,896]{3,2,1,0:T(8,128)(2,1)S(1)}, bf16[4,1,336,896]{3,2,1,0:T(8,128)(2,1)}, u32[]{:S(2)}, u32[]{:S(2)}) collective-permute-start(bf16[4,1,336,896]{3,2,1,0:T(8,128)(2,1)S(1)} %maximum_select_fusion.2.near_ref), channel_id=1, source_target_pairs={{0,16},{16,0},{1,17},{17,1},{2,18},{18,2},{3,19},{19,3},{4,20},{20... | collective-permute-start | bytes 7225352 | tf_op jit(solution)/shard_map/ppermute | solution.py:388
  260.3 22.2 %collective-permute-start.34 = (bf16[3,112,896]{2,1,0:T(8,128)(2,1)}, bf16[3,112,896]{2,1,0:T(8,128)(2,1)}, u32[]{:S(2)}, u32[]{:S(2)}) collective-permute-start(bf16[3,112,896]{2,1,0:T(8,128)(2,1)} %broadcast_select_fusion), channel_id=1, source_target_pairs={{0,4},{4,0},{8,12},{12,8},{1,5},{5,1},{9,13},{13,9},{2,6},{6,2},{1... | collective-permute-start | bytes 1806344 | tf_op jit(solution)/shard_map/ppermute | solution.py:388
  261.6 13.5 %collective-permute-start.31 = (bf16[128,1792]{1,0:T(8,128)(2,1)}, bf16[128,1792]{1,0:T(8,128)(2,1)}, u32[]{:S(2)}, u32[]{:S(2)}) collective-permute-start(bf16[128,1792]{1,0:T(8,128)(2,1)} %get-tuple-element.19), channel_id=1, source_target_pairs={{0,1},{1,0},{2,3},{3,2},{4,5},{5,4},{6,7},{7,6},{8,9},{9,8},{10,11... | collective-permute-start | bytes 1376264 | tf_op jit(solution)/shard_map/ppermute | solution.py:388
  261.9 23.2 %collective-permute-start.35 = (bf16[3,112,896]{2,1,0:T(8,128)(2,1)}, bf16[3,112,896]{2,1,0:T(8,128)(2,1)}, u32[]{:S(2)}, u32[]{:S(2)}) collective-permute-start(bf16[3,112,896]{2,1,0:T(8,128)(2,1)} %broadcast_select_fusion), channel_id=1, source_target_pairs={{0,8},{4,12},{8,0},{12,4},{1,9},{5,13},{9,1},{13,5},{2,10},{6,14},... | collective-permute-start | bytes 1806344 | tf_op jit(solution)/shard_map/ppermute | solution.py:388
  263.5 22.7 %collective-permute-start.30 = (f32[3,1536]{1,0:T(4,128)S(1)}, f32[3,1536]{1,0:T(4,128)S(1)}, u32[]{:S(2)}, u32[]{:S(2)}) collective-permute-start(f32[3,1536]{1,0:T(4,128)S(1)} %reshape.583), channel_id=1, source_target_pairs={{0,2},{1,3},{2,0},{3,1},{4,6},{5,7},{6,4},{7,5},{8,10},{9,11},{10,... | collective-permute-start | bytes 55304 | tf_op jit(solution)/shard_map/ppermute | solution.py:388
  275.1 19.7 %collective-permute-start.32 = (bf16[80,1792]{1,0:T(8,128)(2,1)}, bf16[80,1792]{1,0:T(8,128)(2,1)}, u32[]{:S(2)}, u32[]{:S(2)}) collective-permute-start(bf16[80,1792]{1,0:T(8,128)(2,1)} %slice.96), channel_id=1, source_target_pairs={{0,5},{1,4},{2,7},{3,6},{4,9},{5,8},{6,11},{7,10},{8,13},{9,12},{1... | collective-permute-start | bytes 860168 | tf_op jit(solution)/shard_map/ppermute | solution.py:594
  283.5 8.1 %collective-permute-start.37 = (bf16[3,48,896]{2,1,0:T(8,128)(2,1)S(1)}, bf16[3,48,896]{2,1,0:T(8,128)(2,1)S(1)}, u32[]{:S(2)}, u32[]{:S(2)}) collective-permute-start(bf16[3,48,896]{2,1,0:T(8,128)(2,1)S(1)} %slice_select_fusion.6), channel_id=1, source_target_pairs={{0,8},{4,12},{8,0},{12,4},{1,9},{5,13},{9,1},{13,5},{2,10},{6,14},... | collective-permute-start | bytes 774152 | tf_op jit(solution)/shard_map/ppermute | solution.py:388
  286.1 8.6 %collective-permute-start.36 = (bf16[3,64,896]{2,1,0:T(8,128)(2,1)S(1)}, bf16[3,64,896]{2,1,0:T(8,128)(2,1)S(1)}, u32[]{:S(2)}, u32[]{:S(2)}) collective-permute-start(bf16[3,64,896]{2,1,0:T(8,128)(2,1)S(1)} %slice_select_fusion.1), channel_id=1, source_target_pairs={{0,4},{4,0},{8,12},{12,8},{1,5},{5,1},{9,13},{13,9},{2,6},{6,2},{1... | collective-permute-start | bytes 1032200 | tf_op jit(solution)/shard_map/ppermute | solution.py:388
  312.5 6.6 %copy-start.27 = (s32[8]{0:T(128)S(1)}, s32[8]{0:T(128)}, u32[]{:S(2)}) copy-start(s32[8]{0:T(128)} %param.20) | copy-start | bytes 100
  312.5 6.5 %copy-start.28 = (s32[8]{0:T(128)S(1)}, s32[8]{0:T(128)}, u32[]{:S(2)}) copy-start(s32[8]{0:T(128)} %param.19) | copy-start | bytes 100
  314.4 25.6 %copy-start.2 = (bf16[4,3,112,896]{3,2,1,0:T(8,128)(2,1)}, bf16[4,3,112,896]{3,2,1,0:T(8,128)(2,1)S(1)}, u32[]{:S(2)}) copy-start(bf16[4,3,112,896]{3,2,1,0:T(8,128)(2,1)S(1)} %maximum_select_fusion.3.near_ref) | copy-start | bytes 7225348
  314.4 25.6 %collective-permute-start.38 = (bf16[4,3,112,896]{3,2,1,0:T(8,128)(2,1)S(1)}, bf16[4,3,112,896]{3,2,1,0:T(8,128)(2,1)}, u32[]{:S(2)}, u32[]{:S(2)}) collective-permute-start(bf16[4,3,112,896]{3,2,1,0:T(8,128)(2,1)S(1)} %maximum_select_fusion.3.near_ref), channel_id=1, source_target_pairs={{0,16},{16,0},{1,17},{17,1},{2,18},{18,2},{3,19},{19,3},{4,20},{20... | collective-permute-start | bytes 7225352 | tf_op jit(solution)/shard_map/ppermute | solution.py:388
  314.5 9.4 %collective-permute-start.23 = (bf16[80,1792]{1,0:T(8,128)(2,1)}, bf16[80,1792]{1,0:T(8,128)(2,1)S(1)}, u32[]{:S(2)}, u32[]{:S(2)}) collective-permute-start(bf16[80,1792]{1,0:T(8,128)(2,1)} %slice.96), channel_id=1, source_target_pairs={{0,4},{4,8},{8,12},{1,5},{5,9},{9,13},{2,6},{6,10},{10,14},{3,7},{... | collective-permute-start | bytes 860168 | tf_op jit(solution)/shard_map/ppermute | solution.py:591
  316.9 23.1 %collective-permute-start.33 = (bf16[2,256,512]{2,1,0:T(8,128)(2,1)}, bf16[2,256,512]{2,1,0:T(8,128)(2,1)S(1)}, u32[]{:S(2)}, u32[]{:S(2)}) collective-permute-start(bf16[2,256,512]{2,1,0:T(8,128)(2,1)} %window_rows.3), channel_id=1, source_target_pairs={{0,1},{1,0},{2,3},{3,2},{4,5},{5,4},{6,7},{7,6},{8,9},{9,8},{10,11... | collective-permute-start | bytes 1572872 | tf_op jit(solution)/shard_map/ppermute | solution.py:388
  348.3 29.6 %copy-start.1 = (bf16[64,4,1792]{2,1,0:T(4,128)(2,1)S(1)}, bf16[64,4,1792]{2,1,0:T(4,128)(2,1)}, u32[]{:S(2)}) copy-start(bf16[64,4,1792]{2,1,0:T(4,128)(2,1)} %param.17) | copy-start | bytes 2752516
  (6 other events, 5.9 us)

commit v4 on v3

--- a/solution.py
+++ b/solution.py
@@ -357,7 +357,7 @@
 HBM = pl.BlockSpec(memory_space=pl.ANY)
 
 
-def call(kernel, groups, in_specs, out_specs, out_shape, scratch, flops, moved, name):
+def call(kernel, groups, in_specs, out_specs, out_shape, scratch, name):
     return pl.pallas_call(
         kernel,
         grid=(groups,),
@@ -368,7 +368,7 @@
         compiler_params=pltpu.CompilerParams(
             dimension_semantics=("arbitrary",), vmem_limit_bytes=VMEM
         ),
-        cost_estimate=pl.CostEstimate(flops=flops, bytes_accessed=moved, transcendentals=0),
+        cost_estimate=pl.CostEstimate(flops=0, bytes_accessed=0, transcendentals=0),
         name=name,
     )
 
@@ -391,7 +391,8 @@
 def after(array, others):
     if not others:
         return array
-    zero = sum(other.reshape(-1)[0].astype(F32) * 0.0 for other in others)
+    first = [lax.slice(other, (0,) * other.ndim, (1,) * other.ndim) for other in others]
+    zero = sum(one.reshape(()).astype(F32) * 0.0 for one in first)
     return jnp.where(zero == 0.0, array, jnp.zeros_like(array))
 
 
@@ -458,6 +459,13 @@
     feature_dim = feat_cols // heads
     tap_count = conv_window.shape[0]
 
+    assert heads == NEAR and dp_count == 2
+    values_t = w_value.T[None]
+    featmap_t = w_featmap.transpose(1, 2, 0)
+    window_t = w_window.transpose(1, 2, 0)
+    out_one, out_two = w_out_one[None], w_out_two[None]
+    held_one = from_groups(own_piece([values_t, featmap_t]), (1, 2, 3), ())
+
     placed = reassign[:, None] == jnp.arange(slots_total, dtype=jnp.int32)[None, :]
     table = jnp.sum(jnp.where(placed[:, :, None], page_table[None], 0), axis=1)
     slot_lengths = jnp.sum(jnp.where(placed, lengths[None, :], 0), axis=1)
@@ -483,20 +491,14 @@
     picked = arrived.reshape(groups * capacity, page_share, width)
     picked = picked.at[pick_rows].get(mode="promise_in_bounds")
 
-    picked = picked.reshape(req_dev, page_span, page_share, width)
+    picked = after(picked.reshape(req_dev, page_span, page_share, width), (held_one,))
     swapped = lax.all_to_all(picked, "tensor", split_axis=0, concat_axis=0, tiled=True)
     tokens = swapped.transpose(1, 0, 2, 3).reshape(rows, width)
     slot = dp_place * req_dev + tensor_place
     length = jnp.sum(jnp.where(jnp.arange(slots_total) == slot, slot_lengths, 0))
 
-    assert heads == NEAR and dp_count == 2
-    values_t = w_value.T[None]
-    featmap_t = w_featmap.transpose(1, 2, 0)
-    window_t = w_window.transpose(1, 2, 0)
-    out_one, out_two = w_out_one[None], w_out_two[None]
-    held_one = from_groups(own_piece([values_t, featmap_t]), (1, 2, 3), ())
     held_out_one = from_groups(own_piece([out_one]), (1, 2, 3), (picked,))
-    near_one = from_plane(held_one, (picked,), (swapped,), (held_out_one,))
+    near_one = from_plane(held_one, (picked,), (swapped,), ())
     held_window = from_groups(own_piece([window_t]), (2,), (swapped,))
     held_out_two = from_groups(own_piece([out_two]), (2, 1, 3), (swapped,))
     places = jnp.concatenate([(seq_place % NEAR) ^ jnp.arange(NEAR), dp_place[None]])
@@ -510,7 +512,6 @@
     first, second = jnp.asarray(first, BF16), jnp.asarray(second, BF16)
     column = np.zeros((1, heads * SLOT), np.float32)
     column[0, HEAD::SLOT] = 1
-    one_cols = 2 * feat_cols + head_cols
 
     def copy_sems(kinds):
         return pltpu.SemaphoreType.DMA((group_count, dp_count * NEAR * kinds))
@@ -544,15 +545,13 @@
             weights_of(2 * feature_dim),
             copy_sems(3),
         ],
-        3 * group_count * rows * width * one_cols,
-        group_count * width * one_cols * 2,
         "linear_rows",
     )(
         places, tokens, gain_one[None], values_t, featmap_t, *near_one, first, second, ones, column
     )
     priors = earlier_blocks(state, "seq")
     held_window, held_out_two = after(held_window, (state,)), after(held_out_two, (state,))
-    near_out_one = from_plane(held_out_one, (swapped,), (held_window,), [*priors, held_out_two])
+    near_out_one = from_plane(held_out_one, (swapped,), (state,), [*priors, held_window, held_out_two])
     residual, normed_two = call(
         functools.partial(out_one_kernel, heads, kept, len(priors)),
         group_count,
@@ -579,8 +578,6 @@
             weights_of(SLOT),
             copy_sems(1),
         ],
-        3 * group_count * rows * width * head_cols,
-        group_count * width * head_cols * 2,
         "linear_out",
     )(
         places, num, queries, first, second, ones, scale, *priors, out_one, *near_out_one, tokens,
@@ -600,7 +597,7 @@
             for j in range(group_count)
         ],
     )
-    near_window = from_plane(held_window, (priors[0],), (residual,), (pair_rows[0],))
+    near_window = from_plane(held_window, priors, (residual,), (pair_rows[0],))
     block_start = (seq_place * rows).astype(jnp.int32)[None]
 
     def window_rows(low, high, at, slot_halo):
@@ -623,8 +620,6 @@
                 pltpu.VMEM((2, dp_count, heads, 3 * SLOT, width // dp_count), BF16),
                 copy_sems(3),
             ],
-            6 * rows * width * 3 * head_cols,
-            2 * width * 3 * head_cols * 2,
             "window_rows",
         )(places, block_start, low, high, slot_halo, window_t, *near_window, taps)
 
@@ -651,8 +646,6 @@
             weights_of(SLOT),
             copy_sems(1),
         ],
-        2 * group_count * rows * width * head_cols,
-        group_count * width * head_cols * 2,
         "window_out",
     )(places, live, mixed_own, mixed_pair, out_two, *near_out_two, residual)
 

time: 380 us -> 363 us (0.955)
  local copies, waits for them, and re-layouts: 43.6 us -> 32.8 us
  other arithmetic: 35 us -> 24.3 us
  waiting for transfers between devices: 139 us -> 149 us
  starting transfers between devices: 62.9 us -> 58.7 us
    ppermute x34, waiting for transfers between devices: 116 us -> 142 us  [across(): lax.ppermute(array, axis, [(i, i ^ bit) for i in range(lax.axis_size(axis...]
    all_to_all x1, waiting for transfers between devices: 12.2 us -> 1.79 us  [on_device(): lax.all_to_all(outgoing, ('dp', 'seq'), split_axis=0, concat_axis=0, tile...]
    select_n x23 -> x22, other arithmetic: 26.4 us -> 16.6 us  [after(): return jnp.where(zero == 0.0, array, jnp.zeros_like(array))]
    reshape x7 -> x0, local copies, waits for them, and re-layouts: 9.49 us -> none  [the longest x6 8.47 us: after(): zero = sum((other.reshape(-1)[0].astype(F32) * 0.0 for other in others))]
    ppermute x3, waiting for transfers between devices: 6.71 us -> 0.01 us  [earlier_blocks(): lax.ppermute(state, axis, [(i, i + by) for i in range(peers - by)])]
    ppermute x34, starting transfers between devices: 37.2 us -> 32.2 us  [across(): lax.ppermute(array, axis, [(i, i ^ bit) for i in range(lax.axis_size(axis...]
  transfers between devices with their start and end apart: 41 -> 41, of which waited for: 17 -> 17; matrix products, arithmetic and copies ran while one was open for 14% -> 8% of each run, Pallas kernels for 7% -> 11%
where the time goes in v4:
time: 363 us; the launch traced here: 362 us
  waiting for transfers between devices  149 us (41%)
  Pallas kernels  62.1 us (17%)
  starting transfers between devices  58.7 us (16%)
  local copies, waits for them, and re-layouts  32.8 us (9%)
  blocking collectives  25.1 us (7%)
  other arithmetic  24.3 us (7%)
  between operations  9.63 us (3%)
    ppermute x34, waiting for transfers between devices, across(): lax.ppermute(array, axis, [(i, i ^ bit) for i in range(lax.axis_size(axis...  142 us
    ppermute x34, starting transfers between devices, across(): lax.ppermute(array, axis, [(i, i ^ bit) for i in range(lax.axis_size(axis...  32.2 us
    pallas_call x2, Pallas kernels, window_rows(): call(functools.partial(window_kernel, heads), 2, [SMEM, SMEM, whole((mid,...  30.7 us
    all_to_all x1, blocking collectives, on_device(): lax.all_to_all(result, 'tensor', split_axis=0, concat_axis=0, tiled=True)  25.1 us
    select_n x22, other arithmetic, after(): return jnp.where(zero == 0.0, array, jnp.zeros_like(array))  16.6 us
    pallas_call x1, Pallas kernels, on_device(): call(functools.partial(linear_kernel, heads, feature_dim, kept), group_co...  13.4 us
    pallas_call x1, Pallas kernels, on_device(): call(functools.partial(out_one_kernel, heads, kept, len(priors)), group_c...  10.6 us
    slice x13, local copies, waits for them, and re-layouts, after(): lax.slice(other, (0,) * other.ndim, (1,) * other.ndim)  9.64 us
  transfers between devices with their start and end apart: 41, of which 17 were waited for; matrix products, arithmetic and copies ran while one was open for 8% of the time, Pallas kernels for 11%

profile of v4, /device:TPU:0, one launch (start us, length us, event | category | flops | bytes accessed | tf_op | source)
XLA Modules:
  0.0 361.7 jit_solution(14087481606460091684)
XLA Ops:
  2.5 2.2 gather_fusion
  4.7 5.2 %all-to-all-start = ((bf16[8,8,4,1792]{3,2,1,0:T(4,128)(2,1)}), bf16[8,8,4,1792]{3,2,1,0:T(4,128)(2,1)S(1)}, u32[]{:S(2)}, u32[]{:S(2)}) async-start(bf16[8,8,4,1792]{3,2,1,0:T(4,128)(2,1)} %bitcast.10), calls=%async_computation | async-start | bytes 1835008 | tf_op jit(solution)/shard_map/all_to_all | solution.py:488
  11.6 1.6 collective-permute-start
  13.6 6.8 %collective-permute-done = bf16[144,896]{1,0:T(8,128)(2,1)S(1)} collective-permute-done((bf16[144,896]{1,0:T(8,128)(2,1)S(1)}, bf16[144,896]{1,0:T(8,128)(2,1)S(1)}, u32[]{:S(2)}, u32[]{:S(2)}) %collective-permute-start) | collective-permute-done | bytes 258080 | tf_op jit(solution)/shard_map/ppermute | solution.py:388
  21.5 1.8 all-to-all-done
  23.3 1.3 gather_fusion.1
  25.1 1.0 copy.40
  26.1 4.9 %all-to-all-start.1 = ((bf16[4,16,4,1792]{3,1,2,0:T(8,128)(2,1)}), bf16[4,16,4,1792]{3,1,2,0:T(8,128)(2,1)S(1)}, u32[]{:S(2)}, u32[]{:S(2)}) async-start(bf16[4,16,4,1792]{3,1,2,0:T(8,128)(2,1)} %copy.40), calls=%async_computation.1 | async-start | bytes 1835008 | tf_op jit(solution)/shard_map/all_to_all | solution.py:495
  31.0 3.8 %collective-permute-start.2 = (bf16[144,896]{1,0:T(8,128)(2,1)S(1)}, bf16[144,896]{1,0:T(8,128)(2,1)S(1)}, u32[]{:S(2)}, u32[]{:S(2)}) collective-permute-start(bf16[144,896]{1,0:T(8,128)(2,1)S(1)} %pad_maximum_fusion.1), channel_id=1, source_target_pairs={{0,3},{1,2},{2,1},{3,0},{4,7},{5,6},{6,5},{7,4},{8,11},{9,10},{10,... | collective-permute-start | bytes 774152 | tf_op jit(solution)/shard_map/ppermute | solution.py:388
  36.0 21.0 %collective-permute-done.2 = bf16[144,896]{1,0:T(8,128)(2,1)S(1)} collective-permute-done((bf16[144,896]{1,0:T(8,128)(2,1)S(1)}, bf16[144,896]{1,0:T(8,128)(2,1)S(1)}, u32[]{:S(2)}, u32[]{:S(2)}) %collective-permute-start.2) | collective-permute-done | bytes 258080 | tf_op jit(solution)/shard_map/ppermute | solution.py:388
  57.0 19.5 %collective-permute-done.1 = bf16[144,896]{1,0:T(8,128)(2,1)S(1)} collective-permute-done((bf16[144,896]{1,0:T(8,128)(2,1)S(1)}, bf16[144,896]{1,0:T(8,128)(2,1)S(1)}, u32[]{:S(2)}, u32[]{:S(2)}) %collective-permute-start.1) | collective-permute-done | bytes 258080 | tf_op jit(solution)/shard_map/ppermute | solution.py:388
  76.5 1.0 maximum_select_fusion.4
  79.9 16.2 %collective-permute-done.4 = bf16[3,144,896]{2,1,0:T(8,128)(2,1)S(1)} collective-permute-done((bf16[3,144,896]{2,1,0:T(8,128)(2,1)}, bf16[3,144,896]{2,1,0:T(8,128)(2,1)S(1)}, u32[]{:S(2)}, u32[]{:S(2)}) %collective-permute-start.4) | collective-permute-done | bytes 774176 | tf_op jit(solution)/shard_map/ppermute | solution.py:388
  97.0 1.5 collective-permute-start.6
  98.6 6.3 %collective-permute-done.6 = bf16[3,64,896]{2,1,0:T(8,128)(2,1)S(1)} collective-permute-done((bf16[3,64,896]{2,1,0:T(8,128)(2,1)S(1)}, bf16[3,64,896]{2,1,0:T(8,128)(2,1)S(1)}, u32[]{:S(2)}, u32[]{:S(2)}) %collective-permute-start.6) | collective-permute-done | bytes 344096 | tf_op jit(solution)/shard_map/ppermute | solution.py:388
  104.9 1.4 collective-permute-done.5
  106.4 1.9 pad_maximum_fusion.near_ref
  109.2 1.5 collective-permute-start.17
  110.7 2.9 collective-permute-start.15
  113.7 5.3 %collective-permute-done.17 = bf16[112,896]{1,0:T(8,128)(2,1)S(1)} collective-permute-done((bf16[112,896]{1,0:T(8,128)(2,1)S(1)}, bf16[112,896]{1,0:T(8,128)(2,1)S(1)}, u32[]{:S(2)}, u32[]{:S(2)}) %collective-permute-start.17) | collective-permute-done | bytes 200736 | tf_op jit(solution)/shard_map/ppermute | solution.py:388
  119.0 8.6 %collective-permute-done.16 = bf16[112,896]{1,0:T(8,128)(2,1)S(1)} collective-permute-done((bf16[112,896]{1,0:T(8,128)(2,1)S(1)}, bf16[112,896]{1,0:T(8,128)(2,1)S(1)}, u32[]{:S(2)}, u32[]{:S(2)}) %collective-permute-start.16) | collective-permute-done | bytes 200736 | tf_op jit(solution)/shard_map/ppermute | solution.py:388
  131.2 1.6 dynamic-slice_select_fusion.2
  132.9 2.5 collective-permute-start.14
  135.9 1.1 reshape.544.x_ref.refs_13_
  137.0 1.9 collective-permute-start.12
  138.9 13.4 %linear_rows.1 = (f32[4,256,512]{2,1,0:T(8,128)}, bf16[4,256,128]{2,1,0:T(8,128)(2,1)}, bf16[4,640,128]{2,1,0:T(8,128)(2,1)}) custom-call(s32[5]{0:T(128)} %pad_add_fusion.place_ref.refs_0_, bf16[256,1792]{1,0:T(8,128)(2,1)} %reshape.544.x_ref.refs_13_, f32[1,1792]{1,0:T(1,128)} %broadcast_in_dim.134.gain_ref, bf16[1,448,1792]{2,1,0:T(8,128)(2,1)} %bitcast.93, ...), custom_call_target="tpu_custom_call" | custom-call | tf_op jit(solution)/shard_map/linear_rows/pallas_call | solution.py:523
  152.3 1.3 slice.94
  155.2 1.1 collective-permute-start.21
  156.3 1.2 dynamic-slice_select_fusion
  157.5 1.2 collective-permute-start.11
  158.7 3.3 collective-permute-start.8
  162.1 2.7 collective-permute-start.9
  164.8 1.5 collective-permute-start.10
  167.9 28.0 %collective-permute-done.20 = bf16[3,64,896]{2,1,0:T(8,128)(2,1)S(1)} collective-permute-done((bf16[3,64,896]{2,1,0:T(8,128)(2,1)S(1)}, bf16[3,64,896]{2,1,0:T(8,128)(2,1)S(1)}, u32[]{:S(2)}, u32[]{:S(2)}) %collective-permute-start.20) | collective-permute-done | bytes 344096 | tf_op jit(solution)/shard_map/ppermute | solution.py:388
  201.8 1.2 fusion.3
  204.2 1.5 maximum_select_fusion.refs_11_
  206.7 2.5 collective-permute-start.25
  209.2 1.2 collective-permute-done.22.refs_12_
  210.4 1.5 copy-done.5
  211.9 10.6 %linear_out.1 = (bf16[256,1792]{1,0:T(8,128)(2,1)}, bf16[256,1792]{1,0:T(8,128)(2,1)}) custom-call(s32[5]{0:T(128)} %pad_add_fusion.place_ref.refs_0_, f32[4,256,512]{2,1,0:T(8,128)} %get-tuple-element.10.refs_1_, bf16[4,256,128]{2,1,0:T(8,128)(2,1)} %get-tuple-element.11.refs_2_, bf16[128,1024]{1,0:T(8,128)(2,1)} %constant.130.clone.first_ref.refs_3_, ...), custom_call_target="tpu_custom_call" | custom-call | tf_op jit(solution)/shard_map/linear_out/pallas_call | solution.py:555
  222.5 1.2 slice.102
  224.4 2.5 collective-permute-start.27
  227.0 2.0 fusion.16
  229.0 1.7 collective-permute-start.24
  230.9 8.3 %collective-permute-done.28 = bf16[1,160,896]{2,1,0:T(8,128)(2,1)S(1)} collective-permute-done((bf16[1,160,896]{2,1,0:T(8,128)(2,1)S(1)}, bf16[1,160,896]{2,1,0:T(8,128)(2,1)S(1)}, u32[]{:S(2)}, u32[]{:S(2)}) %collective-permute-start.28) | collective-permute-done | bytes 286752 | tf_op jit(solution)/shard_map/ppermute | solution.py:388
  239.3 2.1 collective-permute-done.24.low_ref
  242.5 1.7 maximum_select_fusion.1.near_ref
  245.7 1.7 collective-permute-start.31
  248.0 1.7 slice.99
  249.7 9.4 %collective-permute-done.31.high_ref = bf16[128,1792]{1,0:T(8,128)(2,1)} collective-permute-done((bf16[128,1792]{1,0:T(8,128)(2,1)}, bf16[128,1792]{1,0:T(8,128)(2,1)}, u32[]{:S(2)}, u32[]{:S(2)}) %collective-permute-start.31) | collective-permute-done | bytes 458784 | tf_op jit(solution)/shard_map/ppermute | solution.py:388
  259.2 4.5 %collective-permute-start.32 = (bf16[80,1792]{1,0:T(8,128)(2,1)}, bf16[80,1792]{1,0:T(8,128)(2,1)S(1)}, u32[]{:S(2)}, u32[]{:S(2)}) collective-permute-start(bf16[80,1792]{1,0:T(8,128)(2,1)} %slice.99), channel_id=1, source_target_pairs={{0,5},{1,4},{2,7},{3,6},{4,9},{5,8},{6,11},{7,10},{8,13},{9,12},{1... | collective-permute-start | bytes 860168 | tf_op jit(solution)/shard_map/ppermute | solution.py:591
  263.6 1.2 slice.130
  266.5 1.0 slice_select_fusion.1
  269.2 5.2 %collective-permute-done.37 = bf16[3,48,896]{2,1,0:T(8,128)(2,1)S(1)} collective-permute-done((bf16[3,48,896]{2,1,0:T(8,128)(2,1)S(1)}, bf16[3,48,896]{2,1,0:T(8,128)(2,1)S(1)}, u32[]{:S(2)}, u32[]{:S(2)}) %collective-permute-start.37) | collective-permute-done | bytes 258080 | tf_op jit(solution)/shard_map/ppermute | solution.py:388
  274.4 2.9 collective-permute-done.36
  278.1 15.3 %window_rows.3 = bf16[2,256,512]{2,1,0:T(8,128)(2,1)} custom-call(s32[5]{0:T(128)} %pad_add_fusion.place_ref.refs_0_, s32[1]{0:T(128)} %bitcast.2.first_ref, bf16[128,1792]{1,0:T(8,128)(2,1)} %copy-done.20, bf16[128,1792]{1,0:T(8,128)(2,1)} %collective-permute-done.31.high_ref, bf16[80,1792]{1,0:T(8,128)(2,1)} %copy-done.21, bf16[3,448,1792]{2,1,0:T(8,128)(2,1)} %bitcast.86, ...), custom_call_target="tpu_custom_call" | custom-call | tf_op jit(solution)/shard_map/window_rows/pallas_call | solution.py:604
  293.5 1.2 slice.129
  295.3 1.9 maximum_select_fusion.2.near_ref
  298.1 4.5 %collective-permute-start.23 = (bf16[80,1792]{1,0:T(8,128)(2,1)}, bf16[80,1792]{1,0:T(8,128)(2,1)S(1)}, u32[]{:S(2)}, u32[]{:S(2)}) collective-permute-start(bf16[80,1792]{1,0:T(8,128)(2,1)} %slice.99), channel_id=1, source_target_pairs={{0,4},{4,8},{8,12},{1,5},{5,9},{9,13},{2,6},{6,10},{10,14},{3,7},{... | collective-permute-start | bytes 860168 | tf_op jit(solution)/shard_map/ppermute | solution.py:588
  304.1 5.0 %collective-permute-done.23.halo_ref = bf16[80,1792]{1,0:T(8,128)(2,1)S(1)} collective-permute-done((bf16[80,1792]{1,0:T(8,128)(2,1)}, bf16[80,1792]{1,0:T(8,128)(2,1)S(1)}, u32[]{:S(2)}, u32[]{:S(2)}) %collective-permute-start.23) | collective-permute-done | bytes 286752 | tf_op jit(solution)/shard_map/ppermute | solution.py:588
  309.8 15.3 %window_rows.2.mixed_ref = bf16[2,256,512]{2,1,0:T(8,128)(2,1)} custom-call(s32[5]{0:T(128)} %pad_add_fusion.place_ref.refs_0_, s32[1]{0:T(128)} %bitcast.2.first_ref, bf16[256,1792]{1,0:T(8,128)(2,1)} %get-tuple-element.13.low_ref.high_ref, bf16[256,1792]{1,0:T(8,128)(2,1)} %get-tuple-element.13.low_ref.high_ref, bf16[80,1792]{1,0:T(8,128)(2,1)} %copy-done.22, ...), custom_call_target="tpu_custom_call" | custom-call | tf_op jit(solution)/shard_map/window_rows/pallas_call | solution.py:604
  326.0 7.5 %window_out.1 = bf16[256,1792]{1,0:T(8,128)(2,1)} custom-call(s32[5]{0:T(128)} %pad_add_fusion.place_ref.refs_0_, s32[1]{0:T(128)} %bitcast.1.live_ref, bf16[2,256,512]{2,1,0:T(8,128)(2,1)} %window_rows.2.mixed_ref, bf16[2,256,512]{2,1,0:T(8,128)(2,1)} %copy-done.19, bf16[1,448,1792]{2,1,0:T(8,128)(2,1)} %bitcast.94, bf16[4,3,112,896]{3,2,1,0:T(8,128)(2,1)} %copy-done.3, ...), custom_call_target="tpu_custom_call" | custom-call | tf_op jit(solution)/shard_map/window_out/pallas_call | solution.py:631
  333.5 1.9 reshape.549
  335.7 25.1 %all_to_all.15 = bf16[4,16,4,1792]{3,2,1,0:T(4,128)(2,1)S(1)} all-to-all(bf16[4,16,4,1792]{3,2,1,0:T(4,128)(2,1)S(1)} %bitcast.91), channel_id=1, replica_groups=mesh['dp'=2,'seq'=4,'tensor'=4] {'tensor'}, dimensions={0} | all-to-all | bytes 1835008 | tf_op jit(solution)/shard_map/all_to_all | solution.py:653
  (166 shorter events, 32.0 us)
Async XLA Ops:
  0.0 2.5 copy-start
  4.7 18.6 %all-to-all-start = ((bf16[8,8,4,1792]{3,2,1,0:T(4,128)(2,1)}), bf16[8,8,4,1792]{3,2,1,0:T(4,128)(2,1)S(1)}, u32[]{:S(2)}, u32[]{:S(2)}) async-start(bf16[8,8,4,1792]{3,2,1,0:T(4,128)(2,1)} %bitcast.10), calls=%async_computation | async-start | bytes 1835008 | tf_op jit(solution)/shard_map/all_to_all | solution.py:488
  11.6 8.7 %collective-permute-start = (bf16[144,896]{1,0:T(8,128)(2,1)S(1)}, bf16[144,896]{1,0:T(8,128)(2,1)S(1)}, u32[]{:S(2)}, u32[]{:S(2)}) collective-permute-start(bf16[144,896]{1,0:T(8,128)(2,1)S(1)} %pad_maximum_fusion.1), channel_id=1, source_target_pairs={{0,1},{1,0},{2,3},{3,2},{4,5},{5,4},{6,7},{7,6},{8,9},{9,8},{10,11... | collective-permute-start | bytes 774152 | tf_op jit(solution)/shard_map/ppermute | solution.py:388
  26.1 52.6 %all-to-all-start.1 = ((bf16[4,16,4,1792]{3,1,2,0:T(8,128)(2,1)}), bf16[4,16,4,1792]{3,1,2,0:T(8,128)(2,1)S(1)}, u32[]{:S(2)}, u32[]{:S(2)}) async-start(bf16[4,16,4,1792]{3,1,2,0:T(8,128)(2,1)} %copy.40), calls=%async_computation.1 | async-start | bytes 1835008 | tf_op jit(solution)/shard_map/all_to_all | solution.py:495
  31.0 26.0 %collective-permute-start.2 = (bf16[144,896]{1,0:T(8,128)(2,1)S(1)}, bf16[144,896]{1,0:T(8,128)(2,1)S(1)}, u32[]{:S(2)}, u32[]{:S(2)}) collective-permute-start(bf16[144,896]{1,0:T(8,128)(2,1)S(1)} %pad_maximum_fusion.1), channel_id=1, source_target_pairs={{0,3},{1,2},{2,1},{3,0},{4,7},{5,6},{6,5},{7,4},{8,11},{9,10},{10,... | collective-permute-start | bytes 774152 | tf_op jit(solution)/shard_map/ppermute | solution.py:388
  34.8 41.7 %collective-permute-start.1 = (bf16[144,896]{1,0:T(8,128)(2,1)S(1)}, bf16[144,896]{1,0:T(8,128)(2,1)S(1)}, u32[]{:S(2)}, u32[]{:S(2)}) collective-permute-start(bf16[144,896]{1,0:T(8,128)(2,1)S(1)} %pad_maximum_fusion.1), channel_id=1, source_target_pairs={{0,2},{1,3},{2,0},{3,1},{4,6},{5,7},{6,4},{7,5},{8,10},{9,11},{10,... | collective-permute-start | bytes 774152 | tf_op jit(solution)/shard_map/ppermute | solution.py:388
  77.5 18.6 %collective-permute-start.4 = (bf16[3,144,896]{2,1,0:T(8,128)(2,1)}, bf16[3,144,896]{2,1,0:T(8,128)(2,1)S(1)}, u32[]{:S(2)}, u32[]{:S(2)}) collective-permute-start(bf16[3,144,896]{2,1,0:T(8,128)(2,1)} %maximum_select_fusion.4), channel_id=1, source_target_pairs={{0,8},{4,12},{8,0},{12,4},{1,9},{5,13},{9,1},{13,5},{2,10},{6,14},... | collective-permute-start | bytes 2322440 | tf_op jit(solution)/shard_map/ppermute | solution.py:388
  77.9 19.0 %collective-permute-start.3 = (bf16[3,144,896]{2,1,0:T(8,128)(2,1)}, bf16[3,144,896]{2,1,0:T(8,128)(2,1)S(1)}, u32[]{:S(2)}, u32[]{:S(2)}) collective-permute-start(bf16[3,144,896]{2,1,0:T(8,128)(2,1)} %maximum_select_fusion.4), channel_id=1, source_target_pairs={{0,4},{4,0},{8,12},{12,8},{1,5},{5,1},{9,13},{13,9},{2,6},{6,2},{1... | collective-permute-start | bytes 2322440 | tf_op jit(solution)/shard_map/ppermute | solution.py:388
  96.2 10.1 %collective-permute-start.5 = (bf16[3,80,896]{2,1,0:T(8,128)(2,1)S(1)}, bf16[3,80,896]{2,1,0:T(8,128)(2,1)S(1)}, u32[]{:S(2)}, u32[]{:S(2)}) collective-permute-start(bf16[3,80,896]{2,1,0:T(8,128)(2,1)S(1)} %slice_select_fusion), channel_id=1, source_target_pairs={{0,4},{4,0},{8,12},{12,8},{1,5},{5,1},{9,13},{13,9},{2,6},{6,2},{1... | collective-permute-start | bytes 1290248 | tf_op jit(solution)/shard_map/ppermute | solution.py:388
  97.0 7.9 %collective-permute-start.6 = (bf16[3,64,896]{2,1,0:T(8,128)(2,1)S(1)}, bf16[3,64,896]{2,1,0:T(8,128)(2,1)S(1)}, u32[]{:S(2)}, u32[]{:S(2)}) collective-permute-start(bf16[3,64,896]{2,1,0:T(8,128)(2,1)S(1)} %slice_select_fusion.3), channel_id=1, source_target_pairs={{0,8},{4,12},{8,0},{12,4},{1,9},{5,13},{9,1},{13,5},{2,10},{6,14},... | collective-permute-start | bytes 1032200 | tf_op jit(solution)/shard_map/ppermute | solution.py:388
  106.4 23.6 %copy-start.24 = (f32[1792]{0:T(1024)S(1)}, f32[1792]{0:T(1024)}, u32[]{:S(2)}) copy-start(f32[1792]{0:T(1024)} %param.21) | copy-start | bytes 21508
  108.2 28.8 %collective-permute-start.7 = (bf16[4,3,144,896]{3,2,1,0:T(8,128)(2,1)}, bf16[4,3,144,896]{3,2,1,0:T(8,128)(2,1)}, u32[]{:S(2)}, u32[]{:S(2)}) collective-permute-start(bf16[4,3,144,896]{3,2,1,0:T(8,128)(2,1)} %pad_maximum_fusion.near_ref), channel_id=1, source_target_pairs={{0,16},{16,0},{1,17},{17,1},{2,18},{18,2},{3,19},{19,3},{4,20},{20... | collective-permute-start | bytes 9289736 | tf_op jit(solution)/shard_map/ppermute | solution.py:388
  109.2 9.8 %collective-permute-start.17 = (bf16[112,896]{1,0:T(8,128)(2,1)S(1)}, bf16[112,896]{1,0:T(8,128)(2,1)S(1)}, u32[]{:S(2)}, u32[]{:S(2)}) collective-permute-start(bf16[112,896]{1,0:T(8,128)(2,1)S(1)} %dynamic-slice_select_fusion.1), channel_id=1, source_target_pairs={{0,3},{1,2},{2,1},{3,0},{4,7},{5,6},{6,5},{7,4},{8,11},{9,10},{10,... | collective-permute-start | bytes 602120 | tf_op jit(solution)/shard_map/ppermute | solution.py:388
  110.7 16.9 %collective-permute-start.16 = (bf16[112,896]{1,0:T(8,128)(2,1)S(1)}, bf16[112,896]{1,0:T(8,128)(2,1)S(1)}, u32[]{:S(2)}, u32[]{:S(2)}) collective-permute-start(bf16[112,896]{1,0:T(8,128)(2,1)S(1)} %dynamic-slice_select_fusion.1), channel_id=1, source_target_pairs={{0,2},{1,3},{2,0},{3,1},{4,6},{5,7},{6,4},{7,5},{8,10},{9,11},{10,... | collective-permute-start | bytes 602120 | tf_op jit(solution)/shard_map/ppermute | solution.py:388
  110.7 16.9 %collective-permute-start.15 = (bf16[112,896]{1,0:T(8,128)(2,1)S(1)}, bf16[112,896]{1,0:T(8,128)(2,1)S(1)}, u32[]{:S(2)}, u32[]{:S(2)}) collective-permute-start(bf16[112,896]{1,0:T(8,128)(2,1)S(1)} %dynamic-slice_select_fusion.1), channel_id=1, source_target_pairs={{0,1},{1,0},{2,3},{3,2},{4,5},{5,4},{6,7},{7,6},{8,9},{9,8},{10,11... | collective-permute-start | bytes 602120 | tf_op jit(solution)/shard_map/ppermute | solution.py:388
  127.7 3.6 copy-start.14
  128.6 25.6 %collective-permute-start.18 = (bf16[3,112,896]{2,1,0:T(8,128)(2,1)}, bf16[3,112,896]{2,1,0:T(8,128)(2,1)}, u32[]{:S(2)}, u32[]{:S(2)}) collective-permute-start(bf16[3,112,896]{2,1,0:T(8,128)(2,1)} %maximum_select_fusion.7), channel_id=1, source_target_pairs={{0,4},{4,0},{8,12},{12,8},{1,5},{5,1},{9,13},{13,9},{2,6},{6,2},{1... | collective-permute-start | bytes 1806344 | tf_op jit(solution)/shard_map/ppermute | solution.py:388
  129.0 35.8 %collective-permute-start.19 = (bf16[3,112,896]{2,1,0:T(8,128)(2,1)}, bf16[3,112,896]{2,1,0:T(8,128)(2,1)S(1)}, u32[]{:S(2)}, u32[]{:S(2)}) collective-permute-start(bf16[3,112,896]{2,1,0:T(8,128)(2,1)} %maximum_select_fusion.7), channel_id=1, source_target_pairs={{0,8},{4,12},{8,0},{12,4},{1,9},{5,13},{9,1},{13,5},{2,10},{6,14},... | collective-permute-start | bytes 1806344 | tf_op jit(solution)/shard_map/ppermute | solution.py:388
  132.9 24.6 %collective-permute-start.14 = (bf16[112,896]{1,0:T(8,128)(2,1)}, bf16[112,896]{1,0:T(8,128)(2,1)S(1)}, u32[]{:S(2)}, u32[]{:S(2)}) collective-permute-start(bf16[112,896]{1,0:T(8,128)(2,1)} %dynamic-slice_select_fusion.2), channel_id=1, source_target_pairs={{0,3},{1,2},{2,1},{3,0},{4,7},{5,6},{6,5},{7,4},{8,11},{9,10},{10,... | collective-permute-start | bytes 602120 | tf_op jit(solution)/shard_map/ppermute | solution.py:388
  135.4 23.3 %collective-permute-start.13 = (bf16[112,896]{1,0:T(8,128)(2,1)}, bf16[112,896]{1,0:T(8,128)(2,1)S(1)}, u32[]{:S(2)}, u32[]{:S(2)}) collective-permute-start(bf16[112,896]{1,0:T(8,128)(2,1)} %dynamic-slice_select_fusion.2), channel_id=1, source_target_pairs={{0,1},{1,0},{2,3},{3,2},{4,5},{5,4},{6,7},{7,6},{8,9},{9,8},{10,11... | collective-permute-start | bytes 602120 | tf_op jit(solution)/shard_map/ppermute | solution.py:388
  137.0 25.1 %collective-permute-start.12 = (bf16[112,896]{1,0:T(8,128)(2,1)}, bf16[112,896]{1,0:T(8,128)(2,1)S(1)}, u32[]{:S(2)}, u32[]{:S(2)}) collective-permute-start(bf16[112,896]{1,0:T(8,128)(2,1)} %dynamic-slice_select_fusion.2), channel_id=1, source_target_pairs={{0,2},{1,3},{2,0},{3,1},{4,6},{5,7},{6,4},{7,5},{8,10},{9,11},{10,... | collective-permute-start | bytes 602120 | tf_op jit(solution)/shard_map/ppermute | solution.py:388
  152.3 14.2 %copy-start.15 = (bf16[112,896]{1,0:T(8,128)(2,1)S(1)}, bf16[112,896]{1,0:T(8,128)(2,1)}, u32[]{:S(2)}) copy-start(bf16[112,896]{1,0:T(8,128)(2,1)} %copy-done.14) | copy-start | bytes 602116
  155.2 11.2 %collective-permute-start.21 = (bf16[3,48,896]{2,1,0:T(8,128)(2,1)S(1)}, bf16[3,48,896]{2,1,0:T(8,128)(2,1)S(1)}, u32[]{:S(2)}, u32[]{:S(2)}) collective-permute-start(bf16[3,48,896]{2,1,0:T(8,128)(2,1)S(1)} %slice_select_fusion.7), channel_id=1, source_target_pairs={{0,8},{4,12},{8,0},{12,4},{1,9},{5,13},{9,1},{13,5},{2,10},{6,14},... | collective-permute-start | bytes 774152 | tf_op jit(solution)/shard_map/ppermute | solution.py:388
  157.5 44.3 %collective-permute-start.11 = (bf16[336,896]{1,0:T(8,128)(2,1)S(1)}, bf16[336,896]{1,0:T(8,128)(2,1)S(1)}, u32[]{:S(2)}, u32[]{:S(2)}) collective-permute-start(bf16[336,896]{1,0:T(8,128)(2,1)S(1)} %bitcast.123), channel_id=1, source_target_pairs={{0,2},{1,3},{2,0},{3,1},{4,6},{5,7},{6,4},{7,5},{8,10},{9,11},{10,... | collective-permute-start | bytes 1806344 | tf_op jit(solution)/shard_map/ppermute | solution.py:388
  158.7 44.3 %copy-start.7 = (bf16[112,896]{1,0:T(8,128)(2,1)}, bf16[112,896]{1,0:T(8,128)(2,1)S(1)}, u32[]{:S(2)}) copy-start(bf16[112,896]{1,0:T(8,128)(2,1)S(1)} %collective-permute-done.13) | copy-start | bytes 602116
  158.7 37.2 %collective-permute-start.8 = (bf16[4,640,128]{2,1,0:T(8,128)(2,1)}, bf16[4,640,128]{2,1,0:T(8,128)(2,1)S(1)}, u32[]{:S(2)}, u32[]{:S(2)}) collective-permute-start(bf16[4,640,128]{2,1,0:T(8,128)(2,1)} %get-tuple-element.12), channel_id=1, source_target_pairs={{0,4},{4,8},{8,12},{1,5},{5,9},{9,13},{2,6},{6,10},{10,14},{3,7},{... | collective-permute-start | bytes 1966088 | tf_op jit(solution)/shard_map/ppermute | solution.py:423
  162.1 41.0 %copy-start.9 = (bf16[112,896]{1,0:T(8,128)(2,1)}, bf16[112,896]{1,0:T(8,128)(2,1)S(1)}, u32[]{:S(2)}) copy-start(bf16[112,896]{1,0:T(8,128)(2,1)S(1)} %collective-permute-done.12) | copy-start | bytes 602116
  162.1 35.3 %collective-permute-start.9 = (bf16[4,640,128]{2,1,0:T(8,128)(2,1)}, bf16[4,640,128]{2,1,0:T(8,128)(2,1)S(1)}, u32[]{:S(2)}, u32[]{:S(2)}) collective-permute-start(bf16[4,640,128]{2,1,0:T(8,128)(2,1)} %get-tuple-element.12), channel_id=1, source_target_pairs={{0,8},{4,12},{1,9},{5,13},{2,10},{6,14},{3,11},{7,15},{16,24},{20,... | collective-permute-start | bytes 1966088 | tf_op jit(solution)/shard_map/ppermute | solution.py:423
  164.8 35.1 %collective-permute-start.10 = (bf16[4,640,128]{2,1,0:T(8,128)(2,1)}, bf16[4,640,128]{2,1,0:T(8,128)(2,1)S(1)}, u32[]{:S(2)}, u32[]{:S(2)}) collective-permute-start(bf16[4,640,128]{2,1,0:T(8,128)(2,1)} %get-tuple-element.12), channel_id=1, source_target_pairs={{0,12},{1,13},{2,14},{3,15},{16,28},{17,29},{18,30},{19,31}} | collective-permute-start | bytes 1966088 | tf_op jit(solution)/shard_map/ppermute | solution.py:423
  166.4 29.5 %collective-permute-start.20 = (bf16[3,64,896]{2,1,0:T(8,128)(2,1)S(1)}, bf16[3,64,896]{2,1,0:T(8,128)(2,1)S(1)}, u32[]{:S(2)}, u32[]{:S(2)}) collective-permute-start(bf16[3,64,896]{2,1,0:T(8,128)(2,1)S(1)} %slice_select_fusion.2), channel_id=1, source_target_pairs={{0,4},{4,0},{8,12},{12,8},{1,5},{5,1},{9,13},{13,9},{2,6},{6,2},{1... | collective-permute-start | bytes 1032200 | tf_op jit(solution)/shard_map/ppermute | solution.py:388
  195.9 0.9 copy-start.16
  204.2 1.7 copy-start.25
  205.8 6.2 %copy-start.4 = (bf16[4,3,112,896]{3,2,1,0:T(8,128)(2,1)}, bf16[4,3,112,896]{3,2,1,0:T(8,128)(2,1)S(1)}, u32[]{:S(2)}) copy-start(bf16[4,3,112,896]{3,2,1,0:T(8,128)(2,1)S(1)} %maximum_select_fusion.refs_11_) | copy-start | bytes 7225348
  205.8 4.7 %collective-permute-start.22 = (bf16[4,3,112,896]{3,2,1,0:T(8,128)(2,1)S(1)}, bf16[4,3,112,896]{3,2,1,0:T(8,128)(2,1)S(1)}, u32[]{:S(2)}, u32[]{:S(2)}) collective-permute-start(bf16[4,3,112,896]{3,2,1,0:T(8,128)(2,1)S(1)} %maximum_select_fusion.refs_11_), channel_id=1, source_target_pairs={{0,16},{16,0},{1,17},{17,1},{2,18},{18,2},{3,19},{19,3},{4,20},{20... | collective-permute-start | bytes 7225352 | tf_op jit(solution)/shard_map/ppermute | solution.py:388
  205.8 18.5 %collective-permute-start.26 = (bf16[1,336,896]{2,1,0:T(8,128)(2,1)}, bf16[1,336,896]{2,1,0:T(8,128)(2,1)S(1)}, u32[]{:S(2)}, u32[]{:S(2)}) collective-permute-start(bf16[1,336,896]{2,1,0:T(8,128)(2,1)} %get-tuple-element.20), channel_id=1, source_target_pairs={{0,8},{4,12},{8,0},{12,4},{1,9},{5,13},{9,1},{13,5},{2,10},{6,14},... | collective-permute-start | bytes 1806344 | tf_op jit(solution)/shard_map/ppermute | solution.py:388
  206.7 24.0 %collective-permute-start.25 = (bf16[1,336,896]{2,1,0:T(8,128)(2,1)}, bf16[1,336,896]{2,1,0:T(8,128)(2,1)S(1)}, u32[]{:S(2)}, u32[]{:S(2)}) collective-permute-start(bf16[1,336,896]{2,1,0:T(8,128)(2,1)} %get-tuple-element.20), channel_id=1, source_target_pairs={{0,4},{4,0},{8,12},{12,8},{1,5},{5,1},{9,13},{13,9},{2,6},{6,2},{1... | collective-permute-start | bytes 1806344 | tf_op jit(solution)/shard_map/ppermute | solution.py:388
  210.4 1.5 copy-start.5
  222.5 20.0 %copy-start.6 = (bf16[1,1,336,896]{3,2,1,0:T(8,128)(2,1)S(1)}, bf16[1,1,336,896]{3,2,1,0:T(8,128)(2,1)}, u32[]{:S(2)}) copy-start(bf16[1,1,336,896]{3,2,1,0:T(8,128)(2,1)} %get-tuple-element.19) | copy-start | bytes 1806340
  224.4 18.0 %copy-start.12 = (bf16[1,336,896]{2,1,0:T(8,128)(2,1)}, bf16[1,336,896]{2,1,0:T(8,128)(2,1)S(1)}, u32[]{:S(2)}) copy-start(bf16[1,336,896]{2,1,0:T(8,128)(2,1)S(1)} %collective-permute-done.26) | copy-start | bytes 1806340
  224.4 14.8 %collective-permute-start.27 = (bf16[1,176,896]{2,1,0:T(8,128)(2,1)S(1)}, bf16[1,176,896]{2,1,0:T(8,128)(2,1)S(1)}, u32[]{:S(2)}, u32[]{:S(2)}) collective-permute-start(bf16[1,176,896]{2,1,0:T(8,128)(2,1)S(1)} %slice_select_fusion.4), channel_id=1, source_target_pairs={{0,4},{4,0},{8,12},{12,8},{1,5},{5,1},{9,13},{13,9},{2,6},{6,2},{1... | collective-permute-start | bytes 946184 | tf_op jit(solution)/shard_map/ppermute | solution.py:388
  229.0 12.3 %collective-permute-start.24 = (bf16[128,1792]{1,0:T(8,128)(2,1)S(1)}, bf16[128,1792]{1,0:T(8,128)(2,1)S(1)}, u32[]{:S(2)}, u32[]{:S(2)}) collective-permute-start(bf16[128,1792]{1,0:T(8,128)(2,1)S(1)} %get-tuple-element.18), channel_id=1, source_target_pairs={{0,1},{1,0},{2,3},{3,2},{4,5},{5,4},{6,7},{7,6},{8,9},{9,8},{10,11... | collective-permute-start | bytes 1376264 | tf_op jit(solution)/shard_map/ppermute | solution.py:388
  230.8 11.7 %copy-start.13 = (bf16[1,336,896]{2,1,0:T(8,128)(2,1)}, bf16[1,336,896]{2,1,0:T(8,128)(2,1)S(1)}, u32[]{:S(2)}) copy-start(bf16[1,336,896]{2,1,0:T(8,128)(2,1)S(1)} %collective-permute-done.25) | copy-start | bytes 1806340
  230.8 8.4 %collective-permute-start.28 = (bf16[1,160,896]{2,1,0:T(8,128)(2,1)S(1)}, bf16[1,160,896]{2,1,0:T(8,128)(2,1)S(1)}, u32[]{:S(2)}, u32[]{:S(2)}) collective-permute-start(bf16[1,160,896]{2,1,0:T(8,128)(2,1)S(1)} %slice_select_fusion.5), channel_id=1, source_target_pairs={{0,8},{4,12},{8,0},{12,4},{1,9},{5,13},{9,1},{13,5},{2,10},{6,14},... | collective-permute-start | bytes 860168 | tf_op jit(solution)/shard_map/ppermute | solution.py:388
  241.3 1.1 copy-start.20
  242.5 1.9 copy-start.8
  242.5 1.9 copy-start.10
  242.5 5.0 %copy-start.23 = (f32[3,3,448]{2,1,0:T(4,128)S(1)}, f32[3,3,448]{2,1,0:T(4,128)}, u32[]{:S(2)}) copy-start(f32[3,3,448]{2,1,0:T(4,128)} %param.27) | copy-start | bytes 48388
  244.2 33.1 %copy-start.2 = (bf16[4,1,336,896]{3,2,1,0:T(8,128)(2,1)}, bf16[4,1,336,896]{3,2,1,0:T(8,128)(2,1)S(1)}, u32[]{:S(2)}) copy-start(bf16[4,1,336,896]{3,2,1,0:T(8,128)(2,1)S(1)} %maximum_select_fusion.1.near_ref) | copy-start | bytes 7225348
  244.2 24.0 %copy-start.11 = (bf16[112,896]{1,0:T(8,128)(2,1)S(1)}, bf16[112,896]{1,0:T(8,128)(2,1)}, u32[]{:S(2)}) copy-start(bf16[112,896]{1,0:T(8,128)(2,1)} %copy-done.9) | copy-start | bytes 602116
  244.3 33.2 %collective-permute-start.29 = (bf16[4,1,336,896]{3,2,1,0:T(8,128)(2,1)S(1)}, bf16[4,1,336,896]{3,2,1,0:T(8,128)(2,1)}, u32[]{:S(2)}, u32[]{:S(2)}) collective-permute-start(bf16[4,1,336,896]{3,2,1,0:T(8,128)(2,1)S(1)} %maximum_select_fusion.1.near_ref), channel_id=1, source_target_pairs={{0,16},{16,0},{1,17},{17,1},{2,18},{18,2},{3,19},{19,3},{4,20},{20... | collective-permute-start | bytes 7225352 | tf_op jit(solution)/shard_map/ppermute | solution.py:388
  245.3 20.2 %collective-permute-start.34 = (bf16[3,112,896]{2,1,0:T(8,128)(2,1)}, bf16[3,112,896]{2,1,0:T(8,128)(2,1)}, u32[]{:S(2)}, u32[]{:S(2)}) collective-permute-start(bf16[3,112,896]{2,1,0:T(8,128)(2,1)} %broadcast_select_fusion.1), channel_id=1, source_target_pairs={{0,4},{4,0},{8,12},{12,8},{1,5},{5,1},{9,13},{13,9},{2,6},{6,2},{1... | collective-permute-start | bytes 1806344 | tf_op jit(solution)/shard_map/ppermute | solution.py:388
  245.7 13.5 %collective-permute-start.31 = (bf16[128,1792]{1,0:T(8,128)(2,1)}, bf16[128,1792]{1,0:T(8,128)(2,1)}, u32[]{:S(2)}, u32[]{:S(2)}) collective-permute-start(bf16[128,1792]{1,0:T(8,128)(2,1)} %get-tuple-element.17), channel_id=1, source_target_pairs={{0,1},{1,0},{2,3},{3,2},{4,5},{5,4},{6,7},{7,6},{8,9},{9,8},{10,11... | collective-permute-start | bytes 1376264 | tf_op jit(solution)/shard_map/ppermute | solution.py:388
  247.4 19.1 %collective-permute-start.35 = (bf16[3,112,896]{2,1,0:T(8,128)(2,1)}, bf16[3,112,896]{2,1,0:T(8,128)(2,1)}, u32[]{:S(2)}, u32[]{:S(2)}) collective-permute-start(bf16[3,112,896]{2,1,0:T(8,128)(2,1)} %broadcast_select_fusion.1), channel_id=1, source_target_pairs={{0,8},{4,12},{8,0},{12,4},{1,9},{5,13},{9,1},{13,5},{2,10},{6,14},... | collective-permute-start | bytes 1806344 | tf_op jit(solution)/shard_map/ppermute | solution.py:388
  247.6 20.1 %collective-permute-start.30 = (f32[3,1536]{1,0:T(4,128)S(1)}, f32[3,1536]{1,0:T(4,128)S(1)}, u32[]{:S(2)}, u32[]{:S(2)}) collective-permute-start(f32[3,1536]{1,0:T(4,128)S(1)} %reshape.548), channel_id=1, source_target_pairs={{0,2},{1,3},{2,0},{3,1},{4,6},{5,7},{6,4},{7,5},{8,10},{9,11},{10,... | collective-permute-start | bytes 55304 | tf_op jit(solution)/shard_map/ppermute | solution.py:388
  259.2 18.2 %collective-permute-start.32 = (bf16[80,1792]{1,0:T(8,128)(2,1)}, bf16[80,1792]{1,0:T(8,128)(2,1)S(1)}, u32[]{:S(2)}, u32[]{:S(2)}) collective-permute-start(bf16[80,1792]{1,0:T(8,128)(2,1)} %slice.99), channel_id=1, source_target_pairs={{0,5},{1,4},{2,7},{3,6},{4,9},{5,8},{6,11},{7,10},{8,13},{9,12},{1... | collective-permute-start | bytes 860168 | tf_op jit(solution)/shard_map/ppermute | solution.py:591
  266.4 8.0 %collective-permute-start.37 = (bf16[3,48,896]{2,1,0:T(8,128)(2,1)S(1)}, bf16[3,48,896]{2,1,0:T(8,128)(2,1)S(1)}, u32[]{:S(2)}, u32[]{:S(2)}) collective-permute-start(bf16[3,48,896]{2,1,0:T(8,128)(2,1)S(1)} %slice_select_fusion.6), channel_id=1, source_target_pairs={{0,8},{4,12},{8,0},{12,4},{1,9},{5,13},{9,1},{13,5},{2,10},{6,14},... | collective-permute-start | bytes 774152 | tf_op jit(solution)/shard_map/ppermute | solution.py:388
  267.6 9.8 %collective-permute-start.36 = (bf16[3,64,896]{2,1,0:T(8,128)(2,1)S(1)}, bf16[3,64,896]{2,1,0:T(8,128)(2,1)S(1)}, u32[]{:S(2)}, u32[]{:S(2)}) collective-permute-start(bf16[3,64,896]{2,1,0:T(8,128)(2,1)S(1)} %slice_select_fusion.1), channel_id=1, source_target_pairs={{0,4},{4,0},{8,12},{12,8},{1,5},{5,1},{9,13},{13,9},{2,6},{6,2},{1... | collective-permute-start | bytes 1032200 | tf_op jit(solution)/shard_map/ppermute | solution.py:388
  295.3 7.4 %copy-start.26 = (s32[8]{0:T(128)S(1)}, s32[8]{0:T(128)}, u32[]{:S(2)}) copy-start(s32[8]{0:T(128)} %param.20) | copy-start | bytes 100
  295.3 7.4 %copy-start.27 = (s32[8]{0:T(128)S(1)}, s32[8]{0:T(128)}, u32[]{:S(2)}) copy-start(s32[8]{0:T(128)} %param.19) | copy-start | bytes 100
  297.2 28.0 %copy-start.3 = (bf16[4,3,112,896]{3,2,1,0:T(8,128)(2,1)}, bf16[4,3,112,896]{3,2,1,0:T(8,128)(2,1)S(1)}, u32[]{:S(2)}) copy-start(bf16[4,3,112,896]{3,2,1,0:T(8,128)(2,1)S(1)} %maximum_select_fusion.2.near_ref) | copy-start | bytes 7225348
  297.2 28.0 %collective-permute-start.38 = (bf16[4,3,112,896]{3,2,1,0:T(8,128)(2,1)S(1)}, bf16[4,3,112,896]{3,2,1,0:T(8,128)(2,1)}, u32[]{:S(2)}, u32[]{:S(2)}) collective-permute-start(bf16[4,3,112,896]{3,2,1,0:T(8,128)(2,1)S(1)} %maximum_select_fusion.2.near_ref), channel_id=1, source_target_pairs={{0,16},{16,0},{1,17},{17,1},{2,18},{18,2},{3,19},{19,3},{4,20},{20... | collective-permute-start | bytes 7225352 | tf_op jit(solution)/shard_map/ppermute | solution.py:388
  297.2 27.9 %collective-permute-start.33 = (bf16[2,256,512]{2,1,0:T(8,128)(2,1)}, bf16[2,256,512]{2,1,0:T(8,128)(2,1)S(1)}, u32[]{:S(2)}, u32[]{:S(2)}) collective-permute-start(bf16[2,256,512]{2,1,0:T(8,128)(2,1)} %window_rows.3), channel_id=1, source_target_pairs={{0,1},{1,0},{2,3},{3,2},{4,5},{5,4},{6,7},{7,6},{8,9},{9,8},{10,11... | collective-permute-start | bytes 1572872 | tf_op jit(solution)/shard_map/ppermute | solution.py:388
  298.1 11.0 %collective-permute-start.23 = (bf16[80,1792]{1,0:T(8,128)(2,1)}, bf16[80,1792]{1,0:T(8,128)(2,1)S(1)}, u32[]{:S(2)}, u32[]{:S(2)}) collective-permute-start(bf16[80,1792]{1,0:T(8,128)(2,1)} %slice.99), channel_id=1, source_target_pairs={{0,4},{4,8},{8,12},{1,5},{5,9},{9,13},{2,6},{6,10},{10,14},{3,7},{... | collective-permute-start | bytes 860168 | tf_op jit(solution)/shard_map/ppermute | solution.py:588
  333.5 28.3 %copy-start.1 = (bf16[64,4,1792]{2,1,0:T(4,128)(2,1)S(1)}, bf16[64,4,1792]{2,1,0:T(4,128)(2,1)}, u32[]{:S(2)}) copy-start(bf16[64,4,1792]{2,1,0:T(4,128)(2,1)} %param.17) | copy-start | bytes 2752516
  (5 other events, 3.9 us)

commit v5 on v4

--- a/solution.py
+++ b/solution.py
@@ -15,7 +15,7 @@
 FEAT_SLOT = 256
 HALO = 80
 NEAR = 4
-VMEM = 60 * 1024 * 1024
+VMEM = 32 * 1024 * 1024
 F32 = jnp.float32
 BF16 = jnp.bfloat16
 
@@ -201,13 +201,27 @@
 def out_one_kernel(
     heads,
     kept,
-    priors,
-    *refs,
+    place_ref,
+    num_ref,
+    q_ref,
+    first_ref,
+    second_ref,
+    ones_ref,
+    scale_ref,
+    prior_ref,
+    own_ref,
+    near_ref,
+    far_ref,
+    x_ref,
+    gain_ref,
+    residual_ref,
+    normed_ref,
+    tail_ref,
+    total_ref,
+    mixed_ref,
+    w_ref,
+    sems,
 ):
-    place_ref, num_ref, q_ref, first_ref, second_ref, ones_ref, scale_ref = refs[:7]
-    prior_refs = refs[7 : 7 + priors]
-    own_ref, near_ref, far_ref, x_ref, gain_ref = refs[7 + priors : 12 + priors]
-    residual_ref, normed_ref, total_ref, mixed_ref, w_ref, sems = refs[12 + priors :]
     step = pl.program_id(0)
 
     @pl.when(step == 0)
@@ -226,9 +240,7 @@
     query_features = (query_features * scale_ref[...]).astype(BF16)
     for h in range(heads):
         at = slice(h * kept, (h + 1) * kept)
-        prior = prior_refs[0][0, at, :].astype(F32)
-        for ref in prior_refs[1:]:
-            prior = prior + ref[0, at, :].astype(F32)
+        prior = prior_ref[0, at, :]
         lanes = slice(h * SLOT, (h + 1) * SLOT)
         total = num_ref[0, :, lanes] + dot(
             query_features[:, h * FEAT_SLOT : h * FEAT_SLOT + kept], prior.astype(BF16)
@@ -240,15 +252,16 @@
     def _():
         residual = (x_ref[...].astype(F32) + total_ref[...]).astype(BF16)
         residual_ref[...] = residual
-        normed_ref[...] = normed_rows(residual.astype(F32), gain_ref[...])
+        normed = normed_rows(residual.astype(F32), gain_ref[...])
+        normed_ref[...] = normed
+        tail_ref[...] = normed[-HALO:]
 
 
 def window_kernel(
     heads,
     place_ref,
     first_ref,
-    low_ref,
-    high_ref,
+    x_ref,
     halo_ref,
     own_ref,
     near_ref,
@@ -262,12 +275,9 @@
     step = pl.program_id(0)
     targets = [(own_ref, kind, HEAD, w_ref, kind * SLOT) for kind in range(3)]
 
-    mid = low_ref.shape[0]
-
     def place_rows():
         rows_ref[:HALO] = halo_ref[...]
-        rows_ref[HALO : HALO + mid] = low_ref[...]
-        rows_ref[HALO + mid :] = high_ref[...]
+        rows_ref[HALO:] = x_ref[...]
 
     @pl.when(step == 0)
     def _():
@@ -278,7 +288,7 @@
         w_ref.shape[0],
         place_rows,
     )
-    rows = 2 * mid
+    rows = x_ref.shape[0]
     lead = HALO - WINDOW
     projected = project(rows_ref, w_ref, step)
     taps = tap_ref[0]
@@ -396,22 +406,33 @@
     return jnp.where(zero == 0.0, array, jnp.zeros_like(array))
 
 
-def from_groups(piece, offsets, over_z):
+def settled(array, others=()):
+    return lax.optimization_barrier(after(array, others))
+
+
+def from_group(piece, over_z):
+    return across(after(piece, over_z), "tensor", 2)[None]
+
+
+def from_groups(piece, over_z, order=(0, 1, 2)):
     piece = after(piece, over_z)
-    return jnp.stack([across(piece, "tensor", offset) for offset in offsets])
-
-
-def from_plane(held, over_xy, diagonal, over_cores):
-    held = after(held, over_xy)
+    beside, beyond = across(piece, "tensor", 1), across(piece, "tensor", 2)
+    found = (beside, beyond, across(beyond, "tensor", 1))
+    return [found[n] for n in order]
+
+
+def neighbours(held):
+    return across(held, "seq", 1), across(held, "seq", 2)
+
+
+def from_plane(held, near_by, diagonal, over_cores):
     half = -(-held.shape[1] // 32) * 16
-    beside, above = across(held, "seq", 1), across(held, "seq", 2)
-    opposite = jnp.concatenate(
-        [
-            across(after(above[:, :half], diagonal), "seq", 1),
-            across(after(beside[:, half:], diagonal), "seq", 2),
-        ],
-        axis=1,
-    )
+    beside, above = near_by
+    opposite = [
+        across(after(above[:, :half], diagonal), "seq", 1),
+        across(after(beside[:, half:], diagonal), "seq", 2),
+    ]
+    opposite = after(jnp.concatenate(opposite, axis=1), over_cores)
     near = after(jnp.stack([held, beside, above, opposite]), over_cores)
     return near, across(near, "dp", 1)
 
@@ -419,13 +440,14 @@
 def earlier_blocks(state, axis):
     peers = lax.axis_size(axis)
     if peers <= 4:
-        return [
+        found = [
             lax.ppermute(state, axis, [(i, i + by) for i in range(peers - by)])
             for by in range(1, peers)
         ]
+        return sum(one.astype(F32) for one in found)
     everything = lax.all_gather(state, axis).astype(F32)
     reached = jnp.arange(peers) < lax.axis_index(axis)
-    return [jnp.sum(jnp.where(reached[:, None, None, None], everything, 0.0), axis=0)]
+    return jnp.sum(jnp.where(reached[:, None, None, None], everything, 0.0), axis=0)
 
 
 def on_device(
@@ -464,7 +486,7 @@
     featmap_t = w_featmap.transpose(1, 2, 0)
     window_t = w_window.transpose(1, 2, 0)
     out_one, out_two = w_out_one[None], w_out_two[None]
-    held_one = from_groups(own_piece([values_t, featmap_t]), (1, 2, 3), ())
+    held_one = settled(jnp.stack(from_groups(own_piece([values_t, featmap_t]), ())))
 
     placed = reassign[:, None] == jnp.arange(slots_total, dtype=jnp.int32)[None, :]
     table = jnp.sum(jnp.where(placed[:, :, None], page_table[None], 0), axis=1)
@@ -497,10 +519,10 @@
     slot = dp_place * req_dev + tensor_place
     length = jnp.sum(jnp.where(jnp.arange(slots_total) == slot, slot_lengths, 0))
 
-    held_out_one = from_groups(own_piece([out_one]), (1, 2, 3), (picked,))
-    near_one = from_plane(held_one, (picked,), (swapped,), ())
-    held_window = from_groups(own_piece([window_t]), (2,), (swapped,))
-    held_out_two = from_groups(own_piece([out_two]), (2, 1, 3), (swapped,))
+    held_out_one = settled(jnp.stack(from_groups(own_piece([out_one]), (picked,))))
+    near_one = from_plane(held_one, neighbours(held_one), (), (held_out_one,))
+    held_window = from_group(own_piece([window_t]), (swapped,))
+    held_out_two = from_groups(own_piece([out_two]), (swapped,), (1, 0, 2))
     places = jnp.concatenate([(seq_place % NEAR) ^ jnp.arange(NEAR), dp_place[None]])
     places = places.astype(jnp.int32)
     taps = conv_window.reshape(tap_count, 3, heads, HEAD).transpose(0, 2, 1, 3)
@@ -549,11 +571,14 @@
     )(
         places, tokens, gain_one[None], values_t, featmap_t, *near_one, first, second, ones, column
     )
-    priors = earlier_blocks(state, "seq")
-    held_window, held_out_two = after(held_window, (state,)), after(held_out_two, (state,))
-    near_out_one = from_plane(held_out_one, (swapped,), (state,), [*priors, held_window, held_out_two])
-    residual, normed_two = call(
-        functools.partial(out_one_kernel, heads, kept, len(priors)),
+    prior = settled(earlier_blocks(state, "seq"))
+    held_out_one = after(held_out_one, (swapped,))
+    near_out_one = from_plane(
+        held_out_one, neighbours(held_out_one), (state,), (prior, held_window)
+    )
+    held_out_two = settled(jnp.stack(held_out_two), (state,))
+    residual, normed_two, tail = call(
+        functools.partial(out_one_kernel, heads, kept),
         group_count,
         [
             SMEM,
@@ -564,14 +589,14 @@
             whole(ones.shape),
             whole(scale.shape),
         ]
-        + [each((heads * kept, SLOT))] * len(priors)
+        + [each((heads * kept, SLOT))]
         + [HBM] * 3
         + [
             whole((rows, width)),
             whole((1, width)),
         ],
-        [whole((rows, width)), whole((rows, width))],
-        [jax.ShapeDtypeStruct((rows, width), BF16)] * 2,
+        [whole((rows, width)), whole((rows, width)), whole((HALO, width))],
+        [jax.ShapeDtypeStruct((n, width), BF16) for n in (rows, rows, HALO)],
         [
             pltpu.VMEM((rows, width), F32),
             pltpu.VMEM((rows, slots), BF16),
@@ -580,14 +605,12 @@
         ],
         "linear_out",
     )(
-        places, num, queries, first, second, ones, scale, *priors, out_one, *near_out_one, tokens,
+        places, num, queries, first, second, ones, scale, prior, out_one, *near_out_one, tokens,
         gain_two[None],
     )
 
-    tail = normed_two[rows - HALO :]
     halo = lax.ppermute(tail, "seq", [(i, i + 1) for i in range(seq_count - 1)])
-    mid = rows // 2
-    pair_rows = [across(normed_two[at : at + mid], "tensor", 1) for at in (0, mid)]
+    pair_rows = across(normed_two, "tensor", 1)
     pair_halo = lax.ppermute(
         tail,
         ("seq", "tensor"),
@@ -597,18 +620,24 @@
             for j in range(group_count)
         ],
     )
-    near_window = from_plane(held_window, priors, (residual,), (pair_rows[0],))
+    held_window, held_out_two = after(held_window, (prior,)), after(held_out_two, (residual,))
+    near_by = neighbours(held_out_two)
+    near_window = from_plane(
+        held_window,
+        neighbours(held_window),
+        (residual, held_out_two),
+        (pair_rows, halo, pair_halo, *near_by),
+    )
     block_start = (seq_place * rows).astype(jnp.int32)[None]
 
-    def window_rows(low, high, at, slot_halo):
+    def window_rows(slot_rows, slot_halo):
         return call(
             functools.partial(window_kernel, heads),
             2,
             [
                 SMEM,
                 SMEM,
-                whole((mid, width)),
-                pl.BlockSpec((mid, width), lambda g: (at, 0)),
+                whole((rows, width)),
                 whole((HALO, width)),
                 *[HBM] * 3,
                 each((tap_count, 3 * slots)),
@@ -621,12 +650,12 @@
                 copy_sems(3),
             ],
             "window_rows",
-        )(places, block_start, low, high, slot_halo, window_t, *near_window, taps)
-
-    mixed_pair = window_rows(*pair_rows, 0, pair_halo)
-    near_out_two = from_plane(held_out_two, (pair_rows[0],), (pair_rows[1],), (mixed_pair,))
+        )(places, block_start, slot_rows, slot_halo, window_t, *near_window, taps)
+
+    mixed_pair = window_rows(pair_rows, pair_halo)
+    near_out_two = from_plane(held_out_two, near_by, (pair_rows,), (mixed_pair,))
     mixed_pair = across(mixed_pair, "tensor", 1)
-    mixed_own = window_rows(normed_two, normed_two, 1, halo)
+    mixed_own = window_rows(normed_two, halo)
     live = (length - seq_place * rows).astype(jnp.int32)[None]
     result = call(
         out_two_kernel,

time: 363 us -> 324 us (0.89)
  waiting for transfers between devices: 149 us -> 77.6 us
  blocking collectives: 25.1 us -> 56.1 us
  starting transfers between devices: 58.7 us -> 49.5 us
  other arithmetic: 24.3 us -> 28.5 us
    ppermute x34 -> x33, waiting for transfers between devices: 142 us -> 56.7 us  [across(): lax.ppermute(array, axis, [(i, i ^ bit) for i in range(lax.axis_size(axis...]
    all_to_all x0 -> x1, blocking collectives: none -> 29.1 us  [on_device(): lax.all_to_all(picked, 'tensor', split_axis=0, concat_axis=0, tiled=True)]
    ppermute x3, waiting for transfers between devices: 0.01 us -> 21 us  [earlier_blocks(): lax.ppermute(state, axis, [(i, i + by) for i in range(peers - by)])]
    unnamed x57 -> x77, local copies, waits for them, and re-layouts: 7.21 us -> 14 us
    ppermute x1, waiting for transfers between devices: 4.98 us -> 0.01 us  [on_device(): halo = lax.ppermute(tail, 'seq', [(i, i + 1) for i in range(seq_count - 1)])]
    all_to_all x1 -> x0, starting transfers between devices: 4.87 us -> none  [on_device(): lax.all_to_all(picked, 'tensor', split_axis=0, concat_axis=0, tiled=True)]
    select_n x22 -> x20, other arithmetic: 16.6 us -> 20.5 us  [after(): return jnp.where(zero == 0.0, array, jnp.zeros_like(array))]
    slice x13 -> x15, local copies, waits for them, and re-layouts: 9.64 us -> 9.35 us  [after(): lax.slice(other, (0,) * other.ndim, (1,) * other.ndim)]
  transfers between devices with their start and end apart: 41 -> 39, of which waited for: 17 -> 19; matrix products, arithmetic and copies ran while one was open for 8% -> 12% of each run, Pallas kernels for 11% -> 18%
where the time goes in v5:
time: 324 us; the launch traced here: 323 us
  waiting for transfers between devices  77.6 us (24%)
  Pallas kernels  65.3 us (20%)
  blocking collectives  56.1 us (17%)
  starting transfers between devices  49.5 us (15%)
  local copies, waits for them, and re-layouts  34.9 us (11%)
  other arithmetic  28.5 us (9%)
  between operations  10.8 us (3%)
    ppermute x33, waiting for transfers between devices, across(): lax.ppermute(array, axis, [(i, i ^ bit) for i in range(lax.axis_size(axis...  56.7 us
    ppermute x33, starting transfers between devices, across(): lax.ppermute(array, axis, [(i, i ^ bit) for i in range(lax.axis_size(axis...  32.3 us
    pallas_call x2, Pallas kernels, window_rows(): call(functools.partial(window_kernel, heads), 2, [SMEM, SMEM, whole((rows...  31.2 us
    all_to_all x1, blocking collectives, on_device(): lax.all_to_all(picked, 'tensor', split_axis=0, concat_axis=0, tiled=True)  29.1 us
    all_to_all x1, blocking collectives, on_device(): lax.all_to_all(result, 'tensor', split_axis=0, concat_axis=0, tiled=True)  27.1 us
    ppermute x3, waiting for transfers between devices, earlier_blocks(): lax.ppermute(state, axis, [(i, i + by) for i in range(peers - by)])  21 us
    select_n x20, other arithmetic, after(): return jnp.where(zero == 0.0, array, jnp.zeros_like(array))  20.5 us
    pallas_call x1, Pallas kernels, on_device(): call(functools.partial(linear_kernel, heads, feature_dim, kept), group_co...  15 us
  transfers between devices with their start and end apart: 39, of which 19 were waited for; matrix products, arithmetic and copies ran while one was open for 12% of the time, Pallas kernels for 18%

profile of v5, /device:TPU:0, one launch (start us, length us, event | category | flops | bytes accessed | tf_op | source)
XLA Modules:
  0.0 322.7 jit_solution(10186484886605495375)
XLA Ops:
  1.9 4.1 %collective-permute-start.1 = (bf16[144,896]{1,0:T(8,128)(2,1)S(1)}, bf16[144,896]{1,0:T(8,128)(2,1)S(1)}, u32[]{:S(2)}, u32[]{:S(2)}) collective-permute-start(bf16[144,896]{1,0:T(8,128)(2,1)S(1)} %pad_maximum_fusion.2), channel_id=1, source_target_pairs={{0,2},{1,3},{2,0},{3,1},{4,6},{5,7},{6,4},{7,5},{8,10},{9,11},{10,... | collective-permute-start | bytes 774152 | tf_op jit(solution)/shard_map/ppermute | solution.py:398
  8.4 2.2 gather_fusion
  10.6 3.7 %all-to-all-start = ((bf16[8,8,4,1792]{3,2,1,0:T(4,128)(2,1)}), bf16[8,8,4,1792]{3,2,1,0:T(4,128)(2,1)S(1)}, u32[]{:S(2)}, u32[]{:S(2)}) async-start(bf16[8,8,4,1792]{3,2,1,0:T(4,128)(2,1)} %bitcast.12), calls=%async_computation | async-start | bytes 1835008 | tf_op jit(solution)/shard_map/all_to_all | solution.py:510
  14.3 1.6 collective-permute-start
  16.0 1.8 collective-permute-done.1
  18.7 4.7 %collective-permute-done = bf16[144,896]{1,0:T(8,128)(2,1)S(1)} collective-permute-done((bf16[144,896]{1,0:T(8,128)(2,1)S(1)}, bf16[144,896]{1,0:T(8,128)(2,1)S(1)}, u32[]{:S(2)}, u32[]{:S(2)}) %collective-permute-start) | collective-permute-done | bytes 258080 | tf_op jit(solution)/shard_map/ppermute | solution.py:398
  23.4 5.4 %collective-permute-done.2 = bf16[144,896]{1,0:T(8,128)(2,1)S(1)} collective-permute-done((bf16[144,896]{1,0:T(8,128)(2,1)S(1)}, bf16[144,896]{1,0:T(8,128)(2,1)S(1)}, u32[]{:S(2)}, u32[]{:S(2)}) %collective-permute-start.2) | collective-permute-done | bytes 258080 | tf_op jit(solution)/shard_map/ppermute | solution.py:398
  28.9 1.6 collective-permute-start.7
  31.1 1.5 collective-permute-start.6
  33.3 1.4 gather_fusion.1
  37.3 1.6 collective-permute-start.4
  38.9 9.2 %collective-permute-done.7 = bf16[3,144,896]{2,1,0:T(8,128)(2,1)S(1)} collective-permute-done((bf16[3,144,896]{2,1,0:T(8,128)(2,1)S(1)}, bf16[3,144,896]{2,1,0:T(8,128)(2,1)S(1)}, u32[]{:S(2)}, u32[]{:S(2)}) %collective-permute-start.7) | collective-permute-done | bytes 774176 | tf_op jit(solution)/shard_map/ppermute | solution.py:398
  48.2 1.2 collective-permute-start.8
  50.7 1.3 collective-permute-start.9
  52.0 1.0 collective-permute-start.3
  54.0 5.2 %collective-permute-done.3 = bf16[112,896]{1,0:T(8,128)(2,1)S(1)} collective-permute-done((bf16[112,896]{1,0:T(8,128)(2,1)S(1)}, bf16[112,896]{1,0:T(8,128)(2,1)S(1)}, u32[]{:S(2)}, u32[]{:S(2)}) %collective-permute-start.3) | collective-permute-done | bytes 200736 | tf_op jit(solution)/shard_map/ppermute | solution.py:398
  59.3 2.1 collective-permute-done.5
  62.8 1.7 maximum_select_fusion.near_ref
  64.8 29.1 %all_to_all.15 = bf16[4,16,4,1792]{3,1,2,0:T(8,128)(2,1)S(1)} all-to-all(bf16[4,16,4,1792]{3,1,2,0:T(8,128)(2,1)S(1)} %copy.40), channel_id=1, replica_groups=mesh['dp'=2,'seq'=4,'tensor'=4] {'tensor'}, dimensions={0} | all-to-all | bytes 1835008 | tf_op jit(solution)/shard_map/all_to_all | solution.py:517
  95.0 2.1 dynamic-slice_select_fusion
  98.9 1.6 collective-permute-start.15
  100.5 1.4 copy.41
  101.9 2.4 reshape.559.x_ref
  104.3 1.2 copy-done.4
  105.5 1.4 copy-done.5
  108.9 15.0 %linear_rows.1 = (f32[4,256,512]{2,1,0:T(8,128)S(1)}, bf16[4,256,128]{2,1,0:T(8,128)(2,1)S(1)}, bf16[4,640,128]{2,1,0:T(8,128)(2,1)S(1)}) custom-call(s32[5]{0:T(128)S(1)} %pad_add_fusion.place_ref, bf16[256,1792]{1,0:T(8,128)(2,1)S(1)} %copy-done.4, f32[1,1792]{1,0:T(1,128)S(1)} %broadcast_in_dim.135.gain_ref, bf16[1,448,1792]{2,1,0:T(8,128)(2,1)S(1)} %bitcast.87, ...), custom_call_target="tpu_custom_call" | custom-call | tf_op jit(solution)/shard_map/linear_rows/pallas_call | solution.py:545
  123.9 3.3 %collective-permute-start.13 = (bf16[4,640,128]{2,1,0:T(8,128)(2,1)S(1)}, bf16[4,640,128]{2,1,0:T(8,128)(2,1)S(1)}, u32[]{:S(2)}, u32[]{:S(2)}) collective-permute-start(bf16[4,640,128]{2,1,0:T(8,128)(2,1)S(1)} %get-tuple-element.13), channel_id=1, source_target_pairs={{0,12},{1,13},{2,14},{3,15},{16,28},{17,29},{18,30},{19,31}} | collective-permute-start | bytes 1966088 | tf_op jit(solution)/shard_map/ppermute | solution.py:444
  127.1 1.3 collective-permute-start.12
  128.5 2.7 collective-permute-start.11
  131.2 1.2 slice.122
  136.4 5.9 %collective-permute-done.13 = bf16[4,640,128]{2,1,0:T(8,128)(2,1)S(1)} collective-permute-done((bf16[4,640,128]{2,1,0:T(8,128)(2,1)S(1)}, bf16[4,640,128]{2,1,0:T(8,128)(2,1)S(1)}, u32[]{:S(2)}, u32[]{:S(2)}) %collective-permute-start.13) | collective-permute-done | bytes 655392 | tf_op jit(solution)/shard_map/ppermute | solution.py:444
  142.3 15.1 %collective-permute-done.12 = bf16[4,640,128]{2,1,0:T(8,128)(2,1)S(1)} collective-permute-done((bf16[4,640,128]{2,1,0:T(8,128)(2,1)S(1)}, bf16[4,640,128]{2,1,0:T(8,128)(2,1)S(1)}, u32[]{:S(2)}, u32[]{:S(2)}) %collective-permute-start.12) | collective-permute-done | bytes 655392 | tf_op jit(solution)/shard_map/ppermute | solution.py:444
  158.7 2.1 collective-permute-done.18
  161.5 1.7 maximum_select_fusion.1.near_ref
  163.3 1.1 dynamic-slice_select_fusion.1
  164.3 2.7 collective-permute-start.23
  167.0 2.2 fusion.2
  169.3 2.5 collective-permute-start.28
  171.8 5.2 %collective-permute-done.23 = bf16[112,896]{1,0:T(8,128)(2,1)S(1)} collective-permute-done((bf16[112,896]{1,0:T(8,128)(2,1)S(1)}, bf16[112,896]{1,0:T(8,128)(2,1)S(1)}, u32[]{:S(2)}, u32[]{:S(2)}) %collective-permute-start.23) | collective-permute-done | bytes 200736 | tf_op jit(solution)/shard_map/ppermute | solution.py:398
  177.0 4.3 %collective-permute-done.24 = bf16[112,896]{1,0:T(8,128)(2,1)S(1)} collective-permute-done((bf16[112,896]{1,0:T(8,128)(2,1)S(1)}, bf16[112,896]{1,0:T(8,128)(2,1)S(1)}, u32[]{:S(2)}, u32[]{:S(2)}) %collective-permute-start.24) | collective-permute-done | bytes 200736 | tf_op jit(solution)/shard_map/ppermute | solution.py:398
  181.3 4.2 %collective-permute-done.25 = bf16[112,896]{1,0:T(8,128)(2,1)S(1)} collective-permute-done((bf16[112,896]{1,0:T(8,128)(2,1)S(1)}, bf16[112,896]{1,0:T(8,128)(2,1)S(1)}, u32[]{:S(2)}, u32[]{:S(2)}) %collective-permute-start.25) | collective-permute-done | bytes 200736 | tf_op jit(solution)/shard_map/ppermute | solution.py:398
  185.6 13.3 %linear_out.1 = (bf16[256,1792]{1,0:T(8,128)(2,1)S(1)}, bf16[256,1792]{1,0:T(8,128)(2,1)S(1)}, bf16[80,1792]{1,0:T(8,128)(2,1)S(1)}) custom-call(s32[5]{0:T(128)S(1)} %pad_add_fusion.place_ref, f32[4,256,512]{2,1,0:T(8,128)S(1)} %get-tuple-element.11.num_ref, bf16[4,256,128]{2,1,0:T(8,128)(2,1)S(1)} %get-tuple-element.12.q_ref, ...), custom_call_target="tpu_custom_call" | custom-call | tf_op jit(solution)/shard_map/linear_out/pallas_call | solution.py:580
  199.0 3.4 %collective-permute-start.20 = (bf16[80,1792]{1,0:T(8,128)(2,1)S(1)}, bf16[80,1792]{1,0:T(8,128)(2,1)S(1)}, u32[]{:S(2)}, u32[]{:S(2)}) collective-permute-start(bf16[80,1792]{1,0:T(8,128)(2,1)S(1)} %get-tuple-element.15), channel_id=1, source_target_pairs={{0,4},{4,8},{8,12},{1,5},{5,9},{9,13},{2,6},{6,10},{10,14},{3,7},{... | collective-permute-start | bytes 860168 | tf_op jit(solution)/shard_map/ppermute | solution.py:612
  202.3 2.9 collective-permute-start.22
  206.7 2.5 collective-permute-start.21
  213.0 1.7 slice_select_fusion.2
  214.7 3.0 collective-permute-start.30
  217.7 1.7 slice_select_fusion.3
  219.4 2.0 collective-permute-start.31
  223.5 7.5 %collective-permute-done.26 = bf16[3,112,896]{2,1,0:T(8,128)(2,1)S(1)} collective-permute-done((bf16[3,112,896]{2,1,0:T(8,128)(2,1)}, bf16[3,112,896]{2,1,0:T(8,128)(2,1)S(1)}, u32[]{:S(2)}, u32[]{:S(2)}) %collective-permute-start.26) | collective-permute-done | bytes 602144 | tf_op jit(solution)/shard_map/ppermute | solution.py:398
  235.4 1.7 collective-permute-done.30
  237.1 1.1 fusion
  238.2 1.9 maximum_select_fusion.2.near_ref
  240.4 1.0 slice_select_fusion.4
  243.4 1.7 collective-permute-done.33
  245.1 1.1 fusion.15
  246.3 2.4 copy-done.2
  248.6 16.0 %window_rows.3 = bf16[2,256,512]{2,1,0:T(8,128)(2,1)} custom-call(s32[5]{0:T(128)S(1)} %pad_add_fusion.place_ref, s32[1]{0:T(128)} %bitcast.2.first_ref, bf16[256,1792]{1,0:T(8,128)(2,1)S(1)} %collective-permute-done.21.x_ref, bf16[80,1792]{1,0:T(8,128)(2,1)S(1)} %copy-done.18, bf16[3,448,1792]{2,1,0:T(8,128)(2,1)S(1)} %bitcast.85, ...), custom_call_target="tpu_custom_call" | custom-call | tf_op jit(solution)/shard_map/window_rows/pallas_call | solution.py:634
  264.6 1.2 slice.133
  266.5 1.9 maximum_select_fusion.3.near_ref
  269.9 2.4 copy-done.3
  273.2 15.3 %window_rows.2.mixed_ref = bf16[2,256,512]{2,1,0:T(8,128)(2,1)S(1)} custom-call(s32[5]{0:T(128)S(1)} %pad_add_fusion.place_ref, s32[1]{0:T(128)} %bitcast.2.first_ref, bf16[256,1792]{1,0:T(8,128)(2,1)S(1)} %copy-done.13, bf16[80,1792]{1,0:T(8,128)(2,1)S(1)} %copy-done.16, bf16[3,448,1792]{2,1,0:T(8,128)(2,1)S(1)} %bitcast.86, ...), custom_call_target="tpu_custom_call" | custom-call | tf_op jit(solution)/shard_map/window_rows/pallas_call | solution.py:634
  288.5 5.7 %window_out.1 = bf16[256,1792]{1,0:T(8,128)(2,1)S(1)} custom-call(s32[5]{0:T(128)S(1)} %pad_add_fusion.place_ref, s32[1]{0:T(128)} %bitcast.1.live_ref, bf16[2,256,512]{2,1,0:T(8,128)(2,1)S(1)} %window_rows.2.mixed_ref, bf16[2,256,512]{2,1,0:T(8,128)(2,1)} %collective-permute-done.34.pair_ref, bf16[1,448,1792]{2,1,0:T(8,128)(2,1)S(1)} %bitcast.89, ...), custom_call_target="tpu_custom_call" | custom-call | tf_op jit(solution)/shard_map/window_out/pallas_call | solution.py:660
  294.7 27.1 %all_to_all.16 = bf16[4,16,4,1792]{3,2,1,0:T(4,128)(2,1)S(1)} all-to-all(bf16[4,16,4,1792]{3,2,1,0:T(4,128)(2,1)S(1)} %bitcast.94), channel_id=1, replica_groups=mesh['dp'=2,'seq'=4,'tensor'=4] {'tensor'}, dimensions={0} | all-to-all | bytes 1835008 | tf_op jit(solution)/shard_map/all_to_all | solution.py:682
  (184 shorter events, 32.8 us)
Async XLA Ops:
  0.0 8.4 %copy-start = (bf16[64,4,1792]{2,1,0:T(4,128)(2,1)S(1)}, bf16[64,4,1792]{2,1,0:T(4,128)(2,1)}, u32[]{:S(2)}) copy-start(bf16[64,4,1792]{2,1,0:T(4,128)(2,1)} %param.17) | copy-start | bytes 2752516
  1.9 15.9 %collective-permute-start.1 = (bf16[144,896]{1,0:T(8,128)(2,1)S(1)}, bf16[144,896]{1,0:T(8,128)(2,1)S(1)}, u32[]{:S(2)}, u32[]{:S(2)}) collective-permute-start(bf16[144,896]{1,0:T(8,128)(2,1)S(1)} %pad_maximum_fusion.2), channel_id=1, source_target_pairs={{0,2},{1,3},{2,0},{3,1},{4,6},{5,7},{6,4},{7,5},{8,10},{9,11},{10,... | collective-permute-start | bytes 774152 | tf_op jit(solution)/shard_map/ppermute | solution.py:398
  10.6 22.7 %all-to-all-start = ((bf16[8,8,4,1792]{3,2,1,0:T(4,128)(2,1)}), bf16[8,8,4,1792]{3,2,1,0:T(4,128)(2,1)S(1)}, u32[]{:S(2)}, u32[]{:S(2)}) async-start(bf16[8,8,4,1792]{3,2,1,0:T(4,128)(2,1)} %bitcast.12), calls=%async_computation | async-start | bytes 1835008 | tf_op jit(solution)/shard_map/all_to_all | solution.py:510
  14.3 9.1 %collective-permute-start = (bf16[144,896]{1,0:T(8,128)(2,1)S(1)}, bf16[144,896]{1,0:T(8,128)(2,1)S(1)}, u32[]{:S(2)}, u32[]{:S(2)}) collective-permute-start(bf16[144,896]{1,0:T(8,128)(2,1)S(1)} %pad_maximum_fusion.2), channel_id=1, source_target_pairs={{0,1},{1,0},{2,3},{3,2},{4,5},{5,4},{6,7},{7,6},{8,9},{9,8},{10,11... | collective-permute-start | bytes 774152 | tf_op jit(solution)/shard_map/ppermute | solution.py:398
  17.8 11.0 %collective-permute-start.2 = (bf16[144,896]{1,0:T(8,128)(2,1)S(1)}, bf16[144,896]{1,0:T(8,128)(2,1)S(1)}, u32[]{:S(2)}, u32[]{:S(2)}) collective-permute-start(bf16[144,896]{1,0:T(8,128)(2,1)S(1)} %collective-permute-done.1), channel_id=1, source_target_pairs={{0,1},{1,0},{2,3},{3,2},{4,5},{5,4},{6,7},{7,6},{8,9},{9,8},{10,11... | collective-permute-start | bytes 774152 | tf_op jit(solution)/shard_map/ppermute | solution.py:398
  28.9 6.2 %copy-start.25 = (bf16[3,144,896]{2,1,0:T(8,128)(2,1)}, bf16[3,144,896]{2,1,0:T(8,128)(2,1)S(1)}, u32[]{:S(2)}) copy-start(bf16[3,144,896]{2,1,0:T(8,128)(2,1)S(1)} %pad_maximum_fusion) | copy-start | bytes 2322436
  28.9 19.2 %collective-permute-start.7 = (bf16[3,144,896]{2,1,0:T(8,128)(2,1)S(1)}, bf16[3,144,896]{2,1,0:T(8,128)(2,1)S(1)}, u32[]{:S(2)}, u32[]{:S(2)}) collective-permute-start(bf16[3,144,896]{2,1,0:T(8,128)(2,1)S(1)} %pad_maximum_fusion), channel_id=1, source_target_pairs={{0,8},{4,12},{8,0},{12,4},{1,9},{5,13},{9,1},{13,5},{2,10},{6,14},... | collective-permute-start | bytes 2322440 | tf_op jit(solution)/shard_map/ppermute | solution.py:398
  31.1 18.6 %collective-permute-start.6 = (bf16[3,144,896]{2,1,0:T(8,128)(2,1)S(1)}, bf16[3,144,896]{2,1,0:T(8,128)(2,1)}, u32[]{:S(2)}, u32[]{:S(2)}) collective-permute-start(bf16[3,144,896]{2,1,0:T(8,128)(2,1)S(1)} %pad_maximum_fusion), channel_id=1, source_target_pairs={{0,4},{4,0},{8,12},{12,8},{1,5},{5,1},{9,13},{13,9},{2,6},{6,2},{1... | collective-permute-start | bytes 2322440 | tf_op jit(solution)/shard_map/ppermute | solution.py:398
  35.1 27.7 %copy-start.26 = (bf16[3,144,896]{2,1,0:T(8,128)(2,1)S(1)}, bf16[3,144,896]{2,1,0:T(8,128)(2,1)}, u32[]{:S(2)}) copy-start(bf16[3,144,896]{2,1,0:T(8,128)(2,1)} %copy-done.25) | copy-start | bytes 2322436
  37.3 15.8 %collective-permute-start.4 = (bf16[112,896]{1,0:T(8,128)(2,1)S(1)}, bf16[112,896]{1,0:T(8,128)(2,1)S(1)}, u32[]{:S(2)}, u32[]{:S(2)}) collective-permute-start(bf16[112,896]{1,0:T(8,128)(2,1)S(1)} %dynamic-slice_select_fusion.2), channel_id=1, source_target_pairs={{0,2},{1,3},{2,0},{3,1},{4,6},{5,7},{6,4},{7,5},{8,10},{9,11},{10,... | collective-permute-start | bytes 602120 | tf_op jit(solution)/shard_map/ppermute | solution.py:398
  48.2 14.7 %copy-start.27 = (bf16[3,144,896]{2,1,0:T(8,128)(2,1)}, bf16[3,144,896]{2,1,0:T(8,128)(2,1)S(1)}, u32[]{:S(2)}) copy-start(bf16[3,144,896]{2,1,0:T(8,128)(2,1)S(1)} %collective-permute-done.7) | copy-start | bytes 2322436
  48.2 14.5 %collective-permute-start.8 = (bf16[3,80,896]{2,1,0:T(8,128)(2,1)S(1)}, bf16[3,80,896]{2,1,0:T(8,128)(2,1)S(1)}, u32[]{:S(2)}, u32[]{:S(2)}) collective-permute-start(bf16[3,80,896]{2,1,0:T(8,128)(2,1)S(1)} %slice.118), channel_id=1, source_target_pairs={{0,4},{4,0},{8,12},{12,8},{1,5},{5,1},{9,13},{13,9},{2,6},{6,2},{1... | collective-permute-start | bytes 1290248 | tf_op jit(solution)/shard_map/ppermute | solution.py:398
  50.7 11.9 %collective-permute-start.9 = (bf16[3,64,896]{2,1,0:T(8,128)(2,1)S(1)}, bf16[3,64,896]{2,1,0:T(8,128)(2,1)S(1)}, u32[]{:S(2)}, u32[]{:S(2)}) collective-permute-start(bf16[3,64,896]{2,1,0:T(8,128)(2,1)S(1)} %slice.119), channel_id=1, source_target_pairs={{0,8},{4,12},{8,0},{12,4},{1,9},{5,13},{9,1},{13,5},{2,10},{6,14},... | collective-permute-start | bytes 1032200 | tf_op jit(solution)/shard_map/ppermute | solution.py:398
  52.0 7.3 %collective-permute-start.3 = (bf16[112,896]{1,0:T(8,128)(2,1)S(1)}, bf16[112,896]{1,0:T(8,128)(2,1)S(1)}, u32[]{:S(2)}, u32[]{:S(2)}) collective-permute-start(bf16[112,896]{1,0:T(8,128)(2,1)S(1)} %dynamic-slice_select_fusion.2), channel_id=1, source_target_pairs={{0,1},{1,0},{2,3},{3,2},{4,5},{5,4},{6,7},{7,6},{8,9},{9,8},{10,11... | collective-permute-start | bytes 602120 | tf_op jit(solution)/shard_map/ppermute | solution.py:398
  53.0 8.4 %collective-permute-start.5 = (bf16[112,896]{1,0:T(8,128)(2,1)S(1)}, bf16[112,896]{1,0:T(8,128)(2,1)S(1)}, u32[]{:S(2)}, u32[]{:S(2)}) collective-permute-start(bf16[112,896]{1,0:T(8,128)(2,1)S(1)} %collective-permute-done.4), channel_id=1, source_target_pairs={{0,1},{1,0},{2,3},{3,2},{4,5},{5,4},{6,7},{7,6},{8,9},{9,8},{10,11... | collective-permute-start | bytes 602120 | tf_op jit(solution)/shard_map/ppermute | solution.py:398
  61.5 35.8 %copy-start.23 = (bf16[3,112,896]{2,1,0:T(8,128)(2,1)}, bf16[3,112,896]{2,1,0:T(8,128)(2,1)S(1)}, u32[]{:S(2)}) copy-start(bf16[3,112,896]{2,1,0:T(8,128)(2,1)S(1)} %pad_maximum_fusion.1) | copy-start | bytes 1806340
  64.6 39.7 %collective-permute-start.10 = (bf16[4,3,144,896]{3,2,1,0:T(8,128)(2,1)S(1)}, bf16[4,3,144,896]{3,2,1,0:T(8,128)(2,1)}, u32[]{:S(2)}, u32[]{:S(2)}) collective-permute-start(bf16[4,3,144,896]{3,2,1,0:T(8,128)(2,1)S(1)} %maximum_select_fusion.near_ref), channel_id=1, source_target_pairs={{0,16},{16,0},{1,17},{17,1},{2,18},{18,2},{3,19},{19,3},{4,20},{20... | collective-permute-start | bytes 9289736 | tf_op jit(solution)/shard_map/ppermute | solution.py:398
  64.7 34.1 %copy-start.34 = (f32[1792]{0:T(1024)S(1)}, f32[1792]{0:T(1024)}, u32[]{:S(2)}) copy-start(f32[1792]{0:T(1024)} %param.21) | copy-start | bytes 21508
  97.1 7.2 %copy-start.8 = (bf16[128,1024]{1,0:T(8,128)(2,1)S(1)}, bf16[128,1024]{1,0:T(8,128)(2,1)}, u32[]{:S(2)}) copy-start(bf16[128,1024]{1,0:T(8,128)(2,1)} %constant.133.clone.first_ref) | copy-start | bytes 786436
  97.1 7.2 %copy-start.19 = (f32[2,1024]{1,0:T(2,128)S(1)}, f32[2,1024]{1,0:T(2,128)}, u32[]{:S(2)}) copy-start(f32[2,1024]{1,0:T(2,128)} %constant.135.clone.ones_ref) | copy-start | bytes 24580
  97.1 7.2 %copy-start.21 = (f32[1,512]{1,0:T(1,128)S(1)}, f32[1,512]{1,0:T(1,128)}, u32[]{:S(2)}) copy-start(f32[1,512]{1,0:T(1,128)} %constant.136.clone.column_ref) | copy-start | bytes 6148
  97.1 31.4 %collective-permute-start.14 = (bf16[336,896]{1,0:T(8,128)(2,1)}, bf16[336,896]{1,0:T(8,128)(2,1)}, u32[]{:S(2)}, u32[]{:S(2)}) collective-permute-start(bf16[336,896]{1,0:T(8,128)(2,1)} %bitcast.33), channel_id=1, source_target_pairs={{0,2},{1,3},{2,0},{3,1},{4,6},{5,7},{6,4},{7,5},{8,10},{9,11},{10,... | collective-permute-start | bytes 1806344 | tf_op jit(solution)/shard_map/ppermute | solution.py:398
  98.2 36.0 %collective-permute-start.16 = (bf16[3,112,896]{2,1,0:T(8,128)(2,1)}, bf16[3,112,896]{2,1,0:T(8,128)(2,1)}, u32[]{:S(2)}, u32[]{:S(2)}) collective-permute-start(bf16[3,112,896]{2,1,0:T(8,128)(2,1)} %broadcast_select_fusion.3), channel_id=1, source_target_pairs={{0,8},{4,12},{8,0},{12,4},{1,9},{5,13},{9,1},{13,5},{2,10},{6,14},... | collective-permute-start | bytes 1806344 | tf_op jit(solution)/shard_map/ppermute | solution.py:398
  98.9 36.4 %collective-permute-start.15 = (bf16[3,112,896]{2,1,0:T(8,128)(2,1)}, bf16[3,112,896]{2,1,0:T(8,128)(2,1)}, u32[]{:S(2)}, u32[]{:S(2)}) collective-permute-start(bf16[3,112,896]{2,1,0:T(8,128)(2,1)} %broadcast_select_fusion.3), channel_id=1, source_target_pairs={{0,4},{4,0},{8,12},{12,8},{1,5},{5,1},{9,13},{13,9},{2,6},{6,2},{1... | collective-permute-start | bytes 1806344 | tf_op jit(solution)/shard_map/ppermute | solution.py:398
  108.9 22.3 %copy-start.24 = (bf16[3,112,896]{2,1,0:T(8,128)(2,1)S(1)}, bf16[3,112,896]{2,1,0:T(8,128)(2,1)}, u32[]{:S(2)}) copy-start(bf16[3,112,896]{2,1,0:T(8,128)(2,1)} %copy-done.23) | copy-start | bytes 1806340
  123.9 18.4 %collective-permute-start.13 = (bf16[4,640,128]{2,1,0:T(8,128)(2,1)S(1)}, bf16[4,640,128]{2,1,0:T(8,128)(2,1)S(1)}, u32[]{:S(2)}, u32[]{:S(2)}) collective-permute-start(bf16[4,640,128]{2,1,0:T(8,128)(2,1)S(1)} %get-tuple-element.13), channel_id=1, source_target_pairs={{0,12},{1,13},{2,14},{3,15},{16,28},{17,29},{18,30},{19,31}} | collective-permute-start | bytes 1966088 | tf_op jit(solution)/shard_map/ppermute | solution.py:444
  127.1 30.2 %collective-permute-start.12 = (bf16[4,640,128]{2,1,0:T(8,128)(2,1)S(1)}, bf16[4,640,128]{2,1,0:T(8,128)(2,1)S(1)}, u32[]{:S(2)}, u32[]{:S(2)}) collective-permute-start(bf16[4,640,128]{2,1,0:T(8,128)(2,1)S(1)} %get-tuple-element.13), channel_id=1, source_target_pairs={{0,8},{4,12},{1,9},{5,13},{2,10},{6,14},{3,11},{7,15},{16,24},{20,... | collective-permute-start | bytes 1966088 | tf_op jit(solution)/shard_map/ppermute | solution.py:444
  128.5 28.9 %collective-permute-start.11 = (bf16[4,640,128]{2,1,0:T(8,128)(2,1)S(1)}, bf16[4,640,128]{2,1,0:T(8,128)(2,1)S(1)}, u32[]{:S(2)}, u32[]{:S(2)}) collective-permute-start(bf16[4,640,128]{2,1,0:T(8,128)(2,1)S(1)} %get-tuple-element.13), channel_id=1, source_target_pairs={{0,4},{4,8},{8,12},{1,5},{5,9},{9,13},{2,6},{6,10},{10,14},{3,7},{... | collective-permute-start | bytes 1966088 | tf_op jit(solution)/shard_map/ppermute | solution.py:444
  135.2 26.1 %collective-permute-start.17 = (bf16[3,64,896]{2,1,0:T(8,128)(2,1)S(1)}, bf16[3,64,896]{2,1,0:T(8,128)(2,1)S(1)}, u32[]{:S(2)}, u32[]{:S(2)}) collective-permute-start(bf16[3,64,896]{2,1,0:T(8,128)(2,1)S(1)} %slice_select_fusion.1), channel_id=1, source_target_pairs={{0,4},{4,0},{8,12},{12,8},{1,5},{5,1},{9,13},{13,9},{2,6},{6,2},{1... | collective-permute-start | bytes 1032200 | tf_op jit(solution)/shard_map/ppermute | solution.py:398
  136.3 24.5 %collective-permute-start.18 = (bf16[3,48,896]{2,1,0:T(8,128)(2,1)S(1)}, bf16[3,48,896]{2,1,0:T(8,128)(2,1)S(1)}, u32[]{:S(2)}, u32[]{:S(2)}) collective-permute-start(bf16[3,48,896]{2,1,0:T(8,128)(2,1)S(1)} %slice_select_fusion.5), channel_id=1, source_target_pairs={{0,8},{4,12},{8,0},{12,4},{1,9},{5,13},{9,1},{13,5},{2,10},{6,14},... | collective-permute-start | bytes 774152 | tf_op jit(solution)/shard_map/ppermute | solution.py:398
  161.4 15.5 %copy-start.35 = (f32[1792]{0:T(1024)S(1)}, f32[1792]{0:T(1024)}, u32[]{:S(2)}) copy-start(f32[1792]{0:T(1024)} %param.25) | copy-start | bytes 21508
  163.2 22.5 %copy-start.6 = (bf16[448,1792]{1,0:T(8,128)(2,1)S(1)}, bf16[448,1792]{1,0:T(8,128)(2,1)}, u32[]{:S(2)}) copy-start(bf16[448,1792]{1,0:T(8,128)(2,1)} %param.24) | copy-start | bytes 4816900
  163.2 22.5 %copy-start.20 = (f32[1,1024]{1,0:T(1,128)S(1)}, f32[1,1024]{1,0:T(1,128)}, u32[]{:S(2)}) copy-start(f32[1,1024]{1,0:T(1,128)} %constant.137.clone.scale_ref) | copy-start | bytes 12292
  163.2 22.4 %collective-permute-start.19 = (bf16[4,3,112,896]{3,2,1,0:T(8,128)(2,1)S(1)}, bf16[4,3,112,896]{3,2,1,0:T(8,128)(2,1)S(1)}, u32[]{:S(2)}, u32[]{:S(2)}) collective-permute-start(bf16[4,3,112,896]{3,2,1,0:T(8,128)(2,1)S(1)} %maximum_select_fusion.1.near_ref), channel_id=1, source_target_pairs={{0,16},{16,0},{1,17},{17,1},{2,18},{18,2},{3,19},{19,3},{4,20},{20... | collective-permute-start | bytes 7225352 | tf_op jit(solution)/shard_map/ppermute | solution.py:398
  164.3 12.7 %collective-permute-start.23 = (bf16[112,896]{1,0:T(8,128)(2,1)S(1)}, bf16[112,896]{1,0:T(8,128)(2,1)S(1)}, u32[]{:S(2)}, u32[]{:S(2)}) collective-permute-start(bf16[112,896]{1,0:T(8,128)(2,1)S(1)} %dynamic-slice_select_fusion.1), channel_id=1, source_target_pairs={{0,2},{1,3},{2,0},{3,1},{4,6},{5,7},{6,4},{7,5},{8,10},{9,11},{10,... | collective-permute-start | bytes 602120 | tf_op jit(solution)/shard_map/ppermute | solution.py:398
  169.3 43.5 %collective-permute-start.28 = (bf16[1,336,896]{2,1,0:T(8,128)(2,1)}, bf16[1,336,896]{2,1,0:T(8,128)(2,1)}, u32[]{:S(2)}, u32[]{:S(2)}) collective-permute-start(bf16[1,336,896]{2,1,0:T(8,128)(2,1)} %get-tuple-element.20), channel_id=1, source_target_pairs={{0,4},{4,0},{8,12},{12,8},{1,5},{5,1},{9,13},{13,9},{2,6},{6,2},{1... | collective-permute-start | bytes 1806344 | tf_op jit(solution)/shard_map/ppermute | solution.py:398
  171.7 41.2 %collective-permute-start.29 = (bf16[1,336,896]{2,1,0:T(8,128)(2,1)}, bf16[1,336,896]{2,1,0:T(8,128)(2,1)}, u32[]{:S(2)}, u32[]{:S(2)}) collective-permute-start(bf16[1,336,896]{2,1,0:T(8,128)(2,1)} %get-tuple-element.20), channel_id=1, source_target_pairs={{0,8},{4,12},{8,0},{12,4},{1,9},{5,13},{9,1},{13,5},{2,10},{6,14},... | collective-permute-start | bytes 1806344 | tf_op jit(solution)/shard_map/ppermute | solution.py:398
  171.7 9.5 %collective-permute-start.24 = (bf16[112,896]{1,0:T(8,128)(2,1)S(1)}, bf16[112,896]{1,0:T(8,128)(2,1)S(1)}, u32[]{:S(2)}, u32[]{:S(2)}) collective-permute-start(bf16[112,896]{1,0:T(8,128)(2,1)S(1)} %dynamic-slice_select_fusion.1), channel_id=1, source_target_pairs={{0,1},{1,0},{2,3},{3,2},{4,5},{5,4},{6,7},{7,6},{8,9},{9,8},{10,11... | collective-permute-start | bytes 602120 | tf_op jit(solution)/shard_map/ppermute | solution.py:398
  177.0 8.5 %collective-permute-start.25 = (bf16[112,896]{1,0:T(8,128)(2,1)S(1)}, bf16[112,896]{1,0:T(8,128)(2,1)S(1)}, u32[]{:S(2)}, u32[]{:S(2)}) collective-permute-start(bf16[112,896]{1,0:T(8,128)(2,1)S(1)} %collective-permute-done.23), channel_id=1, source_target_pairs={{0,1},{1,0},{2,3},{3,2},{4,5},{5,4},{6,7},{7,6},{8,9},{9,8},{10,11... | collective-permute-start | bytes 602120 | tf_op jit(solution)/shard_map/ppermute | solution.py:398
  185.6 52.6 %copy-start.22 = (bf16[3,112,896]{2,1,0:T(8,128)(2,1)}, bf16[3,112,896]{2,1,0:T(8,128)(2,1)S(1)}, u32[]{:S(2)}) copy-start(bf16[3,112,896]{2,1,0:T(8,128)(2,1)S(1)} %maximum_select_fusion.6) | copy-start | bytes 1806340
  199.0 15.7 %collective-permute-start.20 = (bf16[80,1792]{1,0:T(8,128)(2,1)S(1)}, bf16[80,1792]{1,0:T(8,128)(2,1)S(1)}, u32[]{:S(2)}, u32[]{:S(2)}) collective-permute-start(bf16[80,1792]{1,0:T(8,128)(2,1)S(1)} %get-tuple-element.15), channel_id=1, source_target_pairs={{0,4},{4,8},{8,12},{1,5},{5,9},{9,13},{2,6},{6,10},{10,14},{3,7},{... | collective-permute-start | bytes 860168 | tf_op jit(solution)/shard_map/ppermute | solution.py:612
  202.3 17.0 %collective-permute-start.22 = (bf16[80,1792]{1,0:T(8,128)(2,1)S(1)}, bf16[80,1792]{1,0:T(8,128)(2,1)S(1)}, u32[]{:S(2)}, u32[]{:S(2)}) collective-permute-start(bf16[80,1792]{1,0:T(8,128)(2,1)S(1)} %get-tuple-element.15), channel_id=1, source_target_pairs={{0,5},{1,4},{2,7},{3,6},{4,9},{5,8},{6,11},{7,10},{8,13},{9,12},{1... | collective-permute-start | bytes 860168 | tf_op jit(solution)/shard_map/ppermute | solution.py:614
  206.7 27.2 %collective-permute-start.21 = (bf16[256,1792]{1,0:T(8,128)(2,1)S(1)}, bf16[256,1792]{1,0:T(8,128)(2,1)S(1)}, u32[]{:S(2)}, u32[]{:S(2)}) collective-permute-start(bf16[256,1792]{1,0:T(8,128)(2,1)S(1)} %get-tuple-element.14.x_ref), channel_id=1, source_target_pairs={{0,1},{1,0},{2,3},{3,2},{4,5},{5,4},{6,7},{7,6},{8,9},{9,8},{10,11... | collective-permute-start | bytes 2752520 | tf_op jit(solution)/shard_map/ppermute | solution.py:398
  212.8 18.2 %collective-permute-start.26 = (bf16[3,112,896]{2,1,0:T(8,128)(2,1)}, bf16[3,112,896]{2,1,0:T(8,128)(2,1)S(1)}, u32[]{:S(2)}, u32[]{:S(2)}) collective-permute-start(bf16[3,112,896]{2,1,0:T(8,128)(2,1)} %copy-done.32), channel_id=1, source_target_pairs={{0,4},{4,0},{8,12},{12,8},{1,5},{5,1},{9,13},{13,9},{2,6},{6,2},{1... | collective-permute-start | bytes 1806344 | tf_op jit(solution)/shard_map/ppermute | solution.py:398
  213.0 19.3 %collective-permute-start.27 = (bf16[3,112,896]{2,1,0:T(8,128)(2,1)}, bf16[3,112,896]{2,1,0:T(8,128)(2,1)S(1)}, u32[]{:S(2)}, u32[]{:S(2)}) collective-permute-start(bf16[3,112,896]{2,1,0:T(8,128)(2,1)} %copy-done.32), channel_id=1, source_target_pairs={{0,8},{4,12},{8,0},{12,4},{1,9},{5,13},{9,1},{13,5},{2,10},{6,14},... | collective-permute-start | bytes 1806344 | tf_op jit(solution)/shard_map/ppermute | solution.py:398
  214.7 23.5 %copy-start.15 = (bf16[80,1792]{1,0:T(8,128)(2,1)}, bf16[80,1792]{1,0:T(8,128)(2,1)S(1)}, u32[]{:S(2)}) copy-start(bf16[80,1792]{1,0:T(8,128)(2,1)S(1)} %collective-permute-done.20.halo_ref) | copy-start | bytes 860164
  214.7 22.4 %collective-permute-start.30 = (bf16[1,176,896]{2,1,0:T(8,128)(2,1)}, bf16[1,176,896]{2,1,0:T(8,128)(2,1)}, u32[]{:S(2)}, u32[]{:S(2)}) collective-permute-start(bf16[1,176,896]{2,1,0:T(8,128)(2,1)} %slice_select_fusion.2), channel_id=1, source_target_pairs={{0,4},{4,0},{8,12},{12,8},{1,5},{5,1},{9,13},{13,9},{2,6},{6,2},{1... | collective-permute-start | bytes 946184 | tf_op jit(solution)/shard_map/ppermute | solution.py:398
  219.4 18.8 %copy-start.17 = (bf16[80,1792]{1,0:T(8,128)(2,1)}, bf16[80,1792]{1,0:T(8,128)(2,1)S(1)}, u32[]{:S(2)}) copy-start(bf16[80,1792]{1,0:T(8,128)(2,1)S(1)} %collective-permute-done.22.halo_ref) | copy-start | bytes 860164
  219.4 16.0 %collective-permute-start.31 = (bf16[1,160,896]{2,1,0:T(8,128)(2,1)}, bf16[1,160,896]{2,1,0:T(8,128)(2,1)S(1)}, u32[]{:S(2)}, u32[]{:S(2)}) collective-permute-start(bf16[1,160,896]{2,1,0:T(8,128)(2,1)} %slice_select_fusion.3), channel_id=1, source_target_pairs={{0,8},{4,12},{8,0},{12,4},{1,9},{5,13},{9,1},{13,5},{2,10},{6,14},... | collective-permute-start | bytes 860168 | tf_op jit(solution)/shard_map/ppermute | solution.py:398
  231.0 3.5 %copy-start.30 = (bf16[3,112,896]{2,1,0:T(8,128)(2,1)}, bf16[3,112,896]{2,1,0:T(8,128)(2,1)S(1)}, u32[]{:S(2)}) copy-start(bf16[3,112,896]{2,1,0:T(8,128)(2,1)S(1)} %collective-permute-done.26) | copy-start | bytes 1806340
  240.1 6.2 %collective-permute-start.32 = (bf16[4,1,336,896]{3,2,1,0:T(8,128)(2,1)S(1)}, bf16[4,1,336,896]{3,2,1,0:T(8,128)(2,1)}, u32[]{:S(2)}, u32[]{:S(2)}) collective-permute-start(bf16[4,1,336,896]{3,2,1,0:T(8,128)(2,1)S(1)} %maximum_select_fusion.2.near_ref), channel_id=1, source_target_pairs={{0,16},{16,0},{1,17},{17,1},{2,18},{18,2},{3,19},{19,3},{4,20},{20... | collective-permute-start | bytes 7225352 | tf_op jit(solution)/shard_map/ppermute | solution.py:398
  240.3 4.8 %collective-permute-start.33 = (f32[3,1536]{1,0:T(4,128)S(1)}, f32[3,1536]{1,0:T(4,128)S(1)}, u32[]{:S(2)}, u32[]{:S(2)}) collective-permute-start(f32[3,1536]{1,0:T(4,128)S(1)} %reshape.563), channel_id=1, source_target_pairs={{0,2},{1,3},{2,0},{3,1},{4,6},{5,7},{6,4},{7,5},{8,10},{9,11},{10,... | collective-permute-start | bytes 55304 | tf_op jit(solution)/shard_map/ppermute | solution.py:398
  240.4 5.8 %copy-start.18 = (bf16[80,1792]{1,0:T(8,128)(2,1)S(1)}, bf16[80,1792]{1,0:T(8,128)(2,1)}, u32[]{:S(2)}) copy-start(bf16[80,1792]{1,0:T(8,128)(2,1)} %copy-done.17) | copy-start | bytes 860164
  241.4 24.9 %collective-permute-start.36 = (bf16[3,48,896]{2,1,0:T(8,128)(2,1)S(1)}, bf16[3,48,896]{2,1,0:T(8,128)(2,1)S(1)}, u32[]{:S(2)}, u32[]{:S(2)}) collective-permute-start(bf16[3,48,896]{2,1,0:T(8,128)(2,1)S(1)} %slice_select_fusion.4), channel_id=1, source_target_pairs={{0,8},{4,12},{8,0},{12,4},{1,9},{5,13},{9,1},{13,5},{2,10},{6,14},... | collective-permute-start | bytes 774152 | tf_op jit(solution)/shard_map/ppermute | solution.py:398
  243.2 23.1 %collective-permute-start.35 = (bf16[3,64,896]{2,1,0:T(8,128)(2,1)S(1)}, bf16[3,64,896]{2,1,0:T(8,128)(2,1)S(1)}, u32[]{:S(2)}, u32[]{:S(2)}) collective-permute-start(bf16[3,64,896]{2,1,0:T(8,128)(2,1)S(1)} %slice_select_fusion), channel_id=1, source_target_pairs={{0,4},{4,0},{8,12},{12,8},{1,5},{5,1},{9,13},{13,9},{2,6},{6,2},{1... | collective-permute-start | bytes 1032200 | tf_op jit(solution)/shard_map/ppermute | solution.py:398
  246.3 2.4 copy-start.2
  248.6 17.8 %copy-start.29 = (bf16[3,112,896]{2,1,0:T(8,128)(2,1)S(1)}, bf16[3,112,896]{2,1,0:T(8,128)(2,1)}, u32[]{:S(2)}) copy-start(bf16[3,112,896]{2,1,0:T(8,128)(2,1)} %copy-done.28) | copy-start | bytes 1806340
  248.6 17.8 %copy-start.31 = (bf16[3,112,896]{2,1,0:T(8,128)(2,1)S(1)}, bf16[3,112,896]{2,1,0:T(8,128)(2,1)}, u32[]{:S(2)}) copy-start(bf16[3,112,896]{2,1,0:T(8,128)(2,1)} %copy-done.30) | copy-start | bytes 1806340
  266.5 3.3 %copy-start.13 = (bf16[256,1792]{1,0:T(8,128)(2,1)S(1)}, bf16[256,1792]{1,0:T(8,128)(2,1)}, u32[]{:S(2)}) copy-start(bf16[256,1792]{1,0:T(8,128)(2,1)} %copy-done.12) | copy-start | bytes 2752516
  268.4 20.0 %collective-permute-start.37 = (bf16[4,3,112,896]{3,2,1,0:T(8,128)(2,1)}, bf16[4,3,112,896]{3,2,1,0:T(8,128)(2,1)}, u32[]{:S(2)}, u32[]{:S(2)}) collective-permute-start(bf16[4,3,112,896]{3,2,1,0:T(8,128)(2,1)} %maximum_select_fusion.3.near_ref), channel_id=1, source_target_pairs={{0,16},{16,0},{1,17},{17,1},{2,18},{18,2},{3,19},{19,3},{4,20},{20... | collective-permute-start | bytes 7225352 | tf_op jit(solution)/shard_map/ppermute | solution.py:398
  268.4 20.0 %collective-permute-start.34 = (bf16[2,256,512]{2,1,0:T(8,128)(2,1)}, bf16[2,256,512]{2,1,0:T(8,128)(2,1)}, u32[]{:S(2)}, u32[]{:S(2)}) collective-permute-start(bf16[2,256,512]{2,1,0:T(8,128)(2,1)} %window_rows.3), channel_id=1, source_target_pairs={{0,1},{1,0},{2,3},{3,2},{4,5},{5,4},{6,7},{7,6},{8,9},{9,8},{10,11... | collective-permute-start | bytes 1572872 | tf_op jit(solution)/shard_map/ppermute | solution.py:398
  273.2 15.3 %copy-start.7 = (bf16[448,1792]{1,0:T(8,128)(2,1)S(1)}, bf16[448,1792]{1,0:T(8,128)(2,1)}, u32[]{:S(2)}) copy-start(bf16[448,1792]{1,0:T(8,128)(2,1)} %param.28) | copy-start | bytes 4816900
  273.2 15.3 %copy-start.11 = (bf16[256,1792]{1,0:T(8,128)(2,1)S(1)}, bf16[256,1792]{1,0:T(8,128)(2,1)}, u32[]{:S(2)}) copy-start(bf16[256,1792]{1,0:T(8,128)(2,1)} %copy-done.10) | copy-start | bytes 2752516
  294.2 28.5 %copy-start.1 = (bf16[64,4,1792]{2,1,0:T(4,128)(2,1)S(1)}, bf16[64,4,1792]{2,1,0:T(4,128)(2,1)}, u32[]{:S(2)}) copy-start(bf16[64,4,1792]{2,1,0:T(4,128)(2,1)} %param.17) | copy-start | bytes 2752516
  (13 other events, 18.1 us)

commit v6 on v5

--- a/solution.py
+++ b/solution.py
@@ -79,25 +79,22 @@
                 copy.wait()
 
 
-def weight_copies(place_ref, near_ref, far_ref, targets, sems, group):
-    near = near_ref.shape[0]
-    cols = near_ref.shape[3]
+def weight_copies(place_ref, piece_refs, targets, sems, group):
     found = []
-    for n in range(2 * near):
+    for n, piece_ref in enumerate(piece_refs):
+        cols = piece_ref.shape[2]
         at = 0
         for own_ref, kind, rows, w_ref, off in targets:
             if group == 0:
-                part, head = n // near, n % near
+                part, head = n // NEAR, n % NEAR
                 src = own_ref.at[
                     kind, head * rows : (head + 1) * rows, part * cols : (part + 1) * cols
                 ]
             else:
-                part, head = place_ref[near], place_ref[n % near]
-                if n >= near:
+                part, head = place_ref[NEAR], place_ref[n % NEAR]
+                if n >= NEAR:
                     part = 1 - part
-                src = (near_ref if n < near else far_ref).at[
-                    n % near, group - 1, at : at + rows, :
-                ]
+                src = piece_ref.at[group - 1, at : at + rows, :]
             dst = w_ref.at[group, part, head, off : off + rows, :]
             found.append(pltpu.make_async_copy(src, dst, sems.at[group, len(found)]))
             at += rows
@@ -127,29 +124,23 @@
     return total
 
 
-def linear_kernel(
-    heads,
-    feature_dim,
-    kept,
-    place_ref,
-    x_ref,
-    gain_ref,
-    value_ref,
-    featmap_ref,
-    near_ref,
-    far_ref,
-    first_ref,
-    second_ref,
-    ones_ref,
-    column_ref,
-    num_ref,
-    q_ref,
-    state_ref,
-    normed_ref,
-    value_w_ref,
-    feat_w_ref,
-    sems,
-):
+def linear_kernel(heads, feature_dim, kept, *refs):
+    place_ref, x_ref, gain_ref, value_ref, featmap_ref = refs[:5]
+    piece_refs = refs[5 : 5 + 2 * NEAR]
+    (
+        first_ref,
+        second_ref,
+        ones_ref,
+        column_ref,
+        num_ref,
+        q_ref,
+        state_ref,
+        state_two_ref,
+        normed_ref,
+        value_w_ref,
+        feat_w_ref,
+        sems,
+    ) = refs[5 + 2 * NEAR :]
     step = pl.program_id(0)
     targets = [
         (value_ref, 0, HEAD, value_w_ref, 0),
@@ -162,7 +153,7 @@
         zero_between_heads(value_w_ref)
 
     run_copies(
-        functools.partial(weight_copies, place_ref, near_ref, far_ref, targets, sems),
+        functools.partial(weight_copies, place_ref, piece_refs, targets, sems),
         value_w_ref.shape[0],
         lambda: normed_ref.__setitem__(
             ..., normed_rows(x_ref[...].astype(F32), gain_ref[...])
@@ -178,6 +169,7 @@
     causal = lax.broadcasted_iota(jnp.int32, (rows, rows), 1) <= lax.broadcasted_iota(
         jnp.int32, (rows, rows), 0
     )
+    states = []
     key_features = features(keys, first_ref[...], second_ref[...], ones_ref[...]).astype(BF16)
     for h in range(heads):
         at = 2 * h * feature_dim
@@ -187,7 +179,15 @@
         value = values[:, h * SLOT : (h + 1) * SLOT]
         num_ref[0, :, h * SLOT : (h + 1) * SLOT] = dot(kernel, value)
         state = dot(key_features[:, h * FEAT_SLOT : h * FEAT_SLOT + kept], value, ((0,), (0,)))
-        state_ref[0, h * kept : (h + 1) * kept, :] = state.astype(BF16)
+        states.append(state.astype(BF16))
+
+    @pl.when(step < pl.num_programs(0) // 2)
+    def _():
+        state_ref[0] = jnp.concatenate(states, axis=0)
+
+    @pl.when(step >= pl.num_programs(0) // 2)
+    def _():
+        state_two_ref[0] = jnp.concatenate(states, axis=0)
 
 
 def add_branch(mixed, w_ref, total_ref):
@@ -198,30 +198,21 @@
         total_ref[:, part * cols : (part + 1) * cols] += share
 
 
-def out_one_kernel(
-    heads,
-    kept,
-    place_ref,
-    num_ref,
-    q_ref,
-    first_ref,
-    second_ref,
-    ones_ref,
-    scale_ref,
-    prior_ref,
-    own_ref,
-    near_ref,
-    far_ref,
-    x_ref,
-    gain_ref,
-    residual_ref,
-    normed_ref,
-    tail_ref,
-    total_ref,
-    mixed_ref,
-    w_ref,
-    sems,
-):
+def out_one_kernel(heads, kept, *refs):
+    place_ref, num_ref, q_ref, first_ref, second_ref, ones_ref, scale_ref, *prior_refs = refs[:9]
+    own_ref = refs[9]
+    piece_refs = refs[10 : 10 + 2 * NEAR]
+    (
+        x_ref,
+        gain_ref,
+        residual_ref,
+        normed_ref,
+        tail_ref,
+        total_ref,
+        mixed_ref,
+        w_ref,
+        sems,
+    ) = refs[10 + 2 * NEAR :]
     step = pl.program_id(0)
 
     @pl.when(step == 0)
@@ -231,7 +222,7 @@
 
     run_copies(
         functools.partial(
-            weight_copies, place_ref, near_ref, far_ref, [(own_ref, 0, HEAD, w_ref, 0)], sems
+            weight_copies, place_ref, piece_refs, [(own_ref, 0, HEAD, w_ref, 0)], sems
         ),
         w_ref.shape[0],
     )
@@ -240,7 +231,7 @@
     query_features = (query_features * scale_ref[...]).astype(BF16)
     for h in range(heads):
         at = slice(h * kept, (h + 1) * kept)
-        prior = prior_ref[0, at, :]
+        prior = jnp.where(step < pl.num_programs(0) // 2, *(ref[0, at, :] for ref in prior_refs))
         lanes = slice(h * SLOT, (h + 1) * SLOT)
         total = num_ref[0, :, lanes] + dot(
             query_features[:, h * FEAT_SLOT : h * FEAT_SLOT + kept], prior.astype(BF16)
@@ -257,21 +248,16 @@
         tail_ref[...] = normed[-HALO:]
 
 
-def window_kernel(
-    heads,
-    place_ref,
-    first_ref,
-    x_ref,
-    halo_ref,
-    own_ref,
-    near_ref,
-    far_ref,
-    tap_ref,
-    mixed_ref,
-    rows_ref,
-    w_ref,
-    sems,
-):
+def window_kernel(heads, *refs):
+    place_ref, first_ref, x_ref, halo_ref, own_ref = refs[:5]
+    piece_refs = refs[5 : 5 + 2 * NEAR]
+    (
+        tap_ref,
+        mixed_ref,
+        rows_ref,
+        w_ref,
+        sems,
+    ) = refs[5 + 2 * NEAR :]
     step = pl.program_id(0)
     targets = [(own_ref, kind, HEAD, w_ref, kind * SLOT) for kind in range(3)]
 
@@ -284,7 +270,7 @@
         zero_between_heads(w_ref)
 
     run_copies(
-        functools.partial(weight_copies, place_ref, near_ref, far_ref, targets, sems),
+        functools.partial(weight_copies, place_ref, piece_refs, targets, sems),
         w_ref.shape[0],
         place_rows,
     )
@@ -318,20 +304,16 @@
             mixed_ref[0, start : start + tile, h * SLOT : (h + 1) * SLOT] = mixed.astype(BF16)
 
 
-def out_two_kernel(
-    place_ref,
-    live_ref,
-    mixed_ref,
-    pair_ref,
-    own_ref,
-    near_ref,
-    far_ref,
-    residual_ref,
-    out_ref,
-    total_ref,
-    w_ref,
-    sems,
-):
+def out_two_kernel(*refs):
+    place_ref, live_ref, mixed_ref, pair_ref, own_ref = refs[:5]
+    piece_refs = refs[5 : 5 + 2 * NEAR]
+    (
+        residual_ref,
+        out_ref,
+        total_ref,
+        w_ref,
+        sems,
+    ) = refs[5 + 2 * NEAR :]
     step = pl.program_id(0)
 
     @pl.when(step == 0)
@@ -341,7 +323,7 @@
 
     run_copies(
         functools.partial(
-            weight_copies, place_ref, near_ref, far_ref, [(own_ref, 0, HEAD, w_ref, 0)], sems
+            weight_copies, place_ref, piece_refs, [(own_ref, 0, HEAD, w_ref, 0)], sems
         ),
         w_ref.shape[0],
     )
@@ -367,7 +349,7 @@
 HBM = pl.BlockSpec(memory_space=pl.ANY)
 
 
-def call(kernel, groups, in_specs, out_specs, out_shape, scratch, name):
+def call(kernel, groups, in_specs, out_specs, out_shape, scratch, flops, name):
     return pl.pallas_call(
         kernel,
         grid=(groups,),
@@ -378,7 +360,7 @@
         compiler_params=pltpu.CompilerParams(
             dimension_semantics=("arbitrary",), vmem_limit_bytes=VMEM
         ),
-        cost_estimate=pl.CostEstimate(flops=0, bytes_accessed=0, transcendentals=0),
+        cost_estimate=pl.CostEstimate(flops=flops, bytes_accessed=0, transcendentals=0),
         name=name,
     )
 
@@ -425,29 +407,37 @@
     return across(held, "seq", 1), across(held, "seq", 2)
 
 
-def from_plane(held, near_by, diagonal, over_cores):
+def from_plane(held, near_by, diagonal, last):
+    beside, above = near_by
+    if diagonal is None:
+        near = [held, beside, above, across(held, "seq", 3)]
+        return near + [across(piece, "dp", 1) for piece in near]
     half = -(-held.shape[1] // 32) * 16
-    beside, above = near_by
     opposite = [
         across(after(above[:, :half], diagonal), "seq", 1),
         across(after(beside[:, half:], diagonal), "seq", 2),
     ]
-    opposite = after(jnp.concatenate(opposite, axis=1), over_cores)
-    near = after(jnp.stack([held, beside, above, opposite]), over_cores)
-    return near, across(near, "dp", 1)
-
-
-def earlier_blocks(state, axis):
-    peers = lax.axis_size(axis)
-    if peers <= 4:
-        found = [
-            lax.ppermute(state, axis, [(i, i + by) for i in range(peers - by)])
-            for by in range(1, peers)
-        ]
-        return sum(one.astype(F32) for one in found)
-    everything = lax.all_gather(state, axis).astype(F32)
-    reached = jnp.arange(peers) < lax.axis_index(axis)
-    return jnp.sum(jnp.where(reached[:, None, None, None], everything, 0.0), axis=0)
+    near = [held, beside, above, after(jnp.concatenate(opposite, axis=1), last)]
+    return near + [across(piece, "dp", 1) for piece in near]
+
+
+def earlier_blocks(one, two, axis):
+    peers, mine = lax.axis_size(axis), lax.axis_index(axis)
+    if peers != 4:
+        both = lax.all_gather(jnp.concatenate([one, two]), axis).astype(F32)
+        reached = (jnp.arange(peers) < mine)[:, None, None, None]
+        total = jnp.sum(jnp.where(reached, both, 0.0), axis=0)
+        return total[: one.shape[0]], total[one.shape[0] :]
+    upward = [(0, 2), (1, 3)]
+    one_beside, two_below = across(one, axis, 1), lax.ppermute(two, axis, upward)
+    pair = (one.astype(F32) + one_beside.astype(F32)).astype(one.dtype)
+    pair = after(pair, (two_below,))
+    two_sent = jnp.where(mine == 2, two.astype(F32), 0.0) + two_below.astype(F32)
+    two_sent = jnp.where(mine < 2, two, two_sent.astype(two.dtype))
+    one_below, two_beside = lax.ppermute(pair, axis, upward), across(two_sent, axis, 1)
+    one_total = jnp.where(mine % 2 == 1, one_beside.astype(F32), 0.0) + one_below.astype(F32)
+    two_total = jnp.where(mine > 0, two_beside.astype(F32), 0.0) + two_below.astype(F32)
+    return one_total, two_total
 
 
 def on_device(
@@ -519,9 +509,9 @@
     slot = dp_place * req_dev + tensor_place
     length = jnp.sum(jnp.where(jnp.arange(slots_total) == slot, slot_lengths, 0))
 
-    held_out_one = settled(jnp.stack(from_groups(own_piece([out_one]), (picked,))))
-    near_one = from_plane(held_one, neighbours(held_one), (), (held_out_one,))
-    held_window = from_group(own_piece([window_t]), (swapped,))
+    held_out_one = settled(jnp.stack(from_groups(own_piece([out_one]), (swapped,))))
+    near_one = from_plane(held_one, neighbours(held_one), (swapped,), ())
+    held_window = from_group(own_piece([window_t]), (held_out_one,))
     held_out_two = from_groups(own_piece([out_two]), (swapped,), (1, 0, 2))
     places = jnp.concatenate([(seq_place % NEAR) ^ jnp.arange(NEAR), dp_place[None]])
     places = places.astype(jnp.int32)
@@ -542,24 +532,29 @@
         return pltpu.VMEM((group_count, dp_count, heads, rows_of_head, width // dp_count), BF16)
 
     slots = heads * SLOT
-    num, queries, state = call(
+    half = group_count // 2
+    halves = [
+        pl.BlockSpec((1, heads * kept, SLOT), lambda g: (jnp.minimum(g, half - 1), 0, 0)),
+        pl.BlockSpec((1, heads * kept, SLOT), lambda g: (jnp.maximum(g - half, 0), 0, 0)),
+    ]
+    num, queries, state, state_two = call(
         functools.partial(linear_kernel, heads, feature_dim, kept),
         group_count,
         [
             SMEM,
             whole((rows, width)),
             whole((1, width)),
-            *[HBM] * 4,
+            *[HBM] * (2 + 2 * NEAR),
             whole(first.shape),
             whole(second.shape),
             whole(ones.shape),
             whole(column.shape),
         ],
-        [each((rows, slots)), each((rows, 2 * feat_cols)), each((heads * kept, SLOT))],
+        [each((rows, slots)), each((rows, 2 * feat_cols)), *halves],
         [
             jax.ShapeDtypeStruct((group_count, rows, slots), F32),
             jax.ShapeDtypeStruct((group_count, rows, 2 * feat_cols), BF16),
-            jax.ShapeDtypeStruct((group_count, heads * kept, SLOT), BF16),
+            *[jax.ShapeDtypeStruct((group_count // 2, heads * kept, SLOT), BF16)] * 2,
         ],
         [
             pltpu.VMEM((rows, width), BF16),
@@ -567,16 +562,16 @@
             weights_of(2 * feature_dim),
             copy_sems(3),
         ],
+        2 * group_count * rows * width * 640,
         "linear_rows",
     )(
         places, tokens, gain_one[None], values_t, featmap_t, *near_one, first, second, ones, column
     )
-    prior = settled(earlier_blocks(state, "seq"))
-    held_out_one = after(held_out_one, (swapped,))
+    prior_one, prior_two = earlier_blocks(state, state_two, "seq")
+    held_window = after(held_window, (state,))
     near_out_one = from_plane(
-        held_out_one, neighbours(held_out_one), (state,), (prior, held_window)
-    )
-    held_out_two = settled(jnp.stack(held_out_two), (state,))
+        held_out_one, neighbours(held_out_one), (state,), (held_window,)
+    )
     residual, normed_two, tail = call(
         functools.partial(out_one_kernel, heads, kept),
         group_count,
@@ -589,8 +584,8 @@
             whole(ones.shape),
             whole(scale.shape),
         ]
-        + [each((heads * kept, SLOT))]
-        + [HBM] * 3
+        + halves
+        + [HBM] * (1 + 2 * NEAR)
         + [
             whole((rows, width)),
             whole((1, width)),
@@ -603,31 +598,19 @@
             weights_of(SLOT),
             copy_sems(1),
         ],
+        2 * group_count * rows * width * 640,
         "linear_out",
     )(
-        places, num, queries, first, second, ones, scale, prior, out_one, *near_out_one, tokens,
+        places, num, queries, first, second, ones, scale, prior_one, prior_two, out_one, *near_out_one, tokens,
         gain_two[None],
     )
 
     halo = lax.ppermute(tail, "seq", [(i, i + 1) for i in range(seq_count - 1)])
     pair_rows = across(normed_two, "tensor", 1)
-    pair_halo = lax.ppermute(
-        tail,
-        ("seq", "tensor"),
-        [
-            (i * group_count + j, (i + 1) * group_count + (j ^ 1))
-            for i in range(seq_count - 1)
-            for j in range(group_count)
-        ],
-    )
-    held_window, held_out_two = after(held_window, (prior,)), after(held_out_two, (residual,))
-    near_by = neighbours(held_out_two)
-    near_window = from_plane(
-        held_window,
-        neighbours(held_window),
-        (residual, held_out_two),
-        (pair_rows, halo, pair_halo, *near_by),
-    )
+    pair_halo = across(halo, "tensor", 1)
+    held_window = after(held_window, (prior_one,))
+    held_out_two = settled(jnp.stack(held_out_two), (residual,))
+    near_window = from_plane(held_window, neighbours(held_window), None, ())
     block_start = (seq_place * rows).astype(jnp.int32)[None]
 
     def window_rows(slot_rows, slot_halo):
@@ -639,7 +622,7 @@
                 SMEM,
                 whole((rows, width)),
                 whole((HALO, width)),
-                *[HBM] * 3,
+                *[HBM] * (1 + 2 * NEAR),
                 each((tap_count, 3 * slots)),
             ],
             each((rows, slots)),
@@ -649,13 +632,16 @@
                 pltpu.VMEM((2, dp_count, heads, 3 * SLOT, width // dp_count), BF16),
                 copy_sems(3),
             ],
-            "window_rows",
+            6 * rows * width * 3 * head_cols,
+        "window_rows",
         )(places, block_start, slot_rows, slot_halo, window_t, *near_window, taps)
 
     mixed_pair = window_rows(pair_rows, pair_halo)
-    near_out_two = from_plane(held_out_two, near_by, (pair_rows,), (mixed_pair,))
-    mixed_pair = across(mixed_pair, "tensor", 1)
+    back = across(mixed_pair, "tensor", 1)
     mixed_own = window_rows(normed_two, halo)
+    near_out_two = from_plane(
+        held_out_two, neighbours(held_out_two), (mixed_pair,), (back, mixed_own)
+    )
     live = (length - seq_place * rows).astype(jnp.int32)[None]
     result = call(
         out_two_kernel,
@@ -665,7 +651,7 @@
             SMEM,
             whole((2, rows, slots)),
             whole((2, rows, slots)),
-            *[HBM] * 3,
+            *[HBM] * (1 + 2 * NEAR),
             whole((rows, width)),
         ],
         whole((rows, width)),
@@ -675,8 +661,9 @@
             weights_of(SLOT),
             copy_sems(1),
         ],
+        2 * group_count * rows * width * head_cols,
         "window_out",
-    )(places, live, mixed_own, mixed_pair, out_two, *near_out_two, residual)
+    )(places, live, mixed_own, back, out_two, *near_out_two, residual)
 
     result = result.reshape(page_span, group_count, page_share, width).transpose(1, 0, 2, 3)
     return lax.all_to_all(result, "tensor", split_axis=0, concat_axis=0, tiled=True)

time: 324 us -> 348 us (1.074)
  waiting for transfers between devices: 77.6 us -> 117 us
  blocking collectives: 56.1 us -> 27.2 us
  local copies, waits for them, and re-layouts: 34.9 us -> 53.7 us
  starting transfers between devices: 49.5 us -> 57.6 us
  other arithmetic: 28.5 us -> 20.7 us
  Pallas kernels: 65.3 us -> 61.8 us
    ppermute x33 -> x47, waiting for transfers between devices: 56.7 us -> 91 us  [across(): lax.ppermute(array, axis, [(i, i ^ bit) for i in range(lax.axis_size(axis...]
    all_to_all x1 -> x0, blocking collectives: 29.1 us -> none  [on_device(): lax.all_to_all(picked, 'tensor', split_axis=0, concat_axis=0, tiled=True)]
    unnamed x77 -> x118, local copies, waits for them, and re-layouts: 14 us -> 35 us
    all_to_all x0 -> x1, waiting for transfers between devices: none -> 19.2 us  [on_device(): lax.all_to_all(picked, 'tensor', split_axis=0, concat_axis=0, tiled=True)]
    ppermute x4 -> x2, waiting for transfers between devices: 21 us -> 4.43 us  [the longest x1 3 us: earlier_blocks(): lax.ppermute(pair, axis, upward)]
    select_n x20 -> x15, other arithmetic: 20.5 us -> 11.9 us  [after(): return jnp.where(zero == 0.0, array, jnp.zeros_like(array))]
    all_to_all x0 -> x1, starting transfers between devices: none -> 5.06 us  [on_device(): lax.all_to_all(picked, 'tensor', split_axis=0, concat_axis=0, tiled=True)]
    ppermute x33 -> x47, starting transfers between devices: 32.3 us -> 36.1 us  [across(): lax.ppermute(array, axis, [(i, i ^ bit) for i in range(lax.axis_size(axis...]
  transfers between devices with their start and end apart: 39 -> 52, of which waited for: 19 -> 18; matrix products, arithmetic and copies ran while one was open for 12% -> 9% of each run, Pallas kernels for 18% -> 16%
where the time goes in v6:
time: 348 us; the launch traced here: 346 us
  waiting for transfers between devices  117 us (34%)
  Pallas kernels  61.8 us (18%)
  starting transfers between devices  57.6 us (17%)
  local copies, waits for them, and re-layouts  53.7 us (15%)
  blocking collectives  27.2 us (8%)
  other arithmetic  20.7 us (6%)
  between operations  8.2 us (2%)
    ppermute x47, waiting for transfers between devices, across(): lax.ppermute(array, axis, [(i, i ^ bit) for i in range(lax.axis_size(axis...  91 us
    ppermute x47, starting transfers between devices, across(): lax.ppermute(array, axis, [(i, i ^ bit) for i in range(lax.axis_size(axis...  36.1 us
    unnamed x118, local copies, waits for them, and re-layouts  35 us
    pallas_call x2, Pallas kernels, window_rows(): call(functools.partial(window_kernel, heads), 2, [SMEM, SMEM, whole((rows...  30.5 us
    all_to_all x1, blocking collectives, on_device(): lax.all_to_all(result, 'tensor', split_axis=0, concat_axis=0, tiled=True)  27.2 us
    all_to_all x1, waiting for transfers between devices, on_device(): lax.all_to_all(picked, 'tensor', split_axis=0, concat_axis=0, tiled=True)  19.2 us
    pallas_call x1, Pallas kernels, on_device(): call(functools.partial(linear_kernel, heads, feature_dim, kept), group_co...  13.1 us
    select_n x15, other arithmetic, after(): return jnp.where(zero == 0.0, array, jnp.zeros_like(array))  11.9 us
  transfers between devices with their start and end apart: 52, of which 18 were waited for; matrix products, arithmetic and copies ran while one was open for 9% of the time, Pallas kernels for 16%

profile of v6, /device:TPU:0, one launch (start us, length us, event | category | flops | bytes accessed | tf_op | source)
XLA Modules:
  0.0 346.3 jit_solution(5533928038662604932)
XLA Ops:
  2.5 2.2 gather_fusion
  4.7 5.2 %all-to-all-start = ((bf16[8,8,4,1792]{3,2,1,0:T(4,128)(2,1)}), bf16[8,8,4,1792]{3,2,1,0:T(4,128)(2,1)S(1)}, u32[]{:S(2)}, u32[]{:S(2)}) async-start(bf16[8,8,4,1792]{3,2,1,0:T(4,128)(2,1)} %bitcast.12), calls=%async_computation | async-start | bytes 1835008 | tf_op jit(solution)/shard_map/all_to_all | solution.py:500
  11.6 2.7 collective-permute-start.1
  14.3 1.6 collective-permute-start
  16.1 10.7 %collective-permute-done.1 = bf16[144,896]{1,0:T(8,128)(2,1)S(1)} collective-permute-done((bf16[144,896]{1,0:T(8,128)(2,1)S(1)}, bf16[144,896]{1,0:T(8,128)(2,1)S(1)}, u32[]{:S(2)}, u32[]{:S(2)}) %collective-permute-start.1) | collective-permute-done | bytes 258080 | tf_op jit(solution)/shard_map/ppermute | solution.py:380
  27.5 7.2 %collective-permute-done.2 = bf16[144,896]{1,0:T(8,128)(2,1)S(1)} collective-permute-done((bf16[144,896]{1,0:T(8,128)(2,1)S(1)}, bf16[144,896]{1,0:T(8,128)(2,1)S(1)}, u32[]{:S(2)}, u32[]{:S(2)}) %collective-permute-start.2) | collective-permute-done | bytes 258080 | tf_op jit(solution)/shard_map/ppermute | solution.py:380
  36.0 2.2 gather_fusion.1
  38.2 1.6 broadcast_select_fusion
  40.8 5.1 %all-to-all-start.1 = ((bf16[4,16,4,1792]{3,1,2,0:T(8,128)(2,1)}), bf16[4,16,4,1792]{3,1,2,0:T(8,128)(2,1)S(1)}, u32[]{:S(2)}, u32[]{:S(2)}) async-start(bf16[4,16,4,1792]{3,1,2,0:T(8,128)(2,1)} %copy.39), calls=%async_computation.1 | async-start | bytes 1835008 | tf_op jit(solution)/shard_map/all_to_all | solution.py:507
  45.8 1.6 collective-permute-start.4
  47.5 1.5 collective-permute-start.3
  48.9 19.2 %all-to-all-done.1 = bf16[4,16,4,1792]{3,1,2,0:T(8,128)(2,1)S(1)} async-done(((bf16[4,16,4,1792]{3,1,2,0:T(8,128)(2,1)}), bf16[4,16,4,1792]{3,1,2,0:T(8,128)(2,1)S(1)}, u32[]{:S(2)}, u32[]{:S(2)}) %all-to-all-start.1) | async-done | bytes 917536 | tf_op jit(solution)/shard_map/all_to_all | solution.py:507
  70.4 1.7 collective-permute-start.5
  73.1 1.5 collective-permute-start.6
  75.1 6.2 %collective-permute-done.5 = bf16[3,80,896]{2,1,0:T(8,128)(2,1)S(1)} collective-permute-done((bf16[3,80,896]{2,1,0:T(8,128)(2,1)S(1)}, bf16[3,80,896]{2,1,0:T(8,128)(2,1)S(1)}, u32[]{:S(2)}, u32[]{:S(2)}) %collective-permute-start.5) | collective-permute-done | bytes 430112 | tf_op jit(solution)/shard_map/ppermute | solution.py:380
  83.9 10.4 %collective-permute-done.16 = bf16[112,896]{1,0:T(8,128)(2,1)S(1)} collective-permute-done((bf16[112,896]{1,0:T(8,128)(2,1)S(1)}, bf16[112,896]{1,0:T(8,128)(2,1)S(1)}, u32[]{:S(2)}, u32[]{:S(2)}) %collective-permute-start.16) | collective-permute-done | bytes 200736 | tf_op jit(solution)/shard_map/ppermute | solution.py:380
  94.3 6.9 %collective-permute-done.15 = bf16[112,896]{1,0:T(8,128)(2,1)S(1)} collective-permute-done((bf16[112,896]{1,0:T(8,128)(2,1)S(1)}, bf16[112,896]{1,0:T(8,128)(2,1)S(1)}, u32[]{:S(2)}, u32[]{:S(2)}) %collective-permute-start.15) | collective-permute-done | bytes 200736 | tf_op jit(solution)/shard_map/ppermute | solution.py:380
  101.6 1.4 copy.40
  103.0 1.7 reshape.323.refs_1_.refs_18_
  104.8 2.6 collective-permute-done.17
  108.1 1.2 pad_maximum_fusion.1.refs_10_
  109.3 1.6 collective-permute-start.18
  111.0 1.4 copy-done.3
  114.3 13.1 %linear_rows.1 = (f32[4,256,512]{2,1,0:T(8,128)S(1)}, bf16[4,256,128]{2,1,0:T(8,128)(2,1)S(1)}, bf16[2,640,128]{2,1,0:T(8,128)(2,1)}, bf16[2,640,128]{2,1,0:T(8,128)(2,1)}) custom-call(s32[5]{0:T(128)S(1)} %pad_add_fusion.refs_0_, bf16[256,1792]{1,0:T(8,128)(2,1)S(1)} %reshape.323.refs_1_.refs_18_, f32[1,1792]{1,0:T(1,128)S(1)} %broadcast_in_dim.130.refs_2_, ...), custom_call_target="tpu_custom_call" | custom-call | flops 2348810240 | tf_op jit(solution)/shard_map/linear_rows/pallas_call | solution.py:540
  127.5 1.3 copy-done.1
  129.5 3.4 collective-permute-start.12
  133.7 1.1 collective-permute-start.35
  136.9 1.2 dynamic-slice_select_fusion
  138.1 1.2 slice.62
  139.9 1.4 collective-permute-done.12
  143.5 2.0 collective-permute-start.20
  145.5 1.1 fusion.5
  146.6 4.5 %collective-permute-start.13 = (bf16[2,640,128]{2,1,0:T(8,128)(2,1)S(1)}, bf16[2,640,128]{2,1,0:T(8,128)(2,1)S(1)}, u32[]{:S(2)}, u32[]{:S(2)}) collective-permute-start(bf16[2,640,128]{2,1,0:T(8,128)(2,1)S(1)} %fusion.5), channel_id=1, source_target_pairs={{0,8},{4,12},{1,9},{5,13},{2,10},{6,14},{3,11},{7,15},{16,24},{20,... | collective-permute-start | bytes 983048 | tf_op jit(solution)/shard_map/ppermute | solution.py:437
  152.1 2.1 collective-permute-done.19.refs_12_
  155.1 3.0 collective-permute-done.13
  161.0 14.0 %collective-permute-done.20 = bf16[336,896]{1,0:T(8,128)(2,1)S(1)} collective-permute-done((bf16[336,896]{1,0:T(8,128)(2,1)S(1)}, bf16[336,896]{1,0:T(8,128)(2,1)S(1)}, u32[]{:S(2)}, u32[]{:S(2)}) %collective-permute-start.20) | collective-permute-done | bytes 602144 | tf_op jit(solution)/shard_map/ppermute | solution.py:380
  175.0 1.7 collective-permute-start.22
  178.8 3.1 collective-permute-done.22
  183.5 2.0 fusion.4
  185.6 4.7 %collective-permute-done.40 = bf16[112,896]{1,0:T(8,128)(2,1)S(1)} collective-permute-done((bf16[112,896]{1,0:T(8,128)(2,1)S(1)}, bf16[112,896]{1,0:T(8,128)(2,1)S(1)}, u32[]{:S(2)}, u32[]{:S(2)}) %collective-permute-start.40) | collective-permute-done | bytes 200736 | tf_op jit(solution)/shard_map/ppermute | solution.py:380
  190.3 1.5 collective-permute-start.14
  194.0 1.7 collective-permute-start.29
  195.7 1.3 collective-permute-start.30
  197.0 4.2 %collective-permute-done.14 = bf16[2,640,128]{2,1,0:T(8,128)(2,1)} collective-permute-done((bf16[2,640,128]{2,1,0:T(8,128)(2,1)}, bf16[2,640,128]{2,1,0:T(8,128)(2,1)}, u32[]{:S(2)}, u32[]{:S(2)}) %collective-permute-start.14) | collective-permute-done | bytes 327712 | tf_op jit(solution)/shard_map/ppermute | solution.py:380
  201.3 1.2 convert_add_fusion.refs_8_
  202.8 1.6 copy-done.2
  204.4 1.4 copy-done.4
  207.7 10.4 %linear_out.1 = (bf16[256,1792]{1,0:T(8,128)(2,1)S(1)}, bf16[256,1792]{1,0:T(8,128)(2,1)}, bf16[80,1792]{1,0:T(8,128)(2,1)S(1)}) custom-call(s32[5]{0:T(128)S(1)} %pad_add_fusion.refs_0_, f32[4,256,512]{2,1,0:T(8,128)S(1)} %copy-done.2, bf16[4,256,128]{2,1,0:T(8,128)(2,1)S(1)} %copy-done.25, bf16[128,1024]{1,0:T(8,128)(2,1)S(1)} %copy-done.10, ...), custom_call_target="tpu_custom_call" | custom-call | flops 2348810240 | tf_op jit(solution)/shard_map/linear_out/pallas_call | solution.py:575
  218.2 1.8 collective-permute-start.36
  220.0 3.4 collective-permute-start.27
  223.4 2.9 collective-permute-done.30.refs_8_
  227.7 2.5 collective-permute-done.27.refs_3_
  232.0 15.1 %collective-permute-done.37.refs_3_ = bf16[80,1792]{1,0:T(8,128)(2,1)S(1)} collective-permute-done((bf16[80,1792]{1,0:T(8,128)(2,1)S(1)}, bf16[80,1792]{1,0:T(8,128)(2,1)S(1)}, u32[]{:S(2)}, u32[]{:S(2)}) %collective-permute-start.37) | collective-permute-done | bytes 286752 | tf_op jit(solution)/shard_map/ppermute | solution.py:380
  247.8 1.5 collective-permute-start.42
  250.2 1.7 collective-permute-start.43
  252.8 2.4 copy-done.26
  259.3 15.3 %window_rows.3 = bf16[2,256,512]{2,1,0:T(8,128)(2,1)S(1)} custom-call(s32[5]{0:T(128)S(1)} %pad_add_fusion.refs_0_, s32[1]{0:T(128)} %bitcast.2.refs_1_, bf16[256,1792]{1,0:T(8,128)(2,1)} %collective-permute-done.36.refs_2_, bf16[80,1792]{1,0:T(8,128)(2,1)S(1)} %copy-done.42, bf16[3,448,1792]{2,1,0:T(8,128)(2,1)S(1)} %bitcast.62, ...), custom_call_target="tpu_custom_call" | custom-call | flops 3699376128 | tf_op jit(solution)/shard_map/window_rows/pallas_call | solution.py:617
  274.6 1.8 collective-permute-start.38
  278.7 2.4 copy-done.27
  281.1 15.2 %window_rows.2.refs_2_ = bf16[2,256,512]{2,1,0:T(8,128)(2,1)S(1)} custom-call(s32[5]{0:T(128)S(1)} %pad_add_fusion.refs_0_, s32[1]{0:T(128)} %bitcast.2.refs_1_, bf16[256,1792]{1,0:T(8,128)(2,1)} %get-tuple-element.16.refs_2_, bf16[80,1792]{1,0:T(8,128)(2,1)S(1)} %copy-done.40, bf16[3,448,1792]{2,1,0:T(8,128)(2,1)S(1)} %bitcast.63, ...), custom_call_target="tpu_custom_call" | custom-call | flops 3699376128 | tf_op jit(solution)/shard_map/window_rows/pallas_call | solution.py:617
  303.1 1.4 copy-done.5
  306.6 1.2 copy-done.14
  309.9 7.7 %window_out.1 = bf16[256,1792]{1,0:T(8,128)(2,1)S(1)} custom-call(s32[5]{0:T(128)S(1)} %pad_add_fusion.refs_0_, s32[1]{0:T(128)} %bitcast.1.refs_1_, bf16[2,256,512]{2,1,0:T(8,128)(2,1)S(1)} %copy-done.23, bf16[2,256,512]{2,1,0:T(8,128)(2,1)S(1)} %copy-done.21, bf16[1,448,1792]{2,1,0:T(8,128)(2,1)S(1)} %bitcast.60, ...), custom_call_target="tpu_custom_call" | custom-call | flops 1644167168 | tf_op jit(solution)/shard_map/window_out/pallas_call | solution.py:646
  318.1 27.2 %all_to_all.15 = bf16[4,16,4,1792]{3,2,1,0:T(4,128)(2,1)S(1)} all-to-all(bf16[4,16,4,1792]{3,2,1,0:T(4,128)(2,1)S(1)} %bitcast.65), channel_id=1, replica_groups=mesh['dp'=2,'seq'=4,'tensor'=4] {'tensor'}, dimensions={0} | all-to-all | bytes 1835008 | tf_op jit(solution)/shard_map/all_to_all | solution.py:669
  (237 shorter events, 53.2 us)
Async XLA Ops:
  4.7 31.3 %all-to-all-start = ((bf16[8,8,4,1792]{3,2,1,0:T(4,128)(2,1)}), bf16[8,8,4,1792]{3,2,1,0:T(4,128)(2,1)S(1)}, u32[]{:S(2)}, u32[]{:S(2)}) async-start(bf16[8,8,4,1792]{3,2,1,0:T(4,128)(2,1)} %bitcast.12), calls=%async_computation | async-start | bytes 1835008 | tf_op jit(solution)/shard_map/all_to_all | solution.py:500
  11.6 15.2 %collective-permute-start.1 = (bf16[144,896]{1,0:T(8,128)(2,1)S(1)}, bf16[144,896]{1,0:T(8,128)(2,1)S(1)}, u32[]{:S(2)}, u32[]{:S(2)}) collective-permute-start(bf16[144,896]{1,0:T(8,128)(2,1)S(1)} %pad_maximum_fusion.2), channel_id=1, source_target_pairs={{0,2},{1,3},{2,0},{3,1},{4,6},{5,7},{6,4},{7,5},{8,10},{9,11},{10,... | collective-permute-start | bytes 774152 | tf_op jit(solution)/shard_map/ppermute | solution.py:380
  14.3 13.2 %collective-permute-start = (bf16[144,896]{1,0:T(8,128)(2,1)S(1)}, bf16[144,896]{1,0:T(8,128)(2,1)S(1)}, u32[]{:S(2)}, u32[]{:S(2)}) collective-permute-start(bf16[144,896]{1,0:T(8,128)(2,1)S(1)} %pad_maximum_fusion.2), channel_id=1, source_target_pairs={{0,1},{1,0},{2,3},{3,2},{4,5},{5,4},{6,7},{7,6},{8,9},{9,8},{10,11... | collective-permute-start | bytes 774152 | tf_op jit(solution)/shard_map/ppermute | solution.py:380
  26.9 7.8 %collective-permute-start.2 = (bf16[144,896]{1,0:T(8,128)(2,1)S(1)}, bf16[144,896]{1,0:T(8,128)(2,1)S(1)}, u32[]{:S(2)}, u32[]{:S(2)}) collective-permute-start(bf16[144,896]{1,0:T(8,128)(2,1)S(1)} %collective-permute-done.1), channel_id=1, source_target_pairs={{0,1},{1,0},{2,3},{3,2},{4,5},{5,4},{6,7},{7,6},{8,9},{9,8},{10,11... | collective-permute-start | bytes 774152 | tf_op jit(solution)/shard_map/ppermute | solution.py:380
  40.8 27.4 %all-to-all-start.1 = ((bf16[4,16,4,1792]{3,1,2,0:T(8,128)(2,1)}), bf16[4,16,4,1792]{3,1,2,0:T(8,128)(2,1)S(1)}, u32[]{:S(2)}, u32[]{:S(2)}) async-start(bf16[4,16,4,1792]{3,1,2,0:T(8,128)(2,1)} %copy.39), calls=%async_computation.1 | async-start | bytes 1835008 | tf_op jit(solution)/shard_map/all_to_all | solution.py:507
  45.8 23.5 %collective-permute-start.4 = (bf16[3,144,896]{2,1,0:T(8,128)(2,1)S(1)}, bf16[3,144,896]{2,1,0:T(8,128)(2,1)}, u32[]{:S(2)}, u32[]{:S(2)}) collective-permute-start(bf16[3,144,896]{2,1,0:T(8,128)(2,1)S(1)} %pad_maximum_fusion.refs_5_), channel_id=1, source_target_pairs={{0,8},{4,12},{8,0},{12,4},{1,9},{5,13},{9,1},{13,5},{2,10},{6,14},... | collective-permute-start | bytes 2322440 | tf_op jit(solution)/shard_map/ppermute | solution.py:380
  47.5 24.6 %collective-permute-start.3 = (bf16[3,144,896]{2,1,0:T(8,128)(2,1)S(1)}, bf16[3,144,896]{2,1,0:T(8,128)(2,1)}, u32[]{:S(2)}, u32[]{:S(2)}) collective-permute-start(bf16[3,144,896]{2,1,0:T(8,128)(2,1)S(1)} %pad_maximum_fusion.refs_5_), channel_id=1, source_target_pairs={{0,4},{4,0},{8,12},{12,8},{1,5},{5,1},{9,13},{13,9},{2,6},{6,2},{1... | collective-permute-start | bytes 2322440 | tf_op jit(solution)/shard_map/ppermute | solution.py:380
  69.3 25.0 %copy-start.54 = (f32[1792]{0:T(1024)S(1)}, f32[1792]{0:T(1024)}, u32[]{:S(2)}) copy-start(f32[1792]{0:T(1024)} %param.21) | copy-start | bytes 21508
  70.4 10.9 %collective-permute-start.5 = (bf16[3,80,896]{2,1,0:T(8,128)(2,1)S(1)}, bf16[3,80,896]{2,1,0:T(8,128)(2,1)S(1)}, u32[]{:S(2)}, u32[]{:S(2)}) collective-permute-start(bf16[3,80,896]{2,1,0:T(8,128)(2,1)S(1)} %slice_select_fusion), channel_id=1, source_target_pairs={{0,4},{4,0},{8,12},{12,8},{1,5},{5,1},{9,13},{13,9},{2,6},{6,2},{1... | collective-permute-start | bytes 1290248 | tf_op jit(solution)/shard_map/ppermute | solution.py:380
  73.1 9.1 %collective-permute-start.6 = (bf16[3,64,896]{2,1,0:T(8,128)(2,1)S(1)}, bf16[3,64,896]{2,1,0:T(8,128)(2,1)S(1)}, u32[]{:S(2)}, u32[]{:S(2)}) collective-permute-start(bf16[3,64,896]{2,1,0:T(8,128)(2,1)S(1)} %slice_select_fusion.3), channel_id=1, source_target_pairs={{0,8},{4,12},{8,0},{12,4},{1,9},{5,13},{9,1},{13,5},{2,10},{6,14},... | collective-permute-start | bytes 1032200 | tf_op jit(solution)/shard_map/ppermute | solution.py:380
  74.6 36.3 %collective-permute-start.7 = (bf16[3,144,896]{2,1,0:T(8,128)(2,1)S(1)}, bf16[3,144,896]{2,1,0:T(8,128)(2,1)}, u32[]{:S(2)}, u32[]{:S(2)}) collective-permute-start(bf16[3,144,896]{2,1,0:T(8,128)(2,1)S(1)} %pad_maximum_fusion.refs_5_), channel_id=1, source_target_pairs={{0,16},{16,0},{1,17},{17,1},{2,18},{18,2},{3,19},{19,3},{4,20},{20... | collective-permute-start | bytes 2322440 | tf_op jit(solution)/shard_map/ppermute | solution.py:380
  74.6 36.3 %collective-permute-start.8 = (bf16[3,144,896]{2,1,0:T(8,128)(2,1)}, bf16[3,144,896]{2,1,0:T(8,128)(2,1)}, u32[]{:S(2)}, u32[]{:S(2)}) collective-permute-start(bf16[3,144,896]{2,1,0:T(8,128)(2,1)} %collective-permute-done.3.refs_6_), channel_id=1, source_target_pairs={{0,16},{16,0},{1,17},{17,1},{2,18},{18,2},{3,19},{19,3},{4,20},{20... | collective-permute-start | bytes 2322440 | tf_op jit(solution)/shard_map/ppermute | solution.py:380
  75.1 35.8 %collective-permute-start.9 = (bf16[3,144,896]{2,1,0:T(8,128)(2,1)}, bf16[3,144,896]{2,1,0:T(8,128)(2,1)}, u32[]{:S(2)}, u32[]{:S(2)}) collective-permute-start(bf16[3,144,896]{2,1,0:T(8,128)(2,1)} %collective-permute-done.4.refs_7_), channel_id=1, source_target_pairs={{0,16},{16,0},{1,17},{17,1},{2,18},{18,2},{3,19},{19,3},{4,20},{20... | collective-permute-start | bytes 2322440 | tf_op jit(solution)/shard_map/ppermute | solution.py:380
  82.9 28.1 %collective-permute-start.10 = (bf16[3,144,896]{2,1,0:T(8,128)(2,1)}, bf16[3,144,896]{2,1,0:T(8,128)(2,1)}, u32[]{:S(2)}, u32[]{:S(2)}) collective-permute-start(bf16[3,144,896]{2,1,0:T(8,128)(2,1)} %constant_dynamic-update-slice_fusion.refs_8_), channel_id=1, source_target_pairs={{0,16},{16,0},{1,17},{17,1},{2,18},{18,2},{3,19},{19,3},{4,20},{20... | collective-permute-start | bytes 2322440 | tf_op jit(solution)/shard_map/ppermute | solution.py:380
  83.8 10.5 %collective-permute-start.16 = (bf16[112,896]{1,0:T(8,128)(2,1)S(1)}, bf16[112,896]{1,0:T(8,128)(2,1)S(1)}, u32[]{:S(2)}, u32[]{:S(2)}) collective-permute-start(bf16[112,896]{1,0:T(8,128)(2,1)S(1)} %dynamic-slice_select_fusion.2), channel_id=1, source_target_pairs={{0,2},{1,3},{2,0},{3,1},{4,6},{5,7},{6,4},{7,5},{8,10},{9,11},{10,... | collective-permute-start | bytes 602120 | tf_op jit(solution)/shard_map/ppermute | solution.py:380
  94.3 7.0 %collective-permute-start.15 = (bf16[112,896]{1,0:T(8,128)(2,1)S(1)}, bf16[112,896]{1,0:T(8,128)(2,1)S(1)}, u32[]{:S(2)}, u32[]{:S(2)}) collective-permute-start(bf16[112,896]{1,0:T(8,128)(2,1)S(1)} %dynamic-slice_select_fusion.2), channel_id=1, source_target_pairs={{0,1},{1,0},{2,3},{3,2},{4,5},{5,4},{6,7},{7,6},{8,9},{9,8},{10,11... | collective-permute-start | bytes 602120 | tf_op jit(solution)/shard_map/ppermute | solution.py:380
  101.3 6.1 %collective-permute-start.17 = (bf16[112,896]{1,0:T(8,128)(2,1)S(1)}, bf16[112,896]{1,0:T(8,128)(2,1)S(1)}, u32[]{:S(2)}, u32[]{:S(2)}) collective-permute-start(bf16[112,896]{1,0:T(8,128)(2,1)S(1)} %collective-permute-done.16), channel_id=1, source_target_pairs={{0,1},{1,0},{2,3},{3,2},{4,5},{5,4},{6,7},{7,6},{8,9},{9,8},{10,11... | collective-permute-start | bytes 602120 | tf_op jit(solution)/shard_map/ppermute | solution.py:380
  109.3 37.3 %collective-permute-start.18 = (bf16[3,112,896]{2,1,0:T(8,128)(2,1)S(1)}, bf16[3,112,896]{2,1,0:T(8,128)(2,1)}, u32[]{:S(2)}, u32[]{:S(2)}) collective-permute-start(bf16[3,112,896]{2,1,0:T(8,128)(2,1)S(1)} %pad_maximum_fusion.1.refs_10_), channel_id=1, source_target_pairs={{0,4},{4,0},{8,12},{12,8},{1,5},{5,1},{9,13},{13,9},{2,6},{6,2},{1... | collective-permute-start | bytes 1806344 | tf_op jit(solution)/shard_map/ppermute | solution.py:380
  129.5 11.8 %collective-permute-start.12 = (bf16[2,640,128]{2,1,0:T(8,128)(2,1)}, bf16[2,640,128]{2,1,0:T(8,128)(2,1)S(1)}, u32[]{:S(2)}, u32[]{:S(2)}) collective-permute-start(bf16[2,640,128]{2,1,0:T(8,128)(2,1)} %get-tuple-element.15), channel_id=1, source_target_pairs={{0,8},{4,12},{1,9},{5,13},{2,10},{6,14},{3,11},{7,15},{16,24},{20,... | collective-permute-start | bytes 983048 | tf_op jit(solution)/shard_map/ppermute | solution.py:432
  132.9 10.6 %collective-permute-start.11 = (bf16[2,640,128]{2,1,0:T(8,128)(2,1)}, bf16[2,640,128]{2,1,0:T(8,128)(2,1)S(1)}, u32[]{:S(2)}, u32[]{:S(2)}) collective-permute-start(bf16[2,640,128]{2,1,0:T(8,128)(2,1)} %get-tuple-element.14), channel_id=1, source_target_pairs={{0,4},{4,0},{8,12},{12,8},{1,5},{5,1},{9,13},{13,9},{2,6},{6,2},{1... | collective-permute-start | bytes 983048 | tf_op jit(solution)/shard_map/ppermute | solution.py:380
  133.7 49.7 %collective-permute-start.35 = (f32[3,1536]{1,0:T(4,128)S(1)}, f32[3,1536]{1,0:T(4,128)S(1)}, u32[]{:S(2)}, u32[]{:S(2)}) collective-permute-start(f32[3,1536]{1,0:T(4,128)S(1)} %reshape.326), channel_id=1, source_target_pairs={{0,2},{1,3},{2,0},{3,1},{4,6},{5,7},{6,4},{7,5},{8,10},{9,11},{10,... | collective-permute-start | bytes 55304 | tf_op jit(solution)/shard_map/ppermute | solution.py:380
  135.7 18.4 %collective-permute-start.19 = (bf16[3,112,896]{2,1,0:T(8,128)(2,1)S(1)}, bf16[3,112,896]{2,1,0:T(8,128)(2,1)}, u32[]{:S(2)}, u32[]{:S(2)}) collective-permute-start(bf16[3,112,896]{2,1,0:T(8,128)(2,1)S(1)} %pad_maximum_fusion.1.refs_10_), channel_id=1, source_target_pairs={{0,8},{4,12},{8,0},{12,4},{1,9},{5,13},{9,1},{13,5},{2,10},{6,14},... | collective-permute-start | bytes 1806344 | tf_op jit(solution)/shard_map/ppermute | solution.py:380
  141.3 42.2 %collective-permute-start.39 = (bf16[112,896]{1,0:T(8,128)(2,1)S(1)}, bf16[112,896]{1,0:T(8,128)(2,1)S(1)}, u32[]{:S(2)}, u32[]{:S(2)}) collective-permute-start(bf16[112,896]{1,0:T(8,128)(2,1)S(1)} %dynamic-slice_select_fusion.1), channel_id=1, source_target_pairs={{0,2},{1,3},{2,0},{3,1},{4,6},{5,7},{6,4},{7,5},{8,10},{9,11},{10,... | collective-permute-start | bytes 602120 | tf_op jit(solution)/shard_map/ppermute | solution.py:380
  143.5 31.5 %collective-permute-start.20 = (bf16[336,896]{1,0:T(8,128)(2,1)S(1)}, bf16[336,896]{1,0:T(8,128)(2,1)S(1)}, u32[]{:S(2)}, u32[]{:S(2)}) collective-permute-start(bf16[336,896]{1,0:T(8,128)(2,1)S(1)} %bitcast.68), channel_id=1, source_target_pairs={{0,2},{1,3},{2,0},{3,1},{4,6},{5,7},{6,4},{7,5},{8,10},{9,11},{10,... | collective-permute-start | bytes 1806344 | tf_op jit(solution)/shard_map/ppermute | solution.py:380
  146.6 11.5 %collective-permute-start.13 = (bf16[2,640,128]{2,1,0:T(8,128)(2,1)S(1)}, bf16[2,640,128]{2,1,0:T(8,128)(2,1)S(1)}, u32[]{:S(2)}, u32[]{:S(2)}) collective-permute-start(bf16[2,640,128]{2,1,0:T(8,128)(2,1)S(1)} %fusion.5), channel_id=1, source_target_pairs={{0,8},{4,12},{1,9},{5,13},{2,10},{6,14},{3,11},{7,15},{16,24},{20,... | collective-permute-start | bytes 983048 | tf_op jit(solution)/shard_map/ppermute | solution.py:437
  154.1 37.6 %collective-permute-start.23 = (bf16[3,112,896]{2,1,0:T(8,128)(2,1)S(1)}, bf16[3,112,896]{2,1,0:T(8,128)(2,1)S(1)}, u32[]{:S(2)}, u32[]{:S(2)}) collective-permute-start(bf16[3,112,896]{2,1,0:T(8,128)(2,1)S(1)} %pad_maximum_fusion.1.refs_10_), channel_id=1, source_target_pairs={{0,16},{16,0},{1,17},{17,1},{2,18},{18,2},{3,19},{19,3},{4,20},{20... | collective-permute-start | bytes 1806344 | tf_op jit(solution)/shard_map/ppermute | solution.py:380
  158.1 23.8 %collective-permute-start.21 = (bf16[3,64,896]{2,1,0:T(8,128)(2,1)S(1)}, bf16[3,64,896]{2,1,0:T(8,128)(2,1)S(1)}, u32[]{:S(2)}, u32[]{:S(2)}) collective-permute-start(bf16[3,64,896]{2,1,0:T(8,128)(2,1)S(1)} %slice_select_fusion.2), channel_id=1, source_target_pairs={{0,4},{4,0},{8,12},{12,8},{1,5},{5,1},{9,13},{13,9},{2,6},{6,2},{1... | collective-permute-start | bytes 1032200 | tf_op jit(solution)/shard_map/ppermute | solution.py:380
  159.8 23.8 %copy-start.45 = (bf16[2,640,128]{2,1,0:T(8,128)(2,1)S(1)}, bf16[2,640,128]{2,1,0:T(8,128)(2,1)}, u32[]{:S(2)}) copy-start(bf16[2,640,128]{2,1,0:T(8,128)(2,1)} %copy-done.44) | copy-start | bytes 983044
  175.0 6.9 %collective-permute-start.22 = (bf16[3,48,896]{2,1,0:T(8,128)(2,1)S(1)}, bf16[3,48,896]{2,1,0:T(8,128)(2,1)S(1)}, u32[]{:S(2)}, u32[]{:S(2)}) collective-permute-start(bf16[3,48,896]{2,1,0:T(8,128)(2,1)S(1)} %slice_select_fusion.5), channel_id=1, source_target_pairs={{0,8},{4,12},{8,0},{12,4},{1,9},{5,13},{9,1},{13,5},{2,10},{6,14},... | collective-permute-start | bytes 774152 | tf_op jit(solution)/shard_map/ppermute | solution.py:380
  181.9 11.2 %collective-permute-start.24 = (bf16[3,112,896]{2,1,0:T(8,128)(2,1)}, bf16[3,112,896]{2,1,0:T(8,128)(2,1)S(1)}, u32[]{:S(2)}, u32[]{:S(2)}) collective-permute-start(bf16[3,112,896]{2,1,0:T(8,128)(2,1)} %collective-permute-done.18.refs_11_), channel_id=1, source_target_pairs={{0,16},{16,0},{1,17},{17,1},{2,18},{18,2},{3,19},{19,3},{4,20},{20... | collective-permute-start | bytes 1806344 | tf_op jit(solution)/shard_map/ppermute | solution.py:380
  181.9 13.8 %collective-permute-start.25 = (bf16[3,112,896]{2,1,0:T(8,128)(2,1)}, bf16[3,112,896]{2,1,0:T(8,128)(2,1)}, u32[]{:S(2)}, u32[]{:S(2)}) collective-permute-start(bf16[3,112,896]{2,1,0:T(8,128)(2,1)} %collective-permute-done.19.refs_12_), channel_id=1, source_target_pairs={{0,16},{16,0},{1,17},{17,1},{2,18},{18,2},{3,19},{19,3},{4,20},{20... | collective-permute-start | bytes 1806344 | tf_op jit(solution)/shard_map/ppermute | solution.py:380
  182.4 20.3 %copy-start.29 = (f32[1,1024]{1,0:T(1,128)S(1)}, f32[1,1024]{1,0:T(1,128)}, u32[]{:S(2)}) copy-start(f32[1,1024]{1,0:T(1,128)} %constant.140.clone.refs_6_) | copy-start | bytes 12292
  183.4 6.9 %collective-permute-start.40 = (bf16[112,896]{1,0:T(8,128)(2,1)S(1)}, bf16[112,896]{1,0:T(8,128)(2,1)S(1)}, u32[]{:S(2)}, u32[]{:S(2)}) collective-permute-start(bf16[112,896]{1,0:T(8,128)(2,1)S(1)} %dynamic-slice_select_fusion.1), channel_id=1, source_target_pairs={{0,1},{1,0},{2,3},{3,2},{4,5},{5,4},{6,7},{7,6},{8,9},{9,8},{10,11... | collective-permute-start | bytes 602120 | tf_op jit(solution)/shard_map/ppermute | solution.py:380
  183.5 18.9 %collective-permute-start.26 = (bf16[3,112,896]{2,1,0:T(8,128)(2,1)}, bf16[3,112,896]{2,1,0:T(8,128)(2,1)}, u32[]{:S(2)}, u32[]{:S(2)}) collective-permute-start(bf16[3,112,896]{2,1,0:T(8,128)(2,1)} %maximum_select_fusion.refs_13_), channel_id=1, source_target_pairs={{0,16},{16,0},{1,17},{17,1},{2,18},{18,2},{3,19},{19,3},{4,20},{20... | collective-permute-start | bytes 1806344 | tf_op jit(solution)/shard_map/ppermute | solution.py:380
  190.3 11.0 %collective-permute-start.14 = (bf16[2,640,128]{2,1,0:T(8,128)(2,1)}, bf16[2,640,128]{2,1,0:T(8,128)(2,1)}, u32[]{:S(2)}, u32[]{:S(2)}) collective-permute-start(bf16[2,640,128]{2,1,0:T(8,128)(2,1)} %fusion.4), channel_id=1, source_target_pairs={{0,4},{4,0},{8,12},{12,8},{1,5},{5,1},{9,13},{13,9},{2,6},{6,2},{1... | collective-permute-start | bytes 983048 | tf_op jit(solution)/shard_map/ppermute | solution.py:380
  192.6 27.4 %collective-permute-start.28 = (bf16[1,336,896]{2,1,0:T(8,128)(2,1)}, bf16[1,336,896]{2,1,0:T(8,128)(2,1)}, u32[]{:S(2)}, u32[]{:S(2)}) collective-permute-start(bf16[1,336,896]{2,1,0:T(8,128)(2,1)} %get-tuple-element.21.refs_5_), channel_id=1, source_target_pairs={{0,4},{4,0},{8,12},{12,8},{1,5},{5,1},{9,13},{13,9},{2,6},{6,2},{1... | collective-permute-start | bytes 1806344 | tf_op jit(solution)/shard_map/ppermute | solution.py:380
  194.0 29.4 %collective-permute-start.29 = (bf16[1,336,896]{2,1,0:T(8,128)(2,1)}, bf16[1,336,896]{2,1,0:T(8,128)(2,1)}, u32[]{:S(2)}, u32[]{:S(2)}) collective-permute-start(bf16[1,336,896]{2,1,0:T(8,128)(2,1)} %get-tuple-element.21.refs_5_), channel_id=1, source_target_pairs={{0,8},{4,12},{8,0},{12,4},{1,9},{5,13},{9,1},{13,5},{2,10},{6,14},... | collective-permute-start | bytes 1806344 | tf_op jit(solution)/shard_map/ppermute | solution.py:380
  195.7 30.6 %collective-permute-start.30 = (bf16[1,336,896]{2,1,0:T(8,128)(2,1)}, bf16[1,336,896]{2,1,0:T(8,128)(2,1)}, u32[]{:S(2)}, u32[]{:S(2)}) collective-permute-start(bf16[1,336,896]{2,1,0:T(8,128)(2,1)} %get-tuple-element.21.refs_5_), channel_id=1, source_target_pairs={{0,12},{4,8},{8,4},{12,0},{1,13},{5,9},{9,5},{13,1},{2,14},{6,10},... | collective-permute-start | bytes 1806344 | tf_op jit(solution)/shard_map/ppermute | solution.py:380
  201.2 25.1 %collective-permute-start.31 = (bf16[1,336,896]{2,1,0:T(8,128)(2,1)}, bf16[1,336,896]{2,1,0:T(8,128)(2,1)S(1)}, u32[]{:S(2)}, u32[]{:S(2)}) collective-permute-start(bf16[1,336,896]{2,1,0:T(8,128)(2,1)} %get-tuple-element.21.refs_5_), channel_id=1, source_target_pairs={{0,16},{16,0},{1,17},{17,1},{2,18},{18,2},{3,19},{19,3},{4,20},{20... | collective-permute-start | bytes 1806344 | tf_op jit(solution)/shard_map/ppermute | solution.py:380
  202.4 15.7 %collective-permute-start.41 = (bf16[112,896]{1,0:T(8,128)(2,1)}, bf16[112,896]{1,0:T(8,128)(2,1)S(1)}, u32[]{:S(2)}, u32[]{:S(2)}) collective-permute-start(bf16[112,896]{1,0:T(8,128)(2,1)} %copy-done.49), channel_id=1, source_target_pairs={{0,1},{1,0},{2,3},{3,2},{4,5},{5,4},{6,7},{7,6},{8,9},{9,8},{10,11... | collective-permute-start | bytes 602120 | tf_op jit(solution)/shard_map/ppermute | solution.py:380
  207.7 24.2 %copy-start.50 = (bf16[112,896]{1,0:T(8,128)(2,1)S(1)}, bf16[112,896]{1,0:T(8,128)(2,1)}, u32[]{:S(2)}) copy-start(bf16[112,896]{1,0:T(8,128)(2,1)} %copy-done.49) | copy-start | bytes 602116
  207.7 24.2 %copy-start.52 = (bf16[112,896]{1,0:T(8,128)(2,1)S(1)}, bf16[112,896]{1,0:T(8,128)(2,1)}, u32[]{:S(2)}) copy-start(bf16[112,896]{1,0:T(8,128)(2,1)} %copy-done.51) | copy-start | bytes 602116
  218.2 34.6 %collective-permute-start.36 = (bf16[256,1792]{1,0:T(8,128)(2,1)}, bf16[256,1792]{1,0:T(8,128)(2,1)}, u32[]{:S(2)}, u32[]{:S(2)}) collective-permute-start(bf16[256,1792]{1,0:T(8,128)(2,1)} %get-tuple-element.16.refs_2_), channel_id=1, source_target_pairs={{0,1},{1,0},{2,3},{3,2},{4,5},{5,4},{6,7},{7,6},{8,9},{9,8},{10,11... | collective-permute-start | bytes 2752520 | tf_op jit(solution)/shard_map/ppermute | solution.py:380
  220.0 10.2 %collective-permute-start.27 = (bf16[80,1792]{1,0:T(8,128)(2,1)S(1)}, bf16[80,1792]{1,0:T(8,128)(2,1)S(1)}, u32[]{:S(2)}, u32[]{:S(2)}) collective-permute-start(bf16[80,1792]{1,0:T(8,128)(2,1)S(1)} %get-tuple-element.17), channel_id=1, source_target_pairs={{0,4},{4,8},{8,12},{1,5},{5,9},{9,13},{2,6},{6,10},{10,14},{3,7},{... | collective-permute-start | bytes 860168 | tf_op jit(solution)/shard_map/ppermute | solution.py:608
  223.4 25.9 %collective-permute-start.32 = (bf16[1,336,896]{2,1,0:T(8,128)(2,1)}, bf16[1,336,896]{2,1,0:T(8,128)(2,1)S(1)}, u32[]{:S(2)}, u32[]{:S(2)}) collective-permute-start(bf16[1,336,896]{2,1,0:T(8,128)(2,1)} %collective-permute-done.28.refs_6_), channel_id=1, source_target_pairs={{0,16},{16,0},{1,17},{17,1},{2,18},{18,2},{3,19},{19,3},{4,20},{20... | collective-permute-start | bytes 1806344 | tf_op jit(solution)/shard_map/ppermute | solution.py:380
  226.3 25.6 %collective-permute-start.33 = (bf16[1,336,896]{2,1,0:T(8,128)(2,1)}, bf16[1,336,896]{2,1,0:T(8,128)(2,1)S(1)}, u32[]{:S(2)}, u32[]{:S(2)}) collective-permute-start(bf16[1,336,896]{2,1,0:T(8,128)(2,1)} %collective-permute-done.29.refs_7_), channel_id=1, source_target_pairs={{0,16},{16,0},{1,17},{17,1},{2,18},{18,2},{3,19},{19,3},{4,20},{20... | collective-permute-start | bytes 1806344 | tf_op jit(solution)/shard_map/ppermute | solution.py:380
  227.2 25.5 %collective-permute-start.34 = (bf16[1,336,896]{2,1,0:T(8,128)(2,1)}, bf16[1,336,896]{2,1,0:T(8,128)(2,1)}, u32[]{:S(2)}, u32[]{:S(2)}) collective-permute-start(bf16[1,336,896]{2,1,0:T(8,128)(2,1)} %collective-permute-done.30.refs_8_), channel_id=1, source_target_pairs={{0,16},{16,0},{1,17},{17,1},{2,18},{18,2},{3,19},{19,3},{4,20},{20... | collective-permute-start | bytes 1806344 | tf_op jit(solution)/shard_map/ppermute | solution.py:380
  230.2 16.9 %collective-permute-start.37 = (bf16[80,1792]{1,0:T(8,128)(2,1)S(1)}, bf16[80,1792]{1,0:T(8,128)(2,1)S(1)}, u32[]{:S(2)}, u32[]{:S(2)}) collective-permute-start(bf16[80,1792]{1,0:T(8,128)(2,1)S(1)} %collective-permute-done.27.refs_3_), channel_id=1, source_target_pairs={{0,1},{1,0},{2,3},{3,2},{4,5},{5,4},{6,7},{7,6},{8,9},{9,8},{10,11... | collective-permute-start | bytes 860168 | tf_op jit(solution)/shard_map/ppermute | solution.py:380
  247.8 29.8 %collective-permute-start.42 = (bf16[3,112,896]{2,1,0:T(8,128)(2,1)S(1)}, bf16[3,112,896]{2,1,0:T(8,128)(2,1)S(1)}, u32[]{:S(2)}, u32[]{:S(2)}) collective-permute-start(bf16[3,112,896]{2,1,0:T(8,128)(2,1)S(1)} %maximum_select_fusion.1.refs_5_), channel_id=1, source_target_pairs={{0,4},{4,0},{8,12},{12,8},{1,5},{5,1},{9,13},{13,9},{2,6},{6,2},{1... | collective-permute-start | bytes 1806344 | tf_op jit(solution)/shard_map/ppermute | solution.py:380
  250.2 27.8 %collective-permute-start.43 = (bf16[3,112,896]{2,1,0:T(8,128)(2,1)S(1)}, bf16[3,112,896]{2,1,0:T(8,128)(2,1)S(1)}, u32[]{:S(2)}, u32[]{:S(2)}) collective-permute-start(bf16[3,112,896]{2,1,0:T(8,128)(2,1)S(1)} %maximum_select_fusion.1.refs_5_), channel_id=1, source_target_pairs={{0,8},{4,12},{8,0},{12,4},{1,9},{5,13},{9,1},{13,5},{2,10},{6,14},... | collective-permute-start | bytes 1806344 | tf_op jit(solution)/shard_map/ppermute | solution.py:380
  252.7 49.6 %collective-permute-start.46 = (bf16[3,112,896]{2,1,0:T(8,128)(2,1)S(1)}, bf16[3,112,896]{2,1,0:T(8,128)(2,1)}, u32[]{:S(2)}, u32[]{:S(2)}) collective-permute-start(bf16[3,112,896]{2,1,0:T(8,128)(2,1)S(1)} %maximum_select_fusion.1.refs_5_), channel_id=1, source_target_pairs={{0,16},{16,0},{1,17},{17,1},{2,18},{18,2},{3,19},{19,3},{4,20},{20... | collective-permute-start | bytes 1806344 | tf_op jit(solution)/shard_map/ppermute | solution.py:380
  259.3 19.4 %copy-start.33 = (bf16[1,336,896]{2,1,0:T(8,128)(2,1)S(1)}, bf16[1,336,896]{2,1,0:T(8,128)(2,1)}, u32[]{:S(2)}) copy-start(bf16[1,336,896]{2,1,0:T(8,128)(2,1)} %copy-done.31) | copy-start | bytes 1806340
  259.3 19.4 %copy-start.36 = (bf16[1,336,896]{2,1,0:T(8,128)(2,1)S(1)}, bf16[1,336,896]{2,1,0:T(8,128)(2,1)}, u32[]{:S(2)}) copy-start(bf16[1,336,896]{2,1,0:T(8,128)(2,1)} %copy-done.34) | copy-start | bytes 1806340
  259.3 19.4 %copy-start.40 = (bf16[80,1792]{1,0:T(8,128)(2,1)S(1)}, bf16[80,1792]{1,0:T(8,128)(2,1)}, u32[]{:S(2)}) copy-start(bf16[80,1792]{1,0:T(8,128)(2,1)} %copy-done.39) | copy-start | bytes 860164
  274.6 23.1 %collective-permute-start.38 = (bf16[2,256,512]{2,1,0:T(8,128)(2,1)S(1)}, bf16[2,256,512]{2,1,0:T(8,128)(2,1)S(1)}, u32[]{:S(2)}, u32[]{:S(2)}) collective-permute-start(bf16[2,256,512]{2,1,0:T(8,128)(2,1)S(1)} %window_rows.3), channel_id=1, source_target_pairs={{0,1},{1,0},{2,3},{3,2},{4,5},{5,4},{6,7},{7,6},{8,9},{9,8},{10,11... | collective-permute-start | bytes 1572872 | tf_op jit(solution)/shard_map/ppermute | solution.py:380
  277.6 19.3 %copy-start.8 = (bf16[3,112,896]{2,1,0:T(8,128)(2,1)}, bf16[3,112,896]{2,1,0:T(8,128)(2,1)S(1)}, u32[]{:S(2)}) copy-start(bf16[3,112,896]{2,1,0:T(8,128)(2,1)S(1)} %collective-permute-done.42.refs_6_) | copy-start | bytes 1806340
  277.6 23.1 %collective-permute-start.45 = (bf16[3,48,896]{2,1,0:T(8,128)(2,1)S(1)}, bf16[3,48,896]{2,1,0:T(8,128)(2,1)S(1)}, u32[]{:S(2)}, u32[]{:S(2)}) collective-permute-start(bf16[3,48,896]{2,1,0:T(8,128)(2,1)S(1)} %slice_select_fusion.4), channel_id=1, source_target_pairs={{0,8},{4,12},{8,0},{12,4},{1,9},{5,13},{9,1},{13,5},{2,10},{6,14},... | collective-permute-start | bytes 774152 | tf_op jit(solution)/shard_map/ppermute | solution.py:380
  278.0 19.7 %copy-start.6 = (bf16[3,112,896]{2,1,0:T(8,128)(2,1)}, bf16[3,112,896]{2,1,0:T(8,128)(2,1)S(1)}, u32[]{:S(2)}) copy-start(bf16[3,112,896]{2,1,0:T(8,128)(2,1)S(1)} %collective-permute-done.43.refs_7_) | copy-start | bytes 1806340
  278.0 22.7 %collective-permute-start.44 = (bf16[3,64,896]{2,1,0:T(8,128)(2,1)S(1)}, bf16[3,64,896]{2,1,0:T(8,128)(2,1)S(1)}, u32[]{:S(2)}, u32[]{:S(2)}) collective-permute-start(bf16[3,64,896]{2,1,0:T(8,128)(2,1)S(1)} %slice_select_fusion.1), channel_id=1, source_target_pairs={{0,4},{4,0},{8,12},{12,8},{1,5},{5,1},{9,13},{13,9},{2,6},{6,2},{1... | collective-permute-start | bytes 1032200 | tf_op jit(solution)/shard_map/ppermute | solution.py:380
  281.1 19.9 %copy-start.56 = (s32[8]{0:T(128)S(1)}, s32[8]{0:T(128)}, u32[]{:S(2)}) copy-start(s32[8]{0:T(128)} %param.20) | copy-start | bytes 100
  281.1 19.9 %copy-start.57 = (s32[8]{0:T(128)S(1)}, s32[8]{0:T(128)}, u32[]{:S(2)}) copy-start(s32[8]{0:T(128)} %param.19) | copy-start | bytes 100
  297.7 4.7 %collective-permute-start.47 = (bf16[3,112,896]{2,1,0:T(8,128)(2,1)S(1)}, bf16[3,112,896]{2,1,0:T(8,128)(2,1)}, u32[]{:S(2)}, u32[]{:S(2)}) collective-permute-start(bf16[3,112,896]{2,1,0:T(8,128)(2,1)S(1)} %collective-permute-done.42.refs_6_), channel_id=1, source_target_pairs={{0,16},{16,0},{1,17},{17,1},{2,18},{18,2},{3,19},{19,3},{4,20},{20... | collective-permute-start | bytes 1806344 | tf_op jit(solution)/shard_map/ppermute | solution.py:380
  297.7 4.7 %collective-permute-start.48 = (bf16[3,112,896]{2,1,0:T(8,128)(2,1)S(1)}, bf16[3,112,896]{2,1,0:T(8,128)(2,1)}, u32[]{:S(2)}, u32[]{:S(2)}) collective-permute-start(bf16[3,112,896]{2,1,0:T(8,128)(2,1)S(1)} %collective-permute-done.43.refs_7_), channel_id=1, source_target_pairs={{0,16},{16,0},{1,17},{17,1},{2,18},{18,2},{3,19},{19,3},{4,20},{20... | collective-permute-start | bytes 1806344 | tf_op jit(solution)/shard_map/ppermute | solution.py:380
  300.8 2.2 collective-permute-start.49
  (46 other events, 185.1 us)

commit v7 on v5

--- a/solution.py
+++ b/solution.py
@@ -267,6 +267,7 @@
     near_ref,
     far_ref,
     tap_ref,
+    _,
     mixed_ref,
     rows_ref,
     w_ref,
@@ -367,7 +368,7 @@
 HBM = pl.BlockSpec(memory_space=pl.ANY)
 
 
-def call(kernel, groups, in_specs, out_specs, out_shape, scratch, name):
+def call(kernel, groups, in_specs, out_specs, out_shape, scratch, name, flops=0):
     return pl.pallas_call(
         kernel,
         grid=(groups,),
@@ -378,7 +379,7 @@
         compiler_params=pltpu.CompilerParams(
             dimension_semantics=("arbitrary",), vmem_limit_bytes=VMEM
         ),
-        cost_estimate=pl.CostEstimate(flops=0, bytes_accessed=0, transcendentals=0),
+        cost_estimate=pl.CostEstimate(flops=flops, bytes_accessed=0, transcendentals=0),
         name=name,
     )
 
@@ -426,13 +427,16 @@
 
 
 def from_plane(held, near_by, diagonal, over_cores):
-    half = -(-held.shape[1] // 32) * 16
     beside, above = near_by
-    opposite = [
-        across(after(above[:, :half], diagonal), "seq", 1),
-        across(after(beside[:, half:], diagonal), "seq", 2),
-    ]
-    opposite = after(jnp.concatenate(opposite, axis=1), over_cores)
+    if diagonal is None:
+        opposite = across(held, "seq", 3)
+    else:
+        half = -(-held.shape[1] // 32) * 16
+        opposite = [
+            across(after(above[:, :half], diagonal), "seq", 1),
+            across(after(beside[:, half:], diagonal), "seq", 2),
+        ]
+        opposite = after(jnp.concatenate(opposite, axis=1), over_cores)
     near = after(jnp.stack([held, beside, above, opposite]), over_cores)
     return near, across(near, "dp", 1)
 
@@ -520,9 +524,9 @@
     length = jnp.sum(jnp.where(jnp.arange(slots_total) == slot, slot_lengths, 0))
 
     held_out_one = settled(jnp.stack(from_groups(own_piece([out_one]), (picked,))))
-    near_one = from_plane(held_one, neighbours(held_one), (), (held_out_one,))
-    held_window = from_group(own_piece([window_t]), (swapped,))
-    held_out_two = from_groups(own_piece([out_two]), (swapped,), (1, 0, 2))
+    near_one = from_plane(held_one, neighbours(held_one), (swapped,), (held_out_one,))
+    out_piece = after(own_piece([out_two]), (swapped,))
+    beyond = from_group(own_piece([window_t, out_two]), (swapped,))
     places = jnp.concatenate([(seq_place % NEAR) ^ jnp.arange(NEAR), dp_place[None]])
     places = places.astype(jnp.int32)
     taps = conv_window.reshape(tap_count, 3, heads, HEAD).transpose(0, 2, 1, 3)
@@ -572,11 +576,15 @@
         places, tokens, gain_one[None], values_t, featmap_t, *near_one, first, second, ones, column
     )
     prior = settled(earlier_blocks(state, "seq"))
-    held_out_one = after(held_out_one, (swapped,))
+    beyond = after(beyond, (state,))
+    held_window, out_beyond = beyond[:, : 3 * HEAD], beyond[0, 3 * HEAD :]
+    held_out_two = [out_beyond, across(out_piece, "tensor", 1), across(out_beyond, "tensor", 1)]
+    held_out_two = settled(jnp.stack(held_out_two), (prior,))
     near_out_one = from_plane(
-        held_out_one, neighbours(held_out_one), (state,), (prior, held_window)
-    )
-    held_out_two = settled(jnp.stack(held_out_two), (state,))
+        held_out_one, neighbours(held_out_one), (state,), (beyond, held_out_two)
+    )
+    held_window = after(held_window, (prior,))
+    near_by_window = neighbours(held_window)
     residual, normed_two, tail = call(
         functools.partial(out_one_kernel, heads, kept),
         group_count,
@@ -620,17 +628,11 @@
             for j in range(group_count)
         ],
     )
-    held_window, held_out_two = after(held_window, (prior,)), after(held_out_two, (residual,))
-    near_by = neighbours(held_out_two)
-    near_window = from_plane(
-        held_window,
-        neighbours(held_window),
-        (residual, held_out_two),
-        (pair_rows, halo, pair_halo, *near_by),
-    )
+    near_window = from_plane(held_window, near_by_window, None, (residual,))
+    held_out_two = after(held_out_two, (residual,))
     block_start = (seq_place * rows).astype(jnp.int32)[None]
 
-    def window_rows(slot_rows, slot_halo):
+    def window_rows(slot_rows, slot_halo, earlier):
         return call(
             functools.partial(window_kernel, heads),
             2,
@@ -641,6 +643,7 @@
                 whole((HALO, width)),
                 *[HBM] * 3,
                 each((tap_count, 3 * slots)),
+                HBM,
             ],
             each((rows, slots)),
             jax.ShapeDtypeStruct((2, rows, slots), BF16),
@@ -650,12 +653,13 @@
                 copy_sems(3),
             ],
             "window_rows",
-        )(places, block_start, slot_rows, slot_halo, window_t, *near_window, taps)
-
-    mixed_pair = window_rows(pair_rows, pair_halo)
-    near_out_two = from_plane(held_out_two, near_by, (pair_rows,), (mixed_pair,))
+            6 * rows * width * 3 * head_cols,
+        )(places, block_start, slot_rows, slot_halo, window_t, *near_window, taps, earlier)
+
+    mixed_own = window_rows(normed_two, halo, normed_two)
+    mixed_pair = window_rows(pair_rows, pair_halo, mixed_own)
+    near_out_two = from_plane(held_out_two, neighbours(held_out_two), None, (mixed_pair,))
     mixed_pair = across(mixed_pair, "tensor", 1)
-    mixed_own = window_rows(normed_two, halo)
     live = (length - seq_place * rows).astype(jnp.int32)[None]
     result = call(
         out_two_kernel,

time: 324 us -> 309 us (0.954)
  blocking collectives: 56.1 us -> 26.2 us
  waiting for transfers between devices: 77.6 us -> 90.9 us
  starting transfers between devices: 49.5 us -> 60.5 us
  other arithmetic: 28.5 us -> 21.7 us
    all_to_all x1 -> x0, blocking collectives: 29.1 us -> none  [on_device(): lax.all_to_all(picked, 'tensor', split_axis=0, concat_axis=0, tiled=True)]
    all_to_all x0 -> x1, waiting for transfers between devices: none -> 18.8 us  [on_device(): lax.all_to_all(picked, 'tensor', split_axis=0, concat_axis=0, tiled=True)]
    ppermute x3, waiting for transfers between devices: 21 us -> 13.1 us  [earlier_blocks(): lax.ppermute(state, axis, [(i, i + by) for i in range(peers - by)])]
    select_n x20 -> x18, other arithmetic: 20.5 us -> 15 us  [after(): return jnp.where(zero == 0.0, array, jnp.zeros_like(array))]
    all_to_all x0 -> x1, starting transfers between devices: none -> 5.06 us  [on_device(): lax.all_to_all(picked, 'tensor', split_axis=0, concat_axis=0, tiled=True)]
    another operation x4 -> x2, other arithmetic: 4.48 us -> 1.19 us  [from_plane(): near = after(jnp.stack([held, beside, above, opposite]), over_cores)]
    slice x15 -> x10, local copies, waits for them, and re-layouts: 9.35 us -> 6.83 us  [after(): lax.slice(other, (0,) * other.ndim, (1,) * other.ndim)]
    ppermute x33 -> x30, waiting for transfers between devices: 56.7 us -> 58.9 us  [across(): lax.ppermute(array, axis, [(i, i ^ bit) for i in range(lax.axis_size(axis...]
  transfers between devices with their start and end apart: 39 -> 37, of which waited for: 19 -> 13; matrix products, arithmetic and copies ran while one was open for 12% -> 9% of each run, Pallas kernels for 18% -> 19%
where the time goes in v7:
time: 309 us; the launch traced here: 307 us
  waiting for transfers between devices  90.9 us (29%)
  Pallas kernels  67.3 us (22%)
  starting transfers between devices  60.5 us (20%)
  local copies, waits for them, and re-layouts  33 us (11%)
  blocking collectives  26.2 us (8%)
  other arithmetic  21.7 us (7%)
  between operations  7.96 us (3%)
    ppermute x30, waiting for transfers between devices, across(): lax.ppermute(array, axis, [(i, i ^ bit) for i in range(lax.axis_size(axis...  58.9 us
    ppermute x30, starting transfers between devices, across(): lax.ppermute(array, axis, [(i, i ^ bit) for i in range(lax.axis_size(axis...  34.3 us
    pallas_call x2, Pallas kernels, window_rows(): call(functools.partial(window_kernel, heads), 2, [SMEM, SMEM, whole((rows...  31.3 us
    all_to_all x1, blocking collectives, on_device(): lax.all_to_all(result, 'tensor', split_axis=0, concat_axis=0, tiled=True)  26.2 us
    all_to_all x1, waiting for transfers between devices, on_device(): lax.all_to_all(picked, 'tensor', split_axis=0, concat_axis=0, tiled=True)  18.8 us
    select_n x18, other arithmetic, after(): return jnp.where(zero == 0.0, array, jnp.zeros_like(array))  15 us
    pallas_call x1, Pallas kernels, on_device(): call(functools.partial(linear_kernel, heads, feature_dim, kept), group_co...  15 us
    unnamed x69, local copies, waits for them, and re-layouts  13.6 us
  transfers between devices with their start and end apart: 37, of which 13 were waited for; matrix products, arithmetic and copies ran while one was open for 9% of the time, Pallas kernels for 19%

profile of v7, /device:TPU:0, one launch (start us, length us, event | category | flops | bytes accessed | tf_op | source)
XLA Modules:
  0.0 307.5 jit_solution(4726394215534312452)
XLA Ops:
  2.5 2.2 gather_fusion
  4.7 5.2 %all-to-all-start = ((bf16[8,8,4,1792]{3,2,1,0:T(4,128)(2,1)}), bf16[8,8,4,1792]{3,2,1,0:T(4,128)(2,1)S(1)}, u32[]{:S(2)}, u32[]{:S(2)}) async-start(bf16[8,8,4,1792]{3,2,1,0:T(4,128)(2,1)} %bitcast.12), calls=%async_computation | async-start | bytes 1835008 | tf_op jit(solution)/shard_map/all_to_all | solution.py:514
  11.6 2.7 collective-permute-start.1
  14.3 1.6 collective-permute-start
  16.1 10.7 %collective-permute-done.1 = bf16[144,896]{1,0:T(8,128)(2,1)S(1)} collective-permute-done((bf16[144,896]{1,0:T(8,128)(2,1)S(1)}, bf16[144,896]{1,0:T(8,128)(2,1)S(1)}, u32[]{:S(2)}, u32[]{:S(2)}) %collective-permute-start.1) | collective-permute-done | bytes 258080 | tf_op jit(solution)/shard_map/ppermute | solution.py:399
  27.5 7.2 %collective-permute-done.2 = bf16[144,896]{1,0:T(8,128)(2,1)S(1)} collective-permute-done((bf16[144,896]{1,0:T(8,128)(2,1)S(1)}, bf16[144,896]{1,0:T(8,128)(2,1)S(1)}, u32[]{:S(2)}, u32[]{:S(2)}) %collective-permute-start.2) | collective-permute-done | bytes 258080 | tf_op jit(solution)/shard_map/ppermute | solution.py:399
  36.0 1.4 gather_fusion.1
  38.8 5.1 %all-to-all-start.1 = ((bf16[4,16,4,1792]{3,1,2,0:T(8,128)(2,1)}), bf16[4,16,4,1792]{3,1,2,0:T(8,128)(2,1)S(1)}, u32[]{:S(2)}, u32[]{:S(2)}) async-start(bf16[4,16,4,1792]{3,1,2,0:T(8,128)(2,1)} %copy.40), calls=%async_computation.1 | async-start | bytes 1835008 | tf_op jit(solution)/shard_map/all_to_all | solution.py:521
  43.9 1.6 collective-permute-start.7
  45.5 1.5 collective-permute-start.6
  48.1 1.7 dynamic-slice_select_fusion
  49.8 2.9 collective-permute-start.4
  52.7 18.8 %all-to-all-done.1 = bf16[4,16,4,1792]{3,1,2,0:T(8,128)(2,1)S(1)} async-done(((bf16[4,16,4,1792]{3,1,2,0:T(8,128)(2,1)}), bf16[4,16,4,1792]{3,1,2,0:T(8,128)(2,1)S(1)}, u32[]{:S(2)}, u32[]{:S(2)}) %all-to-all-start.1) | async-done | bytes 917536 | tf_op jit(solution)/shard_map/all_to_all | solution.py:521
  72.8 1.7 collective-permute-start.8
  75.5 1.5 collective-permute-start.9
  77.0 2.0 collective-permute-start.5
  79.0 4.7 %collective-permute-done.3 = bf16[112,896]{1,0:T(8,128)(2,1)S(1)} collective-permute-done((bf16[112,896]{1,0:T(8,128)(2,1)}, bf16[112,896]{1,0:T(8,128)(2,1)S(1)}, u32[]{:S(2)}, u32[]{:S(2)}) %collective-permute-start.3) | collective-permute-done | bytes 200736 | tf_op jit(solution)/shard_map/ppermute | solution.py:399
  83.7 2.1 collective-permute-done.5
  85.9 1.8 pad_maximum_fusion.1
  87.7 1.2 slice.80
  89.8 1.7 maximum_select_fusion.near_ref
  91.7 1.2 constant_dynamic-slice_fusion
  92.9 1.7 broadcast_select_fusion.2
  94.5 1.1 maximum_select_fusion.4
  97.0 1.4 copy.41
  98.4 2.4 reshape.446.x_ref
  100.8 1.2 copy-done.2
  102.0 1.4 copy-done.3
  104.3 1.0 copy-done.10
  105.4 15.0 %linear_rows.1 = (f32[4,256,512]{2,1,0:T(8,128)S(1)}, bf16[4,256,128]{2,1,0:T(8,128)(2,1)S(1)}, bf16[4,640,128]{2,1,0:T(8,128)(2,1)S(1)}) custom-call(s32[5]{0:T(128)S(1)} %pad_add_fusion.place_ref, bf16[256,1792]{1,0:T(8,128)(2,1)S(1)} %copy-done.2, f32[1,1792]{1,0:T(1,128)S(1)} %broadcast_in_dim.135.gain_ref, bf16[1,448,1792]{2,1,0:T(8,128)(2,1)S(1)} %bitcast.77, ...), custom_call_target="tpu_custom_call" | custom-call | tf_op jit(solution)/shard_map/linear_rows/pallas_call | solution.py:549
  120.3 4.5 %collective-permute-start.13 = (bf16[4,640,128]{2,1,0:T(8,128)(2,1)S(1)}, bf16[4,640,128]{2,1,0:T(8,128)(2,1)S(1)}, u32[]{:S(2)}, u32[]{:S(2)}) collective-permute-start(bf16[4,640,128]{2,1,0:T(8,128)(2,1)S(1)} %get-tuple-element.13), channel_id=1, source_target_pairs={{0,12},{1,13},{2,14},{3,15},{16,28},{17,29},{18,30},{19,31}} | collective-permute-start | bytes 1966088 | tf_op jit(solution)/shard_map/ppermute | solution.py:448
  124.8 1.3 collective-permute-start.12
  127.3 6.6 %collective-permute-done.14 = bf16[448,896]{1,0:T(8,128)(2,1)} collective-permute-done((bf16[448,896]{1,0:T(8,128)(2,1)}, bf16[448,896]{1,0:T(8,128)(2,1)}, u32[]{:S(2)}, u32[]{:S(2)}) %collective-permute-start.14) | collective-permute-done | bytes 802848 | tf_op jit(solution)/shard_map/ppermute | solution.py:399
  134.0 2.7 collective-permute-start.11
  136.6 1.2 select_bitcast_fusion
  141.1 1.1 collective-permute-start.19
  142.2 13.1 %collective-permute-done.12 = bf16[4,640,128]{2,1,0:T(8,128)(2,1)S(1)} collective-permute-done((bf16[4,640,128]{2,1,0:T(8,128)(2,1)S(1)}, bf16[4,640,128]{2,1,0:T(8,128)(2,1)S(1)}, u32[]{:S(2)}, u32[]{:S(2)}) %collective-permute-start.12) | collective-permute-done | bytes 655392 | tf_op jit(solution)/shard_map/ppermute | solution.py:448
  155.3 2.0 collective-permute-start.16
  158.8 2.3 collective-permute-done.16
  163.2 1.9 maximum_select_fusion.1.near_ref
  165.3 2.2 collective-permute-start.25
  167.9 1.4 collective-permute-start.23
  169.8 13.3 %linear_out.1 = (bf16[256,1792]{1,0:T(8,128)(2,1)S(1)}, bf16[256,1792]{1,0:T(8,128)(2,1)S(1)}, bf16[80,1792]{1,0:T(8,128)(2,1)S(1)}) custom-call(s32[5]{0:T(128)S(1)} %pad_add_fusion.place_ref, f32[4,256,512]{2,1,0:T(8,128)S(1)} %get-tuple-element.11.num_ref, bf16[4,256,128]{2,1,0:T(8,128)(2,1)S(1)} %get-tuple-element.12.q_ref, ...), custom_call_target="tpu_custom_call" | custom-call | tf_op jit(solution)/shard_map/linear_out/pallas_call | solution.py:588
  184.3 10.9 %collective-permute-done.24 = bf16[1,336,896]{2,1,0:T(8,128)(2,1)S(1)} collective-permute-done((bf16[1,336,896]{2,1,0:T(8,128)(2,1)S(1)}, bf16[1,336,896]{2,1,0:T(8,128)(2,1)S(1)}, u32[]{:S(2)}, u32[]{:S(2)}) %collective-permute-start.24) | collective-permute-done | bytes 602144 | tf_op jit(solution)/shard_map/ppermute | solution.py:399
  195.1 1.1 collective-permute-done.23
  197.1 2.7 collective-permute-start.27
  200.1 1.7 collective-permute-done.27
  201.9 2.2 collective-permute-start.22
  204.1 5.4 %collective-permute-start.29 = (bf16[80,1792]{1,0:T(8,128)(2,1)}, bf16[80,1792]{1,0:T(8,128)(2,1)S(1)}, u32[]{:S(2)}, u32[]{:S(2)}) collective-permute-start(bf16[80,1792]{1,0:T(8,128)(2,1)} %copy-done.21), channel_id=1, source_target_pairs={{0,5},{1,4},{2,7},{3,6},{4,9},{5,8},{6,11},{7,10},{8,13},{9,12},{1... | collective-permute-start | bytes 860168 | tf_op jit(solution)/shard_map/ppermute | solution.py:622
  209.4 1.1 broadcast_select_fusion.1
  210.6 1.1 fusion.13
  211.8 2.9 collective-permute-start.32
  215.3 2.4 copy-done.15
  217.7 15.3 %window_rows.2._.mixed_ref = bf16[2,256,512]{2,1,0:T(8,128)(2,1)S(1)} custom-call(s32[5]{0:T(128)S(1)} %pad_add_fusion.place_ref, s32[1]{0:T(128)} %bitcast.2.first_ref, bf16[256,1792]{1,0:T(8,128)(2,1)S(1)} %copy-done.20, bf16[80,1792]{1,0:T(8,128)(2,1)S(1)} %collective-permute-done.22.halo_ref, bf16[3,448,1792]{2,1,0:T(8,128)(2,1)S(1)} %bitcast.81, ...), custom_call_target="tpu_custom_call" | custom-call | flops 3699376128 | tf_op jit(solution)/shard_map/window_rows/pallas_call | solution.py:636
  233.0 16.0 %window_rows.3 = bf16[2,256,512]{2,1,0:T(8,128)(2,1)} custom-call(s32[5]{0:T(128)S(1)} %pad_add_fusion.place_ref, s32[1]{0:T(128)} %bitcast.2.first_ref, bf16[256,1792]{1,0:T(8,128)(2,1)S(1)} %collective-permute-done.28.x_ref, bf16[80,1792]{1,0:T(8,128)(2,1)S(1)} %collective-permute-done.29.halo_ref, bf16[3,448,1792]{2,1,0:T(8,128)(2,1)S(1)} %bitcast.82, ...), custom_call_target="tpu_custom_call" | custom-call | flops 3699376128 | tf_op jit(solution)/shard_map/window_rows/pallas_call | solution.py:636
  249.0 1.3 slice.91
  251.6 2.3 collective-permute-start.30
  255.5 11.1 %collective-permute-done.30.pair_ref = bf16[2,256,512]{2,1,0:T(8,128)(2,1)S(1)} collective-permute-done((bf16[2,256,512]{2,1,0:T(8,128)(2,1)}, bf16[2,256,512]{2,1,0:T(8,128)(2,1)S(1)}, u32[]{:S(2)}, u32[]{:S(2)}) %collective-permute-start.30) | collective-permute-done | bytes 524320 | tf_op jit(solution)/shard_map/ppermute | solution.py:399
  267.4 1.4 copy-done.5
  268.8 1.2 copy-done.9
  270.0 1.0 copy-done.12
  271.0 1.0 copy-done.14
  272.1 7.7 %window_out.1 = bf16[256,1792]{1,0:T(8,128)(2,1)S(1)} custom-call(s32[5]{0:T(128)S(1)} %pad_add_fusion.place_ref, s32[1]{0:T(128)} %bitcast.1.live_ref, bf16[2,256,512]{2,1,0:T(8,128)(2,1)S(1)} %copy-done.12, bf16[2,256,512]{2,1,0:T(8,128)(2,1)S(1)} %copy-done.14, bf16[1,448,1792]{2,1,0:T(8,128)(2,1)S(1)} %bitcast.79, ...), custom_call_target="tpu_custom_call" | custom-call | tf_op jit(solution)/shard_map/window_out/pallas_call | solution.py:664
  280.4 26.2 %all_to_all.15 = bf16[4,16,4,1792]{3,2,1,0:T(4,128)(2,1)S(1)} all-to-all(bf16[4,16,4,1792]{3,2,1,0:T(4,128)(2,1)S(1)} %bitcast.86), channel_id=1, replica_groups=mesh['dp'=2,'seq'=4,'tensor'=4] {'tensor'}, dimensions={0} | all-to-all | bytes 1835008 | tf_op jit(solution)/shard_map/all_to_all | solution.py:686
  (162 shorter events, 24.4 us)
Async XLA Ops:
  0.0 2.5 copy-start
  4.7 31.3 %all-to-all-start = ((bf16[8,8,4,1792]{3,2,1,0:T(4,128)(2,1)}), bf16[8,8,4,1792]{3,2,1,0:T(4,128)(2,1)S(1)}, u32[]{:S(2)}, u32[]{:S(2)}) async-start(bf16[8,8,4,1792]{3,2,1,0:T(4,128)(2,1)} %bitcast.12), calls=%async_computation | async-start | bytes 1835008 | tf_op jit(solution)/shard_map/all_to_all | solution.py:514
  11.6 15.2 %collective-permute-start.1 = (bf16[144,896]{1,0:T(8,128)(2,1)S(1)}, bf16[144,896]{1,0:T(8,128)(2,1)S(1)}, u32[]{:S(2)}, u32[]{:S(2)}) collective-permute-start(bf16[144,896]{1,0:T(8,128)(2,1)S(1)} %pad_maximum_fusion.2), channel_id=1, source_target_pairs={{0,2},{1,3},{2,0},{3,1},{4,6},{5,7},{6,4},{7,5},{8,10},{9,11},{10,... | collective-permute-start | bytes 774152 | tf_op jit(solution)/shard_map/ppermute | solution.py:399
  14.3 13.2 %collective-permute-start = (bf16[144,896]{1,0:T(8,128)(2,1)S(1)}, bf16[144,896]{1,0:T(8,128)(2,1)S(1)}, u32[]{:S(2)}, u32[]{:S(2)}) collective-permute-start(bf16[144,896]{1,0:T(8,128)(2,1)S(1)} %pad_maximum_fusion.2), channel_id=1, source_target_pairs={{0,1},{1,0},{2,3},{3,2},{4,5},{5,4},{6,7},{7,6},{8,9},{9,8},{10,11... | collective-permute-start | bytes 774152 | tf_op jit(solution)/shard_map/ppermute | solution.py:399
  26.9 7.8 %collective-permute-start.2 = (bf16[144,896]{1,0:T(8,128)(2,1)S(1)}, bf16[144,896]{1,0:T(8,128)(2,1)S(1)}, u32[]{:S(2)}, u32[]{:S(2)}) collective-permute-start(bf16[144,896]{1,0:T(8,128)(2,1)S(1)} %collective-permute-done.1), channel_id=1, source_target_pairs={{0,1},{1,0},{2,3},{3,2},{4,5},{5,4},{6,7},{7,6},{8,9},{9,8},{10,11... | collective-permute-start | bytes 774152 | tf_op jit(solution)/shard_map/ppermute | solution.py:399
  34.8 10.7 %copy-start.25 = (bf16[3,144,896]{2,1,0:T(8,128)(2,1)}, bf16[3,144,896]{2,1,0:T(8,128)(2,1)S(1)}, u32[]{:S(2)}) copy-start(bf16[3,144,896]{2,1,0:T(8,128)(2,1)S(1)} %pad_maximum_fusion) | copy-start | bytes 2322436
  38.8 32.7 %all-to-all-start.1 = ((bf16[4,16,4,1792]{3,1,2,0:T(8,128)(2,1)}), bf16[4,16,4,1792]{3,1,2,0:T(8,128)(2,1)S(1)}, u32[]{:S(2)}, u32[]{:S(2)}) async-start(bf16[4,16,4,1792]{3,1,2,0:T(8,128)(2,1)} %copy.40), calls=%async_computation.1 | async-start | bytes 1835008 | tf_op jit(solution)/shard_map/all_to_all | solution.py:521
  43.9 28.9 %collective-permute-start.7 = (bf16[3,144,896]{2,1,0:T(8,128)(2,1)S(1)}, bf16[3,144,896]{2,1,0:T(8,128)(2,1)S(1)}, u32[]{:S(2)}, u32[]{:S(2)}) collective-permute-start(bf16[3,144,896]{2,1,0:T(8,128)(2,1)S(1)} %pad_maximum_fusion), channel_id=1, source_target_pairs={{0,8},{4,12},{8,0},{12,4},{1,9},{5,13},{9,1},{13,5},{2,10},{6,14},... | collective-permute-start | bytes 2322440 | tf_op jit(solution)/shard_map/ppermute | solution.py:399
  45.5 29.0 %collective-permute-start.6 = (bf16[3,144,896]{2,1,0:T(8,128)(2,1)S(1)}, bf16[3,144,896]{2,1,0:T(8,128)(2,1)}, u32[]{:S(2)}, u32[]{:S(2)}) collective-permute-start(bf16[3,144,896]{2,1,0:T(8,128)(2,1)S(1)} %pad_maximum_fusion), channel_id=1, source_target_pairs={{0,4},{4,0},{8,12},{12,8},{1,5},{5,1},{9,13},{13,9},{2,6},{6,2},{1... | collective-permute-start | bytes 2322440 | tf_op jit(solution)/shard_map/ppermute | solution.py:399
  49.8 27.2 %collective-permute-start.4 = (bf16[112,896]{1,0:T(8,128)(2,1)}, bf16[112,896]{1,0:T(8,128)(2,1)}, u32[]{:S(2)}, u32[]{:S(2)}) collective-permute-start(bf16[112,896]{1,0:T(8,128)(2,1)} %dynamic-slice_select_fusion), channel_id=1, source_target_pairs={{0,2},{1,3},{2,0},{3,1},{4,6},{5,7},{6,4},{7,5},{8,10},{9,11},{10,... | collective-permute-start | bytes 602120 | tf_op jit(solution)/shard_map/ppermute | solution.py:399
  71.5 18.2 %copy-start.23 = (bf16[4,16,4,1792]{3,1,2,0:T(8,128)(2,1)}, bf16[4,16,4,1792]{3,1,2,0:T(8,128)(2,1)S(1)}, u32[]{:S(2)}) copy-start(bf16[4,16,4,1792]{3,1,2,0:T(8,128)(2,1)S(1)} %all-to-all-done.1) | copy-start | bytes 2752516
  71.5 18.3 %copy-start.26 = (bf16[3,144,896]{2,1,0:T(8,128)(2,1)S(1)}, bf16[3,144,896]{2,1,0:T(8,128)(2,1)}, u32[]{:S(2)}) copy-start(bf16[3,144,896]{2,1,0:T(8,128)(2,1)} %copy-done.25) | copy-start | bytes 2322436
  72.8 17.0 %copy-start.27 = (bf16[3,144,896]{2,1,0:T(8,128)(2,1)}, bf16[3,144,896]{2,1,0:T(8,128)(2,1)S(1)}, u32[]{:S(2)}) copy-start(bf16[3,144,896]{2,1,0:T(8,128)(2,1)S(1)} %collective-permute-done.7) | copy-start | bytes 2322436
  72.8 16.8 %collective-permute-start.8 = (bf16[3,80,896]{2,1,0:T(8,128)(2,1)S(1)}, bf16[3,80,896]{2,1,0:T(8,128)(2,1)S(1)}, u32[]{:S(2)}, u32[]{:S(2)}) collective-permute-start(bf16[3,80,896]{2,1,0:T(8,128)(2,1)S(1)} %slice_select_fusion.1), channel_id=1, source_target_pairs={{0,4},{4,0},{8,12},{12,8},{1,5},{5,1},{9,13},{13,9},{2,6},{6,2},{1... | collective-permute-start | bytes 1290248 | tf_op jit(solution)/shard_map/ppermute | solution.py:399
  75.5 14.1 %collective-permute-start.9 = (bf16[3,64,896]{2,1,0:T(8,128)(2,1)S(1)}, bf16[3,64,896]{2,1,0:T(8,128)(2,1)S(1)}, u32[]{:S(2)}, u32[]{:S(2)}) collective-permute-start(bf16[3,64,896]{2,1,0:T(8,128)(2,1)S(1)} %slice_select_fusion.3), channel_id=1, source_target_pairs={{0,8},{4,12},{8,0},{12,4},{1,9},{5,13},{9,1},{13,5},{2,10},{6,14},... | collective-permute-start | bytes 1032200 | tf_op jit(solution)/shard_map/ppermute | solution.py:399
  77.0 6.7 %collective-permute-start.3 = (bf16[112,896]{1,0:T(8,128)(2,1)}, bf16[112,896]{1,0:T(8,128)(2,1)S(1)}, u32[]{:S(2)}, u32[]{:S(2)}) collective-permute-start(bf16[112,896]{1,0:T(8,128)(2,1)} %dynamic-slice_select_fusion), channel_id=1, source_target_pairs={{0,1},{1,0},{2,3},{3,2},{4,5},{5,4},{6,7},{7,6},{8,9},{9,8},{10,11... | collective-permute-start | bytes 602120 | tf_op jit(solution)/shard_map/ppermute | solution.py:399
  77.0 8.8 %collective-permute-start.5 = (bf16[112,896]{1,0:T(8,128)(2,1)}, bf16[112,896]{1,0:T(8,128)(2,1)S(1)}, u32[]{:S(2)}, u32[]{:S(2)}) collective-permute-start(bf16[112,896]{1,0:T(8,128)(2,1)} %collective-permute-done.4), channel_id=1, source_target_pairs={{0,1},{1,0},{2,3},{3,2},{4,5},{5,4},{6,7},{7,6},{8,9},{9,8},{10,11... | collective-permute-start | bytes 602120 | tf_op jit(solution)/shard_map/ppermute | solution.py:399
  91.6 4.3 %copy-start.30 = (f32[1792]{0:T(1024)S(1)}, f32[1792]{0:T(1024)}, u32[]{:S(2)}) copy-start(f32[1792]{0:T(1024)} %param.21) | copy-start | bytes 21508
  91.6 5.4 %copy-start.24 = (bf16[4,16,4,1792]{3,1,2,0:T(8,128)(2,1)S(1)}, bf16[4,16,4,1792]{3,1,2,0:T(8,128)(2,1)}, u32[]{:S(2)}) copy-start(bf16[4,16,4,1792]{3,1,2,0:T(8,128)(2,1)} %copy-done.23) | copy-start | bytes 2752516
  91.6 9.2 %collective-permute-start.10 = (bf16[4,3,144,896]{3,2,1,0:T(8,128)(2,1)S(1)}, bf16[4,3,144,896]{3,2,1,0:T(8,128)(2,1)}, u32[]{:S(2)}, u32[]{:S(2)}) collective-permute-start(bf16[4,3,144,896]{3,2,1,0:T(8,128)(2,1)S(1)} %maximum_select_fusion.near_ref), channel_id=1, source_target_pairs={{0,16},{16,0},{1,17},{17,1},{2,18},{18,2},{3,19},{19,3},{4,20},{20... | collective-permute-start | bytes 9289736 | tf_op jit(solution)/shard_map/ppermute | solution.py:399
  94.5 6.3 %copy-start.6 = (bf16[128,1024]{1,0:T(8,128)(2,1)S(1)}, bf16[128,1024]{1,0:T(8,128)(2,1)}, u32[]{:S(2)}) copy-start(bf16[128,1024]{1,0:T(8,128)(2,1)} %constant.128.clone.first_ref) | copy-start | bytes 786436
  94.5 6.3 %copy-start.16 = (f32[2,1024]{1,0:T(2,128)S(1)}, f32[2,1024]{1,0:T(2,128)}, u32[]{:S(2)}) copy-start(f32[2,1024]{1,0:T(2,128)} %constant.130.clone.ones_ref) | copy-start | bytes 24580
  94.5 6.3 %copy-start.18 = (f32[1,512]{1,0:T(1,128)S(1)}, f32[1,512]{1,0:T(1,128)}, u32[]{:S(2)}) copy-start(f32[1,512]{1,0:T(1,128)} %constant.131.clone.column_ref) | copy-start | bytes 6148
  95.6 38.4 %collective-permute-start.14 = (bf16[448,896]{1,0:T(8,128)(2,1)}, bf16[448,896]{1,0:T(8,128)(2,1)}, u32[]{:S(2)}, u32[]{:S(2)}) collective-permute-start(bf16[448,896]{1,0:T(8,128)(2,1)} %maximum_select_fusion.4), channel_id=1, source_target_pairs={{0,2},{1,3},{2,0},{3,1},{4,6},{5,7},{6,4},{7,5},{8,10},{9,11},{10,... | collective-permute-start | bytes 2408456 | tf_op jit(solution)/shard_map/ppermute | solution.py:399
  95.9 42.6 %collective-permute-start.17 = (bf16[3,112,896]{2,1,0:T(8,128)(2,1)}, bf16[3,112,896]{2,1,0:T(8,128)(2,1)}, u32[]{:S(2)}, u32[]{:S(2)}) collective-permute-start(bf16[3,112,896]{2,1,0:T(8,128)(2,1)} %pad_maximum_fusion.1), channel_id=1, source_target_pairs={{0,4},{4,0},{8,12},{12,8},{1,5},{5,1},{9,13},{13,9},{2,6},{6,2},{1... | collective-permute-start | bytes 1806344 | tf_op jit(solution)/shard_map/ppermute | solution.py:399
  96.6 43.0 %collective-permute-start.18 = (bf16[3,112,896]{2,1,0:T(8,128)(2,1)}, bf16[3,112,896]{2,1,0:T(8,128)(2,1)}, u32[]{:S(2)}, u32[]{:S(2)}) collective-permute-start(bf16[3,112,896]{2,1,0:T(8,128)(2,1)} %pad_maximum_fusion.1), channel_id=1, source_target_pairs={{0,8},{4,12},{8,0},{12,4},{1,9},{5,13},{9,1},{13,5},{2,10},{6,14},... | collective-permute-start | bytes 1806344 | tf_op jit(solution)/shard_map/ppermute | solution.py:399
  100.8 1.2 copy-start.2
  102.0 1.4 copy-start.3
  105.4 33.1 %copy-start.28 = (bf16[112,896]{1,0:T(8,128)(2,1)S(1)}, bf16[112,896]{1,0:T(8,128)(2,1)}, u32[]{:S(2)}) copy-start(bf16[112,896]{1,0:T(8,128)(2,1)} %get-tuple-element.17) | copy-start | bytes 602116
  120.3 20.7 %collective-permute-start.13 = (bf16[4,640,128]{2,1,0:T(8,128)(2,1)S(1)}, bf16[4,640,128]{2,1,0:T(8,128)(2,1)S(1)}, u32[]{:S(2)}, u32[]{:S(2)}) collective-permute-start(bf16[4,640,128]{2,1,0:T(8,128)(2,1)S(1)} %get-tuple-element.13), channel_id=1, source_target_pairs={{0,12},{1,13},{2,14},{3,15},{16,28},{17,29},{18,30},{19,31}} | collective-permute-start | bytes 1966088 | tf_op jit(solution)/shard_map/ppermute | solution.py:448
  124.8 30.5 %collective-permute-start.12 = (bf16[4,640,128]{2,1,0:T(8,128)(2,1)S(1)}, bf16[4,640,128]{2,1,0:T(8,128)(2,1)S(1)}, u32[]{:S(2)}, u32[]{:S(2)}) collective-permute-start(bf16[4,640,128]{2,1,0:T(8,128)(2,1)S(1)} %get-tuple-element.13), channel_id=1, source_target_pairs={{0,8},{4,12},{1,9},{5,13},{2,10},{6,14},{3,11},{7,15},{16,24},{20,... | collective-permute-start | bytes 1966088 | tf_op jit(solution)/shard_map/ppermute | solution.py:448
  134.0 23.4 %collective-permute-start.11 = (bf16[4,640,128]{2,1,0:T(8,128)(2,1)S(1)}, bf16[4,640,128]{2,1,0:T(8,128)(2,1)S(1)}, u32[]{:S(2)}, u32[]{:S(2)}) collective-permute-start(bf16[4,640,128]{2,1,0:T(8,128)(2,1)S(1)} %get-tuple-element.13), channel_id=1, source_target_pairs={{0,4},{4,8},{8,12},{1,5},{5,9},{9,13},{2,6},{6,10},{10,14},{3,7},{... | collective-permute-start | bytes 1966088 | tf_op jit(solution)/shard_map/ppermute | solution.py:448
  138.5 20.2 %collective-permute-start.15 = (bf16[112,896]{1,0:T(8,128)(2,1)S(1)}, bf16[112,896]{1,0:T(8,128)(2,1)S(1)}, u32[]{:S(2)}, u32[]{:S(2)}) collective-permute-start(bf16[112,896]{1,0:T(8,128)(2,1)S(1)} %copy-done.28), channel_id=1, source_target_pairs={{0,1},{1,0},{2,3},{3,2},{4,5},{5,4},{6,7},{7,6},{8,9},{9,8},{10,11... | collective-permute-start | bytes 602120 | tf_op jit(solution)/shard_map/ppermute | solution.py:399
  139.6 23.5 %collective-permute-start.20 = (bf16[3,48,896]{2,1,0:T(8,128)(2,1)S(1)}, bf16[3,48,896]{2,1,0:T(8,128)(2,1)S(1)}, u32[]{:S(2)}, u32[]{:S(2)}) collective-permute-start(bf16[3,48,896]{2,1,0:T(8,128)(2,1)S(1)} %slice_select_fusion.4), channel_id=1, source_target_pairs={{0,8},{4,12},{8,0},{12,4},{1,9},{5,13},{9,1},{13,5},{2,10},{6,14},... | collective-permute-start | bytes 774152 | tf_op jit(solution)/shard_map/ppermute | solution.py:399
  141.1 22.0 %collective-permute-start.19 = (bf16[3,64,896]{2,1,0:T(8,128)(2,1)S(1)}, bf16[3,64,896]{2,1,0:T(8,128)(2,1)S(1)}, u32[]{:S(2)}, u32[]{:S(2)}) collective-permute-start(bf16[3,64,896]{2,1,0:T(8,128)(2,1)S(1)} %slice_select_fusion.2), channel_id=1, source_target_pairs={{0,4},{4,0},{8,12},{12,8},{1,5},{5,1},{9,13},{13,9},{2,6},{6,2},{1... | collective-permute-start | bytes 1032200 | tf_op jit(solution)/shard_map/ppermute | solution.py:399
  155.3 5.7 %collective-permute-start.16 = (bf16[112,896]{1,0:T(8,128)(2,1)S(1)}, bf16[112,896]{1,0:T(8,128)(2,1)S(1)}, u32[]{:S(2)}, u32[]{:S(2)}) collective-permute-start(bf16[112,896]{1,0:T(8,128)(2,1)S(1)} %get-tuple-element.22), channel_id=1, source_target_pairs={{0,1},{1,0},{2,3},{3,2},{4,5},{5,4},{6,7},{7,6},{8,9},{9,8},{10,11... | collective-permute-start | bytes 602120 | tf_op jit(solution)/shard_map/ppermute | solution.py:399
  161.1 2.0 copy-start.22
  163.2 6.1 %copy-start.31 = (f32[1792]{0:T(1024)S(1)}, f32[1792]{0:T(1024)}, u32[]{:S(2)}) copy-start(f32[1792]{0:T(1024)} %param.25) | copy-start | bytes 21508
  165.1 4.7 %copy-start.4 = (bf16[448,1792]{1,0:T(8,128)(2,1)S(1)}, bf16[448,1792]{1,0:T(8,128)(2,1)}, u32[]{:S(2)}) copy-start(bf16[448,1792]{1,0:T(8,128)(2,1)} %param.24) | copy-start | bytes 4816900
  165.1 4.7 %copy-start.17 = (f32[1,1024]{1,0:T(1,128)S(1)}, f32[1,1024]{1,0:T(1,128)}, u32[]{:S(2)}) copy-start(f32[1,1024]{1,0:T(1,128)} %constant.132.clone.scale_ref) | copy-start | bytes 12292
  165.1 4.7 %collective-permute-start.21 = (bf16[4,3,112,896]{3,2,1,0:T(8,128)(2,1)S(1)}, bf16[4,3,112,896]{3,2,1,0:T(8,128)(2,1)S(1)}, u32[]{:S(2)}, u32[]{:S(2)}) collective-permute-start(bf16[4,3,112,896]{3,2,1,0:T(8,128)(2,1)S(1)} %maximum_select_fusion.1.near_ref), channel_id=1, source_target_pairs={{0,16},{16,0},{1,17},{17,1},{2,18},{18,2},{3,19},{19,3},{4,20},{20... | collective-permute-start | bytes 7225352 | tf_op jit(solution)/shard_map/ppermute | solution.py:399
  165.3 19.0 %collective-permute-start.25 = (bf16[1,336,896]{2,1,0:T(8,128)(2,1)S(1)}, bf16[1,336,896]{2,1,0:T(8,128)(2,1)S(1)}, u32[]{:S(2)}, u32[]{:S(2)}) collective-permute-start(bf16[1,336,896]{2,1,0:T(8,128)(2,1)S(1)} %slice_select_fusion), channel_id=1, source_target_pairs={{0,12},{4,8},{8,4},{12,0},{1,13},{5,9},{9,5},{13,1},{2,14},{6,10},... | collective-permute-start | bytes 1806344 | tf_op jit(solution)/shard_map/ppermute | solution.py:399
  167.4 27.7 %collective-permute-start.24 = (bf16[1,336,896]{2,1,0:T(8,128)(2,1)S(1)}, bf16[1,336,896]{2,1,0:T(8,128)(2,1)S(1)}, u32[]{:S(2)}, u32[]{:S(2)}) collective-permute-start(bf16[1,336,896]{2,1,0:T(8,128)(2,1)S(1)} %slice_select_fusion), channel_id=1, source_target_pairs={{0,8},{4,12},{8,0},{12,4},{1,9},{5,13},{9,1},{13,5},{2,10},{6,14},... | collective-permute-start | bytes 1806344 | tf_op jit(solution)/shard_map/ppermute | solution.py:399
  167.9 28.3 %collective-permute-start.23 = (bf16[1,336,896]{2,1,0:T(8,128)(2,1)S(1)}, bf16[1,336,896]{2,1,0:T(8,128)(2,1)S(1)}, u32[]{:S(2)}, u32[]{:S(2)}) collective-permute-start(bf16[1,336,896]{2,1,0:T(8,128)(2,1)S(1)} %slice_select_fusion), channel_id=1, source_target_pairs={{0,4},{4,0},{8,12},{12,8},{1,5},{5,1},{9,13},{13,9},{2,6},{6,2},{1... | collective-permute-start | bytes 1806344 | tf_op jit(solution)/shard_map/ppermute | solution.py:399
  183.1 13.5 %copy-start.8 = (bf16[256,1792]{1,0:T(8,128)(2,1)}, bf16[256,1792]{1,0:T(8,128)(2,1)S(1)}, u32[]{:S(2)}) copy-start(bf16[256,1792]{1,0:T(8,128)(2,1)S(1)} %get-tuple-element.16.residual_ref) | copy-start | bytes 2752516
  183.1 13.5 %copy-start.19 = (bf16[256,1792]{1,0:T(8,128)(2,1)}, bf16[256,1792]{1,0:T(8,128)(2,1)S(1)}, u32[]{:S(2)}) copy-start(bf16[256,1792]{1,0:T(8,128)(2,1)S(1)} %get-tuple-element.14.x_ref._) | copy-start | bytes 2752516
  183.1 13.5 %copy-start.21 = (bf16[80,1792]{1,0:T(8,128)(2,1)}, bf16[80,1792]{1,0:T(8,128)(2,1)S(1)}, u32[]{:S(2)}) copy-start(bf16[80,1792]{1,0:T(8,128)(2,1)S(1)} %get-tuple-element.15) | copy-start | bytes 860164
  196.7 18.0 %collective-permute-start.26 = (bf16[4,1,336,896]{3,2,1,0:T(8,128)(2,1)S(1)}, bf16[4,1,336,896]{3,2,1,0:T(8,128)(2,1)}, u32[]{:S(2)}, u32[]{:S(2)}) collective-permute-start(bf16[4,1,336,896]{3,2,1,0:T(8,128)(2,1)S(1)} %maximum_select_fusion.2.near_ref), channel_id=1, source_target_pairs={{0,16},{16,0},{1,17},{17,1},{2,18},{18,2},{3,19},{19,3},{4,20},{20... | collective-permute-start | bytes 7225352 | tf_op jit(solution)/shard_map/ppermute | solution.py:399
  196.9 18.4 %copy-start.20 = (bf16[256,1792]{1,0:T(8,128)(2,1)S(1)}, bf16[256,1792]{1,0:T(8,128)(2,1)}, u32[]{:S(2)}) copy-start(bf16[256,1792]{1,0:T(8,128)(2,1)} %copy-done.19) | copy-start | bytes 2752516
  197.1 4.8 %collective-permute-start.27 = (f32[3,1536]{1,0:T(4,128)S(1)}, f32[3,1536]{1,0:T(4,128)S(1)}, u32[]{:S(2)}, u32[]{:S(2)}) collective-permute-start(f32[3,1536]{1,0:T(4,128)S(1)} %reshape.451), channel_id=1, source_target_pairs={{0,2},{1,3},{2,0},{3,1},{4,6},{5,7},{6,4},{7,5},{8,10},{9,11},{10,... | collective-permute-start | bytes 55304 | tf_op jit(solution)/shard_map/ppermute | solution.py:399
  199.8 33.2 %collective-permute-start.28 = (bf16[256,1792]{1,0:T(8,128)(2,1)}, bf16[256,1792]{1,0:T(8,128)(2,1)S(1)}, u32[]{:S(2)}, u32[]{:S(2)}) collective-permute-start(bf16[256,1792]{1,0:T(8,128)(2,1)} %copy-done.19), channel_id=1, source_target_pairs={{0,1},{1,0},{2,3},{3,2},{4,5},{5,4},{6,7},{7,6},{8,9},{9,8},{10,11... | collective-permute-start | bytes 2752520 | tf_op jit(solution)/shard_map/ppermute | solution.py:399
  201.9 9.9 %collective-permute-start.22 = (bf16[80,1792]{1,0:T(8,128)(2,1)}, bf16[80,1792]{1,0:T(8,128)(2,1)S(1)}, u32[]{:S(2)}, u32[]{:S(2)}) collective-permute-start(bf16[80,1792]{1,0:T(8,128)(2,1)} %copy-done.21), channel_id=1, source_target_pairs={{0,4},{4,8},{8,12},{1,5},{5,9},{9,13},{2,6},{6,10},{10,14},{3,7},{... | collective-permute-start | bytes 860168 | tf_op jit(solution)/shard_map/ppermute | solution.py:620
  204.1 28.9 %collective-permute-start.29 = (bf16[80,1792]{1,0:T(8,128)(2,1)}, bf16[80,1792]{1,0:T(8,128)(2,1)S(1)}, u32[]{:S(2)}, u32[]{:S(2)}) collective-permute-start(bf16[80,1792]{1,0:T(8,128)(2,1)} %copy-done.21), channel_id=1, source_target_pairs={{0,5},{1,4},{2,7},{3,6},{4,9},{5,8},{6,11},{7,10},{8,13},{9,12},{1... | collective-permute-start | bytes 860168 | tf_op jit(solution)/shard_map/ppermute | solution.py:622
  210.6 40.4 %collective-permute-start.33 = (bf16[3,112,896]{2,1,0:T(8,128)(2,1)S(1)}, bf16[3,112,896]{2,1,0:T(8,128)(2,1)S(1)}, u32[]{:S(2)}, u32[]{:S(2)}) collective-permute-start(bf16[3,112,896]{2,1,0:T(8,128)(2,1)S(1)} %broadcast_select_fusion.1), channel_id=1, source_target_pairs={{0,12},{4,8},{8,4},{12,0},{1,13},{5,9},{9,5},{13,1},{2,14},{6,10},... | collective-permute-start | bytes 1806344 | tf_op jit(solution)/shard_map/ppermute | solution.py:399
  211.8 39.2 %collective-permute-start.32 = (bf16[3,112,896]{2,1,0:T(8,128)(2,1)S(1)}, bf16[3,112,896]{2,1,0:T(8,128)(2,1)S(1)}, u32[]{:S(2)}, u32[]{:S(2)}) collective-permute-start(bf16[3,112,896]{2,1,0:T(8,128)(2,1)S(1)} %broadcast_select_fusion.1), channel_id=1, source_target_pairs={{0,8},{4,12},{8,0},{12,4},{1,9},{5,13},{9,1},{13,5},{2,10},{6,14},... | collective-permute-start | bytes 1806344 | tf_op jit(solution)/shard_map/ppermute | solution.py:399
  214.6 36.4 %collective-permute-start.31 = (bf16[3,112,896]{2,1,0:T(8,128)(2,1)S(1)}, bf16[3,112,896]{2,1,0:T(8,128)(2,1)S(1)}, u32[]{:S(2)}, u32[]{:S(2)}) collective-permute-start(bf16[3,112,896]{2,1,0:T(8,128)(2,1)S(1)} %broadcast_select_fusion.1), channel_id=1, source_target_pairs={{0,4},{4,0},{8,12},{12,8},{1,5},{5,1},{9,13},{13,9},{2,6},{6,2},{1... | collective-permute-start | bytes 1806344 | tf_op jit(solution)/shard_map/ppermute | solution.py:399
  215.3 2.4 copy-start.15
  233.0 16.1 %copy-start.11 = (bf16[2,256,512]{2,1,0:T(8,128)(2,1)}, bf16[2,256,512]{2,1,0:T(8,128)(2,1)S(1)}, u32[]{:S(2)}) copy-start(bf16[2,256,512]{2,1,0:T(8,128)(2,1)S(1)} %window_rows.2._.mixed_ref) | copy-start | bytes 1572868
  251.0 2.9 copy-start.32
  251.0 2.9 copy-start.33
  251.5 15.9 %collective-permute-start.34 = (bf16[4,3,112,896]{3,2,1,0:T(8,128)(2,1)S(1)}, bf16[4,3,112,896]{3,2,1,0:T(8,128)(2,1)}, u32[]{:S(2)}, u32[]{:S(2)}) collective-permute-start(bf16[4,3,112,896]{3,2,1,0:T(8,128)(2,1)S(1)} %maximum_select_fusion.3.near_ref), channel_id=1, source_target_pairs={{0,16},{16,0},{1,17},{17,1},{2,18},{18,2},{3,19},{19,3},{4,20},{20... | collective-permute-start | bytes 7225352 | tf_op jit(solution)/shard_map/ppermute | solution.py:399
  251.6 15.0 %collective-permute-start.30 = (bf16[2,256,512]{2,1,0:T(8,128)(2,1)}, bf16[2,256,512]{2,1,0:T(8,128)(2,1)S(1)}, u32[]{:S(2)}, u32[]{:S(2)}) collective-permute-start(bf16[2,256,512]{2,1,0:T(8,128)(2,1)} %window_rows.3), channel_id=1, source_target_pairs={{0,1},{1,0},{2,3},{3,2},{4,5},{5,4},{6,7},{7,6},{8,9},{9,8},{10,11... | collective-permute-start | bytes 1572872 | tf_op jit(solution)/shard_map/ppermute | solution.py:399
  267.4 1.4 copy-start.5
  279.8 27.7 %copy-start.1 = (bf16[64,4,1792]{2,1,0:T(4,128)(2,1)S(1)}, bf16[64,4,1792]{2,1,0:T(4,128)(2,1)}, u32[]{:S(2)}) copy-start(bf16[64,4,1792]{2,1,0:T(4,128)(2,1)} %param.17) | copy-start | bytes 2752516
  (7 other events, 6.8 us)

commit v8 on v7

--- a/solution.py
+++ b/solution.py
@@ -15,7 +15,7 @@
 FEAT_SLOT = 256
 HALO = 80
 NEAR = 4
-VMEM = 32 * 1024 * 1024
+VMEM = 60 * 1024 * 1024
 F32 = jnp.float32
 BF16 = jnp.bfloat16
 
@@ -79,52 +79,43 @@
                 copy.wait()
 
 
-def weight_copies(place_ref, near_ref, far_ref, targets, sems, group):
-    near = near_ref.shape[0]
+def weight_copies(place_ref, near_ref, far_ref, targets, pieces, sems, group):
+    found = []
+
+    def copy(src, dst):
+        found.append(pltpu.make_async_copy(src, dst, sems.at[group, len(found)]))
+
+    if group == 0:
+        for own_ref, kind, w_ref, off in targets:
+            rows = own_ref.shape[2]
+            for n in range(NEAR):
+                copy(own_ref.at[kind, place_ref[n]], w_ref.at[0, n, off : off + rows, :])
+        return found
     cols = near_ref.shape[3]
-    found = []
-    for n in range(2 * near):
+    for ref, part in ((near_ref, place_ref[NEAR]), (far_ref, 1 - place_ref[NEAR])):
         at = 0
-        for own_ref, kind, rows, w_ref, off in targets:
-            if group == 0:
-                part, head = n // near, n % near
-                src = own_ref.at[
-                    kind, head * rows : (head + 1) * rows, part * cols : (part + 1) * cols
-                ]
-            else:
-                part, head = place_ref[near], place_ref[n % near]
-                if n >= near:
-                    part = 1 - part
-                src = (near_ref if n < near else far_ref).at[
-                    n % near, group - 1, at : at + rows, :
-                ]
-            dst = w_ref.at[group, part, head, off : off + rows, :]
-            found.append(pltpu.make_async_copy(src, dst, sems.at[group, len(found)]))
+        lanes = pl.ds(pl.multiple_of(part * cols, SLOT), cols)
+        for rows, w_ref, off in pieces:
+            copy(ref.at[:, group - 1, at : at + rows, :], w_ref.at[group, :, off : off + rows, lanes])
             at += rows
     return found
 
 
 def zero_between_heads(w_ref):
-    groups, parts, heads, rows, cols = w_ref.shape
+    groups, heads, rows, width = w_ref.shape
     for at in range(HEAD, rows, SLOT):
-        w_ref[:, :, :, at : at + SLOT - HEAD, :] = jnp.zeros(
-            (groups, parts, heads, SLOT - HEAD, cols), BF16
+        w_ref[:, :, at : at + SLOT - HEAD, :] = jnp.zeros(
+            (groups, heads, SLOT - HEAD, width), BF16
         )
 
 
-def group_weights(w_ref, step, part):
-    heads, rows, cols = w_ref.shape[2:]
-    return w_ref[step, part].reshape(heads * rows, cols)
+def group_weights(w_ref, step):
+    heads, rows, width = w_ref.shape[1:]
+    return w_ref[step].reshape(heads * rows, width)
 
 
 def project(rows_ref, w_ref, step):
-    parts, cols = w_ref.shape[1], w_ref.shape[4]
-    total = None
-    for part in range(parts):
-        rows = rows_ref[:, part * cols : (part + 1) * cols]
-        share = dot(rows, group_weights(w_ref, step, part), ((1,), (1,)))
-        total = share if total is None else total + share
-    return total
+    return dot(rows_ref[...], group_weights(w_ref, step), ((1,), (1,)))
 
 
 def linear_kernel(
@@ -152,17 +143,18 @@
 ):
     step = pl.program_id(0)
     targets = [
-        (value_ref, 0, HEAD, value_w_ref, 0),
-        (featmap_ref, 0, feature_dim, feat_w_ref, 0),
-        (featmap_ref, 1, feature_dim, feat_w_ref, feature_dim),
+        (value_ref, 0, value_w_ref, 0),
+        (featmap_ref, 0, feat_w_ref, 0),
+        (featmap_ref, 1, feat_w_ref, feature_dim),
     ]
+    pieces = [(HEAD, value_w_ref, 0), (2 * feature_dim, feat_w_ref, 0)]
 
     @pl.when(step == 0)
     def _():
         zero_between_heads(value_w_ref)
 
     run_copies(
-        functools.partial(weight_copies, place_ref, near_ref, far_ref, targets, sems),
+        functools.partial(weight_copies, place_ref, near_ref, far_ref, targets, pieces, sems),
         value_w_ref.shape[0],
         lambda: normed_ref.__setitem__(
             ..., normed_rows(x_ref[...].astype(F32), gain_ref[...])
@@ -187,15 +179,13 @@
         value = values[:, h * SLOT : (h + 1) * SLOT]
         num_ref[0, :, h * SLOT : (h + 1) * SLOT] = dot(kernel, value)
         state = dot(key_features[:, h * FEAT_SLOT : h * FEAT_SLOT + kept], value, ((0,), (0,)))
-        state_ref[0, h * kept : (h + 1) * kept, :] = state.astype(BF16)
+        head = pl.multiple_of(place_ref[h] * kept, 16)
+        state_ref[0, pl.ds(head, kept), :] = state.astype(BF16)
 
 
 def add_branch(mixed, w_ref, total_ref):
     step = pl.program_id(0)
-    parts, cols = w_ref.shape[1], w_ref.shape[4]
-    for part in range(parts):
-        share = dot(mixed, group_weights(w_ref, step, part)).astype(BF16).astype(F32)
-        total_ref[:, part * cols : (part + 1) * cols] += share
+    total_ref[...] += dot(mixed, group_weights(w_ref, step)).astype(BF16).astype(F32)
 
 
 def out_one_kernel(
@@ -215,7 +205,8 @@
     x_ref,
     gain_ref,
     residual_ref,
-    normed_ref,
+    low_ref,
+    high_ref,
     tail_ref,
     total_ref,
     mixed_ref,
@@ -231,7 +222,13 @@
 
     run_copies(
         functools.partial(
-            weight_copies, place_ref, near_ref, far_ref, [(own_ref, 0, HEAD, w_ref, 0)], sems
+            weight_copies,
+            place_ref,
+            near_ref,
+            far_ref,
+            [(own_ref, 0, w_ref, 0)],
+            [(HEAD, w_ref, 0)],
+            sems,
         ),
         w_ref.shape[0],
     )
@@ -239,13 +236,12 @@
     query_features = features(q_ref[0], first_ref[...], second_ref[...], ones_ref[...])
     query_features = (query_features * scale_ref[...]).astype(BF16)
     for h in range(heads):
-        at = slice(h * kept, (h + 1) * kept)
-        prior = prior_ref[0, at, :]
+        prior = prior_ref[0, pl.ds(pl.multiple_of(place_ref[h] * kept, 16), kept), :]
         lanes = slice(h * SLOT, (h + 1) * SLOT)
         total = num_ref[0, :, lanes] + dot(
             query_features[:, h * FEAT_SLOT : h * FEAT_SLOT + kept], prior.astype(BF16)
         )
-        mixed_ref[:, lanes] = (total / total[:, HEAD : HEAD + 1]).astype(BF16)
+        mixed_ref[:, lanes] = (total * (1.0 / total[:, HEAD : HEAD + 1])).astype(BF16)
     add_branch(mixed_ref[...], w_ref, total_ref)
 
     @pl.when(step == pl.num_programs(0) - 1)
@@ -253,15 +249,18 @@
         residual = (x_ref[...].astype(F32) + total_ref[...]).astype(BF16)
         residual_ref[...] = residual
         normed = normed_rows(residual.astype(F32), gain_ref[...])
-        normed_ref[...] = normed
-        tail_ref[...] = normed[-HALO:]
+        mid = low_ref.shape[0]
+        low_ref[...] = normed[:mid]
+        high_ref[...] = normed[mid:]
+        tail_ref[...] = normed[normed.shape[0] - HALO :]
 
 
 def window_kernel(
     heads,
     place_ref,
     first_ref,
-    x_ref,
+    low_ref,
+    high_ref,
     halo_ref,
     own_ref,
     near_ref,
@@ -274,22 +273,25 @@
     sems,
 ):
     step = pl.program_id(0)
-    targets = [(own_ref, kind, HEAD, w_ref, kind * SLOT) for kind in range(3)]
+    targets = [(own_ref, kind, w_ref, kind * SLOT) for kind in range(3)]
+    pieces = [(HEAD, w_ref, kind * SLOT) for kind in range(3)]
+    mid = low_ref.shape[0]
 
     def place_rows():
         rows_ref[:HALO] = halo_ref[...]
-        rows_ref[HALO:] = x_ref[...]
+        rows_ref[HALO : HALO + mid] = low_ref[...]
+        rows_ref[HALO + mid :] = high_ref[...]
 
     @pl.when(step == 0)
     def _():
         zero_between_heads(w_ref)
 
     run_copies(
-        functools.partial(weight_copies, place_ref, near_ref, far_ref, targets, sems),
+        functools.partial(weight_copies, place_ref, near_ref, far_ref, targets, pieces, sems),
         w_ref.shape[0],
         place_rows,
     )
-    rows = x_ref.shape[0]
+    rows = mid + high_ref.shape[0]
     lead = HALO - WINDOW
     projected = project(rows_ref, w_ref, step)
     taps = tap_ref[0]
@@ -314,7 +316,7 @@
                 allowed = band & (col >= WINDOW - start - first_ref[0])
             logits = jnp.where(allowed, logits * HEAD**-0.5, -jnp.inf)
             weights = jnp.exp(logits - jnp.max(logits, axis=1, keepdims=True))
-            weights = weights / jnp.sum(weights, axis=1, keepdims=True)
+            weights = weights * (1.0 / jnp.sum(weights, axis=1, keepdims=True))
             mixed = dot(weights.astype(BF16), values[start : start + span])
             mixed_ref[0, start : start + tile, h * SLOT : (h + 1) * SLOT] = mixed.astype(BF16)
 
@@ -342,7 +344,13 @@
 
     run_copies(
         functools.partial(
-            weight_copies, place_ref, near_ref, far_ref, [(own_ref, 0, HEAD, w_ref, 0)], sems
+            weight_copies,
+            place_ref,
+            near_ref,
+            far_ref,
+            [(own_ref, 0, w_ref, 0)],
+            [(HEAD, w_ref, 0)],
+            sems,
         ),
         w_ref.shape[0],
     )
@@ -388,9 +396,9 @@
     head, part = lax.axis_index("seq") % NEAR, lax.axis_index("dp")
     found = []
     for weights in whole_weights:
-        kinds, rows, cols = weights.shape
-        rows, cols = rows // NEAR, cols // lax.axis_size("dp")
-        piece = lax.dynamic_slice(weights, (0, head * rows, part * cols), (kinds, rows, cols))
+        kinds, _, rows, cols = weights.shape
+        cols = cols // lax.axis_size("dp")
+        piece = lax.dynamic_slice(weights, (0, head, 0, part * cols), (kinds, 1, rows, cols))
         found.append(piece.reshape(kinds * rows, cols))
     return jnp.concatenate(found, axis=0)
 
@@ -448,10 +456,10 @@
             lax.ppermute(state, axis, [(i, i + by) for i in range(peers - by)])
             for by in range(1, peers)
         ]
-        return sum(one.astype(F32) for one in found)
+        return sum(one.astype(F32) for one in found), found[0]
     everything = lax.all_gather(state, axis).astype(F32)
     reached = jnp.arange(peers) < lax.axis_index(axis)
-    return jnp.sum(jnp.where(reached[:, None, None, None], everything, 0.0), axis=0)
+    return jnp.sum(jnp.where(reached[:, None, None, None], everything, 0.0), axis=0), state
 
 
 def on_device(
@@ -486,10 +494,10 @@
     tap_count = conv_window.shape[0]
 
     assert heads == NEAR and dp_count == 2
-    values_t = w_value.T[None]
-    featmap_t = w_featmap.transpose(1, 2, 0)
-    window_t = w_window.transpose(1, 2, 0)
-    out_one, out_two = w_out_one[None], w_out_two[None]
+    values_t = w_value.T.reshape(1, heads, HEAD, width)
+    featmap_t = w_featmap.transpose(1, 2, 0).reshape(2, heads, feature_dim, width)
+    window_t = w_window.transpose(1, 2, 0).reshape(3, heads, HEAD, width)
+    out_one, out_two = (w.reshape(1, heads, HEAD, width) for w in (w_out_one, w_out_two))
     held_one = settled(jnp.stack(from_groups(own_piece([values_t, featmap_t]), ())))
 
     placed = reassign[:, None] == jnp.arange(slots_total, dtype=jnp.int32)[None, :]
@@ -530,6 +538,7 @@
     places = jnp.concatenate([(seq_place % NEAR) ^ jnp.arange(NEAR), dp_place[None]])
     places = places.astype(jnp.int32)
     taps = conv_window.reshape(tap_count, 3, heads, HEAD).transpose(0, 2, 1, 3)
+    taps = jnp.take(taps, places[:NEAR], axis=1, mode="clip")
     taps = jnp.pad(taps, ((0, 0), (0, 0), (0, 0), (0, SLOT - HEAD)))
     taps = taps.reshape(tap_count, 3 * heads * SLOT)
     taps = jnp.stack([taps, across(taps, "tensor", 2)])
@@ -540,12 +549,13 @@
     column[0, HEAD::SLOT] = 1
 
     def copy_sems(kinds):
-        return pltpu.SemaphoreType.DMA((group_count, dp_count * NEAR * kinds))
+        return pltpu.SemaphoreType.DMA((group_count, NEAR * kinds))
 
     def weights_of(rows_of_head):
-        return pltpu.VMEM((group_count, dp_count, heads, rows_of_head, width // dp_count), BF16)
+        return pltpu.VMEM((group_count, heads, rows_of_head, width), BF16)
 
     slots = heads * SLOT
+    mid = 3 * rows // 4
     num, queries, state = call(
         functools.partial(linear_kernel, heads, feature_dim, kept),
         group_count,
@@ -575,17 +585,16 @@
     )(
         places, tokens, gain_one[None], values_t, featmap_t, *near_one, first, second, ones, column
     )
-    prior = settled(earlier_blocks(state, "seq"))
-    beyond = after(beyond, (state,))
+    prior, first_arrived = earlier_blocks(state, "seq")
+    prior = settled(prior)
+    beyond = after(beyond, (first_arrived,))
     held_window, out_beyond = beyond[:, : 3 * HEAD], beyond[0, 3 * HEAD :]
     held_out_two = [out_beyond, across(out_piece, "tensor", 1), across(out_beyond, "tensor", 1)]
-    held_out_two = settled(jnp.stack(held_out_two), (prior,))
-    near_out_one = from_plane(
-        held_out_one, neighbours(held_out_one), (state,), (beyond, held_out_two)
-    )
+    held_out_two = settled(jnp.stack(held_out_two))
+    near_out_one = from_plane(held_out_one, neighbours(held_out_one), (state,), (prior, beyond))
     held_window = after(held_window, (prior,))
     near_by_window = neighbours(held_window)
-    residual, normed_two, tail = call(
+    residual, low, high, tail = call(
         functools.partial(out_one_kernel, heads, kept),
         group_count,
         [
@@ -603,8 +612,8 @@
             whole((rows, width)),
             whole((1, width)),
         ],
-        [whole((rows, width)), whole((rows, width)), whole((HALO, width))],
-        [jax.ShapeDtypeStruct((n, width), BF16) for n in (rows, rows, HALO)],
+        [whole((n, width)) for n in (rows, mid, rows - mid, HALO)],
+        [jax.ShapeDtypeStruct((n, width), BF16) for n in (rows, mid, rows - mid, HALO)],
         [
             pltpu.VMEM((rows, width), F32),
             pltpu.VMEM((rows, slots), BF16),
@@ -618,7 +627,7 @@
     )
 
     halo = lax.ppermute(tail, "seq", [(i, i + 1) for i in range(seq_count - 1)])
-    pair_rows = across(normed_two, "tensor", 1)
+    pair_low, pair_high = across(low, "tensor", 1), across(high, "tensor", 1)
     pair_halo = lax.ppermute(
         tail,
         ("seq", "tensor"),
@@ -628,18 +637,19 @@
             for j in range(group_count)
         ],
     )
-    near_window = from_plane(held_window, near_by_window, None, (residual,))
+    near_window = from_plane(held_window, near_by_window, None, (pair_low, held_out_two))
     held_out_two = after(held_out_two, (residual,))
     block_start = (seq_place * rows).astype(jnp.int32)[None]
 
-    def window_rows(slot_rows, slot_halo, earlier):
+    def window_rows(slot_low, slot_high, slot_halo, earlier):
         return call(
             functools.partial(window_kernel, heads),
             2,
             [
                 SMEM,
                 SMEM,
-                whole((rows, width)),
+                whole((mid, width)),
+                whole((rows - mid, width)),
                 whole((HALO, width)),
                 *[HBM] * 3,
                 each((tap_count, 3 * slots)),
@@ -649,16 +659,16 @@
             jax.ShapeDtypeStruct((2, rows, slots), BF16),
             [
                 pltpu.VMEM((HALO + rows, width), BF16),
-                pltpu.VMEM((2, dp_count, heads, 3 * SLOT, width // dp_count), BF16),
+                pltpu.VMEM((2, heads, 3 * SLOT, width), BF16),
                 copy_sems(3),
             ],
             "window_rows",
             6 * rows * width * 3 * head_cols,
-        )(places, block_start, slot_rows, slot_halo, window_t, *near_window, taps, earlier)
-
-    mixed_own = window_rows(normed_two, halo, normed_two)
-    mixed_pair = window_rows(pair_rows, pair_halo, mixed_own)
+        )(places, block_start, slot_low, slot_high, slot_halo, window_t, *near_window, taps, earlier)
+
+    mixed_pair = window_rows(pair_low, pair_high, pair_halo, halo)
     near_out_two = from_plane(held_out_two, neighbours(held_out_two), None, (mixed_pair,))
+    mixed_own = window_rows(low, high, halo, mixed_pair)
     mixed_pair = across(mixed_pair, "tensor", 1)
     live = (length - seq_place * rows).astype(jnp.int32)[None]
     result = call(

time: 309 us -> 312 us (level)
  waiting for transfers between devices: 90.9 us -> 108 us
  Pallas kernels: 67.3 us -> 58.3 us
  starting transfers between devices: 60.5 us -> 54.4 us
    ppermute x30 -> x31, waiting for transfers between devices: 58.9 us -> 68.6 us  [across(): lax.ppermute(array, axis, [(i, i ^ bit) for i in range(lax.axis_size(axis...]
    unnamed x69 -> x54, local copies, waits for them, and re-layouts: 13.6 us -> 4.84 us
    ppermute x3, waiting for transfers between devices: 13.1 us -> 20.7 us  [earlier_blocks(): lax.ppermute(state, axis, [(i, i + by) for i in range(peers - by)])]
    ppermute x30 -> x31, starting transfers between devices: 34.3 us -> 29.3 us  [across(): lax.ppermute(array, axis, [(i, i ^ bit) for i in range(lax.axis_size(axis...]
    slice x10 -> x12, local copies, waits for them, and re-layouts: 6.83 us -> 9.1 us  [after(): lax.slice(other, (0,) * other.ndim, (1,) * other.ndim)]
    select_n x18 -> x17, other arithmetic: 15 us -> 16 us  [after(): return jnp.where(zero == 0.0, array, jnp.zeros_like(array))]
  transfers between devices with their start and end apart: 37 -> 38, of which waited for: 13 -> 14; matrix products, arithmetic and copies ran while one was open for 9% -> 11% of each run, Pallas kernels for 19% -> 17%
where the time goes in v8:
time: 312 us; the launch traced here: 311 us
  waiting for transfers between devices  108 us (35%)
  Pallas kernels  58.3 us (19%)
  starting transfers between devices  54.4 us (17%)
  local copies, waits for them, and re-layouts  30.9 us (10%)
  blocking collectives  25.9 us (8%)
  other arithmetic  24.6 us (8%)
  between operations  8.91 us (3%)
    ppermute x31, waiting for transfers between devices, across(): lax.ppermute(array, axis, [(i, i ^ bit) for i in range(lax.axis_size(axis...  68.6 us
    ppermute x31, starting transfers between devices, across(): lax.ppermute(array, axis, [(i, i ^ bit) for i in range(lax.axis_size(axis...  29.3 us
    pallas_call x2, Pallas kernels, window_rows(): call(functools.partial(window_kernel, heads), 2, [SMEM, SMEM, whole((mid,...  28.5 us
    all_to_all x1, blocking collectives, on_device(): lax.all_to_all(result, 'tensor', split_axis=0, concat_axis=0, tiled=True)  25.9 us
    ppermute x3, waiting for transfers between devices, earlier_blocks(): lax.ppermute(state, axis, [(i, i + by) for i in range(peers - by)])  20.7 us
    all_to_all x1, waiting for transfers between devices, on_device(): lax.all_to_all(picked, 'tensor', split_axis=0, concat_axis=0, tiled=True)  18.8 us
    select_n x17, other arithmetic, after(): return jnp.where(zero == 0.0, array, jnp.zeros_like(array))  16 us
    pallas_call x1, Pallas kernels, on_device(): call(functools.partial(linear_kernel, heads, feature_dim, kept), group_co...  12.4 us
  transfers between devices with their start and end apart: 38, of which 14 were waited for; matrix products, arithmetic and copies ran while one was open for 11% of the time, Pallas kernels for 17%

profile of v8, /device:TPU:0, one launch (start us, length us, event | category | flops | bytes accessed | tf_op | source)
XLA Modules:
  0.0 311.1 jit_solution(12074068209504491622)
XLA Ops:
  2.5 2.2 gather_fusion
  4.7 5.2 %all-to-all-start = ((bf16[8,8,4,1792]{3,2,1,0:T(4,128)(2,1)}), bf16[8,8,4,1792]{3,2,1,0:T(4,128)(2,1)S(1)}, u32[]{:S(2)}, u32[]{:S(2)}) async-start(bf16[8,8,4,1792]{3,2,1,0:T(4,128)(2,1)} %bitcast.15), calls=%async_computation | async-start | bytes 1835008 | tf_op jit(solution)/shard_map/all_to_all | solution.py:522
  11.6 2.7 collective-permute-start.1
  14.3 1.6 collective-permute-start
  16.1 10.7 %collective-permute-done.1 = bf16[144,896]{1,0:T(8,128)(2,1)S(1)} collective-permute-done((bf16[144,896]{1,0:T(8,128)(2,1)S(1)}, bf16[144,896]{1,0:T(8,128)(2,1)S(1)}, u32[]{:S(2)}, u32[]{:S(2)}) %collective-permute-start.1) | collective-permute-done | bytes 258080 | tf_op jit(solution)/shard_map/ppermute | solution.py:407
  27.5 7.2 %collective-permute-done.2 = bf16[144,896]{1,0:T(8,128)(2,1)S(1)} collective-permute-done((bf16[144,896]{1,0:T(8,128)(2,1)S(1)}, bf16[144,896]{1,0:T(8,128)(2,1)S(1)}, u32[]{:S(2)}, u32[]{:S(2)}) %collective-permute-start.2) | collective-permute-done | bytes 258080 | tf_op jit(solution)/shard_map/ppermute | solution.py:407
  36.0 1.4 gather_fusion.1
  37.8 1.0 copy.44
  38.8 5.1 %all-to-all-start.1 = ((bf16[4,16,4,1792]{3,1,2,0:T(8,128)(2,1)}), bf16[4,16,4,1792]{3,1,2,0:T(8,128)(2,1)S(1)}, u32[]{:S(2)}, u32[]{:S(2)}) async-start(bf16[4,16,4,1792]{3,1,2,0:T(8,128)(2,1)} %copy.44), calls=%async_computation.1 | async-start | bytes 1835008 | tf_op jit(solution)/shard_map/all_to_all | solution.py:529
  43.9 1.6 collective-permute-start.7
  45.5 1.5 collective-permute-start.6
  48.2 1.6 select_bitcast_fusion.1
  49.8 2.9 collective-permute-start.4
  52.7 18.8 %all-to-all-done.1 = bf16[4,16,4,1792]{3,1,2,0:T(8,128)(2,1)S(1)} async-done(((bf16[4,16,4,1792]{3,1,2,0:T(8,128)(2,1)}), bf16[4,16,4,1792]{3,1,2,0:T(8,128)(2,1)S(1)}, u32[]{:S(2)}, u32[]{:S(2)}) %all-to-all-start.1) | async-done | bytes 917536 | tf_op jit(solution)/shard_map/all_to_all | solution.py:529
  72.8 1.7 collective-permute-start.8
  74.5 1.0 slice_select_fusion.3
  75.5 1.5 collective-permute-start.9
  77.0 2.0 collective-permute-start.5
  79.1 4.7 %collective-permute-done.3 = bf16[112,896]{1,0:T(8,128)(2,1)S(1)} collective-permute-done((bf16[112,896]{1,0:T(8,128)(2,1)}, bf16[112,896]{1,0:T(8,128)(2,1)S(1)}, u32[]{:S(2)}, u32[]{:S(2)}) %collective-permute-start.3) | collective-permute-done | bytes 200736 | tf_op jit(solution)/shard_map/ppermute | solution.py:407
  83.7 2.1 collective-permute-done.5
  85.9 1.8 pad_maximum_fusion.1
  87.7 1.1 slice.88
  89.6 1.8 maximum_select_fusion.near_ref
  92.8 2.0 constant_dynamic-slice_fusion
  95.9 1.4 copy.45
  97.3 2.4 reshape.473.x_ref
  99.7 12.4 %linear_rows.1 = (f32[4,256,512]{2,1,0:T(8,128)}, bf16[4,256,128]{2,1,0:T(8,128)(2,1)}, bf16[4,640,128]{2,1,0:T(8,128)(2,1)}) custom-call(s32[5]{0:T(128)} %pad_add_fusion.place_ref, bf16[256,1792]{1,0:T(8,128)(2,1)} %reshape.473.x_ref, f32[1,1792]{1,0:T(1,128)} %broadcast_in_dim.128.gain_ref, bf16[1,4,112,1792]{3,2,1,0:T(8,128)(2,1)} %bitcast.96, ...), custom_call_target="tpu_custom_call" | custom-call | tf_op jit(solution)/shard_map/linear_rows/pallas_call | solution.py:559
  112.1 4.4 %collective-permute-start.13 = (bf16[4,640,128]{2,1,0:T(8,128)(2,1)}, bf16[4,640,128]{2,1,0:T(8,128)(2,1)S(1)}, u32[]{:S(2)}, u32[]{:S(2)}) collective-permute-start(bf16[4,640,128]{2,1,0:T(8,128)(2,1)} %get-tuple-element.14), channel_id=1, source_target_pairs={{0,12},{1,13},{2,14},{3,15},{16,28},{17,29},{18,30},{19,31}} | collective-permute-start | bytes 1966088 | tf_op jit(solution)/shard_map/ppermute | solution.py:456
  116.5 1.3 collective-permute-start.12
  117.9 2.7 collective-permute-start.11
  120.5 1.7 broadcast_select_fusion.2
  122.7 1.2 slice.71
  124.5 1.0 slice_select_fusion.4
  125.6 1.0 slice_select_fusion.2
  126.6 5.3 %collective-permute-done.13 = bf16[4,640,128]{2,1,0:T(8,128)(2,1)S(1)} collective-permute-done((bf16[4,640,128]{2,1,0:T(8,128)(2,1)}, bf16[4,640,128]{2,1,0:T(8,128)(2,1)S(1)}, u32[]{:S(2)}, u32[]{:S(2)}) %collective-permute-start.13) | collective-permute-done | bytes 655392 | tf_op jit(solution)/shard_map/ppermute | solution.py:456
  132.0 15.3 %collective-permute-done.12 = bf16[4,640,128]{2,1,0:T(8,128)(2,1)S(1)} collective-permute-done((bf16[4,640,128]{2,1,0:T(8,128)(2,1)}, bf16[4,640,128]{2,1,0:T(8,128)(2,1)S(1)}, u32[]{:S(2)}, u32[]{:S(2)}) %collective-permute-start.12) | collective-permute-done | bytes 655392 | tf_op jit(solution)/shard_map/ppermute | solution.py:456
  149.9 9.4 %collective-permute-done.14 = bf16[448,896]{1,0:T(8,128)(2,1)S(1)} collective-permute-done((bf16[448,896]{1,0:T(8,128)(2,1)S(1)}, bf16[448,896]{1,0:T(8,128)(2,1)S(1)}, u32[]{:S(2)}, u32[]{:S(2)}) %collective-permute-start.14) | collective-permute-done | bytes 802848 | tf_op jit(solution)/shard_map/ppermute | solution.py:407
  160.7 1.9 maximum_select_fusion.1.near_ref
  163.4 3.8 %collective-permute-done.19.far_ref = bf16[4,3,112,896]{3,2,1,0:T(8,128)(2,1)S(1)} collective-permute-done((bf16[4,3,112,896]{3,2,1,0:T(8,128)(2,1)S(1)}, bf16[4,3,112,896]{3,2,1,0:T(8,128)(2,1)S(1)}, u32[]{:S(2)}, u32[]{:S(2)}) %collective-permute-start.19) | collective-permute-done | bytes 2408480 | tf_op jit(solution)/shard_map/ppermute | solution.py:407
  167.2 1.5 copy-done.10
  168.7 10.5 %linear_out.1 = (bf16[256,1792]{1,0:T(8,128)(2,1)}, bf16[192,1792]{1,0:T(8,128)(2,1)}, bf16[64,1792]{1,0:T(8,128)(2,1)}, bf16[80,1792]{1,0:T(8,128)(2,1)}) custom-call(s32[5]{0:T(128)} %pad_add_fusion.place_ref, f32[4,256,512]{2,1,0:T(8,128)} %get-tuple-element.12.num_ref, bf16[4,256,128]{2,1,0:T(8,128)(2,1)} %get-tuple-element.13.q_ref, ...), custom_call_target="tpu_custom_call" | custom-call | tf_op jit(solution)/shard_map/linear_out/pallas_call | solution.py:597
  179.5 1.7 collective-permute-start.25
  181.2 1.8 collective-permute-start.24
  183.0 2.1 collective-permute-start.23
  186.0 15.3 %collective-permute-done.23 = bf16[112,896]{1,0:T(8,128)(2,1)S(1)} collective-permute-done((bf16[112,896]{1,0:T(8,128)(2,1)S(1)}, bf16[112,896]{1,0:T(8,128)(2,1)S(1)}, u32[]{:S(2)}, u32[]{:S(2)}) %collective-permute-start.23) | collective-permute-done | bytes 200736 | tf_op jit(solution)/shard_map/ppermute | solution.py:407
  204.4 3.7 %collective-permute-done.25 = bf16[1,336,896]{2,1,0:T(8,128)(2,1)} collective-permute-done((bf16[1,336,896]{2,1,0:T(8,128)(2,1)S(1)}, bf16[1,336,896]{2,1,0:T(8,128)(2,1)}, u32[]{:S(2)}, u32[]{:S(2)}) %collective-permute-start.25) | collective-permute-done | bytes 602144 | tf_op jit(solution)/shard_map/ppermute | solution.py:407
  208.2 2.1 maximum_select_fusion.2.near_ref
  210.4 3.7 %collective-permute-start.20 = (bf16[80,1792]{1,0:T(8,128)(2,1)S(1)}, bf16[80,1792]{1,0:T(8,128)(2,1)}, u32[]{:S(2)}, u32[]{:S(2)}) collective-permute-start(bf16[80,1792]{1,0:T(8,128)(2,1)S(1)} %copy-done.21), channel_id=1, source_target_pairs={{0,4},{4,8},{8,12},{1,5},{5,9},{9,13},{2,6},{6,10},{10,14},{3,7},{... | collective-permute-start | bytes 860168 | tf_op jit(solution)/shard_map/ppermute | solution.py:629
  214.9 1.8 collective-permute-start.28
  216.7 2.8 collective-permute-start.30
  219.4 1.8 collective-permute-start.29
  221.2 1.3 slice.79
  224.1 8.6 %collective-permute-done.29.high_ref = bf16[64,1792]{1,0:T(8,128)(2,1)S(1)} collective-permute-done((bf16[64,1792]{1,0:T(8,128)(2,1)}, bf16[64,1792]{1,0:T(8,128)(2,1)S(1)}, u32[]{:S(2)}, u32[]{:S(2)}) %collective-permute-start.29) | collective-permute-done | bytes 229408 | tf_op jit(solution)/shard_map/ppermute | solution.py:407
  233.7 1.0 fusion.13
  235.4 14.2 %window_rows.2._ = bf16[2,256,512]{2,1,0:T(8,128)(2,1)} custom-call(s32[5]{0:T(128)} %pad_add_fusion.place_ref, s32[1]{0:T(128)} %bitcast.2.first_ref, bf16[192,1792]{1,0:T(8,128)(2,1)} %copy-done.19, bf16[64,1792]{1,0:T(8,128)(2,1)} %copy-done.23, bf16[80,1792]{1,0:T(8,128)(2,1)} %copy-done.22, bf16[3,4,112,1792]{3,2,1,0:T(8,128)(2,1)} %bitcast.121, ...), custom_call_target="tpu_custom_call" | custom-call | flops 3699376128 | tf_op jit(solution)/shard_map/window_rows/pallas_call | solution.py:645
  249.6 1.2 slice.101
  251.5 1.9 collective-permute-done.33
  253.4 1.1 collective-permute-done.32
  254.5 2.1 maximum_select_fusion.3.near_ref
  256.7 1.8 collective-permute-start.31
  260.0 14.3 %window_rows.3.mixed_ref = bf16[2,256,512]{2,1,0:T(8,128)(2,1)} custom-call(s32[5]{0:T(128)} %pad_add_fusion.place_ref, s32[1]{0:T(128)} %bitcast.2.first_ref, bf16[192,1792]{1,0:T(8,128)(2,1)} %get-tuple-element.15.low_ref, bf16[64,1792]{1,0:T(8,128)(2,1)} %get-tuple-element.16.high_ref, bf16[80,1792]{1,0:T(8,128)(2,1)} %collective-permute-done.20._.halo_ref, ...), custom_call_target="tpu_custom_call" | custom-call | flops 3699376128 | tf_op jit(solution)/shard_map/window_rows/pallas_call | solution.py:645
  275.1 7.0 %window_out.1 = bf16[256,1792]{1,0:T(8,128)(2,1)} custom-call(s32[5]{0:T(128)} %pad_add_fusion.place_ref, s32[1]{0:T(128)} %bitcast.1.live_ref, bf16[2,256,512]{2,1,0:T(8,128)(2,1)} %window_rows.3.mixed_ref, bf16[2,256,512]{2,1,0:T(8,128)(2,1)} %copy-done.15, bf16[1,4,112,1792]{3,2,1,0:T(8,128)(2,1)} %bitcast.100, bf16[4,3,112,896]{3,2,1,0:T(8,128)(2,1)} %copy-done.3, ...), custom_call_target="tpu_custom_call" | custom-call | tf_op jit(solution)/shard_map/window_out/pallas_call | solution.py:674
  282.1 1.9 reshape.481
  284.3 25.9 %all_to_all.15 = bf16[4,16,4,1792]{3,2,1,0:T(4,128)(2,1)S(1)} all-to-all(bf16[4,16,4,1792]{3,2,1,0:T(4,128)(2,1)S(1)} %bitcast.91), channel_id=1, replica_groups=mesh['dp'=2,'seq'=4,'tensor'=4] {'tensor'}, dimensions={0} | all-to-all | bytes 1835008 | tf_op jit(solution)/shard_map/all_to_all | solution.py:696
  (154 shorter events, 23.0 us)
Async XLA Ops:
  0.0 2.5 copy-start
  4.7 31.3 %all-to-all-start = ((bf16[8,8,4,1792]{3,2,1,0:T(4,128)(2,1)}), bf16[8,8,4,1792]{3,2,1,0:T(4,128)(2,1)S(1)}, u32[]{:S(2)}, u32[]{:S(2)}) async-start(bf16[8,8,4,1792]{3,2,1,0:T(4,128)(2,1)} %bitcast.15), calls=%async_computation | async-start | bytes 1835008 | tf_op jit(solution)/shard_map/all_to_all | solution.py:522
  11.6 15.2 %collective-permute-start.1 = (bf16[144,896]{1,0:T(8,128)(2,1)S(1)}, bf16[144,896]{1,0:T(8,128)(2,1)S(1)}, u32[]{:S(2)}, u32[]{:S(2)}) collective-permute-start(bf16[144,896]{1,0:T(8,128)(2,1)S(1)} %pad_maximum_fusion.3), channel_id=1, source_target_pairs={{0,2},{1,3},{2,0},{3,1},{4,6},{5,7},{6,4},{7,5},{8,10},{9,11},{10,... | collective-permute-start | bytes 774152 | tf_op jit(solution)/shard_map/ppermute | solution.py:407
  14.3 13.2 %collective-permute-start = (bf16[144,896]{1,0:T(8,128)(2,1)S(1)}, bf16[144,896]{1,0:T(8,128)(2,1)S(1)}, u32[]{:S(2)}, u32[]{:S(2)}) collective-permute-start(bf16[144,896]{1,0:T(8,128)(2,1)S(1)} %pad_maximum_fusion.3), channel_id=1, source_target_pairs={{0,1},{1,0},{2,3},{3,2},{4,5},{5,4},{6,7},{7,6},{8,9},{9,8},{10,11... | collective-permute-start | bytes 774152 | tf_op jit(solution)/shard_map/ppermute | solution.py:407
  26.9 7.8 %collective-permute-start.2 = (bf16[144,896]{1,0:T(8,128)(2,1)S(1)}, bf16[144,896]{1,0:T(8,128)(2,1)S(1)}, u32[]{:S(2)}, u32[]{:S(2)}) collective-permute-start(bf16[144,896]{1,0:T(8,128)(2,1)S(1)} %collective-permute-done.1), channel_id=1, source_target_pairs={{0,1},{1,0},{2,3},{3,2},{4,5},{5,4},{6,7},{7,6},{8,9},{9,8},{10,11... | collective-permute-start | bytes 774152 | tf_op jit(solution)/shard_map/ppermute | solution.py:407
  34.8 10.7 %copy-start.8 = (bf16[3,144,896]{2,1,0:T(8,128)(2,1)}, bf16[3,144,896]{2,1,0:T(8,128)(2,1)S(1)}, u32[]{:S(2)}) copy-start(bf16[3,144,896]{2,1,0:T(8,128)(2,1)S(1)} %pad_maximum_fusion) | copy-start | bytes 2322436
  38.8 32.7 %all-to-all-start.1 = ((bf16[4,16,4,1792]{3,1,2,0:T(8,128)(2,1)}), bf16[4,16,4,1792]{3,1,2,0:T(8,128)(2,1)S(1)}, u32[]{:S(2)}, u32[]{:S(2)}) async-start(bf16[4,16,4,1792]{3,1,2,0:T(8,128)(2,1)} %copy.44), calls=%async_computation.1 | async-start | bytes 1835008 | tf_op jit(solution)/shard_map/all_to_all | solution.py:529
  43.9 28.9 %collective-permute-start.7 = (bf16[3,144,896]{2,1,0:T(8,128)(2,1)S(1)}, bf16[3,144,896]{2,1,0:T(8,128)(2,1)S(1)}, u32[]{:S(2)}, u32[]{:S(2)}) collective-permute-start(bf16[3,144,896]{2,1,0:T(8,128)(2,1)S(1)} %pad_maximum_fusion), channel_id=1, source_target_pairs={{0,8},{4,12},{8,0},{12,4},{1,9},{5,13},{9,1},{13,5},{2,10},{6,14},... | collective-permute-start | bytes 2322440 | tf_op jit(solution)/shard_map/ppermute | solution.py:407
  45.5 29.0 %collective-permute-start.6 = (bf16[3,144,896]{2,1,0:T(8,128)(2,1)S(1)}, bf16[3,144,896]{2,1,0:T(8,128)(2,1)}, u32[]{:S(2)}, u32[]{:S(2)}) collective-permute-start(bf16[3,144,896]{2,1,0:T(8,128)(2,1)S(1)} %pad_maximum_fusion), channel_id=1, source_target_pairs={{0,4},{4,0},{8,12},{12,8},{1,5},{5,1},{9,13},{13,9},{2,6},{6,2},{1... | collective-permute-start | bytes 2322440 | tf_op jit(solution)/shard_map/ppermute | solution.py:407
  49.8 27.2 %collective-permute-start.4 = (bf16[112,896]{1,0:T(8,128)(2,1)}, bf16[112,896]{1,0:T(8,128)(2,1)}, u32[]{:S(2)}, u32[]{:S(2)}) collective-permute-start(bf16[112,896]{1,0:T(8,128)(2,1)} %select_bitcast_fusion.1), channel_id=1, source_target_pairs={{0,2},{1,3},{2,0},{3,1},{4,6},{5,7},{6,4},{7,5},{8,10},{9,11},{10,... | collective-permute-start | bytes 602120 | tf_op jit(solution)/shard_map/ppermute | solution.py:407
  71.5 18.0 %copy-start.6 = (bf16[4,16,4,1792]{3,1,2,0:T(8,128)(2,1)}, bf16[4,16,4,1792]{3,1,2,0:T(8,128)(2,1)S(1)}, u32[]{:S(2)}) copy-start(bf16[4,16,4,1792]{3,1,2,0:T(8,128)(2,1)S(1)} %all-to-all-done.1) | copy-start | bytes 2752516
  71.5 18.0 %copy-start.9 = (bf16[3,144,896]{2,1,0:T(8,128)(2,1)S(1)}, bf16[3,144,896]{2,1,0:T(8,128)(2,1)}, u32[]{:S(2)}) copy-start(bf16[3,144,896]{2,1,0:T(8,128)(2,1)} %copy-done.8) | copy-start | bytes 2322436
  72.8 16.8 %copy-start.13 = (bf16[3,144,896]{2,1,0:T(8,128)(2,1)}, bf16[3,144,896]{2,1,0:T(8,128)(2,1)S(1)}, u32[]{:S(2)}) copy-start(bf16[3,144,896]{2,1,0:T(8,128)(2,1)S(1)} %collective-permute-done.7) | copy-start | bytes 2322436
  72.8 16.6 %collective-permute-start.8 = (bf16[3,80,896]{2,1,0:T(8,128)(2,1)S(1)}, bf16[3,80,896]{2,1,0:T(8,128)(2,1)S(1)}, u32[]{:S(2)}, u32[]{:S(2)}) collective-permute-start(bf16[3,80,896]{2,1,0:T(8,128)(2,1)S(1)} %slice_select_fusion.1), channel_id=1, source_target_pairs={{0,4},{4,0},{8,12},{12,8},{1,5},{5,1},{9,13},{13,9},{2,6},{6,2},{1... | collective-permute-start | bytes 1290248 | tf_op jit(solution)/shard_map/ppermute | solution.py:407
  75.5 13.9 %collective-permute-start.9 = (bf16[3,64,896]{2,1,0:T(8,128)(2,1)S(1)}, bf16[3,64,896]{2,1,0:T(8,128)(2,1)S(1)}, u32[]{:S(2)}, u32[]{:S(2)}) collective-permute-start(bf16[3,64,896]{2,1,0:T(8,128)(2,1)S(1)} %slice_select_fusion.3), channel_id=1, source_target_pairs={{0,8},{4,12},{8,0},{12,4},{1,9},{5,13},{9,1},{13,5},{2,10},{6,14},... | collective-permute-start | bytes 1032200 | tf_op jit(solution)/shard_map/ppermute | solution.py:407
  77.0 6.7 %collective-permute-start.3 = (bf16[112,896]{1,0:T(8,128)(2,1)}, bf16[112,896]{1,0:T(8,128)(2,1)S(1)}, u32[]{:S(2)}, u32[]{:S(2)}) collective-permute-start(bf16[112,896]{1,0:T(8,128)(2,1)} %select_bitcast_fusion.1), channel_id=1, source_target_pairs={{0,1},{1,0},{2,3},{3,2},{4,5},{5,4},{6,7},{7,6},{8,9},{9,8},{10,11... | collective-permute-start | bytes 602120 | tf_op jit(solution)/shard_map/ppermute | solution.py:407
  77.0 8.8 %collective-permute-start.5 = (bf16[112,896]{1,0:T(8,128)(2,1)}, bf16[112,896]{1,0:T(8,128)(2,1)S(1)}, u32[]{:S(2)}, u32[]{:S(2)}) collective-permute-start(bf16[112,896]{1,0:T(8,128)(2,1)} %collective-permute-done.4), channel_id=1, source_target_pairs={{0,1},{1,0},{2,3},{3,2},{4,5},{5,4},{6,7},{7,6},{8,9},{9,8},{10,11... | collective-permute-start | bytes 602120 | tf_op jit(solution)/shard_map/ppermute | solution.py:407
  89.6 1.9 copy-start.17
  89.6 6.3 %copy-start.7 = (bf16[4,16,4,1792]{3,1,2,0:T(8,128)(2,1)S(1)}, bf16[4,16,4,1792]{3,1,2,0:T(8,128)(2,1)}, u32[]{:S(2)}) copy-start(bf16[4,16,4,1792]{3,1,2,0:T(8,128)(2,1)} %copy-done.6) | copy-start | bytes 2752516
  91.4 8.2 %copy-start.2 = (bf16[4,3,144,896]{3,2,1,0:T(8,128)(2,1)}, bf16[4,3,144,896]{3,2,1,0:T(8,128)(2,1)S(1)}, u32[]{:S(2)}) copy-start(bf16[4,3,144,896]{3,2,1,0:T(8,128)(2,1)S(1)} %maximum_select_fusion.near_ref) | copy-start | bytes 9289732
  91.5 8.2 %collective-permute-start.10 = (bf16[4,3,144,896]{3,2,1,0:T(8,128)(2,1)S(1)}, bf16[4,3,144,896]{3,2,1,0:T(8,128)(2,1)}, u32[]{:S(2)}, u32[]{:S(2)}) collective-permute-start(bf16[4,3,144,896]{3,2,1,0:T(8,128)(2,1)S(1)} %maximum_select_fusion.near_ref), channel_id=1, source_target_pairs={{0,16},{16,0},{1,17},{17,1},{2,18},{18,2},{3,19},{19,3},{4,20},{20... | collective-permute-start | bytes 9289736 | tf_op jit(solution)/shard_map/ppermute | solution.py:407
  92.2 30.1 %collective-permute-start.15 = (bf16[3,112,896]{2,1,0:T(8,128)(2,1)}, bf16[3,112,896]{2,1,0:T(8,128)(2,1)}, u32[]{:S(2)}, u32[]{:S(2)}) collective-permute-start(bf16[3,112,896]{2,1,0:T(8,128)(2,1)} %pad_maximum_fusion.1), channel_id=1, source_target_pairs={{0,4},{4,0},{8,12},{12,8},{1,5},{5,1},{9,13},{13,9},{2,6},{6,2},{1... | collective-permute-start | bytes 1806344 | tf_op jit(solution)/shard_map/ppermute | solution.py:407
  94.8 30.7 %collective-permute-start.16 = (bf16[3,112,896]{2,1,0:T(8,128)(2,1)}, bf16[3,112,896]{2,1,0:T(8,128)(2,1)}, u32[]{:S(2)}, u32[]{:S(2)}) collective-permute-start(bf16[3,112,896]{2,1,0:T(8,128)(2,1)} %pad_maximum_fusion.1), channel_id=1, source_target_pairs={{0,8},{4,12},{8,0},{12,4},{1,9},{5,13},{9,1},{13,5},{2,10},{6,14},... | collective-permute-start | bytes 1806344 | tf_op jit(solution)/shard_map/ppermute | solution.py:407
  99.7 22.5 %copy-start.12 = (bf16[3,1,112,896]{3,2,1,0:T(8,128)(2,1)S(1)}, bf16[3,1,112,896]{3,2,1,0:T(8,128)(2,1)}, u32[]{:S(2)}) copy-start(bf16[3,1,112,896]{3,2,1,0:T(8,128)(2,1)} %constant_dynamic-slice_fusion) | copy-start | bytes 1806340
  112.1 19.9 %collective-permute-start.13 = (bf16[4,640,128]{2,1,0:T(8,128)(2,1)}, bf16[4,640,128]{2,1,0:T(8,128)(2,1)S(1)}, u32[]{:S(2)}, u32[]{:S(2)}) collective-permute-start(bf16[4,640,128]{2,1,0:T(8,128)(2,1)} %get-tuple-element.14), channel_id=1, source_target_pairs={{0,12},{1,13},{2,14},{3,15},{16,28},{17,29},{18,30},{19,31}} | collective-permute-start | bytes 1966088 | tf_op jit(solution)/shard_map/ppermute | solution.py:456
  116.5 30.8 %collective-permute-start.12 = (bf16[4,640,128]{2,1,0:T(8,128)(2,1)}, bf16[4,640,128]{2,1,0:T(8,128)(2,1)S(1)}, u32[]{:S(2)}, u32[]{:S(2)}) collective-permute-start(bf16[4,640,128]{2,1,0:T(8,128)(2,1)} %get-tuple-element.14), channel_id=1, source_target_pairs={{0,8},{4,12},{1,9},{5,13},{2,10},{6,14},{3,11},{7,15},{16,24},{20,... | collective-permute-start | bytes 1966088 | tf_op jit(solution)/shard_map/ppermute | solution.py:456
  117.9 29.4 %collective-permute-start.11 = (bf16[4,640,128]{2,1,0:T(8,128)(2,1)}, bf16[4,640,128]{2,1,0:T(8,128)(2,1)S(1)}, u32[]{:S(2)}, u32[]{:S(2)}) collective-permute-start(bf16[4,640,128]{2,1,0:T(8,128)(2,1)} %get-tuple-element.14), channel_id=1, source_target_pairs={{0,4},{4,8},{8,12},{1,5},{5,9},{9,13},{2,6},{6,10},{10,14},{3,7},{... | collective-permute-start | bytes 1966088 | tf_op jit(solution)/shard_map/ppermute | solution.py:456
  122.3 36.9 %collective-permute-start.14 = (bf16[448,896]{1,0:T(8,128)(2,1)S(1)}, bf16[448,896]{1,0:T(8,128)(2,1)S(1)}, u32[]{:S(2)}, u32[]{:S(2)}) collective-permute-start(bf16[448,896]{1,0:T(8,128)(2,1)S(1)} %maximum_select_fusion.4), channel_id=1, source_target_pairs={{0,2},{1,3},{2,0},{3,1},{4,6},{5,7},{6,4},{7,5},{8,10},{9,11},{10,... | collective-permute-start | bytes 2408456 | tf_op jit(solution)/shard_map/ppermute | solution.py:407
  125.5 35.0 %collective-permute-start.18 = (bf16[3,48,896]{2,1,0:T(8,128)(2,1)S(1)}, bf16[3,48,896]{2,1,0:T(8,128)(2,1)S(1)}, u32[]{:S(2)}, u32[]{:S(2)}) collective-permute-start(bf16[3,48,896]{2,1,0:T(8,128)(2,1)S(1)} %slice_select_fusion.4), channel_id=1, source_target_pairs={{0,8},{4,12},{8,0},{12,4},{1,9},{5,13},{9,1},{13,5},{2,10},{6,14},... | collective-permute-start | bytes 774152 | tf_op jit(solution)/shard_map/ppermute | solution.py:407
  132.0 28.6 %collective-permute-start.17 = (bf16[3,64,896]{2,1,0:T(8,128)(2,1)S(1)}, bf16[3,64,896]{2,1,0:T(8,128)(2,1)S(1)}, u32[]{:S(2)}, u32[]{:S(2)}) collective-permute-start(bf16[3,64,896]{2,1,0:T(8,128)(2,1)S(1)} %slice_select_fusion.2), channel_id=1, source_target_pairs={{0,4},{4,0},{8,12},{12,8},{1,5},{5,1},{9,13},{13,9},{2,6},{6,2},{1... | collective-permute-start | bytes 1032200 | tf_op jit(solution)/shard_map/ppermute | solution.py:407
  147.5 13.1 %copy-start.5 = (f32[4,640,128]{2,1,0:T(8,128)}, f32[4,640,128]{2,1,0:T(8,128)S(1)}, u32[]{:S(2)}) copy-start(f32[4,640,128]{2,1,0:T(8,128)S(1)} %convert_add_fusion.prior_ref) | copy-start | bytes 3932164
  160.7 2.0 copy-start.18
  162.6 6.2 %copy-start.4 = (bf16[4,3,112,896]{3,2,1,0:T(8,128)(2,1)}, bf16[4,3,112,896]{3,2,1,0:T(8,128)(2,1)S(1)}, u32[]{:S(2)}) copy-start(bf16[4,3,112,896]{3,2,1,0:T(8,128)(2,1)S(1)} %maximum_select_fusion.1.near_ref) | copy-start | bytes 7225348
  162.6 4.7 %collective-permute-start.19 = (bf16[4,3,112,896]{3,2,1,0:T(8,128)(2,1)S(1)}, bf16[4,3,112,896]{3,2,1,0:T(8,128)(2,1)S(1)}, u32[]{:S(2)}, u32[]{:S(2)}) collective-permute-start(bf16[4,3,112,896]{3,2,1,0:T(8,128)(2,1)S(1)} %maximum_select_fusion.1.near_ref), channel_id=1, source_target_pairs={{0,16},{16,0},{1,17},{17,1},{2,18},{18,2},{3,19},{19,3},{4,20},{20... | collective-permute-start | bytes 7225352 | tf_op jit(solution)/shard_map/ppermute | solution.py:407
  163.4 19.6 %collective-permute-start.22 = (bf16[112,896]{1,0:T(8,128)(2,1)}, bf16[112,896]{1,0:T(8,128)(2,1)S(1)}, u32[]{:S(2)}, u32[]{:S(2)}) collective-permute-start(bf16[112,896]{1,0:T(8,128)(2,1)} %get-tuple-element.19), channel_id=1, source_target_pairs={{0,1},{1,0},{2,3},{3,2},{4,5},{5,4},{6,7},{7,6},{8,9},{9,8},{10,11... | collective-permute-start | bytes 602120 | tf_op jit(solution)/shard_map/ppermute | solution.py:407
  167.2 1.5 copy-start.10
  179.2 23.2 %collective-permute-start.21 = (bf16[192,1792]{1,0:T(8,128)(2,1)}, bf16[192,1792]{1,0:T(8,128)(2,1)S(1)}, u32[]{:S(2)}, u32[]{:S(2)}) collective-permute-start(bf16[192,1792]{1,0:T(8,128)(2,1)} %get-tuple-element.15.low_ref), channel_id=1, source_target_pairs={{0,1},{1,0},{2,3},{3,2},{4,5},{5,4},{6,7},{7,6},{8,9},{9,8},{10,11... | collective-permute-start | bytes 2064392 | tf_op jit(solution)/shard_map/ppermute | solution.py:407
  179.4 25.0 %collective-permute-start.26 = (bf16[1,336,896]{2,1,0:T(8,128)(2,1)S(1)}, bf16[1,336,896]{2,1,0:T(8,128)(2,1)S(1)}, u32[]{:S(2)}, u32[]{:S(2)}) collective-permute-start(bf16[1,336,896]{2,1,0:T(8,128)(2,1)S(1)} %slice_select_fusion), channel_id=1, source_target_pairs={{0,12},{4,8},{8,4},{12,0},{1,13},{5,9},{9,5},{13,1},{2,14},{6,10},... | collective-permute-start | bytes 1806344 | tf_op jit(solution)/shard_map/ppermute | solution.py:407
  179.5 28.7 %collective-permute-start.25 = (bf16[1,336,896]{2,1,0:T(8,128)(2,1)S(1)}, bf16[1,336,896]{2,1,0:T(8,128)(2,1)}, u32[]{:S(2)}, u32[]{:S(2)}) collective-permute-start(bf16[1,336,896]{2,1,0:T(8,128)(2,1)S(1)} %slice_select_fusion), channel_id=1, source_target_pairs={{0,8},{4,12},{8,0},{12,4},{1,9},{5,13},{9,1},{13,5},{2,10},{6,14},... | collective-permute-start | bytes 1806344 | tf_op jit(solution)/shard_map/ppermute | solution.py:407
  181.2 27.0 %collective-permute-start.24 = (bf16[1,336,896]{2,1,0:T(8,128)(2,1)S(1)}, bf16[1,336,896]{2,1,0:T(8,128)(2,1)}, u32[]{:S(2)}, u32[]{:S(2)}) collective-permute-start(bf16[1,336,896]{2,1,0:T(8,128)(2,1)S(1)} %slice_select_fusion), channel_id=1, source_target_pairs={{0,4},{4,0},{8,12},{12,8},{1,5},{5,1},{9,13},{13,9},{2,6},{6,2},{1... | collective-permute-start | bytes 1806344 | tf_op jit(solution)/shard_map/ppermute | solution.py:407
  183.0 18.3 %collective-permute-start.23 = (bf16[112,896]{1,0:T(8,128)(2,1)S(1)}, bf16[112,896]{1,0:T(8,128)(2,1)S(1)}, u32[]{:S(2)}, u32[]{:S(2)}) collective-permute-start(bf16[112,896]{1,0:T(8,128)(2,1)S(1)} %get-tuple-element.24), channel_id=1, source_target_pairs={{0,1},{1,0},{2,3},{3,2},{4,5},{5,4},{6,7},{7,6},{8,9},{9,8},{10,11... | collective-permute-start | bytes 602120 | tf_op jit(solution)/shard_map/ppermute | solution.py:407
  202.5 0.9 copy-start.19
  204.4 3.7 %copy-start.14 = (bf16[1,336,896]{2,1,0:T(8,128)(2,1)}, bf16[1,336,896]{2,1,0:T(8,128)(2,1)S(1)}, u32[]{:S(2)}) copy-start(bf16[1,336,896]{2,1,0:T(8,128)(2,1)S(1)} %collective-permute-done.26) | copy-start | bytes 1806340
  208.2 2.2 copy-start.21
  208.2 5.9 %copy-start.16 = (f32[3,3,448]{2,1,0:T(4,128)S(1)}, f32[3,3,448]{2,1,0:T(4,128)}, u32[]{:S(2)}) copy-start(f32[3,3,448]{2,1,0:T(4,128)} %param.27) | copy-start | bytes 48388
  210.3 24.4 %copy-start.11 = (bf16[4,1,336,896]{3,2,1,0:T(8,128)(2,1)}, bf16[4,1,336,896]{3,2,1,0:T(8,128)(2,1)S(1)}, u32[]{:S(2)}) copy-start(bf16[4,1,336,896]{3,2,1,0:T(8,128)(2,1)S(1)} %maximum_select_fusion.2.near_ref) | copy-start | bytes 7225348
  210.3 24.4 %collective-permute-start.27 = (bf16[4,1,336,896]{3,2,1,0:T(8,128)(2,1)S(1)}, bf16[4,1,336,896]{3,2,1,0:T(8,128)(2,1)}, u32[]{:S(2)}, u32[]{:S(2)}) collective-permute-start(bf16[4,1,336,896]{3,2,1,0:T(8,128)(2,1)S(1)} %maximum_select_fusion.2.near_ref), channel_id=1, source_target_pairs={{0,16},{16,0},{1,17},{17,1},{2,18},{18,2},{3,19},{19,3},{4,20},{20... | collective-permute-start | bytes 7225352 | tf_op jit(solution)/shard_map/ppermute | solution.py:407
  210.4 22.3 %collective-permute-start.20 = (bf16[80,1792]{1,0:T(8,128)(2,1)S(1)}, bf16[80,1792]{1,0:T(8,128)(2,1)}, u32[]{:S(2)}, u32[]{:S(2)}) collective-permute-start(bf16[80,1792]{1,0:T(8,128)(2,1)S(1)} %copy-done.21), channel_id=1, source_target_pairs={{0,4},{4,8},{8,12},{1,5},{5,9},{9,13},{2,6},{6,10},{10,14},{3,7},{... | collective-permute-start | bytes 860168 | tf_op jit(solution)/shard_map/ppermute | solution.py:629
  214.9 9.3 %collective-permute-start.28 = (f32[3,1536]{1,0:T(4,128)S(1)}, f32[3,1536]{1,0:T(4,128)S(1)}, u32[]{:S(2)}, u32[]{:S(2)}) collective-permute-start(f32[3,1536]{1,0:T(4,128)S(1)} %reshape.480), channel_id=1, source_target_pairs={{0,2},{1,3},{2,0},{3,1},{4,6},{5,7},{6,4},{7,5},{8,10},{9,11},{10,... | collective-permute-start | bytes 55304 | tf_op jit(solution)/shard_map/ppermute | solution.py:407
  216.7 18.0 %collective-permute-start.30 = (bf16[80,1792]{1,0:T(8,128)(2,1)S(1)}, bf16[80,1792]{1,0:T(8,128)(2,1)S(1)}, u32[]{:S(2)}, u32[]{:S(2)}) collective-permute-start(bf16[80,1792]{1,0:T(8,128)(2,1)S(1)} %copy-done.21), channel_id=1, source_target_pairs={{0,5},{1,4},{2,7},{3,6},{4,9},{5,8},{6,11},{7,10},{8,13},{9,12},{1... | collective-permute-start | bytes 860168 | tf_op jit(solution)/shard_map/ppermute | solution.py:631
  219.4 13.2 %collective-permute-start.29 = (bf16[64,1792]{1,0:T(8,128)(2,1)}, bf16[64,1792]{1,0:T(8,128)(2,1)S(1)}, u32[]{:S(2)}, u32[]{:S(2)}) collective-permute-start(bf16[64,1792]{1,0:T(8,128)(2,1)} %get-tuple-element.16.high_ref), channel_id=1, source_target_pairs={{0,1},{1,0},{2,3},{3,2},{4,5},{5,4},{6,7},{7,6},{8,9},{9,8},{10,11... | collective-permute-start | bytes 688136 | tf_op jit(solution)/shard_map/ppermute | solution.py:407
  224.1 27.4 %collective-permute-start.34 = (bf16[3,112,896]{2,1,0:T(8,128)(2,1)}, bf16[3,112,896]{2,1,0:T(8,128)(2,1)}, u32[]{:S(2)}, u32[]{:S(2)}) collective-permute-start(bf16[3,112,896]{2,1,0:T(8,128)(2,1)} %broadcast_select_fusion.1), channel_id=1, source_target_pairs={{0,12},{4,8},{8,4},{12,0},{1,13},{5,9},{9,5},{13,1},{2,14},{6,10},... | collective-permute-start | bytes 1806344 | tf_op jit(solution)/shard_map/ppermute | solution.py:407
  232.7 2.0 copy-start.23
  232.7 20.7 %collective-permute-start.33 = (bf16[3,112,896]{2,1,0:T(8,128)(2,1)}, bf16[3,112,896]{2,1,0:T(8,128)(2,1)}, u32[]{:S(2)}, u32[]{:S(2)}) collective-permute-start(bf16[3,112,896]{2,1,0:T(8,128)(2,1)} %broadcast_select_fusion.1), channel_id=1, source_target_pairs={{0,8},{4,12},{8,0},{12,4},{1,9},{5,13},{9,1},{13,5},{2,10},{6,14},... | collective-permute-start | bytes 1806344 | tf_op jit(solution)/shard_map/ppermute | solution.py:407
  232.7 21.8 %collective-permute-start.32 = (bf16[3,112,896]{2,1,0:T(8,128)(2,1)}, bf16[3,112,896]{2,1,0:T(8,128)(2,1)}, u32[]{:S(2)}, u32[]{:S(2)}) collective-permute-start(bf16[3,112,896]{2,1,0:T(8,128)(2,1)} %broadcast_select_fusion.1), channel_id=1, source_target_pairs={{0,4},{4,0},{8,12},{12,8},{1,5},{5,1},{9,13},{13,9},{2,6},{6,2},{1... | collective-permute-start | bytes 1806344 | tf_op jit(solution)/shard_map/ppermute | solution.py:407
  234.7 0.7 copy-start.22
  254.5 2.2 copy-start.20
  254.5 4.0 %copy-start.24 = (s32[8]{0:T(128)S(1)}, s32[8]{0:T(128)}, u32[]{:S(2)}) copy-start(s32[8]{0:T(128)} %param.20) | copy-start | bytes 100
  254.5 4.0 %copy-start.25 = (s32[8]{0:T(128)S(1)}, s32[8]{0:T(128)}, u32[]{:S(2)}) copy-start(s32[8]{0:T(128)} %param.19) | copy-start | bytes 100
  256.6 17.7 %copy-start.3 = (bf16[4,3,112,896]{3,2,1,0:T(8,128)(2,1)}, bf16[4,3,112,896]{3,2,1,0:T(8,128)(2,1)S(1)}, u32[]{:S(2)}) copy-start(bf16[4,3,112,896]{3,2,1,0:T(8,128)(2,1)S(1)} %maximum_select_fusion.3.near_ref) | copy-start | bytes 7225348
  256.6 17.7 %collective-permute-start.35 = (bf16[4,3,112,896]{3,2,1,0:T(8,128)(2,1)S(1)}, bf16[4,3,112,896]{3,2,1,0:T(8,128)(2,1)}, u32[]{:S(2)}, u32[]{:S(2)}) collective-permute-start(bf16[4,3,112,896]{3,2,1,0:T(8,128)(2,1)S(1)} %maximum_select_fusion.3.near_ref), channel_id=1, source_target_pairs={{0,16},{16,0},{1,17},{17,1},{2,18},{18,2},{3,19},{19,3},{4,20},{20... | collective-permute-start | bytes 7225352 | tf_op jit(solution)/shard_map/ppermute | solution.py:407
  256.7 17.6 %collective-permute-start.31 = (bf16[2,256,512]{2,1,0:T(8,128)(2,1)S(1)}, bf16[2,256,512]{2,1,0:T(8,128)(2,1)S(1)}, u32[]{:S(2)}, u32[]{:S(2)}) collective-permute-start(bf16[2,256,512]{2,1,0:T(8,128)(2,1)S(1)} %copy-done.20), channel_id=1, source_target_pairs={{0,1},{1,0},{2,3},{3,2},{4,5},{5,4},{6,7},{7,6},{8,9},{9,8},{10,11... | collective-permute-start | bytes 1572872 | tf_op jit(solution)/shard_map/ppermute | solution.py:407
  274.3 0.8 copy-start.15
  282.0 29.1 %copy-start.1 = (bf16[64,4,1792]{2,1,0:T(4,128)(2,1)S(1)}, bf16[64,4,1792]{2,1,0:T(4,128)(2,1)}, u32[]{:S(2)}) copy-start(bf16[64,4,1792]{2,1,0:T(4,128)(2,1)} %param.17) | copy-start | bytes 2752516

commit v9 on v8

--- a/solution.py
+++ b/solution.py
@@ -60,21 +60,26 @@
     return (dot(rows, first) + ones[0:1]) * (dot(rows, second) + ones[1:2])
 
 
-def run_copies(copies_of, groups, meanwhile=None):
+def run_copies(copies_of, groups, loads, meanwhile=None):
     step = pl.program_id(0)
 
     @pl.when(step == 0)
     def _():
+        for copy, _ in loads:
+            copy.start()
         for group in range(groups):
             for copy in copies_of(group):
                 copy.start()
-        if meanwhile is not None:
-            meanwhile()
 
     for group in range(groups):
 
         @pl.when(step == group)
         def _(group=group):
+            for copy, at in loads:
+                if at == group:
+                    copy.wait()
+            if meanwhile is not None and group == 0:
+                meanwhile()
             for copy in copies_of(group):
                 copy.wait()
 
@@ -136,6 +141,7 @@
     num_ref,
     q_ref,
     state_ref,
+    tokens_ref,
     normed_ref,
     value_w_ref,
     feat_w_ref,
@@ -149,16 +155,20 @@
     ]
     pieces = [(HEAD, value_w_ref, 0), (2 * feature_dim, feat_w_ref, 0)]
 
+    groups = value_w_ref.shape[0]
+
     @pl.when(step == 0)
     def _():
         zero_between_heads(value_w_ref)
 
+    def normalize():
+        normed_ref[...] = normed_rows(tokens_ref[...].astype(F32), gain_ref[...])
+
     run_copies(
         functools.partial(weight_copies, place_ref, near_ref, far_ref, targets, pieces, sems),
-        value_w_ref.shape[0],
-        lambda: normed_ref.__setitem__(
-            ..., normed_rows(x_ref[...].astype(F32), gain_ref[...])
-        ),
+        groups,
+        [(pltpu.make_async_copy(x_ref, tokens_ref, sems.at[groups, 0]), 0)],
+        normalize,
     )
     rows = x_ref.shape[0]
     width = 2 * heads * feature_dim
@@ -208,18 +218,21 @@
     low_ref,
     high_ref,
     tail_ref,
+    tokens_ref,
     total_ref,
     mixed_ref,
     w_ref,
     sems,
 ):
     step = pl.program_id(0)
+    groups = w_ref.shape[0]
 
     @pl.when(step == 0)
     def _():
         total_ref[...] = jnp.zeros_like(total_ref)
         zero_between_heads(w_ref)
 
+    loads = [(pltpu.make_async_copy(x_ref, tokens_ref, sems.at[groups, 0]), groups - 1)]
     run_copies(
         functools.partial(
             weight_copies,
@@ -230,7 +243,8 @@
             [(HEAD, w_ref, 0)],
             sems,
         ),
-        w_ref.shape[0],
+        groups,
+        loads,
     )
 
     query_features = features(q_ref[0], first_ref[...], second_ref[...], ones_ref[...])
@@ -246,7 +260,7 @@
 
     @pl.when(step == pl.num_programs(0) - 1)
     def _():
-        residual = (x_ref[...].astype(F32) + total_ref[...]).astype(BF16)
+        residual = (tokens_ref[...].astype(F32) + total_ref[...]).astype(BF16)
         residual_ref[...] = residual
         normed = normed_rows(residual.astype(F32), gain_ref[...])
         mid = low_ref.shape[0]
@@ -277,10 +291,11 @@
     pieces = [(HEAD, w_ref, kind * SLOT) for kind in range(3)]
     mid = low_ref.shape[0]
 
-    def place_rows():
-        rows_ref[:HALO] = halo_ref[...]
-        rows_ref[HALO : HALO + mid] = low_ref[...]
-        rows_ref[HALO + mid :] = high_ref[...]
+    groups = w_ref.shape[0]
+    loads = [
+        (pltpu.make_async_copy(src, rows_ref.at[at : at + src.shape[0], :], sems.at[groups, n]), 0)
+        for n, (src, at) in enumerate(((halo_ref, 0), (low_ref, HALO), (high_ref, HALO + mid)))
+    ]
 
     @pl.when(step == 0)
     def _():
@@ -288,8 +303,8 @@
 
     run_copies(
         functools.partial(weight_copies, place_ref, near_ref, far_ref, targets, pieces, sems),
-        w_ref.shape[0],
-        place_rows,
+        groups,
+        loads,
     )
     rows = mid + high_ref.shape[0]
     lead = HALO - WINDOW
@@ -331,11 +346,19 @@
     far_ref,
     residual_ref,
     out_ref,
+    mixed_all_ref,
+    rows_ref,
     total_ref,
     w_ref,
     sems,
 ):
     step = pl.program_id(0)
+    groups = w_ref.shape[0]
+    loads = [
+        (pltpu.make_async_copy(mixed_ref, mixed_all_ref.at[:2], sems.at[groups, 0]), 0),
+        (pltpu.make_async_copy(pair_ref, mixed_all_ref.at[2:], sems.at[groups, 1]), 2),
+        (pltpu.make_async_copy(residual_ref, rows_ref, sems.at[groups, 2]), groups - 1),
+    ]
 
     @pl.when(step == 0)
     def _():
@@ -352,14 +375,14 @@
             [(HEAD, w_ref, 0)],
             sems,
         ),
-        w_ref.shape[0],
-    )
-    mixed = jnp.where(step < 2, mixed_ref[step % 2], pair_ref[step % 2])
-    add_branch(mixed, w_ref, total_ref)
+        groups,
+        loads,
+    )
+    add_branch(mixed_all_ref[step], w_ref, total_ref)
 
     @pl.when(step == pl.num_programs(0) - 1)
     def _():
-        result = (residual_ref[...].astype(F32) + total_ref[...]).astype(BF16)
+        result = (rows_ref[...].astype(F32) + total_ref[...]).astype(BF16)
         row = lax.broadcasted_iota(jnp.int32, result.shape, 0)
         out_ref[...] = jnp.where(row < live_ref[0], result, jnp.zeros_like(result))
 
@@ -376,7 +399,7 @@
 HBM = pl.BlockSpec(memory_space=pl.ANY)
 
 
-def call(kernel, groups, in_specs, out_specs, out_shape, scratch, name, flops=0):
+def call(kernel, groups, in_specs, out_specs, out_shape, scratch, name):
     return pl.pallas_call(
         kernel,
         grid=(groups,),
@@ -387,7 +410,7 @@
         compiler_params=pltpu.CompilerParams(
             dimension_semantics=("arbitrary",), vmem_limit_bytes=VMEM
         ),
-        cost_estimate=pl.CostEstimate(flops=flops, bytes_accessed=0, transcendentals=0),
+        cost_estimate=pl.CostEstimate(flops=0, bytes_accessed=0, transcendentals=0),
         name=name,
     )
 
@@ -456,10 +479,10 @@
             lax.ppermute(state, axis, [(i, i + by) for i in range(peers - by)])
             for by in range(1, peers)
         ]
-        return sum(one.astype(F32) for one in found), found[0]
+        return sum(one.astype(F32) for one in found)
     everything = lax.all_gather(state, axis).astype(F32)
     reached = jnp.arange(peers) < lax.axis_index(axis)
-    return jnp.sum(jnp.where(reached[:, None, None, None], everything, 0.0), axis=0), state
+    return jnp.sum(jnp.where(reached[:, None, None, None], everything, 0.0), axis=0)
 
 
 def on_device(
@@ -549,7 +572,7 @@
     column[0, HEAD::SLOT] = 1
 
     def copy_sems(kinds):
-        return pltpu.SemaphoreType.DMA((group_count, NEAR * kinds))
+        return pltpu.SemaphoreType.DMA((group_count + 1, NEAR * kinds))
 
     def weights_of(rows_of_head):
         return pltpu.VMEM((group_count, heads, rows_of_head, width), BF16)
@@ -561,7 +584,7 @@
         group_count,
         [
             SMEM,
-            whole((rows, width)),
+            HBM,
             whole((1, width)),
             *[HBM] * 4,
             whole(first.shape),
@@ -577,6 +600,7 @@
         ],
         [
             pltpu.VMEM((rows, width), BF16),
+            pltpu.VMEM((rows, width), BF16),
             weights_of(SLOT),
             weights_of(2 * feature_dim),
             copy_sems(3),
@@ -585,13 +609,14 @@
     )(
         places, tokens, gain_one[None], values_t, featmap_t, *near_one, first, second, ones, column
     )
-    prior, first_arrived = earlier_blocks(state, "seq")
-    prior = settled(prior)
-    beyond = after(beyond, (first_arrived,))
+    prior = settled(earlier_blocks(state, "seq"))
+    beyond = after(beyond, (state,))
     held_window, out_beyond = beyond[:, : 3 * HEAD], beyond[0, 3 * HEAD :]
     held_out_two = [out_beyond, across(out_piece, "tensor", 1), across(out_beyond, "tensor", 1)]
-    held_out_two = settled(jnp.stack(held_out_two))
-    near_out_one = from_plane(held_out_one, neighbours(held_out_one), (state,), (prior, beyond))
+    held_out_two = settled(jnp.stack(held_out_two), (prior,))
+    near_out_one = from_plane(
+        held_out_one, neighbours(held_out_one), (state,), (beyond, held_out_two)
+    )
     held_window = after(held_window, (prior,))
     near_by_window = neighbours(held_window)
     residual, low, high, tail = call(
@@ -607,14 +632,12 @@
             whole(scale.shape),
         ]
         + [each((heads * kept, SLOT))]
-        + [HBM] * 3
-        + [
-            whole((rows, width)),
-            whole((1, width)),
-        ],
+        + [HBM] * 4
+        + [whole((1, width))],
         [whole((n, width)) for n in (rows, mid, rows - mid, HALO)],
         [jax.ShapeDtypeStruct((n, width), BF16) for n in (rows, mid, rows - mid, HALO)],
         [
+            pltpu.VMEM((rows, width), BF16),
             pltpu.VMEM((rows, width), F32),
             pltpu.VMEM((rows, slots), BF16),
             weights_of(SLOT),
@@ -637,7 +660,7 @@
             for j in range(group_count)
         ],
     )
-    near_window = from_plane(held_window, near_by_window, None, (pair_low, held_out_two))
+    near_window = from_plane(held_window, near_by_window, (residual,), (pair_low, pair_halo))
     held_out_two = after(held_out_two, (residual,))
     block_start = (seq_place * rows).astype(jnp.int32)[None]
 
@@ -648,10 +671,7 @@
             [
                 SMEM,
                 SMEM,
-                whole((mid, width)),
-                whole((rows - mid, width)),
-                whole((HALO, width)),
-                *[HBM] * 3,
+                *[HBM] * 6,
                 each((tap_count, 3 * slots)),
                 HBM,
             ],
@@ -663,7 +683,6 @@
                 copy_sems(3),
             ],
             "window_rows",
-            6 * rows * width * 3 * head_cols,
         )(places, block_start, slot_low, slot_high, slot_halo, window_t, *near_window, taps, earlier)
 
     mixed_pair = window_rows(pair_low, pair_high, pair_halo, halo)
@@ -677,14 +696,13 @@
         [
             SMEM,
             SMEM,
-            whole((2, rows, slots)),
-            whole((2, rows, slots)),
-            *[HBM] * 3,
-            whole((rows, width)),
+            *[HBM] * 6,
         ],
         whole((rows, width)),
         jax.ShapeDtypeStruct((rows, width), BF16),
         [
+            pltpu.VMEM((group_count, rows, slots), BF16),
+            pltpu.VMEM((rows, width), BF16),
             pltpu.VMEM((rows, width), F32),
             weights_of(SLOT),
             copy_sems(1),

time: 312 us -> 320 us (1.026)
  starting transfers between devices: 54.4 us -> 59 us
    ppermute x31 -> x32, waiting for transfers between devices: 68.6 us -> 44 us  [across(): lax.ppermute(array, axis, [(i, i ^ bit) for i in range(lax.axis_size(axis...]
    ppermute x1, waiting for transfers between devices: 0.01 us -> 22 us  [on_device(): halo = lax.ppermute(tail, 'seq', [(i, i + 1) for i in range(seq_count - 1)])]
    ppermute x1, waiting for transfers between devices: 0.01 us -> 14.1 us  [on_device(): lax.ppermute(tail, ('seq', 'tensor'), [(i * group_count + j, (i + 1) * gr...]
    ppermute x3, waiting for transfers between devices: 20.7 us -> 7.7 us  [earlier_blocks(): lax.ppermute(state, axis, [(i, i + by) for i in range(peers - by)])]
    select_n x17 -> x20, other arithmetic: 16 us -> 19.8 us  [after(): return jnp.where(zero == 0.0, array, jnp.zeros_like(array))]
    ppermute x31 -> x32, starting transfers between devices: 29.3 us -> 30.8 us  [across(): lax.ppermute(array, axis, [(i, i ^ bit) for i in range(lax.axis_size(axis...]
  transfers between devices with their start and end apart: 38 -> 39, of which waited for: 14 -> 13; matrix products, arithmetic and copies ran while one was open for 11% -> 11% of each run, Pallas kernels for 17% -> 16%
where the time goes in v9:
time: 320 us; the launch traced here: 317 us
  waiting for transfers between devices  107 us (33%)
  starting transfers between devices  59 us (18%)
  Pallas kernels  57.7 us (18%)
  local copies, waits for them, and re-layouts  30.1 us (9%)
  other arithmetic  27.6 us (9%)
  blocking collectives  26.9 us (8%)
  between operations  9.24 us (3%)
    ppermute x32, waiting for transfers between devices, across(): lax.ppermute(array, axis, [(i, i ^ bit) for i in range(lax.axis_size(axis...  44 us
    ppermute x32, starting transfers between devices, across(): lax.ppermute(array, axis, [(i, i ^ bit) for i in range(lax.axis_size(axis...  30.8 us
    pallas_call x2, Pallas kernels, window_rows(): call(functools.partial(window_kernel, heads), 2, [SMEM, SMEM, *[HBM] * 6,...  28.2 us
    all_to_all x1, blocking collectives, on_device(): lax.all_to_all(result, 'tensor', split_axis=0, concat_axis=0, tiled=True)  26.9 us
    ppermute x1, waiting for transfers between devices, on_device(): halo = lax.ppermute(tail, 'seq', [(i, i + 1) for i in range(seq_count - 1)])  22 us
    select_n x20, other arithmetic, after(): return jnp.where(zero == 0.0, array, jnp.zeros_like(array))  19.8 us
    all_to_all x1, waiting for transfers between devices, on_device(): lax.all_to_all(picked, 'tensor', split_axis=0, concat_axis=0, tiled=True)  18.9 us
    ppermute x1, waiting for transfers between devices, on_device(): lax.ppermute(tail, ('seq', 'tensor'), [(i * group_count + j, (i + 1) * gr...  14.1 us
  transfers between devices with their start and end apart: 39, of which 13 were waited for; matrix products, arithmetic and copies ran while one was open for 11% of the time, Pallas kernels for 16%

profile of v9, /device:TPU:0, one launch (start us, length us, event | category | flops | bytes accessed | tf_op | source)
XLA Modules:
  0.0 317.2 jit_solution(14590389294168233790)
XLA Ops:
  2.5 2.2 gather_fusion
  4.7 5.2 %all-to-all-start = ((bf16[8,8,4,1792]{3,2,1,0:T(4,128)(2,1)}), bf16[8,8,4,1792]{3,2,1,0:T(4,128)(2,1)S(1)}, u32[]{:S(2)}, u32[]{:S(2)}) async-start(bf16[8,8,4,1792]{3,2,1,0:T(4,128)(2,1)} %bitcast.15), calls=%async_computation | async-start | bytes 1835008 | tf_op jit(solution)/shard_map/all_to_all | solution.py:545
  11.6 2.7 collective-permute-start.1
  14.3 1.6 collective-permute-start
  16.1 10.7 %collective-permute-done.1 = bf16[144,896]{1,0:T(8,128)(2,1)S(1)} collective-permute-done((bf16[144,896]{1,0:T(8,128)(2,1)S(1)}, bf16[144,896]{1,0:T(8,128)(2,1)S(1)}, u32[]{:S(2)}, u32[]{:S(2)}) %collective-permute-start.1) | collective-permute-done | bytes 258080 | tf_op jit(solution)/shard_map/ppermute | solution.py:430
  27.5 7.2 %collective-permute-done.2 = bf16[144,896]{1,0:T(8,128)(2,1)S(1)} collective-permute-done((bf16[144,896]{1,0:T(8,128)(2,1)S(1)}, bf16[144,896]{1,0:T(8,128)(2,1)S(1)}, u32[]{:S(2)}, u32[]{:S(2)}) %collective-permute-start.2) | collective-permute-done | bytes 258080 | tf_op jit(solution)/shard_map/ppermute | solution.py:430
  36.0 1.4 gather_fusion.1
  37.9 1.0 copy.44
  38.9 5.1 %all-to-all-start.1 = ((bf16[4,16,4,1792]{3,1,2,0:T(8,128)(2,1)}), bf16[4,16,4,1792]{3,1,2,0:T(8,128)(2,1)S(1)}, u32[]{:S(2)}, u32[]{:S(2)}) async-start(bf16[4,16,4,1792]{3,1,2,0:T(8,128)(2,1)} %copy.44), calls=%async_computation.1 | async-start | bytes 1835008 | tf_op jit(solution)/shard_map/all_to_all | solution.py:552
  43.9 1.6 collective-permute-start.7
  45.5 1.5 collective-permute-start.6
  48.2 1.6 select_bitcast_fusion.1
  49.8 2.9 collective-permute-start.4
  52.7 18.9 %all-to-all-done.1 = bf16[4,16,4,1792]{3,1,2,0:T(8,128)(2,1)S(1)} async-done(((bf16[4,16,4,1792]{3,1,2,0:T(8,128)(2,1)}), bf16[4,16,4,1792]{3,1,2,0:T(8,128)(2,1)S(1)}, u32[]{:S(2)}, u32[]{:S(2)}) %all-to-all-start.1) | async-done | bytes 917536 | tf_op jit(solution)/shard_map/all_to_all | solution.py:552
  72.9 1.7 collective-permute-start.8
  74.5 1.0 slice_select_fusion.3
  75.5 1.5 collective-permute-start.9
  77.1 2.0 collective-permute-start.5
  79.1 4.7 %collective-permute-done.3 = bf16[112,896]{1,0:T(8,128)(2,1)S(1)} collective-permute-done((bf16[112,896]{1,0:T(8,128)(2,1)}, bf16[112,896]{1,0:T(8,128)(2,1)S(1)}, u32[]{:S(2)}, u32[]{:S(2)}) %collective-permute-start.3) | collective-permute-done | bytes 200736 | tf_op jit(solution)/shard_map/ppermute | solution.py:430
  83.8 2.1 collective-permute-done.5
  85.9 1.8 pad_maximum_fusion.1
  87.7 1.3 slice.101
  89.9 1.7 maximum_select_fusion.near_ref
  91.7 2.1 constant_dynamic-slice_fusion
  94.8 1.0 maximum_select_fusion.4
  98.3 1.4 copy.45
  99.7 2.4 reshape.531.x_ref
  102.1 12.4 %linear_rows.1 = (f32[4,256,512]{2,1,0:T(8,128)}, bf16[4,256,128]{2,1,0:T(8,128)(2,1)}, bf16[4,640,128]{2,1,0:T(8,128)(2,1)}) custom-call(s32[5]{0:T(128)} %pad_add_fusion.place_ref, bf16[256,1792]{1,0:T(8,128)(2,1)} %reshape.531.x_ref, f32[1,1792]{1,0:T(1,128)} %broadcast_in_dim.131.gain_ref, bf16[1,4,112,1792]{3,2,1,0:T(8,128)(2,1)} %bitcast.98, ...), custom_call_target="tpu_custom_call" | custom-call | tf_op jit(solution)/shard_map/linear_rows/pallas_call | solution.py:582
  114.5 4.5 %collective-permute-start.13 = (bf16[4,640,128]{2,1,0:T(8,128)(2,1)}, bf16[4,640,128]{2,1,0:T(8,128)(2,1)S(1)}, u32[]{:S(2)}, u32[]{:S(2)}) collective-permute-start(bf16[4,640,128]{2,1,0:T(8,128)(2,1)} %get-tuple-element.14), channel_id=1, source_target_pairs={{0,12},{1,13},{2,14},{3,15},{16,28},{17,29},{18,30},{19,31}} | collective-permute-start | bytes 1966088 | tf_op jit(solution)/shard_map/ppermute | solution.py:479
  119.0 1.3 collective-permute-start.12
  120.3 1.3 slice.79
  122.3 11.0 %collective-permute-done.14 = bf16[448,896]{1,0:T(8,128)(2,1)} collective-permute-done((bf16[448,896]{1,0:T(8,128)(2,1)}, bf16[448,896]{1,0:T(8,128)(2,1)}, u32[]{:S(2)}, u32[]{:S(2)}) %collective-permute-start.14) | collective-permute-done | bytes 802848 | tf_op jit(solution)/shard_map/ppermute | solution.py:430
  133.3 2.7 collective-permute-start.11
  136.0 1.2 select_bitcast_fusion
  139.3 1.0 slice_select_fusion.2
  140.4 1.1 collective-permute-start.19
  141.5 2.0 collective-permute-start.16
  143.5 7.7 %collective-permute-done.11 = bf16[4,640,128]{2,1,0:T(8,128)(2,1)S(1)} collective-permute-done((bf16[4,640,128]{2,1,0:T(8,128)(2,1)}, bf16[4,640,128]{2,1,0:T(8,128)(2,1)S(1)}, u32[]{:S(2)}, u32[]{:S(2)}) %collective-permute-start.11) | collective-permute-done | bytes 655392 | tf_op jit(solution)/shard_map/ppermute | solution.py:479
  154.6 2.0 collective-permute-done.20
  156.6 2.9 collective-permute-done.19
  159.6 1.9 maximum_select_fusion.1.near_ref
  161.6 1.0 slice_select_fusion
  164.2 2.0 collective-permute-done.21.far_ref
  166.2 1.5 copy-done.11
  167.7 10.4 %linear_out.1 = (bf16[256,1792]{1,0:T(8,128)(2,1)}, bf16[192,1792]{1,0:T(8,128)(2,1)}, bf16[64,1792]{1,0:T(8,128)(2,1)}, bf16[80,1792]{1,0:T(8,128)(2,1)}) custom-call(s32[5]{0:T(128)} %pad_add_fusion.place_ref, f32[4,256,512]{2,1,0:T(8,128)} %get-tuple-element.12.num_ref, bf16[4,256,128]{2,1,0:T(8,128)(2,1)} %get-tuple-element.13.q_ref, ...), custom_call_target="tpu_custom_call" | custom-call | tf_op jit(solution)/shard_map/linear_out/pallas_call | solution.py:622
  178.1 1.2 slice.89
  180.0 1.0 slice_select_fusion.4
  181.6 4.9 %collective-permute-start.24 = (bf16[80,1792]{1,0:T(8,128)(2,1)}, bf16[80,1792]{1,0:T(8,128)(2,1)S(1)}, u32[]{:S(2)}, u32[]{:S(2)}) collective-permute-start(bf16[80,1792]{1,0:T(8,128)(2,1)} %get-tuple-element.17), channel_id=1, source_target_pairs={{0,5},{1,4},{2,7},{3,6},{4,9},{5,8},{6,11},{7,10},{8,13},{9,12},{1... | collective-permute-start | bytes 860168 | tf_op jit(solution)/shard_map/ppermute | solution.py:654
  186.4 1.0 slice_select_fusion.5
  187.6 14.1 %collective-permute-done.24.halo_ref = bf16[80,1792]{1,0:T(8,128)(2,1)S(1)} collective-permute-done((bf16[80,1792]{1,0:T(8,128)(2,1)}, bf16[80,1792]{1,0:T(8,128)(2,1)S(1)}, u32[]{:S(2)}, u32[]{:S(2)}) %collective-permute-start.24) | collective-permute-done | bytes 286752 | tf_op jit(solution)/shard_map/ppermute | solution.py:654
  204.1 1.7 maximum_select_fusion.2.near_ref
  206.7 1.8 collective-permute-start.30
  209.8 2.6 collective-permute-start.35
  212.4 2.4 collective-permute-start.34
  215.2 1.3 collective-permute-done.31.high_ref
  216.5 4.7 %collective-permute-start.22 = (bf16[80,1792]{1,0:T(8,128)(2,1)}, bf16[80,1792]{1,0:T(8,128)(2,1)S(1)}, u32[]{:S(2)}, u32[]{:S(2)}) collective-permute-start(bf16[80,1792]{1,0:T(8,128)(2,1)} %get-tuple-element.17), channel_id=1, source_target_pairs={{0,4},{4,8},{8,12},{1,5},{5,9},{9,13},{2,6},{6,10},{10,14},{3,7},{... | collective-permute-start | bytes 860168 | tf_op jit(solution)/shard_map/ppermute | solution.py:652
  222.7 22.0 %collective-permute-done.22._.halo_ref = bf16[80,1792]{1,0:T(8,128)(2,1)S(1)} collective-permute-done((bf16[80,1792]{1,0:T(8,128)(2,1)}, bf16[80,1792]{1,0:T(8,128)(2,1)S(1)}, u32[]{:S(2)}, u32[]{:S(2)}) %collective-permute-start.22) | collective-permute-done | bytes 286752 | tf_op jit(solution)/shard_map/ppermute | solution.py:652
  245.5 14.1 %window_rows.2._ = bf16[2,256,512]{2,1,0:T(8,128)(2,1)} custom-call(s32[5]{0:T(128)} %pad_add_fusion.place_ref, s32[1]{0:T(128)} %bitcast.2.first_ref, bf16[192,1792]{1,0:T(8,128)(2,1)} %copy-done.16, bf16[64,1792]{1,0:T(8,128)(2,1)} %copy-done.20, bf16[80,1792]{1,0:T(8,128)(2,1)} %copy-done.18, bf16[3,4,112,1792]{3,2,1,0:T(8,128)(2,1)} %bitcast.88, ...), custom_call_target="tpu_custom_call" | custom-call | tf_op jit(solution)/shard_map/window_rows/pallas_call | solution.py:668
  259.6 1.2 slice.116
  261.6 1.9 maximum_select_fusion.3.near_ref
  265.6 14.1 %window_rows.3.mixed_ref = bf16[2,256,512]{2,1,0:T(8,128)(2,1)} custom-call(s32[5]{0:T(128)} %pad_add_fusion.place_ref, s32[1]{0:T(128)} %bitcast.2.first_ref, bf16[192,1792]{1,0:T(8,128)(2,1)} %get-tuple-element.15.low_ref, bf16[64,1792]{1,0:T(8,128)(2,1)} %get-tuple-element.16.high_ref, bf16[80,1792]{1,0:T(8,128)(2,1)} %copy-done.15, ...), custom_call_target="tpu_custom_call" | custom-call | tf_op jit(solution)/shard_map/window_rows/pallas_call | solution.py:668
  280.5 6.7 %window_out.1 = bf16[256,1792]{1,0:T(8,128)(2,1)} custom-call(s32[5]{0:T(128)} %pad_add_fusion.place_ref, s32[1]{0:T(128)} %bitcast.1.live_ref, bf16[2,256,512]{2,1,0:T(8,128)(2,1)} %window_rows.3.mixed_ref, bf16[2,256,512]{2,1,0:T(8,128)(2,1)} %copy-done.17, bf16[1,4,112,1792]{3,2,1,0:T(8,128)(2,1)} %bitcast.102, bf16[4,3,112,896]{3,2,1,0:T(8,128)(2,1)} %copy-done.4, ...), custom_call_target="tpu_custom_call" | custom-call | tf_op jit(solution)/shard_map/window_out/pallas_call | solution.py:693
  287.2 1.9 reshape.539
  289.4 26.9 %all_to_all.15 = bf16[4,16,4,1792]{3,2,1,0:T(4,128)(2,1)S(1)} all-to-all(bf16[4,16,4,1792]{3,2,1,0:T(4,128)(2,1)S(1)} %bitcast.93), channel_id=1, replica_groups=mesh['dp'=2,'seq'=4,'tensor'=4] {'tensor'}, dimensions={0} | all-to-all | bytes 1835008 | tf_op jit(solution)/shard_map/all_to_all | solution.py:714
  (159 shorter events, 26.5 us)
Async XLA Ops:
  0.0 2.5 copy-start
  4.7 31.4 %all-to-all-start = ((bf16[8,8,4,1792]{3,2,1,0:T(4,128)(2,1)}), bf16[8,8,4,1792]{3,2,1,0:T(4,128)(2,1)S(1)}, u32[]{:S(2)}, u32[]{:S(2)}) async-start(bf16[8,8,4,1792]{3,2,1,0:T(4,128)(2,1)} %bitcast.15), calls=%async_computation | async-start | bytes 1835008 | tf_op jit(solution)/shard_map/all_to_all | solution.py:545
  11.6 15.2 %collective-permute-start.1 = (bf16[144,896]{1,0:T(8,128)(2,1)S(1)}, bf16[144,896]{1,0:T(8,128)(2,1)S(1)}, u32[]{:S(2)}, u32[]{:S(2)}) collective-permute-start(bf16[144,896]{1,0:T(8,128)(2,1)S(1)} %pad_maximum_fusion.2), channel_id=1, source_target_pairs={{0,2},{1,3},{2,0},{3,1},{4,6},{5,7},{6,4},{7,5},{8,10},{9,11},{10,... | collective-permute-start | bytes 774152 | tf_op jit(solution)/shard_map/ppermute | solution.py:430
  14.3 13.2 %collective-permute-start = (bf16[144,896]{1,0:T(8,128)(2,1)S(1)}, bf16[144,896]{1,0:T(8,128)(2,1)S(1)}, u32[]{:S(2)}, u32[]{:S(2)}) collective-permute-start(bf16[144,896]{1,0:T(8,128)(2,1)S(1)} %pad_maximum_fusion.2), channel_id=1, source_target_pairs={{0,1},{1,0},{2,3},{3,2},{4,5},{5,4},{6,7},{7,6},{8,9},{9,8},{10,11... | collective-permute-start | bytes 774152 | tf_op jit(solution)/shard_map/ppermute | solution.py:430
  26.9 7.8 %collective-permute-start.2 = (bf16[144,896]{1,0:T(8,128)(2,1)S(1)}, bf16[144,896]{1,0:T(8,128)(2,1)S(1)}, u32[]{:S(2)}, u32[]{:S(2)}) collective-permute-start(bf16[144,896]{1,0:T(8,128)(2,1)S(1)} %collective-permute-done.1), channel_id=1, source_target_pairs={{0,1},{1,0},{2,3},{3,2},{4,5},{5,4},{6,7},{7,6},{8,9},{9,8},{10,11... | collective-permute-start | bytes 774152 | tf_op jit(solution)/shard_map/ppermute | solution.py:430
  34.8 10.8 %copy-start.9 = (bf16[3,144,896]{2,1,0:T(8,128)(2,1)}, bf16[3,144,896]{2,1,0:T(8,128)(2,1)S(1)}, u32[]{:S(2)}) copy-start(bf16[3,144,896]{2,1,0:T(8,128)(2,1)S(1)} %pad_maximum_fusion) | copy-start | bytes 2322436
  38.9 32.7 %all-to-all-start.1 = ((bf16[4,16,4,1792]{3,1,2,0:T(8,128)(2,1)}), bf16[4,16,4,1792]{3,1,2,0:T(8,128)(2,1)S(1)}, u32[]{:S(2)}, u32[]{:S(2)}) async-start(bf16[4,16,4,1792]{3,1,2,0:T(8,128)(2,1)} %copy.44), calls=%async_computation.1 | async-start | bytes 1835008 | tf_op jit(solution)/shard_map/all_to_all | solution.py:552
  43.9 28.9 %collective-permute-start.7 = (bf16[3,144,896]{2,1,0:T(8,128)(2,1)S(1)}, bf16[3,144,896]{2,1,0:T(8,128)(2,1)S(1)}, u32[]{:S(2)}, u32[]{:S(2)}) collective-permute-start(bf16[3,144,896]{2,1,0:T(8,128)(2,1)S(1)} %pad_maximum_fusion), channel_id=1, source_target_pairs={{0,8},{4,12},{8,0},{12,4},{1,9},{5,13},{9,1},{13,5},{2,10},{6,14},... | collective-permute-start | bytes 2322440 | tf_op jit(solution)/shard_map/ppermute | solution.py:430
  45.5 29.0 %collective-permute-start.6 = (bf16[3,144,896]{2,1,0:T(8,128)(2,1)S(1)}, bf16[3,144,896]{2,1,0:T(8,128)(2,1)}, u32[]{:S(2)}, u32[]{:S(2)}) collective-permute-start(bf16[3,144,896]{2,1,0:T(8,128)(2,1)S(1)} %pad_maximum_fusion), channel_id=1, source_target_pairs={{0,4},{4,0},{8,12},{12,8},{1,5},{5,1},{9,13},{13,9},{2,6},{6,2},{1... | collective-permute-start | bytes 2322440 | tf_op jit(solution)/shard_map/ppermute | solution.py:430
  49.8 27.3 %collective-permute-start.4 = (bf16[112,896]{1,0:T(8,128)(2,1)}, bf16[112,896]{1,0:T(8,128)(2,1)}, u32[]{:S(2)}, u32[]{:S(2)}) collective-permute-start(bf16[112,896]{1,0:T(8,128)(2,1)} %select_bitcast_fusion.1), channel_id=1, source_target_pairs={{0,2},{1,3},{2,0},{3,1},{4,6},{5,7},{6,4},{7,5},{8,10},{9,11},{10,... | collective-permute-start | bytes 602120 | tf_op jit(solution)/shard_map/ppermute | solution.py:430
  71.6 18.3 %copy-start.7 = (bf16[4,16,4,1792]{3,1,2,0:T(8,128)(2,1)}, bf16[4,16,4,1792]{3,1,2,0:T(8,128)(2,1)S(1)}, u32[]{:S(2)}) copy-start(bf16[4,16,4,1792]{3,1,2,0:T(8,128)(2,1)S(1)} %all-to-all-done.1) | copy-start | bytes 2752516
  71.6 18.3 %copy-start.10 = (bf16[3,144,896]{2,1,0:T(8,128)(2,1)S(1)}, bf16[3,144,896]{2,1,0:T(8,128)(2,1)}, u32[]{:S(2)}) copy-start(bf16[3,144,896]{2,1,0:T(8,128)(2,1)} %copy-done.9) | copy-start | bytes 2322436
  72.8 17.1 %copy-start.14 = (bf16[3,144,896]{2,1,0:T(8,128)(2,1)}, bf16[3,144,896]{2,1,0:T(8,128)(2,1)S(1)}, u32[]{:S(2)}) copy-start(bf16[3,144,896]{2,1,0:T(8,128)(2,1)S(1)} %collective-permute-done.7) | copy-start | bytes 2322436
  72.9 16.8 %collective-permute-start.8 = (bf16[3,80,896]{2,1,0:T(8,128)(2,1)S(1)}, bf16[3,80,896]{2,1,0:T(8,128)(2,1)S(1)}, u32[]{:S(2)}, u32[]{:S(2)}) collective-permute-start(bf16[3,80,896]{2,1,0:T(8,128)(2,1)S(1)} %slice_select_fusion.1), channel_id=1, source_target_pairs={{0,4},{4,0},{8,12},{12,8},{1,5},{5,1},{9,13},{13,9},{2,6},{6,2},{1... | collective-permute-start | bytes 1290248 | tf_op jit(solution)/shard_map/ppermute | solution.py:430
  75.5 14.1 %collective-permute-start.9 = (bf16[3,64,896]{2,1,0:T(8,128)(2,1)S(1)}, bf16[3,64,896]{2,1,0:T(8,128)(2,1)S(1)}, u32[]{:S(2)}, u32[]{:S(2)}) collective-permute-start(bf16[3,64,896]{2,1,0:T(8,128)(2,1)S(1)} %slice_select_fusion.3), channel_id=1, source_target_pairs={{0,8},{4,12},{8,0},{12,4},{1,9},{5,13},{9,1},{13,5},{2,10},{6,14},... | collective-permute-start | bytes 1032200 | tf_op jit(solution)/shard_map/ppermute | solution.py:430
  77.1 6.7 %collective-permute-start.3 = (bf16[112,896]{1,0:T(8,128)(2,1)}, bf16[112,896]{1,0:T(8,128)(2,1)S(1)}, u32[]{:S(2)}, u32[]{:S(2)}) collective-permute-start(bf16[112,896]{1,0:T(8,128)(2,1)} %select_bitcast_fusion.1), channel_id=1, source_target_pairs={{0,1},{1,0},{2,3},{3,2},{4,5},{5,4},{6,7},{7,6},{8,9},{9,8},{10,11... | collective-permute-start | bytes 602120 | tf_op jit(solution)/shard_map/ppermute | solution.py:430
  77.1 8.8 %collective-permute-start.5 = (bf16[112,896]{1,0:T(8,128)(2,1)}, bf16[112,896]{1,0:T(8,128)(2,1)S(1)}, u32[]{:S(2)}, u32[]{:S(2)}) collective-permute-start(bf16[112,896]{1,0:T(8,128)(2,1)} %collective-permute-done.4), channel_id=1, source_target_pairs={{0,1},{1,0},{2,3},{3,2},{4,5},{5,4},{6,7},{7,6},{8,9},{9,8},{10,11... | collective-permute-start | bytes 602120 | tf_op jit(solution)/shard_map/ppermute | solution.py:430
  91.6 8.1 %copy-start.3 = (bf16[4,3,144,896]{3,2,1,0:T(8,128)(2,1)}, bf16[4,3,144,896]{3,2,1,0:T(8,128)(2,1)S(1)}, u32[]{:S(2)}) copy-start(bf16[4,3,144,896]{3,2,1,0:T(8,128)(2,1)S(1)} %maximum_select_fusion.near_ref) | copy-start | bytes 9289732
  91.6 4.5 %copy-start.22 = (f32[1792]{0:T(1024)S(1)}, f32[1792]{0:T(1024)}, u32[]{:S(2)}) copy-start(f32[1792]{0:T(1024)} %param.21) | copy-start | bytes 21508
  91.7 6.7 %copy-start.8 = (bf16[4,16,4,1792]{3,1,2,0:T(8,128)(2,1)S(1)}, bf16[4,16,4,1792]{3,1,2,0:T(8,128)(2,1)}, u32[]{:S(2)}) copy-start(bf16[4,16,4,1792]{3,1,2,0:T(8,128)(2,1)} %copy-done.7) | copy-start | bytes 2752516
  91.7 10.4 %collective-permute-start.10 = (bf16[4,3,144,896]{3,2,1,0:T(8,128)(2,1)S(1)}, bf16[4,3,144,896]{3,2,1,0:T(8,128)(2,1)}, u32[]{:S(2)}, u32[]{:S(2)}) collective-permute-start(bf16[4,3,144,896]{3,2,1,0:T(8,128)(2,1)S(1)} %maximum_select_fusion.near_ref), channel_id=1, source_target_pairs={{0,16},{16,0},{1,17},{17,1},{2,18},{18,2},{3,19},{19,3},{4,20},{20... | collective-permute-start | bytes 9289736 | tf_op jit(solution)/shard_map/ppermute | solution.py:430
  95.8 37.5 %collective-permute-start.14 = (bf16[448,896]{1,0:T(8,128)(2,1)}, bf16[448,896]{1,0:T(8,128)(2,1)}, u32[]{:S(2)}, u32[]{:S(2)}) collective-permute-start(bf16[448,896]{1,0:T(8,128)(2,1)} %maximum_select_fusion.4), channel_id=1, source_target_pairs={{0,2},{1,3},{2,0},{3,1},{4,6},{5,7},{6,4},{7,5},{8,10},{9,11},{10,... | collective-permute-start | bytes 2408456 | tf_op jit(solution)/shard_map/ppermute | solution.py:430
  96.7 41.1 %collective-permute-start.17 = (bf16[3,112,896]{2,1,0:T(8,128)(2,1)}, bf16[3,112,896]{2,1,0:T(8,128)(2,1)}, u32[]{:S(2)}, u32[]{:S(2)}) collective-permute-start(bf16[3,112,896]{2,1,0:T(8,128)(2,1)} %pad_maximum_fusion.1), channel_id=1, source_target_pairs={{0,4},{4,0},{8,12},{12,8},{1,5},{5,1},{9,13},{13,9},{2,6},{6,2},{1... | collective-permute-start | bytes 1806344 | tf_op jit(solution)/shard_map/ppermute | solution.py:430
  97.9 41.0 %collective-permute-start.18 = (bf16[3,112,896]{2,1,0:T(8,128)(2,1)}, bf16[3,112,896]{2,1,0:T(8,128)(2,1)}, u32[]{:S(2)}, u32[]{:S(2)}) collective-permute-start(bf16[3,112,896]{2,1,0:T(8,128)(2,1)} %pad_maximum_fusion.1), channel_id=1, source_target_pairs={{0,8},{4,12},{8,0},{12,4},{1,9},{5,13},{9,1},{13,5},{2,10},{6,14},... | collective-permute-start | bytes 1806344 | tf_op jit(solution)/shard_map/ppermute | solution.py:430
  114.5 25.9 %collective-permute-start.13 = (bf16[4,640,128]{2,1,0:T(8,128)(2,1)}, bf16[4,640,128]{2,1,0:T(8,128)(2,1)S(1)}, u32[]{:S(2)}, u32[]{:S(2)}) collective-permute-start(bf16[4,640,128]{2,1,0:T(8,128)(2,1)} %get-tuple-element.14), channel_id=1, source_target_pairs={{0,12},{1,13},{2,14},{3,15},{16,28},{17,29},{18,30},{19,31}} | collective-permute-start | bytes 1966088 | tf_op jit(solution)/shard_map/ppermute | solution.py:479
  119.0 22.5 %collective-permute-start.12 = (bf16[4,640,128]{2,1,0:T(8,128)(2,1)}, bf16[4,640,128]{2,1,0:T(8,128)(2,1)S(1)}, u32[]{:S(2)}, u32[]{:S(2)}) collective-permute-start(bf16[4,640,128]{2,1,0:T(8,128)(2,1)} %get-tuple-element.14), channel_id=1, source_target_pairs={{0,8},{4,12},{1,9},{5,13},{2,10},{6,14},{3,11},{7,15},{16,24},{20,... | collective-permute-start | bytes 1966088 | tf_op jit(solution)/shard_map/ppermute | solution.py:479
  133.3 17.9 %collective-permute-start.11 = (bf16[4,640,128]{2,1,0:T(8,128)(2,1)}, bf16[4,640,128]{2,1,0:T(8,128)(2,1)S(1)}, u32[]{:S(2)}, u32[]{:S(2)}) collective-permute-start(bf16[4,640,128]{2,1,0:T(8,128)(2,1)} %get-tuple-element.14), channel_id=1, source_target_pairs={{0,4},{4,8},{8,12},{1,5},{5,9},{9,13},{2,6},{6,10},{10,14},{3,7},{... | collective-permute-start | bytes 1966088 | tf_op jit(solution)/shard_map/ppermute | solution.py:479
  137.8 14.8 %collective-permute-start.15 = (bf16[112,896]{1,0:T(8,128)(2,1)S(1)}, bf16[112,896]{1,0:T(8,128)(2,1)S(1)}, u32[]{:S(2)}, u32[]{:S(2)}) collective-permute-start(bf16[112,896]{1,0:T(8,128)(2,1)S(1)} %get-tuple-element.19), channel_id=1, source_target_pairs={{0,1},{1,0},{2,3},{3,2},{4,5},{5,4},{6,7},{7,6},{8,9},{9,8},{10,11... | collective-permute-start | bytes 602120 | tf_op jit(solution)/shard_map/ppermute | solution.py:430
  138.9 17.7 %collective-permute-start.20 = (bf16[3,48,896]{2,1,0:T(8,128)(2,1)S(1)}, bf16[3,48,896]{2,1,0:T(8,128)(2,1)S(1)}, u32[]{:S(2)}, u32[]{:S(2)}) collective-permute-start(bf16[3,48,896]{2,1,0:T(8,128)(2,1)S(1)} %slice_select_fusion.6), channel_id=1, source_target_pairs={{0,8},{4,12},{8,0},{12,4},{1,9},{5,13},{9,1},{13,5},{2,10},{6,14},... | collective-permute-start | bytes 774152 | tf_op jit(solution)/shard_map/ppermute | solution.py:430
  140.4 19.1 %collective-permute-start.19 = (bf16[3,64,896]{2,1,0:T(8,128)(2,1)S(1)}, bf16[3,64,896]{2,1,0:T(8,128)(2,1)S(1)}, u32[]{:S(2)}, u32[]{:S(2)}) collective-permute-start(bf16[3,64,896]{2,1,0:T(8,128)(2,1)S(1)} %slice_select_fusion.2), channel_id=1, source_target_pairs={{0,4},{4,0},{8,12},{12,8},{1,5},{5,1},{9,13},{13,9},{2,6},{6,2},{1... | collective-permute-start | bytes 1032200 | tf_op jit(solution)/shard_map/ppermute | solution.py:430
  141.5 11.2 %collective-permute-start.16 = (bf16[112,896]{1,0:T(8,128)(2,1)S(1)}, bf16[112,896]{1,0:T(8,128)(2,1)S(1)}, u32[]{:S(2)}, u32[]{:S(2)}) collective-permute-start(bf16[112,896]{1,0:T(8,128)(2,1)S(1)} %get-tuple-element.24), channel_id=1, source_target_pairs={{0,1},{1,0},{2,3},{3,2},{4,5},{5,4},{6,7},{7,6},{8,9},{9,8},{10,11... | collective-permute-start | bytes 602120 | tf_op jit(solution)/shard_map/ppermute | solution.py:430
  151.4 8.2 %copy-start.6 = (f32[4,640,128]{2,1,0:T(8,128)}, f32[4,640,128]{2,1,0:T(8,128)S(1)}, u32[]{:S(2)}) copy-start(f32[4,640,128]{2,1,0:T(8,128)S(1)} %convert_add_fusion.prior_ref) | copy-start | bytes 3932164
  159.6 4.0 %copy-start.23 = (f32[1792]{0:T(1024)S(1)}, f32[1792]{0:T(1024)}, u32[]{:S(2)}) copy-start(f32[1792]{0:T(1024)} %param.25) | copy-start | bytes 21508
  161.5 6.2 %copy-start.5 = (bf16[4,3,112,896]{3,2,1,0:T(8,128)(2,1)}, bf16[4,3,112,896]{3,2,1,0:T(8,128)(2,1)S(1)}, u32[]{:S(2)}) copy-start(bf16[4,3,112,896]{3,2,1,0:T(8,128)(2,1)S(1)} %maximum_select_fusion.1.near_ref) | copy-start | bytes 7225348
  161.5 4.7 %collective-permute-start.21 = (bf16[4,3,112,896]{3,2,1,0:T(8,128)(2,1)S(1)}, bf16[4,3,112,896]{3,2,1,0:T(8,128)(2,1)S(1)}, u32[]{:S(2)}, u32[]{:S(2)}) collective-permute-start(bf16[4,3,112,896]{3,2,1,0:T(8,128)(2,1)S(1)} %maximum_select_fusion.1.near_ref), channel_id=1, source_target_pairs={{0,16},{16,0},{1,17},{17,1},{2,18},{18,2},{3,19},{19,3},{4,20},{20... | collective-permute-start | bytes 7225352 | tf_op jit(solution)/shard_map/ppermute | solution.py:430
  162.6 17.4 %collective-permute-start.26 = (bf16[1,336,896]{2,1,0:T(8,128)(2,1)}, bf16[1,336,896]{2,1,0:T(8,128)(2,1)}, u32[]{:S(2)}, u32[]{:S(2)}) collective-permute-start(bf16[1,336,896]{2,1,0:T(8,128)(2,1)} %slice_select_fusion), channel_id=1, source_target_pairs={{0,8},{4,12},{8,0},{12,4},{1,9},{5,13},{9,1},{13,5},{2,10},{6,14},... | collective-permute-start | bytes 1806344 | tf_op jit(solution)/shard_map/ppermute | solution.py:430
  162.6 23.9 %collective-permute-start.25 = (bf16[1,336,896]{2,1,0:T(8,128)(2,1)}, bf16[1,336,896]{2,1,0:T(8,128)(2,1)}, u32[]{:S(2)}, u32[]{:S(2)}) collective-permute-start(bf16[1,336,896]{2,1,0:T(8,128)(2,1)} %slice_select_fusion), channel_id=1, source_target_pairs={{0,4},{4,0},{8,12},{12,8},{1,5},{5,1},{9,13},{13,9},{2,6},{6,2},{1... | collective-permute-start | bytes 1806344 | tf_op jit(solution)/shard_map/ppermute | solution.py:430
  166.2 1.5 copy-start.11
  179.9 22.3 %collective-permute-start.23 = (bf16[192,1792]{1,0:T(8,128)(2,1)}, bf16[192,1792]{1,0:T(8,128)(2,1)S(1)}, u32[]{:S(2)}, u32[]{:S(2)}) collective-permute-start(bf16[192,1792]{1,0:T(8,128)(2,1)} %get-tuple-element.15.low_ref), channel_id=1, source_target_pairs={{0,1},{1,0},{2,3},{3,2},{4,5},{5,4},{6,7},{7,6},{8,9},{9,8},{10,11... | collective-permute-start | bytes 2064392 | tf_op jit(solution)/shard_map/ppermute | solution.py:430
  181.0 23.0 %collective-permute-start.27 = (bf16[1,176,896]{2,1,0:T(8,128)(2,1)S(1)}, bf16[1,176,896]{2,1,0:T(8,128)(2,1)S(1)}, u32[]{:S(2)}, u32[]{:S(2)}) collective-permute-start(bf16[1,176,896]{2,1,0:T(8,128)(2,1)S(1)} %slice_select_fusion.4), channel_id=1, source_target_pairs={{0,4},{4,0},{8,12},{12,8},{1,5},{5,1},{9,13},{13,9},{2,6},{6,2},{1... | collective-permute-start | bytes 946184 | tf_op jit(solution)/shard_map/ppermute | solution.py:430
  181.6 20.1 %collective-permute-start.24 = (bf16[80,1792]{1,0:T(8,128)(2,1)}, bf16[80,1792]{1,0:T(8,128)(2,1)S(1)}, u32[]{:S(2)}, u32[]{:S(2)}) collective-permute-start(bf16[80,1792]{1,0:T(8,128)(2,1)} %get-tuple-element.17), channel_id=1, source_target_pairs={{0,5},{1,4},{2,7},{3,6},{4,9},{5,8},{6,11},{7,10},{8,13},{9,12},{1... | collective-permute-start | bytes 860168 | tf_op jit(solution)/shard_map/ppermute | solution.py:654
  187.4 16.5 %collective-permute-start.28 = (bf16[1,160,896]{2,1,0:T(8,128)(2,1)S(1)}, bf16[1,160,896]{2,1,0:T(8,128)(2,1)S(1)}, u32[]{:S(2)}, u32[]{:S(2)}) collective-permute-start(bf16[1,160,896]{2,1,0:T(8,128)(2,1)S(1)} %slice_select_fusion.5), channel_id=1, source_target_pairs={{0,8},{4,12},{8,0},{12,4},{1,9},{5,13},{9,1},{13,5},{2,10},{6,14},... | collective-permute-start | bytes 860168 | tf_op jit(solution)/shard_map/ppermute | solution.py:430
  201.7 4.2 %copy-start.18 = (bf16[80,1792]{1,0:T(8,128)(2,1)}, bf16[80,1792]{1,0:T(8,128)(2,1)S(1)}, u32[]{:S(2)}) copy-start(bf16[80,1792]{1,0:T(8,128)(2,1)S(1)} %collective-permute-done.24.halo_ref) | copy-start | bytes 860164
  202.2 1.9 copy-start.16
  204.1 1.9 copy-start.21
  204.1 4.4 %copy-start.19 = (bf16[64,1792]{1,0:T(8,128)(2,1)S(1)}, bf16[64,1792]{1,0:T(8,128)(2,1)}, u32[]{:S(2)}) copy-start(bf16[64,1792]{1,0:T(8,128)(2,1)} %get-tuple-element.16.high_ref) | copy-start | bytes 688132
  205.9 38.9 %copy-start.2 = (bf16[4,1,336,896]{3,2,1,0:T(8,128)(2,1)}, bf16[4,1,336,896]{3,2,1,0:T(8,128)(2,1)S(1)}, u32[]{:S(2)}) copy-start(bf16[4,1,336,896]{3,2,1,0:T(8,128)(2,1)S(1)} %maximum_select_fusion.2.near_ref) | copy-start | bytes 7225348
  205.9 38.8 %collective-permute-start.29 = (bf16[4,1,336,896]{3,2,1,0:T(8,128)(2,1)S(1)}, bf16[4,1,336,896]{3,2,1,0:T(8,128)(2,1)}, u32[]{:S(2)}, u32[]{:S(2)}) collective-permute-start(bf16[4,1,336,896]{3,2,1,0:T(8,128)(2,1)S(1)} %maximum_select_fusion.2.near_ref), channel_id=1, source_target_pairs={{0,16},{16,0},{1,17},{17,1},{2,18},{18,2},{3,19},{19,3},{4,20},{20... | collective-permute-start | bytes 7225352 | tf_op jit(solution)/shard_map/ppermute | solution.py:430
  206.7 8.1 %collective-permute-start.30 = (f32[3,1536]{1,0:T(4,128)S(1)}, f32[3,1536]{1,0:T(4,128)S(1)}, u32[]{:S(2)}, u32[]{:S(2)}) collective-permute-start(f32[3,1536]{1,0:T(4,128)S(1)} %reshape.538), channel_id=1, source_target_pairs={{0,2},{1,3},{2,0},{3,1},{4,6},{5,7},{6,4},{7,5},{8,10},{9,11},{10,... | collective-permute-start | bytes 55304 | tf_op jit(solution)/shard_map/ppermute | solution.py:430
  208.6 7.9 %collective-permute-start.31 = (bf16[64,1792]{1,0:T(8,128)(2,1)S(1)}, bf16[64,1792]{1,0:T(8,128)(2,1)S(1)}, u32[]{:S(2)}, u32[]{:S(2)}) collective-permute-start(bf16[64,1792]{1,0:T(8,128)(2,1)S(1)} %copy-done.19), channel_id=1, source_target_pairs={{0,1},{1,0},{2,3},{3,2},{4,5},{5,4},{6,7},{7,6},{8,9},{9,8},{10,11... | collective-permute-start | bytes 688136 | tf_op jit(solution)/shard_map/ppermute | solution.py:430
  209.8 51.7 %collective-permute-start.35 = (bf16[3,112,896]{2,1,0:T(8,128)(2,1)}, bf16[3,112,896]{2,1,0:T(8,128)(2,1)}, u32[]{:S(2)}, u32[]{:S(2)}) collective-permute-start(bf16[3,112,896]{2,1,0:T(8,128)(2,1)} %broadcast_select_fusion.1), channel_id=1, source_target_pairs={{0,12},{4,8},{8,4},{12,0},{1,13},{5,9},{9,5},{13,1},{2,14},{6,10},... | collective-permute-start | bytes 1806344 | tf_op jit(solution)/shard_map/ppermute | solution.py:430
  212.4 49.1 %collective-permute-start.34 = (bf16[3,112,896]{2,1,0:T(8,128)(2,1)}, bf16[3,112,896]{2,1,0:T(8,128)(2,1)}, u32[]{:S(2)}, u32[]{:S(2)}) collective-permute-start(bf16[3,112,896]{2,1,0:T(8,128)(2,1)} %broadcast_select_fusion.1), channel_id=1, source_target_pairs={{0,8},{4,12},{8,0},{12,4},{1,9},{5,13},{9,1},{13,5},{2,10},{6,14},... | collective-permute-start | bytes 1806344 | tf_op jit(solution)/shard_map/ppermute | solution.py:430
  214.8 46.7 %collective-permute-start.33 = (bf16[3,112,896]{2,1,0:T(8,128)(2,1)}, bf16[3,112,896]{2,1,0:T(8,128)(2,1)}, u32[]{:S(2)}, u32[]{:S(2)}) collective-permute-start(bf16[3,112,896]{2,1,0:T(8,128)(2,1)} %broadcast_select_fusion.1), channel_id=1, source_target_pairs={{0,4},{4,0},{8,12},{12,8},{1,5},{5,1},{9,13},{13,9},{2,6},{6,2},{1... | collective-permute-start | bytes 1806344 | tf_op jit(solution)/shard_map/ppermute | solution.py:430
  216.5 28.3 %copy-start.20 = (bf16[64,1792]{1,0:T(8,128)(2,1)}, bf16[64,1792]{1,0:T(8,128)(2,1)S(1)}, u32[]{:S(2)}) copy-start(bf16[64,1792]{1,0:T(8,128)(2,1)S(1)} %collective-permute-done.31.high_ref) | copy-start | bytes 688132
  216.5 28.3 %collective-permute-start.22 = (bf16[80,1792]{1,0:T(8,128)(2,1)}, bf16[80,1792]{1,0:T(8,128)(2,1)S(1)}, u32[]{:S(2)}, u32[]{:S(2)}) collective-permute-start(bf16[80,1792]{1,0:T(8,128)(2,1)} %get-tuple-element.17), channel_id=1, source_target_pairs={{0,4},{4,8},{8,12},{1,5},{5,9},{9,13},{2,6},{6,10},{10,14},{3,7},{... | collective-permute-start | bytes 860168 | tf_op jit(solution)/shard_map/ppermute | solution.py:652
  245.5 16.1 %copy-start.12 = (bf16[1,3,112,896]{3,2,1,0:T(8,128)(2,1)S(1)}, bf16[1,3,112,896]{3,2,1,0:T(8,128)(2,1)}, u32[]{:S(2)}) copy-start(bf16[1,3,112,896]{3,2,1,0:T(8,128)(2,1)} %fusion.14) | copy-start | bytes 1806340
  261.5 2.0 copy-start.13
  261.6 2.5 copy-start.24
  261.6 2.5 copy-start.25
  263.5 16.2 %copy-start.4 = (bf16[4,3,112,896]{3,2,1,0:T(8,128)(2,1)}, bf16[4,3,112,896]{3,2,1,0:T(8,128)(2,1)S(1)}, u32[]{:S(2)}) copy-start(bf16[4,3,112,896]{3,2,1,0:T(8,128)(2,1)S(1)} %maximum_select_fusion.3.near_ref) | copy-start | bytes 7225348
  263.5 16.2 %collective-permute-start.36 = (bf16[4,3,112,896]{3,2,1,0:T(8,128)(2,1)S(1)}, bf16[4,3,112,896]{3,2,1,0:T(8,128)(2,1)}, u32[]{:S(2)}, u32[]{:S(2)}) collective-permute-start(bf16[4,3,112,896]{3,2,1,0:T(8,128)(2,1)S(1)} %maximum_select_fusion.3.near_ref), channel_id=1, source_target_pairs={{0,16},{16,0},{1,17},{17,1},{2,18},{18,2},{3,19},{19,3},{4,20},{20... | collective-permute-start | bytes 7225352 | tf_op jit(solution)/shard_map/ppermute | solution.py:430
  263.6 16.1 %collective-permute-start.32 = (bf16[2,256,512]{2,1,0:T(8,128)(2,1)S(1)}, bf16[2,256,512]{2,1,0:T(8,128)(2,1)S(1)}, u32[]{:S(2)}, u32[]{:S(2)}) collective-permute-start(bf16[2,256,512]{2,1,0:T(8,128)(2,1)S(1)} %copy-done.13), channel_id=1, source_target_pairs={{0,1},{1,0},{2,3},{3,2},{4,5},{5,4},{6,7},{7,6},{8,9},{9,8},{10,11... | collective-permute-start | bytes 1572872 | tf_op jit(solution)/shard_map/ppermute | solution.py:430
  279.7 0.8 copy-start.17
  287.2 30.0 %copy-start.1 = (bf16[64,4,1792]{2,1,0:T(4,128)(2,1)S(1)}, bf16[64,4,1792]{2,1,0:T(4,128)(2,1)}, u32[]{:S(2)}) copy-start(bf16[64,4,1792]{2,1,0:T(4,128)(2,1)} %param.17) | copy-start | bytes 2752516
  (1 other events, 0.7 us)

commit v10 on v9

--- a/solution.py
+++ b/solution.py
@@ -141,6 +141,7 @@
     num_ref,
     q_ref,
     state_ref,
+    state_two_ref,
     tokens_ref,
     normed_ref,
     value_w_ref,
@@ -180,6 +181,7 @@
     causal = lax.broadcasted_iota(jnp.int32, (rows, rows), 1) <= lax.broadcasted_iota(
         jnp.int32, (rows, rows), 0
     )
+    states = []
     key_features = features(keys, first_ref[...], second_ref[...], ones_ref[...]).astype(BF16)
     for h in range(heads):
         at = 2 * h * feature_dim
@@ -189,8 +191,13 @@
         value = values[:, h * SLOT : (h + 1) * SLOT]
         num_ref[0, :, h * SLOT : (h + 1) * SLOT] = dot(kernel, value)
         state = dot(key_features[:, h * FEAT_SLOT : h * FEAT_SLOT + kept], value, ((0,), (0,)))
-        head = pl.multiple_of(place_ref[h] * kept, 16)
-        state_ref[0, pl.ds(head, kept), :] = state.astype(BF16)
+        states.append(state.astype(BF16))
+    for first_step, ref in ((0, state_ref), (groups // 2, state_two_ref)):
+
+        @pl.when((step >= first_step) & (step < first_step + groups // 2))
+        def _(ref=ref):
+            for h in range(heads):
+                ref[0, pl.ds(pl.multiple_of(place_ref[h] * kept, 16), kept), :] = states[h]
 
 
 def add_branch(mixed, w_ref, total_ref):
@@ -209,6 +216,7 @@
     ones_ref,
     scale_ref,
     prior_ref,
+    prior_two_ref,
     own_ref,
     near_ref,
     far_ref,
@@ -250,7 +258,8 @@
     query_features = features(q_ref[0], first_ref[...], second_ref[...], ones_ref[...])
     query_features = (query_features * scale_ref[...]).astype(BF16)
     for h in range(heads):
-        prior = prior_ref[0, pl.ds(pl.multiple_of(place_ref[h] * kept, 16), kept), :]
+        at = pl.ds(pl.multiple_of(place_ref[h] * kept, 16), kept)
+        prior = jnp.where(step < groups // 2, prior_ref[0, at, :], prior_two_ref[0, at, :])
         lanes = slice(h * SLOT, (h + 1) * SLOT)
         total = num_ref[0, :, lanes] + dot(
             query_features[:, h * FEAT_SLOT : h * FEAT_SLOT + kept], prior.astype(BF16)
@@ -472,17 +481,22 @@
     return near, across(near, "dp", 1)
 
 
-def earlier_blocks(state, axis):
-    peers = lax.axis_size(axis)
-    if peers <= 4:
-        found = [
-            lax.ppermute(state, axis, [(i, i + by) for i in range(peers - by)])
-            for by in range(1, peers)
-        ]
-        return sum(one.astype(F32) for one in found)
-    everything = lax.all_gather(state, axis).astype(F32)
-    reached = jnp.arange(peers) < lax.axis_index(axis)
-    return jnp.sum(jnp.where(reached[:, None, None, None], everything, 0.0), axis=0)
+def earlier_blocks(one, two, axis, second):
+    peers, mine = lax.axis_size(axis), lax.axis_index(axis)
+    if peers != 4:
+        both = lax.all_gather(jnp.concatenate([one, two]), axis).astype(F32)
+        reached = (jnp.arange(peers) < mine)[:, None, None, None]
+        total = jnp.sum(jnp.where(reached, both, 0.0), axis=0)
+        return total[: one.shape[0]], total[one.shape[0] :]
+    upward = [(0, 2), (1, 3)]
+    one_beside, two_below = across(one, axis, 1), lax.ppermute(two, axis, upward)
+    pair = after((one.astype(F32) + one_beside.astype(F32)).astype(one.dtype), second)
+    two_sent = jnp.where(mine == 2, two.astype(F32), 0.0) + two_below.astype(F32)
+    two_sent = jnp.where(mine < 2, two, two_sent.astype(two.dtype))
+    one_below, two_beside = lax.ppermute(pair, axis, upward), across(two_sent, axis, 1)
+    one_total = jnp.where(mine % 2 == 1, one_beside.astype(F32), 0.0) + one_below.astype(F32)
+    two_total = jnp.where(mine > 0, two_beside.astype(F32), 0.0) + two_below.astype(F32)
+    return one_total, two_total
 
 
 def on_device(
@@ -556,7 +570,6 @@
 
     held_out_one = settled(jnp.stack(from_groups(own_piece([out_one]), (picked,))))
     near_one = from_plane(held_one, neighbours(held_one), (swapped,), (held_out_one,))
-    out_piece = after(own_piece([out_two]), (swapped,))
     beyond = from_group(own_piece([window_t, out_two]), (swapped,))
     places = jnp.concatenate([(seq_place % NEAR) ^ jnp.arange(NEAR), dp_place[None]])
     places = places.astype(jnp.int32)
@@ -579,7 +592,12 @@
 
     slots = heads * SLOT
     mid = 3 * rows // 4
-    num, queries, state = call(
+    half = group_count // 2
+    halves = [
+        pl.BlockSpec((1, heads * kept, SLOT), lambda g: (jnp.minimum(g, half - 1), 0, 0)),
+        pl.BlockSpec((1, heads * kept, SLOT), lambda g: (jnp.maximum(g - half, 0), 0, 0)),
+    ]
+    num, queries, state, state_two = call(
         functools.partial(linear_kernel, heads, feature_dim, kept),
         group_count,
         [
@@ -592,11 +610,11 @@
             whole(ones.shape),
             whole(column.shape),
         ],
-        [each((rows, slots)), each((rows, 2 * feat_cols)), each((heads * kept, SLOT))],
+        [each((rows, slots)), each((rows, 2 * feat_cols)), *halves],
         [
             jax.ShapeDtypeStruct((group_count, rows, slots), F32),
             jax.ShapeDtypeStruct((group_count, rows, 2 * feat_cols), BF16),
-            jax.ShapeDtypeStruct((group_count, heads * kept, SLOT), BF16),
+            *[jax.ShapeDtypeStruct((half, heads * kept, SLOT), BF16)] * 2,
         ],
         [
             pltpu.VMEM((rows, width), BF16),
@@ -609,15 +627,17 @@
     )(
         places, tokens, gain_one[None], values_t, featmap_t, *near_one, first, second, ones, column
     )
-    prior = settled(earlier_blocks(state, "seq"))
+    prior_one, prior_two = earlier_blocks(state, state_two, "seq", (beyond,))
+    prior_two = settled(prior_two, (prior_one,))
     beyond = after(beyond, (state,))
+    out_piece = after(own_piece([out_two]), (state,))
     held_window, out_beyond = beyond[:, : 3 * HEAD], beyond[0, 3 * HEAD :]
     held_out_two = [out_beyond, across(out_piece, "tensor", 1), across(out_beyond, "tensor", 1)]
-    held_out_two = settled(jnp.stack(held_out_two), (prior,))
+    held_out_two = settled(jnp.stack(held_out_two), (prior_two,))
     near_out_one = from_plane(
-        held_out_one, neighbours(held_out_one), (state,), (beyond, held_out_two)
-    )
-    held_window = after(held_window, (prior,))
+        held_out_one, neighbours(held_out_one), (state,), (held_out_two,)
+    )
+    held_window = after(held_window, (prior_two,))
     near_by_window = neighbours(held_window)
     residual, low, high, tail = call(
         functools.partial(out_one_kernel, heads, kept),
@@ -631,7 +651,7 @@
             whole(ones.shape),
             whole(scale.shape),
         ]
-        + [each((heads * kept, SLOT))]
+        + halves
         + [HBM] * 4
         + [whole((1, width))],
         [whole((n, width)) for n in (rows, mid, rows - mid, HALO)],
@@ -645,7 +665,7 @@
         ],
         "linear_out",
     )(
-        places, num, queries, first, second, ones, scale, prior, out_one, *near_out_one, tokens,
+        places, num, queries, first, second, ones, scale, prior_one, prior_two, out_one, *near_out_one, tokens,
         gain_two[None],
     )
 
@@ -660,7 +680,7 @@
             for j in range(group_count)
         ],
     )
-    near_window = from_plane(held_window, near_by_window, (residual,), (pair_low, pair_halo))
+    near_window = from_plane(held_window, near_by_window, (residual,), (pair_low, pair_halo, halo))
     held_out_two = after(held_out_two, (residual,))
     block_start = (seq_place * rows).astype(jnp.int32)[None]
 
@@ -685,7 +705,7 @@
             "window_rows",
         )(places, block_start, slot_low, slot_high, slot_halo, window_t, *near_window, taps, earlier)
 
-    mixed_pair = window_rows(pair_low, pair_high, pair_halo, halo)
+    mixed_pair = window_rows(pair_low, pair_high, pair_halo, low)
     near_out_two = from_plane(held_out_two, neighbours(held_out_two), None, (mixed_pair,))
     mixed_own = window_rows(low, high, halo, mixed_pair)
     mixed_pair = across(mixed_pair, "tensor", 1)

time: 320 us -> 321 us (level)
  local copies, waits for them, and re-layouts: 30.1 us -> 34.8 us
    ppermute x32 -> x34, waiting for transfers between devices: 44 us -> 72.3 us  [across(): lax.ppermute(array, axis, [(i, i ^ bit) for i in range(lax.axis_size(axis...]
    ppermute x1, waiting for transfers between devices: 22 us -> 0.99 us  [on_device(): halo = lax.ppermute(tail, 'seq', [(i, i + 1) for i in range(seq_count - 1)])]
    ppermute x1, waiting for transfers between devices: 14.1 us -> 1.23 us  [on_device(): lax.ppermute(tail, ('seq', 'tensor'), [(i * group_count + j, (i + 1) * gr...]
    ppermute x3 -> x2, waiting for transfers between devices: 7.7 us -> 11.9 us  [the longest x1 6.53 us: earlier_blocks(): lax.ppermute(pair, axis, upward)]
    ppermute x32 -> x34, starting transfers between devices: 30.8 us -> 33.6 us  [across(): lax.ppermute(array, axis, [(i, i ^ bit) for i in range(lax.axis_size(axis...]
    select_n x20 -> x22, other arithmetic: 19.8 us -> 18.1 us  [after(): return jnp.where(zero == 0.0, array, jnp.zeros_like(array))]
    ppermute x3 -> x2, starting transfers between devices: 8.48 us -> 6.95 us  [the longest x1 3.57 us: earlier_blocks(): lax.ppermute(pair, axis, upward)]
    slice x12 -> x14, local copies, waits for them, and re-layouts: 9.29 us -> 10.3 us  [after(): lax.slice(other, (0,) * other.ndim, (1,) * other.ndim)]
  transfers between devices with their start and end apart: 39 -> 40, of which waited for: 13 -> 14; matrix products, arithmetic and copies ran while one was open for 11% -> 12% of each run, Pallas kernels for 16% -> 16%
where the time goes in v10:
time: 321 us; the launch traced here: 319 us
  waiting for transfers between devices  105 us (33%)
  Pallas kernels  58.3 us (18%)
  starting transfers between devices  58.2 us (18%)
  local copies, waits for them, and re-layouts  34.8 us (11%)
  other arithmetic  26.4 us (8%)
  blocking collectives  26.1 us (8%)
  between operations  10.2 us (3%)
    ppermute x34, waiting for transfers between devices, across(): lax.ppermute(array, axis, [(i, i ^ bit) for i in range(lax.axis_size(axis...  72.3 us
    ppermute x34, starting transfers between devices, across(): lax.ppermute(array, axis, [(i, i ^ bit) for i in range(lax.axis_size(axis...  33.6 us
    pallas_call x2, Pallas kernels, window_rows(): call(functools.partial(window_kernel, heads), 2, [SMEM, SMEM, *[HBM] * 6,...  28.2 us
    all_to_all x1, blocking collectives, on_device(): lax.all_to_all(result, 'tensor', split_axis=0, concat_axis=0, tiled=True)  26.1 us
    all_to_all x1, waiting for transfers between devices, on_device(): lax.all_to_all(picked, 'tensor', split_axis=0, concat_axis=0, tiled=True)  18.8 us
    select_n x22, other arithmetic, after(): return jnp.where(zero == 0.0, array, jnp.zeros_like(array))  18.1 us
    pallas_call x1, Pallas kernels, on_device(): call(functools.partial(linear_kernel, heads, feature_dim, kept), group_co...  12.8 us
    pallas_call x1, Pallas kernels, on_device(): call(functools.partial(out_one_kernel, heads, kept), group_count, [SMEM,...  10.6 us
  transfers between devices with their start and end apart: 40, of which 14 were waited for; matrix products, arithmetic and copies ran while one was open for 12% of the time, Pallas kernels for 16%

profile of v10, /device:TPU:0, one launch (start us, length us, event | category | flops | bytes accessed | tf_op | source)
XLA Modules:
  0.0 319.2 jit_solution(17683596582970982766)
XLA Ops:
  2.5 2.2 gather_fusion
  4.7 5.2 %all-to-all-start = ((bf16[8,8,4,1792]{3,2,1,0:T(4,128)(2,1)}), bf16[8,8,4,1792]{3,2,1,0:T(4,128)(2,1)S(1)}, u32[]{:S(2)}, u32[]{:S(2)}) async-start(bf16[8,8,4,1792]{3,2,1,0:T(4,128)(2,1)} %bitcast.15), calls=%async_computation | async-start | bytes 1835008 | tf_op jit(solution)/shard_map/all_to_all | solution.py:559
  11.6 2.7 collective-permute-start.1
  14.3 1.6 collective-permute-start
  16.1 10.7 %collective-permute-done.1 = bf16[144,896]{1,0:T(8,128)(2,1)S(1)} collective-permute-done((bf16[144,896]{1,0:T(8,128)(2,1)S(1)}, bf16[144,896]{1,0:T(8,128)(2,1)S(1)}, u32[]{:S(2)}, u32[]{:S(2)}) %collective-permute-start.1) | collective-permute-done | bytes 258080 | tf_op jit(solution)/shard_map/ppermute | solution.py:439
  27.5 7.2 %collective-permute-done.2 = bf16[144,896]{1,0:T(8,128)(2,1)S(1)} collective-permute-done((bf16[144,896]{1,0:T(8,128)(2,1)S(1)}, bf16[144,896]{1,0:T(8,128)(2,1)S(1)}, u32[]{:S(2)}, u32[]{:S(2)}) %collective-permute-start.2) | collective-permute-done | bytes 258080 | tf_op jit(solution)/shard_map/ppermute | solution.py:439
  36.0 1.4 gather_fusion.1
  37.9 1.0 copy.44
  38.8 5.1 %all-to-all-start.1 = ((bf16[4,16,4,1792]{3,1,2,0:T(8,128)(2,1)}), bf16[4,16,4,1792]{3,1,2,0:T(8,128)(2,1)S(1)}, u32[]{:S(2)}, u32[]{:S(2)}) async-start(bf16[4,16,4,1792]{3,1,2,0:T(8,128)(2,1)} %copy.44), calls=%async_computation.1 | async-start | bytes 1835008 | tf_op jit(solution)/shard_map/all_to_all | solution.py:566
  43.9 1.6 collective-permute-start.7
  45.5 1.5 collective-permute-start.6
  48.2 1.7 select_bitcast_fusion.1
  49.8 2.9 collective-permute-start.4
  52.8 18.8 %all-to-all-done.1 = bf16[4,16,4,1792]{3,1,2,0:T(8,128)(2,1)S(1)} async-done(((bf16[4,16,4,1792]{3,1,2,0:T(8,128)(2,1)}), bf16[4,16,4,1792]{3,1,2,0:T(8,128)(2,1)S(1)}, u32[]{:S(2)}, u32[]{:S(2)}) %all-to-all-start.1) | async-done | bytes 917536 | tf_op jit(solution)/shard_map/all_to_all | solution.py:566
  72.9 1.7 collective-permute-start.8
  74.5 1.0 slice_select_fusion.3
  75.5 1.5 collective-permute-start.9
  77.1 2.0 collective-permute-start.5
  79.1 4.7 %collective-permute-done.3 = bf16[112,896]{1,0:T(8,128)(2,1)S(1)} collective-permute-done((bf16[112,896]{1,0:T(8,128)(2,1)}, bf16[112,896]{1,0:T(8,128)(2,1)S(1)}, u32[]{:S(2)}, u32[]{:S(2)}) %collective-permute-start.3) | collective-permute-done | bytes 200736 | tf_op jit(solution)/shard_map/ppermute | solution.py:439
  83.8 2.1 collective-permute-done.5
  85.9 1.9 pad_maximum_fusion.1
  87.8 1.2 slice.109
  89.8 1.8 maximum_select_fusion.near_ref
  92.4 2.3 constant_dynamic-slice_fusion
  96.5 1.4 copy.45
  97.9 2.4 reshape.540.x_ref
  100.2 12.8 %linear_rows.1 = (f32[4,256,512]{2,1,0:T(8,128)}, bf16[4,256,128]{2,1,0:T(8,128)(2,1)}, bf16[2,640,128]{2,1,0:T(8,128)(2,1)}, bf16[2,640,128]{2,1,0:T(8,128)(2,1)}) custom-call(s32[5]{0:T(128)} %pad_add_fusion.place_ref, bf16[256,1792]{1,0:T(8,128)(2,1)} %reshape.540.x_ref, f32[1,1792]{1,0:T(1,128)} %broadcast_in_dim.143.gain_ref, ...), custom_call_target="tpu_custom_call" | custom-call | tf_op jit(solution)/shard_map/linear_rows/pallas_call | solution.py:600
  113.1 1.3 slice.88
  116.5 1.2 collective-permute-start.11
  117.7 3.4 %collective-permute-start.14 = (bf16[2,640,128]{2,1,0:T(8,128)(2,1)}, bf16[2,640,128]{2,1,0:T(8,128)(2,1)S(1)}, u32[]{:S(2)}, u32[]{:S(2)}) collective-permute-start(bf16[2,640,128]{2,1,0:T(8,128)(2,1)} %get-tuple-element.16), channel_id=1, source_target_pairs={{0,8},{4,12},{1,9},{5,13},{2,10},{6,14},{3,11},{7,15},{16,24},{20,... | collective-permute-start | bytes 983048 | tf_op jit(solution)/shard_map/ppermute | solution.py:492
  122.2 1.0 slice_select_fusion.2
  124.2 5.4 %collective-permute-done.14 = bf16[2,640,128]{2,1,0:T(8,128)(2,1)S(1)} collective-permute-done((bf16[2,640,128]{2,1,0:T(8,128)(2,1)}, bf16[2,640,128]{2,1,0:T(8,128)(2,1)S(1)}, u32[]{:S(2)}, u32[]{:S(2)}) %collective-permute-start.14) | collective-permute-done | bytes 327712 | tf_op jit(solution)/shard_map/ppermute | solution.py:492
  129.5 2.0 collective-permute-start.16
  131.7 21.6 %collective-permute-done.12 = bf16[448,896]{1,0:T(8,128)(2,1)S(1)} collective-permute-done((bf16[448,896]{1,0:T(8,128)(2,1)S(1)}, bf16[448,896]{1,0:T(8,128)(2,1)S(1)}, u32[]{:S(2)}, u32[]{:S(2)}) %collective-permute-start.12) | collective-permute-done | bytes 802848 | tf_op jit(solution)/shard_map/ppermute | solution.py:439
  153.3 1.6 collective-permute-start.15
  156.2 3.6 %collective-permute-start.13 = (bf16[2,640,128]{2,1,0:T(8,128)(2,1)S(1)}, bf16[2,640,128]{2,1,0:T(8,128)(2,1)S(1)}, u32[]{:S(2)}, u32[]{:S(2)}) collective-permute-start(bf16[2,640,128]{2,1,0:T(8,128)(2,1)S(1)} %fusion.6), channel_id=1, source_target_pairs={{0,8},{4,12},{1,9},{5,13},{2,10},{6,14},{3,11},{7,15},{16,24},{20,... | collective-permute-start | bytes 983048 | tf_op jit(solution)/shard_map/ppermute | solution.py:496
  159.9 6.5 %collective-permute-done.13 = bf16[2,640,128]{2,1,0:T(8,128)(2,1)S(1)} collective-permute-done((bf16[2,640,128]{2,1,0:T(8,128)(2,1)S(1)}, bf16[2,640,128]{2,1,0:T(8,128)(2,1)S(1)}, u32[]{:S(2)}, u32[]{:S(2)}) %collective-permute-start.13) | collective-permute-done | bytes 327712 | tf_op jit(solution)/shard_map/ppermute | solution.py:496
  169.1 3.1 collective-permute-done.17
  173.6 1.9 maximum_select_fusion.1.near_ref
  175.6 1.1 slice_select_fusion
  176.6 2.5 collective-permute-start.27
  180.3 1.5 copy-done.12
  181.8 10.6 %linear_out.1 = (bf16[256,1792]{1,0:T(8,128)(2,1)}, bf16[192,1792]{1,0:T(8,128)(2,1)}, bf16[64,1792]{1,0:T(8,128)(2,1)}, bf16[80,1792]{1,0:T(8,128)(2,1)}) custom-call(s32[5]{0:T(128)} %pad_add_fusion.place_ref, f32[4,256,512]{2,1,0:T(8,128)} %get-tuple-element.13.num_ref, bf16[4,256,128]{2,1,0:T(8,128)(2,1)} %get-tuple-element.14.q_ref, ...), custom_call_target="tpu_custom_call" | custom-call | tf_op jit(solution)/shard_map/linear_out/pallas_call | solution.py:642
  192.5 3.4 %collective-permute-start.23 = (bf16[80,1792]{1,0:T(8,128)(2,1)}, bf16[80,1792]{1,0:T(8,128)(2,1)S(1)}, u32[]{:S(2)}, u32[]{:S(2)}) collective-permute-start(bf16[80,1792]{1,0:T(8,128)(2,1)} %get-tuple-element.19), channel_id=1, source_target_pairs={{0,4},{4,8},{8,12},{1,5},{5,9},{9,13},{2,6},{6,10},{10,14},{3,7},{... | collective-permute-start | bytes 860168 | tf_op jit(solution)/shard_map/ppermute | solution.py:672
  195.8 4.0 %collective-permute-start.25 = (bf16[80,1792]{1,0:T(8,128)(2,1)}, bf16[80,1792]{1,0:T(8,128)(2,1)S(1)}, u32[]{:S(2)}, u32[]{:S(2)}) collective-permute-start(bf16[80,1792]{1,0:T(8,128)(2,1)} %get-tuple-element.19), channel_id=1, source_target_pairs={{0,5},{1,4},{2,7},{3,6},{4,9},{5,8},{6,11},{7,10},{8,13},{9,12},{1... | collective-permute-start | bytes 860168 | tf_op jit(solution)/shard_map/ppermute | solution.py:674
  199.8 1.2 slice.97
  201.6 1.8 collective-permute-start.24
  203.4 1.0 slice_select_fusion.4
  206.1 1.2 collective-permute-done.25.halo_ref
  209.5 13.6 %collective-permute-done.24.low_ref = bf16[192,1792]{1,0:T(8,128)(2,1)S(1)} collective-permute-done((bf16[192,1792]{1,0:T(8,128)(2,1)}, bf16[192,1792]{1,0:T(8,128)(2,1)S(1)}, u32[]{:S(2)}, u32[]{:S(2)}) %collective-permute-start.24) | collective-permute-done | bytes 688160 | tf_op jit(solution)/shard_map/ppermute | solution.py:439
  225.6 1.7 maximum_select_fusion.2.near_ref
  229.9 2.0 collective-permute-start.35
  231.9 1.5 collective-permute-start.34
  233.4 1.3 gather_fusion.2
  236.2 4.1 %collective-permute-done.31 = f32[3,1536]{1,0:T(4,128)} collective-permute-done((f32[3,1536]{1,0:T(4,128)}, f32[3,1536]{1,0:T(4,128)}, u32[]{:S(2)}, u32[]{:S(2)}) %collective-permute-start.31) | collective-permute-done | bytes 18464 | tf_op jit(solution)/shard_map/ppermute | solution.py:439
  240.4 1.4 pad_maximum_fusion.3.tap_ref
  242.9 5.1 %collective-permute-done.32.high_ref = bf16[64,1792]{1,0:T(8,128)(2,1)S(1)} collective-permute-done((bf16[64,1792]{1,0:T(8,128)(2,1)S(1)}, bf16[64,1792]{1,0:T(8,128)(2,1)S(1)}, u32[]{:S(2)}, u32[]{:S(2)}) %collective-permute-start.32) | collective-permute-done | bytes 229408 | tf_op jit(solution)/shard_map/ppermute | solution.py:439
  248.7 14.1 %window_rows.2._ = bf16[2,256,512]{2,1,0:T(8,128)(2,1)} custom-call(s32[5]{0:T(128)} %pad_add_fusion.place_ref, s32[1]{0:T(128)} %bitcast.2.first_ref, bf16[192,1792]{1,0:T(8,128)(2,1)} %copy-done.17, bf16[64,1792]{1,0:T(8,128)(2,1)} %copy-done.24, bf16[80,1792]{1,0:T(8,128)(2,1)} %copy-done.22, bf16[3,4,112,1792]{3,2,1,0:T(8,128)(2,1)} %bitcast.91, ...), custom_call_target="tpu_custom_call" | custom-call | tf_op jit(solution)/shard_map/window_rows/pallas_call | solution.py:688
  262.9 1.2 slice.126
  264.7 1.9 maximum_select_fusion.3.near_ref
  268.4 14.1 %window_rows.3.mixed_ref = bf16[2,256,512]{2,1,0:T(8,128)(2,1)} custom-call(s32[5]{0:T(128)} %pad_add_fusion.place_ref, s32[1]{0:T(128)} %bitcast.2.first_ref, bf16[192,1792]{1,0:T(8,128)(2,1)} %get-tuple-element.17._.low_ref, bf16[64,1792]{1,0:T(8,128)(2,1)} %get-tuple-element.18.high_ref, bf16[80,1792]{1,0:T(8,128)(2,1)} %copy-done.21, ...), custom_call_target="tpu_custom_call" | custom-call | tf_op jit(solution)/shard_map/window_rows/pallas_call | solution.py:688
  283.3 6.7 %window_out.1 = bf16[256,1792]{1,0:T(8,128)(2,1)} custom-call(s32[5]{0:T(128)} %pad_add_fusion.place_ref, s32[1]{0:T(128)} %bitcast.1.live_ref, bf16[2,256,512]{2,1,0:T(8,128)(2,1)} %window_rows.3.mixed_ref, bf16[2,256,512]{2,1,0:T(8,128)(2,1)} %copy-done.18, bf16[1,4,112,1792]{3,2,1,0:T(8,128)(2,1)} %bitcast.105, bf16[4,3,112,896]{3,2,1,0:T(8,128)(2,1)} %copy-done.4, ...), custom_call_target="tpu_custom_call" | custom-call | tf_op jit(solution)/shard_map/window_out/pallas_call | solution.py:713
  290.0 1.9 reshape.548
  292.2 26.1 %all_to_all.15 = bf16[4,16,4,1792]{3,2,1,0:T(4,128)(2,1)S(1)} all-to-all(bf16[4,16,4,1792]{3,2,1,0:T(4,128)(2,1)S(1)} %bitcast.96), channel_id=1, replica_groups=mesh['dp'=2,'seq'=4,'tensor'=4] {'tensor'}, dimensions={0} | all-to-all | bytes 1835008 | tf_op jit(solution)/shard_map/all_to_all | solution.py:734
  (172 shorter events, 31.4 us)
Async XLA Ops:
  0.0 2.5 copy-start
  4.7 31.3 %all-to-all-start = ((bf16[8,8,4,1792]{3,2,1,0:T(4,128)(2,1)}), bf16[8,8,4,1792]{3,2,1,0:T(4,128)(2,1)S(1)}, u32[]{:S(2)}, u32[]{:S(2)}) async-start(bf16[8,8,4,1792]{3,2,1,0:T(4,128)(2,1)} %bitcast.15), calls=%async_computation | async-start | bytes 1835008 | tf_op jit(solution)/shard_map/all_to_all | solution.py:559
  11.6 15.2 %collective-permute-start.1 = (bf16[144,896]{1,0:T(8,128)(2,1)S(1)}, bf16[144,896]{1,0:T(8,128)(2,1)S(1)}, u32[]{:S(2)}, u32[]{:S(2)}) collective-permute-start(bf16[144,896]{1,0:T(8,128)(2,1)S(1)} %pad_maximum_fusion.2), channel_id=1, source_target_pairs={{0,2},{1,3},{2,0},{3,1},{4,6},{5,7},{6,4},{7,5},{8,10},{9,11},{10,... | collective-permute-start | bytes 774152 | tf_op jit(solution)/shard_map/ppermute | solution.py:439
  14.3 13.2 %collective-permute-start = (bf16[144,896]{1,0:T(8,128)(2,1)S(1)}, bf16[144,896]{1,0:T(8,128)(2,1)S(1)}, u32[]{:S(2)}, u32[]{:S(2)}) collective-permute-start(bf16[144,896]{1,0:T(8,128)(2,1)S(1)} %pad_maximum_fusion.2), channel_id=1, source_target_pairs={{0,1},{1,0},{2,3},{3,2},{4,5},{5,4},{6,7},{7,6},{8,9},{9,8},{10,11... | collective-permute-start | bytes 774152 | tf_op jit(solution)/shard_map/ppermute | solution.py:439
  26.9 7.8 %collective-permute-start.2 = (bf16[144,896]{1,0:T(8,128)(2,1)S(1)}, bf16[144,896]{1,0:T(8,128)(2,1)S(1)}, u32[]{:S(2)}, u32[]{:S(2)}) collective-permute-start(bf16[144,896]{1,0:T(8,128)(2,1)S(1)} %collective-permute-done.1), channel_id=1, source_target_pairs={{0,1},{1,0},{2,3},{3,2},{4,5},{5,4},{6,7},{7,6},{8,9},{9,8},{10,11... | collective-permute-start | bytes 774152 | tf_op jit(solution)/shard_map/ppermute | solution.py:439
  34.8 10.8 %copy-start.8 = (bf16[3,144,896]{2,1,0:T(8,128)(2,1)}, bf16[3,144,896]{2,1,0:T(8,128)(2,1)S(1)}, u32[]{:S(2)}) copy-start(bf16[3,144,896]{2,1,0:T(8,128)(2,1)S(1)} %pad_maximum_fusion) | copy-start | bytes 2322436
  38.8 32.7 %all-to-all-start.1 = ((bf16[4,16,4,1792]{3,1,2,0:T(8,128)(2,1)}), bf16[4,16,4,1792]{3,1,2,0:T(8,128)(2,1)S(1)}, u32[]{:S(2)}, u32[]{:S(2)}) async-start(bf16[4,16,4,1792]{3,1,2,0:T(8,128)(2,1)} %copy.44), calls=%async_computation.1 | async-start | bytes 1835008 | tf_op jit(solution)/shard_map/all_to_all | solution.py:566
  43.9 28.9 %collective-permute-start.7 = (bf16[3,144,896]{2,1,0:T(8,128)(2,1)S(1)}, bf16[3,144,896]{2,1,0:T(8,128)(2,1)S(1)}, u32[]{:S(2)}, u32[]{:S(2)}) collective-permute-start(bf16[3,144,896]{2,1,0:T(8,128)(2,1)S(1)} %pad_maximum_fusion), channel_id=1, source_target_pairs={{0,8},{4,12},{8,0},{12,4},{1,9},{5,13},{9,1},{13,5},{2,10},{6,14},... | collective-permute-start | bytes 2322440 | tf_op jit(solution)/shard_map/ppermute | solution.py:439
  45.5 29.0 %collective-permute-start.6 = (bf16[3,144,896]{2,1,0:T(8,128)(2,1)S(1)}, bf16[3,144,896]{2,1,0:T(8,128)(2,1)}, u32[]{:S(2)}, u32[]{:S(2)}) collective-permute-start(bf16[3,144,896]{2,1,0:T(8,128)(2,1)S(1)} %pad_maximum_fusion), channel_id=1, source_target_pairs={{0,4},{4,0},{8,12},{12,8},{1,5},{5,1},{9,13},{13,9},{2,6},{6,2},{1... | collective-permute-start | bytes 2322440 | tf_op jit(solution)/shard_map/ppermute | solution.py:439
  49.8 27.2 %collective-permute-start.4 = (bf16[112,896]{1,0:T(8,128)(2,1)}, bf16[112,896]{1,0:T(8,128)(2,1)}, u32[]{:S(2)}, u32[]{:S(2)}) collective-permute-start(bf16[112,896]{1,0:T(8,128)(2,1)} %select_bitcast_fusion.1), channel_id=1, source_target_pairs={{0,2},{1,3},{2,0},{3,1},{4,6},{5,7},{6,4},{7,5},{8,10},{9,11},{10,... | collective-permute-start | bytes 602120 | tf_op jit(solution)/shard_map/ppermute | solution.py:439
  71.6 18.2 %copy-start.6 = (bf16[4,16,4,1792]{3,1,2,0:T(8,128)(2,1)}, bf16[4,16,4,1792]{3,1,2,0:T(8,128)(2,1)S(1)}, u32[]{:S(2)}) copy-start(bf16[4,16,4,1792]{3,1,2,0:T(8,128)(2,1)S(1)} %all-to-all-done.1) | copy-start | bytes 2752516
  71.6 18.2 %copy-start.9 = (bf16[3,144,896]{2,1,0:T(8,128)(2,1)S(1)}, bf16[3,144,896]{2,1,0:T(8,128)(2,1)}, u32[]{:S(2)}) copy-start(bf16[3,144,896]{2,1,0:T(8,128)(2,1)} %copy-done.8) | copy-start | bytes 2322436
  72.8 17.0 %copy-start.16 = (bf16[3,144,896]{2,1,0:T(8,128)(2,1)}, bf16[3,144,896]{2,1,0:T(8,128)(2,1)S(1)}, u32[]{:S(2)}) copy-start(bf16[3,144,896]{2,1,0:T(8,128)(2,1)S(1)} %collective-permute-done.7) | copy-start | bytes 2322436
  72.9 16.8 %collective-permute-start.8 = (bf16[3,80,896]{2,1,0:T(8,128)(2,1)S(1)}, bf16[3,80,896]{2,1,0:T(8,128)(2,1)S(1)}, u32[]{:S(2)}, u32[]{:S(2)}) collective-permute-start(bf16[3,80,896]{2,1,0:T(8,128)(2,1)S(1)} %slice_select_fusion.1), channel_id=1, source_target_pairs={{0,4},{4,0},{8,12},{12,8},{1,5},{5,1},{9,13},{13,9},{2,6},{6,2},{1... | collective-permute-start | bytes 1290248 | tf_op jit(solution)/shard_map/ppermute | solution.py:439
  75.5 14.1 %collective-permute-start.9 = (bf16[3,64,896]{2,1,0:T(8,128)(2,1)S(1)}, bf16[3,64,896]{2,1,0:T(8,128)(2,1)S(1)}, u32[]{:S(2)}, u32[]{:S(2)}) collective-permute-start(bf16[3,64,896]{2,1,0:T(8,128)(2,1)S(1)} %slice_select_fusion.3), channel_id=1, source_target_pairs={{0,8},{4,12},{8,0},{12,4},{1,9},{5,13},{9,1},{13,5},{2,10},{6,14},... | collective-permute-start | bytes 1032200 | tf_op jit(solution)/shard_map/ppermute | solution.py:439
  77.1 6.7 %collective-permute-start.3 = (bf16[112,896]{1,0:T(8,128)(2,1)}, bf16[112,896]{1,0:T(8,128)(2,1)S(1)}, u32[]{:S(2)}, u32[]{:S(2)}) collective-permute-start(bf16[112,896]{1,0:T(8,128)(2,1)} %select_bitcast_fusion.1), channel_id=1, source_target_pairs={{0,1},{1,0},{2,3},{3,2},{4,5},{5,4},{6,7},{7,6},{8,9},{9,8},{10,11... | collective-permute-start | bytes 602120 | tf_op jit(solution)/shard_map/ppermute | solution.py:439
  77.1 8.8 %collective-permute-start.5 = (bf16[112,896]{1,0:T(8,128)(2,1)}, bf16[112,896]{1,0:T(8,128)(2,1)S(1)}, u32[]{:S(2)}, u32[]{:S(2)}) collective-permute-start(bf16[112,896]{1,0:T(8,128)(2,1)} %collective-permute-done.4), channel_id=1, source_target_pairs={{0,1},{1,0},{2,3},{3,2},{4,5},{5,4},{6,7},{7,6},{8,9},{9,8},{10,11... | collective-permute-start | bytes 602120 | tf_op jit(solution)/shard_map/ppermute | solution.py:439
  89.8 6.0 %copy-start.25 = (f32[1792]{0:T(1024)S(1)}, f32[1792]{0:T(1024)}, u32[]{:S(2)}) copy-start(f32[1792]{0:T(1024)} %param.21) | copy-start | bytes 21508
  89.8 6.6 %copy-start.7 = (bf16[4,16,4,1792]{3,1,2,0:T(8,128)(2,1)S(1)}, bf16[4,16,4,1792]{3,1,2,0:T(8,128)(2,1)}, u32[]{:S(2)}) copy-start(bf16[4,16,4,1792]{3,1,2,0:T(8,128)(2,1)} %copy-done.6) | copy-start | bytes 2752516
  91.7 8.6 %copy-start.3 = (bf16[4,3,144,896]{3,2,1,0:T(8,128)(2,1)}, bf16[4,3,144,896]{3,2,1,0:T(8,128)(2,1)S(1)}, u32[]{:S(2)}) copy-start(bf16[4,3,144,896]{3,2,1,0:T(8,128)(2,1)S(1)} %maximum_select_fusion.near_ref) | copy-start | bytes 9289732
  91.7 8.6 %collective-permute-start.10 = (bf16[4,3,144,896]{3,2,1,0:T(8,128)(2,1)S(1)}, bf16[4,3,144,896]{3,2,1,0:T(8,128)(2,1)}, u32[]{:S(2)}, u32[]{:S(2)}) collective-permute-start(bf16[4,3,144,896]{3,2,1,0:T(8,128)(2,1)S(1)} %maximum_select_fusion.near_ref), channel_id=1, source_target_pairs={{0,16},{16,0},{1,17},{17,1},{2,18},{18,2},{3,19},{19,3},{4,20},{20... | collective-permute-start | bytes 9289736 | tf_op jit(solution)/shard_map/ppermute | solution.py:439
  91.8 29.3 %collective-permute-start.18 = (bf16[3,112,896]{2,1,0:T(8,128)(2,1)}, bf16[3,112,896]{2,1,0:T(8,128)(2,1)}, u32[]{:S(2)}, u32[]{:S(2)}) collective-permute-start(bf16[3,112,896]{2,1,0:T(8,128)(2,1)} %pad_maximum_fusion.1), channel_id=1, source_target_pairs={{0,4},{4,0},{8,12},{12,8},{1,5},{5,1},{9,13},{13,9},{2,6},{6,2},{1... | collective-permute-start | bytes 1806344 | tf_op jit(solution)/shard_map/ppermute | solution.py:439
  94.7 27.5 %collective-permute-start.19 = (bf16[3,112,896]{2,1,0:T(8,128)(2,1)}, bf16[3,112,896]{2,1,0:T(8,128)(2,1)}, u32[]{:S(2)}, u32[]{:S(2)}) collective-permute-start(bf16[3,112,896]{2,1,0:T(8,128)(2,1)} %pad_maximum_fusion.1), channel_id=1, source_target_pairs={{0,8},{4,12},{8,0},{12,4},{1,9},{5,13},{9,1},{13,5},{2,10},{6,14},... | collective-permute-start | bytes 1806344 | tf_op jit(solution)/shard_map/ppermute | solution.py:439
  100.2 15.8 %copy-start.14 = (bf16[3,1,112,896]{3,2,1,0:T(8,128)(2,1)S(1)}, bf16[3,1,112,896]{3,2,1,0:T(8,128)(2,1)}, u32[]{:S(2)}) copy-start(bf16[3,1,112,896]{3,2,1,0:T(8,128)(2,1)} %constant_dynamic-slice_fusion) | copy-start | bytes 1806340
  113.1 18.5 %copy-start.20 = (bf16[2,640,128]{2,1,0:T(8,128)(2,1)S(1)}, bf16[2,640,128]{2,1,0:T(8,128)(2,1)}, u32[]{:S(2)}) copy-start(bf16[2,640,128]{2,1,0:T(8,128)(2,1)} %get-tuple-element.16) | copy-start | bytes 983044
  113.1 43.0 %copy-start.19 = (bf16[2,640,128]{2,1,0:T(8,128)(2,1)S(1)}, bf16[2,640,128]{2,1,0:T(8,128)(2,1)}, u32[]{:S(2)}) copy-start(bf16[2,640,128]{2,1,0:T(8,128)(2,1)} %get-tuple-element.15) | copy-start | bytes 983044
  116.2 37.1 %collective-permute-start.12 = (bf16[448,896]{1,0:T(8,128)(2,1)S(1)}, bf16[448,896]{1,0:T(8,128)(2,1)S(1)}, u32[]{:S(2)}, u32[]{:S(2)}) collective-permute-start(bf16[448,896]{1,0:T(8,128)(2,1)S(1)} %maximum_select_fusion.4), channel_id=1, source_target_pairs={{0,2},{1,3},{2,0},{3,1},{4,6},{5,7},{6,4},{7,5},{8,10},{9,11},{10,... | collective-permute-start | bytes 2408456 | tf_op jit(solution)/shard_map/ppermute | solution.py:439
  116.5 39.6 %collective-permute-start.11 = (bf16[2,640,128]{2,1,0:T(8,128)(2,1)}, bf16[2,640,128]{2,1,0:T(8,128)(2,1)S(1)}, u32[]{:S(2)}, u32[]{:S(2)}) collective-permute-start(bf16[2,640,128]{2,1,0:T(8,128)(2,1)} %get-tuple-element.15), channel_id=1, source_target_pairs={{0,4},{4,0},{8,12},{12,8},{1,5},{5,1},{9,13},{13,9},{2,6},{6,2},{1... | collective-permute-start | bytes 983048 | tf_op jit(solution)/shard_map/ppermute | solution.py:439
  117.7 11.8 %collective-permute-start.14 = (bf16[2,640,128]{2,1,0:T(8,128)(2,1)}, bf16[2,640,128]{2,1,0:T(8,128)(2,1)S(1)}, u32[]{:S(2)}, u32[]{:S(2)}) collective-permute-start(bf16[2,640,128]{2,1,0:T(8,128)(2,1)} %get-tuple-element.16), channel_id=1, source_target_pairs={{0,8},{4,12},{1,9},{5,13},{2,10},{6,14},{3,11},{7,15},{16,24},{20,... | collective-permute-start | bytes 983048 | tf_op jit(solution)/shard_map/ppermute | solution.py:492
  122.1 51.4 %collective-permute-start.21 = (bf16[3,48,896]{2,1,0:T(8,128)(2,1)S(1)}, bf16[3,48,896]{2,1,0:T(8,128)(2,1)S(1)}, u32[]{:S(2)}, u32[]{:S(2)}) collective-permute-start(bf16[3,48,896]{2,1,0:T(8,128)(2,1)S(1)} %slice_select_fusion.6), channel_id=1, source_target_pairs={{0,8},{4,12},{8,0},{12,4},{1,9},{5,13},{9,1},{13,5},{2,10},{6,14},... | collective-permute-start | bytes 774152 | tf_op jit(solution)/shard_map/ppermute | solution.py:439
  123.2 50.3 %collective-permute-start.20 = (bf16[3,64,896]{2,1,0:T(8,128)(2,1)S(1)}, bf16[3,64,896]{2,1,0:T(8,128)(2,1)S(1)}, u32[]{:S(2)}, u32[]{:S(2)}) collective-permute-start(bf16[3,64,896]{2,1,0:T(8,128)(2,1)S(1)} %slice_select_fusion.2), channel_id=1, source_target_pairs={{0,4},{4,0},{8,12},{12,8},{1,5},{5,1},{9,13},{13,9},{2,6},{6,2},{1... | collective-permute-start | bytes 1032200 | tf_op jit(solution)/shard_map/ppermute | solution.py:439
  129.5 39.6 %collective-permute-start.16 = (bf16[112,896]{1,0:T(8,128)(2,1)S(1)}, bf16[112,896]{1,0:T(8,128)(2,1)S(1)}, u32[]{:S(2)}, u32[]{:S(2)}) collective-permute-start(bf16[112,896]{1,0:T(8,128)(2,1)S(1)} %get-tuple-element.21), channel_id=1, source_target_pairs={{0,1},{1,0},{2,3},{3,2},{4,5},{5,4},{6,7},{7,6},{8,9},{9,8},{10,11... | collective-permute-start | bytes 602120 | tf_op jit(solution)/shard_map/ppermute | solution.py:439
  153.3 14.5 %collective-permute-start.15 = (bf16[2,640,128]{2,1,0:T(8,128)(2,1)S(1)}, bf16[2,640,128]{2,1,0:T(8,128)(2,1)S(1)}, u32[]{:S(2)}, u32[]{:S(2)}) collective-permute-start(bf16[2,640,128]{2,1,0:T(8,128)(2,1)S(1)} %fusion.5), channel_id=1, source_target_pairs={{0,4},{4,0},{8,12},{12,8},{1,5},{5,1},{9,13},{13,9},{2,6},{6,2},{1... | collective-permute-start | bytes 983048 | tf_op jit(solution)/shard_map/ppermute | solution.py:439
  156.2 10.2 %collective-permute-start.13 = (bf16[2,640,128]{2,1,0:T(8,128)(2,1)S(1)}, bf16[2,640,128]{2,1,0:T(8,128)(2,1)S(1)}, u32[]{:S(2)}, u32[]{:S(2)}) collective-permute-start(bf16[2,640,128]{2,1,0:T(8,128)(2,1)S(1)} %fusion.6), channel_id=1, source_target_pairs={{0,8},{4,12},{1,9},{5,13},{2,10},{6,14},{3,11},{7,15},{16,24},{20,... | collective-permute-start | bytes 983048 | tf_op jit(solution)/shard_map/ppermute | solution.py:496
  166.4 5.7 %collective-permute-start.17 = (bf16[112,896]{1,0:T(8,128)(2,1)S(1)}, bf16[112,896]{1,0:T(8,128)(2,1)S(1)}, u32[]{:S(2)}, u32[]{:S(2)}) collective-permute-start(bf16[112,896]{1,0:T(8,128)(2,1)S(1)} %get-tuple-element.26), channel_id=1, source_target_pairs={{0,1},{1,0},{2,3},{3,2},{4,5},{5,4},{6,7},{7,6},{8,9},{9,8},{10,11... | collective-permute-start | bytes 602120 | tf_op jit(solution)/shard_map/ppermute | solution.py:439
  166.5 5.7 %copy-start.10 = (f32[2,640,128]{2,1,0:T(8,128)}, f32[2,640,128]{2,1,0:T(8,128)S(1)}, u32[]{:S(2)}) copy-start(f32[2,640,128]{2,1,0:T(8,128)S(1)} %fusion.prior_ref) | copy-start | bytes 1966084
  167.9 4.3 %copy-start.11 = (f32[2,640,128]{2,1,0:T(8,128)}, f32[2,640,128]{2,1,0:T(8,128)S(1)}, u32[]{:S(2)}) copy-start(f32[2,640,128]{2,1,0:T(8,128)S(1)} %fusion.3.prior_two_ref) | copy-start | bytes 1966084
  173.6 6.1 %copy-start.26 = (f32[1792]{0:T(1024)S(1)}, f32[1792]{0:T(1024)}, u32[]{:S(2)}) copy-start(f32[1792]{0:T(1024)} %param.25) | copy-start | bytes 21508
  175.5 6.3 %copy-start.5 = (bf16[4,3,112,896]{3,2,1,0:T(8,128)(2,1)}, bf16[4,3,112,896]{3,2,1,0:T(8,128)(2,1)S(1)}, u32[]{:S(2)}) copy-start(bf16[4,3,112,896]{3,2,1,0:T(8,128)(2,1)S(1)} %maximum_select_fusion.1.near_ref) | copy-start | bytes 7225348
  175.5 4.8 %collective-permute-start.22 = (bf16[4,3,112,896]{3,2,1,0:T(8,128)(2,1)S(1)}, bf16[4,3,112,896]{3,2,1,0:T(8,128)(2,1)S(1)}, u32[]{:S(2)}, u32[]{:S(2)}) collective-permute-start(bf16[4,3,112,896]{3,2,1,0:T(8,128)(2,1)S(1)} %maximum_select_fusion.1.near_ref), channel_id=1, source_target_pairs={{0,16},{16,0},{1,17},{17,1},{2,18},{18,2},{3,19},{19,3},{4,20},{20... | collective-permute-start | bytes 7225352 | tf_op jit(solution)/shard_map/ppermute | solution.py:439
  176.6 26.7 %collective-permute-start.27 = (bf16[1,336,896]{2,1,0:T(8,128)(2,1)}, bf16[1,336,896]{2,1,0:T(8,128)(2,1)}, u32[]{:S(2)}, u32[]{:S(2)}) collective-permute-start(bf16[1,336,896]{2,1,0:T(8,128)(2,1)} %slice_select_fusion), channel_id=1, source_target_pairs={{0,8},{4,12},{8,0},{12,4},{1,9},{5,13},{9,1},{13,5},{2,10},{6,14},... | collective-permute-start | bytes 1806344 | tf_op jit(solution)/shard_map/ppermute | solution.py:439
  179.1 25.9 %collective-permute-start.26 = (bf16[1,336,896]{2,1,0:T(8,128)(2,1)}, bf16[1,336,896]{2,1,0:T(8,128)(2,1)}, u32[]{:S(2)}, u32[]{:S(2)}) collective-permute-start(bf16[1,336,896]{2,1,0:T(8,128)(2,1)} %slice_select_fusion), channel_id=1, source_target_pairs={{0,4},{4,0},{8,12},{12,8},{1,5},{5,1},{9,13},{13,9},{2,6},{6,2},{1... | collective-permute-start | bytes 1806344 | tf_op jit(solution)/shard_map/ppermute | solution.py:439
  192.5 16.4 %collective-permute-start.23 = (bf16[80,1792]{1,0:T(8,128)(2,1)}, bf16[80,1792]{1,0:T(8,128)(2,1)S(1)}, u32[]{:S(2)}, u32[]{:S(2)}) collective-permute-start(bf16[80,1792]{1,0:T(8,128)(2,1)} %get-tuple-element.19), channel_id=1, source_target_pairs={{0,4},{4,8},{8,12},{1,5},{5,9},{9,13},{2,6},{6,10},{10,14},{3,7},{... | collective-permute-start | bytes 860168 | tf_op jit(solution)/shard_map/ppermute | solution.py:672
  195.8 11.5 %collective-permute-start.25 = (bf16[80,1792]{1,0:T(8,128)(2,1)}, bf16[80,1792]{1,0:T(8,128)(2,1)S(1)}, u32[]{:S(2)}, u32[]{:S(2)}) collective-permute-start(bf16[80,1792]{1,0:T(8,128)(2,1)} %get-tuple-element.19), channel_id=1, source_target_pairs={{0,5},{1,4},{2,7},{3,6},{4,9},{5,8},{6,11},{7,10},{8,13},{9,12},{1... | collective-permute-start | bytes 860168 | tf_op jit(solution)/shard_map/ppermute | solution.py:674
  201.6 21.6 %collective-permute-start.24 = (bf16[192,1792]{1,0:T(8,128)(2,1)}, bf16[192,1792]{1,0:T(8,128)(2,1)S(1)}, u32[]{:S(2)}, u32[]{:S(2)}) collective-permute-start(bf16[192,1792]{1,0:T(8,128)(2,1)} %get-tuple-element.17._.low_ref), channel_id=1, source_target_pairs={{0,1},{1,0},{2,3},{3,2},{4,5},{5,4},{6,7},{7,6},{8,9},{9,8},{10,11... | collective-permute-start | bytes 2064392 | tf_op jit(solution)/shard_map/ppermute | solution.py:439
  204.4 21.1 %collective-permute-start.28 = (bf16[1,176,896]{2,1,0:T(8,128)(2,1)S(1)}, bf16[1,176,896]{2,1,0:T(8,128)(2,1)S(1)}, u32[]{:S(2)}, u32[]{:S(2)}) collective-permute-start(bf16[1,176,896]{2,1,0:T(8,128)(2,1)S(1)} %slice_select_fusion.4), channel_id=1, source_target_pairs={{0,4},{4,0},{8,12},{12,8},{1,5},{5,1},{9,13},{13,9},{2,6},{6,2},{1... | collective-permute-start | bytes 946184 | tf_op jit(solution)/shard_map/ppermute | solution.py:439
  206.0 19.5 %collective-permute-start.29 = (bf16[1,160,896]{2,1,0:T(8,128)(2,1)S(1)}, bf16[1,160,896]{2,1,0:T(8,128)(2,1)S(1)}, u32[]{:S(2)}, u32[]{:S(2)}) collective-permute-start(bf16[1,160,896]{2,1,0:T(8,128)(2,1)S(1)} %slice_select_fusion.5), channel_id=1, source_target_pairs={{0,8},{4,12},{8,0},{12,4},{1,9},{5,13},{9,1},{13,5},{2,10},{6,14},... | collective-permute-start | bytes 860168 | tf_op jit(solution)/shard_map/ppermute | solution.py:439
  207.4 40.7 %copy-start.22 = (bf16[80,1792]{1,0:T(8,128)(2,1)}, bf16[80,1792]{1,0:T(8,128)(2,1)S(1)}, u32[]{:S(2)}) copy-start(bf16[80,1792]{1,0:T(8,128)(2,1)S(1)} %collective-permute-done.25.halo_ref) | copy-start | bytes 860164
  208.9 16.7 %copy-start.21 = (bf16[80,1792]{1,0:T(8,128)(2,1)}, bf16[80,1792]{1,0:T(8,128)(2,1)S(1)}, u32[]{:S(2)}) copy-start(bf16[80,1792]{1,0:T(8,128)(2,1)S(1)} %collective-permute-done.23.halo_ref) | copy-start | bytes 860164
  223.1 2.5 copy-start.17
  225.6 16.1 %copy-start.23 = (bf16[64,1792]{1,0:T(8,128)(2,1)S(1)}, bf16[64,1792]{1,0:T(8,128)(2,1)}, u32[]{:S(2)}) copy-start(bf16[64,1792]{1,0:T(8,128)(2,1)} %get-tuple-element.18.high_ref) | copy-start | bytes 688132
  227.4 20.7 %copy-start.2 = (bf16[4,1,336,896]{3,2,1,0:T(8,128)(2,1)}, bf16[4,1,336,896]{3,2,1,0:T(8,128)(2,1)S(1)}, u32[]{:S(2)}) copy-start(bf16[4,1,336,896]{3,2,1,0:T(8,128)(2,1)S(1)} %maximum_select_fusion.2.near_ref) | copy-start | bytes 7225348
  227.4 20.6 %collective-permute-start.30 = (bf16[4,1,336,896]{3,2,1,0:T(8,128)(2,1)S(1)}, bf16[4,1,336,896]{3,2,1,0:T(8,128)(2,1)}, u32[]{:S(2)}, u32[]{:S(2)}) collective-permute-start(bf16[4,1,336,896]{3,2,1,0:T(8,128)(2,1)S(1)} %maximum_select_fusion.2.near_ref), channel_id=1, source_target_pairs={{0,16},{16,0},{1,17},{17,1},{2,18},{18,2},{3,19},{19,3},{4,20},{20... | collective-permute-start | bytes 7225352 | tf_op jit(solution)/shard_map/ppermute | solution.py:439
  229.9 34.7 %collective-permute-start.36 = (bf16[3,112,896]{2,1,0:T(8,128)(2,1)}, bf16[3,112,896]{2,1,0:T(8,128)(2,1)}, u32[]{:S(2)}, u32[]{:S(2)}) collective-permute-start(bf16[3,112,896]{2,1,0:T(8,128)(2,1)} %broadcast_select_fusion.1), channel_id=1, source_target_pairs={{0,12},{4,8},{8,4},{12,0},{1,13},{5,9},{9,5},{13,1},{2,14},{6,10},... | collective-permute-start | bytes 1806344 | tf_op jit(solution)/shard_map/ppermute | solution.py:439
  229.9 34.7 %collective-permute-start.35 = (bf16[3,112,896]{2,1,0:T(8,128)(2,1)}, bf16[3,112,896]{2,1,0:T(8,128)(2,1)}, u32[]{:S(2)}, u32[]{:S(2)}) collective-permute-start(bf16[3,112,896]{2,1,0:T(8,128)(2,1)} %broadcast_select_fusion.1), channel_id=1, source_target_pairs={{0,8},{4,12},{8,0},{12,4},{1,9},{5,13},{9,1},{13,5},{2,10},{6,14},... | collective-permute-start | bytes 1806344 | tf_op jit(solution)/shard_map/ppermute | solution.py:439
  231.9 32.7 %collective-permute-start.34 = (bf16[3,112,896]{2,1,0:T(8,128)(2,1)}, bf16[3,112,896]{2,1,0:T(8,128)(2,1)}, u32[]{:S(2)}, u32[]{:S(2)}) collective-permute-start(bf16[3,112,896]{2,1,0:T(8,128)(2,1)} %broadcast_select_fusion.1), channel_id=1, source_target_pairs={{0,4},{4,0},{8,12},{12,8},{1,5},{5,1},{9,13},{13,9},{2,6},{6,2},{1... | collective-permute-start | bytes 1806344 | tf_op jit(solution)/shard_map/ppermute | solution.py:439
  235.3 5.0 %collective-permute-start.31 = (f32[3,1536]{1,0:T(4,128)}, f32[3,1536]{1,0:T(4,128)}, u32[]{:S(2)}, u32[]{:S(2)}) collective-permute-start(f32[3,1536]{1,0:T(4,128)} %reshape.547), channel_id=1, source_target_pairs={{0,2},{1,3},{2,0},{3,1},{4,6},{5,7},{6,4},{7,5},{8,10},{9,11},{10,... | collective-permute-start | bytes 55304 | tf_op jit(solution)/shard_map/ppermute | solution.py:439
  241.8 6.3 %collective-permute-start.32 = (bf16[64,1792]{1,0:T(8,128)(2,1)S(1)}, bf16[64,1792]{1,0:T(8,128)(2,1)S(1)}, u32[]{:S(2)}, u32[]{:S(2)}) collective-permute-start(bf16[64,1792]{1,0:T(8,128)(2,1)S(1)} %copy-done.23), channel_id=1, source_target_pairs={{0,1},{1,0},{2,3},{3,2},{4,5},{5,4},{6,7},{7,6},{8,9},{9,8},{10,11... | collective-permute-start | bytes 688136 | tf_op jit(solution)/shard_map/ppermute | solution.py:439
  248.7 15.9 %copy-start.13 = (bf16[1,3,112,896]{3,2,1,0:T(8,128)(2,1)S(1)}, bf16[1,3,112,896]{3,2,1,0:T(8,128)(2,1)}, u32[]{:S(2)}) copy-start(bf16[1,3,112,896]{3,2,1,0:T(8,128)(2,1)} %fusion.20) | copy-start | bytes 1806340
  264.6 2.4 copy-start.27
  266.6 15.9 %copy-start.4 = (bf16[4,3,112,896]{3,2,1,0:T(8,128)(2,1)}, bf16[4,3,112,896]{3,2,1,0:T(8,128)(2,1)S(1)}, u32[]{:S(2)}) copy-start(bf16[4,3,112,896]{3,2,1,0:T(8,128)(2,1)S(1)} %maximum_select_fusion.3.near_ref) | copy-start | bytes 7225348
  266.6 15.9 %collective-permute-start.37 = (bf16[4,3,112,896]{3,2,1,0:T(8,128)(2,1)S(1)}, bf16[4,3,112,896]{3,2,1,0:T(8,128)(2,1)}, u32[]{:S(2)}, u32[]{:S(2)}) collective-permute-start(bf16[4,3,112,896]{3,2,1,0:T(8,128)(2,1)S(1)} %maximum_select_fusion.3.near_ref), channel_id=1, source_target_pairs={{0,16},{16,0},{1,17},{17,1},{2,18},{18,2},{3,19},{19,3},{4,20},{20... | collective-permute-start | bytes 7225352 | tf_op jit(solution)/shard_map/ppermute | solution.py:439
  266.7 15.8 %collective-permute-start.33 = (bf16[2,256,512]{2,1,0:T(8,128)(2,1)S(1)}, bf16[2,256,512]{2,1,0:T(8,128)(2,1)S(1)}, u32[]{:S(2)}, u32[]{:S(2)}) collective-permute-start(bf16[2,256,512]{2,1,0:T(8,128)(2,1)S(1)} %copy-done.15), channel_id=1, source_target_pairs={{0,1},{1,0},{2,3},{3,2},{4,5},{5,4},{6,7},{7,6},{8,9},{9,8},{10,11... | collective-permute-start | bytes 1572872 | tf_op jit(solution)/shard_map/ppermute | solution.py:439
  290.0 29.2 %copy-start.1 = (bf16[64,4,1792]{2,1,0:T(4,128)(2,1)S(1)}, bf16[64,4,1792]{2,1,0:T(4,128)(2,1)}, u32[]{:S(2)}) copy-start(bf16[64,4,1792]{2,1,0:T(4,128)(2,1)} %param.17) | copy-start | bytes 2752516
  (5 other events, 7.5 us)

commit v11 on v9

--- a/solution.py
+++ b/solution.py
@@ -215,8 +215,7 @@
     x_ref,
     gain_ref,
     residual_ref,
-    low_ref,
-    high_ref,
+    normed_ref,
     tail_ref,
     tokens_ref,
     total_ref,
@@ -263,9 +262,7 @@
         residual = (tokens_ref[...].astype(F32) + total_ref[...]).astype(BF16)
         residual_ref[...] = residual
         normed = normed_rows(residual.astype(F32), gain_ref[...])
-        mid = low_ref.shape[0]
-        low_ref[...] = normed[:mid]
-        high_ref[...] = normed[mid:]
+        normed_ref[...] = normed
         tail_ref[...] = normed[normed.shape[0] - HALO :]
 
 
@@ -273,8 +270,7 @@
     heads,
     place_ref,
     first_ref,
-    low_ref,
-    high_ref,
+    x_ref,
     halo_ref,
     own_ref,
     near_ref,
@@ -289,12 +285,11 @@
     step = pl.program_id(0)
     targets = [(own_ref, kind, w_ref, kind * SLOT) for kind in range(3)]
     pieces = [(HEAD, w_ref, kind * SLOT) for kind in range(3)]
-    mid = low_ref.shape[0]
 
     groups = w_ref.shape[0]
     loads = [
         (pltpu.make_async_copy(src, rows_ref.at[at : at + src.shape[0], :], sems.at[groups, n]), 0)
-        for n, (src, at) in enumerate(((halo_ref, 0), (low_ref, HALO), (high_ref, HALO + mid)))
+        for n, (src, at) in enumerate(((halo_ref, 0), (x_ref, HALO)))
     ]
 
     @pl.when(step == 0)
@@ -306,7 +301,7 @@
         groups,
         loads,
     )
-    rows = mid + high_ref.shape[0]
+    rows = x_ref.shape[0]
     lead = HALO - WINDOW
     projected = project(rows_ref, w_ref, step)
     taps = tap_ref[0]
@@ -521,7 +516,15 @@
     featmap_t = w_featmap.transpose(1, 2, 0).reshape(2, heads, feature_dim, width)
     window_t = w_window.transpose(1, 2, 0).reshape(3, heads, HEAD, width)
     out_one, out_two = (w.reshape(1, heads, HEAD, width) for w in (w_out_one, w_out_two))
-    held_one = settled(jnp.stack(from_groups(own_piece([values_t, featmap_t]), ())))
+    places = jnp.concatenate([(seq_place % NEAR) ^ jnp.arange(NEAR), dp_place[None]])
+    places = places.astype(jnp.int32)
+    taps = conv_window.reshape(tap_count, 3, heads, HEAD).transpose(0, 2, 1, 3)
+    taps = jnp.take(taps, places[:NEAR], axis=1, mode="clip")
+    taps = jnp.pad(taps, ((0, 0), (0, 0), (0, 0), (0, SLOT - HEAD)))
+    taps = taps.reshape(tap_count, 3 * heads * SLOT)
+    taps = settled(jnp.stack([taps, across(taps, "tensor", 2)]))
+    held_one = from_groups(own_piece([values_t, featmap_t]), ())
+    held_one = settled(jnp.stack(held_one), (taps,))
 
     placed = reassign[:, None] == jnp.arange(slots_total, dtype=jnp.int32)[None, :]
     table = jnp.sum(jnp.where(placed[:, :, None], page_table[None], 0), axis=1)
@@ -558,14 +561,6 @@
     near_one = from_plane(held_one, neighbours(held_one), (swapped,), (held_out_one,))
     out_piece = after(own_piece([out_two]), (swapped,))
     beyond = from_group(own_piece([window_t, out_two]), (swapped,))
-    places = jnp.concatenate([(seq_place % NEAR) ^ jnp.arange(NEAR), dp_place[None]])
-    places = places.astype(jnp.int32)
-    taps = conv_window.reshape(tap_count, 3, heads, HEAD).transpose(0, 2, 1, 3)
-    taps = jnp.take(taps, places[:NEAR], axis=1, mode="clip")
-    taps = jnp.pad(taps, ((0, 0), (0, 0), (0, 0), (0, SLOT - HEAD)))
-    taps = taps.reshape(tap_count, 3 * heads * SLOT)
-    taps = jnp.stack([taps, across(taps, "tensor", 2)])
-
     first, second, ones, scale, kept = feature_tables(heads, feature_dim)
     first, second = jnp.asarray(first, BF16), jnp.asarray(second, BF16)
     column = np.zeros((1, heads * SLOT), np.float32)
@@ -578,7 +573,6 @@
         return pltpu.VMEM((group_count, heads, rows_of_head, width), BF16)
 
     slots = heads * SLOT
-    mid = 3 * rows // 4
     num, queries, state = call(
         functools.partial(linear_kernel, heads, feature_dim, kept),
         group_count,
@@ -619,7 +613,7 @@
     )
     held_window = after(held_window, (prior,))
     near_by_window = neighbours(held_window)
-    residual, low, high, tail = call(
+    residual, normed_two, tail = call(
         functools.partial(out_one_kernel, heads, kept),
         group_count,
         [
@@ -634,8 +628,8 @@
         + [each((heads * kept, SLOT))]
         + [HBM] * 4
         + [whole((1, width))],
-        [whole((n, width)) for n in (rows, mid, rows - mid, HALO)],
-        [jax.ShapeDtypeStruct((n, width), BF16) for n in (rows, mid, rows - mid, HALO)],
+        [whole((n, width)) for n in (rows, rows, HALO)],
+        [jax.ShapeDtypeStruct((n, width), BF16) for n in (rows, rows, HALO)],
         [
             pltpu.VMEM((rows, width), BF16),
             pltpu.VMEM((rows, width), F32),
@@ -650,7 +644,7 @@
     )
 
     halo = lax.ppermute(tail, "seq", [(i, i + 1) for i in range(seq_count - 1)])
-    pair_low, pair_high = across(low, "tensor", 1), across(high, "tensor", 1)
+    pair_rows = across(normed_two, "tensor", 1)
     pair_halo = lax.ppermute(
         tail,
         ("seq", "tensor"),
@@ -660,18 +654,18 @@
             for j in range(group_count)
         ],
     )
-    near_window = from_plane(held_window, near_by_window, (residual,), (pair_low, pair_halo))
-    held_out_two = after(held_out_two, (residual,))
+    near_window = from_plane(held_window, near_by_window, (residual,), (pair_rows, pair_halo))
+    held_out_two = after(held_out_two, (halo,))
     block_start = (seq_place * rows).astype(jnp.int32)[None]
 
-    def window_rows(slot_low, slot_high, slot_halo, earlier):
+    def window_rows(slot_rows, slot_halo, earlier):
         return call(
             functools.partial(window_kernel, heads),
             2,
             [
                 SMEM,
                 SMEM,
-                *[HBM] * 6,
+                *[HBM] * 5,
                 each((tap_count, 3 * slots)),
                 HBM,
             ],
@@ -683,11 +677,11 @@
                 copy_sems(3),
             ],
             "window_rows",
-        )(places, block_start, slot_low, slot_high, slot_halo, window_t, *near_window, taps, earlier)
-
-    mixed_pair = window_rows(pair_low, pair_high, pair_halo, halo)
+        )(places, block_start, slot_rows, slot_halo, window_t, *near_window, taps, earlier)
+
+    mixed_pair = window_rows(pair_rows, pair_halo, normed_two)
     near_out_two = from_plane(held_out_two, neighbours(held_out_two), None, (mixed_pair,))
-    mixed_own = window_rows(low, high, halo, mixed_pair)
+    mixed_own = window_rows(normed_two, halo, mixed_pair)
     mixed_pair = across(mixed_pair, "tensor", 1)
     live = (length - seq_place * rows).astype(jnp.int32)[None]
     result = call(

time: 320 us -> 303 us (0.947)
  waiting for transfers between devices: 107 us -> 94.9 us
  starting transfers between devices: 59 us -> 55.6 us
    ppermute x1, waiting for transfers between devices: 22 us -> 6.7 us  [on_device(): halo = lax.ppermute(tail, 'seq', [(i, i + 1) for i in range(seq_count - 1)])]
    ppermute x32 -> x31, waiting for transfers between devices: 44 us -> 41 us  [across(): lax.ppermute(array, axis, [(i, i ^ bit) for i in range(lax.axis_size(axis...]
    slice x12 -> x14, local copies, waits for them, and re-layouts: 9.29 us -> 10.2 us  [after(): lax.slice(other, (0,) * other.ndim, (1,) * other.ndim)]
    ppermute x32 -> x31, starting transfers between devices: 30.8 us -> 30.6 us  [across(): lax.ppermute(array, axis, [(i, i ^ bit) for i in range(lax.axis_size(axis...]
    select_n x20 -> x21, other arithmetic: 19.8 us -> 20 us  [after(): return jnp.where(zero == 0.0, array, jnp.zeros_like(array))]
  transfers between devices with their start and end apart: 39 -> 38, of which waited for: 13 -> 16; matrix products, arithmetic and copies ran while one was open for 11% -> 13% of each run, Pallas kernels for 16% -> 17%
where the time goes in v11:
time: 303 us; the launch traced here: 302 us
  waiting for transfers between devices  94.9 us (31%)
  Pallas kernels  57.7 us (19%)
  starting transfers between devices  55.6 us (18%)
  local copies, waits for them, and re-layouts  31.2 us (10%)
  other arithmetic  26.9 us (9%)
  blocking collectives  26 us (9%)
  between operations  9.87 us (3%)
    ppermute x31, waiting for transfers between devices, across(): lax.ppermute(array, axis, [(i, i ^ bit) for i in range(lax.axis_size(axis...  41 us
    ppermute x31, starting transfers between devices, across(): lax.ppermute(array, axis, [(i, i ^ bit) for i in range(lax.axis_size(axis...  30.6 us
    pallas_call x2, Pallas kernels, window_rows(): call(functools.partial(window_kernel, heads), 2, [SMEM, SMEM, *[HBM] * 5,...  28.2 us
    all_to_all x1, blocking collectives, on_device(): lax.all_to_all(result, 'tensor', split_axis=0, concat_axis=0, tiled=True)  26 us
    all_to_all x1, waiting for transfers between devices, on_device(): lax.all_to_all(picked, 'tensor', split_axis=0, concat_axis=0, tiled=True)  20.7 us
    select_n x21, other arithmetic, after(): return jnp.where(zero == 0.0, array, jnp.zeros_like(array))  20 us
    ppermute x1, waiting for transfers between devices, on_device(): lax.ppermute(tail, ('seq', 'tensor'), [(i * group_count + j, (i + 1) * gr...  17.2 us
    pallas_call x1, Pallas kernels, on_device(): call(functools.partial(linear_kernel, heads, feature_dim, kept), group_co...  12.4 us
  transfers between devices with their start and end apart: 38, of which 16 were waited for; matrix products, arithmetic and copies ran while one was open for 13% of the time, Pallas kernels for 17%

profile of v11, /device:TPU:0, one launch (start us, length us, event | category | flops | bytes accessed | tf_op | source)
XLA Modules:
  0.0 302.1 jit_solution(232992098286819166)
XLA Ops:
  1.9 4.1 %collective-permute-start.2 = (bf16[144,896]{1,0:T(8,128)(2,1)S(1)}, bf16[144,896]{1,0:T(8,128)(2,1)S(1)}, u32[]{:S(2)}, u32[]{:S(2)}) collective-permute-start(bf16[144,896]{1,0:T(8,128)(2,1)S(1)} %pad_maximum_fusion.1), channel_id=1, source_target_pairs={{0,2},{1,3},{2,0},{3,1},{4,6},{5,7},{6,4},{7,5},{8,10},{9,11},{10,... | collective-permute-start | bytes 774152 | tf_op jit(solution)/shard_map/ppermute | solution.py:425
  6.0 1.6 collective-permute-start.1
  10.0 2.2 gather_fusion.1
  12.2 3.7 %all-to-all-start = ((bf16[8,8,4,1792]{3,2,1,0:T(4,128)(2,1)}), bf16[8,8,4,1792]{3,2,1,0:T(4,128)(2,1)S(1)}, u32[]{:S(2)}, u32[]{:S(2)}) async-start(bf16[8,8,4,1792]{3,2,1,0:T(4,128)(2,1)} %bitcast.20), calls=%async_computation | async-start | bytes 1835008 | tf_op jit(solution)/shard_map/all_to_all | solution.py:548
  18.6 3.1 %collective-permute-done = f32[3,1536]{1,0:T(4,128)S(1)} collective-permute-done((f32[3,1536]{1,0:T(4,128)S(1)}, f32[3,1536]{1,0:T(4,128)S(1)}, u32[]{:S(2)}, u32[]{:S(2)}) %collective-permute-start) | collective-permute-done | bytes 18464 | tf_op jit(solution)/shard_map/ppermute | solution.py:425
  22.8 3.4 %collective-permute-done.3 = bf16[144,896]{1,0:T(8,128)(2,1)S(1)} collective-permute-done((bf16[144,896]{1,0:T(8,128)(2,1)S(1)}, bf16[144,896]{1,0:T(8,128)(2,1)S(1)}, u32[]{:S(2)}, u32[]{:S(2)}) %collective-permute-start.3) | collective-permute-done | bytes 258080 | tf_op jit(solution)/shard_map/ppermute | solution.py:425
  27.6 1.8 all-to-all-done
  29.4 1.3 gather_fusion.2
  32.2 3.5 %all-to-all-start.1 = ((bf16[4,16,4,1792]{3,1,2,0:T(8,128)(2,1)}), bf16[4,16,4,1792]{3,1,2,0:T(8,128)(2,1)S(1)}, u32[]{:S(2)}, u32[]{:S(2)}) async-start(bf16[4,16,4,1792]{3,1,2,0:T(8,128)(2,1)} %copy.47), calls=%async_computation.1 | async-start | bytes 1835008 | tf_op jit(solution)/shard_map/all_to_all | solution.py:555
  35.7 1.1 collective-permute-start.8
  36.8 1.0 collective-permute-start.7
  38.9 1.6 select_bitcast_fusion.1
  40.6 2.9 collective-permute-start.5
  43.5 20.7 %all-to-all-done.1 = bf16[4,16,4,1792]{3,1,2,0:T(8,128)(2,1)S(1)} async-done(((bf16[4,16,4,1792]{3,1,2,0:T(8,128)(2,1)}), bf16[4,16,4,1792]{3,1,2,0:T(8,128)(2,1)S(1)}, u32[]{:S(2)}, u32[]{:S(2)}) %all-to-all-start.1) | async-done | bytes 917536 | tf_op jit(solution)/shard_map/all_to_all | solution.py:555
  65.5 1.1 collective-permute-start.9
  66.6 1.0 slice_select_fusion.3
  68.3 2.0 collective-permute-start.6
  70.3 4.9 %collective-permute-done.4 = bf16[112,896]{1,0:T(8,128)(2,1)S(1)} collective-permute-done((bf16[112,896]{1,0:T(8,128)(2,1)}, bf16[112,896]{1,0:T(8,128)(2,1)S(1)}, u32[]{:S(2)}, u32[]{:S(2)}) %collective-permute-start.4) | collective-permute-done | bytes 200736 | tf_op jit(solution)/shard_map/ppermute | solution.py:425
  75.2 2.1 collective-permute-done.6
  77.4 1.8 pad_maximum_fusion
  79.2 1.2 slice.109
  81.3 1.7 maximum_select_fusion.near_ref
  83.1 2.1 constant_dynamic-slice_fusion
  86.2 1.0 maximum_select_fusion.4
  88.1 1.4 collective-permute-start.18
  90.2 1.7 collective-permute-start.19
  91.9 1.4 copy.48
  93.3 2.4 reshape.543.x_ref
  95.7 12.4 %linear_rows.1 = (f32[4,256,512]{2,1,0:T(8,128)}, bf16[4,256,128]{2,1,0:T(8,128)(2,1)}, bf16[4,640,128]{2,1,0:T(8,128)(2,1)}) custom-call(s32[5]{0:T(128)} %pad_add_fusion.place_ref, bf16[256,1792]{1,0:T(8,128)(2,1)} %reshape.543.x_ref, f32[1,1792]{1,0:T(1,128)} %broadcast_in_dim.128.gain_ref, bf16[1,4,112,1792]{3,2,1,0:T(8,128)(2,1)} %bitcast.100, ...), custom_call_target="tpu_custom_call" | custom-call | tf_op jit(solution)/shard_map/linear_rows/pallas_call | solution.py:576
  108.1 2.3 collective-permute-start.14
  110.4 1.3 collective-permute-start.13
  111.8 1.2 slice.85
  113.5 11.2 %collective-permute-done.15 = bf16[448,896]{1,0:T(8,128)(2,1)} collective-permute-done((bf16[448,896]{1,0:T(8,128)(2,1)}, bf16[448,896]{1,0:T(8,128)(2,1)}, u32[]{:S(2)}, u32[]{:S(2)}) %collective-permute-start.15) | collective-permute-done | bytes 802848 | tf_op jit(solution)/shard_map/ppermute | solution.py:425
  124.7 3.5 %collective-permute-start.12 = (bf16[4,640,128]{2,1,0:T(8,128)(2,1)}, bf16[4,640,128]{2,1,0:T(8,128)(2,1)S(1)}, u32[]{:S(2)}, u32[]{:S(2)}) collective-permute-start(bf16[4,640,128]{2,1,0:T(8,128)(2,1)} %get-tuple-element.13), channel_id=1, source_target_pairs={{0,4},{4,8},{8,12},{1,5},{5,9},{9,13},{2,6},{6,10},{10,14},{3,7},{... | collective-permute-start | bytes 1966088 | tf_op jit(solution)/shard_map/ppermute | solution.py:474
  128.3 1.2 select_bitcast_fusion
  131.1 1.7 collective-permute-start.21
  132.8 1.0 slice_select_fusion.2
  133.9 2.0 collective-permute-start.17
  136.0 7.5 %collective-permute-done.12 = bf16[4,640,128]{2,1,0:T(8,128)(2,1)S(1)} collective-permute-done((bf16[4,640,128]{2,1,0:T(8,128)(2,1)}, bf16[4,640,128]{2,1,0:T(8,128)(2,1)S(1)}, u32[]{:S(2)}, u32[]{:S(2)}) %collective-permute-start.12) | collective-permute-done | bytes 655392 | tf_op jit(solution)/shard_map/ppermute | solution.py:474
  146.7 2.3 collective-permute-done.21
  149.1 2.9 collective-permute-done.20
  152.1 1.9 maximum_select_fusion.1.near_ref
  154.1 1.0 slice_select_fusion
  155.1 2.0 collective-permute-start.26
  158.7 1.5 copy-done.11
  160.2 10.4 %linear_out.1 = (bf16[256,1792]{1,0:T(8,128)(2,1)}, bf16[256,1792]{1,0:T(8,128)(2,1)}, bf16[80,1792]{1,0:T(8,128)(2,1)}) custom-call(s32[5]{0:T(128)} %pad_add_fusion.place_ref, f32[4,256,512]{2,1,0:T(8,128)} %get-tuple-element.11.num_ref, bf16[4,256,128]{2,1,0:T(8,128)(2,1)} %get-tuple-element.12.q_ref, bf16[128,1024]{1,0:T(8,128)(2,1)} %constant.131.clone.first_ref, ...), custom_call_target="tpu_custom_call" | custom-call | tf_op jit(solution)/shard_map/linear_out/pallas_call | solution.py:616
  170.7 1.2 slice.95
  172.6 1.0 slice_select_fusion.4
  173.9 5.1 %collective-permute-start.25 = (bf16[80,1792]{1,0:T(8,128)(2,1)}, bf16[80,1792]{1,0:T(8,128)(2,1)S(1)}, u32[]{:S(2)}, u32[]{:S(2)}) collective-permute-start(bf16[80,1792]{1,0:T(8,128)(2,1)} %get-tuple-element.15), channel_id=1, source_target_pairs={{0,5},{1,4},{2,7},{3,6},{4,9},{5,8},{6,11},{7,10},{8,13},{9,12},{1... | collective-permute-start | bytes 860168 | tf_op jit(solution)/shard_map/ppermute | solution.py:648
  180.2 17.2 %collective-permute-done.25.halo_ref = bf16[80,1792]{1,0:T(8,128)(2,1)S(1)} collective-permute-done((bf16[80,1792]{1,0:T(8,128)(2,1)}, bf16[80,1792]{1,0:T(8,128)(2,1)S(1)}, u32[]{:S(2)}, u32[]{:S(2)}) %collective-permute-start.25) | collective-permute-done | bytes 286752 | tf_op jit(solution)/shard_map/ppermute | solution.py:648
  199.8 1.7 maximum_select_fusion.2.near_ref
  201.6 5.5 %collective-permute-start.23 = (bf16[80,1792]{1,0:T(8,128)(2,1)S(1)}, bf16[80,1792]{1,0:T(8,128)(2,1)S(1)}, u32[]{:S(2)}, u32[]{:S(2)}) collective-permute-start(bf16[80,1792]{1,0:T(8,128)(2,1)S(1)} %copy-done.23), channel_id=1, source_target_pairs={{0,4},{4,8},{8,12},{1,5},{5,9},{9,13},{2,6},{6,10},{10,14},{3,7},{... | collective-permute-start | bytes 860168 | tf_op jit(solution)/shard_map/ppermute | solution.py:646
  207.1 6.7 %collective-permute-done.23.halo_ref = bf16[80,1792]{1,0:T(8,128)(2,1)S(1)} collective-permute-done((bf16[80,1792]{1,0:T(8,128)(2,1)S(1)}, bf16[80,1792]{1,0:T(8,128)(2,1)S(1)}, u32[]{:S(2)}, u32[]{:S(2)}) %collective-permute-start.23) | collective-permute-done | bytes 286752 | tf_op jit(solution)/shard_map/ppermute | solution.py:646
  216.5 1.9 collective-permute-start.34
  218.5 2.0 collective-permute-start.33
  222.0 14.2 %window_rows.2._ = bf16[2,256,512]{2,1,0:T(8,128)(2,1)} custom-call(s32[5]{0:T(128)} %pad_add_fusion.place_ref, s32[1]{0:T(128)} %bitcast.2.first_ref, bf16[256,1792]{1,0:T(8,128)(2,1)} %copy-done.15, bf16[80,1792]{1,0:T(8,128)(2,1)} %copy-done.18, bf16[3,4,112,1792]{3,2,1,0:T(8,128)(2,1)} %bitcast.90, bf16[4,1,336,896]{3,2,1,0:T(8,128)(2,1)} %copy-done.2, ...), custom_call_target="tpu_custom_call" | custom-call | tf_op jit(solution)/shard_map/window_rows/pallas_call | solution.py:662
  236.2 1.2 slice.124
  238.1 8.1 %collective-permute-done.33 = bf16[3,112,896]{2,1,0:T(8,128)(2,1)} collective-permute-done((bf16[3,112,896]{2,1,0:T(8,128)(2,1)}, bf16[3,112,896]{2,1,0:T(8,128)(2,1)}, u32[]{:S(2)}, u32[]{:S(2)}) %collective-permute-start.33) | collective-permute-done | bytes 602144 | tf_op jit(solution)/shard_map/ppermute | solution.py:425
  246.1 1.4 collective-permute-done.32
  247.5 1.9 maximum_select_fusion.3.near_ref
  251.4 14.1 %window_rows.3.mixed_ref = bf16[2,256,512]{2,1,0:T(8,128)(2,1)} custom-call(s32[5]{0:T(128)} %pad_add_fusion.place_ref, s32[1]{0:T(128)} %bitcast.2.first_ref, bf16[256,1792]{1,0:T(8,128)(2,1)} %get-tuple-element.14._.x_ref, bf16[80,1792]{1,0:T(8,128)(2,1)} %copy-done.19, bf16[3,4,112,1792]{3,2,1,0:T(8,128)(2,1)} %bitcast.91, ...), custom_call_target="tpu_custom_call" | custom-call | tf_op jit(solution)/shard_map/window_rows/pallas_call | solution.py:662
  266.3 6.7 %window_out.1 = bf16[256,1792]{1,0:T(8,128)(2,1)} custom-call(s32[5]{0:T(128)} %pad_add_fusion.place_ref, s32[1]{0:T(128)} %bitcast.1.live_ref, bf16[2,256,512]{2,1,0:T(8,128)(2,1)} %window_rows.3.mixed_ref, bf16[2,256,512]{2,1,0:T(8,128)(2,1)} %copy-done.16, bf16[1,4,112,1792]{3,2,1,0:T(8,128)(2,1)} %bitcast.104, bf16[4,3,112,896]{3,2,1,0:T(8,128)(2,1)} %copy-done.4, ...), custom_call_target="tpu_custom_call" | custom-call | tf_op jit(solution)/shard_map/window_out/pallas_call | solution.py:687
  273.0 1.9 reshape.549
  275.2 26.0 %all_to_all.15 = bf16[4,16,4,1792]{3,2,1,0:T(4,128)(2,1)S(1)} all-to-all(bf16[4,16,4,1792]{3,2,1,0:T(4,128)(2,1)S(1)} %bitcast.95), channel_id=1, replica_groups=mesh['dp'=2,'seq'=4,'tensor'=4] {'tensor'}, dimensions={0} | all-to-all | bytes 1835008 | tf_op jit(solution)/shard_map/all_to_all | solution.py:708
  (159 shorter events, 28.9 us)
Async XLA Ops:
  0.0 9.9 %copy-start = (bf16[64,4,1792]{2,1,0:T(4,128)(2,1)S(1)}, bf16[64,4,1792]{2,1,0:T(4,128)(2,1)}, u32[]{:S(2)}) copy-start(bf16[64,4,1792]{2,1,0:T(4,128)(2,1)} %param.17) | copy-start | bytes 2752516
  0.9 15.0 %copy-start.20 = (f32[3,3,448]{2,1,0:T(4,128)S(1)}, f32[3,3,448]{2,1,0:T(4,128)}, u32[]{:S(2)}) copy-start(f32[3,3,448]{2,1,0:T(4,128)} %param.27) | copy-start | bytes 48388
  1.9 16.0 %collective-permute-start.2 = (bf16[144,896]{1,0:T(8,128)(2,1)S(1)}, bf16[144,896]{1,0:T(8,128)(2,1)S(1)}, u32[]{:S(2)}, u32[]{:S(2)}) collective-permute-start(bf16[144,896]{1,0:T(8,128)(2,1)S(1)} %pad_maximum_fusion.1), channel_id=1, source_target_pairs={{0,2},{1,3},{2,0},{3,1},{4,6},{5,7},{6,4},{7,5},{8,10},{9,11},{10,... | collective-permute-start | bytes 774152 | tf_op jit(solution)/shard_map/ppermute | solution.py:425
  6.0 16.8 %collective-permute-start.1 = (bf16[144,896]{1,0:T(8,128)(2,1)S(1)}, bf16[144,896]{1,0:T(8,128)(2,1)S(1)}, u32[]{:S(2)}, u32[]{:S(2)}) collective-permute-start(bf16[144,896]{1,0:T(8,128)(2,1)S(1)} %pad_maximum_fusion.1), channel_id=1, source_target_pairs={{0,1},{1,0},{2,3},{3,2},{4,5},{5,4},{6,7},{7,6},{8,9},{9,8},{10,11... | collective-permute-start | bytes 774152 | tf_op jit(solution)/shard_map/ppermute | solution.py:425
  12.2 17.2 %all-to-all-start = ((bf16[8,8,4,1792]{3,2,1,0:T(4,128)(2,1)}), bf16[8,8,4,1792]{3,2,1,0:T(4,128)(2,1)S(1)}, u32[]{:S(2)}, u32[]{:S(2)}) async-start(bf16[8,8,4,1792]{3,2,1,0:T(4,128)(2,1)} %bitcast.20), calls=%async_computation | async-start | bytes 1835008 | tf_op jit(solution)/shard_map/all_to_all | solution.py:548
  16.6 5.0 %collective-permute-start = (f32[3,1536]{1,0:T(4,128)S(1)}, f32[3,1536]{1,0:T(4,128)S(1)}, u32[]{:S(2)}, u32[]{:S(2)}) collective-permute-start(f32[3,1536]{1,0:T(4,128)S(1)} %reshape.533), channel_id=1, source_target_pairs={{0,2},{1,3},{2,0},{3,1},{4,6},{5,7},{6,4},{7,5},{8,10},{9,11},{10,... | collective-permute-start | bytes 55304 | tf_op jit(solution)/shard_map/ppermute | solution.py:425
  17.9 8.4 %collective-permute-start.3 = (bf16[144,896]{1,0:T(8,128)(2,1)S(1)}, bf16[144,896]{1,0:T(8,128)(2,1)S(1)}, u32[]{:S(2)}, u32[]{:S(2)}) collective-permute-start(bf16[144,896]{1,0:T(8,128)(2,1)S(1)} %collective-permute-done.2), channel_id=1, source_target_pairs={{0,1},{1,0},{2,3},{3,2},{4,5},{5,4},{6,7},{7,6},{8,9},{9,8},{10,11... | collective-permute-start | bytes 774152 | tf_op jit(solution)/shard_map/ppermute | solution.py:425
  21.7 9.4 %copy-start.17 = (f32[2,3,1536]{2,1,0:T(4,128)}, f32[2,3,1536]{2,1,0:T(4,128)S(1)}, u32[]{:S(2)}) copy-start(f32[2,3,1536]{2,1,0:T(4,128)S(1)} %pad_maximum_fusion.2.tap_ref) | copy-start | bytes 110596
  26.4 10.4 %copy-start.9 = (bf16[3,144,896]{2,1,0:T(8,128)(2,1)}, bf16[3,144,896]{2,1,0:T(8,128)(2,1)S(1)}, u32[]{:S(2)}) copy-start(bf16[3,144,896]{2,1,0:T(8,128)(2,1)S(1)} %maximum_select_fusion.5) | copy-start | bytes 2322436
  32.2 32.1 %all-to-all-start.1 = ((bf16[4,16,4,1792]{3,1,2,0:T(8,128)(2,1)}), bf16[4,16,4,1792]{3,1,2,0:T(8,128)(2,1)S(1)}, u32[]{:S(2)}, u32[]{:S(2)}) async-start(bf16[4,16,4,1792]{3,1,2,0:T(8,128)(2,1)} %copy.47), calls=%async_computation.1 | async-start | bytes 1835008 | tf_op jit(solution)/shard_map/all_to_all | solution.py:555
  35.7 29.8 %collective-permute-start.8 = (bf16[3,144,896]{2,1,0:T(8,128)(2,1)S(1)}, bf16[3,144,896]{2,1,0:T(8,128)(2,1)S(1)}, u32[]{:S(2)}, u32[]{:S(2)}) collective-permute-start(bf16[3,144,896]{2,1,0:T(8,128)(2,1)S(1)} %maximum_select_fusion.5), channel_id=1, source_target_pairs={{0,8},{4,12},{8,0},{12,4},{1,9},{5,13},{9,1},{13,5},{2,10},{6,14},... | collective-permute-start | bytes 2322440 | tf_op jit(solution)/shard_map/ppermute | solution.py:425
  36.8 29.8 %collective-permute-start.7 = (bf16[3,144,896]{2,1,0:T(8,128)(2,1)S(1)}, bf16[3,144,896]{2,1,0:T(8,128)(2,1)}, u32[]{:S(2)}, u32[]{:S(2)}) collective-permute-start(bf16[3,144,896]{2,1,0:T(8,128)(2,1)S(1)} %maximum_select_fusion.5), channel_id=1, source_target_pairs={{0,4},{4,0},{8,12},{12,8},{1,5},{5,1},{9,13},{13,9},{2,6},{6,2},{1... | collective-permute-start | bytes 2322440 | tf_op jit(solution)/shard_map/ppermute | solution.py:425
  40.6 27.7 %collective-permute-start.5 = (bf16[112,896]{1,0:T(8,128)(2,1)}, bf16[112,896]{1,0:T(8,128)(2,1)}, u32[]{:S(2)}, u32[]{:S(2)}) collective-permute-start(bf16[112,896]{1,0:T(8,128)(2,1)} %select_bitcast_fusion.1), channel_id=1, source_target_pairs={{0,2},{1,3},{2,0},{3,1},{4,6},{5,7},{6,4},{7,5},{8,10},{9,11},{10,... | collective-permute-start | bytes 602120 | tf_op jit(solution)/shard_map/ppermute | solution.py:425
  64.2 17.0 %copy-start.7 = (bf16[4,16,4,1792]{3,1,2,0:T(8,128)(2,1)}, bf16[4,16,4,1792]{3,1,2,0:T(8,128)(2,1)S(1)}, u32[]{:S(2)}) copy-start(bf16[4,16,4,1792]{3,1,2,0:T(8,128)(2,1)S(1)} %all-to-all-done.1) | copy-start | bytes 2752516
  64.2 17.0 %copy-start.10 = (bf16[3,144,896]{2,1,0:T(8,128)(2,1)S(1)}, bf16[3,144,896]{2,1,0:T(8,128)(2,1)}, u32[]{:S(2)}) copy-start(bf16[3,144,896]{2,1,0:T(8,128)(2,1)} %copy-done.9) | copy-start | bytes 2322436
  65.5 15.8 %copy-start.14 = (bf16[3,144,896]{2,1,0:T(8,128)(2,1)}, bf16[3,144,896]{2,1,0:T(8,128)(2,1)S(1)}, u32[]{:S(2)}) copy-start(bf16[3,144,896]{2,1,0:T(8,128)(2,1)S(1)} %collective-permute-done.8) | copy-start | bytes 2322436
  65.5 15.6 %collective-permute-start.9 = (bf16[3,80,896]{2,1,0:T(8,128)(2,1)S(1)}, bf16[3,80,896]{2,1,0:T(8,128)(2,1)S(1)}, u32[]{:S(2)}, u32[]{:S(2)}) collective-permute-start(bf16[3,80,896]{2,1,0:T(8,128)(2,1)S(1)} %slice_select_fusion.1), channel_id=1, source_target_pairs={{0,4},{4,0},{8,12},{12,8},{1,5},{5,1},{9,13},{13,9},{2,6},{6,2},{1... | collective-permute-start | bytes 1290248 | tf_op jit(solution)/shard_map/ppermute | solution.py:425
  67.6 13.4 %collective-permute-start.10 = (bf16[3,64,896]{2,1,0:T(8,128)(2,1)S(1)}, bf16[3,64,896]{2,1,0:T(8,128)(2,1)S(1)}, u32[]{:S(2)}, u32[]{:S(2)}) collective-permute-start(bf16[3,64,896]{2,1,0:T(8,128)(2,1)S(1)} %slice_select_fusion.3), channel_id=1, source_target_pairs={{0,8},{4,12},{8,0},{12,4},{1,9},{5,13},{9,1},{13,5},{2,10},{6,14},... | collective-permute-start | bytes 1032200 | tf_op jit(solution)/shard_map/ppermute | solution.py:425
  68.3 6.9 %collective-permute-start.4 = (bf16[112,896]{1,0:T(8,128)(2,1)}, bf16[112,896]{1,0:T(8,128)(2,1)S(1)}, u32[]{:S(2)}, u32[]{:S(2)}) collective-permute-start(bf16[112,896]{1,0:T(8,128)(2,1)} %select_bitcast_fusion.1), channel_id=1, source_target_pairs={{0,1},{1,0},{2,3},{3,2},{4,5},{5,4},{6,7},{7,6},{8,9},{9,8},{10,11... | collective-permute-start | bytes 602120 | tf_op jit(solution)/shard_map/ppermute | solution.py:425
  68.3 9.1 %collective-permute-start.6 = (bf16[112,896]{1,0:T(8,128)(2,1)}, bf16[112,896]{1,0:T(8,128)(2,1)S(1)}, u32[]{:S(2)}, u32[]{:S(2)}) collective-permute-start(bf16[112,896]{1,0:T(8,128)(2,1)} %collective-permute-done.5), channel_id=1, source_target_pairs={{0,1},{1,0},{2,3},{3,2},{4,5},{5,4},{6,7},{7,6},{8,9},{9,8},{10,11... | collective-permute-start | bytes 602120 | tf_op jit(solution)/shard_map/ppermute | solution.py:425
  83.0 10.3 %copy-start.3 = (bf16[4,3,144,896]{3,2,1,0:T(8,128)(2,1)}, bf16[4,3,144,896]{3,2,1,0:T(8,128)(2,1)S(1)}, u32[]{:S(2)}) copy-start(bf16[4,3,144,896]{3,2,1,0:T(8,128)(2,1)S(1)} %maximum_select_fusion.near_ref) | copy-start | bytes 9289732
  83.0 4.5 %copy-start.21 = (f32[1792]{0:T(1024)S(1)}, f32[1792]{0:T(1024)}, u32[]{:S(2)}) copy-start(f32[1792]{0:T(1024)} %param.21) | copy-start | bytes 21508
  83.0 8.8 %copy-start.8 = (bf16[4,16,4,1792]{3,1,2,0:T(8,128)(2,1)S(1)}, bf16[4,16,4,1792]{3,1,2,0:T(8,128)(2,1)}, u32[]{:S(2)}) copy-start(bf16[4,16,4,1792]{3,1,2,0:T(8,128)(2,1)} %copy-done.7) | copy-start | bytes 2752516
  83.1 12.6 %collective-permute-start.11 = (bf16[4,3,144,896]{3,2,1,0:T(8,128)(2,1)S(1)}, bf16[4,3,144,896]{3,2,1,0:T(8,128)(2,1)}, u32[]{:S(2)}, u32[]{:S(2)}) collective-permute-start(bf16[4,3,144,896]{3,2,1,0:T(8,128)(2,1)S(1)} %maximum_select_fusion.near_ref), channel_id=1, source_target_pairs={{0,16},{16,0},{1,17},{17,1},{2,18},{18,2},{3,19},{19,3},{4,20},{20... | collective-permute-start | bytes 9289736 | tf_op jit(solution)/shard_map/ppermute | solution.py:425
  87.2 37.5 %collective-permute-start.15 = (bf16[448,896]{1,0:T(8,128)(2,1)}, bf16[448,896]{1,0:T(8,128)(2,1)}, u32[]{:S(2)}, u32[]{:S(2)}) collective-permute-start(bf16[448,896]{1,0:T(8,128)(2,1)} %maximum_select_fusion.4), channel_id=1, source_target_pairs={{0,2},{1,3},{2,0},{3,1},{4,6},{5,7},{6,4},{7,5},{8,10},{9,11},{10,... | collective-permute-start | bytes 2408456 | tf_op jit(solution)/shard_map/ppermute | solution.py:425
  88.1 41.9 %collective-permute-start.18 = (bf16[3,112,896]{2,1,0:T(8,128)(2,1)}, bf16[3,112,896]{2,1,0:T(8,128)(2,1)}, u32[]{:S(2)}, u32[]{:S(2)}) collective-permute-start(bf16[3,112,896]{2,1,0:T(8,128)(2,1)} %pad_maximum_fusion), channel_id=1, source_target_pairs={{0,4},{4,0},{8,12},{12,8},{1,5},{5,1},{9,13},{13,9},{2,6},{6,2},{1... | collective-permute-start | bytes 1806344 | tf_op jit(solution)/shard_map/ppermute | solution.py:425
  90.2 40.9 %collective-permute-start.19 = (bf16[3,112,896]{2,1,0:T(8,128)(2,1)}, bf16[3,112,896]{2,1,0:T(8,128)(2,1)}, u32[]{:S(2)}, u32[]{:S(2)}) collective-permute-start(bf16[3,112,896]{2,1,0:T(8,128)(2,1)} %pad_maximum_fusion), channel_id=1, source_target_pairs={{0,8},{4,12},{8,0},{12,4},{1,9},{5,13},{9,1},{13,5},{2,10},{6,14},... | collective-permute-start | bytes 1806344 | tf_op jit(solution)/shard_map/ppermute | solution.py:425
  108.1 25.7 %collective-permute-start.14 = (bf16[4,640,128]{2,1,0:T(8,128)(2,1)}, bf16[4,640,128]{2,1,0:T(8,128)(2,1)S(1)}, u32[]{:S(2)}, u32[]{:S(2)}) collective-permute-start(bf16[4,640,128]{2,1,0:T(8,128)(2,1)} %get-tuple-element.13), channel_id=1, source_target_pairs={{0,12},{1,13},{2,14},{3,15},{16,28},{17,29},{18,30},{19,31}} | collective-permute-start | bytes 1966088 | tf_op jit(solution)/shard_map/ppermute | solution.py:474
  110.4 23.5 %collective-permute-start.13 = (bf16[4,640,128]{2,1,0:T(8,128)(2,1)}, bf16[4,640,128]{2,1,0:T(8,128)(2,1)S(1)}, u32[]{:S(2)}, u32[]{:S(2)}) collective-permute-start(bf16[4,640,128]{2,1,0:T(8,128)(2,1)} %get-tuple-element.13), channel_id=1, source_target_pairs={{0,8},{4,12},{1,9},{5,13},{2,10},{6,14},{3,11},{7,15},{16,24},{20,... | collective-permute-start | bytes 1966088 | tf_op jit(solution)/shard_map/ppermute | solution.py:474
  124.7 18.7 %collective-permute-start.12 = (bf16[4,640,128]{2,1,0:T(8,128)(2,1)}, bf16[4,640,128]{2,1,0:T(8,128)(2,1)S(1)}, u32[]{:S(2)}, u32[]{:S(2)}) collective-permute-start(bf16[4,640,128]{2,1,0:T(8,128)(2,1)} %get-tuple-element.13), channel_id=1, source_target_pairs={{0,4},{4,8},{8,12},{1,5},{5,9},{9,13},{2,6},{6,10},{10,14},{3,7},{... | collective-permute-start | bytes 1966088 | tf_op jit(solution)/shard_map/ppermute | solution.py:474
  130.0 14.9 %collective-permute-start.16 = (bf16[112,896]{1,0:T(8,128)(2,1)S(1)}, bf16[112,896]{1,0:T(8,128)(2,1)S(1)}, u32[]{:S(2)}, u32[]{:S(2)}) collective-permute-start(bf16[112,896]{1,0:T(8,128)(2,1)S(1)} %get-tuple-element.17), channel_id=1, source_target_pairs={{0,1},{1,0},{2,3},{3,2},{4,5},{5,4},{6,7},{7,6},{8,9},{9,8},{10,11... | collective-permute-start | bytes 602120 | tf_op jit(solution)/shard_map/ppermute | solution.py:425
  131.1 18.0 %collective-permute-start.21 = (bf16[3,48,896]{2,1,0:T(8,128)(2,1)S(1)}, bf16[3,48,896]{2,1,0:T(8,128)(2,1)S(1)}, u32[]{:S(2)}, u32[]{:S(2)}) collective-permute-start(bf16[3,48,896]{2,1,0:T(8,128)(2,1)S(1)} %slice_select_fusion.6), channel_id=1, source_target_pairs={{0,8},{4,12},{8,0},{12,4},{1,9},{5,13},{9,1},{13,5},{2,10},{6,14},... | collective-permute-start | bytes 774152 | tf_op jit(solution)/shard_map/ppermute | solution.py:425
  133.8 18.2 %collective-permute-start.20 = (bf16[3,64,896]{2,1,0:T(8,128)(2,1)S(1)}, bf16[3,64,896]{2,1,0:T(8,128)(2,1)S(1)}, u32[]{:S(2)}, u32[]{:S(2)}) collective-permute-start(bf16[3,64,896]{2,1,0:T(8,128)(2,1)S(1)} %slice_select_fusion.2), channel_id=1, source_target_pairs={{0,4},{4,0},{8,12},{12,8},{1,5},{5,1},{9,13},{13,9},{2,6},{6,2},{1... | collective-permute-start | bytes 1032200 | tf_op jit(solution)/shard_map/ppermute | solution.py:425
  133.9 11.0 %collective-permute-start.17 = (bf16[112,896]{1,0:T(8,128)(2,1)S(1)}, bf16[112,896]{1,0:T(8,128)(2,1)S(1)}, u32[]{:S(2)}, u32[]{:S(2)}) collective-permute-start(bf16[112,896]{1,0:T(8,128)(2,1)S(1)} %get-tuple-element.22), channel_id=1, source_target_pairs={{0,1},{1,0},{2,3},{3,2},{4,5},{5,4},{6,7},{7,6},{8,9},{9,8},{10,11... | collective-permute-start | bytes 602120 | tf_op jit(solution)/shard_map/ppermute | solution.py:425
  143.7 8.4 %copy-start.6 = (f32[4,640,128]{2,1,0:T(8,128)}, f32[4,640,128]{2,1,0:T(8,128)S(1)}, u32[]{:S(2)}) copy-start(f32[4,640,128]{2,1,0:T(8,128)S(1)} %convert_add_fusion.prior_ref) | copy-start | bytes 3932164
  152.1 5.0 %copy-start.22 = (f32[1792]{0:T(1024)S(1)}, f32[1792]{0:T(1024)}, u32[]{:S(2)}) copy-start(f32[1792]{0:T(1024)} %param.25) | copy-start | bytes 21508
  154.0 6.2 %copy-start.5 = (bf16[4,3,112,896]{3,2,1,0:T(8,128)(2,1)}, bf16[4,3,112,896]{3,2,1,0:T(8,128)(2,1)S(1)}, u32[]{:S(2)}) copy-start(bf16[4,3,112,896]{3,2,1,0:T(8,128)(2,1)S(1)} %maximum_select_fusion.1.near_ref) | copy-start | bytes 7225348
  154.0 4.7 %collective-permute-start.22 = (bf16[4,3,112,896]{3,2,1,0:T(8,128)(2,1)S(1)}, bf16[4,3,112,896]{3,2,1,0:T(8,128)(2,1)S(1)}, u32[]{:S(2)}, u32[]{:S(2)}) collective-permute-start(bf16[4,3,112,896]{3,2,1,0:T(8,128)(2,1)S(1)} %maximum_select_fusion.1.near_ref), channel_id=1, source_target_pairs={{0,16},{16,0},{1,17},{17,1},{2,18},{18,2},{3,19},{19,3},{4,20},{20... | collective-permute-start | bytes 7225352 | tf_op jit(solution)/shard_map/ppermute | solution.py:425
  155.1 17.4 %collective-permute-start.27 = (bf16[1,336,896]{2,1,0:T(8,128)(2,1)}, bf16[1,336,896]{2,1,0:T(8,128)(2,1)}, u32[]{:S(2)}, u32[]{:S(2)}) collective-permute-start(bf16[1,336,896]{2,1,0:T(8,128)(2,1)} %slice_select_fusion), channel_id=1, source_target_pairs={{0,8},{4,12},{8,0},{12,4},{1,9},{5,13},{9,1},{13,5},{2,10},{6,14},... | collective-permute-start | bytes 1806344 | tf_op jit(solution)/shard_map/ppermute | solution.py:425
  155.1 23.9 %collective-permute-start.26 = (bf16[1,336,896]{2,1,0:T(8,128)(2,1)}, bf16[1,336,896]{2,1,0:T(8,128)(2,1)}, u32[]{:S(2)}, u32[]{:S(2)}) collective-permute-start(bf16[1,336,896]{2,1,0:T(8,128)(2,1)} %slice_select_fusion), channel_id=1, source_target_pairs={{0,4},{4,0},{8,12},{12,8},{1,5},{5,1},{9,13},{13,9},{2,6},{6,2},{1... | collective-permute-start | bytes 1806344 | tf_op jit(solution)/shard_map/ppermute | solution.py:425
  158.7 1.5 copy-start.11
  170.6 27.3 %collective-permute-start.24 = (bf16[256,1792]{1,0:T(8,128)(2,1)}, bf16[256,1792]{1,0:T(8,128)(2,1)S(1)}, u32[]{:S(2)}, u32[]{:S(2)}) collective-permute-start(bf16[256,1792]{1,0:T(8,128)(2,1)} %get-tuple-element.14._.x_ref), channel_id=1, source_target_pairs={{0,1},{1,0},{2,3},{3,2},{4,5},{5,4},{6,7},{7,6},{8,9},{9,8},{10,11... | collective-permute-start | bytes 2752520 | tf_op jit(solution)/shard_map/ppermute | solution.py:425
  173.6 26.1 %collective-permute-start.28 = (bf16[1,176,896]{2,1,0:T(8,128)(2,1)S(1)}, bf16[1,176,896]{2,1,0:T(8,128)(2,1)S(1)}, u32[]{:S(2)}, u32[]{:S(2)}) collective-permute-start(bf16[1,176,896]{2,1,0:T(8,128)(2,1)S(1)} %slice_select_fusion.4), channel_id=1, source_target_pairs={{0,4},{4,0},{8,12},{12,8},{1,5},{5,1},{9,13},{13,9},{2,6},{6,2},{1... | collective-permute-start | bytes 946184 | tf_op jit(solution)/shard_map/ppermute | solution.py:425
  173.9 23.4 %collective-permute-start.25 = (bf16[80,1792]{1,0:T(8,128)(2,1)}, bf16[80,1792]{1,0:T(8,128)(2,1)S(1)}, u32[]{:S(2)}, u32[]{:S(2)}) collective-permute-start(bf16[80,1792]{1,0:T(8,128)(2,1)} %get-tuple-element.15), channel_id=1, source_target_pairs={{0,5},{1,4},{2,7},{3,6},{4,9},{5,8},{6,11},{7,10},{8,13},{9,12},{1... | collective-permute-start | bytes 860168 | tf_op jit(solution)/shard_map/ppermute | solution.py:648
  180.0 19.6 %collective-permute-start.29 = (bf16[1,160,896]{2,1,0:T(8,128)(2,1)S(1)}, bf16[1,160,896]{2,1,0:T(8,128)(2,1)S(1)}, u32[]{:S(2)}, u32[]{:S(2)}) collective-permute-start(bf16[1,160,896]{2,1,0:T(8,128)(2,1)S(1)} %slice_select_fusion.5), channel_id=1, source_target_pairs={{0,8},{4,12},{8,0},{12,4},{1,9},{5,13},{9,1},{13,5},{2,10},{6,14},... | collective-permute-start | bytes 860168 | tf_op jit(solution)/shard_map/ppermute | solution.py:425
  197.3 4.2 %copy-start.18 = (bf16[80,1792]{1,0:T(8,128)(2,1)}, bf16[80,1792]{1,0:T(8,128)(2,1)S(1)}, u32[]{:S(2)}) copy-start(bf16[80,1792]{1,0:T(8,128)(2,1)S(1)} %collective-permute-done.25.halo_ref) | copy-start | bytes 860164
  197.9 1.9 copy-start.15
  199.8 1.8 copy-start.23
  201.5 20.5 %copy-start.2 = (bf16[4,1,336,896]{3,2,1,0:T(8,128)(2,1)}, bf16[4,1,336,896]{3,2,1,0:T(8,128)(2,1)S(1)}, u32[]{:S(2)}) copy-start(bf16[4,1,336,896]{3,2,1,0:T(8,128)(2,1)S(1)} %maximum_select_fusion.2.near_ref) | copy-start | bytes 7225348
  201.5 20.5 %collective-permute-start.30 = (bf16[4,1,336,896]{3,2,1,0:T(8,128)(2,1)S(1)}, bf16[4,1,336,896]{3,2,1,0:T(8,128)(2,1)}, u32[]{:S(2)}, u32[]{:S(2)}) collective-permute-start(bf16[4,1,336,896]{3,2,1,0:T(8,128)(2,1)S(1)} %maximum_select_fusion.2.near_ref), channel_id=1, source_target_pairs={{0,16},{16,0},{1,17},{17,1},{2,18},{18,2},{3,19},{19,3},{4,20},{20... | collective-permute-start | bytes 7225352 | tf_op jit(solution)/shard_map/ppermute | solution.py:425
  201.6 12.2 %collective-permute-start.23 = (bf16[80,1792]{1,0:T(8,128)(2,1)S(1)}, bf16[80,1792]{1,0:T(8,128)(2,1)S(1)}, u32[]{:S(2)}, u32[]{:S(2)}) collective-permute-start(bf16[80,1792]{1,0:T(8,128)(2,1)S(1)} %copy-done.23), channel_id=1, source_target_pairs={{0,4},{4,8},{8,12},{1,5},{5,9},{9,13},{2,6},{6,10},{10,14},{3,7},{... | collective-permute-start | bytes 860168 | tf_op jit(solution)/shard_map/ppermute | solution.py:646
  213.8 0.7 copy-start.19
  216.5 21.5 %collective-permute-start.34 = (bf16[3,112,896]{2,1,0:T(8,128)(2,1)}, bf16[3,112,896]{2,1,0:T(8,128)(2,1)}, u32[]{:S(2)}, u32[]{:S(2)}) collective-permute-start(bf16[3,112,896]{2,1,0:T(8,128)(2,1)} %broadcast_select_fusion.1), channel_id=1, source_target_pairs={{0,12},{4,8},{8,4},{12,0},{1,13},{5,9},{9,5},{13,1},{2,14},{6,10},... | collective-permute-start | bytes 1806344 | tf_op jit(solution)/shard_map/ppermute | solution.py:425
  218.5 27.7 %collective-permute-start.33 = (bf16[3,112,896]{2,1,0:T(8,128)(2,1)}, bf16[3,112,896]{2,1,0:T(8,128)(2,1)}, u32[]{:S(2)}, u32[]{:S(2)}) collective-permute-start(bf16[3,112,896]{2,1,0:T(8,128)(2,1)} %broadcast_select_fusion.1), channel_id=1, source_target_pairs={{0,8},{4,12},{8,0},{12,4},{1,9},{5,13},{9,1},{13,5},{2,10},{6,14},... | collective-permute-start | bytes 1806344 | tf_op jit(solution)/shard_map/ppermute | solution.py:425
  220.5 27.0 %collective-permute-start.32 = (bf16[3,112,896]{2,1,0:T(8,128)(2,1)}, bf16[3,112,896]{2,1,0:T(8,128)(2,1)}, u32[]{:S(2)}, u32[]{:S(2)}) collective-permute-start(bf16[3,112,896]{2,1,0:T(8,128)(2,1)} %broadcast_select_fusion.1), channel_id=1, source_target_pairs={{0,4},{4,0},{8,12},{12,8},{1,5},{5,1},{9,13},{13,9},{2,6},{6,2},{1... | collective-permute-start | bytes 1806344 | tf_op jit(solution)/shard_map/ppermute | solution.py:425
  222.0 25.5 %copy-start.12 = (bf16[1,3,112,896]{3,2,1,0:T(8,128)(2,1)S(1)}, bf16[1,3,112,896]{3,2,1,0:T(8,128)(2,1)}, u32[]{:S(2)}) copy-start(bf16[1,3,112,896]{3,2,1,0:T(8,128)(2,1)} %fusion.14) | copy-start | bytes 1806340
  247.5 2.0 copy-start.13
  247.5 2.4 copy-start.24
  247.5 2.4 copy-start.25
  249.5 16.0 %copy-start.4 = (bf16[4,3,112,896]{3,2,1,0:T(8,128)(2,1)}, bf16[4,3,112,896]{3,2,1,0:T(8,128)(2,1)S(1)}, u32[]{:S(2)}) copy-start(bf16[4,3,112,896]{3,2,1,0:T(8,128)(2,1)S(1)} %maximum_select_fusion.3.near_ref) | copy-start | bytes 7225348
  249.5 16.0 %collective-permute-start.35 = (bf16[4,3,112,896]{3,2,1,0:T(8,128)(2,1)S(1)}, bf16[4,3,112,896]{3,2,1,0:T(8,128)(2,1)}, u32[]{:S(2)}, u32[]{:S(2)}) collective-permute-start(bf16[4,3,112,896]{3,2,1,0:T(8,128)(2,1)S(1)} %maximum_select_fusion.3.near_ref), channel_id=1, source_target_pairs={{0,16},{16,0},{1,17},{17,1},{2,18},{18,2},{3,19},{19,3},{4,20},{20... | collective-permute-start | bytes 7225352 | tf_op jit(solution)/shard_map/ppermute | solution.py:425
  249.6 15.9 %collective-permute-start.31 = (bf16[2,256,512]{2,1,0:T(8,128)(2,1)S(1)}, bf16[2,256,512]{2,1,0:T(8,128)(2,1)S(1)}, u32[]{:S(2)}, u32[]{:S(2)}) collective-permute-start(bf16[2,256,512]{2,1,0:T(8,128)(2,1)S(1)} %copy-done.13), channel_id=1, source_target_pairs={{0,1},{1,0},{2,3},{3,2},{4,5},{5,4},{6,7},{7,6},{8,9},{9,8},{10,11... | collective-permute-start | bytes 1572872 | tf_op jit(solution)/shard_map/ppermute | solution.py:425
  265.5 0.8 copy-start.16
  273.0 29.2 %copy-start.1 = (bf16[64,4,1792]{2,1,0:T(4,128)(2,1)S(1)}, bf16[64,4,1792]{2,1,0:T(4,128)(2,1)}, u32[]{:S(2)}) copy-start(bf16[64,4,1792]{2,1,0:T(4,128)(2,1)} %param.17) | copy-start | bytes 2752516

commit v12 on v11

--- a/solution.py
+++ b/solution.py
@@ -452,10 +452,10 @@
     return across(held, "seq", 1), across(held, "seq", 2)
 
 
-def from_plane(held, near_by, diagonal, over_cores):
+def from_plane(held, near_by, diagonal, over_cores, over_across=()):
     beside, above = near_by
     if diagonal is None:
-        opposite = across(held, "seq", 3)
+        opposite = across(after(held, over_across), "seq", 3)
     else:
         half = -(-held.shape[1] // 32) * 16
         opposite = [
@@ -654,8 +654,11 @@
             for j in range(group_count)
         ],
     )
-    near_window = from_plane(held_window, near_by_window, (residual,), (pair_rows, pair_halo))
-    held_out_two = after(held_out_two, (halo,))
+    held_out_two = after(held_out_two, (residual,))
+    near_by_two = neighbours(held_out_two)
+    near_window = from_plane(
+        held_window, near_by_window, (residual,), (pair_rows, pair_halo, *near_by_two)
+    )
     block_start = (seq_place * rows).astype(jnp.int32)[None]
 
     def window_rows(slot_rows, slot_halo, earlier):
@@ -680,7 +683,7 @@
         )(places, block_start, slot_rows, slot_halo, window_t, *near_window, taps, earlier)
 
     mixed_pair = window_rows(pair_rows, pair_halo, normed_two)
-    near_out_two = from_plane(held_out_two, neighbours(held_out_two), None, (mixed_pair,))
+    near_out_two = from_plane(held_out_two, near_by_two, None, (mixed_pair,))
     mixed_own = window_rows(normed_two, halo, mixed_pair)
     mixed_pair = across(mixed_pair, "tensor", 1)
     live = (length - seq_place * rows).astype(jnp.int32)[None]

time: 303 us -> 296 us (0.977)
  waiting for transfers between devices: 94.9 us -> 85.1 us
    ppermute x31, waiting for transfers between devices: 41 us -> 33.7 us  [across(): lax.ppermute(array, axis, [(i, i ^ bit) for i in range(lax.axis_size(axis...]
    ppermute x31, starting transfers between devices: 30.6 us -> 34.5 us  [across(): lax.ppermute(array, axis, [(i, i ^ bit) for i in range(lax.axis_size(axis...]
    slice x14 -> x15, local copies, waits for them, and re-layouts: 10.2 us -> 10.4 us  [after(): lax.slice(other, (0,) * other.ndim, (1,) * other.ndim)]
  transfers between devices with their start and end apart: 38 -> 38, of which waited for: 16 -> 15; matrix products, arithmetic and copies ran while one was open for 13% -> 14% of each run, Pallas kernels for 17% -> 17%
where the time goes in v12:
time: 296 us; the launch traced here: 294 us
  waiting for transfers between devices  85.1 us (29%)
  Pallas kernels  57.8 us (20%)
  starting transfers between devices  57 us (19%)
  local copies, waits for them, and re-layouts  31.5 us (11%)
  other arithmetic  27.7 us (9%)
  blocking collectives  25 us (8%)
  between operations  10.2 us (3%)
    ppermute x31, starting transfers between devices, across(): lax.ppermute(array, axis, [(i, i ^ bit) for i in range(lax.axis_size(axis...  34.5 us
    ppermute x31, waiting for transfers between devices, across(): lax.ppermute(array, axis, [(i, i ^ bit) for i in range(lax.axis_size(axis...  33.7 us
    pallas_call x2, Pallas kernels, window_rows(): call(functools.partial(window_kernel, heads), 2, [SMEM, SMEM, *[HBM] * 5,...  28.2 us
    all_to_all x1, blocking collectives, on_device(): lax.all_to_all(result, 'tensor', split_axis=0, concat_axis=0, tiled=True)  25 us
    all_to_all x1, waiting for transfers between devices, on_device(): lax.all_to_all(picked, 'tensor', split_axis=0, concat_axis=0, tiled=True)  20.9 us
    select_n x21, other arithmetic, after(): return jnp.where(zero == 0.0, array, jnp.zeros_like(array))  20.1 us
    ppermute x1, waiting for transfers between devices, on_device(): lax.ppermute(tail, ('seq', 'tensor'), [(i * group_count + j, (i + 1) * gr...  16.6 us
    pallas_call x1, Pallas kernels, on_device(): call(functools.partial(linear_kernel, heads, feature_dim, kept), group_co...  12.4 us
  transfers between devices with their start and end apart: 38, of which 15 were waited for; matrix products, arithmetic and copies ran while one was open for 14% of the time, Pallas kernels for 17%

profile of v12, /device:TPU:0, one launch (start us, length us, event | category | flops | bytes accessed | tf_op | source)
XLA Modules:
  0.0 294.3 jit_solution(17675037964718669475)
XLA Ops:
  1.9 4.1 %collective-permute-start.2 = (bf16[144,896]{1,0:T(8,128)(2,1)S(1)}, bf16[144,896]{1,0:T(8,128)(2,1)S(1)}, u32[]{:S(2)}, u32[]{:S(2)}) collective-permute-start(bf16[144,896]{1,0:T(8,128)(2,1)S(1)} %pad_maximum_fusion.1), channel_id=1, source_target_pairs={{0,2},{1,3},{2,0},{3,1},{4,6},{5,7},{6,4},{7,5},{8,10},{9,11},{10,... | collective-permute-start | bytes 774152 | tf_op jit(solution)/shard_map/ppermute | solution.py:425
  6.0 1.6 collective-permute-start.1
  10.0 2.2 gather_fusion.1
  12.2 3.7 %all-to-all-start = ((bf16[8,8,4,1792]{3,2,1,0:T(4,128)(2,1)}), bf16[8,8,4,1792]{3,2,1,0:T(4,128)(2,1)S(1)}, u32[]{:S(2)}, u32[]{:S(2)}) async-start(bf16[8,8,4,1792]{3,2,1,0:T(4,128)(2,1)} %bitcast.20), calls=%async_computation | async-start | bytes 1835008 | tf_op jit(solution)/shard_map/all_to_all | solution.py:548
  18.6 3.1 %collective-permute-done = f32[3,1536]{1,0:T(4,128)S(1)} collective-permute-done((f32[3,1536]{1,0:T(4,128)S(1)}, f32[3,1536]{1,0:T(4,128)S(1)}, u32[]{:S(2)}, u32[]{:S(2)}) %collective-permute-start) | collective-permute-done | bytes 18464 | tf_op jit(solution)/shard_map/ppermute | solution.py:425
  22.8 3.5 %collective-permute-done.3 = bf16[144,896]{1,0:T(8,128)(2,1)S(1)} collective-permute-done((bf16[144,896]{1,0:T(8,128)(2,1)S(1)}, bf16[144,896]{1,0:T(8,128)(2,1)S(1)}, u32[]{:S(2)}, u32[]{:S(2)}) %collective-permute-start.3) | collective-permute-done | bytes 258080 | tf_op jit(solution)/shard_map/ppermute | solution.py:425
  27.5 1.9 all-to-all-done
  29.4 1.3 gather_fusion.2
  32.2 3.5 %all-to-all-start.1 = ((bf16[4,16,4,1792]{3,1,2,0:T(8,128)(2,1)}), bf16[4,16,4,1792]{3,1,2,0:T(8,128)(2,1)S(1)}, u32[]{:S(2)}, u32[]{:S(2)}) async-start(bf16[4,16,4,1792]{3,1,2,0:T(8,128)(2,1)} %copy.47), calls=%async_computation.1 | async-start | bytes 1835008 | tf_op jit(solution)/shard_map/all_to_all | solution.py:555
  35.7 1.1 collective-permute-start.8
  38.8 1.6 select_bitcast_fusion.1
  40.5 2.9 collective-permute-start.5
  43.4 20.9 %all-to-all-done.1 = bf16[4,16,4,1792]{3,1,2,0:T(8,128)(2,1)S(1)} async-done(((bf16[4,16,4,1792]{3,1,2,0:T(8,128)(2,1)}), bf16[4,16,4,1792]{3,1,2,0:T(8,128)(2,1)S(1)}, u32[]{:S(2)}, u32[]{:S(2)}) %all-to-all-start.1) | async-done | bytes 917536 | tf_op jit(solution)/shard_map/all_to_all | solution.py:555
  65.4 1.1 collective-permute-start.9
  66.5 1.0 slice_select_fusion.3
  68.2 2.0 collective-permute-start.6
  70.2 4.9 %collective-permute-done.4 = bf16[112,896]{1,0:T(8,128)(2,1)S(1)} collective-permute-done((bf16[112,896]{1,0:T(8,128)(2,1)}, bf16[112,896]{1,0:T(8,128)(2,1)S(1)}, u32[]{:S(2)}, u32[]{:S(2)}) %collective-permute-start.4) | collective-permute-done | bytes 200736 | tf_op jit(solution)/shard_map/ppermute | solution.py:425
  75.1 2.1 collective-permute-done.6
  77.3 1.8 pad_maximum_fusion
  79.1 1.2 slice.116
  81.0 1.7 maximum_select_fusion.near_ref
  82.9 2.1 constant_dynamic-slice_fusion
  86.0 1.0 maximum_select_fusion.4
  87.9 1.4 collective-permute-start.18
  89.9 1.7 collective-permute-start.19
  91.6 1.4 copy.48
  93.0 2.4 reshape.546.x_ref
  95.3 12.4 %linear_rows.1 = (f32[4,256,512]{2,1,0:T(8,128)}, bf16[4,256,128]{2,1,0:T(8,128)(2,1)}, bf16[4,640,128]{2,1,0:T(8,128)(2,1)}) custom-call(s32[5]{0:T(128)} %pad_add_fusion.place_ref, bf16[256,1792]{1,0:T(8,128)(2,1)} %reshape.546.x_ref, f32[1,1792]{1,0:T(1,128)} %broadcast_in_dim.128.gain_ref, bf16[1,4,112,1792]{3,2,1,0:T(8,128)(2,1)} %bitcast.101, ...), custom_call_target="tpu_custom_call" | custom-call | tf_op jit(solution)/shard_map/linear_rows/pallas_call | solution.py:576
  107.8 2.3 collective-permute-start.14
  110.1 1.3 collective-permute-start.13
  111.4 1.2 slice.91
  113.2 11.3 %collective-permute-done.15 = bf16[448,896]{1,0:T(8,128)(2,1)} collective-permute-done((bf16[448,896]{1,0:T(8,128)(2,1)}, bf16[448,896]{1,0:T(8,128)(2,1)}, u32[]{:S(2)}, u32[]{:S(2)}) %collective-permute-start.15) | collective-permute-done | bytes 802848 | tf_op jit(solution)/shard_map/ppermute | solution.py:425
  124.5 3.5 %collective-permute-start.12 = (bf16[4,640,128]{2,1,0:T(8,128)(2,1)}, bf16[4,640,128]{2,1,0:T(8,128)(2,1)S(1)}, u32[]{:S(2)}, u32[]{:S(2)}) collective-permute-start(bf16[4,640,128]{2,1,0:T(8,128)(2,1)} %get-tuple-element.13), channel_id=1, source_target_pairs={{0,4},{4,8},{8,12},{1,5},{5,9},{9,13},{2,6},{6,10},{10,14},{3,7},{... | collective-permute-start | bytes 1966088 | tf_op jit(solution)/shard_map/ppermute | solution.py:474
  128.0 1.2 select_bitcast_fusion
  130.9 1.7 collective-permute-start.21
  132.6 1.0 slice_select_fusion.2
  133.8 2.0 collective-permute-start.17
  135.8 7.4 %collective-permute-done.12 = bf16[4,640,128]{2,1,0:T(8,128)(2,1)S(1)} collective-permute-done((bf16[4,640,128]{2,1,0:T(8,128)(2,1)}, bf16[4,640,128]{2,1,0:T(8,128)(2,1)S(1)}, u32[]{:S(2)}, u32[]{:S(2)}) %collective-permute-start.12) | collective-permute-done | bytes 655392 | tf_op jit(solution)/shard_map/ppermute | solution.py:474
  146.6 2.3 collective-permute-done.21
  148.9 2.9 collective-permute-done.20
  151.9 1.9 maximum_select_fusion.1.near_ref
  153.9 1.0 slice_select_fusion
  154.9 2.0 collective-permute-start.28
  158.4 1.5 copy-done.11
  159.9 10.5 %linear_out.1 = (bf16[256,1792]{1,0:T(8,128)(2,1)}, bf16[256,1792]{1,0:T(8,128)(2,1)}, bf16[80,1792]{1,0:T(8,128)(2,1)}) custom-call(s32[5]{0:T(128)} %pad_add_fusion.place_ref, f32[4,256,512]{2,1,0:T(8,128)} %get-tuple-element.11.num_ref, bf16[4,256,128]{2,1,0:T(8,128)(2,1)} %get-tuple-element.12.q_ref, bf16[128,1024]{1,0:T(8,128)(2,1)} %constant.130.clone.first_ref, ...), custom_call_target="tpu_custom_call" | custom-call | tf_op jit(solution)/shard_map/linear_out/pallas_call | solution.py:616
  170.4 1.2 slice.100
  173.4 1.7 collective-permute-start.27
  175.0 3.4 %collective-permute-start.25 = (bf16[80,1792]{1,0:T(8,128)(2,1)}, bf16[80,1792]{1,0:T(8,128)(2,1)S(1)}, u32[]{:S(2)}, u32[]{:S(2)}) collective-permute-start(bf16[80,1792]{1,0:T(8,128)(2,1)} %get-tuple-element.15), channel_id=1, source_target_pairs={{0,5},{1,4},{2,7},{3,6},{4,9},{5,8},{6,11},{7,10},{8,13},{9,12},{1... | collective-permute-start | bytes 860168 | tf_op jit(solution)/shard_map/ppermute | solution.py:648
  178.5 1.0 slice_select_fusion.4
  179.5 1.8 collective-permute-start.30
  182.3 16.6 %collective-permute-done.25.halo_ref = bf16[80,1792]{1,0:T(8,128)(2,1)S(1)} collective-permute-done((bf16[80,1792]{1,0:T(8,128)(2,1)}, bf16[80,1792]{1,0:T(8,128)(2,1)S(1)}, u32[]{:S(2)}, u32[]{:S(2)}) %collective-permute-start.25) | collective-permute-done | bytes 286752 | tf_op jit(solution)/shard_map/ppermute | solution.py:648
  198.9 3.3 %collective-permute-start.31 = (bf16[1,160,896]{2,1,0:T(8,128)(2,1)S(1)}, bf16[1,160,896]{2,1,0:T(8,128)(2,1)S(1)}, u32[]{:S(2)}, u32[]{:S(2)}) collective-permute-start(bf16[1,160,896]{2,1,0:T(8,128)(2,1)S(1)} %slice_select_fusion.5), channel_id=1, source_target_pairs={{0,8},{4,12},{8,0},{12,4},{1,9},{5,13},{9,1},{13,5},{2,10},{6,14},... | collective-permute-start | bytes 860168 | tf_op jit(solution)/shard_map/ppermute | solution.py:425
  208.7 1.9 maximum_select_fusion.2.near_ref
  210.7 1.7 collective-permute-start.34
  213.3 2.1 collective-permute-done.32.far_ref
  215.4 14.1 %window_rows.2._ = bf16[2,256,512]{2,1,0:T(8,128)(2,1)} custom-call(s32[5]{0:T(128)} %pad_add_fusion.place_ref, s32[1]{0:T(128)} %bitcast.2.first_ref, bf16[256,1792]{1,0:T(8,128)(2,1)} %copy-done.15, bf16[80,1792]{1,0:T(8,128)(2,1)} %copy-done.20, bf16[3,4,112,1792]{3,2,1,0:T(8,128)(2,1)} %bitcast.91, bf16[4,1,336,896]{3,2,1,0:T(8,128)(2,1)} %copy-done.2, ...), custom_call_target="tpu_custom_call" | custom-call | tf_op jit(solution)/shard_map/window_rows/pallas_call | solution.py:665
  229.6 1.2 slice.133
  231.4 1.9 maximum_select_fusion.3.near_ref
  234.0 4.6 %collective-permute-start.23 = (bf16[80,1792]{1,0:T(8,128)(2,1)}, bf16[80,1792]{1,0:T(8,128)(2,1)}, u32[]{:S(2)}, u32[]{:S(2)}) collective-permute-start(bf16[80,1792]{1,0:T(8,128)(2,1)} %get-tuple-element.15), channel_id=1, source_target_pairs={{0,4},{4,8},{8,12},{1,5},{5,9},{9,13},{2,6},{6,10},{10,14},{3,7},{... | collective-permute-start | bytes 860168 | tf_op jit(solution)/shard_map/ppermute | solution.py:646
  239.9 4.6 %collective-permute-done.23.halo_ref = bf16[80,1792]{1,0:T(8,128)(2,1)} collective-permute-done((bf16[80,1792]{1,0:T(8,128)(2,1)}, bf16[80,1792]{1,0:T(8,128)(2,1)}, u32[]{:S(2)}, u32[]{:S(2)}) %collective-permute-start.23) | collective-permute-done | bytes 286752 | tf_op jit(solution)/shard_map/ppermute | solution.py:646
  244.5 14.1 %window_rows.3.mixed_ref = bf16[2,256,512]{2,1,0:T(8,128)(2,1)} custom-call(s32[5]{0:T(128)} %pad_add_fusion.place_ref, s32[1]{0:T(128)} %bitcast.2.first_ref, bf16[256,1792]{1,0:T(8,128)(2,1)} %get-tuple-element.14._.x_ref, bf16[80,1792]{1,0:T(8,128)(2,1)} %collective-permute-done.23.halo_ref, bf16[3,4,112,1792]{3,2,1,0:T(8,128)(2,1)} %bitcast.92, ...), custom_call_target="tpu_custom_call" | custom-call | tf_op jit(solution)/shard_map/window_rows/pallas_call | solution.py:665
  259.5 6.7 %window_out.1 = bf16[256,1792]{1,0:T(8,128)(2,1)} custom-call(s32[5]{0:T(128)} %pad_add_fusion.place_ref, s32[1]{0:T(128)} %bitcast.1.live_ref, bf16[2,256,512]{2,1,0:T(8,128)(2,1)} %window_rows.3.mixed_ref, bf16[2,256,512]{2,1,0:T(8,128)(2,1)} %copy-done.18, bf16[1,4,112,1792]{3,2,1,0:T(8,128)(2,1)} %bitcast.105, bf16[4,3,112,896]{3,2,1,0:T(8,128)(2,1)} %copy-done.4, ...), custom_call_target="tpu_custom_call" | custom-call | tf_op jit(solution)/shard_map/window_out/pallas_call | solution.py:690
  266.2 1.9 reshape.552
  268.4 25.0 %all_to_all.15 = bf16[4,16,4,1792]{3,2,1,0:T(4,128)(2,1)S(1)} all-to-all(bf16[4,16,4,1792]{3,2,1,0:T(4,128)(2,1)S(1)} %bitcast.96), channel_id=1, replica_groups=mesh['dp'=2,'seq'=4,'tensor'=4] {'tensor'}, dimensions={0} | all-to-all | bytes 1835008 | tf_op jit(solution)/shard_map/all_to_all | solution.py:711
  (160 shorter events, 30.6 us)
Async XLA Ops:
  0.0 9.9 %copy-start = (bf16[64,4,1792]{2,1,0:T(4,128)(2,1)S(1)}, bf16[64,4,1792]{2,1,0:T(4,128)(2,1)}, u32[]{:S(2)}) copy-start(bf16[64,4,1792]{2,1,0:T(4,128)(2,1)} %param.17) | copy-start | bytes 2752516
  0.9 15.0 %copy-start.21 = (f32[3,3,448]{2,1,0:T(4,128)S(1)}, f32[3,3,448]{2,1,0:T(4,128)}, u32[]{:S(2)}) copy-start(f32[3,3,448]{2,1,0:T(4,128)} %param.27) | copy-start | bytes 48388
  1.9 16.0 %collective-permute-start.2 = (bf16[144,896]{1,0:T(8,128)(2,1)S(1)}, bf16[144,896]{1,0:T(8,128)(2,1)S(1)}, u32[]{:S(2)}, u32[]{:S(2)}) collective-permute-start(bf16[144,896]{1,0:T(8,128)(2,1)S(1)} %pad_maximum_fusion.1), channel_id=1, source_target_pairs={{0,2},{1,3},{2,0},{3,1},{4,6},{5,7},{6,4},{7,5},{8,10},{9,11},{10,... | collective-permute-start | bytes 774152 | tf_op jit(solution)/shard_map/ppermute | solution.py:425
  6.0 16.8 %collective-permute-start.1 = (bf16[144,896]{1,0:T(8,128)(2,1)S(1)}, bf16[144,896]{1,0:T(8,128)(2,1)S(1)}, u32[]{:S(2)}, u32[]{:S(2)}) collective-permute-start(bf16[144,896]{1,0:T(8,128)(2,1)S(1)} %pad_maximum_fusion.1), channel_id=1, source_target_pairs={{0,1},{1,0},{2,3},{3,2},{4,5},{5,4},{6,7},{7,6},{8,9},{9,8},{10,11... | collective-permute-start | bytes 774152 | tf_op jit(solution)/shard_map/ppermute | solution.py:425
  12.2 17.2 %all-to-all-start = ((bf16[8,8,4,1792]{3,2,1,0:T(4,128)(2,1)}), bf16[8,8,4,1792]{3,2,1,0:T(4,128)(2,1)S(1)}, u32[]{:S(2)}, u32[]{:S(2)}) async-start(bf16[8,8,4,1792]{3,2,1,0:T(4,128)(2,1)} %bitcast.20), calls=%async_computation | async-start | bytes 1835008 | tf_op jit(solution)/shard_map/all_to_all | solution.py:548
  16.7 5.0 %collective-permute-start = (f32[3,1536]{1,0:T(4,128)S(1)}, f32[3,1536]{1,0:T(4,128)S(1)}, u32[]{:S(2)}, u32[]{:S(2)}) collective-permute-start(f32[3,1536]{1,0:T(4,128)S(1)} %reshape.536), channel_id=1, source_target_pairs={{0,2},{1,3},{2,0},{3,1},{4,6},{5,7},{6,4},{7,5},{8,10},{9,11},{10,... | collective-permute-start | bytes 55304 | tf_op jit(solution)/shard_map/ppermute | solution.py:425
  17.9 8.4 %collective-permute-start.3 = (bf16[144,896]{1,0:T(8,128)(2,1)S(1)}, bf16[144,896]{1,0:T(8,128)(2,1)S(1)}, u32[]{:S(2)}, u32[]{:S(2)}) collective-permute-start(bf16[144,896]{1,0:T(8,128)(2,1)S(1)} %collective-permute-done.2), channel_id=1, source_target_pairs={{0,1},{1,0},{2,3},{3,2},{4,5},{5,4},{6,7},{7,6},{8,9},{9,8},{10,11... | collective-permute-start | bytes 774152 | tf_op jit(solution)/shard_map/ppermute | solution.py:425
  21.7 9.4 %copy-start.19 = (f32[2,3,1536]{2,1,0:T(4,128)}, f32[2,3,1536]{2,1,0:T(4,128)S(1)}, u32[]{:S(2)}) copy-start(f32[2,3,1536]{2,1,0:T(4,128)S(1)} %pad_maximum_fusion.2.tap_ref) | copy-start | bytes 110596
  26.4 10.4 %copy-start.9 = (bf16[3,144,896]{2,1,0:T(8,128)(2,1)}, bf16[3,144,896]{2,1,0:T(8,128)(2,1)S(1)}, u32[]{:S(2)}) copy-start(bf16[3,144,896]{2,1,0:T(8,128)(2,1)S(1)} %maximum_select_fusion.5) | copy-start | bytes 2322436
  32.2 32.1 %all-to-all-start.1 = ((bf16[4,16,4,1792]{3,1,2,0:T(8,128)(2,1)}), bf16[4,16,4,1792]{3,1,2,0:T(8,128)(2,1)S(1)}, u32[]{:S(2)}, u32[]{:S(2)}) async-start(bf16[4,16,4,1792]{3,1,2,0:T(8,128)(2,1)} %copy.47), calls=%async_computation.1 | async-start | bytes 1835008 | tf_op jit(solution)/shard_map/all_to_all | solution.py:555
  35.7 29.7 %collective-permute-start.8 = (bf16[3,144,896]{2,1,0:T(8,128)(2,1)S(1)}, bf16[3,144,896]{2,1,0:T(8,128)(2,1)S(1)}, u32[]{:S(2)}, u32[]{:S(2)}) collective-permute-start(bf16[3,144,896]{2,1,0:T(8,128)(2,1)S(1)} %maximum_select_fusion.5), channel_id=1, source_target_pairs={{0,8},{4,12},{8,0},{12,4},{1,9},{5,13},{9,1},{13,5},{2,10},{6,14},... | collective-permute-start | bytes 2322440 | tf_op jit(solution)/shard_map/ppermute | solution.py:425
  36.8 29.7 %collective-permute-start.7 = (bf16[3,144,896]{2,1,0:T(8,128)(2,1)S(1)}, bf16[3,144,896]{2,1,0:T(8,128)(2,1)}, u32[]{:S(2)}, u32[]{:S(2)}) collective-permute-start(bf16[3,144,896]{2,1,0:T(8,128)(2,1)S(1)} %maximum_select_fusion.5), channel_id=1, source_target_pairs={{0,4},{4,0},{8,12},{12,8},{1,5},{5,1},{9,13},{13,9},{2,6},{6,2},{1... | collective-permute-start | bytes 2322440 | tf_op jit(solution)/shard_map/ppermute | solution.py:425
  40.5 27.8 %collective-permute-start.5 = (bf16[112,896]{1,0:T(8,128)(2,1)}, bf16[112,896]{1,0:T(8,128)(2,1)}, u32[]{:S(2)}, u32[]{:S(2)}) collective-permute-start(bf16[112,896]{1,0:T(8,128)(2,1)} %select_bitcast_fusion.1), channel_id=1, source_target_pairs={{0,2},{1,3},{2,0},{3,1},{4,6},{5,7},{6,4},{7,5},{8,10},{9,11},{10,... | collective-permute-start | bytes 602120 | tf_op jit(solution)/shard_map/ppermute | solution.py:425
  64.2 16.8 %copy-start.7 = (bf16[4,16,4,1792]{3,1,2,0:T(8,128)(2,1)}, bf16[4,16,4,1792]{3,1,2,0:T(8,128)(2,1)S(1)}, u32[]{:S(2)}) copy-start(bf16[4,16,4,1792]{3,1,2,0:T(8,128)(2,1)S(1)} %all-to-all-done.1) | copy-start | bytes 2752516
  64.3 16.8 %copy-start.10 = (bf16[3,144,896]{2,1,0:T(8,128)(2,1)S(1)}, bf16[3,144,896]{2,1,0:T(8,128)(2,1)}, u32[]{:S(2)}) copy-start(bf16[3,144,896]{2,1,0:T(8,128)(2,1)} %copy-done.9) | copy-start | bytes 2322436
  65.4 15.6 %copy-start.14 = (bf16[3,144,896]{2,1,0:T(8,128)(2,1)}, bf16[3,144,896]{2,1,0:T(8,128)(2,1)S(1)}, u32[]{:S(2)}) copy-start(bf16[3,144,896]{2,1,0:T(8,128)(2,1)S(1)} %collective-permute-done.8) | copy-start | bytes 2322436
  65.4 15.4 %collective-permute-start.9 = (bf16[3,80,896]{2,1,0:T(8,128)(2,1)S(1)}, bf16[3,80,896]{2,1,0:T(8,128)(2,1)S(1)}, u32[]{:S(2)}, u32[]{:S(2)}) collective-permute-start(bf16[3,80,896]{2,1,0:T(8,128)(2,1)S(1)} %slice_select_fusion.1), channel_id=1, source_target_pairs={{0,4},{4,0},{8,12},{12,8},{1,5},{5,1},{9,13},{13,9},{2,6},{6,2},{1... | collective-permute-start | bytes 1290248 | tf_op jit(solution)/shard_map/ppermute | solution.py:425
  67.6 13.3 %collective-permute-start.10 = (bf16[3,64,896]{2,1,0:T(8,128)(2,1)S(1)}, bf16[3,64,896]{2,1,0:T(8,128)(2,1)S(1)}, u32[]{:S(2)}, u32[]{:S(2)}) collective-permute-start(bf16[3,64,896]{2,1,0:T(8,128)(2,1)S(1)} %slice_select_fusion.3), channel_id=1, source_target_pairs={{0,8},{4,12},{8,0},{12,4},{1,9},{5,13},{9,1},{13,5},{2,10},{6,14},... | collective-permute-start | bytes 1032200 | tf_op jit(solution)/shard_map/ppermute | solution.py:425
  68.2 6.9 %collective-permute-start.4 = (bf16[112,896]{1,0:T(8,128)(2,1)}, bf16[112,896]{1,0:T(8,128)(2,1)S(1)}, u32[]{:S(2)}, u32[]{:S(2)}) collective-permute-start(bf16[112,896]{1,0:T(8,128)(2,1)} %select_bitcast_fusion.1), channel_id=1, source_target_pairs={{0,1},{1,0},{2,3},{3,2},{4,5},{5,4},{6,7},{7,6},{8,9},{9,8},{10,11... | collective-permute-start | bytes 602120 | tf_op jit(solution)/shard_map/ppermute | solution.py:425
  68.2 9.1 %collective-permute-start.6 = (bf16[112,896]{1,0:T(8,128)(2,1)}, bf16[112,896]{1,0:T(8,128)(2,1)S(1)}, u32[]{:S(2)}, u32[]{:S(2)}) collective-permute-start(bf16[112,896]{1,0:T(8,128)(2,1)} %collective-permute-done.5), channel_id=1, source_target_pairs={{0,1},{1,0},{2,3},{3,2},{4,5},{5,4},{6,7},{7,6},{8,9},{9,8},{10,11... | collective-permute-start | bytes 602120 | tf_op jit(solution)/shard_map/ppermute | solution.py:425
  82.8 10.2 %copy-start.3 = (bf16[4,3,144,896]{3,2,1,0:T(8,128)(2,1)}, bf16[4,3,144,896]{3,2,1,0:T(8,128)(2,1)S(1)}, u32[]{:S(2)}) copy-start(bf16[4,3,144,896]{3,2,1,0:T(8,128)(2,1)S(1)} %maximum_select_fusion.near_ref) | copy-start | bytes 9289732
  82.8 4.5 %copy-start.22 = (f32[1792]{0:T(1024)S(1)}, f32[1792]{0:T(1024)}, u32[]{:S(2)}) copy-start(f32[1792]{0:T(1024)} %param.21) | copy-start | bytes 21508
  82.8 8.7 %copy-start.8 = (bf16[4,16,4,1792]{3,1,2,0:T(8,128)(2,1)S(1)}, bf16[4,16,4,1792]{3,1,2,0:T(8,128)(2,1)}, u32[]{:S(2)}) copy-start(bf16[4,16,4,1792]{3,1,2,0:T(8,128)(2,1)} %copy-done.7) | copy-start | bytes 2752516
  82.8 12.5 %collective-permute-start.11 = (bf16[4,3,144,896]{3,2,1,0:T(8,128)(2,1)S(1)}, bf16[4,3,144,896]{3,2,1,0:T(8,128)(2,1)}, u32[]{:S(2)}, u32[]{:S(2)}) collective-permute-start(bf16[4,3,144,896]{3,2,1,0:T(8,128)(2,1)S(1)} %maximum_select_fusion.near_ref), channel_id=1, source_target_pairs={{0,16},{16,0},{1,17},{17,1},{2,18},{18,2},{3,19},{19,3},{4,20},{20... | collective-permute-start | bytes 9289736 | tf_op jit(solution)/shard_map/ppermute | solution.py:425
  87.0 37.5 %collective-permute-start.15 = (bf16[448,896]{1,0:T(8,128)(2,1)}, bf16[448,896]{1,0:T(8,128)(2,1)}, u32[]{:S(2)}, u32[]{:S(2)}) collective-permute-start(bf16[448,896]{1,0:T(8,128)(2,1)} %maximum_select_fusion.4), channel_id=1, source_target_pairs={{0,2},{1,3},{2,0},{3,1},{4,6},{5,7},{6,4},{7,5},{8,10},{9,11},{10,... | collective-permute-start | bytes 2408456 | tf_op jit(solution)/shard_map/ppermute | solution.py:425
  87.9 41.9 %collective-permute-start.18 = (bf16[3,112,896]{2,1,0:T(8,128)(2,1)}, bf16[3,112,896]{2,1,0:T(8,128)(2,1)}, u32[]{:S(2)}, u32[]{:S(2)}) collective-permute-start(bf16[3,112,896]{2,1,0:T(8,128)(2,1)} %pad_maximum_fusion), channel_id=1, source_target_pairs={{0,4},{4,0},{8,12},{12,8},{1,5},{5,1},{9,13},{13,9},{2,6},{6,2},{1... | collective-permute-start | bytes 1806344 | tf_op jit(solution)/shard_map/ppermute | solution.py:425
  89.9 41.0 %collective-permute-start.19 = (bf16[3,112,896]{2,1,0:T(8,128)(2,1)}, bf16[3,112,896]{2,1,0:T(8,128)(2,1)}, u32[]{:S(2)}, u32[]{:S(2)}) collective-permute-start(bf16[3,112,896]{2,1,0:T(8,128)(2,1)} %pad_maximum_fusion), channel_id=1, source_target_pairs={{0,8},{4,12},{8,0},{12,4},{1,9},{5,13},{9,1},{13,5},{2,10},{6,14},... | collective-permute-start | bytes 1806344 | tf_op jit(solution)/shard_map/ppermute | solution.py:425
  107.8 25.9 %collective-permute-start.14 = (bf16[4,640,128]{2,1,0:T(8,128)(2,1)}, bf16[4,640,128]{2,1,0:T(8,128)(2,1)S(1)}, u32[]{:S(2)}, u32[]{:S(2)}) collective-permute-start(bf16[4,640,128]{2,1,0:T(8,128)(2,1)} %get-tuple-element.13), channel_id=1, source_target_pairs={{0,12},{1,13},{2,14},{3,15},{16,28},{17,29},{18,30},{19,31}} | collective-permute-start | bytes 1966088 | tf_op jit(solution)/shard_map/ppermute | solution.py:474
  110.1 23.6 %collective-permute-start.13 = (bf16[4,640,128]{2,1,0:T(8,128)(2,1)}, bf16[4,640,128]{2,1,0:T(8,128)(2,1)S(1)}, u32[]{:S(2)}, u32[]{:S(2)}) collective-permute-start(bf16[4,640,128]{2,1,0:T(8,128)(2,1)} %get-tuple-element.13), channel_id=1, source_target_pairs={{0,8},{4,12},{1,9},{5,13},{2,10},{6,14},{3,11},{7,15},{16,24},{20,... | collective-permute-start | bytes 1966088 | tf_op jit(solution)/shard_map/ppermute | solution.py:474
  124.5 18.7 %collective-permute-start.12 = (bf16[4,640,128]{2,1,0:T(8,128)(2,1)}, bf16[4,640,128]{2,1,0:T(8,128)(2,1)S(1)}, u32[]{:S(2)}, u32[]{:S(2)}) collective-permute-start(bf16[4,640,128]{2,1,0:T(8,128)(2,1)} %get-tuple-element.13), channel_id=1, source_target_pairs={{0,4},{4,8},{8,12},{1,5},{5,9},{9,13},{2,6},{6,10},{10,14},{3,7},{... | collective-permute-start | bytes 1966088 | tf_op jit(solution)/shard_map/ppermute | solution.py:474
  129.8 14.8 %collective-permute-start.16 = (bf16[112,896]{1,0:T(8,128)(2,1)S(1)}, bf16[112,896]{1,0:T(8,128)(2,1)S(1)}, u32[]{:S(2)}, u32[]{:S(2)}) collective-permute-start(bf16[112,896]{1,0:T(8,128)(2,1)S(1)} %get-tuple-element.17), channel_id=1, source_target_pairs={{0,1},{1,0},{2,3},{3,2},{4,5},{5,4},{6,7},{7,6},{8,9},{9,8},{10,11... | collective-permute-start | bytes 602120 | tf_op jit(solution)/shard_map/ppermute | solution.py:425
  130.9 18.0 %collective-permute-start.21 = (bf16[3,48,896]{2,1,0:T(8,128)(2,1)S(1)}, bf16[3,48,896]{2,1,0:T(8,128)(2,1)S(1)}, u32[]{:S(2)}, u32[]{:S(2)}) collective-permute-start(bf16[3,48,896]{2,1,0:T(8,128)(2,1)S(1)} %slice_select_fusion.6), channel_id=1, source_target_pairs={{0,8},{4,12},{8,0},{12,4},{1,9},{5,13},{9,1},{13,5},{2,10},{6,14},... | collective-permute-start | bytes 774152 | tf_op jit(solution)/shard_map/ppermute | solution.py:425
  133.6 18.1 %collective-permute-start.20 = (bf16[3,64,896]{2,1,0:T(8,128)(2,1)S(1)}, bf16[3,64,896]{2,1,0:T(8,128)(2,1)S(1)}, u32[]{:S(2)}, u32[]{:S(2)}) collective-permute-start(bf16[3,64,896]{2,1,0:T(8,128)(2,1)S(1)} %slice_select_fusion.2), channel_id=1, source_target_pairs={{0,4},{4,0},{8,12},{12,8},{1,5},{5,1},{9,13},{13,9},{2,6},{6,2},{1... | collective-permute-start | bytes 1032200 | tf_op jit(solution)/shard_map/ppermute | solution.py:425
  133.8 10.9 %collective-permute-start.17 = (bf16[112,896]{1,0:T(8,128)(2,1)S(1)}, bf16[112,896]{1,0:T(8,128)(2,1)S(1)}, u32[]{:S(2)}, u32[]{:S(2)}) collective-permute-start(bf16[112,896]{1,0:T(8,128)(2,1)S(1)} %get-tuple-element.22), channel_id=1, source_target_pairs={{0,1},{1,0},{2,3},{3,2},{4,5},{5,4},{6,7},{7,6},{8,9},{9,8},{10,11... | collective-permute-start | bytes 602120 | tf_op jit(solution)/shard_map/ppermute | solution.py:425
  143.4 8.4 %copy-start.6 = (f32[4,640,128]{2,1,0:T(8,128)}, f32[4,640,128]{2,1,0:T(8,128)S(1)}, u32[]{:S(2)}) copy-start(f32[4,640,128]{2,1,0:T(8,128)S(1)} %convert_add_fusion.prior_ref) | copy-start | bytes 3932164
  151.9 5.0 %copy-start.23 = (f32[1792]{0:T(1024)S(1)}, f32[1792]{0:T(1024)}, u32[]{:S(2)}) copy-start(f32[1792]{0:T(1024)} %param.25) | copy-start | bytes 21508
  153.8 6.2 %copy-start.5 = (bf16[4,3,112,896]{3,2,1,0:T(8,128)(2,1)}, bf16[4,3,112,896]{3,2,1,0:T(8,128)(2,1)S(1)}, u32[]{:S(2)}) copy-start(bf16[4,3,112,896]{3,2,1,0:T(8,128)(2,1)S(1)} %maximum_select_fusion.1.near_ref) | copy-start | bytes 7225348
  153.8 4.7 %collective-permute-start.22 = (bf16[4,3,112,896]{3,2,1,0:T(8,128)(2,1)S(1)}, bf16[4,3,112,896]{3,2,1,0:T(8,128)(2,1)S(1)}, u32[]{:S(2)}, u32[]{:S(2)}) collective-permute-start(bf16[4,3,112,896]{3,2,1,0:T(8,128)(2,1)S(1)} %maximum_select_fusion.1.near_ref), channel_id=1, source_target_pairs={{0,16},{16,0},{1,17},{17,1},{2,18},{18,2},{3,19},{19,3},{4,20},{20... | collective-permute-start | bytes 7225352 | tf_op jit(solution)/shard_map/ppermute | solution.py:425
  154.9 20.1 %collective-permute-start.29 = (bf16[1,336,896]{2,1,0:T(8,128)(2,1)}, bf16[1,336,896]{2,1,0:T(8,128)(2,1)}, u32[]{:S(2)}, u32[]{:S(2)}) collective-permute-start(bf16[1,336,896]{2,1,0:T(8,128)(2,1)} %slice_select_fusion), channel_id=1, source_target_pairs={{0,8},{4,12},{8,0},{12,4},{1,9},{5,13},{9,1},{13,5},{2,10},{6,14},... | collective-permute-start | bytes 1806344 | tf_op jit(solution)/shard_map/ppermute | solution.py:425
  154.9 24.6 %collective-permute-start.28 = (bf16[1,336,896]{2,1,0:T(8,128)(2,1)}, bf16[1,336,896]{2,1,0:T(8,128)(2,1)}, u32[]{:S(2)}, u32[]{:S(2)}) collective-permute-start(bf16[1,336,896]{2,1,0:T(8,128)(2,1)} %slice_select_fusion), channel_id=1, source_target_pairs={{0,4},{4,0},{8,12},{12,8},{1,5},{5,1},{9,13},{13,9},{2,6},{6,2},{1... | collective-permute-start | bytes 1806344 | tf_op jit(solution)/shard_map/ppermute | solution.py:425
  158.4 1.5 copy-start.11
  172.1 33.9 %collective-permute-start.24 = (bf16[256,1792]{1,0:T(8,128)(2,1)}, bf16[256,1792]{1,0:T(8,128)(2,1)S(1)}, u32[]{:S(2)}, u32[]{:S(2)}) collective-permute-start(bf16[256,1792]{1,0:T(8,128)(2,1)} %get-tuple-element.14._.x_ref), channel_id=1, source_target_pairs={{0,1},{1,0},{2,3},{3,2},{4,5},{5,4},{6,7},{7,6},{8,9},{9,8},{10,11... | collective-permute-start | bytes 2752520 | tf_op jit(solution)/shard_map/ppermute | solution.py:425
  173.1 30.6 %collective-permute-start.26 = (bf16[3,112,896]{2,1,0:T(8,128)(2,1)}, bf16[3,112,896]{2,1,0:T(8,128)(2,1)S(1)}, u32[]{:S(2)}, u32[]{:S(2)}) collective-permute-start(bf16[3,112,896]{2,1,0:T(8,128)(2,1)} %broadcast_select_fusion.1), channel_id=1, source_target_pairs={{0,4},{4,0},{8,12},{12,8},{1,5},{5,1},{9,13},{13,9},{2,6},{6,2},{1... | collective-permute-start | bytes 1806344 | tf_op jit(solution)/shard_map/ppermute | solution.py:425
  173.4 31.5 %collective-permute-start.27 = (bf16[3,112,896]{2,1,0:T(8,128)(2,1)}, bf16[3,112,896]{2,1,0:T(8,128)(2,1)S(1)}, u32[]{:S(2)}, u32[]{:S(2)}) collective-permute-start(bf16[3,112,896]{2,1,0:T(8,128)(2,1)} %broadcast_select_fusion.1), channel_id=1, source_target_pairs={{0,8},{4,12},{8,0},{12,4},{1,9},{5,13},{9,1},{13,5},{2,10},{6,14},... | collective-permute-start | bytes 1806344 | tf_op jit(solution)/shard_map/ppermute | solution.py:425
  175.0 23.8 %collective-permute-start.25 = (bf16[80,1792]{1,0:T(8,128)(2,1)}, bf16[80,1792]{1,0:T(8,128)(2,1)S(1)}, u32[]{:S(2)}, u32[]{:S(2)}) collective-permute-start(bf16[80,1792]{1,0:T(8,128)(2,1)} %get-tuple-element.15), channel_id=1, source_target_pairs={{0,5},{1,4},{2,7},{3,6},{4,9},{5,8},{6,11},{7,10},{8,13},{9,12},{1... | collective-permute-start | bytes 860168 | tf_op jit(solution)/shard_map/ppermute | solution.py:648
  179.5 29.1 %collective-permute-start.30 = (bf16[1,176,896]{2,1,0:T(8,128)(2,1)S(1)}, bf16[1,176,896]{2,1,0:T(8,128)(2,1)S(1)}, u32[]{:S(2)}, u32[]{:S(2)}) collective-permute-start(bf16[1,176,896]{2,1,0:T(8,128)(2,1)S(1)} %slice_select_fusion.4), channel_id=1, source_target_pairs={{0,4},{4,0},{8,12},{12,8},{1,5},{5,1},{9,13},{13,9},{2,6},{6,2},{1... | collective-permute-start | bytes 946184 | tf_op jit(solution)/shard_map/ppermute | solution.py:425
  198.9 11.7 %copy-start.20 = (bf16[80,1792]{1,0:T(8,128)(2,1)}, bf16[80,1792]{1,0:T(8,128)(2,1)S(1)}, u32[]{:S(2)}) copy-start(bf16[80,1792]{1,0:T(8,128)(2,1)S(1)} %collective-permute-done.25.halo_ref) | copy-start | bytes 860164
  198.9 9.7 %collective-permute-start.31 = (bf16[1,160,896]{2,1,0:T(8,128)(2,1)S(1)}, bf16[1,160,896]{2,1,0:T(8,128)(2,1)S(1)}, u32[]{:S(2)}, u32[]{:S(2)}) collective-permute-start(bf16[1,160,896]{2,1,0:T(8,128)(2,1)S(1)} %slice_select_fusion.5), channel_id=1, source_target_pairs={{0,8},{4,12},{8,0},{12,4},{1,9},{5,13},{9,1},{13,5},{2,10},{6,14},... | collective-permute-start | bytes 860168 | tf_op jit(solution)/shard_map/ppermute | solution.py:425
  203.7 3.8 %copy-start.16 = (bf16[3,112,896]{2,1,0:T(8,128)(2,1)}, bf16[3,112,896]{2,1,0:T(8,128)(2,1)S(1)}, u32[]{:S(2)}) copy-start(bf16[3,112,896]{2,1,0:T(8,128)(2,1)S(1)} %collective-permute-done.26) | copy-start | bytes 1806340
  204.8 3.7 %copy-start.17 = (bf16[3,112,896]{2,1,0:T(8,128)(2,1)}, bf16[3,112,896]{2,1,0:T(8,128)(2,1)S(1)}, u32[]{:S(2)}) copy-start(bf16[3,112,896]{2,1,0:T(8,128)(2,1)S(1)} %collective-permute-done.27) | copy-start | bytes 1806340
  206.0 0.9 copy-start.15
  210.6 4.8 %copy-start.2 = (bf16[4,1,336,896]{3,2,1,0:T(8,128)(2,1)}, bf16[4,1,336,896]{3,2,1,0:T(8,128)(2,1)S(1)}, u32[]{:S(2)}) copy-start(bf16[4,1,336,896]{3,2,1,0:T(8,128)(2,1)S(1)} %maximum_select_fusion.2.near_ref) | copy-start | bytes 7225348
  210.6 4.8 %collective-permute-start.32 = (bf16[4,1,336,896]{3,2,1,0:T(8,128)(2,1)S(1)}, bf16[4,1,336,896]{3,2,1,0:T(8,128)(2,1)}, u32[]{:S(2)}, u32[]{:S(2)}) collective-permute-start(bf16[4,1,336,896]{3,2,1,0:T(8,128)(2,1)S(1)} %maximum_select_fusion.2.near_ref), channel_id=1, source_target_pairs={{0,16},{16,0},{1,17},{17,1},{2,18},{18,2},{3,19},{19,3},{4,20},{20... | collective-permute-start | bytes 7225352 | tf_op jit(solution)/shard_map/ppermute | solution.py:425
  210.7 20.6 %collective-permute-start.34 = (bf16[3,112,896]{2,1,0:T(8,128)(2,1)}, bf16[3,112,896]{2,1,0:T(8,128)(2,1)}, u32[]{:S(2)}, u32[]{:S(2)}) collective-permute-start(bf16[3,112,896]{2,1,0:T(8,128)(2,1)} %broadcast_select_fusion.1), channel_id=1, source_target_pairs={{0,12},{4,8},{8,4},{12,0},{1,13},{5,9},{9,5},{13,1},{2,14},{6,10},... | collective-permute-start | bytes 1806344 | tf_op jit(solution)/shard_map/ppermute | solution.py:425
  215.4 15.9 %copy-start.12 = (bf16[1,3,112,896]{3,2,1,0:T(8,128)(2,1)S(1)}, bf16[1,3,112,896]{3,2,1,0:T(8,128)(2,1)}, u32[]{:S(2)}) copy-start(bf16[1,3,112,896]{3,2,1,0:T(8,128)(2,1)} %fusion.14) | copy-start | bytes 1806340
  231.3 2.2 copy-start.13
  231.3 7.3 %copy-start.24 = (s32[8]{0:T(128)S(1)}, s32[8]{0:T(128)}, u32[]{:S(2)}) copy-start(s32[8]{0:T(128)} %param.20) | copy-start | bytes 100
  231.3 7.3 %copy-start.25 = (s32[8]{0:T(128)S(1)}, s32[8]{0:T(128)}, u32[]{:S(2)}) copy-start(s32[8]{0:T(128)} %param.19) | copy-start | bytes 100
  233.3 25.3 %copy-start.4 = (bf16[4,3,112,896]{3,2,1,0:T(8,128)(2,1)}, bf16[4,3,112,896]{3,2,1,0:T(8,128)(2,1)S(1)}, u32[]{:S(2)}) copy-start(bf16[4,3,112,896]{3,2,1,0:T(8,128)(2,1)S(1)} %maximum_select_fusion.3.near_ref) | copy-start | bytes 7225348
  233.3 25.4 %collective-permute-start.35 = (bf16[4,3,112,896]{3,2,1,0:T(8,128)(2,1)S(1)}, bf16[4,3,112,896]{3,2,1,0:T(8,128)(2,1)}, u32[]{:S(2)}, u32[]{:S(2)}) collective-permute-start(bf16[4,3,112,896]{3,2,1,0:T(8,128)(2,1)S(1)} %maximum_select_fusion.3.near_ref), channel_id=1, source_target_pairs={{0,16},{16,0},{1,17},{17,1},{2,18},{18,2},{3,19},{19,3},{4,20},{20... | collective-permute-start | bytes 7225352 | tf_op jit(solution)/shard_map/ppermute | solution.py:425
  233.5 25.1 %collective-permute-start.33 = (bf16[2,256,512]{2,1,0:T(8,128)(2,1)S(1)}, bf16[2,256,512]{2,1,0:T(8,128)(2,1)S(1)}, u32[]{:S(2)}, u32[]{:S(2)}) collective-permute-start(bf16[2,256,512]{2,1,0:T(8,128)(2,1)S(1)} %copy-done.13), channel_id=1, source_target_pairs={{0,1},{1,0},{2,3},{3,2},{4,5},{5,4},{6,7},{7,6},{8,9},{9,8},{10,11... | collective-permute-start | bytes 1572872 | tf_op jit(solution)/shard_map/ppermute | solution.py:425
  234.0 10.6 %collective-permute-start.23 = (bf16[80,1792]{1,0:T(8,128)(2,1)}, bf16[80,1792]{1,0:T(8,128)(2,1)}, u32[]{:S(2)}, u32[]{:S(2)}) collective-permute-start(bf16[80,1792]{1,0:T(8,128)(2,1)} %get-tuple-element.15), channel_id=1, source_target_pairs={{0,4},{4,8},{8,12},{1,5},{5,9},{9,13},{2,6},{6,10},{10,14},{3,7},{... | collective-permute-start | bytes 860168 | tf_op jit(solution)/shard_map/ppermute | solution.py:646
  258.6 0.8 copy-start.18
  266.1 28.2 %copy-start.1 = (bf16[64,4,1792]{2,1,0:T(4,128)(2,1)S(1)}, bf16[64,4,1792]{2,1,0:T(4,128)(2,1)}, u32[]{:S(2)}) copy-start(bf16[64,4,1792]{2,1,0:T(4,128)(2,1)} %param.17) | copy-start | bytes 2752516

commit v13 on v12

--- a/solution.py
+++ b/solution.py
@@ -452,10 +452,13 @@
     return across(held, "seq", 1), across(held, "seq", 2)
 
 
-def from_plane(held, near_by, diagonal, over_cores, over_across=()):
+def from_plane(held, near_by, diagonal, over_cores, by_one_way=False):
     beside, above = near_by
-    if diagonal is None:
-        opposite = across(after(held, over_across), "seq", 3)
+    if by_one_way:
+        beside = settled(beside, diagonal)
+        opposite = across(after(above, (beside,)), "seq", 1)
+    elif diagonal is None:
+        opposite = across(held, "seq", 3)
     else:
         half = -(-held.shape[1] // 32) * 16
         opposite = [
@@ -558,9 +561,12 @@
     length = jnp.sum(jnp.where(jnp.arange(slots_total) == slot, slot_lengths, 0))
 
     held_out_one = settled(jnp.stack(from_groups(own_piece([out_one]), (picked,))))
-    near_one = from_plane(held_one, neighbours(held_one), (swapped,), (held_out_one,))
+    beyond_piece = settled(own_piece([window_t, out_two]), (swapped,))
+    near_one = from_plane(
+        held_one, neighbours(held_one), (swapped,), (held_out_one, tokens, beyond_piece)
+    )
     out_piece = after(own_piece([out_two]), (swapped,))
-    beyond = from_group(own_piece([window_t, out_two]), (swapped,))
+    beyond = from_group(beyond_piece, ())
     first, second, ones, scale, kept = feature_tables(heads, feature_dim)
     first, second = jnp.asarray(first, BF16), jnp.asarray(second, BF16)
     column = np.zeros((1, heads * SLOT), np.float32)

time: 296 us -> 296 us (level)
    all_to_all x1, waiting for transfers between devices: 20.9 us -> 0.01 us  [on_device(): lax.all_to_all(picked, 'tensor', split_axis=0, concat_axis=0, tiled=True)]
    ppermute x31, waiting for transfers between devices: 33.7 us -> 53.3 us  [across(): lax.ppermute(array, axis, [(i, i ^ bit) for i in range(lax.axis_size(axis...]
    slice x15 -> x17, local copies, waits for them, and re-layouts: 10.4 us -> 12.5 us  [after(): lax.slice(other, (0,) * other.ndim, (1,) * other.ndim)]
  transfers between devices with their start and end apart: 38 -> 38, of which waited for: 15 -> 15; matrix products, arithmetic and copies ran while one was open for 14% -> 13% of each run, Pallas kernels for 17% -> 17%
where the time goes in v13:
time: 296 us; the launch traced here: 295 us
  waiting for transfers between devices  84.1 us (28%)
  Pallas kernels  57.7 us (19%)
  starting transfers between devices  55.4 us (19%)
  local copies, waits for them, and re-layouts  30.3 us (10%)
  other arithmetic  29.7 us (10%)
  blocking collectives  25.4 us (9%)
  between operations  12.3 us (4%)
    ppermute x31, waiting for transfers between devices, across(): lax.ppermute(array, axis, [(i, i ^ bit) for i in range(lax.axis_size(axis...  53.3 us
    ppermute x31, starting transfers between devices, across(): lax.ppermute(array, axis, [(i, i ^ bit) for i in range(lax.axis_size(axis...  33.6 us
    pallas_call x2, Pallas kernels, window_rows(): call(functools.partial(window_kernel, heads), 2, [SMEM, SMEM, *[HBM] * 5,...  28.3 us
    all_to_all x1, blocking collectives, on_device(): lax.all_to_all(result, 'tensor', split_axis=0, concat_axis=0, tiled=True)  25.4 us
    select_n x21, other arithmetic, after(): return jnp.where(zero == 0.0, array, jnp.zeros_like(array))  23 us
    ppermute x1, waiting for transfers between devices, on_device(): lax.ppermute(tail, ('seq', 'tensor'), [(i * group_count + j, (i + 1) * gr...  16.3 us
    slice x17, local copies, waits for them, and re-layouts, after(): lax.slice(other, (0,) * other.ndim, (1,) * other.ndim)  12.5 us
    pallas_call x1, Pallas kernels, on_device(): call(functools.partial(linear_kernel, heads, feature_dim, kept), group_co...  12.3 us
  transfers between devices with their start and end apart: 38, of which 15 were waited for; matrix products, arithmetic and copies ran while one was open for 13% of the time, Pallas kernels for 17%

profile of v13, /device:TPU:0, one launch (start us, length us, event | category | flops | bytes accessed | tf_op | source)
XLA Modules:
  0.0 295.0 jit_solution(14071724823379900039)
XLA Ops:
  1.9 4.1 %collective-permute-start.2 = (bf16[144,896]{1,0:T(8,128)(2,1)S(1)}, bf16[144,896]{1,0:T(8,128)(2,1)S(1)}, u32[]{:S(2)}, u32[]{:S(2)}) collective-permute-start(bf16[144,896]{1,0:T(8,128)(2,1)S(1)} %pad_maximum_fusion.1), channel_id=1, source_target_pairs={{0,2},{1,3},{2,0},{3,1},{4,6},{5,7},{6,4},{7,5},{8,10},{9,11},{10,... | collective-permute-start | bytes 774152 | tf_op jit(solution)/shard_map/ppermute | solution.py:425
  6.0 1.6 collective-permute-start.1
  10.0 2.2 gather_fusion.1
  12.2 3.7 %all-to-all-start = ((bf16[8,8,4,1792]{3,2,1,0:T(4,128)(2,1)}), bf16[8,8,4,1792]{3,2,1,0:T(4,128)(2,1)S(1)}, u32[]{:S(2)}, u32[]{:S(2)}) async-start(bf16[8,8,4,1792]{3,2,1,0:T(4,128)(2,1)} %bitcast.20), calls=%async_computation | async-start | bytes 1835008 | tf_op jit(solution)/shard_map/all_to_all | solution.py:551
  18.6 3.1 %collective-permute-done = f32[3,1536]{1,0:T(4,128)S(1)} collective-permute-done((f32[3,1536]{1,0:T(4,128)S(1)}, f32[3,1536]{1,0:T(4,128)S(1)}, u32[]{:S(2)}, u32[]{:S(2)}) %collective-permute-start) | collective-permute-done | bytes 18464 | tf_op jit(solution)/shard_map/ppermute | solution.py:425
  22.9 3.4 %collective-permute-done.3 = bf16[144,896]{1,0:T(8,128)(2,1)S(1)} collective-permute-done((bf16[144,896]{1,0:T(8,128)(2,1)S(1)}, bf16[144,896]{1,0:T(8,128)(2,1)S(1)}, u32[]{:S(2)}, u32[]{:S(2)}) %collective-permute-start.3) | collective-permute-done | bytes 258080 | tf_op jit(solution)/shard_map/ppermute | solution.py:425
  27.6 1.8 all-to-all-done
  29.4 1.3 gather_fusion.2
  32.2 3.5 %all-to-all-start.1 = ((bf16[4,16,4,1792]{3,1,2,0:T(8,128)(2,1)}), bf16[4,16,4,1792]{3,1,2,0:T(8,128)(2,1)S(1)}, u32[]{:S(2)}, u32[]{:S(2)}) async-start(bf16[4,16,4,1792]{3,1,2,0:T(8,128)(2,1)} %copy.47), calls=%async_computation.1 | async-start | bytes 1835008 | tf_op jit(solution)/shard_map/all_to_all | solution.py:558
  35.7 1.1 collective-permute-start.8
  36.8 1.1 collective-permute-start.7
  40.0 3.0 %collective-permute-start.5 = (bf16[112,896]{1,0:T(8,128)(2,1)S(1)}, bf16[112,896]{1,0:T(8,128)(2,1)S(1)}, u32[]{:S(2)}, u32[]{:S(2)}) collective-permute-start(bf16[112,896]{1,0:T(8,128)(2,1)S(1)} %select_bitcast_fusion.1), channel_id=1, source_target_pairs={{0,2},{1,3},{2,0},{3,1},{4,6},{5,7},{6,4},{7,5},{8,10},{9,11},{10,... | collective-permute-start | bytes 602120 | tf_op jit(solution)/shard_map/ppermute | solution.py:425
  43.0 1.1 constant_dynamic-slice_fusion
  44.1 1.5 collective-permute-start.4
  45.7 22.3 %collective-permute-done.5 = bf16[112,896]{1,0:T(8,128)(2,1)S(1)} collective-permute-done((bf16[112,896]{1,0:T(8,128)(2,1)S(1)}, bf16[112,896]{1,0:T(8,128)(2,1)S(1)}, u32[]{:S(2)}, u32[]{:S(2)}) %collective-permute-start.5) | collective-permute-done | bytes 200736 | tf_op jit(solution)/shard_map/ppermute | solution.py:425
  69.1 1.8 slice_select_fusion.1
  71.7 1.0 slice_select_fusion.3
  73.2 1.1 collective-permute-done.6
  75.2 1.1 slice.126
  78.3 1.6 broadcast_select_fusion.2
  80.0 1.0 maximum_select_fusion.4
  81.0 1.2 slice.129
  83.6 1.1 maximum_select_fusion.6
  84.8 1.9 maximum_select_fusion.near_ref
  88.4 1.2 collective-permute-start.18
  90.3 1.6 collective-permute-start.19
  92.5 12.3 %linear_rows.1 = (f32[4,256,512]{2,1,0:T(8,128)}, bf16[4,256,128]{2,1,0:T(8,128)(2,1)}, bf16[4,640,128]{2,1,0:T(8,128)(2,1)}) custom-call(s32[5]{0:T(128)} %pad_add_fusion.place_ref, bf16[256,1792]{1,0:T(8,128)(2,1)} %copy-done.6, f32[1,1792]{1,0:T(1,128)} %broadcast_in_dim.128.gain_ref, bf16[1,4,112,1792]{3,2,1,0:T(8,128)(2,1)} %bitcast.103, ...), custom_call_target="tpu_custom_call" | custom-call | tf_op jit(solution)/shard_map/linear_rows/pallas_call | solution.py:582
  104.9 3.1 %collective-permute-start.14 = (bf16[4,640,128]{2,1,0:T(8,128)(2,1)}, bf16[4,640,128]{2,1,0:T(8,128)(2,1)S(1)}, u32[]{:S(2)}, u32[]{:S(2)}) collective-permute-start(bf16[4,640,128]{2,1,0:T(8,128)(2,1)} %get-tuple-element.13), channel_id=1, source_target_pairs={{0,12},{1,13},{2,14},{3,15},{16,28},{17,29},{18,30},{19,31}} | collective-permute-start | bytes 1966088 | tf_op jit(solution)/shard_map/ppermute | solution.py:477
  108.0 1.3 collective-permute-start.13
  109.4 1.2 slice.101
  111.2 14.2 %collective-permute-done.15 = bf16[448,896]{1,0:T(8,128)(2,1)S(1)} collective-permute-done((bf16[448,896]{1,0:T(8,128)(2,1)}, bf16[448,896]{1,0:T(8,128)(2,1)S(1)}, u32[]{:S(2)}, u32[]{:S(2)}) %collective-permute-start.15) | collective-permute-done | bytes 802848 | tf_op jit(solution)/shard_map/ppermute | solution.py:425
  125.4 2.7 collective-permute-start.12
  128.2 1.2 select_bitcast_fusion
  131.0 1.2 collective-permute-start.21
  132.2 1.0 slice_select_fusion.2
  133.6 2.0 collective-permute-start.17
  135.6 7.8 %collective-permute-done.12 = bf16[4,640,128]{2,1,0:T(8,128)(2,1)S(1)} collective-permute-done((bf16[4,640,128]{2,1,0:T(8,128)(2,1)}, bf16[4,640,128]{2,1,0:T(8,128)(2,1)S(1)}, u32[]{:S(2)}, u32[]{:S(2)}) %collective-permute-start.12) | collective-permute-done | bytes 655392 | tf_op jit(solution)/shard_map/ppermute | solution.py:477
  146.8 1.6 collective-permute-done.21
  148.3 2.9 collective-permute-done.20
  151.4 1.9 maximum_select_fusion.1.near_ref
  153.3 1.0 slice_select_fusion
  154.4 1.7 collective-permute-start.28
  156.7 1.2 collective-permute-done.22.far_ref
  157.9 1.5 copy-done.11
  159.4 10.4 %linear_out.1 = (bf16[256,1792]{1,0:T(8,128)(2,1)}, bf16[256,1792]{1,0:T(8,128)(2,1)}, bf16[80,1792]{1,0:T(8,128)(2,1)}) custom-call(s32[5]{0:T(128)} %pad_add_fusion.place_ref, f32[4,256,512]{2,1,0:T(8,128)} %get-tuple-element.11.num_ref, bf16[4,256,128]{2,1,0:T(8,128)(2,1)} %get-tuple-element.12.q_ref, bf16[128,1024]{1,0:T(8,128)(2,1)} %constant.131.clone.first_ref, ...), custom_call_target="tpu_custom_call" | custom-call | tf_op jit(solution)/shard_map/linear_out/pallas_call | solution.py:622
  169.8 1.2 slice.110
  173.2 1.2 collective-permute-start.27
  174.4 3.6 %collective-permute-start.25 = (bf16[80,1792]{1,0:T(8,128)(2,1)}, bf16[80,1792]{1,0:T(8,128)(2,1)S(1)}, u32[]{:S(2)}, u32[]{:S(2)}) collective-permute-start(bf16[80,1792]{1,0:T(8,128)(2,1)} %get-tuple-element.15), channel_id=1, source_target_pairs={{0,5},{1,4},{2,7},{3,6},{4,9},{5,8},{6,11},{7,10},{8,13},{9,12},{1... | collective-permute-start | bytes 860168 | tf_op jit(solution)/shard_map/ppermute | solution.py:654
  178.1 1.0 slice_select_fusion.4
  179.1 2.1 collective-permute-start.30
  182.1 16.3 %collective-permute-done.25.halo_ref = bf16[80,1792]{1,0:T(8,128)(2,1)S(1)} collective-permute-done((bf16[80,1792]{1,0:T(8,128)(2,1)}, bf16[80,1792]{1,0:T(8,128)(2,1)S(1)}, u32[]{:S(2)}, u32[]{:S(2)}) %collective-permute-start.25) | collective-permute-done | bytes 286752 | tf_op jit(solution)/shard_map/ppermute | solution.py:654
  198.5 3.6 %collective-permute-start.31 = (bf16[1,160,896]{2,1,0:T(8,128)(2,1)S(1)}, bf16[1,160,896]{2,1,0:T(8,128)(2,1)S(1)}, u32[]{:S(2)}, u32[]{:S(2)}) collective-permute-start(bf16[1,160,896]{2,1,0:T(8,128)(2,1)S(1)} %slice_select_fusion.5), channel_id=1, source_target_pairs={{0,8},{4,12},{8,0},{12,4},{1,9},{5,13},{9,1},{13,5},{2,10},{6,14},... | collective-permute-start | bytes 860168 | tf_op jit(solution)/shard_map/ppermute | solution.py:425
  208.8 1.9 maximum_select_fusion.2.near_ref
  210.8 1.4 collective-permute-start.34
  213.2 2.4 collective-permute-done.32.far_ref
  215.6 14.1 %window_rows.2._ = bf16[2,256,512]{2,1,0:T(8,128)(2,1)} custom-call(s32[5]{0:T(128)} %pad_add_fusion.place_ref, s32[1]{0:T(128)} %bitcast.2.first_ref, bf16[256,1792]{1,0:T(8,128)(2,1)} %copy-done.13, bf16[80,1792]{1,0:T(8,128)(2,1)} %copy-done.19, bf16[3,4,112,1792]{3,2,1,0:T(8,128)(2,1)} %bitcast.93, bf16[4,1,336,896]{3,2,1,0:T(8,128)(2,1)} %copy-done.2, ...), custom_call_target="tpu_custom_call" | custom-call | tf_op jit(solution)/shard_map/window_rows/pallas_call | solution.py:671
  229.7 1.1 slice.145
  231.6 1.9 maximum_select_fusion.3.near_ref
  234.0 3.8 %collective-permute-start.23 = (bf16[80,1792]{1,0:T(8,128)(2,1)}, bf16[80,1792]{1,0:T(8,128)(2,1)S(1)}, u32[]{:S(2)}, u32[]{:S(2)}) collective-permute-start(bf16[80,1792]{1,0:T(8,128)(2,1)} %get-tuple-element.15), channel_id=1, source_target_pairs={{0,4},{4,8},{8,12},{1,5},{5,9},{9,13},{2,6},{6,10},{10,14},{3,7},{... | collective-permute-start | bytes 860168 | tf_op jit(solution)/shard_map/ppermute | solution.py:652
  239.3 4.9 %collective-permute-done.23.halo_ref = bf16[80,1792]{1,0:T(8,128)(2,1)S(1)} collective-permute-done((bf16[80,1792]{1,0:T(8,128)(2,1)}, bf16[80,1792]{1,0:T(8,128)(2,1)S(1)}, u32[]{:S(2)}, u32[]{:S(2)}) %collective-permute-start.23) | collective-permute-done | bytes 286752 | tf_op jit(solution)/shard_map/ppermute | solution.py:652
  244.9 14.1 %window_rows.3.mixed_ref = bf16[2,256,512]{2,1,0:T(8,128)(2,1)} custom-call(s32[5]{0:T(128)} %pad_add_fusion.place_ref, s32[1]{0:T(128)} %bitcast.2.first_ref, bf16[256,1792]{1,0:T(8,128)(2,1)} %get-tuple-element.14._.x_ref, bf16[80,1792]{1,0:T(8,128)(2,1)} %copy-done.20, bf16[3,4,112,1792]{3,2,1,0:T(8,128)(2,1)} %bitcast.94, ...), custom_call_target="tpu_custom_call" | custom-call | tf_op jit(solution)/shard_map/window_rows/pallas_call | solution.py:671
  259.8 6.6 %window_out.1 = bf16[256,1792]{1,0:T(8,128)(2,1)} custom-call(s32[5]{0:T(128)} %pad_add_fusion.place_ref, s32[1]{0:T(128)} %bitcast.1.live_ref, bf16[2,256,512]{2,1,0:T(8,128)(2,1)} %window_rows.3.mixed_ref, bf16[2,256,512]{2,1,0:T(8,128)(2,1)} %copy-done.17, bf16[1,4,112,1792]{3,2,1,0:T(8,128)(2,1)} %bitcast.107, bf16[4,3,112,896]{3,2,1,0:T(8,128)(2,1)} %copy-done.4, ...), custom_call_target="tpu_custom_call" | custom-call | tf_op jit(solution)/shard_map/window_out/pallas_call | solution.py:696
  266.5 1.9 reshape.560
  268.7 25.4 %all_to_all.15 = bf16[4,16,4,1792]{3,2,1,0:T(4,128)(2,1)S(1)} all-to-all(bf16[4,16,4,1792]{3,2,1,0:T(4,128)(2,1)S(1)} %bitcast.98), channel_id=1, replica_groups=mesh['dp'=2,'seq'=4,'tensor'=4] {'tensor'}, dimensions={0} | all-to-all | bytes 1835008 | tf_op jit(solution)/shard_map/all_to_all | solution.py:717
  (162 shorter events, 33.8 us)
Async XLA Ops:
  0.0 9.9 %copy-start = (bf16[64,4,1792]{2,1,0:T(4,128)(2,1)S(1)}, bf16[64,4,1792]{2,1,0:T(4,128)(2,1)}, u32[]{:S(2)}) copy-start(bf16[64,4,1792]{2,1,0:T(4,128)(2,1)} %param.17) | copy-start | bytes 2752516
  0.9 15.0 %copy-start.21 = (f32[3,3,448]{2,1,0:T(4,128)S(1)}, f32[3,3,448]{2,1,0:T(4,128)}, u32[]{:S(2)}) copy-start(f32[3,3,448]{2,1,0:T(4,128)} %param.27) | copy-start | bytes 48388
  1.9 16.0 %collective-permute-start.2 = (bf16[144,896]{1,0:T(8,128)(2,1)S(1)}, bf16[144,896]{1,0:T(8,128)(2,1)S(1)}, u32[]{:S(2)}, u32[]{:S(2)}) collective-permute-start(bf16[144,896]{1,0:T(8,128)(2,1)S(1)} %pad_maximum_fusion.1), channel_id=1, source_target_pairs={{0,2},{1,3},{2,0},{3,1},{4,6},{5,7},{6,4},{7,5},{8,10},{9,11},{10,... | collective-permute-start | bytes 774152 | tf_op jit(solution)/shard_map/ppermute | solution.py:425
  6.0 16.9 %collective-permute-start.1 = (bf16[144,896]{1,0:T(8,128)(2,1)S(1)}, bf16[144,896]{1,0:T(8,128)(2,1)S(1)}, u32[]{:S(2)}, u32[]{:S(2)}) collective-permute-start(bf16[144,896]{1,0:T(8,128)(2,1)S(1)} %pad_maximum_fusion.1), channel_id=1, source_target_pairs={{0,1},{1,0},{2,3},{3,2},{4,5},{5,4},{6,7},{7,6},{8,9},{9,8},{10,11... | collective-permute-start | bytes 774152 | tf_op jit(solution)/shard_map/ppermute | solution.py:425
  12.2 17.2 %all-to-all-start = ((bf16[8,8,4,1792]{3,2,1,0:T(4,128)(2,1)}), bf16[8,8,4,1792]{3,2,1,0:T(4,128)(2,1)S(1)}, u32[]{:S(2)}, u32[]{:S(2)}) async-start(bf16[8,8,4,1792]{3,2,1,0:T(4,128)(2,1)} %bitcast.20), calls=%async_computation | async-start | bytes 1835008 | tf_op jit(solution)/shard_map/all_to_all | solution.py:551
  16.6 5.0 %collective-permute-start = (f32[3,1536]{1,0:T(4,128)S(1)}, f32[3,1536]{1,0:T(4,128)S(1)}, u32[]{:S(2)}, u32[]{:S(2)}) collective-permute-start(f32[3,1536]{1,0:T(4,128)S(1)} %reshape.544), channel_id=1, source_target_pairs={{0,2},{1,3},{2,0},{3,1},{4,6},{5,7},{6,4},{7,5},{8,10},{9,11},{10,... | collective-permute-start | bytes 55304 | tf_op jit(solution)/shard_map/ppermute | solution.py:425
  17.9 8.4 %collective-permute-start.3 = (bf16[144,896]{1,0:T(8,128)(2,1)S(1)}, bf16[144,896]{1,0:T(8,128)(2,1)S(1)}, u32[]{:S(2)}, u32[]{:S(2)}) collective-permute-start(bf16[144,896]{1,0:T(8,128)(2,1)S(1)} %collective-permute-done.2), channel_id=1, source_target_pairs={{0,1},{1,0},{2,3},{3,2},{4,5},{5,4},{6,7},{7,6},{8,9},{9,8},{10,11... | collective-permute-start | bytes 774152 | tf_op jit(solution)/shard_map/ppermute | solution.py:425
  21.7 9.4 %copy-start.18 = (f32[2,3,1536]{2,1,0:T(4,128)}, f32[2,3,1536]{2,1,0:T(4,128)S(1)}, u32[]{:S(2)}) copy-start(f32[2,3,1536]{2,1,0:T(4,128)S(1)} %pad_maximum_fusion.2.tap_ref) | copy-start | bytes 110596
  26.4 10.4 %copy-start.10 = (bf16[3,144,896]{2,1,0:T(8,128)(2,1)}, bf16[3,144,896]{2,1,0:T(8,128)(2,1)S(1)}, u32[]{:S(2)}) copy-start(bf16[3,144,896]{2,1,0:T(8,128)(2,1)S(1)} %maximum_select_fusion.5) | copy-start | bytes 2322436
  32.2 35.7 %all-to-all-start.1 = ((bf16[4,16,4,1792]{3,1,2,0:T(8,128)(2,1)}), bf16[4,16,4,1792]{3,1,2,0:T(8,128)(2,1)S(1)}, u32[]{:S(2)}, u32[]{:S(2)}) async-start(bf16[4,16,4,1792]{3,1,2,0:T(8,128)(2,1)} %copy.47), calls=%async_computation.1 | async-start | bytes 1835008 | tf_op jit(solution)/shard_map/all_to_all | solution.py:558
  35.7 33.4 %collective-permute-start.8 = (bf16[3,144,896]{2,1,0:T(8,128)(2,1)S(1)}, bf16[3,144,896]{2,1,0:T(8,128)(2,1)}, u32[]{:S(2)}, u32[]{:S(2)}) collective-permute-start(bf16[3,144,896]{2,1,0:T(8,128)(2,1)S(1)} %maximum_select_fusion.5), channel_id=1, source_target_pairs={{0,8},{4,12},{8,0},{12,4},{1,9},{5,13},{9,1},{13,5},{2,10},{6,14},... | collective-permute-start | bytes 2322440 | tf_op jit(solution)/shard_map/ppermute | solution.py:425
  36.8 34.9 %collective-permute-start.7 = (bf16[3,144,896]{2,1,0:T(8,128)(2,1)S(1)}, bf16[3,144,896]{2,1,0:T(8,128)(2,1)}, u32[]{:S(2)}, u32[]{:S(2)}) collective-permute-start(bf16[3,144,896]{2,1,0:T(8,128)(2,1)S(1)} %maximum_select_fusion.5), channel_id=1, source_target_pairs={{0,4},{4,0},{8,12},{12,8},{1,5},{5,1},{9,13},{13,9},{2,6},{6,2},{1... | collective-permute-start | bytes 2322440 | tf_op jit(solution)/shard_map/ppermute | solution.py:425
  40.0 27.9 %collective-permute-start.5 = (bf16[112,896]{1,0:T(8,128)(2,1)S(1)}, bf16[112,896]{1,0:T(8,128)(2,1)S(1)}, u32[]{:S(2)}, u32[]{:S(2)}) collective-permute-start(bf16[112,896]{1,0:T(8,128)(2,1)S(1)} %select_bitcast_fusion.1), channel_id=1, source_target_pairs={{0,2},{1,3},{2,0},{3,1},{4,6},{5,7},{6,4},{7,5},{8,10},{9,11},{10,... | collective-permute-start | bytes 602120 | tf_op jit(solution)/shard_map/ppermute | solution.py:425
  44.1 29.1 %collective-permute-start.4 = (bf16[112,896]{1,0:T(8,128)(2,1)S(1)}, bf16[112,896]{1,0:T(8,128)(2,1)S(1)}, u32[]{:S(2)}, u32[]{:S(2)}) collective-permute-start(bf16[112,896]{1,0:T(8,128)(2,1)S(1)} %select_bitcast_fusion.1), channel_id=1, source_target_pairs={{0,1},{1,0},{2,3},{3,2},{4,5},{5,4},{6,7},{7,6},{8,9},{9,8},{10,11... | collective-permute-start | bytes 602120 | tf_op jit(solution)/shard_map/ppermute | solution.py:425
  67.9 6.4 %collective-permute-start.6 = (bf16[112,896]{1,0:T(8,128)(2,1)S(1)}, bf16[112,896]{1,0:T(8,128)(2,1)S(1)}, u32[]{:S(2)}, u32[]{:S(2)}) collective-permute-start(bf16[112,896]{1,0:T(8,128)(2,1)S(1)} %collective-permute-done.5), channel_id=1, source_target_pairs={{0,1},{1,0},{2,3},{3,2},{4,5},{5,4},{6,7},{7,6},{8,9},{9,8},{10,11... | collective-permute-start | bytes 602120 | tf_op jit(solution)/shard_map/ppermute | solution.py:425
  70.9 12.7 %collective-permute-start.9 = (bf16[3,80,896]{2,1,0:T(8,128)(2,1)}, bf16[3,80,896]{2,1,0:T(8,128)(2,1)}, u32[]{:S(2)}, u32[]{:S(2)}) collective-permute-start(bf16[3,80,896]{2,1,0:T(8,128)(2,1)} %slice_select_fusion.1), channel_id=1, source_target_pairs={{0,4},{4,0},{8,12},{12,8},{1,5},{5,1},{9,13},{13,9},{2,6},{6,2},{1... | collective-permute-start | bytes 1290248 | tf_op jit(solution)/shard_map/ppermute | solution.py:425
  72.8 10.9 %collective-permute-start.10 = (bf16[3,64,896]{2,1,0:T(8,128)(2,1)S(1)}, bf16[3,64,896]{2,1,0:T(8,128)(2,1)S(1)}, u32[]{:S(2)}, u32[]{:S(2)}) collective-permute-start(bf16[3,64,896]{2,1,0:T(8,128)(2,1)S(1)} %slice_select_fusion.3), channel_id=1, source_target_pairs={{0,8},{4,12},{8,0},{12,4},{1,9},{5,13},{9,1},{13,5},{2,10},{6,14},... | collective-permute-start | bytes 1032200 | tf_op jit(solution)/shard_map/ppermute | solution.py:425
  77.7 9.0 %copy-start.6 = (bf16[256,1792]{1,0:T(8,128)(2,1)}, bf16[256,1792]{1,0:T(8,128)(2,1)S(1)}, u32[]{:S(2)}) copy-start(bf16[256,1792]{1,0:T(8,128)(2,1)S(1)} %reshape.554.x_ref) | copy-start | bytes 2752516
  84.8 3.0 %copy-start.22 = (f32[1792]{0:T(1024)S(1)}, f32[1792]{0:T(1024)}, u32[]{:S(2)}) copy-start(f32[1792]{0:T(1024)} %param.21) | copy-start | bytes 21508
  86.7 5.8 %copy-start.3 = (bf16[4,3,144,896]{3,2,1,0:T(8,128)(2,1)}, bf16[4,3,144,896]{3,2,1,0:T(8,128)(2,1)S(1)}, u32[]{:S(2)}) copy-start(bf16[4,3,144,896]{3,2,1,0:T(8,128)(2,1)S(1)} %maximum_select_fusion.near_ref) | copy-start | bytes 9289732
  86.7 5.8 %collective-permute-start.11 = (bf16[4,3,144,896]{3,2,1,0:T(8,128)(2,1)S(1)}, bf16[4,3,144,896]{3,2,1,0:T(8,128)(2,1)}, u32[]{:S(2)}, u32[]{:S(2)}) collective-permute-start(bf16[4,3,144,896]{3,2,1,0:T(8,128)(2,1)S(1)} %maximum_select_fusion.near_ref), channel_id=1, source_target_pairs={{0,16},{16,0},{1,17},{17,1},{2,18},{18,2},{3,19},{19,3},{4,20},{20... | collective-permute-start | bytes 9289736 | tf_op jit(solution)/shard_map/ppermute | solution.py:425
  86.8 38.6 %collective-permute-start.15 = (bf16[448,896]{1,0:T(8,128)(2,1)}, bf16[448,896]{1,0:T(8,128)(2,1)S(1)}, u32[]{:S(2)}, u32[]{:S(2)}) collective-permute-start(bf16[448,896]{1,0:T(8,128)(2,1)} %maximum_select_fusion.4), channel_id=1, source_target_pairs={{0,2},{1,3},{2,0},{3,1},{4,6},{5,7},{6,4},{7,5},{8,10},{9,11},{10,... | collective-permute-start | bytes 2408456 | tf_op jit(solution)/shard_map/ppermute | solution.py:425
  88.4 41.5 %collective-permute-start.18 = (bf16[3,112,896]{2,1,0:T(8,128)(2,1)}, bf16[3,112,896]{2,1,0:T(8,128)(2,1)}, u32[]{:S(2)}, u32[]{:S(2)}) collective-permute-start(bf16[3,112,896]{2,1,0:T(8,128)(2,1)} %pad_maximum_fusion), channel_id=1, source_target_pairs={{0,4},{4,0},{8,12},{12,8},{1,5},{5,1},{9,13},{13,9},{2,6},{6,2},{1... | collective-permute-start | bytes 1806344 | tf_op jit(solution)/shard_map/ppermute | solution.py:425
  90.3 40.7 %collective-permute-start.19 = (bf16[3,112,896]{2,1,0:T(8,128)(2,1)}, bf16[3,112,896]{2,1,0:T(8,128)(2,1)}, u32[]{:S(2)}, u32[]{:S(2)}) collective-permute-start(bf16[3,112,896]{2,1,0:T(8,128)(2,1)} %pad_maximum_fusion), channel_id=1, source_target_pairs={{0,8},{4,12},{8,0},{12,4},{1,9},{5,13},{9,1},{13,5},{2,10},{6,14},... | collective-permute-start | bytes 1806344 | tf_op jit(solution)/shard_map/ppermute | solution.py:425
  104.9 28.3 %collective-permute-start.14 = (bf16[4,640,128]{2,1,0:T(8,128)(2,1)}, bf16[4,640,128]{2,1,0:T(8,128)(2,1)S(1)}, u32[]{:S(2)}, u32[]{:S(2)}) collective-permute-start(bf16[4,640,128]{2,1,0:T(8,128)(2,1)} %get-tuple-element.13), channel_id=1, source_target_pairs={{0,12},{1,13},{2,14},{3,15},{16,28},{17,29},{18,30},{19,31}} | collective-permute-start | bytes 1966088 | tf_op jit(solution)/shard_map/ppermute | solution.py:477
  108.0 25.5 %collective-permute-start.13 = (bf16[4,640,128]{2,1,0:T(8,128)(2,1)}, bf16[4,640,128]{2,1,0:T(8,128)(2,1)S(1)}, u32[]{:S(2)}, u32[]{:S(2)}) collective-permute-start(bf16[4,640,128]{2,1,0:T(8,128)(2,1)} %get-tuple-element.13), channel_id=1, source_target_pairs={{0,8},{4,12},{1,9},{5,13},{2,10},{6,14},{3,11},{7,15},{16,24},{20,... | collective-permute-start | bytes 1966088 | tf_op jit(solution)/shard_map/ppermute | solution.py:477
  125.4 2.7 copy-start.14
  125.4 18.0 %collective-permute-start.12 = (bf16[4,640,128]{2,1,0:T(8,128)(2,1)}, bf16[4,640,128]{2,1,0:T(8,128)(2,1)S(1)}, u32[]{:S(2)}, u32[]{:S(2)}) collective-permute-start(bf16[4,640,128]{2,1,0:T(8,128)(2,1)} %get-tuple-element.13), channel_id=1, source_target_pairs={{0,4},{4,8},{8,12},{1,5},{5,9},{9,13},{2,6},{6,10},{10,14},{3,7},{... | collective-permute-start | bytes 1966088 | tf_op jit(solution)/shard_map/ppermute | solution.py:477
  129.9 14.9 %collective-permute-start.16 = (bf16[112,896]{1,0:T(8,128)(2,1)}, bf16[112,896]{1,0:T(8,128)(2,1)S(1)}, u32[]{:S(2)}, u32[]{:S(2)}) collective-permute-start(bf16[112,896]{1,0:T(8,128)(2,1)} %get-tuple-element.17), channel_id=1, source_target_pairs={{0,1},{1,0},{2,3},{3,2},{4,5},{5,4},{6,7},{7,6},{8,9},{9,8},{10,11... | collective-permute-start | bytes 602120 | tf_op jit(solution)/shard_map/ppermute | solution.py:425
  131.0 17.3 %collective-permute-start.21 = (bf16[3,48,896]{2,1,0:T(8,128)(2,1)S(1)}, bf16[3,48,896]{2,1,0:T(8,128)(2,1)S(1)}, u32[]{:S(2)}, u32[]{:S(2)}) collective-permute-start(bf16[3,48,896]{2,1,0:T(8,128)(2,1)S(1)} %slice_select_fusion.6), channel_id=1, source_target_pairs={{0,8},{4,12},{8,0},{12,4},{1,9},{5,13},{9,1},{13,5},{2,10},{6,14},... | collective-permute-start | bytes 774152 | tf_op jit(solution)/shard_map/ppermute | solution.py:425
  133.2 18.0 %collective-permute-start.20 = (bf16[3,64,896]{2,1,0:T(8,128)(2,1)S(1)}, bf16[3,64,896]{2,1,0:T(8,128)(2,1)S(1)}, u32[]{:S(2)}, u32[]{:S(2)}) collective-permute-start(bf16[3,64,896]{2,1,0:T(8,128)(2,1)S(1)} %slice_select_fusion.2), channel_id=1, source_target_pairs={{0,4},{4,0},{8,12},{12,8},{1,5},{5,1},{9,13},{13,9},{2,6},{6,2},{1... | collective-permute-start | bytes 1032200 | tf_op jit(solution)/shard_map/ppermute | solution.py:425
  133.6 11.3 %collective-permute-start.17 = (bf16[112,896]{1,0:T(8,128)(2,1)S(1)}, bf16[112,896]{1,0:T(8,128)(2,1)S(1)}, u32[]{:S(2)}, u32[]{:S(2)}) collective-permute-start(bf16[112,896]{1,0:T(8,128)(2,1)S(1)} %get-tuple-element.22), channel_id=1, source_target_pairs={{0,1},{1,0},{2,3},{3,2},{4,5},{5,4},{6,7},{7,6},{8,9},{9,8},{10,11... | collective-permute-start | bytes 602120 | tf_op jit(solution)/shard_map/ppermute | solution.py:425
  143.6 7.7 %copy-start.9 = (f32[4,640,128]{2,1,0:T(8,128)}, f32[4,640,128]{2,1,0:T(8,128)S(1)}, u32[]{:S(2)}) copy-start(f32[4,640,128]{2,1,0:T(8,128)S(1)} %convert_add_fusion.prior_ref) | copy-start | bytes 3932164
  145.0 26.8 %copy-start.7 = (bf16[3,112,896]{2,1,0:T(8,128)(2,1)}, bf16[3,112,896]{2,1,0:T(8,128)(2,1)S(1)}, u32[]{:S(2)}) copy-start(bf16[3,112,896]{2,1,0:T(8,128)(2,1)S(1)} %maximum_select_fusion.7) | copy-start | bytes 1806340
  151.4 4.8 %copy-start.23 = (f32[1792]{0:T(1024)S(1)}, f32[1792]{0:T(1024)}, u32[]{:S(2)}) copy-start(f32[1792]{0:T(1024)} %param.25) | copy-start | bytes 21508
  153.2 6.2 %copy-start.5 = (bf16[4,3,112,896]{3,2,1,0:T(8,128)(2,1)}, bf16[4,3,112,896]{3,2,1,0:T(8,128)(2,1)S(1)}, u32[]{:S(2)}) copy-start(bf16[4,3,112,896]{3,2,1,0:T(8,128)(2,1)S(1)} %maximum_select_fusion.1.near_ref) | copy-start | bytes 7225348
  153.2 4.7 %collective-permute-start.22 = (bf16[4,3,112,896]{3,2,1,0:T(8,128)(2,1)S(1)}, bf16[4,3,112,896]{3,2,1,0:T(8,128)(2,1)S(1)}, u32[]{:S(2)}, u32[]{:S(2)}) collective-permute-start(bf16[4,3,112,896]{3,2,1,0:T(8,128)(2,1)S(1)} %maximum_select_fusion.1.near_ref), channel_id=1, source_target_pairs={{0,16},{16,0},{1,17},{17,1},{2,18},{18,2},{3,19},{19,3},{4,20},{20... | collective-permute-start | bytes 7225352 | tf_op jit(solution)/shard_map/ppermute | solution.py:425
  154.4 20.0 %collective-permute-start.29 = (bf16[1,336,896]{2,1,0:T(8,128)(2,1)}, bf16[1,336,896]{2,1,0:T(8,128)(2,1)}, u32[]{:S(2)}, u32[]{:S(2)}) collective-permute-start(bf16[1,336,896]{2,1,0:T(8,128)(2,1)} %slice_select_fusion), channel_id=1, source_target_pairs={{0,8},{4,12},{8,0},{12,4},{1,9},{5,13},{9,1},{13,5},{2,10},{6,14},... | collective-permute-start | bytes 1806344 | tf_op jit(solution)/shard_map/ppermute | solution.py:425
  154.4 24.7 %collective-permute-start.28 = (bf16[1,336,896]{2,1,0:T(8,128)(2,1)}, bf16[1,336,896]{2,1,0:T(8,128)(2,1)}, u32[]{:S(2)}, u32[]{:S(2)}) collective-permute-start(bf16[1,336,896]{2,1,0:T(8,128)(2,1)} %slice_select_fusion), channel_id=1, source_target_pairs={{0,4},{4,0},{8,12},{12,8},{1,5},{5,1},{9,13},{13,9},{2,6},{6,2},{1... | collective-permute-start | bytes 1806344 | tf_op jit(solution)/shard_map/ppermute | solution.py:425
  157.9 1.5 copy-start.11
  171.7 34.2 %collective-permute-start.24 = (bf16[256,1792]{1,0:T(8,128)(2,1)}, bf16[256,1792]{1,0:T(8,128)(2,1)S(1)}, u32[]{:S(2)}, u32[]{:S(2)}) collective-permute-start(bf16[256,1792]{1,0:T(8,128)(2,1)} %get-tuple-element.14._.x_ref), channel_id=1, source_target_pairs={{0,1},{1,0},{2,3},{3,2},{4,5},{5,4},{6,7},{7,6},{8,9},{9,8},{10,11... | collective-permute-start | bytes 2752520 | tf_op jit(solution)/shard_map/ppermute | solution.py:425
  172.7 30.8 %collective-permute-start.26 = (bf16[3,112,896]{2,1,0:T(8,128)(2,1)}, bf16[3,112,896]{2,1,0:T(8,128)(2,1)S(1)}, u32[]{:S(2)}, u32[]{:S(2)}) collective-permute-start(bf16[3,112,896]{2,1,0:T(8,128)(2,1)} %broadcast_select_fusion.1), channel_id=1, source_target_pairs={{0,4},{4,0},{8,12},{12,8},{1,5},{5,1},{9,13},{13,9},{2,6},{6,2},{1... | collective-permute-start | bytes 1806344 | tf_op jit(solution)/shard_map/ppermute | solution.py:425
  173.2 31.4 %collective-permute-start.27 = (bf16[3,112,896]{2,1,0:T(8,128)(2,1)}, bf16[3,112,896]{2,1,0:T(8,128)(2,1)S(1)}, u32[]{:S(2)}, u32[]{:S(2)}) collective-permute-start(bf16[3,112,896]{2,1,0:T(8,128)(2,1)} %broadcast_select_fusion.1), channel_id=1, source_target_pairs={{0,8},{4,12},{8,0},{12,4},{1,9},{5,13},{9,1},{13,5},{2,10},{6,14},... | collective-permute-start | bytes 1806344 | tf_op jit(solution)/shard_map/ppermute | solution.py:425
  174.4 24.0 %collective-permute-start.25 = (bf16[80,1792]{1,0:T(8,128)(2,1)}, bf16[80,1792]{1,0:T(8,128)(2,1)S(1)}, u32[]{:S(2)}, u32[]{:S(2)}) collective-permute-start(bf16[80,1792]{1,0:T(8,128)(2,1)} %get-tuple-element.15), channel_id=1, source_target_pairs={{0,5},{1,4},{2,7},{3,6},{4,9},{5,8},{6,11},{7,10},{8,13},{9,12},{1... | collective-permute-start | bytes 860168 | tf_op jit(solution)/shard_map/ppermute | solution.py:654
  179.1 29.6 %collective-permute-start.30 = (bf16[1,176,896]{2,1,0:T(8,128)(2,1)S(1)}, bf16[1,176,896]{2,1,0:T(8,128)(2,1)S(1)}, u32[]{:S(2)}, u32[]{:S(2)}) collective-permute-start(bf16[1,176,896]{2,1,0:T(8,128)(2,1)S(1)} %slice_select_fusion.4), channel_id=1, source_target_pairs={{0,4},{4,0},{8,12},{12,8},{1,5},{5,1},{9,13},{13,9},{2,6},{6,2},{1... | collective-permute-start | bytes 946184 | tf_op jit(solution)/shard_map/ppermute | solution.py:425
  198.4 10.2 %copy-start.19 = (bf16[80,1792]{1,0:T(8,128)(2,1)}, bf16[80,1792]{1,0:T(8,128)(2,1)S(1)}, u32[]{:S(2)}) copy-start(bf16[80,1792]{1,0:T(8,128)(2,1)S(1)} %collective-permute-done.25.halo_ref) | copy-start | bytes 860164
  198.5 10.2 %collective-permute-start.31 = (bf16[1,160,896]{2,1,0:T(8,128)(2,1)S(1)}, bf16[1,160,896]{2,1,0:T(8,128)(2,1)S(1)}, u32[]{:S(2)}, u32[]{:S(2)}) collective-permute-start(bf16[1,160,896]{2,1,0:T(8,128)(2,1)S(1)} %slice_select_fusion.5), channel_id=1, source_target_pairs={{0,8},{4,12},{8,0},{12,4},{1,9},{5,13},{9,1},{13,5},{2,10},{6,14},... | collective-permute-start | bytes 860168 | tf_op jit(solution)/shard_map/ppermute | solution.py:425
  203.5 3.9 %copy-start.15 = (bf16[3,112,896]{2,1,0:T(8,128)(2,1)}, bf16[3,112,896]{2,1,0:T(8,128)(2,1)S(1)}, u32[]{:S(2)}) copy-start(bf16[3,112,896]{2,1,0:T(8,128)(2,1)S(1)} %collective-permute-done.26) | copy-start | bytes 1806340
  204.7 4.0 %copy-start.16 = (bf16[3,112,896]{2,1,0:T(8,128)(2,1)}, bf16[3,112,896]{2,1,0:T(8,128)(2,1)S(1)}, u32[]{:S(2)}) copy-start(bf16[3,112,896]{2,1,0:T(8,128)(2,1)S(1)} %collective-permute-done.27) | copy-start | bytes 1806340
  205.9 0.9 copy-start.13
  208.8 3.5 %copy-start.8 = (bf16[3,112,896]{2,1,0:T(8,128)(2,1)S(1)}, bf16[3,112,896]{2,1,0:T(8,128)(2,1)}, u32[]{:S(2)}) copy-start(bf16[3,112,896]{2,1,0:T(8,128)(2,1)} %copy-done.7) | copy-start | bytes 1806340
  210.8 4.8 %copy-start.2 = (bf16[4,1,336,896]{3,2,1,0:T(8,128)(2,1)}, bf16[4,1,336,896]{3,2,1,0:T(8,128)(2,1)S(1)}, u32[]{:S(2)}) copy-start(bf16[4,1,336,896]{3,2,1,0:T(8,128)(2,1)S(1)} %maximum_select_fusion.2.near_ref) | copy-start | bytes 7225348
  210.8 4.8 %collective-permute-start.32 = (bf16[4,1,336,896]{3,2,1,0:T(8,128)(2,1)S(1)}, bf16[4,1,336,896]{3,2,1,0:T(8,128)(2,1)}, u32[]{:S(2)}, u32[]{:S(2)}) collective-permute-start(bf16[4,1,336,896]{3,2,1,0:T(8,128)(2,1)S(1)} %maximum_select_fusion.2.near_ref), channel_id=1, source_target_pairs={{0,16},{16,0},{1,17},{17,1},{2,18},{18,2},{3,19},{19,3},{4,20},{20... | collective-permute-start | bytes 7225352 | tf_op jit(solution)/shard_map/ppermute | solution.py:425
  210.8 20.7 %collective-permute-start.34 = (bf16[3,112,896]{2,1,0:T(8,128)(2,1)}, bf16[3,112,896]{2,1,0:T(8,128)(2,1)}, u32[]{:S(2)}, u32[]{:S(2)}) collective-permute-start(bf16[3,112,896]{2,1,0:T(8,128)(2,1)} %broadcast_select_fusion.1), channel_id=1, source_target_pairs={{0,12},{4,8},{8,4},{12,0},{1,13},{5,9},{9,5},{13,1},{2,14},{6,10},... | collective-permute-start | bytes 1806344 | tf_op jit(solution)/shard_map/ppermute | solution.py:425
  215.6 16.0 %copy-start.12 = (bf16[1,3,112,896]{3,2,1,0:T(8,128)(2,1)S(1)}, bf16[1,3,112,896]{3,2,1,0:T(8,128)(2,1)}, u32[]{:S(2)}) copy-start(bf16[1,3,112,896]{3,2,1,0:T(8,128)(2,1)} %fusion.14) | copy-start | bytes 1806340
  231.5 6.2 %copy-start.24 = (s32[8]{0:T(128)S(1)}, s32[8]{0:T(128)}, u32[]{:S(2)}) copy-start(s32[8]{0:T(128)} %param.20) | copy-start | bytes 100
  231.6 6.2 %copy-start.25 = (s32[8]{0:T(128)S(1)}, s32[8]{0:T(128)}, u32[]{:S(2)}) copy-start(s32[8]{0:T(128)} %param.19) | copy-start | bytes 100
  233.4 25.5 %copy-start.4 = (bf16[4,3,112,896]{3,2,1,0:T(8,128)(2,1)}, bf16[4,3,112,896]{3,2,1,0:T(8,128)(2,1)S(1)}, u32[]{:S(2)}) copy-start(bf16[4,3,112,896]{3,2,1,0:T(8,128)(2,1)S(1)} %maximum_select_fusion.3.near_ref) | copy-start | bytes 7225348
  233.5 25.6 %collective-permute-start.35 = (bf16[4,3,112,896]{3,2,1,0:T(8,128)(2,1)S(1)}, bf16[4,3,112,896]{3,2,1,0:T(8,128)(2,1)}, u32[]{:S(2)}, u32[]{:S(2)}) collective-permute-start(bf16[4,3,112,896]{3,2,1,0:T(8,128)(2,1)S(1)} %maximum_select_fusion.3.near_ref), channel_id=1, source_target_pairs={{0,16},{16,0},{1,17},{17,1},{2,18},{18,2},{3,19},{19,3},{4,20},{20... | collective-permute-start | bytes 7225352 | tf_op jit(solution)/shard_map/ppermute | solution.py:425
  233.6 25.4 %collective-permute-start.33 = (bf16[2,256,512]{2,1,0:T(8,128)(2,1)}, bf16[2,256,512]{2,1,0:T(8,128)(2,1)S(1)}, u32[]{:S(2)}, u32[]{:S(2)}) collective-permute-start(bf16[2,256,512]{2,1,0:T(8,128)(2,1)} %window_rows.2._), channel_id=1, source_target_pairs={{0,1},{1,0},{2,3},{3,2},{4,5},{5,4},{6,7},{7,6},{8,9},{9,8},{10,11... | collective-permute-start | bytes 1572872 | tf_op jit(solution)/shard_map/ppermute | solution.py:425
  234.0 10.2 %collective-permute-start.23 = (bf16[80,1792]{1,0:T(8,128)(2,1)}, bf16[80,1792]{1,0:T(8,128)(2,1)S(1)}, u32[]{:S(2)}, u32[]{:S(2)}) collective-permute-start(bf16[80,1792]{1,0:T(8,128)(2,1)} %get-tuple-element.15), channel_id=1, source_target_pairs={{0,4},{4,8},{8,12},{1,5},{5,9},{9,13},{2,6},{6,10},{10,14},{3,7},{... | collective-permute-start | bytes 860168 | tf_op jit(solution)/shard_map/ppermute | solution.py:652
  244.2 0.7 copy-start.20
  259.0 0.8 copy-start.17
  266.5 28.5 %copy-start.1 = (bf16[64,4,1792]{2,1,0:T(4,128)(2,1)S(1)}, bf16[64,4,1792]{2,1,0:T(4,128)(2,1)}, u32[]{:S(2)}) copy-start(bf16[64,4,1792]{2,1,0:T(4,128)(2,1)} %param.17) | copy-start | bytes 2752516

commit v14 on v12

--- a/solution.py
+++ b/solution.py
@@ -462,6 +462,8 @@
             across(after(above[:, :half], diagonal), "seq", 1),
             across(after(beside[:, half:], diagonal), "seq", 2),
         ]
+        if callable(over_cores):
+            over_cores = over_cores(opposite)
         opposite = after(jnp.concatenate(opposite, axis=1), over_cores)
     near = after(jnp.stack([held, beside, above, opposite]), over_cores)
     return near, across(near, "dp", 1)
@@ -654,11 +656,15 @@
             for j in range(group_count)
         ],
     )
-    held_out_two = after(held_out_two, (residual,))
-    near_by_two = neighbours(held_out_two)
-    near_window = from_plane(
-        held_window, near_by_window, (residual,), (pair_rows, pair_halo, *near_by_two)
-    )
+    near_by_two = []
+
+    def before_window(opposite):
+        held = after(held_out_two, opposite)
+        near_by_two.extend([held, *neighbours(held)])
+        return (pair_rows, pair_halo, halo, *near_by_two[1:])
+
+    near_window = from_plane(held_window, near_by_window, (residual,), before_window)
+    held_out_two, *near_by_two = near_by_two
     block_start = (seq_place * rows).astype(jnp.int32)[None]
 
     def window_rows(slot_rows, slot_halo, earlier):

time: 296 us -> 299 us (1.010)
  starting transfers between devices: 57 us -> 51.9 us
  local copies, waits for them, and re-layouts: 31.5 us -> 35.3 us
    ppermute x1, waiting for transfers between devices: 16.6 us -> 7.53 us  [on_device(): lax.ppermute(tail, ('seq', 'tensor'), [(i * group_count + j, (i + 1) * gr...]
    ppermute x31, waiting for transfers between devices: 33.7 us -> 39.6 us  [across(): lax.ppermute(array, axis, [(i, i ^ bit) for i in range(lax.axis_size(axis...]
    ppermute x1, waiting for transfers between devices: 4.57 us -> 9.72 us  [on_device(): halo = lax.ppermute(tail, 'seq', [(i, i + 1) for i in range(seq_count - 1)])]
    slice x15 -> x18, local copies, waits for them, and re-layouts: 10.4 us -> 12.5 us  [after(): lax.slice(other, (0,) * other.ndim, (1,) * other.ndim)]
  transfers between devices with their start and end apart: 38 -> 38, of which waited for: 15 -> 16; matrix products, arithmetic and copies ran while one was open for 14% -> 14% of each run, Pallas kernels for 17% -> 17%
where the time goes in v14:
time: 299 us; the launch traced here: 298 us
  waiting for transfers between devices  86.6 us (29%)
  Pallas kernels  57.8 us (19%)
  starting transfers between devices  51.9 us (17%)
  local copies, waits for them, and re-layouts  35.3 us (12%)
  other arithmetic  28 us (9%)
  blocking collectives  26 us (9%)
  between operations  12.3 us (4%)
    ppermute x31, waiting for transfers between devices, across(): lax.ppermute(array, axis, [(i, i ^ bit) for i in range(lax.axis_size(axis...  39.6 us
    ppermute x31, starting transfers between devices, across(): lax.ppermute(array, axis, [(i, i ^ bit) for i in range(lax.axis_size(axis...  32 us
    pallas_call x2, Pallas kernels, window_rows(): call(functools.partial(window_kernel, heads), 2, [SMEM, SMEM, *[HBM] * 5,...  28.2 us
    all_to_all x1, blocking collectives, on_device(): lax.all_to_all(result, 'tensor', split_axis=0, concat_axis=0, tiled=True)  26 us
    all_to_all x1, waiting for transfers between devices, on_device(): lax.all_to_all(picked, 'tensor', split_axis=0, concat_axis=0, tiled=True)  20.6 us
    select_n x21, other arithmetic, after(): return jnp.where(zero == 0.0, array, jnp.zeros_like(array))  20.1 us
    slice x18, local copies, waits for them, and re-layouts, after(): lax.slice(other, (0,) * other.ndim, (1,) * other.ndim)  12.5 us
    pallas_call x1, Pallas kernels, on_device(): call(functools.partial(linear_kernel, heads, feature_dim, kept), group_co...  12.4 us
  transfers between devices with their start and end apart: 38, of which 16 were waited for; matrix products, arithmetic and copies ran while one was open for 14% of the time, Pallas kernels for 17%

profile of v14, /device:TPU:0, one launch (start us, length us, event | category | flops | bytes accessed | tf_op | source)
XLA Modules:
  0.0 298.0 jit_solution(16963529379905422576)
XLA Ops:
  1.9 4.1 %collective-permute-start.2 = (bf16[144,896]{1,0:T(8,128)(2,1)S(1)}, bf16[144,896]{1,0:T(8,128)(2,1)S(1)}, u32[]{:S(2)}, u32[]{:S(2)}) collective-permute-start(bf16[144,896]{1,0:T(8,128)(2,1)S(1)} %pad_maximum_fusion.1), channel_id=1, source_target_pairs={{0,2},{1,3},{2,0},{3,1},{4,6},{5,7},{6,4},{7,5},{8,10},{9,11},{10,... | collective-permute-start | bytes 774152 | tf_op jit(solution)/shard_map/ppermute | solution.py:425
  6.0 1.6 collective-permute-start.1
  10.0 2.2 gather_fusion.1
  12.2 3.7 %all-to-all-start = ((bf16[8,8,4,1792]{3,2,1,0:T(4,128)(2,1)}), bf16[8,8,4,1792]{3,2,1,0:T(4,128)(2,1)S(1)}, u32[]{:S(2)}, u32[]{:S(2)}) async-start(bf16[8,8,4,1792]{3,2,1,0:T(4,128)(2,1)} %bitcast.20), calls=%async_computation | async-start | bytes 1835008 | tf_op jit(solution)/shard_map/all_to_all | solution.py:550
  18.6 3.1 %collective-permute-done = f32[3,1536]{1,0:T(4,128)S(1)} collective-permute-done((f32[3,1536]{1,0:T(4,128)S(1)}, f32[3,1536]{1,0:T(4,128)S(1)}, u32[]{:S(2)}, u32[]{:S(2)}) %collective-permute-start) | collective-permute-done | bytes 18464 | tf_op jit(solution)/shard_map/ppermute | solution.py:425
  22.9 3.4 %collective-permute-done.3 = bf16[144,896]{1,0:T(8,128)(2,1)S(1)} collective-permute-done((bf16[144,896]{1,0:T(8,128)(2,1)S(1)}, bf16[144,896]{1,0:T(8,128)(2,1)S(1)}, u32[]{:S(2)}, u32[]{:S(2)}) %collective-permute-start.3) | collective-permute-done | bytes 258080 | tf_op jit(solution)/shard_map/ppermute | solution.py:425
  27.6 1.8 all-to-all-done
  29.4 1.3 gather_fusion.2
  32.2 3.5 %all-to-all-start.1 = ((bf16[4,16,4,1792]{3,1,2,0:T(8,128)(2,1)}), bf16[4,16,4,1792]{3,1,2,0:T(8,128)(2,1)S(1)}, u32[]{:S(2)}, u32[]{:S(2)}) async-start(bf16[4,16,4,1792]{3,1,2,0:T(8,128)(2,1)} %copy.47), calls=%async_computation.1 | async-start | bytes 1835008 | tf_op jit(solution)/shard_map/all_to_all | solution.py:557
  35.7 1.1 collective-permute-start.8
  36.8 1.1 collective-permute-start.7
  39.0 1.7 select_bitcast_fusion.1
  40.7 2.9 collective-permute-start.5
  43.6 20.6 %all-to-all-done.1 = bf16[4,16,4,1792]{3,1,2,0:T(8,128)(2,1)S(1)} async-done(((bf16[4,16,4,1792]{3,1,2,0:T(8,128)(2,1)}), bf16[4,16,4,1792]{3,1,2,0:T(8,128)(2,1)S(1)}, u32[]{:S(2)}, u32[]{:S(2)}) %all-to-all-start.1) | async-done | bytes 917536 | tf_op jit(solution)/shard_map/all_to_all | solution.py:557
  65.6 1.1 collective-permute-start.9
  66.6 1.0 slice_select_fusion.3
  68.3 2.0 collective-permute-start.6
  70.4 4.9 %collective-permute-done.4 = bf16[112,896]{1,0:T(8,128)(2,1)S(1)} collective-permute-done((bf16[112,896]{1,0:T(8,128)(2,1)}, bf16[112,896]{1,0:T(8,128)(2,1)S(1)}, u32[]{:S(2)}, u32[]{:S(2)}) %collective-permute-start.4) | collective-permute-done | bytes 200736 | tf_op jit(solution)/shard_map/ppermute | solution.py:425
  75.2 2.1 collective-permute-done.6
  77.4 1.8 pad_maximum_fusion
  79.2 1.2 slice.128
  81.2 1.7 maximum_select_fusion.near_ref
  83.0 2.1 constant_dynamic-slice_fusion
  86.1 1.1 maximum_select_fusion.4
  88.0 1.4 collective-permute-start.18
  90.1 1.7 collective-permute-start.19
  91.8 1.4 copy.48
  93.2 2.4 reshape.562.x_ref
  95.6 12.4 %linear_rows.1 = (f32[4,256,512]{2,1,0:T(8,128)}, bf16[4,256,128]{2,1,0:T(8,128)(2,1)}, bf16[4,640,128]{2,1,0:T(8,128)(2,1)}) custom-call(s32[5]{0:T(128)} %pad_add_fusion.place_ref, bf16[256,1792]{1,0:T(8,128)(2,1)} %reshape.562.x_ref, f32[1,1792]{1,0:T(1,128)} %broadcast_in_dim.128.gain_ref, bf16[1,4,112,1792]{3,2,1,0:T(8,128)(2,1)} %bitcast.102, ...), custom_call_target="tpu_custom_call" | custom-call | tf_op jit(solution)/shard_map/linear_rows/pallas_call | solution.py:578
  108.0 2.3 collective-permute-start.14
  110.3 1.3 collective-permute-start.13
  111.7 1.2 slice.100
  113.5 11.2 %collective-permute-done.15 = bf16[448,896]{1,0:T(8,128)(2,1)} collective-permute-done((bf16[448,896]{1,0:T(8,128)(2,1)}, bf16[448,896]{1,0:T(8,128)(2,1)}, u32[]{:S(2)}, u32[]{:S(2)}) %collective-permute-start.15) | collective-permute-done | bytes 802848 | tf_op jit(solution)/shard_map/ppermute | solution.py:425
  124.6 3.5 %collective-permute-start.12 = (bf16[4,640,128]{2,1,0:T(8,128)(2,1)}, bf16[4,640,128]{2,1,0:T(8,128)(2,1)S(1)}, u32[]{:S(2)}, u32[]{:S(2)}) collective-permute-start(bf16[4,640,128]{2,1,0:T(8,128)(2,1)} %get-tuple-element.13), channel_id=1, source_target_pairs={{0,4},{4,8},{8,12},{1,5},{5,9},{9,13},{2,6},{6,10},{10,14},{3,7},{... | collective-permute-start | bytes 1966088 | tf_op jit(solution)/shard_map/ppermute | solution.py:476
  128.2 1.2 select_bitcast_fusion
  131.1 1.7 collective-permute-start.21
  132.8 1.0 slice_select_fusion.2
  133.9 2.0 collective-permute-start.17
  136.0 7.4 %collective-permute-done.12 = bf16[4,640,128]{2,1,0:T(8,128)(2,1)S(1)} collective-permute-done((bf16[4,640,128]{2,1,0:T(8,128)(2,1)}, bf16[4,640,128]{2,1,0:T(8,128)(2,1)S(1)}, u32[]{:S(2)}, u32[]{:S(2)}) %collective-permute-start.12) | collective-permute-done | bytes 655392 | tf_op jit(solution)/shard_map/ppermute | solution.py:476
  146.7 2.3 collective-permute-done.21
  149.0 2.9 collective-permute-done.20
  152.0 1.9 maximum_select_fusion.1.near_ref
  154.0 1.0 slice_select_fusion
  155.0 2.0 collective-permute-start.28
  158.6 1.5 copy-done.11
  160.1 10.4 %linear_out.1 = (bf16[256,1792]{1,0:T(8,128)(2,1)}, bf16[256,1792]{1,0:T(8,128)(2,1)}, bf16[80,1792]{1,0:T(8,128)(2,1)}) custom-call(s32[5]{0:T(128)} %pad_add_fusion.place_ref, f32[4,256,512]{2,1,0:T(8,128)} %get-tuple-element.11.num_ref, bf16[4,256,128]{2,1,0:T(8,128)(2,1)} %get-tuple-element.12.q_ref, bf16[128,1024]{1,0:T(8,128)(2,1)} %constant.134.clone.first_ref, ...), custom_call_target="tpu_custom_call" | custom-call | tf_op jit(solution)/shard_map/linear_out/pallas_call | solution.py:618
  170.5 1.2 slice.110
  174.7 1.7 collective-permute-start.29
  176.4 6.9 %collective-permute-done.29 = bf16[1,160,896]{2,1,0:T(8,128)(2,1)S(1)} collective-permute-done((bf16[1,160,896]{2,1,0:T(8,128)(2,1)S(1)}, bf16[1,160,896]{2,1,0:T(8,128)(2,1)S(1)}, u32[]{:S(2)}, u32[]{:S(2)}) %collective-permute-start.29) | collective-permute-done | bytes 286752 | tf_op jit(solution)/shard_map/ppermute | solution.py:425
  186.5 1.7 collective-permute-start.30
  188.5 1.6 collective-permute-start.25
  190.2 3.8 %collective-permute-start.23 = (bf16[80,1792]{1,0:T(8,128)(2,1)S(1)}, bf16[80,1792]{1,0:T(8,128)(2,1)S(1)}, u32[]{:S(2)}, u32[]{:S(2)}) collective-permute-start(bf16[80,1792]{1,0:T(8,128)(2,1)S(1)} %copy-done.25), channel_id=1, source_target_pairs={{0,4},{4,8},{8,12},{1,5},{5,9},{9,13},{2,6},{6,10},{10,14},{3,7},{... | collective-permute-start | bytes 860168 | tf_op jit(solution)/shard_map/ppermute | solution.py:648
  194.9 7.5 %collective-permute-done.25.halo_ref = bf16[80,1792]{1,0:T(8,128)(2,1)S(1)} collective-permute-done((bf16[80,1792]{1,0:T(8,128)(2,1)S(1)}, bf16[80,1792]{1,0:T(8,128)(2,1)S(1)}, u32[]{:S(2)}, u32[]{:S(2)}) %collective-permute-start.25) | collective-permute-done | bytes 286752 | tf_op jit(solution)/shard_map/ppermute | solution.py:650
  203.0 9.7 %collective-permute-done.23.halo_ref = bf16[80,1792]{1,0:T(8,128)(2,1)S(1)} collective-permute-done((bf16[80,1792]{1,0:T(8,128)(2,1)S(1)}, bf16[80,1792]{1,0:T(8,128)(2,1)S(1)}, u32[]{:S(2)}, u32[]{:S(2)}) %collective-permute-start.23) | collective-permute-done | bytes 286752 | tf_op jit(solution)/shard_map/ppermute | solution.py:648
  220.8 1.9 maximum_select_fusion.2.near_ref
  222.8 2.6 collective-permute-start.34
  226.3 1.2 collective-permute-done.32.far_ref
  227.5 14.2 %window_rows.2._ = bf16[2,256,512]{2,1,0:T(8,128)(2,1)} custom-call(s32[5]{0:T(128)} %pad_add_fusion.place_ref, s32[1]{0:T(128)} %bitcast.2.first_ref, bf16[256,1792]{1,0:T(8,128)(2,1)} %copy-done.15, bf16[80,1792]{1,0:T(8,128)(2,1)} %copy-done.21, bf16[3,4,112,1792]{3,2,1,0:T(8,128)(2,1)} %bitcast.92, bf16[4,1,336,896]{3,2,1,0:T(8,128)(2,1)} %copy-done.2, ...), custom_call_target="tpu_custom_call" | custom-call | tf_op jit(solution)/shard_map/window_rows/pallas_call | solution.py:671
  241.7 1.2 slice.148
  243.5 1.9 maximum_select_fusion.3.near_ref
  247.2 14.1 %window_rows.3.mixed_ref = bf16[2,256,512]{2,1,0:T(8,128)(2,1)} custom-call(s32[5]{0:T(128)} %pad_add_fusion.place_ref, s32[1]{0:T(128)} %bitcast.2.first_ref, bf16[256,1792]{1,0:T(8,128)(2,1)} %get-tuple-element.14._.x_ref, bf16[80,1792]{1,0:T(8,128)(2,1)} %copy-done.20, bf16[3,4,112,1792]{3,2,1,0:T(8,128)(2,1)} %bitcast.93, ...), custom_call_target="tpu_custom_call" | custom-call | tf_op jit(solution)/shard_map/window_rows/pallas_call | solution.py:671
  262.2 6.7 %window_out.1 = bf16[256,1792]{1,0:T(8,128)(2,1)} custom-call(s32[5]{0:T(128)} %pad_add_fusion.place_ref, s32[1]{0:T(128)} %bitcast.1.live_ref, bf16[2,256,512]{2,1,0:T(8,128)(2,1)} %window_rows.3.mixed_ref, bf16[2,256,512]{2,1,0:T(8,128)(2,1)} %copy-done.18, bf16[1,4,112,1792]{3,2,1,0:T(8,128)(2,1)} %bitcast.106, bf16[4,3,112,896]{3,2,1,0:T(8,128)(2,1)} %copy-done.4, ...), custom_call_target="tpu_custom_call" | custom-call | tf_op jit(solution)/shard_map/window_out/pallas_call | solution.py:696
  268.9 1.9 reshape.568
  271.1 26.0 %all_to_all.15 = bf16[4,16,4,1792]{3,2,1,0:T(4,128)(2,1)S(1)} all-to-all(bf16[4,16,4,1792]{3,2,1,0:T(4,128)(2,1)S(1)} %bitcast.97), channel_id=1, replica_groups=mesh['dp'=2,'seq'=4,'tensor'=4] {'tensor'}, dimensions={0} | all-to-all | bytes 1835008 | tf_op jit(solution)/shard_map/all_to_all | solution.py:717
  (167 shorter events, 34.5 us)
Async XLA Ops:
  0.0 9.9 %copy-start = (bf16[64,4,1792]{2,1,0:T(4,128)(2,1)S(1)}, bf16[64,4,1792]{2,1,0:T(4,128)(2,1)}, u32[]{:S(2)}) copy-start(bf16[64,4,1792]{2,1,0:T(4,128)(2,1)} %param.17) | copy-start | bytes 2752516
  0.9 15.0 %copy-start.22 = (f32[3,3,448]{2,1,0:T(4,128)S(1)}, f32[3,3,448]{2,1,0:T(4,128)}, u32[]{:S(2)}) copy-start(f32[3,3,448]{2,1,0:T(4,128)} %param.27) | copy-start | bytes 48388
  1.9 16.0 %collective-permute-start.2 = (bf16[144,896]{1,0:T(8,128)(2,1)S(1)}, bf16[144,896]{1,0:T(8,128)(2,1)S(1)}, u32[]{:S(2)}, u32[]{:S(2)}) collective-permute-start(bf16[144,896]{1,0:T(8,128)(2,1)S(1)} %pad_maximum_fusion.1), channel_id=1, source_target_pairs={{0,2},{1,3},{2,0},{3,1},{4,6},{5,7},{6,4},{7,5},{8,10},{9,11},{10,... | collective-permute-start | bytes 774152 | tf_op jit(solution)/shard_map/ppermute | solution.py:425
  6.0 16.9 %collective-permute-start.1 = (bf16[144,896]{1,0:T(8,128)(2,1)S(1)}, bf16[144,896]{1,0:T(8,128)(2,1)S(1)}, u32[]{:S(2)}, u32[]{:S(2)}) collective-permute-start(bf16[144,896]{1,0:T(8,128)(2,1)S(1)} %pad_maximum_fusion.1), channel_id=1, source_target_pairs={{0,1},{1,0},{2,3},{3,2},{4,5},{5,4},{6,7},{7,6},{8,9},{9,8},{10,11... | collective-permute-start | bytes 774152 | tf_op jit(solution)/shard_map/ppermute | solution.py:425
  12.2 17.2 %all-to-all-start = ((bf16[8,8,4,1792]{3,2,1,0:T(4,128)(2,1)}), bf16[8,8,4,1792]{3,2,1,0:T(4,128)(2,1)S(1)}, u32[]{:S(2)}, u32[]{:S(2)}) async-start(bf16[8,8,4,1792]{3,2,1,0:T(4,128)(2,1)} %bitcast.20), calls=%async_computation | async-start | bytes 1835008 | tf_op jit(solution)/shard_map/all_to_all | solution.py:550
  16.7 5.0 %collective-permute-start = (f32[3,1536]{1,0:T(4,128)S(1)}, f32[3,1536]{1,0:T(4,128)S(1)}, u32[]{:S(2)}, u32[]{:S(2)}) collective-permute-start(f32[3,1536]{1,0:T(4,128)S(1)} %reshape.552), channel_id=1, source_target_pairs={{0,2},{1,3},{2,0},{3,1},{4,6},{5,7},{6,4},{7,5},{8,10},{9,11},{10,... | collective-permute-start | bytes 55304 | tf_op jit(solution)/shard_map/ppermute | solution.py:425
  17.9 8.4 %collective-permute-start.3 = (bf16[144,896]{1,0:T(8,128)(2,1)S(1)}, bf16[144,896]{1,0:T(8,128)(2,1)S(1)}, u32[]{:S(2)}, u32[]{:S(2)}) collective-permute-start(bf16[144,896]{1,0:T(8,128)(2,1)S(1)} %collective-permute-done.2), channel_id=1, source_target_pairs={{0,1},{1,0},{2,3},{3,2},{4,5},{5,4},{6,7},{7,6},{8,9},{9,8},{10,11... | collective-permute-start | bytes 774152 | tf_op jit(solution)/shard_map/ppermute | solution.py:425
  21.7 9.4 %copy-start.19 = (f32[2,3,1536]{2,1,0:T(4,128)}, f32[2,3,1536]{2,1,0:T(4,128)S(1)}, u32[]{:S(2)}) copy-start(f32[2,3,1536]{2,1,0:T(4,128)S(1)} %pad_maximum_fusion.2.tap_ref) | copy-start | bytes 110596
  26.4 10.4 %copy-start.9 = (bf16[3,144,896]{2,1,0:T(8,128)(2,1)}, bf16[3,144,896]{2,1,0:T(8,128)(2,1)S(1)}, u32[]{:S(2)}) copy-start(bf16[3,144,896]{2,1,0:T(8,128)(2,1)S(1)} %maximum_select_fusion.5) | copy-start | bytes 2322436
  32.2 32.1 %all-to-all-start.1 = ((bf16[4,16,4,1792]{3,1,2,0:T(8,128)(2,1)}), bf16[4,16,4,1792]{3,1,2,0:T(8,128)(2,1)S(1)}, u32[]{:S(2)}, u32[]{:S(2)}) async-start(bf16[4,16,4,1792]{3,1,2,0:T(8,128)(2,1)} %copy.47), calls=%async_computation.1 | async-start | bytes 1835008 | tf_op jit(solution)/shard_map/all_to_all | solution.py:557
  35.7 29.8 %collective-permute-start.8 = (bf16[3,144,896]{2,1,0:T(8,128)(2,1)S(1)}, bf16[3,144,896]{2,1,0:T(8,128)(2,1)S(1)}, u32[]{:S(2)}, u32[]{:S(2)}) collective-permute-start(bf16[3,144,896]{2,1,0:T(8,128)(2,1)S(1)} %maximum_select_fusion.5), channel_id=1, source_target_pairs={{0,8},{4,12},{8,0},{12,4},{1,9},{5,13},{9,1},{13,5},{2,10},{6,14},... | collective-permute-start | bytes 2322440 | tf_op jit(solution)/shard_map/ppermute | solution.py:425
  36.8 29.8 %collective-permute-start.7 = (bf16[3,144,896]{2,1,0:T(8,128)(2,1)S(1)}, bf16[3,144,896]{2,1,0:T(8,128)(2,1)}, u32[]{:S(2)}, u32[]{:S(2)}) collective-permute-start(bf16[3,144,896]{2,1,0:T(8,128)(2,1)S(1)} %maximum_select_fusion.5), channel_id=1, source_target_pairs={{0,4},{4,0},{8,12},{12,8},{1,5},{5,1},{9,13},{13,9},{2,6},{6,2},{1... | collective-permute-start | bytes 2322440 | tf_op jit(solution)/shard_map/ppermute | solution.py:425
  40.7 27.6 %collective-permute-start.5 = (bf16[112,896]{1,0:T(8,128)(2,1)}, bf16[112,896]{1,0:T(8,128)(2,1)}, u32[]{:S(2)}, u32[]{:S(2)}) collective-permute-start(bf16[112,896]{1,0:T(8,128)(2,1)} %select_bitcast_fusion.1), channel_id=1, source_target_pairs={{0,2},{1,3},{2,0},{3,1},{4,6},{5,7},{6,4},{7,5},{8,10},{9,11},{10,... | collective-permute-start | bytes 602120 | tf_op jit(solution)/shard_map/ppermute | solution.py:425
  64.2 16.9 %copy-start.7 = (bf16[4,16,4,1792]{3,1,2,0:T(8,128)(2,1)}, bf16[4,16,4,1792]{3,1,2,0:T(8,128)(2,1)S(1)}, u32[]{:S(2)}) copy-start(bf16[4,16,4,1792]{3,1,2,0:T(8,128)(2,1)S(1)} %all-to-all-done.1) | copy-start | bytes 2752516
  64.3 16.9 %copy-start.10 = (bf16[3,144,896]{2,1,0:T(8,128)(2,1)S(1)}, bf16[3,144,896]{2,1,0:T(8,128)(2,1)}, u32[]{:S(2)}) copy-start(bf16[3,144,896]{2,1,0:T(8,128)(2,1)} %copy-done.9) | copy-start | bytes 2322436
  65.5 15.7 %copy-start.14 = (bf16[3,144,896]{2,1,0:T(8,128)(2,1)}, bf16[3,144,896]{2,1,0:T(8,128)(2,1)S(1)}, u32[]{:S(2)}) copy-start(bf16[3,144,896]{2,1,0:T(8,128)(2,1)S(1)} %collective-permute-done.8) | copy-start | bytes 2322436
  65.6 15.4 %collective-permute-start.9 = (bf16[3,80,896]{2,1,0:T(8,128)(2,1)S(1)}, bf16[3,80,896]{2,1,0:T(8,128)(2,1)S(1)}, u32[]{:S(2)}, u32[]{:S(2)}) collective-permute-start(bf16[3,80,896]{2,1,0:T(8,128)(2,1)S(1)} %slice_select_fusion.1), channel_id=1, source_target_pairs={{0,4},{4,0},{8,12},{12,8},{1,5},{5,1},{9,13},{13,9},{2,6},{6,2},{1... | collective-permute-start | bytes 1290248 | tf_op jit(solution)/shard_map/ppermute | solution.py:425
  67.7 13.3 %collective-permute-start.10 = (bf16[3,64,896]{2,1,0:T(8,128)(2,1)S(1)}, bf16[3,64,896]{2,1,0:T(8,128)(2,1)S(1)}, u32[]{:S(2)}, u32[]{:S(2)}) collective-permute-start(bf16[3,64,896]{2,1,0:T(8,128)(2,1)S(1)} %slice_select_fusion.3), channel_id=1, source_target_pairs={{0,8},{4,12},{8,0},{12,4},{1,9},{5,13},{9,1},{13,5},{2,10},{6,14},... | collective-permute-start | bytes 1032200 | tf_op jit(solution)/shard_map/ppermute | solution.py:425
  68.3 6.9 %collective-permute-start.4 = (bf16[112,896]{1,0:T(8,128)(2,1)}, bf16[112,896]{1,0:T(8,128)(2,1)S(1)}, u32[]{:S(2)}, u32[]{:S(2)}) collective-permute-start(bf16[112,896]{1,0:T(8,128)(2,1)} %select_bitcast_fusion.1), channel_id=1, source_target_pairs={{0,1},{1,0},{2,3},{3,2},{4,5},{5,4},{6,7},{7,6},{8,9},{9,8},{10,11... | collective-permute-start | bytes 602120 | tf_op jit(solution)/shard_map/ppermute | solution.py:425
  68.3 9.1 %collective-permute-start.6 = (bf16[112,896]{1,0:T(8,128)(2,1)}, bf16[112,896]{1,0:T(8,128)(2,1)S(1)}, u32[]{:S(2)}, u32[]{:S(2)}) collective-permute-start(bf16[112,896]{1,0:T(8,128)(2,1)} %collective-permute-done.5), channel_id=1, source_target_pairs={{0,1},{1,0},{2,3},{3,2},{4,5},{5,4},{6,7},{7,6},{8,9},{9,8},{10,11... | collective-permute-start | bytes 602120 | tf_op jit(solution)/shard_map/ppermute | solution.py:425
  82.9 10.3 %copy-start.3 = (bf16[4,3,144,896]{3,2,1,0:T(8,128)(2,1)}, bf16[4,3,144,896]{3,2,1,0:T(8,128)(2,1)S(1)}, u32[]{:S(2)}) copy-start(bf16[4,3,144,896]{3,2,1,0:T(8,128)(2,1)S(1)} %maximum_select_fusion.near_ref) | copy-start | bytes 9289732
  82.9 4.5 %copy-start.23 = (f32[1792]{0:T(1024)S(1)}, f32[1792]{0:T(1024)}, u32[]{:S(2)}) copy-start(f32[1792]{0:T(1024)} %param.21) | copy-start | bytes 21508
  82.9 8.8 %copy-start.8 = (bf16[4,16,4,1792]{3,1,2,0:T(8,128)(2,1)S(1)}, bf16[4,16,4,1792]{3,1,2,0:T(8,128)(2,1)}, u32[]{:S(2)}) copy-start(bf16[4,16,4,1792]{3,1,2,0:T(8,128)(2,1)} %copy-done.7) | copy-start | bytes 2752516
  83.0 12.6 %collective-permute-start.11 = (bf16[4,3,144,896]{3,2,1,0:T(8,128)(2,1)S(1)}, bf16[4,3,144,896]{3,2,1,0:T(8,128)(2,1)}, u32[]{:S(2)}, u32[]{:S(2)}) collective-permute-start(bf16[4,3,144,896]{3,2,1,0:T(8,128)(2,1)S(1)} %maximum_select_fusion.near_ref), channel_id=1, source_target_pairs={{0,16},{16,0},{1,17},{17,1},{2,18},{18,2},{3,19},{19,3},{4,20},{20... | collective-permute-start | bytes 9289736 | tf_op jit(solution)/shard_map/ppermute | solution.py:425
  87.1 37.5 %collective-permute-start.15 = (bf16[448,896]{1,0:T(8,128)(2,1)}, bf16[448,896]{1,0:T(8,128)(2,1)}, u32[]{:S(2)}, u32[]{:S(2)}) collective-permute-start(bf16[448,896]{1,0:T(8,128)(2,1)} %maximum_select_fusion.4), channel_id=1, source_target_pairs={{0,2},{1,3},{2,0},{3,1},{4,6},{5,7},{6,4},{7,5},{8,10},{9,11},{10,... | collective-permute-start | bytes 2408456 | tf_op jit(solution)/shard_map/ppermute | solution.py:425
  88.0 42.0 %collective-permute-start.18 = (bf16[3,112,896]{2,1,0:T(8,128)(2,1)}, bf16[3,112,896]{2,1,0:T(8,128)(2,1)}, u32[]{:S(2)}, u32[]{:S(2)}) collective-permute-start(bf16[3,112,896]{2,1,0:T(8,128)(2,1)} %pad_maximum_fusion), channel_id=1, source_target_pairs={{0,4},{4,0},{8,12},{12,8},{1,5},{5,1},{9,13},{13,9},{2,6},{6,2},{1... | collective-permute-start | bytes 1806344 | tf_op jit(solution)/shard_map/ppermute | solution.py:425
  90.1 41.0 %collective-permute-start.19 = (bf16[3,112,896]{2,1,0:T(8,128)(2,1)}, bf16[3,112,896]{2,1,0:T(8,128)(2,1)}, u32[]{:S(2)}, u32[]{:S(2)}) collective-permute-start(bf16[3,112,896]{2,1,0:T(8,128)(2,1)} %pad_maximum_fusion), channel_id=1, source_target_pairs={{0,8},{4,12},{8,0},{12,4},{1,9},{5,13},{9,1},{13,5},{2,10},{6,14},... | collective-permute-start | bytes 1806344 | tf_op jit(solution)/shard_map/ppermute | solution.py:425
  108.0 25.8 %collective-permute-start.14 = (bf16[4,640,128]{2,1,0:T(8,128)(2,1)}, bf16[4,640,128]{2,1,0:T(8,128)(2,1)S(1)}, u32[]{:S(2)}, u32[]{:S(2)}) collective-permute-start(bf16[4,640,128]{2,1,0:T(8,128)(2,1)} %get-tuple-element.13), channel_id=1, source_target_pairs={{0,12},{1,13},{2,14},{3,15},{16,28},{17,29},{18,30},{19,31}} | collective-permute-start | bytes 1966088 | tf_op jit(solution)/shard_map/ppermute | solution.py:476
  110.3 23.6 %collective-permute-start.13 = (bf16[4,640,128]{2,1,0:T(8,128)(2,1)}, bf16[4,640,128]{2,1,0:T(8,128)(2,1)S(1)}, u32[]{:S(2)}, u32[]{:S(2)}) collective-permute-start(bf16[4,640,128]{2,1,0:T(8,128)(2,1)} %get-tuple-element.13), channel_id=1, source_target_pairs={{0,8},{4,12},{1,9},{5,13},{2,10},{6,14},{3,11},{7,15},{16,24},{20,... | collective-permute-start | bytes 1966088 | tf_op jit(solution)/shard_map/ppermute | solution.py:476
  124.6 18.7 %collective-permute-start.12 = (bf16[4,640,128]{2,1,0:T(8,128)(2,1)}, bf16[4,640,128]{2,1,0:T(8,128)(2,1)S(1)}, u32[]{:S(2)}, u32[]{:S(2)}) collective-permute-start(bf16[4,640,128]{2,1,0:T(8,128)(2,1)} %get-tuple-element.13), channel_id=1, source_target_pairs={{0,4},{4,8},{8,12},{1,5},{5,9},{9,13},{2,6},{6,10},{10,14},{3,7},{... | collective-permute-start | bytes 1966088 | tf_op jit(solution)/shard_map/ppermute | solution.py:476
  130.0 14.8 %collective-permute-start.16 = (bf16[112,896]{1,0:T(8,128)(2,1)S(1)}, bf16[112,896]{1,0:T(8,128)(2,1)S(1)}, u32[]{:S(2)}, u32[]{:S(2)}) collective-permute-start(bf16[112,896]{1,0:T(8,128)(2,1)S(1)} %get-tuple-element.17), channel_id=1, source_target_pairs={{0,1},{1,0},{2,3},{3,2},{4,5},{5,4},{6,7},{7,6},{8,9},{9,8},{10,11... | collective-permute-start | bytes 602120 | tf_op jit(solution)/shard_map/ppermute | solution.py:425
  131.1 17.9 %collective-permute-start.21 = (bf16[3,48,896]{2,1,0:T(8,128)(2,1)S(1)}, bf16[3,48,896]{2,1,0:T(8,128)(2,1)S(1)}, u32[]{:S(2)}, u32[]{:S(2)}) collective-permute-start(bf16[3,48,896]{2,1,0:T(8,128)(2,1)S(1)} %slice_select_fusion.6), channel_id=1, source_target_pairs={{0,8},{4,12},{8,0},{12,4},{1,9},{5,13},{9,1},{13,5},{2,10},{6,14},... | collective-permute-start | bytes 774152 | tf_op jit(solution)/shard_map/ppermute | solution.py:425
  133.8 18.1 %collective-permute-start.20 = (bf16[3,64,896]{2,1,0:T(8,128)(2,1)S(1)}, bf16[3,64,896]{2,1,0:T(8,128)(2,1)S(1)}, u32[]{:S(2)}, u32[]{:S(2)}) collective-permute-start(bf16[3,64,896]{2,1,0:T(8,128)(2,1)S(1)} %slice_select_fusion.2), channel_id=1, source_target_pairs={{0,4},{4,0},{8,12},{12,8},{1,5},{5,1},{9,13},{13,9},{2,6},{6,2},{1... | collective-permute-start | bytes 1032200 | tf_op jit(solution)/shard_map/ppermute | solution.py:425
  133.9 10.9 %collective-permute-start.17 = (bf16[112,896]{1,0:T(8,128)(2,1)S(1)}, bf16[112,896]{1,0:T(8,128)(2,1)S(1)}, u32[]{:S(2)}, u32[]{:S(2)}) collective-permute-start(bf16[112,896]{1,0:T(8,128)(2,1)S(1)} %get-tuple-element.22), channel_id=1, source_target_pairs={{0,1},{1,0},{2,3},{3,2},{4,5},{5,4},{6,7},{7,6},{8,9},{9,8},{10,11... | collective-permute-start | bytes 602120 | tf_op jit(solution)/shard_map/ppermute | solution.py:425
  143.6 8.4 %copy-start.6 = (f32[4,640,128]{2,1,0:T(8,128)}, f32[4,640,128]{2,1,0:T(8,128)S(1)}, u32[]{:S(2)}) copy-start(f32[4,640,128]{2,1,0:T(8,128)S(1)} %convert_add_fusion.prior_ref) | copy-start | bytes 3932164
  152.0 5.0 %copy-start.24 = (f32[1792]{0:T(1024)S(1)}, f32[1792]{0:T(1024)}, u32[]{:S(2)}) copy-start(f32[1792]{0:T(1024)} %param.25) | copy-start | bytes 21508
  153.9 6.2 %copy-start.5 = (bf16[4,3,112,896]{3,2,1,0:T(8,128)(2,1)}, bf16[4,3,112,896]{3,2,1,0:T(8,128)(2,1)S(1)}, u32[]{:S(2)}) copy-start(bf16[4,3,112,896]{3,2,1,0:T(8,128)(2,1)S(1)} %maximum_select_fusion.1.near_ref) | copy-start | bytes 7225348
  153.9 4.7 %collective-permute-start.22 = (bf16[4,3,112,896]{3,2,1,0:T(8,128)(2,1)S(1)}, bf16[4,3,112,896]{3,2,1,0:T(8,128)(2,1)S(1)}, u32[]{:S(2)}, u32[]{:S(2)}) collective-permute-start(bf16[4,3,112,896]{3,2,1,0:T(8,128)(2,1)S(1)} %maximum_select_fusion.1.near_ref), channel_id=1, source_target_pairs={{0,16},{16,0},{1,17},{17,1},{2,18},{18,2},{3,19},{19,3},{4,20},{20... | collective-permute-start | bytes 7225352 | tf_op jit(solution)/shard_map/ppermute | solution.py:425
  155.0 17.3 %collective-permute-start.26 = (bf16[1,336,896]{2,1,0:T(8,128)(2,1)}, bf16[1,336,896]{2,1,0:T(8,128)(2,1)}, u32[]{:S(2)}, u32[]{:S(2)}) collective-permute-start(bf16[1,336,896]{2,1,0:T(8,128)(2,1)} %slice_select_fusion), channel_id=1, source_target_pairs={{0,8},{4,12},{8,0},{12,4},{1,9},{5,13},{9,1},{13,5},{2,10},{6,14},... | collective-permute-start | bytes 1806344 | tf_op jit(solution)/shard_map/ppermute | solution.py:425
  155.0 18.7 %collective-permute-start.28 = (bf16[1,336,896]{2,1,0:T(8,128)(2,1)}, bf16[1,336,896]{2,1,0:T(8,128)(2,1)}, u32[]{:S(2)}, u32[]{:S(2)}) collective-permute-start(bf16[1,336,896]{2,1,0:T(8,128)(2,1)} %slice_select_fusion), channel_id=1, source_target_pairs={{0,4},{4,0},{8,12},{12,8},{1,5},{5,1},{9,13},{13,9},{2,6},{6,2},{1... | collective-permute-start | bytes 1806344 | tf_op jit(solution)/shard_map/ppermute | solution.py:425
  158.6 1.5 copy-start.11
  170.5 18.0 %copy-start.25 = (bf16[80,1792]{1,0:T(8,128)(2,1)S(1)}, bf16[80,1792]{1,0:T(8,128)(2,1)}, u32[]{:S(2)}) copy-start(bf16[80,1792]{1,0:T(8,128)(2,1)} %get-tuple-element.15) | copy-start | bytes 860164
  173.3 10.5 %collective-permute-start.27 = (bf16[1,176,896]{2,1,0:T(8,128)(2,1)S(1)}, bf16[1,176,896]{2,1,0:T(8,128)(2,1)S(1)}, u32[]{:S(2)}, u32[]{:S(2)}) collective-permute-start(bf16[1,176,896]{2,1,0:T(8,128)(2,1)S(1)} %slice_select_fusion.4), channel_id=1, source_target_pairs={{0,4},{4,0},{8,12},{12,8},{1,5},{5,1},{9,13},{13,9},{2,6},{6,2},{1... | collective-permute-start | bytes 946184 | tf_op jit(solution)/shard_map/ppermute | solution.py:425
  174.7 8.7 %collective-permute-start.29 = (bf16[1,160,896]{2,1,0:T(8,128)(2,1)S(1)}, bf16[1,160,896]{2,1,0:T(8,128)(2,1)S(1)}, u32[]{:S(2)}, u32[]{:S(2)}) collective-permute-start(bf16[1,160,896]{2,1,0:T(8,128)(2,1)S(1)} %slice_select_fusion.5), channel_id=1, source_target_pairs={{0,8},{4,12},{8,0},{12,4},{1,9},{5,13},{9,1},{13,5},{2,10},{6,14},... | collective-permute-start | bytes 860168 | tf_op jit(solution)/shard_map/ppermute | solution.py:425
  176.4 36.9 %collective-permute-start.24 = (bf16[256,1792]{1,0:T(8,128)(2,1)}, bf16[256,1792]{1,0:T(8,128)(2,1)S(1)}, u32[]{:S(2)}, u32[]{:S(2)}) collective-permute-start(bf16[256,1792]{1,0:T(8,128)(2,1)} %get-tuple-element.14._.x_ref), channel_id=1, source_target_pairs={{0,1},{1,0},{2,3},{3,2},{4,5},{5,4},{6,7},{7,6},{8,9},{9,8},{10,11... | collective-permute-start | bytes 2752520 | tf_op jit(solution)/shard_map/ppermute | solution.py:425
  186.5 30.1 %collective-permute-start.30 = (bf16[3,112,896]{2,1,0:T(8,128)(2,1)}, bf16[3,112,896]{2,1,0:T(8,128)(2,1)S(1)}, u32[]{:S(2)}, u32[]{:S(2)}) collective-permute-start(bf16[3,112,896]{2,1,0:T(8,128)(2,1)} %broadcast_select_fusion.1), channel_id=1, source_target_pairs={{0,4},{4,0},{8,12},{12,8},{1,5},{5,1},{9,13},{13,9},{2,6},{6,2},{1... | collective-permute-start | bytes 1806344 | tf_op jit(solution)/shard_map/ppermute | solution.py:425
  188.2 30.3 %collective-permute-start.31 = (bf16[3,112,896]{2,1,0:T(8,128)(2,1)}, bf16[3,112,896]{2,1,0:T(8,128)(2,1)S(1)}, u32[]{:S(2)}, u32[]{:S(2)}) collective-permute-start(bf16[3,112,896]{2,1,0:T(8,128)(2,1)} %broadcast_select_fusion.1), channel_id=1, source_target_pairs={{0,8},{4,12},{8,0},{12,4},{1,9},{5,13},{9,1},{13,5},{2,10},{6,14},... | collective-permute-start | bytes 1806344 | tf_op jit(solution)/shard_map/ppermute | solution.py:425
  188.5 13.9 %collective-permute-start.25 = (bf16[80,1792]{1,0:T(8,128)(2,1)S(1)}, bf16[80,1792]{1,0:T(8,128)(2,1)S(1)}, u32[]{:S(2)}, u32[]{:S(2)}) collective-permute-start(bf16[80,1792]{1,0:T(8,128)(2,1)S(1)} %copy-done.25), channel_id=1, source_target_pairs={{0,5},{1,4},{2,7},{3,6},{4,9},{5,8},{6,11},{7,10},{8,13},{9,12},{1... | collective-permute-start | bytes 860168 | tf_op jit(solution)/shard_map/ppermute | solution.py:650
  190.2 22.5 %collective-permute-start.23 = (bf16[80,1792]{1,0:T(8,128)(2,1)S(1)}, bf16[80,1792]{1,0:T(8,128)(2,1)S(1)}, u32[]{:S(2)}, u32[]{:S(2)}) collective-permute-start(bf16[80,1792]{1,0:T(8,128)(2,1)S(1)} %copy-done.25), channel_id=1, source_target_pairs={{0,4},{4,8},{8,12},{1,5},{5,9},{9,13},{2,6},{6,10},{10,14},{3,7},{... | collective-permute-start | bytes 860168 | tf_op jit(solution)/shard_map/ppermute | solution.py:648
  202.5 25.0 %copy-start.21 = (bf16[80,1792]{1,0:T(8,128)(2,1)}, bf16[80,1792]{1,0:T(8,128)(2,1)S(1)}, u32[]{:S(2)}) copy-start(bf16[80,1792]{1,0:T(8,128)(2,1)S(1)} %collective-permute-done.25.halo_ref) | copy-start | bytes 860164
  212.7 8.1 %copy-start.20 = (bf16[80,1792]{1,0:T(8,128)(2,1)}, bf16[80,1792]{1,0:T(8,128)(2,1)S(1)}, u32[]{:S(2)}) copy-start(bf16[80,1792]{1,0:T(8,128)(2,1)S(1)} %collective-permute-done.23.halo_ref) | copy-start | bytes 860164
  213.3 0.9 copy-start.15
  218.5 0.9 copy-start.17
  222.7 4.8 %copy-start.2 = (bf16[4,1,336,896]{3,2,1,0:T(8,128)(2,1)}, bf16[4,1,336,896]{3,2,1,0:T(8,128)(2,1)S(1)}, u32[]{:S(2)}) copy-start(bf16[4,1,336,896]{3,2,1,0:T(8,128)(2,1)S(1)} %maximum_select_fusion.2.near_ref) | copy-start | bytes 7225348
  222.7 4.8 %collective-permute-start.32 = (bf16[4,1,336,896]{3,2,1,0:T(8,128)(2,1)S(1)}, bf16[4,1,336,896]{3,2,1,0:T(8,128)(2,1)}, u32[]{:S(2)}, u32[]{:S(2)}) collective-permute-start(bf16[4,1,336,896]{3,2,1,0:T(8,128)(2,1)S(1)} %maximum_select_fusion.2.near_ref), channel_id=1, source_target_pairs={{0,16},{16,0},{1,17},{17,1},{2,18},{18,2},{3,19},{19,3},{4,20},{20... | collective-permute-start | bytes 7225352 | tf_op jit(solution)/shard_map/ppermute | solution.py:425
  222.8 20.7 %collective-permute-start.34 = (bf16[3,112,896]{2,1,0:T(8,128)(2,1)}, bf16[3,112,896]{2,1,0:T(8,128)(2,1)}, u32[]{:S(2)}, u32[]{:S(2)}) collective-permute-start(bf16[3,112,896]{2,1,0:T(8,128)(2,1)} %broadcast_select_fusion.1), channel_id=1, source_target_pairs={{0,12},{4,8},{8,4},{12,0},{1,13},{5,9},{9,5},{13,1},{2,14},{6,10},... | collective-permute-start | bytes 1806344 | tf_op jit(solution)/shard_map/ppermute | solution.py:425
  227.5 15.9 %copy-start.12 = (bf16[1,3,112,896]{3,2,1,0:T(8,128)(2,1)S(1)}, bf16[1,3,112,896]{3,2,1,0:T(8,128)(2,1)}, u32[]{:S(2)}) copy-start(bf16[1,3,112,896]{3,2,1,0:T(8,128)(2,1)} %fusion.14) | copy-start | bytes 1806340
  243.4 2.2 copy-start.13
  243.5 2.2 copy-start.26
  243.5 2.2 copy-start.27
  245.4 15.9 %copy-start.4 = (bf16[4,3,112,896]{3,2,1,0:T(8,128)(2,1)}, bf16[4,3,112,896]{3,2,1,0:T(8,128)(2,1)S(1)}, u32[]{:S(2)}) copy-start(bf16[4,3,112,896]{3,2,1,0:T(8,128)(2,1)S(1)} %maximum_select_fusion.3.near_ref) | copy-start | bytes 7225348
  245.4 15.9 %collective-permute-start.35 = (bf16[4,3,112,896]{3,2,1,0:T(8,128)(2,1)S(1)}, bf16[4,3,112,896]{3,2,1,0:T(8,128)(2,1)}, u32[]{:S(2)}, u32[]{:S(2)}) collective-permute-start(bf16[4,3,112,896]{3,2,1,0:T(8,128)(2,1)S(1)} %maximum_select_fusion.3.near_ref), channel_id=1, source_target_pairs={{0,16},{16,0},{1,17},{17,1},{2,18},{18,2},{3,19},{19,3},{4,20},{20... | collective-permute-start | bytes 7225352 | tf_op jit(solution)/shard_map/ppermute | solution.py:425
  245.6 15.7 %collective-permute-start.33 = (bf16[2,256,512]{2,1,0:T(8,128)(2,1)S(1)}, bf16[2,256,512]{2,1,0:T(8,128)(2,1)S(1)}, u32[]{:S(2)}, u32[]{:S(2)}) collective-permute-start(bf16[2,256,512]{2,1,0:T(8,128)(2,1)S(1)} %copy-done.13), channel_id=1, source_target_pairs={{0,1},{1,0},{2,3},{3,2},{4,5},{5,4},{6,7},{7,6},{8,9},{9,8},{10,11... | collective-permute-start | bytes 1572872 | tf_op jit(solution)/shard_map/ppermute | solution.py:425
  268.8 29.2 %copy-start.1 = (bf16[64,4,1792]{2,1,0:T(4,128)(2,1)S(1)}, bf16[64,4,1792]{2,1,0:T(4,128)(2,1)}, u32[]{:S(2)}) copy-start(bf16[64,4,1792]{2,1,0:T(4,128)(2,1)} %param.17) | copy-start | bytes 2752516
  (2 other events, 1.6 us)

commit v15 on v12

--- a/solution.py
+++ b/solution.py
@@ -452,7 +452,7 @@
     return across(held, "seq", 1), across(held, "seq", 2)
 
 
-def from_plane(held, near_by, diagonal, over_cores, over_across=()):
+def from_plane(held, near_by, diagonal, over_cores, over_across=(), others=()):
     beside, above = near_by
     if diagonal is None:
         opposite = across(after(held, over_across), "seq", 3)
@@ -463,7 +463,10 @@
             across(after(beside[:, half:], diagonal), "seq", 2),
         ]
         opposite = after(jnp.concatenate(opposite, axis=1), over_cores)
-    near = after(jnp.stack([held, beside, above, opposite]), over_cores)
+    near = [held, beside, above, opposite]
+    for other in others:
+        near[3] = near[3] + other.reshape(near[3].shape) * jnp.zeros((), BF16)
+    near = after(jnp.stack(near), over_cores)
     return near, across(near, "dp", 1)
 
 
@@ -657,7 +660,7 @@
     held_out_two = after(held_out_two, (residual,))
     near_by_two = neighbours(held_out_two)
     near_window = from_plane(
-        held_window, near_by_window, (residual,), (pair_rows, pair_halo, *near_by_two)
+        held_window, near_by_window, (residual,), (pair_rows, pair_halo), (), near_by_two
     )
     block_start = (seq_place * rows).astype(jnp.int32)[None]
 

time: 296 us -> 299 us (1.010)
  waiting for transfers between devices: 85.1 us -> 89.6 us
    slice x15 -> x13, local copies, waits for them, and re-layouts: 10.4 us -> 9.58 us  [after(): lax.slice(other, (0,) * other.ndim, (1,) * other.ndim)]
  transfers between devices with their start and end apart: 38 -> 38, of which waited for: 15 -> 16; matrix products, arithmetic and copies ran while one was open for 14% -> 13% of each run, Pallas kernels for 17% -> 17%
where the time goes in v15:
time: 299 us; the launch traced here: 297 us
  waiting for transfers between devices  89.6 us (30%)
  Pallas kernels  57.8 us (19%)
  starting transfers between devices  57.6 us (19%)
  local copies, waits for them, and re-layouts  30.5 us (10%)
  other arithmetic  27 us (9%)
  blocking collectives  25 us (8%)
  between operations  9.3 us (3%)
    ppermute x31, waiting for transfers between devices, across(): lax.ppermute(array, axis, [(i, i ^ bit) for i in range(lax.axis_size(axis...  36.7 us
    ppermute x31, starting transfers between devices, across(): lax.ppermute(array, axis, [(i, i ^ bit) for i in range(lax.axis_size(axis...  35.3 us
    pallas_call x2, Pallas kernels, window_rows(): call(functools.partial(window_kernel, heads), 2, [SMEM, SMEM, *[HBM] * 5,...  28.3 us
    all_to_all x1, blocking collectives, on_device(): lax.all_to_all(result, 'tensor', split_axis=0, concat_axis=0, tiled=True)  25 us
    all_to_all x1, waiting for transfers between devices, on_device(): lax.all_to_all(picked, 'tensor', split_axis=0, concat_axis=0, tiled=True)  20.8 us
    select_n x21, other arithmetic, after(): return jnp.where(zero == 0.0, array, jnp.zeros_like(array))  19.9 us
    ppermute x1, waiting for transfers between devices, on_device(): lax.ppermute(tail, ('seq', 'tensor'), [(i * group_count + j, (i + 1) * gr...  18.3 us
    pallas_call x1, Pallas kernels, on_device(): call(functools.partial(linear_kernel, heads, feature_dim, kept), group_co...  12.4 us
  transfers between devices with their start and end apart: 38, of which 16 were waited for; matrix products, arithmetic and copies ran while one was open for 13% of the time, Pallas kernels for 17%

profile of v15, /device:TPU:0, one launch (start us, length us, event | category | flops | bytes accessed | tf_op | source)
XLA Modules:
  0.0 296.7 jit_solution(8541813150780918802)
XLA Ops:
  1.9 4.1 %collective-permute-start.2 = (bf16[144,896]{1,0:T(8,128)(2,1)S(1)}, bf16[144,896]{1,0:T(8,128)(2,1)S(1)}, u32[]{:S(2)}, u32[]{:S(2)}) collective-permute-start(bf16[144,896]{1,0:T(8,128)(2,1)S(1)} %pad_maximum_fusion.1), channel_id=1, source_target_pairs={{0,2},{1,3},{2,0},{3,1},{4,6},{5,7},{6,4},{7,5},{8,10},{9,11},{10,... | collective-permute-start | bytes 774152 | tf_op jit(solution)/shard_map/ppermute | solution.py:425
  6.0 1.6 collective-permute-start.1
  10.0 2.2 gather_fusion.1
  12.2 3.7 %all-to-all-start = ((bf16[8,8,4,1792]{3,2,1,0:T(4,128)(2,1)}), bf16[8,8,4,1792]{3,2,1,0:T(4,128)(2,1)S(1)}, u32[]{:S(2)}, u32[]{:S(2)}) async-start(bf16[8,8,4,1792]{3,2,1,0:T(4,128)(2,1)} %bitcast.20), calls=%async_computation | async-start | bytes 1835008 | tf_op jit(solution)/shard_map/all_to_all | solution.py:551
  18.6 3.1 %collective-permute-done = f32[3,1536]{1,0:T(4,128)S(1)} collective-permute-done((f32[3,1536]{1,0:T(4,128)S(1)}, f32[3,1536]{1,0:T(4,128)S(1)}, u32[]{:S(2)}, u32[]{:S(2)}) %collective-permute-start) | collective-permute-done | bytes 18464 | tf_op jit(solution)/shard_map/ppermute | solution.py:425
  22.8 3.4 %collective-permute-done.3 = bf16[144,896]{1,0:T(8,128)(2,1)S(1)} collective-permute-done((bf16[144,896]{1,0:T(8,128)(2,1)S(1)}, bf16[144,896]{1,0:T(8,128)(2,1)S(1)}, u32[]{:S(2)}, u32[]{:S(2)}) %collective-permute-start.3) | collective-permute-done | bytes 258080 | tf_op jit(solution)/shard_map/ppermute | solution.py:425
  27.5 1.8 all-to-all-done
  29.4 1.3 gather_fusion.2
  32.2 3.5 %all-to-all-start.1 = ((bf16[4,16,4,1792]{3,1,2,0:T(8,128)(2,1)}), bf16[4,16,4,1792]{3,1,2,0:T(8,128)(2,1)S(1)}, u32[]{:S(2)}, u32[]{:S(2)}) async-start(bf16[4,16,4,1792]{3,1,2,0:T(8,128)(2,1)} %copy.47), calls=%async_computation.1 | async-start | bytes 1835008 | tf_op jit(solution)/shard_map/all_to_all | solution.py:558
  35.7 1.1 collective-permute-start.8
  38.9 1.6 select_bitcast_fusion.1
  40.5 2.9 collective-permute-start.5
  43.5 20.8 %all-to-all-done.1 = bf16[4,16,4,1792]{3,1,2,0:T(8,128)(2,1)S(1)} async-done(((bf16[4,16,4,1792]{3,1,2,0:T(8,128)(2,1)}), bf16[4,16,4,1792]{3,1,2,0:T(8,128)(2,1)S(1)}, u32[]{:S(2)}, u32[]{:S(2)}) %all-to-all-start.1) | async-done | bytes 917536 | tf_op jit(solution)/shard_map/all_to_all | solution.py:558
  65.5 1.1 collective-permute-start.9
  66.6 1.0 slice_select_fusion.3
  68.2 2.0 collective-permute-start.6
  70.3 4.9 %collective-permute-done.4 = bf16[112,896]{1,0:T(8,128)(2,1)S(1)} collective-permute-done((bf16[112,896]{1,0:T(8,128)(2,1)}, bf16[112,896]{1,0:T(8,128)(2,1)S(1)}, u32[]{:S(2)}, u32[]{:S(2)}) %collective-permute-start.4) | collective-permute-done | bytes 200736 | tf_op jit(solution)/shard_map/ppermute | solution.py:425
  75.1 2.1 collective-permute-done.6
  77.3 1.8 pad_maximum_fusion
  79.1 1.2 slice.106
  81.2 1.7 maximum_select_fusion.near_ref
  83.0 2.1 constant_dynamic-slice_fusion
  86.1 1.0 maximum_select_fusion.4
  88.0 1.4 collective-permute-start.18
  90.1 1.7 collective-permute-start.19
  91.8 1.4 copy.48
  93.2 2.4 reshape.592.x_ref
  95.6 12.4 %linear_rows.1 = (f32[4,256,512]{2,1,0:T(8,128)}, bf16[4,256,128]{2,1,0:T(8,128)(2,1)}, bf16[4,640,128]{2,1,0:T(8,128)(2,1)}) custom-call(s32[5]{0:T(128)} %pad_add_fusion.place_ref, bf16[256,1792]{1,0:T(8,128)(2,1)} %reshape.592.x_ref, f32[1,1792]{1,0:T(1,128)} %broadcast_in_dim.128.gain_ref, bf16[1,4,112,1792]{3,2,1,0:T(8,128)(2,1)} %bitcast.109, ...), custom_call_target="tpu_custom_call" | custom-call | tf_op jit(solution)/shard_map/linear_rows/pallas_call | solution.py:579
  108.0 2.3 collective-permute-start.14
  110.3 1.3 collective-permute-start.13
  111.6 1.2 slice.83
  113.5 11.1 %collective-permute-done.15 = bf16[448,896]{1,0:T(8,128)(2,1)} collective-permute-done((bf16[448,896]{1,0:T(8,128)(2,1)}, bf16[448,896]{1,0:T(8,128)(2,1)}, u32[]{:S(2)}, u32[]{:S(2)}) %collective-permute-start.15) | collective-permute-done | bytes 802848 | tf_op jit(solution)/shard_map/ppermute | solution.py:425
  124.6 3.5 %collective-permute-start.12 = (bf16[4,640,128]{2,1,0:T(8,128)(2,1)}, bf16[4,640,128]{2,1,0:T(8,128)(2,1)S(1)}, u32[]{:S(2)}, u32[]{:S(2)}) collective-permute-start(bf16[4,640,128]{2,1,0:T(8,128)(2,1)} %get-tuple-element.13), channel_id=1, source_target_pairs={{0,4},{4,8},{8,12},{1,5},{5,9},{9,13},{2,6},{6,10},{10,14},{3,7},{... | collective-permute-start | bytes 1966088 | tf_op jit(solution)/shard_map/ppermute | solution.py:477
  128.2 1.2 select_bitcast_fusion
  131.0 1.7 collective-permute-start.21
  132.7 1.0 slice_select_fusion.2
  133.8 2.0 collective-permute-start.17
  135.9 7.5 %collective-permute-done.12 = bf16[4,640,128]{2,1,0:T(8,128)(2,1)S(1)} collective-permute-done((bf16[4,640,128]{2,1,0:T(8,128)(2,1)}, bf16[4,640,128]{2,1,0:T(8,128)(2,1)S(1)}, u32[]{:S(2)}, u32[]{:S(2)}) %collective-permute-start.12) | collective-permute-done | bytes 655392 | tf_op jit(solution)/shard_map/ppermute | solution.py:477
  146.6 2.3 collective-permute-done.21
  149.0 2.9 collective-permute-done.20
  152.0 1.9 maximum_select_fusion.1.near_ref
  154.0 1.0 slice_select_fusion
  155.9 1.7 collective-permute-start.27
  158.6 1.5 copy-done.12
  160.1 10.4 %linear_out.1 = (bf16[256,1792]{1,0:T(8,128)(2,1)}, bf16[256,1792]{1,0:T(8,128)(2,1)}, bf16[80,1792]{1,0:T(8,128)(2,1)}) custom-call(s32[5]{0:T(128)} %pad_add_fusion.place_ref, f32[4,256,512]{2,1,0:T(8,128)} %get-tuple-element.11.num_ref, bf16[4,256,128]{2,1,0:T(8,128)(2,1)} %get-tuple-element.12.q_ref, bf16[128,1024]{1,0:T(8,128)(2,1)} %constant.129.clone.first_ref, ...), custom_call_target="tpu_custom_call" | custom-call | tf_op jit(solution)/shard_map/linear_out/pallas_call | solution.py:619
  170.5 1.3 slice.93
  173.3 2.0 collective-permute-start.30
  175.3 3.5 %collective-permute-start.25 = (bf16[80,1792]{1,0:T(8,128)(2,1)}, bf16[80,1792]{1,0:T(8,128)(2,1)S(1)}, u32[]{:S(2)}, u32[]{:S(2)}) collective-permute-start(bf16[80,1792]{1,0:T(8,128)(2,1)} %get-tuple-element.15), channel_id=1, source_target_pairs={{0,5},{1,4},{2,7},{3,6},{4,9},{5,8},{6,11},{7,10},{8,13},{9,12},{1... | collective-permute-start | bytes 860168 | tf_op jit(solution)/shard_map/ppermute | solution.py:651
  179.8 2.1 collective-permute-start.29
  182.9 18.3 %collective-permute-done.25.halo_ref = bf16[80,1792]{1,0:T(8,128)(2,1)S(1)} collective-permute-done((bf16[80,1792]{1,0:T(8,128)(2,1)}, bf16[80,1792]{1,0:T(8,128)(2,1)S(1)}, u32[]{:S(2)}, u32[]{:S(2)}) %collective-permute-start.25) | collective-permute-done | bytes 286752 | tf_op jit(solution)/shard_map/ppermute | solution.py:651
  201.2 3.6 %collective-permute-start.28 = (bf16[1,176,896]{2,1,0:T(8,128)(2,1)S(1)}, bf16[1,176,896]{2,1,0:T(8,128)(2,1)S(1)}, u32[]{:S(2)}, u32[]{:S(2)}) collective-permute-start(bf16[1,176,896]{2,1,0:T(8,128)(2,1)S(1)} %slice_select_fusion.4), channel_id=1, source_target_pairs={{0,4},{4,0},{8,12},{12,8},{1,5},{5,1},{9,13},{13,9},{2,6},{6,2},{1... | collective-permute-start | bytes 946184 | tf_op jit(solution)/shard_map/ppermute | solution.py:425
  207.9 3.2 %collective-permute-done.28 = bf16[1,176,896]{2,1,0:T(8,128)(2,1)S(1)} collective-permute-done((bf16[1,176,896]{2,1,0:T(8,128)(2,1)S(1)}, bf16[1,176,896]{2,1,0:T(8,128)(2,1)S(1)}, u32[]{:S(2)}, u32[]{:S(2)}) %collective-permute-start.28) | collective-permute-done | bytes 315424 | tf_op jit(solution)/shard_map/ppermute | solution.py:425
  211.3 1.7 maximum_select_fusion.2.near_ref
  213.1 1.8 collective-permute-start.34
  215.9 2.0 collective-permute-done.32.far_ref
  217.8 14.2 %window_rows.2._ = bf16[2,256,512]{2,1,0:T(8,128)(2,1)} custom-call(s32[5]{0:T(128)} %pad_add_fusion.place_ref, s32[1]{0:T(128)} %bitcast.2.first_ref, bf16[256,1792]{1,0:T(8,128)(2,1)} %copy-done.18, bf16[80,1792]{1,0:T(8,128)(2,1)} %copy-done.21, bf16[3,4,112,1792]{3,2,1,0:T(8,128)(2,1)} %bitcast.95, bf16[4,1,336,896]{3,2,1,0:T(8,128)(2,1)} %copy-done.2, ...), custom_call_target="tpu_custom_call" | custom-call | tf_op jit(solution)/shard_map/window_rows/pallas_call | solution.py:668
  232.0 1.2 slice.121
  233.9 1.9 maximum_select_fusion.3.near_ref
  236.6 4.4 %collective-permute-start.23 = (bf16[80,1792]{1,0:T(8,128)(2,1)}, bf16[80,1792]{1,0:T(8,128)(2,1)}, u32[]{:S(2)}, u32[]{:S(2)}) collective-permute-start(bf16[80,1792]{1,0:T(8,128)(2,1)} %get-tuple-element.15), channel_id=1, source_target_pairs={{0,4},{4,8},{8,12},{1,5},{5,9},{9,13},{2,6},{6,10},{10,14},{3,7},{... | collective-permute-start | bytes 860168 | tf_op jit(solution)/shard_map/ppermute | solution.py:649
  242.5 4.4 %collective-permute-done.23.halo_ref = bf16[80,1792]{1,0:T(8,128)(2,1)} collective-permute-done((bf16[80,1792]{1,0:T(8,128)(2,1)}, bf16[80,1792]{1,0:T(8,128)(2,1)}, u32[]{:S(2)}, u32[]{:S(2)}) %collective-permute-start.23) | collective-permute-done | bytes 286752 | tf_op jit(solution)/shard_map/ppermute | solution.py:649
  246.9 14.1 %window_rows.3.mixed_ref = bf16[2,256,512]{2,1,0:T(8,128)(2,1)} custom-call(s32[5]{0:T(128)} %pad_add_fusion.place_ref, s32[1]{0:T(128)} %bitcast.2.first_ref, bf16[256,1792]{1,0:T(8,128)(2,1)} %get-tuple-element.14._.x_ref, bf16[80,1792]{1,0:T(8,128)(2,1)} %collective-permute-done.23.halo_ref, bf16[3,4,112,1792]{3,2,1,0:T(8,128)(2,1)} %bitcast.96, ...), custom_call_target="tpu_custom_call" | custom-call | tf_op jit(solution)/shard_map/window_rows/pallas_call | solution.py:668
  261.9 6.7 %window_out.1 = bf16[256,1792]{1,0:T(8,128)(2,1)} custom-call(s32[5]{0:T(128)} %pad_add_fusion.place_ref, s32[1]{0:T(128)} %bitcast.1.live_ref, bf16[2,256,512]{2,1,0:T(8,128)(2,1)} %window_rows.3.mixed_ref, bf16[2,256,512]{2,1,0:T(8,128)(2,1)} %copy-done.19, bf16[1,4,112,1792]{3,2,1,0:T(8,128)(2,1)} %bitcast.113, bf16[4,3,112,896]{3,2,1,0:T(8,128)(2,1)} %copy-done.4, ...), custom_call_target="tpu_custom_call" | custom-call | tf_op jit(solution)/shard_map/window_out/pallas_call | solution.py:693
  268.6 1.9 reshape.598
  270.8 25.0 %all_to_all.15 = bf16[4,16,4,1792]{3,2,1,0:T(4,128)(2,1)S(1)} all-to-all(bf16[4,16,4,1792]{3,2,1,0:T(4,128)(2,1)S(1)} %bitcast.100), channel_id=1, replica_groups=mesh['dp'=2,'seq'=4,'tensor'=4] {'tensor'}, dimensions={0} | all-to-all | bytes 1835008 | tf_op jit(solution)/shard_map/all_to_all | solution.py:714
  (162 shorter events, 30.0 us)
Async XLA Ops:
  0.0 9.9 %copy-start = (bf16[64,4,1792]{2,1,0:T(4,128)(2,1)S(1)}, bf16[64,4,1792]{2,1,0:T(4,128)(2,1)}, u32[]{:S(2)}) copy-start(bf16[64,4,1792]{2,1,0:T(4,128)(2,1)} %param.17) | copy-start | bytes 2752516
  0.9 15.0 %copy-start.22 = (f32[3,3,448]{2,1,0:T(4,128)S(1)}, f32[3,3,448]{2,1,0:T(4,128)}, u32[]{:S(2)}) copy-start(f32[3,3,448]{2,1,0:T(4,128)} %param.27) | copy-start | bytes 48388
  1.9 16.0 %collective-permute-start.2 = (bf16[144,896]{1,0:T(8,128)(2,1)S(1)}, bf16[144,896]{1,0:T(8,128)(2,1)S(1)}, u32[]{:S(2)}, u32[]{:S(2)}) collective-permute-start(bf16[144,896]{1,0:T(8,128)(2,1)S(1)} %pad_maximum_fusion.1), channel_id=1, source_target_pairs={{0,2},{1,3},{2,0},{3,1},{4,6},{5,7},{6,4},{7,5},{8,10},{9,11},{10,... | collective-permute-start | bytes 774152 | tf_op jit(solution)/shard_map/ppermute | solution.py:425
  6.0 16.8 %collective-permute-start.1 = (bf16[144,896]{1,0:T(8,128)(2,1)S(1)}, bf16[144,896]{1,0:T(8,128)(2,1)S(1)}, u32[]{:S(2)}, u32[]{:S(2)}) collective-permute-start(bf16[144,896]{1,0:T(8,128)(2,1)S(1)} %pad_maximum_fusion.1), channel_id=1, source_target_pairs={{0,1},{1,0},{2,3},{3,2},{4,5},{5,4},{6,7},{7,6},{8,9},{9,8},{10,11... | collective-permute-start | bytes 774152 | tf_op jit(solution)/shard_map/ppermute | solution.py:425
  12.2 17.2 %all-to-all-start = ((bf16[8,8,4,1792]{3,2,1,0:T(4,128)(2,1)}), bf16[8,8,4,1792]{3,2,1,0:T(4,128)(2,1)S(1)}, u32[]{:S(2)}, u32[]{:S(2)}) async-start(bf16[8,8,4,1792]{3,2,1,0:T(4,128)(2,1)} %bitcast.20), calls=%async_computation | async-start | bytes 1835008 | tf_op jit(solution)/shard_map/all_to_all | solution.py:551
  16.7 5.0 %collective-permute-start = (f32[3,1536]{1,0:T(4,128)S(1)}, f32[3,1536]{1,0:T(4,128)S(1)}, u32[]{:S(2)}, u32[]{:S(2)}) collective-permute-start(f32[3,1536]{1,0:T(4,128)S(1)} %reshape.582), channel_id=1, source_target_pairs={{0,2},{1,3},{2,0},{3,1},{4,6},{5,7},{6,4},{7,5},{8,10},{9,11},{10,... | collective-permute-start | bytes 55304 | tf_op jit(solution)/shard_map/ppermute | solution.py:425
  17.9 8.4 %collective-permute-start.3 = (bf16[144,896]{1,0:T(8,128)(2,1)S(1)}, bf16[144,896]{1,0:T(8,128)(2,1)S(1)}, u32[]{:S(2)}, u32[]{:S(2)}) collective-permute-start(bf16[144,896]{1,0:T(8,128)(2,1)S(1)} %collective-permute-done.2), channel_id=1, source_target_pairs={{0,1},{1,0},{2,3},{3,2},{4,5},{5,4},{6,7},{7,6},{8,9},{9,8},{10,11... | collective-permute-start | bytes 774152 | tf_op jit(solution)/shard_map/ppermute | solution.py:425
  21.7 9.4 %copy-start.20 = (f32[2,3,1536]{2,1,0:T(4,128)}, f32[2,3,1536]{2,1,0:T(4,128)S(1)}, u32[]{:S(2)}) copy-start(f32[2,3,1536]{2,1,0:T(4,128)S(1)} %pad_maximum_fusion.2.tap_ref) | copy-start | bytes 110596
  26.4 10.4 %copy-start.10 = (bf16[3,144,896]{2,1,0:T(8,128)(2,1)}, bf16[3,144,896]{2,1,0:T(8,128)(2,1)S(1)}, u32[]{:S(2)}) copy-start(bf16[3,144,896]{2,1,0:T(8,128)(2,1)S(1)} %maximum_select_fusion.5) | copy-start | bytes 2322436
  32.2 32.1 %all-to-all-start.1 = ((bf16[4,16,4,1792]{3,1,2,0:T(8,128)(2,1)}), bf16[4,16,4,1792]{3,1,2,0:T(8,128)(2,1)S(1)}, u32[]{:S(2)}, u32[]{:S(2)}) async-start(bf16[4,16,4,1792]{3,1,2,0:T(8,128)(2,1)} %copy.47), calls=%async_computation.1 | async-start | bytes 1835008 | tf_op jit(solution)/shard_map/all_to_all | solution.py:558
  35.7 29.7 %collective-permute-start.8 = (bf16[3,144,896]{2,1,0:T(8,128)(2,1)S(1)}, bf16[3,144,896]{2,1,0:T(8,128)(2,1)S(1)}, u32[]{:S(2)}, u32[]{:S(2)}) collective-permute-start(bf16[3,144,896]{2,1,0:T(8,128)(2,1)S(1)} %maximum_select_fusion.5), channel_id=1, source_target_pairs={{0,8},{4,12},{8,0},{12,4},{1,9},{5,13},{9,1},{13,5},{2,10},{6,14},... | collective-permute-start | bytes 2322440 | tf_op jit(solution)/shard_map/ppermute | solution.py:425
  36.8 29.7 %collective-permute-start.7 = (bf16[3,144,896]{2,1,0:T(8,128)(2,1)S(1)}, bf16[3,144,896]{2,1,0:T(8,128)(2,1)}, u32[]{:S(2)}, u32[]{:S(2)}) collective-permute-start(bf16[3,144,896]{2,1,0:T(8,128)(2,1)S(1)} %maximum_select_fusion.5), channel_id=1, source_target_pairs={{0,4},{4,0},{8,12},{12,8},{1,5},{5,1},{9,13},{13,9},{2,6},{6,2},{1... | collective-permute-start | bytes 2322440 | tf_op jit(solution)/shard_map/ppermute | solution.py:425
  40.5 27.7 %collective-permute-start.5 = (bf16[112,896]{1,0:T(8,128)(2,1)}, bf16[112,896]{1,0:T(8,128)(2,1)}, u32[]{:S(2)}, u32[]{:S(2)}) collective-permute-start(bf16[112,896]{1,0:T(8,128)(2,1)} %select_bitcast_fusion.1), channel_id=1, source_target_pairs={{0,2},{1,3},{2,0},{3,1},{4,6},{5,7},{6,4},{7,5},{8,10},{9,11},{10,... | collective-permute-start | bytes 602120 | tf_op jit(solution)/shard_map/ppermute | solution.py:425
  64.2 16.9 %copy-start.7 = (bf16[4,16,4,1792]{3,1,2,0:T(8,128)(2,1)}, bf16[4,16,4,1792]{3,1,2,0:T(8,128)(2,1)S(1)}, u32[]{:S(2)}) copy-start(bf16[4,16,4,1792]{3,1,2,0:T(8,128)(2,1)S(1)} %all-to-all-done.1) | copy-start | bytes 2752516
  64.3 16.9 %copy-start.11 = (bf16[3,144,896]{2,1,0:T(8,128)(2,1)S(1)}, bf16[3,144,896]{2,1,0:T(8,128)(2,1)}, u32[]{:S(2)}) copy-start(bf16[3,144,896]{2,1,0:T(8,128)(2,1)} %copy-done.10) | copy-start | bytes 2322436
  65.4 15.8 %copy-start.17 = (bf16[3,144,896]{2,1,0:T(8,128)(2,1)}, bf16[3,144,896]{2,1,0:T(8,128)(2,1)S(1)}, u32[]{:S(2)}) copy-start(bf16[3,144,896]{2,1,0:T(8,128)(2,1)S(1)} %collective-permute-done.8) | copy-start | bytes 2322436
  65.5 15.5 %collective-permute-start.9 = (bf16[3,80,896]{2,1,0:T(8,128)(2,1)S(1)}, bf16[3,80,896]{2,1,0:T(8,128)(2,1)S(1)}, u32[]{:S(2)}, u32[]{:S(2)}) collective-permute-start(bf16[3,80,896]{2,1,0:T(8,128)(2,1)S(1)} %slice_select_fusion.1), channel_id=1, source_target_pairs={{0,4},{4,0},{8,12},{12,8},{1,5},{5,1},{9,13},{13,9},{2,6},{6,2},{1... | collective-permute-start | bytes 1290248 | tf_op jit(solution)/shard_map/ppermute | solution.py:425
  67.6 13.4 %collective-permute-start.10 = (bf16[3,64,896]{2,1,0:T(8,128)(2,1)S(1)}, bf16[3,64,896]{2,1,0:T(8,128)(2,1)S(1)}, u32[]{:S(2)}, u32[]{:S(2)}) collective-permute-start(bf16[3,64,896]{2,1,0:T(8,128)(2,1)S(1)} %slice_select_fusion.3), channel_id=1, source_target_pairs={{0,8},{4,12},{8,0},{12,4},{1,9},{5,13},{9,1},{13,5},{2,10},{6,14},... | collective-permute-start | bytes 1032200 | tf_op jit(solution)/shard_map/ppermute | solution.py:425
  68.2 6.9 %collective-permute-start.4 = (bf16[112,896]{1,0:T(8,128)(2,1)}, bf16[112,896]{1,0:T(8,128)(2,1)S(1)}, u32[]{:S(2)}, u32[]{:S(2)}) collective-permute-start(bf16[112,896]{1,0:T(8,128)(2,1)} %select_bitcast_fusion.1), channel_id=1, source_target_pairs={{0,1},{1,0},{2,3},{3,2},{4,5},{5,4},{6,7},{7,6},{8,9},{9,8},{10,11... | collective-permute-start | bytes 602120 | tf_op jit(solution)/shard_map/ppermute | solution.py:425
  68.2 9.1 %collective-permute-start.6 = (bf16[112,896]{1,0:T(8,128)(2,1)}, bf16[112,896]{1,0:T(8,128)(2,1)S(1)}, u32[]{:S(2)}, u32[]{:S(2)}) collective-permute-start(bf16[112,896]{1,0:T(8,128)(2,1)} %collective-permute-done.5), channel_id=1, source_target_pairs={{0,1},{1,0},{2,3},{3,2},{4,5},{5,4},{6,7},{7,6},{8,9},{9,8},{10,11... | collective-permute-start | bytes 602120 | tf_op jit(solution)/shard_map/ppermute | solution.py:425
  82.9 10.2 %copy-start.3 = (bf16[4,3,144,896]{3,2,1,0:T(8,128)(2,1)}, bf16[4,3,144,896]{3,2,1,0:T(8,128)(2,1)S(1)}, u32[]{:S(2)}) copy-start(bf16[4,3,144,896]{3,2,1,0:T(8,128)(2,1)S(1)} %maximum_select_fusion.near_ref) | copy-start | bytes 9289732
  82.9 4.5 %copy-start.23 = (f32[1792]{0:T(1024)S(1)}, f32[1792]{0:T(1024)}, u32[]{:S(2)}) copy-start(f32[1792]{0:T(1024)} %param.21) | copy-start | bytes 21508
  83.0 8.8 %copy-start.8 = (bf16[4,16,4,1792]{3,1,2,0:T(8,128)(2,1)S(1)}, bf16[4,16,4,1792]{3,1,2,0:T(8,128)(2,1)}, u32[]{:S(2)}) copy-start(bf16[4,16,4,1792]{3,1,2,0:T(8,128)(2,1)} %copy-done.7) | copy-start | bytes 2752516
  83.0 12.6 %collective-permute-start.11 = (bf16[4,3,144,896]{3,2,1,0:T(8,128)(2,1)S(1)}, bf16[4,3,144,896]{3,2,1,0:T(8,128)(2,1)}, u32[]{:S(2)}, u32[]{:S(2)}) collective-permute-start(bf16[4,3,144,896]{3,2,1,0:T(8,128)(2,1)S(1)} %maximum_select_fusion.near_ref), channel_id=1, source_target_pairs={{0,16},{16,0},{1,17},{17,1},{2,18},{18,2},{3,19},{19,3},{4,20},{20... | collective-permute-start | bytes 9289736 | tf_op jit(solution)/shard_map/ppermute | solution.py:425
  87.1 37.5 %collective-permute-start.15 = (bf16[448,896]{1,0:T(8,128)(2,1)}, bf16[448,896]{1,0:T(8,128)(2,1)}, u32[]{:S(2)}, u32[]{:S(2)}) collective-permute-start(bf16[448,896]{1,0:T(8,128)(2,1)} %maximum_select_fusion.4), channel_id=1, source_target_pairs={{0,2},{1,3},{2,0},{3,1},{4,6},{5,7},{6,4},{7,5},{8,10},{9,11},{10,... | collective-permute-start | bytes 2408456 | tf_op jit(solution)/shard_map/ppermute | solution.py:425
  88.0 41.9 %collective-permute-start.18 = (bf16[3,112,896]{2,1,0:T(8,128)(2,1)}, bf16[3,112,896]{2,1,0:T(8,128)(2,1)}, u32[]{:S(2)}, u32[]{:S(2)}) collective-permute-start(bf16[3,112,896]{2,1,0:T(8,128)(2,1)} %pad_maximum_fusion), channel_id=1, source_target_pairs={{0,4},{4,0},{8,12},{12,8},{1,5},{5,1},{9,13},{13,9},{2,6},{6,2},{1... | collective-permute-start | bytes 1806344 | tf_op jit(solution)/shard_map/ppermute | solution.py:425
  90.1 40.9 %collective-permute-start.19 = (bf16[3,112,896]{2,1,0:T(8,128)(2,1)}, bf16[3,112,896]{2,1,0:T(8,128)(2,1)}, u32[]{:S(2)}, u32[]{:S(2)}) collective-permute-start(bf16[3,112,896]{2,1,0:T(8,128)(2,1)} %pad_maximum_fusion), channel_id=1, source_target_pairs={{0,8},{4,12},{8,0},{12,4},{1,9},{5,13},{9,1},{13,5},{2,10},{6,14},... | collective-permute-start | bytes 1806344 | tf_op jit(solution)/shard_map/ppermute | solution.py:425
  108.0 25.8 %collective-permute-start.14 = (bf16[4,640,128]{2,1,0:T(8,128)(2,1)}, bf16[4,640,128]{2,1,0:T(8,128)(2,1)S(1)}, u32[]{:S(2)}, u32[]{:S(2)}) collective-permute-start(bf16[4,640,128]{2,1,0:T(8,128)(2,1)} %get-tuple-element.13), channel_id=1, source_target_pairs={{0,12},{1,13},{2,14},{3,15},{16,28},{17,29},{18,30},{19,31}} | collective-permute-start | bytes 1966088 | tf_op jit(solution)/shard_map/ppermute | solution.py:477
  110.3 23.5 %collective-permute-start.13 = (bf16[4,640,128]{2,1,0:T(8,128)(2,1)}, bf16[4,640,128]{2,1,0:T(8,128)(2,1)S(1)}, u32[]{:S(2)}, u32[]{:S(2)}) collective-permute-start(bf16[4,640,128]{2,1,0:T(8,128)(2,1)} %get-tuple-element.13), channel_id=1, source_target_pairs={{0,8},{4,12},{1,9},{5,13},{2,10},{6,14},{3,11},{7,15},{16,24},{20,... | collective-permute-start | bytes 1966088 | tf_op jit(solution)/shard_map/ppermute | solution.py:477
  124.6 18.7 %collective-permute-start.12 = (bf16[4,640,128]{2,1,0:T(8,128)(2,1)}, bf16[4,640,128]{2,1,0:T(8,128)(2,1)S(1)}, u32[]{:S(2)}, u32[]{:S(2)}) collective-permute-start(bf16[4,640,128]{2,1,0:T(8,128)(2,1)} %get-tuple-element.13), channel_id=1, source_target_pairs={{0,4},{4,8},{8,12},{1,5},{5,9},{9,13},{2,6},{6,10},{10,14},{3,7},{... | collective-permute-start | bytes 1966088 | tf_op jit(solution)/shard_map/ppermute | solution.py:477
  129.9 14.9 %collective-permute-start.16 = (bf16[112,896]{1,0:T(8,128)(2,1)S(1)}, bf16[112,896]{1,0:T(8,128)(2,1)S(1)}, u32[]{:S(2)}, u32[]{:S(2)}) collective-permute-start(bf16[112,896]{1,0:T(8,128)(2,1)S(1)} %get-tuple-element.17), channel_id=1, source_target_pairs={{0,1},{1,0},{2,3},{3,2},{4,5},{5,4},{6,7},{7,6},{8,9},{9,8},{10,11... | collective-permute-start | bytes 602120 | tf_op jit(solution)/shard_map/ppermute | solution.py:425
  131.0 18.0 %collective-permute-start.21 = (bf16[3,48,896]{2,1,0:T(8,128)(2,1)S(1)}, bf16[3,48,896]{2,1,0:T(8,128)(2,1)S(1)}, u32[]{:S(2)}, u32[]{:S(2)}) collective-permute-start(bf16[3,48,896]{2,1,0:T(8,128)(2,1)S(1)} %slice_select_fusion.6), channel_id=1, source_target_pairs={{0,8},{4,12},{8,0},{12,4},{1,9},{5,13},{9,1},{13,5},{2,10},{6,14},... | collective-permute-start | bytes 774152 | tf_op jit(solution)/shard_map/ppermute | solution.py:425
  133.7 18.2 %collective-permute-start.20 = (bf16[3,64,896]{2,1,0:T(8,128)(2,1)S(1)}, bf16[3,64,896]{2,1,0:T(8,128)(2,1)S(1)}, u32[]{:S(2)}, u32[]{:S(2)}) collective-permute-start(bf16[3,64,896]{2,1,0:T(8,128)(2,1)S(1)} %slice_select_fusion.2), channel_id=1, source_target_pairs={{0,4},{4,0},{8,12},{12,8},{1,5},{5,1},{9,13},{13,9},{2,6},{6,2},{1... | collective-permute-start | bytes 1032200 | tf_op jit(solution)/shard_map/ppermute | solution.py:425
  133.8 11.0 %collective-permute-start.17 = (bf16[112,896]{1,0:T(8,128)(2,1)S(1)}, bf16[112,896]{1,0:T(8,128)(2,1)S(1)}, u32[]{:S(2)}, u32[]{:S(2)}) collective-permute-start(bf16[112,896]{1,0:T(8,128)(2,1)S(1)} %get-tuple-element.22), channel_id=1, source_target_pairs={{0,1},{1,0},{2,3},{3,2},{4,5},{5,4},{6,7},{7,6},{8,9},{9,8},{10,11... | collective-permute-start | bytes 602120 | tf_op jit(solution)/shard_map/ppermute | solution.py:425
  143.6 8.4 %copy-start.6 = (f32[4,640,128]{2,1,0:T(8,128)}, f32[4,640,128]{2,1,0:T(8,128)S(1)}, u32[]{:S(2)}) copy-start(f32[4,640,128]{2,1,0:T(8,128)S(1)} %convert_add_fusion.prior_ref) | copy-start | bytes 3932164
  152.0 3.3 %copy-start.24 = (f32[1792]{0:T(1024)S(1)}, f32[1792]{0:T(1024)}, u32[]{:S(2)}) copy-start(f32[1792]{0:T(1024)} %param.25) | copy-start | bytes 21508
  153.9 6.2 %copy-start.5 = (bf16[4,3,112,896]{3,2,1,0:T(8,128)(2,1)}, bf16[4,3,112,896]{3,2,1,0:T(8,128)(2,1)S(1)}, u32[]{:S(2)}) copy-start(bf16[4,3,112,896]{3,2,1,0:T(8,128)(2,1)S(1)} %maximum_select_fusion.1.near_ref) | copy-start | bytes 7225348
  153.9 4.7 %collective-permute-start.22 = (bf16[4,3,112,896]{3,2,1,0:T(8,128)(2,1)S(1)}, bf16[4,3,112,896]{3,2,1,0:T(8,128)(2,1)S(1)}, u32[]{:S(2)}, u32[]{:S(2)}) collective-permute-start(bf16[4,3,112,896]{3,2,1,0:T(8,128)(2,1)S(1)} %maximum_select_fusion.1.near_ref), channel_id=1, source_target_pairs={{0,16},{16,0},{1,17},{17,1},{2,18},{18,2},{3,19},{19,3},{4,20},{20... | collective-permute-start | bytes 7225352 | tf_op jit(solution)/shard_map/ppermute | solution.py:425
  155.0 20.3 %collective-permute-start.26 = (bf16[1,336,896]{2,1,0:T(8,128)(2,1)}, bf16[1,336,896]{2,1,0:T(8,128)(2,1)}, u32[]{:S(2)}, u32[]{:S(2)}) collective-permute-start(bf16[1,336,896]{2,1,0:T(8,128)(2,1)} %slice_select_fusion), channel_id=1, source_target_pairs={{0,4},{4,0},{8,12},{12,8},{1,5},{5,1},{9,13},{13,9},{2,6},{6,2},{1... | collective-permute-start | bytes 1806344 | tf_op jit(solution)/shard_map/ppermute | solution.py:425
  155.9 23.9 %collective-permute-start.27 = (bf16[1,336,896]{2,1,0:T(8,128)(2,1)}, bf16[1,336,896]{2,1,0:T(8,128)(2,1)}, u32[]{:S(2)}, u32[]{:S(2)}) collective-permute-start(bf16[1,336,896]{2,1,0:T(8,128)(2,1)} %slice_select_fusion), channel_id=1, source_target_pairs={{0,8},{4,12},{8,0},{12,4},{1,9},{5,13},{9,1},{13,5},{2,10},{6,14},... | collective-permute-start | bytes 1806344 | tf_op jit(solution)/shard_map/ppermute | solution.py:425
  158.6 1.5 copy-start.12
  170.5 4.8 %copy-start.9 = (bf16[256,1792]{1,0:T(8,128)(2,1)S(1)}, bf16[256,1792]{1,0:T(8,128)(2,1)}, u32[]{:S(2)}) copy-start(bf16[256,1792]{1,0:T(8,128)(2,1)} %get-tuple-element.14._.x_ref) | copy-start | bytes 2752516
  173.3 32.0 %collective-permute-start.31 = (bf16[3,112,896]{2,1,0:T(8,128)(2,1)}, bf16[3,112,896]{2,1,0:T(8,128)(2,1)S(1)}, u32[]{:S(2)}, u32[]{:S(2)}) collective-permute-start(bf16[3,112,896]{2,1,0:T(8,128)(2,1)} %broadcast_select_fusion.1), channel_id=1, source_target_pairs={{0,8},{4,12},{8,0},{12,4},{1,9},{5,13},{9,1},{13,5},{2,10},{6,14},... | collective-permute-start | bytes 1806344 | tf_op jit(solution)/shard_map/ppermute | solution.py:425
  173.3 32.0 %collective-permute-start.30 = (bf16[3,112,896]{2,1,0:T(8,128)(2,1)}, bf16[3,112,896]{2,1,0:T(8,128)(2,1)S(1)}, u32[]{:S(2)}, u32[]{:S(2)}) collective-permute-start(bf16[3,112,896]{2,1,0:T(8,128)(2,1)} %broadcast_select_fusion.1), channel_id=1, source_target_pairs={{0,4},{4,0},{8,12},{12,8},{1,5},{5,1},{9,13},{13,9},{2,6},{6,2},{1... | collective-permute-start | bytes 1806344 | tf_op jit(solution)/shard_map/ppermute | solution.py:425
  175.3 30.1 %collective-permute-start.24 = (bf16[256,1792]{1,0:T(8,128)(2,1)S(1)}, bf16[256,1792]{1,0:T(8,128)(2,1)S(1)}, u32[]{:S(2)}, u32[]{:S(2)}) collective-permute-start(bf16[256,1792]{1,0:T(8,128)(2,1)S(1)} %copy-done.9), channel_id=1, source_target_pairs={{0,1},{1,0},{2,3},{3,2},{4,5},{5,4},{6,7},{7,6},{8,9},{9,8},{10,11... | collective-permute-start | bytes 2752520 | tf_op jit(solution)/shard_map/ppermute | solution.py:425
  175.3 25.9 %collective-permute-start.25 = (bf16[80,1792]{1,0:T(8,128)(2,1)}, bf16[80,1792]{1,0:T(8,128)(2,1)S(1)}, u32[]{:S(2)}, u32[]{:S(2)}) collective-permute-start(bf16[80,1792]{1,0:T(8,128)(2,1)} %get-tuple-element.15), channel_id=1, source_target_pairs={{0,5},{1,4},{2,7},{3,6},{4,9},{5,8},{6,11},{7,10},{8,13},{9,12},{1... | collective-permute-start | bytes 860168 | tf_op jit(solution)/shard_map/ppermute | solution.py:651
  179.8 28.1 %collective-permute-start.29 = (bf16[1,160,896]{2,1,0:T(8,128)(2,1)S(1)}, bf16[1,160,896]{2,1,0:T(8,128)(2,1)S(1)}, u32[]{:S(2)}, u32[]{:S(2)}) collective-permute-start(bf16[1,160,896]{2,1,0:T(8,128)(2,1)S(1)} %slice_select_fusion.5), channel_id=1, source_target_pairs={{0,8},{4,12},{8,0},{12,4},{1,9},{5,13},{9,1},{13,5},{2,10},{6,14},... | collective-permute-start | bytes 860168 | tf_op jit(solution)/shard_map/ppermute | solution.py:425
  201.2 10.1 %copy-start.21 = (bf16[80,1792]{1,0:T(8,128)(2,1)}, bf16[80,1792]{1,0:T(8,128)(2,1)S(1)}, u32[]{:S(2)}) copy-start(bf16[80,1792]{1,0:T(8,128)(2,1)S(1)} %collective-permute-done.25.halo_ref) | copy-start | bytes 860164
  201.2 9.8 %collective-permute-start.28 = (bf16[1,176,896]{2,1,0:T(8,128)(2,1)S(1)}, bf16[1,176,896]{2,1,0:T(8,128)(2,1)S(1)}, u32[]{:S(2)}, u32[]{:S(2)}) collective-permute-start(bf16[1,176,896]{2,1,0:T(8,128)(2,1)S(1)} %slice_select_fusion.4), channel_id=1, source_target_pairs={{0,4},{4,0},{8,12},{12,8},{1,5},{5,1},{9,13},{13,9},{2,6},{6,2},{1... | collective-permute-start | bytes 946184 | tf_op jit(solution)/shard_map/ppermute | solution.py:425
  205.3 0.8 copy-start.13
  205.4 1.3 copy-start.15
  206.1 4.9 %copy-start.18 = (bf16[256,1792]{1,0:T(8,128)(2,1)}, bf16[256,1792]{1,0:T(8,128)(2,1)S(1)}, u32[]{:S(2)}) copy-start(bf16[256,1792]{1,0:T(8,128)(2,1)S(1)} %collective-permute-done.24.x_ref) | copy-start | bytes 2752516
  213.0 4.8 %copy-start.2 = (bf16[4,1,336,896]{3,2,1,0:T(8,128)(2,1)}, bf16[4,1,336,896]{3,2,1,0:T(8,128)(2,1)S(1)}, u32[]{:S(2)}) copy-start(bf16[4,1,336,896]{3,2,1,0:T(8,128)(2,1)S(1)} %maximum_select_fusion.2.near_ref) | copy-start | bytes 7225348
  213.0 4.8 %collective-permute-start.32 = (bf16[4,1,336,896]{3,2,1,0:T(8,128)(2,1)S(1)}, bf16[4,1,336,896]{3,2,1,0:T(8,128)(2,1)}, u32[]{:S(2)}, u32[]{:S(2)}) collective-permute-start(bf16[4,1,336,896]{3,2,1,0:T(8,128)(2,1)S(1)} %maximum_select_fusion.2.near_ref), channel_id=1, source_target_pairs={{0,16},{16,0},{1,17},{17,1},{2,18},{18,2},{3,19},{19,3},{4,20},{20... | collective-permute-start | bytes 7225352 | tf_op jit(solution)/shard_map/ppermute | solution.py:425
  213.1 20.7 %collective-permute-start.34 = (bf16[3,112,896]{2,1,0:T(8,128)(2,1)}, bf16[3,112,896]{2,1,0:T(8,128)(2,1)}, u32[]{:S(2)}, u32[]{:S(2)}) collective-permute-start(bf16[3,112,896]{2,1,0:T(8,128)(2,1)} %broadcast_select_fusion.1), channel_id=1, source_target_pairs={{0,12},{4,8},{8,4},{12,0},{1,13},{5,9},{9,5},{13,1},{2,14},{6,10},... | collective-permute-start | bytes 1806344 | tf_op jit(solution)/shard_map/ppermute | solution.py:425
  217.8 16.0 %copy-start.14 = (bf16[3,112,896]{2,1,0:T(8,128)(2,1)S(1)}, bf16[3,112,896]{2,1,0:T(8,128)(2,1)}, u32[]{:S(2)}) copy-start(bf16[3,112,896]{2,1,0:T(8,128)(2,1)} %copy-done.13) | copy-start | bytes 1806340
  233.9 2.2 copy-start.16
  233.9 7.1 %copy-start.25 = (s32[8]{0:T(128)S(1)}, s32[8]{0:T(128)}, u32[]{:S(2)}) copy-start(s32[8]{0:T(128)} %param.20) | copy-start | bytes 100
  233.9 7.1 %copy-start.26 = (s32[8]{0:T(128)S(1)}, s32[8]{0:T(128)}, u32[]{:S(2)}) copy-start(s32[8]{0:T(128)} %param.19) | copy-start | bytes 100
  235.8 25.2 %copy-start.4 = (bf16[4,3,112,896]{3,2,1,0:T(8,128)(2,1)}, bf16[4,3,112,896]{3,2,1,0:T(8,128)(2,1)S(1)}, u32[]{:S(2)}) copy-start(bf16[4,3,112,896]{3,2,1,0:T(8,128)(2,1)S(1)} %maximum_select_fusion.3.near_ref) | copy-start | bytes 7225348
  235.8 25.2 %collective-permute-start.35 = (bf16[4,3,112,896]{3,2,1,0:T(8,128)(2,1)S(1)}, bf16[4,3,112,896]{3,2,1,0:T(8,128)(2,1)}, u32[]{:S(2)}, u32[]{:S(2)}) collective-permute-start(bf16[4,3,112,896]{3,2,1,0:T(8,128)(2,1)S(1)} %maximum_select_fusion.3.near_ref), channel_id=1, source_target_pairs={{0,16},{16,0},{1,17},{17,1},{2,18},{18,2},{3,19},{19,3},{4,20},{20... | collective-permute-start | bytes 7225352 | tf_op jit(solution)/shard_map/ppermute | solution.py:425
  236.0 25.0 %collective-permute-start.33 = (bf16[2,256,512]{2,1,0:T(8,128)(2,1)S(1)}, bf16[2,256,512]{2,1,0:T(8,128)(2,1)S(1)}, u32[]{:S(2)}, u32[]{:S(2)}) collective-permute-start(bf16[2,256,512]{2,1,0:T(8,128)(2,1)S(1)} %copy-done.16), channel_id=1, source_target_pairs={{0,1},{1,0},{2,3},{3,2},{4,5},{5,4},{6,7},{7,6},{8,9},{9,8},{10,11... | collective-permute-start | bytes 1572872 | tf_op jit(solution)/shard_map/ppermute | solution.py:425
  236.6 10.3 %collective-permute-start.23 = (bf16[80,1792]{1,0:T(8,128)(2,1)}, bf16[80,1792]{1,0:T(8,128)(2,1)}, u32[]{:S(2)}, u32[]{:S(2)}) collective-permute-start(bf16[80,1792]{1,0:T(8,128)(2,1)} %get-tuple-element.15), channel_id=1, source_target_pairs={{0,4},{4,8},{8,12},{1,5},{5,9},{9,13},{2,6},{6,10},{10,14},{3,7},{... | collective-permute-start | bytes 860168 | tf_op jit(solution)/shard_map/ppermute | solution.py:649
  268.6 28.2 %copy-start.1 = (bf16[64,4,1792]{2,1,0:T(4,128)(2,1)S(1)}, bf16[64,4,1792]{2,1,0:T(4,128)(2,1)}, u32[]{:S(2)}) copy-start(bf16[64,4,1792]{2,1,0:T(4,128)(2,1)} %param.17) | copy-start | bytes 2752516
  (1 other events, 0.8 us)

commit v16 on v12

--- a/solution.py
+++ b/solution.py
@@ -452,9 +452,12 @@
     return across(held, "seq", 1), across(held, "seq", 2)
 
 
-def from_plane(held, near_by, diagonal, over_cores, over_across=()):
+def from_plane(held, near_by, diagonal, over_cores, over_across=(), by_one_way=False):
     beside, above = near_by
-    if diagonal is None:
+    if by_one_way:
+        beside = settled(beside, diagonal)
+        opposite = across(after(above, (beside,)), "seq", 1)
+    elif diagonal is None:
         opposite = across(after(held, over_across), "seq", 3)
     else:
         half = -(-held.shape[1] // 32) * 16
@@ -657,7 +660,7 @@
     held_out_two = after(held_out_two, (residual,))
     near_by_two = neighbours(held_out_two)
     near_window = from_plane(
-        held_window, near_by_window, (residual,), (pair_rows, pair_halo, *near_by_two)
+        held_window, near_by_window, (residual,), (pair_rows, pair_halo, *near_by_two), (), True
     )
     block_start = (seq_place * rows).astype(jnp.int32)[None]
 

time: 296 us -> 295 us (level)
  starting transfers between devices: 57 us -> 52.8 us
    ppermute x31 -> x30, starting transfers between devices: 34.5 us -> 28.7 us  [across(): lax.ppermute(array, axis, [(i, i ^ bit) for i in range(lax.axis_size(axis...]
    ppermute x31 -> x30, waiting for transfers between devices: 33.7 us -> 36.2 us  [across(): lax.ppermute(array, axis, [(i, i ^ bit) for i in range(lax.axis_size(axis...]
    slice x15 -> x16, local copies, waits for them, and re-layouts: 10.4 us -> 11.1 us  [after(): lax.slice(other, (0,) * other.ndim, (1,) * other.ndim)]
  transfers between devices with their start and end apart: 38 -> 37, of which waited for: 15 -> 16; matrix products, arithmetic and copies ran while one was open for 14% -> 14% of each run, Pallas kernels for 17% -> 17%
where the time goes in v16:
time: 295 us; the launch traced here: 293 us
  waiting for transfers between devices  86.5 us (29%)
  Pallas kernels  57.8 us (20%)
  starting transfers between devices  52.8 us (18%)
  local copies, waits for them, and re-layouts  31.3 us (11%)
  other arithmetic  28.9 us (10%)
  blocking collectives  25.2 us (9%)
  between operations  10.9 us (4%)
    ppermute x30, waiting for transfers between devices, across(): lax.ppermute(array, axis, [(i, i ^ bit) for i in range(lax.axis_size(axis...  36.2 us
    ppermute x30, starting transfers between devices, across(): lax.ppermute(array, axis, [(i, i ^ bit) for i in range(lax.axis_size(axis...  28.7 us
    pallas_call x2, Pallas kernels, window_rows(): call(functools.partial(window_kernel, heads), 2, [SMEM, SMEM, *[HBM] * 5,...  28.3 us
    all_to_all x1, blocking collectives, on_device(): lax.all_to_all(result, 'tensor', split_axis=0, concat_axis=0, tiled=True)  25.2 us
    select_n x21, other arithmetic, after(): return jnp.where(zero == 0.0, array, jnp.zeros_like(array))  21.4 us
    all_to_all x1, waiting for transfers between devices, on_device(): lax.all_to_all(picked, 'tensor', split_axis=0, concat_axis=0, tiled=True)  20.9 us
    ppermute x1, waiting for transfers between devices, on_device(): lax.ppermute(tail, ('seq', 'tensor'), [(i * group_count + j, (i + 1) * gr...  15.6 us
    pallas_call x1, Pallas kernels, on_device(): call(functools.partial(linear_kernel, heads, feature_dim, kept), group_co...  12.4 us
  transfers between devices with their start and end apart: 37, of which 16 were waited for; matrix products, arithmetic and copies ran while one was open for 14% of the time, Pallas kernels for 17%

profile of v16, /device:TPU:0, one launch (start us, length us, event | category | flops | bytes accessed | tf_op | source)
XLA Modules:
  0.0 293.3 jit_solution(9389300037184142284)
XLA Ops:
  1.9 4.1 %collective-permute-start.2 = (bf16[144,896]{1,0:T(8,128)(2,1)S(1)}, bf16[144,896]{1,0:T(8,128)(2,1)S(1)}, u32[]{:S(2)}, u32[]{:S(2)}) collective-permute-start(bf16[144,896]{1,0:T(8,128)(2,1)S(1)} %pad_maximum_fusion.1), channel_id=1, source_target_pairs={{0,2},{1,3},{2,0},{3,1},{4,6},{5,7},{6,4},{7,5},{8,10},{9,11},{10,... | collective-permute-start | bytes 774152 | tf_op jit(solution)/shard_map/ppermute | solution.py:425
  6.0 1.6 collective-permute-start.1
  10.0 2.2 gather_fusion.1
  12.2 3.7 %all-to-all-start = ((bf16[8,8,4,1792]{3,2,1,0:T(4,128)(2,1)}), bf16[8,8,4,1792]{3,2,1,0:T(4,128)(2,1)S(1)}, u32[]{:S(2)}, u32[]{:S(2)}) async-start(bf16[8,8,4,1792]{3,2,1,0:T(4,128)(2,1)} %bitcast.20), calls=%async_computation | async-start | bytes 1835008 | tf_op jit(solution)/shard_map/all_to_all | solution.py:551
  18.6 3.1 %collective-permute-done = f32[3,1536]{1,0:T(4,128)S(1)} collective-permute-done((f32[3,1536]{1,0:T(4,128)S(1)}, f32[3,1536]{1,0:T(4,128)S(1)}, u32[]{:S(2)}, u32[]{:S(2)}) %collective-permute-start) | collective-permute-done | bytes 18464 | tf_op jit(solution)/shard_map/ppermute | solution.py:425
  22.8 3.5 %collective-permute-done.3 = bf16[144,896]{1,0:T(8,128)(2,1)S(1)} collective-permute-done((bf16[144,896]{1,0:T(8,128)(2,1)S(1)}, bf16[144,896]{1,0:T(8,128)(2,1)S(1)}, u32[]{:S(2)}, u32[]{:S(2)}) %collective-permute-start.3) | collective-permute-done | bytes 258080 | tf_op jit(solution)/shard_map/ppermute | solution.py:425
  27.5 1.9 all-to-all-done
  29.4 1.3 gather_fusion.2
  32.2 3.5 %all-to-all-start.1 = ((bf16[4,16,4,1792]{3,1,2,0:T(8,128)(2,1)}), bf16[4,16,4,1792]{3,1,2,0:T(8,128)(2,1)S(1)}, u32[]{:S(2)}, u32[]{:S(2)}) async-start(bf16[4,16,4,1792]{3,1,2,0:T(8,128)(2,1)} %copy.47), calls=%async_computation.1 | async-start | bytes 1835008 | tf_op jit(solution)/shard_map/all_to_all | solution.py:558
  35.7 1.1 collective-permute-start.8
  38.8 1.6 select_bitcast_fusion.1
  40.5 2.9 collective-permute-start.5
  43.4 20.9 %all-to-all-done.1 = bf16[4,16,4,1792]{3,1,2,0:T(8,128)(2,1)S(1)} async-done(((bf16[4,16,4,1792]{3,1,2,0:T(8,128)(2,1)}), bf16[4,16,4,1792]{3,1,2,0:T(8,128)(2,1)S(1)}, u32[]{:S(2)}, u32[]{:S(2)}) %all-to-all-start.1) | async-done | bytes 917536 | tf_op jit(solution)/shard_map/all_to_all | solution.py:558
  65.4 1.1 collective-permute-start.9
  66.5 1.0 slice_select_fusion.3
  68.2 2.0 collective-permute-start.6
  70.2 4.9 %collective-permute-done.4 = bf16[112,896]{1,0:T(8,128)(2,1)S(1)} collective-permute-done((bf16[112,896]{1,0:T(8,128)(2,1)}, bf16[112,896]{1,0:T(8,128)(2,1)S(1)}, u32[]{:S(2)}, u32[]{:S(2)}) %collective-permute-start.4) | collective-permute-done | bytes 200736 | tf_op jit(solution)/shard_map/ppermute | solution.py:425
  75.1 2.1 collective-permute-done.6
  77.3 1.8 pad_maximum_fusion
  79.1 1.2 slice.107
  81.0 1.7 maximum_select_fusion.near_ref
  82.9 2.1 constant_dynamic-slice_fusion
  86.0 1.0 maximum_select_fusion.4
  87.9 1.4 collective-permute-start.18
  89.9 1.7 collective-permute-start.19
  91.6 1.4 copy.48
  93.0 2.4 reshape.495.x_ref
  95.3 12.4 %linear_rows.1 = (f32[4,256,512]{2,1,0:T(8,128)}, bf16[4,256,128]{2,1,0:T(8,128)(2,1)}, bf16[4,640,128]{2,1,0:T(8,128)(2,1)}) custom-call(s32[5]{0:T(128)} %pad_add_fusion.place_ref, bf16[256,1792]{1,0:T(8,128)(2,1)} %reshape.495.x_ref, f32[1,1792]{1,0:T(1,128)} %broadcast_in_dim.122.gain_ref, bf16[1,4,112,1792]{3,2,1,0:T(8,128)(2,1)} %bitcast.102, ...), custom_call_target="tpu_custom_call" | custom-call | tf_op jit(solution)/shard_map/linear_rows/pallas_call | solution.py:579
  107.8 2.3 collective-permute-start.14
  110.1 1.3 collective-permute-start.13
  111.4 1.2 slice.83
  113.2 11.3 %collective-permute-done.15 = bf16[448,896]{1,0:T(8,128)(2,1)} collective-permute-done((bf16[448,896]{1,0:T(8,128)(2,1)}, bf16[448,896]{1,0:T(8,128)(2,1)}, u32[]{:S(2)}, u32[]{:S(2)}) %collective-permute-start.15) | collective-permute-done | bytes 802848 | tf_op jit(solution)/shard_map/ppermute | solution.py:425
  124.5 3.5 %collective-permute-start.12 = (bf16[4,640,128]{2,1,0:T(8,128)(2,1)}, bf16[4,640,128]{2,1,0:T(8,128)(2,1)S(1)}, u32[]{:S(2)}, u32[]{:S(2)}) collective-permute-start(bf16[4,640,128]{2,1,0:T(8,128)(2,1)} %get-tuple-element.13), channel_id=1, source_target_pairs={{0,4},{4,8},{8,12},{1,5},{5,9},{9,13},{2,6},{6,10},{10,14},{3,7},{... | collective-permute-start | bytes 1966088 | tf_op jit(solution)/shard_map/ppermute | solution.py:477
  128.0 1.2 select_bitcast_fusion
  130.9 1.7 collective-permute-start.21
  133.7 2.0 collective-permute-start.17
  135.8 7.4 %collective-permute-done.12 = bf16[4,640,128]{2,1,0:T(8,128)(2,1)S(1)} collective-permute-done((bf16[4,640,128]{2,1,0:T(8,128)(2,1)}, bf16[4,640,128]{2,1,0:T(8,128)(2,1)S(1)}, u32[]{:S(2)}, u32[]{:S(2)}) %collective-permute-start.12) | collective-permute-done | bytes 655392 | tf_op jit(solution)/shard_map/ppermute | solution.py:477
  146.6 2.3 collective-permute-done.21
  148.9 2.9 collective-permute-done.20
  151.9 1.9 maximum_select_fusion.1.near_ref
  153.9 1.0 slice_select_fusion
  155.2 1.7 collective-permute-start.29
  157.4 1.0 collective-permute-done.22.far_ref
  158.4 1.5 copy-done.11
  159.9 10.5 %linear_out.1 = (bf16[256,1792]{1,0:T(8,128)(2,1)}, bf16[256,1792]{1,0:T(8,128)(2,1)}, bf16[80,1792]{1,0:T(8,128)(2,1)}) custom-call(s32[5]{0:T(128)} %pad_add_fusion.place_ref, f32[4,256,512]{2,1,0:T(8,128)} %get-tuple-element.11.num_ref, bf16[4,256,128]{2,1,0:T(8,128)(2,1)} %get-tuple-element.12.q_ref, bf16[128,1024]{1,0:T(8,128)(2,1)} %constant.130.clone.first_ref, ...), custom_call_target="tpu_custom_call" | custom-call | tf_op jit(solution)/shard_map/linear_out/pallas_call | solution.py:619
  170.4 1.2 slice.92
  173.3 1.7 collective-permute-start.27
  175.0 1.1 broadcast_select_fusion.2
  177.3 2.0 broadcast_select_fusion.1
  179.3 5.3 %collective-permute-start.25 = (bf16[80,1792]{1,0:T(8,128)(2,1)}, bf16[80,1792]{1,0:T(8,128)(2,1)S(1)}, u32[]{:S(2)}, u32[]{:S(2)}) collective-permute-start(bf16[80,1792]{1,0:T(8,128)(2,1)} %get-tuple-element.15), channel_id=1, source_target_pairs={{0,5},{1,4},{2,7},{3,6},{4,9},{5,8},{6,11},{7,10},{8,13},{9,12},{1... | collective-permute-start | bytes 860168 | tf_op jit(solution)/shard_map/ppermute | solution.py:651
  185.5 15.6 %collective-permute-done.25.halo_ref = bf16[80,1792]{1,0:T(8,128)(2,1)S(1)} collective-permute-done((bf16[80,1792]{1,0:T(8,128)(2,1)}, bf16[80,1792]{1,0:T(8,128)(2,1)S(1)}, u32[]{:S(2)}, u32[]{:S(2)}) %collective-permute-start.25) | collective-permute-done | bytes 286752 | tf_op jit(solution)/shard_map/ppermute | solution.py:651
  205.9 2.2 collective-permute-done.30
  208.1 2.0 maximum_select_fusion.2.near_ref
  210.2 1.4 collective-permute-start.33
  212.6 2.4 collective-permute-done.31.far_ref
  214.9 14.2 %window_rows.2._ = bf16[2,256,512]{2,1,0:T(8,128)(2,1)} custom-call(s32[5]{0:T(128)} %pad_add_fusion.place_ref, s32[1]{0:T(128)} %bitcast.2.first_ref, bf16[256,1792]{1,0:T(8,128)(2,1)} %copy-done.16, bf16[80,1792]{1,0:T(8,128)(2,1)} %copy-done.21, bf16[3,4,112,1792]{3,2,1,0:T(8,128)(2,1)} %bitcast.91, bf16[4,1,336,896]{3,2,1,0:T(8,128)(2,1)} %copy-done.2, ...), custom_call_target="tpu_custom_call" | custom-call | tf_op jit(solution)/shard_map/window_rows/pallas_call | solution.py:668
  229.1 1.2 slice.123
  230.9 1.9 maximum_select_fusion.3.near_ref
  233.0 4.4 %collective-permute-start.23 = (bf16[80,1792]{1,0:T(8,128)(2,1)}, bf16[80,1792]{1,0:T(8,128)(2,1)}, u32[]{:S(2)}, u32[]{:S(2)}) collective-permute-start(bf16[80,1792]{1,0:T(8,128)(2,1)} %get-tuple-element.15), channel_id=1, source_target_pairs={{0,4},{4,8},{8,12},{1,5},{5,9},{9,13},{2,6},{6,10},{10,14},{3,7},{... | collective-permute-start | bytes 860168 | tf_op jit(solution)/shard_map/ppermute | solution.py:649
  238.8 4.5 %collective-permute-done.23.halo_ref = bf16[80,1792]{1,0:T(8,128)(2,1)} collective-permute-done((bf16[80,1792]{1,0:T(8,128)(2,1)}, bf16[80,1792]{1,0:T(8,128)(2,1)}, u32[]{:S(2)}, u32[]{:S(2)}) %collective-permute-start.23) | collective-permute-done | bytes 286752 | tf_op jit(solution)/shard_map/ppermute | solution.py:649
  243.3 14.1 %window_rows.3.mixed_ref = bf16[2,256,512]{2,1,0:T(8,128)(2,1)} custom-call(s32[5]{0:T(128)} %pad_add_fusion.place_ref, s32[1]{0:T(128)} %bitcast.2.first_ref, bf16[256,1792]{1,0:T(8,128)(2,1)} %get-tuple-element.14._.x_ref, bf16[80,1792]{1,0:T(8,128)(2,1)} %collective-permute-done.23.halo_ref, bf16[3,4,112,1792]{3,2,1,0:T(8,128)(2,1)} %bitcast.92, ...), custom_call_target="tpu_custom_call" | custom-call | tf_op jit(solution)/shard_map/window_rows/pallas_call | solution.py:668
  258.3 6.7 %window_out.1 = bf16[256,1792]{1,0:T(8,128)(2,1)} custom-call(s32[5]{0:T(128)} %pad_add_fusion.place_ref, s32[1]{0:T(128)} %bitcast.1.live_ref, bf16[2,256,512]{2,1,0:T(8,128)(2,1)} %window_rows.3.mixed_ref, bf16[2,256,512]{2,1,0:T(8,128)(2,1)} %copy-done.19, bf16[1,4,112,1792]{3,2,1,0:T(8,128)(2,1)} %bitcast.106, bf16[4,3,112,896]{3,2,1,0:T(8,128)(2,1)} %copy-done.4, ...), custom_call_target="tpu_custom_call" | custom-call | tf_op jit(solution)/shard_map/window_out/pallas_call | solution.py:693
  265.0 1.9 reshape.501
  267.2 25.2 %all_to_all.15 = bf16[4,16,4,1792]{3,2,1,0:T(4,128)(2,1)S(1)} all-to-all(bf16[4,16,4,1792]{3,2,1,0:T(4,128)(2,1)S(1)} %bitcast.96), channel_id=1, replica_groups=mesh['dp'=2,'seq'=4,'tensor'=4] {'tensor'}, dimensions={0} | all-to-all | bytes 1835008 | tf_op jit(solution)/shard_map/all_to_all | solution.py:714
  (160 shorter events, 29.1 us)
Async XLA Ops:
  0.0 9.9 %copy-start = (bf16[64,4,1792]{2,1,0:T(4,128)(2,1)S(1)}, bf16[64,4,1792]{2,1,0:T(4,128)(2,1)}, u32[]{:S(2)}) copy-start(bf16[64,4,1792]{2,1,0:T(4,128)(2,1)} %param.17) | copy-start | bytes 2752516
  0.9 15.0 %copy-start.22 = (f32[3,3,448]{2,1,0:T(4,128)S(1)}, f32[3,3,448]{2,1,0:T(4,128)}, u32[]{:S(2)}) copy-start(f32[3,3,448]{2,1,0:T(4,128)} %param.27) | copy-start | bytes 48388
  1.9 16.0 %collective-permute-start.2 = (bf16[144,896]{1,0:T(8,128)(2,1)S(1)}, bf16[144,896]{1,0:T(8,128)(2,1)S(1)}, u32[]{:S(2)}, u32[]{:S(2)}) collective-permute-start(bf16[144,896]{1,0:T(8,128)(2,1)S(1)} %pad_maximum_fusion.1), channel_id=1, source_target_pairs={{0,2},{1,3},{2,0},{3,1},{4,6},{5,7},{6,4},{7,5},{8,10},{9,11},{10,... | collective-permute-start | bytes 774152 | tf_op jit(solution)/shard_map/ppermute | solution.py:425
  6.0 16.8 %collective-permute-start.1 = (bf16[144,896]{1,0:T(8,128)(2,1)S(1)}, bf16[144,896]{1,0:T(8,128)(2,1)S(1)}, u32[]{:S(2)}, u32[]{:S(2)}) collective-permute-start(bf16[144,896]{1,0:T(8,128)(2,1)S(1)} %pad_maximum_fusion.1), channel_id=1, source_target_pairs={{0,1},{1,0},{2,3},{3,2},{4,5},{5,4},{6,7},{7,6},{8,9},{9,8},{10,11... | collective-permute-start | bytes 774152 | tf_op jit(solution)/shard_map/ppermute | solution.py:425
  12.2 17.2 %all-to-all-start = ((bf16[8,8,4,1792]{3,2,1,0:T(4,128)(2,1)}), bf16[8,8,4,1792]{3,2,1,0:T(4,128)(2,1)S(1)}, u32[]{:S(2)}, u32[]{:S(2)}) async-start(bf16[8,8,4,1792]{3,2,1,0:T(4,128)(2,1)} %bitcast.20), calls=%async_computation | async-start | bytes 1835008 | tf_op jit(solution)/shard_map/all_to_all | solution.py:551
  16.6 5.0 %collective-permute-start = (f32[3,1536]{1,0:T(4,128)S(1)}, f32[3,1536]{1,0:T(4,128)S(1)}, u32[]{:S(2)}, u32[]{:S(2)}) collective-permute-start(f32[3,1536]{1,0:T(4,128)S(1)} %reshape.485), channel_id=1, source_target_pairs={{0,2},{1,3},{2,0},{3,1},{4,6},{5,7},{6,4},{7,5},{8,10},{9,11},{10,... | collective-permute-start | bytes 55304 | tf_op jit(solution)/shard_map/ppermute | solution.py:425
  17.9 8.4 %collective-permute-start.3 = (bf16[144,896]{1,0:T(8,128)(2,1)S(1)}, bf16[144,896]{1,0:T(8,128)(2,1)S(1)}, u32[]{:S(2)}, u32[]{:S(2)}) collective-permute-start(bf16[144,896]{1,0:T(8,128)(2,1)S(1)} %collective-permute-done.2), channel_id=1, source_target_pairs={{0,1},{1,0},{2,3},{3,2},{4,5},{5,4},{6,7},{7,6},{8,9},{9,8},{10,11... | collective-permute-start | bytes 774152 | tf_op jit(solution)/shard_map/ppermute | solution.py:425
  21.7 9.4 %copy-start.20 = (f32[2,3,1536]{2,1,0:T(4,128)}, f32[2,3,1536]{2,1,0:T(4,128)S(1)}, u32[]{:S(2)}) copy-start(f32[2,3,1536]{2,1,0:T(4,128)S(1)} %pad_maximum_fusion.2.tap_ref) | copy-start | bytes 110596
  26.4 10.4 %copy-start.9 = (bf16[3,144,896]{2,1,0:T(8,128)(2,1)}, bf16[3,144,896]{2,1,0:T(8,128)(2,1)S(1)}, u32[]{:S(2)}) copy-start(bf16[3,144,896]{2,1,0:T(8,128)(2,1)S(1)} %maximum_select_fusion.5) | copy-start | bytes 2322436
  32.2 32.1 %all-to-all-start.1 = ((bf16[4,16,4,1792]{3,1,2,0:T(8,128)(2,1)}), bf16[4,16,4,1792]{3,1,2,0:T(8,128)(2,1)S(1)}, u32[]{:S(2)}, u32[]{:S(2)}) async-start(bf16[4,16,4,1792]{3,1,2,0:T(8,128)(2,1)} %copy.47), calls=%async_computation.1 | async-start | bytes 1835008 | tf_op jit(solution)/shard_map/all_to_all | solution.py:558
  35.7 29.7 %collective-permute-start.8 = (bf16[3,144,896]{2,1,0:T(8,128)(2,1)S(1)}, bf16[3,144,896]{2,1,0:T(8,128)(2,1)S(1)}, u32[]{:S(2)}, u32[]{:S(2)}) collective-permute-start(bf16[3,144,896]{2,1,0:T(8,128)(2,1)S(1)} %maximum_select_fusion.5), channel_id=1, source_target_pairs={{0,8},{4,12},{8,0},{12,4},{1,9},{5,13},{9,1},{13,5},{2,10},{6,14},... | collective-permute-start | bytes 2322440 | tf_op jit(solution)/shard_map/ppermute | solution.py:425
  36.8 29.7 %collective-permute-start.7 = (bf16[3,144,896]{2,1,0:T(8,128)(2,1)S(1)}, bf16[3,144,896]{2,1,0:T(8,128)(2,1)}, u32[]{:S(2)}, u32[]{:S(2)}) collective-permute-start(bf16[3,144,896]{2,1,0:T(8,128)(2,1)S(1)} %maximum_select_fusion.5), channel_id=1, source_target_pairs={{0,4},{4,0},{8,12},{12,8},{1,5},{5,1},{9,13},{13,9},{2,6},{6,2},{1... | collective-permute-start | bytes 2322440 | tf_op jit(solution)/shard_map/ppermute | solution.py:425
  40.5 27.8 %collective-permute-start.5 = (bf16[112,896]{1,0:T(8,128)(2,1)}, bf16[112,896]{1,0:T(8,128)(2,1)}, u32[]{:S(2)}, u32[]{:S(2)}) collective-permute-start(bf16[112,896]{1,0:T(8,128)(2,1)} %select_bitcast_fusion.1), channel_id=1, source_target_pairs={{0,2},{1,3},{2,0},{3,1},{4,6},{5,7},{6,4},{7,5},{8,10},{9,11},{10,... | collective-permute-start | bytes 602120 | tf_op jit(solution)/shard_map/ppermute | solution.py:425
  64.2 16.8 %copy-start.7 = (bf16[4,16,4,1792]{3,1,2,0:T(8,128)(2,1)}, bf16[4,16,4,1792]{3,1,2,0:T(8,128)(2,1)S(1)}, u32[]{:S(2)}) copy-start(bf16[4,16,4,1792]{3,1,2,0:T(8,128)(2,1)S(1)} %all-to-all-done.1) | copy-start | bytes 2752516
  64.2 16.8 %copy-start.10 = (bf16[3,144,896]{2,1,0:T(8,128)(2,1)S(1)}, bf16[3,144,896]{2,1,0:T(8,128)(2,1)}, u32[]{:S(2)}) copy-start(bf16[3,144,896]{2,1,0:T(8,128)(2,1)} %copy-done.9) | copy-start | bytes 2322436
  65.4 15.6 %copy-start.15 = (bf16[3,144,896]{2,1,0:T(8,128)(2,1)}, bf16[3,144,896]{2,1,0:T(8,128)(2,1)S(1)}, u32[]{:S(2)}) copy-start(bf16[3,144,896]{2,1,0:T(8,128)(2,1)S(1)} %collective-permute-done.8) | copy-start | bytes 2322436
  65.4 15.4 %collective-permute-start.9 = (bf16[3,80,896]{2,1,0:T(8,128)(2,1)S(1)}, bf16[3,80,896]{2,1,0:T(8,128)(2,1)S(1)}, u32[]{:S(2)}, u32[]{:S(2)}) collective-permute-start(bf16[3,80,896]{2,1,0:T(8,128)(2,1)S(1)} %slice_select_fusion.1), channel_id=1, source_target_pairs={{0,4},{4,0},{8,12},{12,8},{1,5},{5,1},{9,13},{13,9},{2,6},{6,2},{1... | collective-permute-start | bytes 1290248 | tf_op jit(solution)/shard_map/ppermute | solution.py:425
  67.5 13.3 %collective-permute-start.10 = (bf16[3,64,896]{2,1,0:T(8,128)(2,1)S(1)}, bf16[3,64,896]{2,1,0:T(8,128)(2,1)S(1)}, u32[]{:S(2)}, u32[]{:S(2)}) collective-permute-start(bf16[3,64,896]{2,1,0:T(8,128)(2,1)S(1)} %slice_select_fusion.3), channel_id=1, source_target_pairs={{0,8},{4,12},{8,0},{12,4},{1,9},{5,13},{9,1},{13,5},{2,10},{6,14},... | collective-permute-start | bytes 1032200 | tf_op jit(solution)/shard_map/ppermute | solution.py:425
  68.2 6.9 %collective-permute-start.4 = (bf16[112,896]{1,0:T(8,128)(2,1)}, bf16[112,896]{1,0:T(8,128)(2,1)S(1)}, u32[]{:S(2)}, u32[]{:S(2)}) collective-permute-start(bf16[112,896]{1,0:T(8,128)(2,1)} %select_bitcast_fusion.1), channel_id=1, source_target_pairs={{0,1},{1,0},{2,3},{3,2},{4,5},{5,4},{6,7},{7,6},{8,9},{9,8},{10,11... | collective-permute-start | bytes 602120 | tf_op jit(solution)/shard_map/ppermute | solution.py:425
  68.2 9.1 %collective-permute-start.6 = (bf16[112,896]{1,0:T(8,128)(2,1)}, bf16[112,896]{1,0:T(8,128)(2,1)S(1)}, u32[]{:S(2)}, u32[]{:S(2)}) collective-permute-start(bf16[112,896]{1,0:T(8,128)(2,1)} %collective-permute-done.5), channel_id=1, source_target_pairs={{0,1},{1,0},{2,3},{3,2},{4,5},{5,4},{6,7},{7,6},{8,9},{9,8},{10,11... | collective-permute-start | bytes 602120 | tf_op jit(solution)/shard_map/ppermute | solution.py:425
  82.8 10.2 %copy-start.3 = (bf16[4,3,144,896]{3,2,1,0:T(8,128)(2,1)}, bf16[4,3,144,896]{3,2,1,0:T(8,128)(2,1)S(1)}, u32[]{:S(2)}) copy-start(bf16[4,3,144,896]{3,2,1,0:T(8,128)(2,1)S(1)} %maximum_select_fusion.near_ref) | copy-start | bytes 9289732
  82.8 4.5 %copy-start.23 = (f32[1792]{0:T(1024)S(1)}, f32[1792]{0:T(1024)}, u32[]{:S(2)}) copy-start(f32[1792]{0:T(1024)} %param.21) | copy-start | bytes 21508
  82.8 8.7 %copy-start.8 = (bf16[4,16,4,1792]{3,1,2,0:T(8,128)(2,1)S(1)}, bf16[4,16,4,1792]{3,1,2,0:T(8,128)(2,1)}, u32[]{:S(2)}) copy-start(bf16[4,16,4,1792]{3,1,2,0:T(8,128)(2,1)} %copy-done.7) | copy-start | bytes 2752516
  82.8 12.5 %collective-permute-start.11 = (bf16[4,3,144,896]{3,2,1,0:T(8,128)(2,1)S(1)}, bf16[4,3,144,896]{3,2,1,0:T(8,128)(2,1)}, u32[]{:S(2)}, u32[]{:S(2)}) collective-permute-start(bf16[4,3,144,896]{3,2,1,0:T(8,128)(2,1)S(1)} %maximum_select_fusion.near_ref), channel_id=1, source_target_pairs={{0,16},{16,0},{1,17},{17,1},{2,18},{18,2},{3,19},{19,3},{4,20},{20... | collective-permute-start | bytes 9289736 | tf_op jit(solution)/shard_map/ppermute | solution.py:425
  87.0 37.5 %collective-permute-start.15 = (bf16[448,896]{1,0:T(8,128)(2,1)}, bf16[448,896]{1,0:T(8,128)(2,1)}, u32[]{:S(2)}, u32[]{:S(2)}) collective-permute-start(bf16[448,896]{1,0:T(8,128)(2,1)} %maximum_select_fusion.4), channel_id=1, source_target_pairs={{0,2},{1,3},{2,0},{3,1},{4,6},{5,7},{6,4},{7,5},{8,10},{9,11},{10,... | collective-permute-start | bytes 2408456 | tf_op jit(solution)/shard_map/ppermute | solution.py:425
  87.9 41.9 %collective-permute-start.18 = (bf16[3,112,896]{2,1,0:T(8,128)(2,1)}, bf16[3,112,896]{2,1,0:T(8,128)(2,1)}, u32[]{:S(2)}, u32[]{:S(2)}) collective-permute-start(bf16[3,112,896]{2,1,0:T(8,128)(2,1)} %pad_maximum_fusion), channel_id=1, source_target_pairs={{0,4},{4,0},{8,12},{12,8},{1,5},{5,1},{9,13},{13,9},{2,6},{6,2},{1... | collective-permute-start | bytes 1806344 | tf_op jit(solution)/shard_map/ppermute | solution.py:425
  89.9 41.0 %collective-permute-start.19 = (bf16[3,112,896]{2,1,0:T(8,128)(2,1)}, bf16[3,112,896]{2,1,0:T(8,128)(2,1)}, u32[]{:S(2)}, u32[]{:S(2)}) collective-permute-start(bf16[3,112,896]{2,1,0:T(8,128)(2,1)} %pad_maximum_fusion), channel_id=1, source_target_pairs={{0,8},{4,12},{8,0},{12,4},{1,9},{5,13},{9,1},{13,5},{2,10},{6,14},... | collective-permute-start | bytes 1806344 | tf_op jit(solution)/shard_map/ppermute | solution.py:425
  107.8 25.9 %collective-permute-start.14 = (bf16[4,640,128]{2,1,0:T(8,128)(2,1)}, bf16[4,640,128]{2,1,0:T(8,128)(2,1)S(1)}, u32[]{:S(2)}, u32[]{:S(2)}) collective-permute-start(bf16[4,640,128]{2,1,0:T(8,128)(2,1)} %get-tuple-element.13), channel_id=1, source_target_pairs={{0,12},{1,13},{2,14},{3,15},{16,28},{17,29},{18,30},{19,31}} | collective-permute-start | bytes 1966088 | tf_op jit(solution)/shard_map/ppermute | solution.py:477
  110.1 23.6 %collective-permute-start.13 = (bf16[4,640,128]{2,1,0:T(8,128)(2,1)}, bf16[4,640,128]{2,1,0:T(8,128)(2,1)S(1)}, u32[]{:S(2)}, u32[]{:S(2)}) collective-permute-start(bf16[4,640,128]{2,1,0:T(8,128)(2,1)} %get-tuple-element.13), channel_id=1, source_target_pairs={{0,8},{4,12},{1,9},{5,13},{2,10},{6,14},{3,11},{7,15},{16,24},{20,... | collective-permute-start | bytes 1966088 | tf_op jit(solution)/shard_map/ppermute | solution.py:477
  124.5 18.7 %collective-permute-start.12 = (bf16[4,640,128]{2,1,0:T(8,128)(2,1)}, bf16[4,640,128]{2,1,0:T(8,128)(2,1)S(1)}, u32[]{:S(2)}, u32[]{:S(2)}) collective-permute-start(bf16[4,640,128]{2,1,0:T(8,128)(2,1)} %get-tuple-element.13), channel_id=1, source_target_pairs={{0,4},{4,8},{8,12},{1,5},{5,9},{9,13},{2,6},{6,10},{10,14},{3,7},{... | collective-permute-start | bytes 1966088 | tf_op jit(solution)/shard_map/ppermute | solution.py:477
  129.8 14.8 %collective-permute-start.16 = (bf16[112,896]{1,0:T(8,128)(2,1)S(1)}, bf16[112,896]{1,0:T(8,128)(2,1)S(1)}, u32[]{:S(2)}, u32[]{:S(2)}) collective-permute-start(bf16[112,896]{1,0:T(8,128)(2,1)S(1)} %get-tuple-element.17), channel_id=1, source_target_pairs={{0,1},{1,0},{2,3},{3,2},{4,5},{5,4},{6,7},{7,6},{8,9},{9,8},{10,11... | collective-permute-start | bytes 602120 | tf_op jit(solution)/shard_map/ppermute | solution.py:425
  130.9 18.0 %collective-permute-start.21 = (bf16[3,48,896]{2,1,0:T(8,128)(2,1)S(1)}, bf16[3,48,896]{2,1,0:T(8,128)(2,1)S(1)}, u32[]{:S(2)}, u32[]{:S(2)}) collective-permute-start(bf16[3,48,896]{2,1,0:T(8,128)(2,1)S(1)} %slice_select_fusion.4), channel_id=1, source_target_pairs={{0,8},{4,12},{8,0},{12,4},{1,9},{5,13},{9,1},{13,5},{2,10},{6,14},... | collective-permute-start | bytes 774152 | tf_op jit(solution)/shard_map/ppermute | solution.py:425
  133.6 18.1 %collective-permute-start.20 = (bf16[3,64,896]{2,1,0:T(8,128)(2,1)S(1)}, bf16[3,64,896]{2,1,0:T(8,128)(2,1)S(1)}, u32[]{:S(2)}, u32[]{:S(2)}) collective-permute-start(bf16[3,64,896]{2,1,0:T(8,128)(2,1)S(1)} %slice_select_fusion.2), channel_id=1, source_target_pairs={{0,4},{4,0},{8,12},{12,8},{1,5},{5,1},{9,13},{13,9},{2,6},{6,2},{1... | collective-permute-start | bytes 1032200 | tf_op jit(solution)/shard_map/ppermute | solution.py:425
  133.7 10.9 %collective-permute-start.17 = (bf16[112,896]{1,0:T(8,128)(2,1)S(1)}, bf16[112,896]{1,0:T(8,128)(2,1)S(1)}, u32[]{:S(2)}, u32[]{:S(2)}) collective-permute-start(bf16[112,896]{1,0:T(8,128)(2,1)S(1)} %get-tuple-element.22), channel_id=1, source_target_pairs={{0,1},{1,0},{2,3},{3,2},{4,5},{5,4},{6,7},{7,6},{8,9},{9,8},{10,11... | collective-permute-start | bytes 602120 | tf_op jit(solution)/shard_map/ppermute | solution.py:425
  143.4 8.4 %copy-start.6 = (f32[4,640,128]{2,1,0:T(8,128)}, f32[4,640,128]{2,1,0:T(8,128)S(1)}, u32[]{:S(2)}) copy-start(f32[4,640,128]{2,1,0:T(8,128)S(1)} %convert_add_fusion.prior_ref) | copy-start | bytes 3932164
  151.9 5.0 %copy-start.24 = (f32[1792]{0:T(1024)S(1)}, f32[1792]{0:T(1024)}, u32[]{:S(2)}) copy-start(f32[1792]{0:T(1024)} %param.25) | copy-start | bytes 21508
  153.8 6.2 %copy-start.5 = (bf16[4,3,112,896]{3,2,1,0:T(8,128)(2,1)}, bf16[4,3,112,896]{3,2,1,0:T(8,128)(2,1)S(1)}, u32[]{:S(2)}) copy-start(bf16[4,3,112,896]{3,2,1,0:T(8,128)(2,1)S(1)} %maximum_select_fusion.1.near_ref) | copy-start | bytes 7225348
  153.8 4.7 %collective-permute-start.22 = (bf16[4,3,112,896]{3,2,1,0:T(8,128)(2,1)S(1)}, bf16[4,3,112,896]{3,2,1,0:T(8,128)(2,1)S(1)}, u32[]{:S(2)}, u32[]{:S(2)}) collective-permute-start(bf16[4,3,112,896]{3,2,1,0:T(8,128)(2,1)S(1)} %maximum_select_fusion.1.near_ref), channel_id=1, source_target_pairs={{0,16},{16,0},{1,17},{17,1},{2,18},{18,2},{3,19},{19,3},{4,20},{20... | collective-permute-start | bytes 7225352 | tf_op jit(solution)/shard_map/ppermute | solution.py:425
  154.9 20.1 %collective-permute-start.28 = (bf16[1,336,896]{2,1,0:T(8,128)(2,1)}, bf16[1,336,896]{2,1,0:T(8,128)(2,1)}, u32[]{:S(2)}, u32[]{:S(2)}) collective-permute-start(bf16[1,336,896]{2,1,0:T(8,128)(2,1)} %slice_select_fusion), channel_id=1, source_target_pairs={{0,4},{4,0},{8,12},{12,8},{1,5},{5,1},{9,13},{13,9},{2,6},{6,2},{1... | collective-permute-start | bytes 1806344 | tf_op jit(solution)/shard_map/ppermute | solution.py:425
  155.2 22.1 %collective-permute-start.29 = (bf16[1,336,896]{2,1,0:T(8,128)(2,1)}, bf16[1,336,896]{2,1,0:T(8,128)(2,1)}, u32[]{:S(2)}, u32[]{:S(2)}) collective-permute-start(bf16[1,336,896]{2,1,0:T(8,128)(2,1)} %slice_select_fusion), channel_id=1, source_target_pairs={{0,8},{4,12},{8,0},{12,4},{1,9},{5,13},{9,1},{13,5},{2,10},{6,14},... | collective-permute-start | bytes 1806344 | tf_op jit(solution)/shard_map/ppermute | solution.py:425
  158.4 1.5 copy-start.11
  173.0 28.7 %collective-permute-start.26 = (bf16[3,112,896]{2,1,0:T(8,128)(2,1)}, bf16[3,112,896]{2,1,0:T(8,128)(2,1)S(1)}, u32[]{:S(2)}, u32[]{:S(2)}) collective-permute-start(bf16[3,112,896]{2,1,0:T(8,128)(2,1)} %broadcast_select_fusion.3), channel_id=1, source_target_pairs={{0,4},{4,0},{8,12},{12,8},{1,5},{5,1},{9,13},{13,9},{2,6},{6,2},{1... | collective-permute-start | bytes 1806344 | tf_op jit(solution)/shard_map/ppermute | solution.py:425
  173.3 29.6 %collective-permute-start.27 = (bf16[3,112,896]{2,1,0:T(8,128)(2,1)}, bf16[3,112,896]{2,1,0:T(8,128)(2,1)S(1)}, u32[]{:S(2)}, u32[]{:S(2)}) collective-permute-start(bf16[3,112,896]{2,1,0:T(8,128)(2,1)} %broadcast_select_fusion.3), channel_id=1, source_target_pairs={{0,8},{4,12},{8,0},{12,4},{1,9},{5,13},{9,1},{13,5},{2,10},{6,14},... | collective-permute-start | bytes 1806344 | tf_op jit(solution)/shard_map/ppermute | solution.py:425
  175.0 29.0 %collective-permute-start.24 = (bf16[256,1792]{1,0:T(8,128)(2,1)}, bf16[256,1792]{1,0:T(8,128)(2,1)S(1)}, u32[]{:S(2)}, u32[]{:S(2)}) collective-permute-start(bf16[256,1792]{1,0:T(8,128)(2,1)} %get-tuple-element.14._.x_ref), channel_id=1, source_target_pairs={{0,1},{1,0},{2,3},{3,2},{4,5},{5,4},{6,7},{7,6},{8,9},{9,8},{10,11... | collective-permute-start | bytes 2752520 | tf_op jit(solution)/shard_map/ppermute | solution.py:425
  176.1 31.9 %copy-start.12 = (bf16[1,336,896]{2,1,0:T(8,128)(2,1)}, bf16[1,336,896]{2,1,0:T(8,128)(2,1)S(1)}, u32[]{:S(2)}) copy-start(bf16[1,336,896]{2,1,0:T(8,128)(2,1)S(1)} %broadcast_select_fusion.2) | copy-start | bytes 1806340
  179.2 28.8 %collective-permute-start.30 = (bf16[1,336,896]{2,1,0:T(8,128)(2,1)}, bf16[1,336,896]{2,1,0:T(8,128)(2,1)}, u32[]{:S(2)}, u32[]{:S(2)}) collective-permute-start(bf16[1,336,896]{2,1,0:T(8,128)(2,1)} %broadcast_select_fusion.1), channel_id=1, source_target_pairs={{0,4},{4,0},{8,12},{12,8},{1,5},{5,1},{9,13},{13,9},{2,6},{6,2},{1... | collective-permute-start | bytes 1806344 | tf_op jit(solution)/shard_map/ppermute | solution.py:425
  179.3 21.8 %collective-permute-start.25 = (bf16[80,1792]{1,0:T(8,128)(2,1)}, bf16[80,1792]{1,0:T(8,128)(2,1)S(1)}, u32[]{:S(2)}, u32[]{:S(2)}) collective-permute-start(bf16[80,1792]{1,0:T(8,128)(2,1)} %get-tuple-element.15), channel_id=1, source_target_pairs={{0,5},{1,4},{2,7},{3,6},{4,9},{5,8},{6,11},{7,10},{8,13},{9,12},{1... | collective-permute-start | bytes 860168 | tf_op jit(solution)/shard_map/ppermute | solution.py:651
  201.1 13.8 %copy-start.21 = (bf16[80,1792]{1,0:T(8,128)(2,1)}, bf16[80,1792]{1,0:T(8,128)(2,1)S(1)}, u32[]{:S(2)}) copy-start(bf16[80,1792]{1,0:T(8,128)(2,1)S(1)} %collective-permute-done.25.halo_ref) | copy-start | bytes 860164
  201.7 2.3 copy-start.17
  202.9 1.7 copy-start.18
  204.1 4.0 %copy-start.16 = (bf16[256,1792]{1,0:T(8,128)(2,1)}, bf16[256,1792]{1,0:T(8,128)(2,1)S(1)}, u32[]{:S(2)}) copy-start(bf16[256,1792]{1,0:T(8,128)(2,1)S(1)} %collective-permute-done.24.x_ref) | copy-start | bytes 2752516
  210.1 4.8 %copy-start.2 = (bf16[4,1,336,896]{3,2,1,0:T(8,128)(2,1)}, bf16[4,1,336,896]{3,2,1,0:T(8,128)(2,1)S(1)}, u32[]{:S(2)}) copy-start(bf16[4,1,336,896]{3,2,1,0:T(8,128)(2,1)S(1)} %maximum_select_fusion.2.near_ref) | copy-start | bytes 7225348
  210.1 4.8 %collective-permute-start.31 = (bf16[4,1,336,896]{3,2,1,0:T(8,128)(2,1)S(1)}, bf16[4,1,336,896]{3,2,1,0:T(8,128)(2,1)}, u32[]{:S(2)}, u32[]{:S(2)}) collective-permute-start(bf16[4,1,336,896]{3,2,1,0:T(8,128)(2,1)S(1)} %maximum_select_fusion.2.near_ref), channel_id=1, source_target_pairs={{0,16},{16,0},{1,17},{17,1},{2,18},{18,2},{3,19},{19,3},{4,20},{20... | collective-permute-start | bytes 7225352 | tf_op jit(solution)/shard_map/ppermute | solution.py:425
  210.2 20.7 %collective-permute-start.33 = (bf16[3,112,896]{2,1,0:T(8,128)(2,1)}, bf16[3,112,896]{2,1,0:T(8,128)(2,1)}, u32[]{:S(2)}, u32[]{:S(2)}) collective-permute-start(bf16[3,112,896]{2,1,0:T(8,128)(2,1)} %broadcast_select_fusion.3), channel_id=1, source_target_pairs={{0,12},{4,8},{8,4},{12,0},{1,13},{5,9},{9,5},{13,1},{2,14},{6,10},... | collective-permute-start | bytes 1806344 | tf_op jit(solution)/shard_map/ppermute | solution.py:425
  214.9 15.9 %copy-start.13 = (bf16[1,3,112,896]{3,2,1,0:T(8,128)(2,1)S(1)}, bf16[1,3,112,896]{3,2,1,0:T(8,128)(2,1)}, u32[]{:S(2)}) copy-start(bf16[1,3,112,896]{3,2,1,0:T(8,128)(2,1)} %fusion.13) | copy-start | bytes 1806340
  230.9 2.2 copy-start.14
  230.9 6.5 %copy-start.25 = (s32[8]{0:T(128)S(1)}, s32[8]{0:T(128)}, u32[]{:S(2)}) copy-start(s32[8]{0:T(128)} %param.20) | copy-start | bytes 100
  230.9 6.5 %copy-start.26 = (s32[8]{0:T(128)S(1)}, s32[8]{0:T(128)}, u32[]{:S(2)}) copy-start(s32[8]{0:T(128)} %param.19) | copy-start | bytes 100
  232.8 24.6 %copy-start.4 = (bf16[4,3,112,896]{3,2,1,0:T(8,128)(2,1)}, bf16[4,3,112,896]{3,2,1,0:T(8,128)(2,1)S(1)}, u32[]{:S(2)}) copy-start(bf16[4,3,112,896]{3,2,1,0:T(8,128)(2,1)S(1)} %maximum_select_fusion.3.near_ref) | copy-start | bytes 7225348
  232.8 24.6 %collective-permute-start.34 = (bf16[4,3,112,896]{3,2,1,0:T(8,128)(2,1)S(1)}, bf16[4,3,112,896]{3,2,1,0:T(8,128)(2,1)}, u32[]{:S(2)}, u32[]{:S(2)}) collective-permute-start(bf16[4,3,112,896]{3,2,1,0:T(8,128)(2,1)S(1)} %maximum_select_fusion.3.near_ref), channel_id=1, source_target_pairs={{0,16},{16,0},{1,17},{17,1},{2,18},{18,2},{3,19},{19,3},{4,20},{20... | collective-permute-start | bytes 7225352 | tf_op jit(solution)/shard_map/ppermute | solution.py:425
  233.0 24.4 %collective-permute-start.32 = (bf16[2,256,512]{2,1,0:T(8,128)(2,1)S(1)}, bf16[2,256,512]{2,1,0:T(8,128)(2,1)S(1)}, u32[]{:S(2)}, u32[]{:S(2)}) collective-permute-start(bf16[2,256,512]{2,1,0:T(8,128)(2,1)S(1)} %copy-done.14), channel_id=1, source_target_pairs={{0,1},{1,0},{2,3},{3,2},{4,5},{5,4},{6,7},{7,6},{8,9},{9,8},{10,11... | collective-permute-start | bytes 1572872 | tf_op jit(solution)/shard_map/ppermute | solution.py:425
  233.0 10.3 %collective-permute-start.23 = (bf16[80,1792]{1,0:T(8,128)(2,1)}, bf16[80,1792]{1,0:T(8,128)(2,1)}, u32[]{:S(2)}, u32[]{:S(2)}) collective-permute-start(bf16[80,1792]{1,0:T(8,128)(2,1)} %get-tuple-element.15), channel_id=1, source_target_pairs={{0,4},{4,8},{8,12},{1,5},{5,9},{9,13},{2,6},{6,10},{10,14},{3,7},{... | collective-permute-start | bytes 860168 | tf_op jit(solution)/shard_map/ppermute | solution.py:649
  257.5 0.8 copy-start.19
  265.0 28.3 %copy-start.1 = (bf16[64,4,1792]{2,1,0:T(4,128)(2,1)S(1)}, bf16[64,4,1792]{2,1,0:T(4,128)(2,1)}, u32[]{:S(2)}) copy-start(bf16[64,4,1792]{2,1,0:T(4,128)(2,1)} %param.17) | copy-start | bytes 2752516
